TPU v7x, 32 devices: a whole 2x2x4 slice. The times are simulated.
32 devices in a mesh: rep: 4 (over x, core), shard: 8 (over z, y).
Axes of the slice: x: 2, y: 2, z: 4, core: 2. Of those that a mesh axis runs over, the one named last changes fastest.
Arguments:
- weight: bfloat16 [4, 8, 512, 2048], P('rep', None, 'shard'), may hold values from -3 to 3
- tracker: float32 [4, 8, 512, 2048], P('rep', None, 'shard'), may hold values from -40 to 40, as said below
- grad_new: bfloat16 [4, 8, 512, 2048], P('rep', None, 'shard'), may hold values from -6 to 6
- grad_old: bfloat16 [4, 8, 512, 2048], P('rep', None, 'shard'), may hold values from -6 to 6
- mix_keep: int32 [4, 2], replicated, may hold values from 4 to 12, as said below
Outputs:
- new_weight: bfloat16 [4, 8, 512, 2048], P('rep', None, 'shard')
- new_tracker: float32 [4, 8, 512, 2048], P('rep', None, 'shard')
- update: bfloat16 [4, 8, 512, 2048], P('rep', None, 'shard')
Inputs may be any that keep to these rules, and one draw needn't show every extreme that they name: `mix_keep`: every entry is one of the integers 4 to 12; some entry equals 4 and some equals 12. `tracker`: finite real values.
All inputs are finite; a program needn't handle non-finite values.
Results may differ from a plain program's by a relative error of at most 0.023.
Values may be sent and summed in bfloat16 or wider, within the bound.
No kernel may reach another device: no remote copies, remote signals or barrier semaphores. Data moves between devices by JAX's collectives and lax.ppermute only.
A program may use at most 128 MiB of HBM per device.

v0:
```python
import math

import jax
import jax.numpy as jnp
from jax import lax
from jax.sharding import PartitionSpec as P

NS_STEPS = 5


coeff_a = 3.4445
coeff_b = -4.775
coeff_c = 2.0315
learn_rate = 0.05


def swapped(shard, axis, bit):
    return lax.ppermute(shard, axis, [(i, i ^ 1 << bit) for i in range(lax.axis_size(axis))])


def gossip_weight(values, keep_row):
    for bit_index in range(keep_row.shape[0]):
        partner = swapped(values, "rep", bit_index)
        own_share = keep_row[bit_index] / 16.0
        other_share = (16.0 - keep_row[bit_index]) / 16.0
        values = (
            own_share * values.astype(jnp.float32) + other_share * partner.astype(jnp.float32)
        ).astype(jnp.bfloat16)
    return values


def gossip_tracker(values, keep_row):
    for bit_index in range(keep_row.shape[0]):
        partner = swapped(values.astype(jnp.bfloat16), "rep", bit_index).astype(values.dtype)
        own_share = keep_row[bit_index] / 16.0
        other_share = (16.0 - keep_row[bit_index]) / 16.0
        values = own_share * values + other_share * partner
    return values


def orthogonalize(block_in):
    update_scale = 0.2 * math.sqrt(max(block_in.shape[1], block_in.shape[2]))
    values = block_in.astype(jnp.float32)
    frob_norm = jnp.sqrt(jnp.sum(values * values, axis=(1, 2), keepdims=True))
    iterate = (values / (frob_norm + 1e-07)).astype(jnp.bfloat16)
    for iteration in range(NS_STEPS):
        gram_matrix = jnp.einsum(
            "kmn,kpn->kmp", iterate, iterate, preferred_element_type=jnp.float32
        ).astype(jnp.bfloat16)
        square = jnp.einsum(
            "kmp,kpq->kmq", gram_matrix, gram_matrix, preferred_element_type=jnp.float32
        )
        polynomial = (coeff_b * gram_matrix.astype(jnp.float32) + coeff_c * square).astype(
            jnp.bfloat16
        )
        product = jnp.einsum(
            "kmp,kpn->kmn", polynomial, iterate, preferred_element_type=jnp.float32
        )
        iterate = (coeff_a * iterate.astype(jnp.float32) + product).astype(jnp.bfloat16)
    return (update_scale * iterate.astype(jnp.float32)).astype(jnp.bfloat16)


def settle(block_in):
    update_block = orthogonalize(block_in[0])[None]
    return lax.all_to_all(update_block, "shard", split_axis=2, concat_axis=0, tiled=True)


def local(weight, tracker, grad_new, grad_old, mix_keep):
    rep_index = lax.axis_index("rep")
    keep_all = mix_keep.astype(jnp.float32)
    keep_row = keep_all[rep_index]
    mixed_w = gossip_weight(weight, keep_row)
    mixed_y = gossip_tracker(tracker, keep_row)
    new_tracker = mixed_y + grad_new.astype(jnp.float32) - grad_old.astype(jnp.float32)
    rounded = new_tracker.astype(jnp.bfloat16)
    shards = lax.axis_size("shard")
    experts = rounded.shape[1]
    packed = rounded.reshape(shards, experts // shards, rounded.shape[2], rounded.shape[3])
    returned = settle(lax.all_to_all(packed, "shard", split_axis=0, concat_axis=2, tiled=True))
    update = returned.reshape(rounded.shape)
    new_weight = (mixed_w.astype(jnp.float32) - learn_rate * update.astype(jnp.float32)).astype(
        jnp.bfloat16
    )
    return (new_weight, new_tracker, update)


def solution(mesh):
    return jax.shard_map(
        local,
        mesh=mesh,
        in_specs=(
            P("rep", None, "shard", None),
            P("rep", None, "shard", None),
            P("rep", None, "shard", None),
            P("rep", None, "shard", None),
            P(),
        ),
        out_specs=(
            P("rep", None, "shard", None),
            P("rep", None, "shard", None),
            P("rep", None, "shard", None),
        ),
        check_vma=False,
    )
```

profile of v0, /device:TPU:0, one launch (start us, length us, event | category | flops | bytes accessed | tf_op | source)
XLA Modules:
  0.0 243.8 jit_solution(1508572174499408415)
XLA Ops:
  0.6 0.0 copy-start.5
  0.6 3.8 %convert_element_type.215 = bf16[1,8,64,2048]{3,2,1,0:T(8,128)(2,1)} convert(f32[1,8,64,2048]{3,2,1,0:T(8,128)} %param.6) | non-fusion elementwise | flops 1048576 | bytes 6291456 | tf_op jit(solution)/shard_map/convert_element_type | solution.py:34
  4.5 0.5 collective-permute-start.2
  4.9 0.0 copy-done.5
  4.9 0.1 constant_dynamic-slice_fusion
  5.0 0.5 fusion.34
  6.8 2.1 collective-permute-done.2
  8.9 3.1 %fusion.3 = bf16[1,8,64,2048]{3,2,1,0:T(8,128)(2,1)S(1)} fusion(bf16[1,8,64,2048]{3,2,1,0:T(8,128)(2,1)S(1)} %collective-permute-done.2, f32[1,8,64,2048]{3,2,1,0:T(8,128)} %param.6, f32[]{:T(128)} %bitcast.2, f32[]{:T(128)} %bitcast.1), kind=kLoop, calls=%fused_computation.16 | loop fusion | flops 5242880 | bytes 8388616 | tf_op jit(solution)/shard_map/convert_element_type | solution.py:34
  12.0 2.9 %collective-permute-start.3 = (bf16[1,8,64,2048]{3,2,1,0:T(8,128)(2,1)S(1)}, bf16[1,8,64,2048]{3,2,1,0:T(8,128)(2,1)S(1)}, u32[]{:S(2)}, u32[]{:S(2)}) collective-permute-start(bf16[1,8,64,2048]{3,2,1,0:T(8,128)(2,1)S(1)} %fusion.3), channel_id=1, source_target_pairs={{0,16},{8,24},{16,0},{24,8},{1,17},{9,25},{17,1},{25,9},{2,18},{10... | collective-permute-start | bytes 6291464 | tf_op jit(solution)/shard_map/ppermute | solution.py:18
  16.2 44.6 %collective-permute-done.3 = bf16[1,8,64,2048]{3,2,1,0:T(8,128)(2,1)S(1)} collective-permute-done((bf16[1,8,64,2048]{3,2,1,0:T(8,128)(2,1)S(1)}, bf16[1,8,64,2048]{3,2,1,0:T(8,128)(2,1)S(1)}, u32[]{:S(2)}, u32[]{:S(2)}) %collective-permute-start.3) | collective-permute-done | bytes 2097184 | tf_op jit(solution)/shard_map/ppermute | solution.py:18
  60.9 0.0 copy-done
  60.9 0.0 copy-done.2
  60.9 0.0 copy-done.3
  60.9 4.9 %convert_bitcast_fusion = (bf16[8,1,64,2048]{3,2,1,0:T(8,128)(2,1)}, f32[1,8,64,2048]{3,2,1,0:T(8,128)}) fusion(bf16[1,8,64,2048]{3,2,1,0:T(8,128)(2,1)S(1)} %copy-done.2, bf16[1,8,64,2048]{3,2,1,0:T(8,128)(2,1)S(1)} %copy-done.3, bf16[1,8,64,2048]{3,2,1,0:T(8,128)(2,1)S(1)} %collective-permute-done.3, f32[]{:T(128)} %bitcast.3, ...), kind=kLoop, calls=%fused_computation.17 | loop fusion | flops 13631488 | bytes 18874384 | tf_op jit(solution)/shard_map/reshape | solution.py:78
  65.8 6.1 %all-to-all-start = ((bf16[8,1,64,2048]{3,2,1,0:T(8,128)(2,1)}), bf16[8,1,64,2048]{3,2,1,0:T(8,128)(2,1)S(1)}, u32[]{:S(2)}, u32[]{:S(2)}) async-start(bf16[8,1,64,2048]{3,2,1,0:T(8,128)(2,1)} %get-tuple-element.3), calls=%async_computation | async-start | bytes 4194304 | tf_op jit(solution)/shard_map/all_to_all | solution.py:79
  71.8 0.0 collective-permute-start
  71.9 47.7 %all-to-all-done = bf16[8,1,64,2048]{3,2,1,0:T(8,128)(2,1)S(1)} async-done(((bf16[8,1,64,2048]{3,2,1,0:T(8,128)(2,1)}), bf16[8,1,64,2048]{3,2,1,0:T(8,128)(2,1)S(1)}, u32[]{:S(2)}, u32[]{:S(2)}) %all-to-all-start) | async-done | bytes 2097184 | tf_op jit(solution)/shard_map/all_to_all | solution.py:79
  119.6 1.7 fusion
  121.9 0.4 fusion.1
  122.3 0.0 copy-start.4
  122.4 1.3 copy-done.4
  123.7 1.3 convolution_convert_fusion.4
  125.0 3.8 %add_convert_fusion.4 = bf16[512,2048]{1,0:T(8,128)(2,1)S(1)} fusion(bf16[512,2048]{1,0:T(8,128)(2,1)} %bitcast.46, bf16[512,512]{1,0:T(8,128)(2,1)S(1)} %convolution_convert_fusion.4), kind=kOutput, calls=%fused_computation.10 | convolution fusion | flops 1347682304 | bytes 4718592 | tf_op jit(solution)/shard_map/kmp,kpn->kmn/dot_general | solution.py:56
  128.7 1.3 convolution_convert_fusion.3
  130.0 2.9 %add_convert_fusion.3 = bf16[512,2048]{1,0:T(8,128)(2,1)} fusion(bf16[512,2048]{1,0:T(8,128)(2,1)S(1)} %add_convert_fusion.4, bf16[512,512]{1,0:T(8,128)(2,1)S(1)} %convolution_convert_fusion.3), kind=kOutput, calls=%fused_computation.9 | convolution fusion | flops 1347682304 | bytes 4718592 | tf_op jit(solution)/shard_map/kmp,kpn->kmn/dot_general | solution.py:56
  132.9 3.6 %convolution_convert_fusion.2 = bf16[512,512]{1,0:T(8,128)(2,1)S(1)} fusion(bf16[512,2048]{1,0:T(8,128)(2,1)} %add_convert_fusion.3), kind=kOutput, calls=%fused_computation.35 | convolution fusion | flops 1074003968 | bytes 2621440 | tf_op jit(solution)/shard_map/kmn,kpn->kmp/dot_general | solution.py:47
  136.6 0.0 copy-done.6
  136.6 2.9 %add_convert_fusion.2 = bf16[512,2048]{1,0:T(8,128)(2,1)} fusion(bf16[512,2048]{1,0:T(8,128)(2,1)S(1)} %copy-done.6, bf16[512,512]{1,0:T(8,128)(2,1)S(1)} %convolution_convert_fusion.2), kind=kOutput, calls=%fused_computation.8 | convolution fusion | flops 1347682304 | bytes 4718592 | tf_op jit(solution)/shard_map/kmp,kpn->kmn/dot_general | solution.py:56
  139.4 3.6 %convolution_convert_fusion.1 = bf16[512,512]{1,0:T(8,128)(2,1)S(1)} fusion(bf16[512,2048]{1,0:T(8,128)(2,1)} %add_convert_fusion.2), kind=kOutput, calls=%fused_computation.34 | convolution fusion | flops 1074003968 | bytes 2621440 | tf_op jit(solution)/shard_map/kmn,kpn->kmp/dot_general | solution.py:47
  143.1 0.0 copy-done.7
  143.1 2.9 %add_convert_fusion.1 = bf16[512,2048]{1,0:T(8,128)(2,1)} fusion(bf16[512,2048]{1,0:T(8,128)(2,1)S(1)} %copy-done.7, bf16[512,512]{1,0:T(8,128)(2,1)S(1)} %convolution_convert_fusion.1), kind=kOutput, calls=%fused_computation.7 | convolution fusion | flops 1347682304 | bytes 4718592 | tf_op jit(solution)/shard_map/kmp,kpn->kmn/dot_general | solution.py:56
  146.0 3.5 %convolution_convert_fusion = bf16[512,512]{1,0:T(8,128)(2,1)S(1)} fusion(bf16[512,2048]{1,0:T(8,128)(2,1)} %add_convert_fusion.1), kind=kOutput, calls=%fused_computation.33 | convolution fusion | flops 1074003968 | bytes 2621440 | tf_op jit(solution)/shard_map/kmn,kpn->kmp/dot_general | solution.py:47
  149.5 4.1 %fusion.2 = bf16[1,1,512,2048]{3,2,1,0:T(8,128)(2,1)S(1)} fusion(bf16[512,2048]{1,0:T(8,128)(2,1)} %add_convert_fusion.1, bf16[512,512]{1,0:T(8,128)(2,1)S(1)} %convolution_convert_fusion), kind=kOutput, calls=%fused_computation.15 | convolution fusion | flops 1350828032 | bytes 4718592 | tf_op jit(solution)/shard_map/kmp,kpn->kmn/dot_general | solution.py:56
  153.6 5.2 %copy.13 = bf16[1,1,512,2048]{3,1,0,2:T(2,128)(2,1)} copy(bf16[1,1,512,2048]{3,2,1,0:T(8,128)(2,1)S(1)} %fusion.2) | data formatting | bytes 4194304 | tf_op jit(solution)/shard_map/broadcast_in_dim | solution.py:64
  158.7 0.5 broadcast.97
  159.3 13.2 %reduce.2 = bf16[512,2048]{1,0:T(8,128)(2,1)S(1)} reduce(bf16[512,1,1,2048]{3,2,1,0:T(2,128)(2,1)} %bitcast.41, bf16[]{:T(256)} %broadcast.97), dimensions={1,2}, to_apply=%bitcast.40.reduce_sub_computation | reduce | bytes 4194306
  172.4 3.8 %reshape.216 = bf16[8,2,65536]{2,1,0:T(2,128)(2,1)} reshape(bf16[512,2048]{1,0:T(8,128)(2,1)S(1)} %reduce.2) | data formatting | bytes 4194304
  176.2 4.3 %all-to-all-start.1 = ((bf16[8,2,65536]{2,1,0:T(2,128)(2,1)}), bf16[8,2,65536]{2,1,0:T(2,128)(2,1)}, u32[]{:S(2)}, u32[]{:S(2)}) async-start(bf16[8,2,65536]{2,1,0:T(2,128)(2,1)} %reshape.216), calls=%async_computation.1 | async-start | bytes 4194304 | tf_op jit(solution)/shard_map/all_to_all | solution.py:65
  180.5 0.0 collective-permute-done
  180.6 3.1 %add_convert_fusion.6 = bf16[1,8,64,2048]{3,2,1,0:T(8,128)(2,1)S(1)} fusion(bf16[1,8,64,2048]{3,2,1,0:T(8,128)(2,1)} %collective-permute-done, bf16[1,8,64,2048]{3,2,1,0:T(8,128)(2,1)} %param.5, f32[]{:T(128)} %bitcast.2, f32[]{:T(128)} %bitcast.1), kind=kLoop, calls=%fused_computation.14 | loop fusion | flops 6291456 | bytes 6291464 | tf_op jit(solution)/shard_map/convert_element_type | solution.py:28
  183.7 1.6 collective-permute-start.1
  185.2 43.2 %all-to-all-done.1 = bf16[8,2,65536]{2,1,0:T(2,128)(2,1)} async-done(((bf16[8,2,65536]{2,1,0:T(2,128)(2,1)}), bf16[8,2,65536]{2,1,0:T(2,128)(2,1)}, u32[]{:S(2)}, u32[]{:S(2)}) %all-to-all-start.1) | async-done | bytes 2097184 | tf_op jit(solution)/shard_map/all_to_all | solution.py:65
  228.4 6.8 %reshape.217 = bf16[512,1,1,2048]{3,2,1,0:T(2,128)(2,1)} reshape(bf16[8,2,65536]{2,1,0:T(2,128)(2,1)} %all-to-all-done.1) | data formatting | bytes 4194304
  235.1 3.5 %copy.11 = bf16[1,1,512,2048]{3,2,0,1:T(8,128)(2,1)S(1)} copy(bf16[1,1,512,2048]{3,1,0,2:T(2,128)(2,1)} %bitcast.42) | data formatting | bytes 4194304
  238.6 0.0 copy-start.1
  238.6 0.0 collective-permute-done.1
  238.6 5.2 %subtract_convert_fusion = bf16[1,8,64,2048]{3,2,1,0:T(8,128)(2,1)} fusion(bf16[1,8,64,2048]{3,2,1,0:T(8,128)(2,1)S(1)} %bitcast.43, bf16[1,8,64,2048]{3,2,1,0:T(8,128)(2,1)} %collective-permute-done.1, bf16[1,8,64,2048]{3,2,1,0:T(8,128)(2,1)S(1)} %add_convert_fusion.6, f32[]{:T(128)} %bitcast.3, f32[]{:T(128)} %bitcast), kind=kLoop, calls=%fused_computation.4 | loop fusion | flops 11534336 | bytes 8388616 | tf_op jit(solution)/shard_map/convert_element_type | solution.py:81
  243.8 0.0 copy-done.1
  (6 shorter events, 0.0 us)
Async XLA Ops:
  0.6 4.3 %copy-start.5 = (s32[4,2]{0,1:T(2,128)S(1)}, s32[4,2]{0,1:T(2,128)}, u32[]{:S(2)}) copy-start(s32[4,2]{0,1:T(2,128)} %param.9) | copy-start | bytes 100
  4.5 4.5 %collective-permute-start.2 = (bf16[1,8,64,2048]{3,2,1,0:T(8,128)(2,1)}, bf16[1,8,64,2048]{3,2,1,0:T(8,128)(2,1)S(1)}, u32[]{:S(2)}, u32[]{:S(2)}) collective-permute-start(bf16[1,8,64,2048]{3,2,1,0:T(8,128)(2,1)} %convert_element_type.215), channel_id=1, source_target_pairs={{0,8},{8,0},{16,24},{24,16},{1,9},{9,1},{17,25},{25,17},{2,10},{10... | collective-permute-start | bytes 6291464 | tf_op jit(solution)/shard_map/ppermute | solution.py:18
  8.9 52.0 %copy-start = (f32[1,8,64,2048]{3,2,1,0:T(8,128)S(1)}, f32[1,8,64,2048]{3,2,1,0:T(8,128)}, u32[]{:S(2)}) copy-start(f32[1,8,64,2048]{3,2,1,0:T(8,128)} %param.6) | copy-start | bytes 12582916
  8.9 52.0 %copy-start.2 = (bf16[1,8,64,2048]{3,2,1,0:T(8,128)(2,1)S(1)}, bf16[1,8,64,2048]{3,2,1,0:T(8,128)(2,1)}, u32[]{:S(2)}) copy-start(bf16[1,8,64,2048]{3,2,1,0:T(8,128)(2,1)} %param.8) | copy-start | bytes 6291460
  8.9 52.0 %copy-start.3 = (bf16[1,8,64,2048]{3,2,1,0:T(8,128)(2,1)S(1)}, bf16[1,8,64,2048]{3,2,1,0:T(8,128)(2,1)}, u32[]{:S(2)}) copy-start(bf16[1,8,64,2048]{3,2,1,0:T(8,128)(2,1)} %param.7) | copy-start | bytes 6291460
  12.0 48.9 %collective-permute-start.3 = (bf16[1,8,64,2048]{3,2,1,0:T(8,128)(2,1)S(1)}, bf16[1,8,64,2048]{3,2,1,0:T(8,128)(2,1)S(1)}, u32[]{:S(2)}, u32[]{:S(2)}) collective-permute-start(bf16[1,8,64,2048]{3,2,1,0:T(8,128)(2,1)S(1)} %fusion.3), channel_id=1, source_target_pairs={{0,16},{8,24},{16,0},{24,8},{1,17},{9,25},{17,1},{25,9},{2,18},{10... | collective-permute-start | bytes 6291464 | tf_op jit(solution)/shard_map/ppermute | solution.py:18
  65.8 53.8 %all-to-all-start = ((bf16[8,1,64,2048]{3,2,1,0:T(8,128)(2,1)}), bf16[8,1,64,2048]{3,2,1,0:T(8,128)(2,1)S(1)}, u32[]{:S(2)}, u32[]{:S(2)}) async-start(bf16[8,1,64,2048]{3,2,1,0:T(8,128)(2,1)} %get-tuple-element.3), calls=%async_computation | async-start | bytes 4194304 | tf_op jit(solution)/shard_map/all_to_all | solution.py:79
  71.8 108.7 %collective-permute-start = (bf16[1,8,64,2048]{3,2,1,0:T(8,128)(2,1)}, bf16[1,8,64,2048]{3,2,1,0:T(8,128)(2,1)}, u32[]{:S(2)}, u32[]{:S(2)}) collective-permute-start(bf16[1,8,64,2048]{3,2,1,0:T(8,128)(2,1)} %param.5), channel_id=1, source_target_pairs={{0,8},{8,0},{16,24},{24,16},{1,9},{9,1},{17,25},{25,17},{2,10},{10... | collective-permute-start | bytes 6291464 | tf_op jit(solution)/shard_map/ppermute | solution.py:18
  122.3 1.3 copy-start.4
  132.9 3.7 %copy-start.6 = (bf16[512,2048]{1,0:T(8,128)(2,1)S(1)}, bf16[512,2048]{1,0:T(8,128)(2,1)}, u32[]{:S(2)}) copy-start(bf16[512,2048]{1,0:T(8,128)(2,1)} %add_convert_fusion.3) | copy-start | bytes 6291460
  139.4 3.7 %copy-start.7 = (bf16[512,2048]{1,0:T(8,128)(2,1)S(1)}, bf16[512,2048]{1,0:T(8,128)(2,1)}, u32[]{:S(2)}) copy-start(bf16[512,2048]{1,0:T(8,128)(2,1)} %add_convert_fusion.2) | copy-start | bytes 6291460
  176.2 52.2 %all-to-all-start.1 = ((bf16[8,2,65536]{2,1,0:T(2,128)(2,1)}), bf16[8,2,65536]{2,1,0:T(2,128)(2,1)}, u32[]{:S(2)}, u32[]{:S(2)}) async-start(bf16[8,2,65536]{2,1,0:T(2,128)(2,1)} %reshape.216), calls=%async_computation.1 | async-start | bytes 4194304 | tf_op jit(solution)/shard_map/all_to_all | solution.py:65
  183.7 55.0 %collective-permute-start.1 = (bf16[1,8,64,2048]{3,2,1,0:T(8,128)(2,1)S(1)}, bf16[1,8,64,2048]{3,2,1,0:T(8,128)(2,1)}, u32[]{:S(2)}, u32[]{:S(2)}) collective-permute-start(bf16[1,8,64,2048]{3,2,1,0:T(8,128)(2,1)S(1)} %add_convert_fusion.6), channel_id=1, source_target_pairs={{0,16},{8,24},{16,0},{24,8},{1,17},{9,25},{17,1},{25,9},{2,18},{10... | collective-permute-start | bytes 6291464 | tf_op jit(solution)/shard_map/ppermute | solution.py:18
  238.6 5.2 %copy-start.1 = (bf16[1,1,512,2048]{3,2,0,1:T(8,128)(2,1)}, bf16[1,1,512,2048]{3,2,0,1:T(8,128)(2,1)S(1)}, u32[]{:S(2)}) copy-start(bf16[1,1,512,2048]{3,2,0,1:T(8,128)(2,1)S(1)} %copy.11) | copy-start | bytes 6291460
where the time goes:
time: 244 us
  waiting for transfers between devices  138 us (57%)
  other arithmetic  35.3 us (14%)
  matrix products  29.8 us (12%)
  local copies, waits for them, and re-layouts  21.6 us (9%)
  starting transfers between devices  15.4 us (6%)
  between operations  4.09 us (2%)
    all_to_all x1, waiting for transfers between devices, local(): lax.all_to_all(packed, 'shard', split_axis=0, concat_axis=2, tiled=True)  47.7 us
    ppermute x4, waiting for transfers between devices, swapped(): lax.ppermute(shard, axis, [(i, i ^ 1 << bit) for i in range(lax.axis_size...  46.7 us
    all_to_all x1, waiting for transfers between devices, settle(): lax.all_to_all(update_block, 'shard', split_axis=2, concat_axis=0, tiled=...  43.2 us
    dot_general x5, matrix products, orthogonalize(): jnp.einsum('kmp,kpn->kmn', polynomial, iterate, preferred_element_type=jn...  16.5 us
    unnamed x20, local copies, waits for them, and re-layouts  15.9 us
    dot_general x5, matrix products, orthogonalize(): jnp.einsum('kmn,kpn->kmp', iterate, iterate, preferred_element_type=jnp.f...  13.4 us
    unnamed x1, other arithmetic  13.2 us
    convert_element_type x2, other arithmetic, gossip_tracker(): values.astype(jnp.bfloat16)  6.91 us
  transfers between devices with their start and end apart: 6, of which 4 were waited for; matrix products, arithmetic and copies ran while one was open for 28% of the time, Pallas kernels for 0%

commit v1 on v0

v1 whole, which is shorter than its diff:
```python
import math

import jax
import jax.numpy as jnp
from jax import lax
from jax.experimental import pallas as pl
from jax.experimental.pallas import tpu as pltpu
from jax.sharding import PartitionSpec as P

NS_STEPS = 5
CHUNKS = 4

coeff_a = 3.4445
coeff_b = -4.775
coeff_c = 2.0315
learn_rate = 0.05

F32 = jnp.float32
BF16 = jnp.bfloat16
ANY = pl.BlockSpec(memory_space=pl.ANY)
SMEM = pl.BlockSpec(memory_space=pltpu.SMEM)
MIB = 1 << 20


def swapped(values, axis, bit):
    return lax.ppermute(values, axis, [(i, i ^ 1 << bit) for i in range(lax.axis_size(axis))])


def cost(flops, moved):
    return pl.CostEstimate(flops=int(flops), bytes_accessed=int(moved), transcendentals=0)


def params(mib):
    return pltpu.CompilerParams(vmem_limit_bytes=mib * MIB)


def slabs(experts):
    return experts // 4 if experts % 4 == 0 else 1


def mix_body(share, own, near, far, far_near, grad_new, grad_old, *rest):
    tracker_out, rounded_out = rest[-2:]
    mixed = (
        share[0] * own[...]
        + share[1] * near[...].astype(F32)
        + share[2] * far[...].astype(F32)
        + share[3] * far_near[...].astype(F32)
    )
    tracker = mixed + grad_new[...].astype(F32) - grad_old[...].astype(F32)
    tracker_out[...] = tracker
    rounded_out[...] = tracker.astype(BF16)


def mix_chunk(chunk, share, own, near, far, far_near, grad_new, grad_old, done):
    experts, rows, columns = own.shape
    width = far.shape[2]
    slab = slabs(experts)
    whole = pl.BlockSpec((slab, rows, width), lambda i: (i, 0, chunk))
    part = pl.BlockSpec((slab, rows, width), lambda i: (i, 0, 0))
    operands = [share, own, near, far, far_near, grad_new, grad_old]
    in_specs = [SMEM, whole, whole, part, part, whole, whole]
    aliases = {}
    if done is not None:
        aliases = {len(operands): 0}
        operands.append(done)
        in_specs.append(ANY)
    size = experts * rows * width
    return pl.pallas_call(
        mix_body,
        grid=(experts // slab,),
        in_specs=in_specs,
        out_specs=(whole, part),
        out_shape=(
            jax.ShapeDtypeStruct(own.shape, F32),
            jax.ShapeDtypeStruct(far.shape, BF16),
        ),
        input_output_aliases=aliases,
        compiler_params=params(24),
        cost_estimate=cost(12 * size, 20 * size),
        name="mix",
    )(*operands)


def split(values):
    high = values.astype(BF16)
    return high, (values - high.astype(F32)).astype(BF16)


def times(left, right):
    return jnp.dot(left, right, preferred_element_type=F32)


def diagonal(size):
    return lax.broadcasted_iota(jnp.int32, (size, size), 0) == lax.broadcasted_iota(
        jnp.int32, (size, size), 1
    )


def polynomial_body(scale, gram_ref, high_ref, low_ref, gram_held, poly_held):
    gram = gram_ref[0]
    size = gram.shape[0]
    on_diagonal = diagonal(size)
    square_norm = jnp.sum(
        jnp.sum(jnp.where(on_diagonal, gram, 0.0), axis=0, keepdims=True), axis=1, keepdims=True
    )
    inverse = 1.0 / (jnp.sqrt(square_norm) + 1e-07)
    gram_held[...] = gram * inverse * inverse
    poly_held[...] = jnp.where(on_diagonal, 1.0, 0.0)

    def step(last):
        gram = gram_held[...]
        gram_high, gram_low = split(gram)
        shift = (
            coeff_b * gram_high.astype(F32) + coeff_c * times(gram_high, gram_high)
        ).astype(BF16)
        poly = poly_held[...]
        poly_high, poly_low = split(poly)
        poly_held[...] = coeff_a * poly + times(shift, poly_high) + times(shift, poly_low)
        if not last:
            half = coeff_a * gram + times(shift, gram_high) + times(shift, gram_low)
            half_high, half_low = split(half)
            gram_held[...] = coeff_a * half + times(half_high, shift) + times(half_low, shift)

    @pl.loop(0, NS_STEPS - 1)
    def _(_):
        step(False)

    step(True)
    high, low = split(poly_held[...] * (scale * inverse))
    high_ref[0] = high
    low_ref[0] = low


def polynomial(gram, scale):
    count, size, _ = gram.shape
    block = pl.BlockSpec((1, size, size), lambda i: (i, 0, 0))
    kept = jax.ShapeDtypeStruct(gram.shape, BF16)

    def body(*refs):
        polynomial_body(scale, *refs)

    return pl.pallas_call(
        body,
        grid=(count,),
        in_specs=[block],
        out_specs=(block, block),
        out_shape=(kept, kept),
        scratch_shapes=[pltpu.VMEM((size, size), F32), pltpu.VMEM((size, size), F32)],
        compiler_params=params(32),
        cost_estimate=cost(2 * 29 * count * size**3, 8 * count * size**2),
        name="polynomial",
    )(gram)


def apply_body(high, low, values, out):
    out[0] = (times(high[0], values[0]) + times(low[0], values[0])).astype(BF16)


def apply_polynomial(high, low, values):
    count, size, width = values.shape
    square = pl.BlockSpec((1, size, size), lambda i: (i, 0, 0))
    block = pl.BlockSpec((1, size, width), lambda i: (i, 0, 0))
    return pl.pallas_call(
        apply_body,
        grid=(count,),
        in_specs=[square, square, block],
        out_specs=block,
        out_shape=jax.ShapeDtypeStruct(values.shape, BF16),
        compiler_params=params(24),
        cost_estimate=cost(4 * count * size**2 * width, 4 * count * size * (size + width)),
        name="apply",
    )(high, low, values)


def settle_body(share, own, far, update, *rest):
    weight_out, update_out = rest[-2:]
    mixed = (share[4] * own[...].astype(F32) + share[5] * far[...].astype(F32)).astype(BF16)
    taken = update[...]
    weight_out[...] = (mixed.astype(F32) - learn_rate * taken.astype(F32)).astype(BF16)
    update_out[...] = taken


def settle_chunk(chunk, share, own, far, update, done):
    experts, rows, columns = own.shape
    width = update.shape[2]
    slab = slabs(experts)
    whole = pl.BlockSpec((slab, rows, width), lambda i: (i, 0, chunk))
    part = pl.BlockSpec((slab, rows, width), lambda i: (i, 0, 0))
    operands = [share, own, far, update]
    in_specs = [SMEM, whole, whole, part]
    aliases = {}
    if done is not None:
        aliases = {len(operands): 0, len(operands) + 1: 1}
        operands += done
        in_specs += [ANY, ANY]
    size = experts * rows * width
    kept = jax.ShapeDtypeStruct(own.shape, BF16)
    return pl.pallas_call(
        settle_body,
        grid=(experts // slab,),
        in_specs=in_specs,
        out_specs=(whole, whole),
        out_shape=(kept, kept),
        input_output_aliases=aliases,
        compiler_params=params(24),
        cost_estimate=cost(8 * size, 10 * size),
        name="settle",
    )(*operands)


def exchange(values):
    return lax.all_to_all(values, "shard", split_axis=0, concat_axis=0, tiled=True)


def local(weight, tracker, grad_new, grad_old, mix_keep):
    shards = lax.axis_size("shard")
    _, experts, rows, columns = tracker.shape
    each = experts // shards
    size = shards * rows
    chunks = CHUNKS
    width = columns // chunks
    weight, tracker, grad_new, grad_old = (
        values.reshape(experts, rows, columns) for values in (weight, tracker, grad_new, grad_old)
    )

    rep_index = lax.axis_index("rep")
    keep = mix_keep.astype(F32) / 16.0
    first, second = keep[rep_index, 0], keep[rep_index, 1]
    far_first = keep[rep_index ^ 2, 0]
    share = jnp.stack(
        [
            second * first,
            second * (1.0 - first),
            (1.0 - second) * far_first,
            (1.0 - second) * (1.0 - far_first),
            second,
            1.0 - second,
        ]
    )

    far = []
    for chunk in range(chunks):
        sent = lax.slice_in_dim(tracker, chunk * width, (chunk + 1) * width, axis=2).astype(BF16)
        far.append(swapped(sent, "rep", 1))
    near = swapped(tracker.astype(BF16), "rep", 0)
    new_tracker = None
    held = []
    gram = None
    for chunk in range(chunks):
        far_near = swapped(far[chunk], "rep", 0)
        new_tracker, rounded = mix_chunk(
            chunk, share, tracker, near, far[chunk], far_near, grad_new, grad_old, new_tracker
        )
        matrix = exchange(rounded).reshape(shards, each, rows, width)
        matrix = matrix.swapaxes(0, 1).reshape(each, size, width)
        held.append(matrix)
        part = jnp.einsum("kmn,kpn->kmp", matrix, matrix, preferred_element_type=F32)
        gram = part if gram is None else gram + part

    weight_near = swapped(weight, "rep", 0)
    weight_own = (
        first * weight.astype(F32) + (1.0 - first) * weight_near.astype(F32)
    ).astype(BF16)
    weight_own, _ = lax.optimization_barrier((weight_own, far[-1]))
    weight_far = swapped(weight_own, "rep", 1)

    high, low = polynomial(gram, 0.2 * math.sqrt(max(size, columns)))
    done = None
    for chunk in range(chunks):
        update = apply_polynomial(high, low, held[chunk])
        update = update.reshape(each, shards, rows, width).swapaxes(0, 1)
        update = exchange(update.reshape(experts, rows, width))
        done = settle_chunk(chunk, share, weight_own, weight_far, update, done)
    shape = (1, experts, rows, columns)
    return done[0].reshape(shape), new_tracker.reshape(shape), done[1].reshape(shape)


def solution(mesh):
    spec = P("rep", None, "shard", None)
    return jax.shard_map(
        local,
        mesh=mesh,
        in_specs=(spec, spec, spec, spec, P()),
        out_specs=(spec, spec, spec),
        check_vma=False,
    )
```

time: 244 us -> 229 us (0.939)
  Pallas kernels: 0 us -> 43.9 us
  waiting for transfers between devices: 138 us -> 105 us
  other arithmetic: 35.3 us -> 7.63 us
  matrix products: 29.8 us -> 3.06 us
  starting transfers between devices: 15.4 us -> 40.3 us
    pallas_call x0 -> x13, Pallas kernels: none -> 43.9 us  [the longest x4 14.8 us: mix_chunk(): pl.pallas_call(mix_body, grid=(experts // slab,), in_specs=in_specs, out_...]
    all_to_all x2 -> x8, waiting for transfers between devices: 90.9 us -> 64.1 us  [exchange(): lax.all_to_all(values, 'shard', split_axis=0, concat_axis=0, tiled=True)]
    dot_general x10 -> x4, matrix products: 29.8 us -> 3.06 us  [local(): jnp.einsum('kmn,kpn->kmp', matrix, matrix, preferred_element_type=F32)]
    all_to_all x2 -> x8, starting transfers between devices: 10.4 us -> 32.6 us  [exchange(): lax.all_to_all(values, 'shard', split_axis=0, concat_axis=0, tiled=True)]
    unnamed x1 -> x0, other arithmetic: 13.2 us -> none
    convert_element_type x6 -> x1, other arithmetic: 15.6 us -> 3.8 us  [local(): weight_own = (first * weight.astype(F32) + (1.0 - first) * weight_near.as...]
    ppermute x4 -> x11, waiting for transfers between devices: 46.7 us -> 40.7 us  [swapped(): lax.ppermute(values, axis, [(i, i ^ 1 << bit) for i in range(lax.axis_siz...]
    broadcast_in_dim x1 -> x0, local copies, waits for them, and re-layouts: 5.19 us -> none  [settle(): update_block = orthogonalize(block_in[0])[None]]
  transfers between devices with their start and end apart: 6 -> 19, of which waited for: 4 -> 12; matrix products, arithmetic and copies ran while one was open for 28% -> 5% of each run, Pallas kernels for 0% -> 16%
where the time goes in v1:
time: 229 us; the launch traced here: 227 us
  waiting for transfers between devices  105 us (46%)
  Pallas kernels  43.9 us (19%)
  starting transfers between devices  40.3 us (18%)
  local copies, waits for them, and re-layouts  22.2 us (10%)
  other arithmetic  7.63 us (3%)
  between operations  5.34 us (2%)
  matrix products  3.06 us (1%)
    all_to_all x8, waiting for transfers between devices, exchange(): lax.all_to_all(values, 'shard', split_axis=0, concat_axis=0, tiled=True)  64.1 us
    ppermute x11, waiting for transfers between devices, swapped(): lax.ppermute(values, axis, [(i, i ^ 1 << bit) for i in range(lax.axis_siz...  40.7 us
    all_to_all x8, starting transfers between devices, exchange(): lax.all_to_all(values, 'shard', split_axis=0, concat_axis=0, tiled=True)  32.6 us
    unnamed x46, local copies, waits for them, and re-layouts  18 us
    pallas_call x4, Pallas kernels, mix_chunk(): pl.pallas_call(mix_body, grid=(experts // slab,), in_specs=in_specs, out_...  14.8 us
    pallas_call x4, Pallas kernels, settle_chunk(): pl.pallas_call(settle_body, grid=(experts // slab,), in_specs=in_specs, o...  13.8 us
    pallas_call x1, Pallas kernels, polynomial(): pl.pallas_call(body, grid=(count,), in_specs=[block], out_specs=(block, b...  9.83 us
    ppermute x11, starting transfers between devices, swapped(): lax.ppermute(values, axis, [(i, i ^ 1 << bit) for i in range(lax.axis_siz...  7.7 us
  transfers between devices with their start and end apart: 19, of which 12 were waited for; matrix products, arithmetic and copies ran while one was open for 5% of the time, Pallas kernels for 16%

profile of v1, /device:TPU:0, one launch (start us, length us, event | category | flops | bytes accessed | tf_op | source)
XLA Modules:
  0.0 227.1 jit_solution(7414885973429361352)
XLA Ops:
  0.6 3.8 %bitcast_convert_fusion = bf16[8,64,2048]{2,1,0:T(8,128)(2,1)} fusion(f32[1,8,64,2048]{3,2,1,0:T(8,128)} %param.6), kind=kLoop, calls=%fused_computation.9 | loop fusion | flops 1048576 | bytes 6291456 | tf_op jit(solution)/shard_map/convert.3
  4.9 2.9 %fusion.1 = (bf16[8,64,512]{2,1,0:T(8,128)(2,1)}, bf16[8,64,512]{2,1,0:T(8,128)(2,1)S(1)}, bf16[8,64,512]{2,1,0:T(8,128)(2,1)S(1)}, bf16[8,64,512]{2,1,0:T(8,128)(2,1)}) fusion(bf16[8,64,2048]{2,1,0:T(8,128)(2,1)} %bitcast_convert_fusion), kind=kLoop, calls=%fused_computation.10 | loop fusion | bytes 4194304 | tf_op jit(solution)/shard_map/slice | solution.py:243
  7.8 2.5 %collective-permute-start.4 = (bf16[8,64,512]{2,1,0:T(8,128)(2,1)S(1)}, bf16[8,64,512]{2,1,0:T(8,128)(2,1)S(1)}, u32[]{:S(2)}, u32[]{:S(2)}) collective-permute-start(bf16[8,64,512]{2,1,0:T(8,128)(2,1)S(1)} %get-tuple-element.43), channel_id=1, source_target_pairs={{0,16},{8,24},{16,0},{24,8},{1,17},{9,25},{17,1},{25,9},{2,18},{10... | collective-permute-start | bytes 1572872 | tf_op jit(solution)/shard_map/ppermute | solution.py:26
  10.3 12.7 %collective-permute-done.4.far = bf16[8,64,512]{2,1,0:T(8,128)(2,1)S(1)} collective-permute-done((bf16[8,64,512]{2,1,0:T(8,128)(2,1)S(1)}, bf16[8,64,512]{2,1,0:T(8,128)(2,1)S(1)}, u32[]{:S(2)}, u32[]{:S(2)}) %collective-permute-start.4) | collective-permute-done | bytes 524320 | tf_op jit(solution)/shard_map/ppermute | solution.py:26
  23.0 10.9 %collective-permute-done.6.far = bf16[8,64,512]{2,1,0:T(8,128)(2,1)S(1)} collective-permute-done((bf16[8,64,512]{2,1,0:T(8,128)(2,1)S(1)}, bf16[8,64,512]{2,1,0:T(8,128)(2,1)S(1)}, u32[]{:S(2)}, u32[]{:S(2)}) %collective-permute-start.6) | collective-permute-done | bytes 524320 | tf_op jit(solution)/shard_map/ppermute | solution.py:26
  39.8 2.2 copy-done
  42.0 1.6 copy-done.4
  43.6 3.7 %mix.4 = (f32[8,64,2048]{2,1,0:T(8,128)}, bf16[8,64,512]{2,1,0:T(8,128)(2,1)S(1)}) custom-call(f32[6]{0:T(128)S(1)} %stack.23.share, f32[8,64,2048]{2,1,0:T(8,128)S(1)} %bitcast.40, bf16[8,64,2048]{2,1,0:T(8,128)(2,1)} %collective-permute-done.3.near, bf16[8,64,512]{2,1,0:T(8,128)(2,1)S(1)} %collective-permute-done.4.far, ...), custom_call_target="tpu_custom_call" | custom-call | flops 3145728 | bytes 5242880 | tf_op jit(solution)/shard_map/mix/pallas_call | solution.py:68
  47.2 3.9 %mix.5 = (f32[8,64,2048]{2,1,0:T(8,128)}, bf16[8,64,512]{2,1,0:T(8,128)(2,1)}) custom-call(f32[6]{0:T(128)S(1)} %stack.23.share, f32[8,64,2048]{2,1,0:T(8,128)S(1)} %bitcast.41, bf16[8,64,2048]{2,1,0:T(8,128)(2,1)} %collective-permute-done.3.near, bf16[8,64,512]{2,1,0:T(8,128)(2,1)S(1)} %collective-permute-done.6.far, ...), custom_call_target="tpu_custom_call", output_to_operand_aliasing={{0}: (7, {})} | custom-call | flops 3145728 | bytes 5242880 | tf_op jit(solution)/shard_map/mix/pallas_call | solution.py:68
  51.2 6.1 %all-to-all-start.1 = ((bf16[8,64,512]{2,1,0:T(8,128)(2,1)}), bf16[8,64,512]{2,1,0:T(8,128)(2,1)}, u32[]{:S(2)}, u32[]{:S(2)}) async-start(bf16[8,64,512]{2,1,0:T(8,128)(2,1)} %get-tuple-element.25), calls=%async_computation.1 | async-start | bytes 1048576 | tf_op jit(solution)/shard_map/all_to_all | solution.py:212
  57.3 1.5 collective-permute-start.8
  58.8 13.8 %all-to-all-done.1 = bf16[8,64,512]{2,1,0:T(8,128)(2,1)} async-done(((bf16[8,64,512]{2,1,0:T(8,128)(2,1)}), bf16[8,64,512]{2,1,0:T(8,128)(2,1)}, u32[]{:S(2)}, u32[]{:S(2)}) %all-to-all-start.1) | async-done | bytes 524320 | tf_op jit(solution)/shard_map/all_to_all | solution.py:212
  72.5 3.6 %all-to-all-start = ((bf16[8,64,512]{2,1,0:T(8,128)(2,1)}), bf16[8,64,512]{2,1,0:T(8,128)(2,1)S(1)}, u32[]{:S(2)}, u32[]{:S(2)}) async-start(bf16[8,64,512]{2,1,0:T(8,128)(2,1)} %copy-done.19), calls=%async_computation | async-start | bytes 1048576 | tf_op jit(solution)/shard_map/all_to_all | solution.py:212
  76.2 1.6 collective-permute-start.1
  78.1 2.2 copy-done.1
  80.3 1.6 copy-done.5
  81.9 3.5 %mix.6 = (f32[8,64,2048]{2,1,0:T(8,128)}, bf16[8,64,512]{2,1,0:T(8,128)(2,1)S(1)}) custom-call(f32[6]{0:T(128)S(1)} %stack.23.share, f32[8,64,2048]{2,1,0:T(8,128)S(1)} %bitcast.42, bf16[8,64,2048]{2,1,0:T(8,128)(2,1)} %collective-permute-done.3.near, bf16[8,64,512]{2,1,0:T(8,128)(2,1)S(1)} %collective-permute-done.8.far, ...), custom_call_target="tpu_custom_call", output_to_operand_aliasing={{0}: (7, {})} | custom-call | flops 3145728 | bytes 5242880 | tf_op jit(solution)/shard_map/mix/pallas_call | solution.py:68
  86.3 4.6 %all-to-all-done = bf16[8,64,512]{2,1,0:T(8,128)(2,1)S(1)} async-done(((bf16[8,64,512]{2,1,0:T(8,128)(2,1)}), bf16[8,64,512]{2,1,0:T(8,128)(2,1)S(1)}, u32[]{:S(2)}, u32[]{:S(2)}) %all-to-all-start) | async-done | bytes 524320 | tf_op jit(solution)/shard_map/all_to_all | solution.py:212
  90.9 3.6 %all-to-all-start.2 = ((bf16[8,64,512]{2,1,0:T(8,128)(2,1)}), bf16[8,64,512]{2,1,0:T(8,128)(2,1)S(1)}, u32[]{:S(2)}, u32[]{:S(2)}) async-start(bf16[8,64,512]{2,1,0:T(8,128)(2,1)} %copy-done.20), calls=%async_computation.2 | async-start | bytes 1048576 | tf_op jit(solution)/shard_map/all_to_all | solution.py:212
  94.6 2.1 collective-permute-done.10.far_near
  96.7 2.2 copy-done.2
  98.9 1.6 copy-done.6
  100.5 3.7 %mix.7 = (f32[8,64,2048]{2,1,0:T(8,128)}, bf16[8,64,512]{2,1,0:T(8,128)(2,1)S(1)}) custom-call(f32[6]{0:T(128)S(1)} %stack.23.share, f32[8,64,2048]{2,1,0:T(8,128)S(1)} %bitcast.43, bf16[8,64,2048]{2,1,0:T(8,128)(2,1)} %collective-permute-done.3.near, bf16[8,64,512]{2,1,0:T(8,128)(2,1)} %collective-permute-done.1.far, ...), custom_call_target="tpu_custom_call", output_to_operand_aliasing={{0}: (7, {})} | custom-call | flops 3145728 | bytes 5242880 | tf_op jit(solution)/shard_map/mix/pallas_call | solution.py:68
  104.9 4.2 %all-to-all-done.2 = bf16[8,64,512]{2,1,0:T(8,128)(2,1)S(1)} async-done(((bf16[8,64,512]{2,1,0:T(8,128)(2,1)}), bf16[8,64,512]{2,1,0:T(8,128)(2,1)S(1)}, u32[]{:S(2)}, u32[]{:S(2)}) %all-to-all-start.2) | async-done | bytes 524320 | tf_op jit(solution)/shard_map/all_to_all | solution.py:212
  109.2 0.8 copy-done.7
  110.0 3.6 %all-to-all-start.3 = ((bf16[8,64,512]{2,1,0:T(8,128)(2,1)}), bf16[8,64,512]{2,1,0:T(8,128)(2,1)S(1)}, u32[]{:S(2)}, u32[]{:S(2)}) async-start(bf16[8,64,512]{2,1,0:T(8,128)(2,1)} %copy-done.21), calls=%async_computation.3 | async-start | bytes 1048576 | tf_op jit(solution)/shard_map/all_to_all | solution.py:212
  113.6 1.7 fusion.2
  116.8 11.5 %all-to-all-done.3 = bf16[8,64,512]{2,1,0:T(8,128)(2,1)S(1)} async-done(((bf16[8,64,512]{2,1,0:T(8,128)(2,1)}), bf16[8,64,512]{2,1,0:T(8,128)(2,1)S(1)}, u32[]{:S(2)}, u32[]{:S(2)}) %all-to-all-start.3) | async-done | bytes 524320 | tf_op jit(solution)/shard_map/all_to_all | solution.py:212
  128.7 9.8 %polynomial.1 = (bf16[1,512,512]{2,1,0:T(8,128)(2,1)S(1)}, bf16[1,512,512]{2,1,0:T(8,128)(2,1)S(1)}) custom-call(f32[1,512,512]{2,1,0:T(8,128)S(1)} %fusion.refs_0_), custom_call_target="tpu_custom_call" | custom-call | flops 7784628224 | bytes 2097152 | tf_op jit(solution)/shard_map/polynomial/pallas_call | solution.py:142
  138.6 1.5 apply.5
  140.1 3.6 %all-to-all-start.5 = ((bf16[8,64,512]{2,1,0:T(8,128)(2,1)}), bf16[8,64,512]{2,1,0:T(8,128)(2,1)S(1)}, u32[]{:S(2)}, u32[]{:S(2)}) async-start(bf16[8,64,512]{2,1,0:T(8,128)(2,1)} %bitcast.21), calls=%async_computation.5 | async-start | bytes 1048576 | tf_op jit(solution)/shard_map/all_to_all | solution.py:212
  143.8 2.5 %apply.6 = bf16[1,512,512]{2,1,0:T(8,128)(2,1)} custom-call(bf16[1,512,512]{2,1,0:T(8,128)(2,1)S(1)} %get-tuple-element.30.high, bf16[1,512,512]{2,1,0:T(8,128)(2,1)S(1)} %get-tuple-element.31.low, bf16[1,512,512]{2,1,0:T(8,128)(2,1)} %bitcast.22.values), custom_call_target="tpu_custom_call" | custom-call | flops 536870912 | bytes 2097152 | tf_op jit(solution)/shard_map/apply/pallas_call | solution.py:163
  146.3 12.1 %all-to-all-done.5.update = bf16[8,64,512]{2,1,0:T(8,128)(2,1)S(1)} async-done(((bf16[8,64,512]{2,1,0:T(8,128)(2,1)}), bf16[8,64,512]{2,1,0:T(8,128)(2,1)S(1)}, u32[]{:S(2)}, u32[]{:S(2)}) %all-to-all-start.5) | async-done | bytes 524320 | tf_op jit(solution)/shard_map/all_to_all | solution.py:212
  158.4 4.1 %all-to-all-start.6 = ((bf16[8,64,512]{2,1,0:T(8,128)(2,1)}), bf16[8,64,512]{2,1,0:T(8,128)(2,1)}, u32[]{:S(2)}, u32[]{:S(2)}) async-start(bf16[8,64,512]{2,1,0:T(8,128)(2,1)} %bitcast.23), calls=%async_computation.6 | async-start | bytes 1048576 | tf_op jit(solution)/shard_map/all_to_all | solution.py:212
  162.6 3.8 %add_convert_fusion.own = bf16[8,64,2048]{2,1,0:T(8,128)(2,1)S(1)} fusion(bf16[8,64,2048]{2,1,0:T(8,128)(2,1)} %collective-permute-done, f32[]{:T(128)S(6)} %sub.12, f32[]{:T(128)} %bitcast.1, bf16[1,8,64,2048]{3,2,1,0:T(8,128)(2,1)} %param.5), kind=kLoop, calls=%fused_computation | loop fusion | flops 6291456 | bytes 6291464 | tf_op jit(solution)/shard_map/convert_element_type | solution.py:263
  166.4 1.6 collective-permute-start.2
  168.7 0.8 copy-done.18
  169.5 7.4 %all-to-all-done.6.update = bf16[8,64,512]{2,1,0:T(8,128)(2,1)} async-done(((bf16[8,64,512]{2,1,0:T(8,128)(2,1)}), bf16[8,64,512]{2,1,0:T(8,128)(2,1)}, u32[]{:S(2)}, u32[]{:S(2)}) %all-to-all-start.6) | async-done | bytes 524320 | tf_op jit(solution)/shard_map/all_to_all | solution.py:212
  176.9 4.1 %all-to-all-start.7 = ((bf16[8,64,512]{2,1,0:T(8,128)(2,1)}), bf16[8,64,512]{2,1,0:T(8,128)(2,1)}, u32[]{:S(2)}, u32[]{:S(2)}) async-start(bf16[8,64,512]{2,1,0:T(8,128)(2,1)} %bitcast.59), calls=%async_computation.7 | async-start | bytes 1048576 | tf_op jit(solution)/shard_map/all_to_all | solution.py:212
  181.0 1.0 copy-done.11
  182.1 1.0 copy-done.14
  184.6 10.6 %all-to-all-done.7.update = bf16[8,64,512]{2,1,0:T(8,128)(2,1)} async-done(((bf16[8,64,512]{2,1,0:T(8,128)(2,1)}), bf16[8,64,512]{2,1,0:T(8,128)(2,1)}, u32[]{:S(2)}, u32[]{:S(2)}) %all-to-all-start.7) | async-done | bytes 524320 | tf_op jit(solution)/shard_map/all_to_all | solution.py:212
  195.2 3.6 %all-to-all-start.4 = ((bf16[8,64,512]{2,1,0:T(8,128)(2,1)}), bf16[8,64,512]{2,1,0:T(8,128)(2,1)S(1)}, u32[]{:S(2)}, u32[]{:S(2)}) async-start(bf16[8,64,512]{2,1,0:T(8,128)(2,1)} %bitcast.58), calls=%async_computation.4 | async-start | bytes 1048576 | tf_op jit(solution)/shard_map/all_to_all | solution.py:212
  198.8 14.5 %collective-permute-done.2.far = bf16[8,64,2048]{2,1,0:T(8,128)(2,1)} collective-permute-done((bf16[8,64,2048]{2,1,0:T(8,128)(2,1)S(1)}, bf16[8,64,2048]{2,1,0:T(8,128)(2,1)}, u32[]{:S(2)}, u32[]{:S(2)}) %collective-permute-start.2) | collective-permute-done | bytes 2097184 | tf_op jit(solution)/shard_map/ppermute | solution.py:26
  213.3 3.5 %settle.4 = (bf16[8,64,2048]{2,1,0:T(8,128)(2,1)}, bf16[8,64,2048]{2,1,0:T(8,128)(2,1)}) custom-call(f32[6]{0:T(128)S(1)} %stack.23.share, bf16[8,64,2048]{2,1,0:T(8,128)(2,1)S(1)} %add_convert_fusion.own, bf16[8,64,2048]{2,1,0:T(8,128)(2,1)} %collective-permute-done.2.far, bf16[8,64,512]{2,1,0:T(8,128)(2,1)} %all-to-all-done.7.update), custom_call_target="tpu_custom_call" | custom-call | flops 2097152 | bytes 2621440 | tf_op jit(solution)/shard_map/settle/pallas_call | solution.py:198
  216.8 3.6 %settle.5 = (bf16[8,64,2048]{2,1,0:T(8,128)(2,1)}, bf16[8,64,2048]{2,1,0:T(8,128)(2,1)}) custom-call(f32[6]{0:T(128)S(1)} %stack.23.share, bf16[8,64,2048]{2,1,0:T(8,128)(2,1)S(1)} %add_convert_fusion.own, bf16[8,64,2048]{2,1,0:T(8,128)(2,1)} %collective-permute-done.2.far, ...), custom_call_target="tpu_custom_call", output_to_operand_aliasing={{0}: (4, {}), {1}: (5, {})} | custom-call | flops 2097152 | bytes 2621440 | tf_op jit(solution)/shard_map/settle/pallas_call | solution.py:198
  220.4 3.4 %settle.6 = (bf16[8,64,2048]{2,1,0:T(8,128)(2,1)}, bf16[8,64,2048]{2,1,0:T(8,128)(2,1)}) custom-call(f32[6]{0:T(128)S(1)} %stack.23.share, bf16[8,64,2048]{2,1,0:T(8,128)(2,1)S(1)} %add_convert_fusion.own, bf16[8,64,2048]{2,1,0:T(8,128)(2,1)} %collective-permute-done.2.far, ...), custom_call_target="tpu_custom_call", output_to_operand_aliasing={{0}: (4, {}), {1}: (5, {})} | custom-call | flops 2097152 | bytes 2621440 | tf_op jit(solution)/shard_map/settle/pallas_call | solution.py:198
  223.8 3.4 %settle.7 = (bf16[8,64,2048]{2,1,0:T(8,128)(2,1)}, bf16[8,64,2048]{2,1,0:T(8,128)(2,1)}) custom-call(f32[6]{0:T(128)S(1)} %stack.23.share, bf16[8,64,2048]{2,1,0:T(8,128)(2,1)S(1)} %add_convert_fusion.own, bf16[8,64,2048]{2,1,0:T(8,128)(2,1)} %collective-permute-done.2.far, ...), custom_call_target="tpu_custom_call", output_to_operand_aliasing={{0}: (4, {}), {1}: (5, {})} | custom-call | flops 2097152 | bytes 2621440 | tf_op jit(solution)/shard_map/settle/pallas_call | solution.py:198
  (59 shorter events, 8.1 us)
Async XLA Ops:
  4.5 29.5 %copy-start.22 = (s32[4,2]{0,1:T(2,128)S(1)}, s32[4,2]{0,1:T(2,128)}, u32[]{:S(2)}) copy-start(s32[4,2]{0,1:T(2,128)} %param.9) | copy-start | bytes 100
  4.5 35.3 %copy-start.3 = (bf16[1,8,64,2048]{3,2,1,0:T(8,128)(2,1)S(1)}, bf16[1,8,64,2048]{3,2,1,0:T(8,128)(2,1)}, u32[]{:S(2)}) copy-start(bf16[1,8,64,2048]{3,2,1,0:T(8,128)(2,1)} %param.7) | copy-start | bytes 6291460
  4.5 35.3 %collective-permute-start.3 = (bf16[8,64,2048]{2,1,0:T(8,128)(2,1)}, bf16[8,64,2048]{2,1,0:T(8,128)(2,1)}, u32[]{:S(2)}, u32[]{:S(2)}) collective-permute-start(bf16[8,64,2048]{2,1,0:T(8,128)(2,1)} %bitcast_convert_fusion), channel_id=1, source_target_pairs={{0,8},{8,0},{16,24},{24,16},{1,9},{9,1},{17,25},{25,17},{2,10},{10... | collective-permute-start | bytes 6291464 | tf_op jit(solution)/shard_map/ppermute | solution.py:26
  7.8 15.2 %collective-permute-start.4 = (bf16[8,64,512]{2,1,0:T(8,128)(2,1)S(1)}, bf16[8,64,512]{2,1,0:T(8,128)(2,1)S(1)}, u32[]{:S(2)}, u32[]{:S(2)}) collective-permute-start(bf16[8,64,512]{2,1,0:T(8,128)(2,1)S(1)} %get-tuple-element.43), channel_id=1, source_target_pairs={{0,16},{8,24},{16,0},{24,8},{1,17},{9,25},{17,1},{25,9},{2,18},{10... | collective-permute-start | bytes 1572872 | tf_op jit(solution)/shard_map/ppermute | solution.py:26
  10.2 23.7 %collective-permute-start.6 = (bf16[8,64,512]{2,1,0:T(8,128)(2,1)S(1)}, bf16[8,64,512]{2,1,0:T(8,128)(2,1)S(1)}, u32[]{:S(2)}, u32[]{:S(2)}) collective-permute-start(bf16[8,64,512]{2,1,0:T(8,128)(2,1)S(1)} %get-tuple-element.42), channel_id=1, source_target_pairs={{0,16},{8,24},{16,0},{24,8},{1,17},{9,25},{17,1},{25,9},{2,18},{10... | collective-permute-start | bytes 1572872 | tf_op jit(solution)/shard_map/ppermute | solution.py:26
  23.0 16.8 %collective-permute-start.5 = (bf16[8,64,512]{2,1,0:T(8,128)(2,1)S(1)}, bf16[8,64,512]{2,1,0:T(8,128)(2,1)}, u32[]{:S(2)}, u32[]{:S(2)}) collective-permute-start(bf16[8,64,512]{2,1,0:T(8,128)(2,1)S(1)} %collective-permute-done.4.far), channel_id=1, source_target_pairs={{0,8},{8,0},{16,24},{24,16},{1,9},{9,1},{17,25},{25,17},{2,10},{10... | collective-permute-start | bytes 1572872 | tf_op jit(solution)/shard_map/ppermute | solution.py:26
  33.9 13.3 %collective-permute-start.7 = (bf16[8,64,512]{2,1,0:T(8,128)(2,1)S(1)}, bf16[8,64,512]{2,1,0:T(8,128)(2,1)}, u32[]{:S(2)}, u32[]{:S(2)}) collective-permute-start(bf16[8,64,512]{2,1,0:T(8,128)(2,1)S(1)} %collective-permute-done.6.far), channel_id=1, source_target_pairs={{0,8},{8,0},{16,24},{24,16},{1,9},{9,1},{17,25},{25,17},{2,10},{10... | collective-permute-start | bytes 1572872 | tf_op jit(solution)/shard_map/ppermute | solution.py:26
  39.8 2.2 copy-start
  42.0 1.6 copy-start.4
  47.2 3.9 %copy-start.19 = (bf16[8,64,512]{2,1,0:T(8,128)(2,1)}, bf16[8,64,512]{2,1,0:T(8,128)(2,1)S(1)}, u32[]{:S(2)}) copy-start(bf16[8,64,512]{2,1,0:T(8,128)(2,1)S(1)} %get-tuple-element.23) | copy-start | bytes 1572868
  51.2 21.3 %all-to-all-start.1 = ((bf16[8,64,512]{2,1,0:T(8,128)(2,1)}), bf16[8,64,512]{2,1,0:T(8,128)(2,1)}, u32[]{:S(2)}, u32[]{:S(2)}) async-start(bf16[8,64,512]{2,1,0:T(8,128)(2,1)} %get-tuple-element.25), calls=%async_computation.1 | async-start | bytes 1048576 | tf_op jit(solution)/shard_map/all_to_all | solution.py:212
  57.3 18.9 %collective-permute-start.8 = (bf16[8,64,512]{2,1,0:T(8,128)(2,1)}, bf16[8,64,512]{2,1,0:T(8,128)(2,1)S(1)}, u32[]{:S(2)}, u32[]{:S(2)}) collective-permute-start(bf16[8,64,512]{2,1,0:T(8,128)(2,1)} %get-tuple-element.41), channel_id=1, source_target_pairs={{0,16},{8,24},{16,0},{24,8},{1,17},{9,25},{17,1},{25,9},{2,18},{10... | collective-permute-start | bytes 1572872 | tf_op jit(solution)/shard_map/ppermute | solution.py:26
  72.5 18.3 %all-to-all-start = ((bf16[8,64,512]{2,1,0:T(8,128)(2,1)}), bf16[8,64,512]{2,1,0:T(8,128)(2,1)S(1)}, u32[]{:S(2)}, u32[]{:S(2)}) async-start(bf16[8,64,512]{2,1,0:T(8,128)(2,1)} %copy-done.19), calls=%async_computation | async-start | bytes 1048576 | tf_op jit(solution)/shard_map/all_to_all | solution.py:212
  76.2 2.0 collective-permute-start.9
  76.2 18.3 %collective-permute-start.1 = (bf16[8,64,512]{2,1,0:T(8,128)(2,1)}, bf16[8,64,512]{2,1,0:T(8,128)(2,1)}, u32[]{:S(2)}, u32[]{:S(2)}) collective-permute-start(bf16[8,64,512]{2,1,0:T(8,128)(2,1)} %get-tuple-element.44), channel_id=1, source_target_pairs={{0,16},{8,24},{16,0},{24,8},{1,17},{9,25},{17,1},{25,9},{2,18},{10... | collective-permute-start | bytes 1572872 | tf_op jit(solution)/shard_map/ppermute | solution.py:26
  78.1 2.2 copy-start.1
  80.3 1.6 copy-start.5
  85.5 0.8 copy-start.20
  90.9 18.3 %all-to-all-start.2 = ((bf16[8,64,512]{2,1,0:T(8,128)(2,1)}), bf16[8,64,512]{2,1,0:T(8,128)(2,1)S(1)}, u32[]{:S(2)}, u32[]{:S(2)}) async-start(bf16[8,64,512]{2,1,0:T(8,128)(2,1)} %copy-done.20), calls=%async_computation.2 | async-start | bytes 1048576 | tf_op jit(solution)/shard_map/all_to_all | solution.py:212
  94.5 2.2 collective-permute-start.10
  96.7 2.2 copy-start.2
  98.9 1.6 copy-start.6
  104.1 0.8 copy-start.21
  109.2 0.8 copy-start.7
  110.0 18.3 %all-to-all-start.3 = ((bf16[8,64,512]{2,1,0:T(8,128)(2,1)}), bf16[8,64,512]{2,1,0:T(8,128)(2,1)S(1)}, u32[]{:S(2)}, u32[]{:S(2)}) async-start(bf16[8,64,512]{2,1,0:T(8,128)(2,1)} %copy-done.21), calls=%async_computation.3 | async-start | bytes 1048576 | tf_op jit(solution)/shard_map/all_to_all | solution.py:212
  113.6 49.0 %collective-permute-start = (bf16[8,64,2048]{2,1,0:T(8,128)(2,1)}, bf16[8,64,2048]{2,1,0:T(8,128)(2,1)}, u32[]{:S(2)}, u32[]{:S(2)}) collective-permute-start(bf16[8,64,2048]{2,1,0:T(8,128)(2,1)} %bitcast.63), channel_id=1, source_target_pairs={{0,8},{8,0},{16,24},{24,16},{1,9},{9,1},{17,25},{25,17},{2,10},{10... | collective-permute-start | bytes 6291464 | tf_op jit(solution)/shard_map/ppermute | solution.py:26
  115.3 1.0 copy-start.8
  138.6 7.7 %copy-start.9 = (bf16[1,512,512]{2,1,0:T(8,128)(2,1)}, bf16[1,512,512]{2,1,0:T(8,128)(2,1)S(1)}, u32[]{:S(2)}) copy-start(bf16[1,512,512]{2,1,0:T(8,128)(2,1)S(1)} %get-tuple-element.30.high) | copy-start | bytes 1572868
  138.6 7.7 %copy-start.12 = (bf16[1,512,512]{2,1,0:T(8,128)(2,1)}, bf16[1,512,512]{2,1,0:T(8,128)(2,1)S(1)}, u32[]{:S(2)}) copy-start(bf16[1,512,512]{2,1,0:T(8,128)(2,1)S(1)} %get-tuple-element.31.low) | copy-start | bytes 1572868
  140.1 18.3 %all-to-all-start.5 = ((bf16[8,64,512]{2,1,0:T(8,128)(2,1)}), bf16[8,64,512]{2,1,0:T(8,128)(2,1)S(1)}, u32[]{:S(2)}, u32[]{:S(2)}) async-start(bf16[8,64,512]{2,1,0:T(8,128)(2,1)} %bitcast.21), calls=%async_computation.5 | async-start | bytes 1048576 | tf_op jit(solution)/shard_map/all_to_all | solution.py:212
  158.4 4.2 %copy-start.15 = (bf16[8,64,512]{2,1,0:T(8,128)(2,1)}, bf16[8,64,512]{2,1,0:T(8,128)(2,1)S(1)}, u32[]{:S(2)}) copy-start(bf16[8,64,512]{2,1,0:T(8,128)(2,1)S(1)} %all-to-all-done.5.update) | copy-start | bytes 1572868
  158.4 18.4 %all-to-all-start.6 = ((bf16[8,64,512]{2,1,0:T(8,128)(2,1)}), bf16[8,64,512]{2,1,0:T(8,128)(2,1)}, u32[]{:S(2)}, u32[]{:S(2)}) async-start(bf16[8,64,512]{2,1,0:T(8,128)(2,1)} %bitcast.23), calls=%async_computation.6 | async-start | bytes 1048576 | tf_op jit(solution)/shard_map/all_to_all | solution.py:212
  162.6 5.4 %copy-start.10 = (bf16[1,512,512]{2,1,0:T(8,128)(2,1)S(1)}, bf16[1,512,512]{2,1,0:T(8,128)(2,1)}, u32[]{:S(2)}) copy-start(bf16[1,512,512]{2,1,0:T(8,128)(2,1)} %copy-done.9) | copy-start | bytes 1572868
  162.6 5.4 %copy-start.13 = (bf16[1,512,512]{2,1,0:T(8,128)(2,1)S(1)}, bf16[1,512,512]{2,1,0:T(8,128)(2,1)}, u32[]{:S(2)}) copy-start(bf16[1,512,512]{2,1,0:T(8,128)(2,1)} %copy-done.12) | copy-start | bytes 1572868
  166.4 46.9 %collective-permute-start.2 = (bf16[8,64,2048]{2,1,0:T(8,128)(2,1)S(1)}, bf16[8,64,2048]{2,1,0:T(8,128)(2,1)}, u32[]{:S(2)}, u32[]{:S(2)}) collective-permute-start(bf16[8,64,2048]{2,1,0:T(8,128)(2,1)S(1)} %add_convert_fusion.own), channel_id=1, source_target_pairs={{0,16},{8,24},{16,0},{24,8},{1,17},{9,25},{17,1},{25,9},{2,18},{10... | collective-permute-start | bytes 6291464 | tf_op jit(solution)/shard_map/ppermute | solution.py:26
  168.7 0.8 copy-start.18
  176.9 18.3 %all-to-all-start.7 = ((bf16[8,64,512]{2,1,0:T(8,128)(2,1)}), bf16[8,64,512]{2,1,0:T(8,128)(2,1)}, u32[]{:S(2)}, u32[]{:S(2)}) async-start(bf16[8,64,512]{2,1,0:T(8,128)(2,1)} %bitcast.59), calls=%async_computation.7 | async-start | bytes 1048576 | tf_op jit(solution)/shard_map/all_to_all | solution.py:212
  181.0 1.0 copy-start.11
  182.1 1.0 copy-start.14
  183.8 0.8 copy-start.17
  195.2 28.6 %all-to-all-start.4 = ((bf16[8,64,512]{2,1,0:T(8,128)(2,1)}), bf16[8,64,512]{2,1,0:T(8,128)(2,1)S(1)}, u32[]{:S(2)}, u32[]{:S(2)}) async-start(bf16[8,64,512]{2,1,0:T(8,128)(2,1)} %bitcast.58), calls=%async_computation.4 | async-start | bytes 1048576 | tf_op jit(solution)/shard_map/all_to_all | solution.py:212
  216.8 3.6 %copy-start.16 = (bf16[8,64,512]{2,1,0:T(8,128)(2,1)S(1)}, bf16[8,64,512]{2,1,0:T(8,128)(2,1)}, u32[]{:S(2)}) copy-start(bf16[8,64,512]{2,1,0:T(8,128)(2,1)} %copy-done.15) | copy-start | bytes 1572868

commit v2 on v0

v2 whole, which is shorter than its diff:
```python
import math

import jax
import jax.numpy as jnp
from jax import lax
from jax.experimental import pallas as pl
from jax.experimental.pallas import tpu as pltpu
from jax.sharding import PartitionSpec as P

NS_STEPS = 5

coeff_a = 3.4445
coeff_b = -4.775
coeff_c = 2.0315
learn_rate = 0.05

F32 = jnp.float32
BF16 = jnp.bfloat16
MIB = 1 << 20


def swapped(values, axis, offset):
    return lax.ppermute(values, axis, [(i, i ^ offset) for i in range(lax.axis_size(axis))])


def cost(flops, moved):
    return pl.CostEstimate(flops=int(flops), bytes_accessed=int(moved), transcendentals=0)


def params(mib):
    return pltpu.CompilerParams(vmem_limit_bytes=mib * MIB)


def split(values):
    high = values.astype(BF16)
    return high, (values - high.astype(F32)).astype(BF16)


def times(left, right):
    return jnp.dot(left, right, preferred_element_type=F32)


def orthogonalize_body(scale, count, *refs):
    blocks, outs = refs[:count], refs[count : 2 * count]
    held, gram_held, poly_held = refs[2 * count :]
    rows = blocks[0].shape[1]
    for place, block in enumerate(blocks):
        held[pl.ds(place * rows, rows), :] = block[0]
    size = held.shape[0]
    gram = lax.dot_general(
        held[...], held[...], (((1,), (1,)), ((), ())), preferred_element_type=F32
    )
    on_diagonal = lax.broadcasted_iota(jnp.int32, (size, size), 0) == lax.broadcasted_iota(
        jnp.int32, (size, size), 1
    )
    square_norm = jnp.sum(
        jnp.sum(jnp.where(on_diagonal, gram, 0.0), axis=0, keepdims=True), axis=1, keepdims=True
    )
    inverse = 1.0 / (jnp.sqrt(square_norm) + 1e-07)
    gram_held[...] = gram * inverse * inverse
    poly_held[...] = jnp.where(on_diagonal, 1.0, 0.0)

    def step(last):
        gram = gram_held[...]
        gram_high, gram_low = split(gram)
        shift = (
            coeff_b * gram_high.astype(F32) + coeff_c * times(gram_high, gram_high)
        ).astype(BF16)
        poly = poly_held[...]
        poly_high, poly_low = split(poly)
        poly_held[...] = coeff_a * poly + times(shift, poly_high) + times(shift, poly_low)
        if not last:
            half = coeff_a * gram + times(shift, gram_high) + times(shift, gram_low)
            half_high, half_low = split(half)
            gram_held[...] = coeff_a * half + times(half_high, shift) + times(half_low, shift)

    @pl.loop(0, NS_STEPS - 1)
    def _(_):
        step(False)

    step(True)
    high, low = split(poly_held[...] * (scale * inverse))
    update = (times(high, held[...]) + times(low, held[...])).astype(BF16)
    for place, out in enumerate(outs):
        out[0] = update[place * rows : (place + 1) * rows]


def orthogonalize(blocks, scale):
    count = len(blocks)
    each, rows, columns = blocks[0].shape
    size = count * rows
    block = pl.BlockSpec((1, rows, columns), lambda i: (i, 0, 0))
    flops = 2 * each * size * size * (29 * size + 3 * columns)

    def body(*refs):
        orthogonalize_body(scale, count, *refs)

    return pl.pallas_call(
        body,
        grid=(each,),
        in_specs=[block] * count,
        out_specs=[block] * count,
        out_shape=[jax.ShapeDtypeStruct(blocks[0].shape, BF16)] * count,
        scratch_shapes=[
            pltpu.VMEM((size, columns), BF16),
            pltpu.VMEM((size, size), F32),
            pltpu.VMEM((size, size), F32),
        ],
        compiler_params=params(40),
        cost_estimate=cost(flops, 4 * each * size * columns),
        name="orthogonalize",
    )(*blocks)


def grouped(shards):
    groups = []
    top = shards
    for length in (shards // 8, shards // 8, shards // 4, shards // 2):
        if length:
            top -= length
            groups.append((top, length))
    return groups if top == 0 else [(0, shards)]


def local(weight, tracker, grad_new, grad_old, mix_keep):
    shards = lax.axis_size("shard")
    _, experts, rows, columns = tracker.shape
    each = experts // shards
    shape = (shards, each, rows, columns)
    weight, tracker, grad_new, grad_old = (
        values.reshape(shape) for values in (weight, tracker, grad_new, grad_old)
    )
    here = lax.axis_index("shard")
    rep_index = lax.axis_index("rep")
    keep = mix_keep.astype(F32) / 16.0
    first, second = keep[rep_index, 0], keep[rep_index, 1]

    def taken(values, start, length):
        return lax.dynamic_slice_in_dim(values, start, length, axis=0)

    new_tracker = jnp.zeros(shape, F32)
    blocks = [None] * shards
    far = None
    for lowest, length in grouped(shards):
        start = (here ^ lowest) // length * length
        own = taken(tracker, start, length)
        near = swapped(own.astype(BF16), "rep", 1)
        mixed = first * own + (1.0 - first) * near.astype(F32)
        far = swapped(mixed.astype(BF16), "rep", 2)
        group = second * mixed + (1.0 - second) * far.astype(F32)
        group += taken(grad_new, start, length).astype(F32)
        group -= taken(grad_old, start, length).astype(F32)
        for offset in reversed(range(lowest, lowest + length)):
            block = taken(group, (here ^ offset) % length, 1)[0].astype(BF16)
            blocks[offset] = swapped(block, "shard", offset) if offset else block
        new_tracker = lax.dynamic_update_slice_in_dim(new_tracker, group, start, axis=0)

    weight_near = swapped(weight, "rep", 1)
    weight_own = (
        first * weight.astype(F32) + (1.0 - first) * weight_near.astype(F32)
    ).astype(BF16)
    weight_own, _ = lax.optimization_barrier((weight_own, far))
    weight_far = swapped(weight_own, "rep", 2)
    mixed_weight = (
        second * weight_own.astype(F32) + (1.0 - second) * weight_far.astype(F32)
    ).astype(BF16)

    scale = 0.2 * math.sqrt(max(shards * rows, columns))
    updates = orthogonalize(blocks, scale)
    update = jnp.zeros(shape, BF16)
    new_weight = jnp.zeros(shape, BF16)
    for offset in reversed(range(shards)):
        block = updates[offset]
        block = swapped(block, "shard", offset) if offset else block
        place = here ^ offset
        kept = taken(mixed_weight, place, 1)[0]
        settled = (kept.astype(F32) - learn_rate * block.astype(F32)).astype(BF16)
        update = lax.dynamic_update_slice_in_dim(update, block[None], place, axis=0)
        new_weight = lax.dynamic_update_slice_in_dim(new_weight, settled[None], place, axis=0)
    shape = (1, experts, rows, columns)
    return new_weight.reshape(shape), new_tracker.reshape(shape), update.reshape(shape)


def solution(mesh):
    spec = P("rep", None, "shard", None)
    return jax.shard_map(
        local,
        mesh=mesh,
        in_specs=(spec, spec, spec, spec, P()),
        out_specs=(spec, spec, spec),
        check_vma=False,
    )
```

time: 244 us -> 159 us (0.65)
  waiting for transfers between devices: 138 us -> 57.5 us
  starting transfers between devices: 15.4 us -> 51.8 us
  matrix products: 29.8 us -> 0 us
  Pallas kernels: 0 us -> 13.4 us
  other arithmetic: 35.3 us -> 23.3 us
  local copies, waits for them, and re-layouts: 21.6 us -> 10.8 us
    all_to_all x2 -> x0, waiting for transfers between devices: 90.9 us -> none  [the longest x1 47.7 us: local(): lax.all_to_all(packed, 'shard', split_axis=0, concat_axis=2, tiled=True)]
    ppermute x4 -> x24, starting transfers between devices: 4.94 us -> 51.8 us  [swapped(): lax.ppermute(values, axis, [(i, i ^ offset) for i in range(lax.axis_size(...]
    dot_general x10 -> x0, matrix products: 29.8 us -> none  [the longest x5 16.5 us: orthogonalize(): jnp.einsum('kmp,kpn->kmn', polynomial, iterate, preferred_element_type=jn...]
    unnamed x20 -> x16, local copies, waits for them, and re-layouts: 15.9 us -> 2.03 us
    pallas_call x0 -> x1, Pallas kernels: none -> 13.4 us  [orthogonalize(): pl.pallas_call(body, grid=(each,), in_specs=[block] * count, out_specs=[b...]
    unnamed x1 -> x0, other arithmetic: 13.2 us -> none
    ppermute x4 -> x24, waiting for transfers between devices: 46.7 us -> 57.5 us  [swapped(): lax.ppermute(values, axis, [(i, i ^ offset) for i in range(lax.axis_size(...]
    all_to_all x2 -> x0, starting transfers between devices: 10.4 us -> none  [the longest x1 6.08 us: local(): lax.all_to_all(packed, 'shard', split_axis=0, concat_axis=2, tiled=True)]
  transfers between devices with their start and end apart: 6 -> 24, of which waited for: 4 -> 14; matrix products, arithmetic and copies ran while one was open for 28% -> 19% of each run, Pallas kernels for 0% -> 8%
where the time goes in v2:
time: 159 us
  waiting for transfers between devices  57.5 us (36%)
  starting transfers between devices  51.8 us (33%)
  other arithmetic  23.3 us (15%)
  Pallas kernels  13.4 us (8%)
  local copies, waits for them, and re-layouts  10.8 us (7%)
  between operations  2.23 us (1%)
    ppermute x24, waiting for transfers between devices, swapped(): lax.ppermute(values, axis, [(i, i ^ offset) for i in range(lax.axis_size(...  57.5 us
    ppermute x24, starting transfers between devices, swapped(): lax.ppermute(values, axis, [(i, i ^ offset) for i in range(lax.axis_size(...  51.8 us
    pallas_call x1, Pallas kernels, orthogonalize(): pl.pallas_call(body, grid=(each,), in_specs=[block] * count, out_specs=[b...  13.4 us
    dynamic_update_slice x4, other arithmetic, local(): lax.dynamic_update_slice_in_dim(new_tracker, group, start, axis=0)  8.96 us
    convert_element_type x3, local copies, waits for them, and re-layouts, local(): near = swapped(own.astype(BF16), 'rep', 1)  7.01 us
    convert_element_type x3, other arithmetic, local(): far = swapped(mixed.astype(BF16), 'rep', 2)  5.51 us
    convert_element_type x1, other arithmetic, local(): weight_own = (first * weight.astype(F32) + (1.0 - first) * weight_near.as...  4.42 us
    convert_element_type x1, other arithmetic, local(): mixed_weight = (second * weight_own.astype(F32) + (1.0 - second) * weight...  3.7 us
  transfers between devices with their start and end apart: 24, of which 14 were waited for; matrix products, arithmetic and copies ran while one was open for 19% of the time, Pallas kernels for 8%

profile of v2, /device:TPU:0, one launch (start us, length us, event | category | flops | bytes accessed | tf_op | source)
XLA Modules:
  0.0 159.0 jit_solution(2246958734872727663)
XLA Ops:
  0.7 2.2 %dynamic-slice_convert_fusion.9 = (bf16[1,1,64,2048]{3,2,1,0:T(8,128)(2,1)}, bf16[1,1,64,2048]{3,2,1,0:T(8,128)(2,1)}) fusion(f32[1,8,64,2048]{3,2,1,0:T(8,128)} %param.6, s32[]{:T(128)S(6)} %select_n.142, s32[]{:T(128)S(6)} %select_n.127), kind=kLoop, calls=%fused_computation.43 | loop fusion | bytes 1048584 | tf_op jit(solution)/shard_map/convert_element_type | solution.py:147
  2.9 0.5 collective-permute-start.11
  3.4 2.1 %fusion.3 = bf16[2,1,64,2048]{3,2,1,0:T(8,128)(2,1)} fusion(f32[1,8,64,2048]{3,2,1,0:T(8,128)} %param.6, s32[]{:T(128)S(6)} %select_n.137), kind=kLoop, calls=%fused_computation.15 | loop fusion | bytes 1048580 | tf_op jit(solution)/shard_map/convert_element_type | solution.py:147
  5.5 0.5 collective-permute-start.7
  5.9 2.7 %fusion.1 = bf16[4,1,64,2048]{3,2,1,0:T(8,128)(2,1)} fusion(f32[1,8,64,2048]{3,2,1,0:T(8,128)} %param.6, s32[]{:T(128)S(6)} %select_n.126), kind=kLoop, calls=%fused_computation.8 | loop fusion | bytes 2097156 | tf_op jit(solution)/shard_map/convert_element_type | solution.py:147
  8.7 0.5 collective-permute-start
  9.2 0.6 constant_dynamic-slice_fusion.1
  11.1 2.2 %fusion.12 = (bf16[1,1,64,2048]{3,2,1,0:T(8,128)(2,1)S(1)}, bf16[1,1,64,2048]{3,2,1,0:T(8,128)(2,1)S(1)}) fusion(bf16[1,1,64,2048]{3,2,1,0:T(8,128)(2,1)S(1)} %collective-permute-done.11, f32[1,8,64,2048]{3,2,1,0:T(8,128)} %param.6, s32[]{:T(128)S(6)} %select_n.142, f32[]{:T(128)S(6)} %sub.59, f32[]{:T(128)} %bitcast.1, ...), kind=kLoop, calls=%fused_computation.44 | loop fusion | flops 1310720 | bytes 2097168 | tf_op jit(solution)/shard_map/convert_element_type | solution.py:149
  13.3 2.7 %collective-permute-start.15 = (bf16[1,1,64,2048]{3,2,1,0:T(8,128)(2,1)S(1)}, bf16[1,1,64,2048]{3,2,1,0:T(8,128)(2,1)S(1)}, u32[]{:S(2)}, u32[]{:S(2)}) collective-permute-start(bf16[1,1,64,2048]{3,2,1,0:T(8,128)(2,1)S(1)} %get-tuple-element.30), channel_id=1, source_target_pairs={{0,16},{8,24},{16,0},{24,8},{1,17},{9,25},{17,1},{25,9},{2,18},{10... | collective-permute-start | bytes 786440 | tf_op jit(solution)/shard_map/ppermute | solution.py:23
  16.1 2.3 %fusion.2 = bf16[2,1,64,2048]{3,2,1,0:T(8,128)(2,1)S(1)} fusion(bf16[2,1,64,2048]{3,2,1,0:T(8,128)(2,1)} %collective-permute-done.7, f32[1,8,64,2048]{3,2,1,0:T(8,128)} %param.6, s32[]{:T(128)S(6)} %select_n.137, f32[]{:T(128)S(6)} %sub.59, f32[]{:T(128)} %bitcast.1), kind=kLoop, calls=%fused_computation.14 | loop fusion | flops 1310720 | bytes 2097164 | tf_op jit(solution)/shard_map/convert_element_type | solution.py:149
  18.5 2.0 %collective-permute-start.8 = (bf16[2,1,64,2048]{3,2,1,0:T(8,128)(2,1)S(1)}, bf16[2,1,64,2048]{3,2,1,0:T(8,128)(2,1)S(1)}, u32[]{:S(2)}, u32[]{:S(2)}) collective-permute-start(bf16[2,1,64,2048]{3,2,1,0:T(8,128)(2,1)S(1)} %fusion.2), channel_id=1, source_target_pairs={{0,16},{8,24},{16,0},{24,8},{1,17},{9,25},{17,1},{25,9},{2,18},{10... | collective-permute-start | bytes 1572872 | tf_op jit(solution)/shard_map/ppermute | solution.py:23
  20.5 2.7 %collective-permute-done.15 = bf16[1,1,64,2048]{3,2,1,0:T(8,128)(2,1)S(1)} collective-permute-done((bf16[1,1,64,2048]{3,2,1,0:T(8,128)(2,1)S(1)}, bf16[1,1,64,2048]{3,2,1,0:T(8,128)(2,1)S(1)}, u32[]{:S(2)}, u32[]{:S(2)}) %collective-permute-start.15) | collective-permute-done | bytes 262176 | tf_op jit(solution)/shard_map/ppermute | solution.py:23
  23.2 0.5 reshape.427
  23.7 2.4 %constant_dynamic-update-slice_fusion.1 = (f32[1,8,64,2048]{3,2,1,0:T(8,128)S(1)}, bf16[1,1,64,2048]{3,2,1,0:T(8,128)(2,1)S(1)}) fusion(f32[1,8,64,2048]{3,2,1,0:T(8,128)S(1)} %reshape.427, s32[]{:T(128)S(6)} %select_n.127, bf16[1,8,64,2048]{3,2,1,0:T(8,128)(2,1)S(1)} %copy-done.5, bf16[1,8,64,2048]{3,2,1,0:T(8,128)(2,1)S(1)} %copy-done.6, ...), kind=kLoop, calls=%fused_computation.79 | loop fusion | flops 1703936 | bytes 2359316 | tf_op jit(solution)/shard_map/dynamic_update_slice | solution.py:156
  26.1 2.7 %collective-permute-done.12 = bf16[1,1,64,2048]{3,2,1,0:T(8,128)(2,1)S(1)} collective-permute-done((bf16[1,1,64,2048]{3,2,1,0:T(8,128)(2,1)S(1)}, bf16[1,1,64,2048]{3,2,1,0:T(8,128)(2,1)S(1)}, u32[]{:S(2)}, u32[]{:S(2)}) %collective-permute-start.12) | collective-permute-done | bytes 262176 | tf_op jit(solution)/shard_map/ppermute | solution.py:23
  28.8 1.5 constant_dynamic-update-slice_fusion
  30.3 4.2 %collective-permute-start.13 = (bf16[1,64,2048]{2,1,0:T(8,128)(2,1)S(1)}, bf16[1,64,2048]{2,1,0:T(8,128)(2,1)S(1)}, u32[]{:S(2)}, u32[]{:S(2)}) collective-permute-start(bf16[1,64,2048]{2,1,0:T(8,128)(2,1)S(1)} %bitcast.138), channel_id=1, source_target_pairs={{0,6},{1,7},{2,4},{3,5},{4,2},{5,3},{6,0},{7,1},{8,14},{9,15},{10,... | collective-permute-start | bytes 786440 | tf_op jit(solution)/shard_map/ppermute | solution.py:23
  34.4 1.2 collective-permute-start.16
  35.6 1.0 fusion
  36.6 1.6 collective-permute-start.2
  38.1 1.9 %collective-permute-done.8 = bf16[2,1,64,2048]{3,2,1,0:T(8,128)(2,1)S(1)} collective-permute-done((bf16[2,1,64,2048]{3,2,1,0:T(8,128)(2,1)S(1)}, bf16[2,1,64,2048]{3,2,1,0:T(8,128)(2,1)S(1)}, u32[]{:S(2)}, u32[]{:S(2)}) %collective-permute-start.8) | collective-permute-done | bytes 524320 | tf_op jit(solution)/shard_map/ppermute | solution.py:23
  40.0 2.8 %bitcast_dynamic-update-slice_fusion.1 = (f32[1,8,64,2048]{3,2,1,0:T(8,128)S(1)}, bf16[2,1,64,2048]{3,2,1,0:T(8,128)(2,1)S(1)}) fusion(f32[1,8,64,2048]{3,2,1,0:T(8,128)S(1)} %get-tuple-element.25, s32[]{:T(128)S(6)} %select_n.137, bf16[1,8,64,2048]{3,2,1,0:T(8,128)(2,1)S(1)} %copy-done.5, bf16[1,8,64,2048]{3,2,1,0:T(8,128)(2,1)S(1)} %copy-done.6, ...), kind=kLoop, calls=%fused_computation.12 | loop fusion | flops 3407872 | bytes 4718612 | tf_op jit(solution)/shard_map/dynamic_update_slice | solution.py:156
  42.8 4.1 %collective-permute-start.10 = (bf16[1,64,2048]{2,1,0:T(8,128)(2,1)S(1)}, bf16[1,64,2048]{2,1,0:T(8,128)(2,1)S(1)}, u32[]{:S(2)}, u32[]{:S(2)}) collective-permute-start(bf16[1,64,2048]{2,1,0:T(8,128)(2,1)S(1)} %get-tuple-element.37), channel_id=1, source_target_pairs={{0,5},{1,4},{2,7},{3,6},{4,1},{5,0},{6,3},{7,2},{8,13},{9,12},{10,... | collective-permute-start | bytes 786440 | tf_op jit(solution)/shard_map/ppermute | solution.py:23
  47.3 4.4 %add_convert_fusion.1 = bf16[8,1,64,2048]{3,2,1,0:T(8,128)(2,1)} fusion(bf16[8,1,64,2048]{3,2,1,0:T(8,128)(2,1)} %collective-permute-done, f32[]{:T(128)S(6)} %sub.59, f32[]{:T(128)} %bitcast.1, bf16[1,8,64,2048]{3,2,1,0:T(8,128)(2,1)S(1)} %copy-done.4), kind=kLoop, calls=%fused_computation.1 | loop fusion | flops 6291456 | bytes 6291464 | tf_op jit(solution)/shard_map/convert_element_type | solution.py:161
  51.7 10.5 %collective-permute-done.2 = bf16[4,1,64,2048]{3,2,1,0:T(8,128)(2,1)S(1)} collective-permute-done((bf16[4,1,64,2048]{3,2,1,0:T(8,128)(2,1)S(1)}, bf16[4,1,64,2048]{3,2,1,0:T(8,128)(2,1)S(1)}, u32[]{:S(2)}, u32[]{:S(2)}) %collective-permute-start.2) | collective-permute-done | bytes 1048608 | tf_op jit(solution)/shard_map/ppermute | solution.py:23
  62.2 1.7 %collective-permute-start.3 = (bf16[8,1,64,2048]{3,2,1,0:T(8,128)(2,1)}, bf16[8,1,64,2048]{3,2,1,0:T(8,128)(2,1)}, u32[]{:S(2)}, u32[]{:S(2)}) collective-permute-start(bf16[8,1,64,2048]{3,2,1,0:T(8,128)(2,1)} %add_convert_fusion.1), channel_id=1, source_target_pairs={{0,16},{8,24},{16,0},{24,8},{1,17},{9,25},{17,1},{25,9},{2,18},{10... | collective-permute-start | bytes 6291464 | tf_op jit(solution)/shard_map/ppermute | solution.py:23
  63.9 2.3 %bitcast_dynamic-update-slice_fusion = (f32[1,8,64,2048]{3,2,1,0:T(8,128)S(1)}, bf16[4,1,64,2048]{3,2,1,0:T(8,128)(2,1)S(1)}) fusion(f32[1,8,64,2048]{3,2,1,0:T(8,128)S(1)} %get-tuple-element.23, s32[]{:T(128)S(6)} %select_n.126, bf16[1,8,64,2048]{3,2,1,0:T(8,128)(2,1)S(1)} %copy-done.5, bf16[1,8,64,2048]{3,2,1,0:T(8,128)(2,1)S(1)} %copy-done.6, ...), kind=kLoop, calls=%fused_computation.5 | loop fusion | flops 6815744 | bytes 9437204 | tf_op jit(solution)/shard_map/dynamic_update_slice | solution.py:156
  66.3 1.6 collective-permute-start.4
  67.9 1.7 %collective-permute-start.5 = (bf16[1,64,2048]{2,1,0:T(8,128)(2,1)S(1)}, bf16[1,64,2048]{2,1,0:T(8,128)(2,1)S(1)}, u32[]{:S(2)}, u32[]{:S(2)}) collective-permute-start(bf16[1,64,2048]{2,1,0:T(8,128)(2,1)S(1)} %get-tuple-element.34), channel_id=1, source_target_pairs={{0,2},{1,3},{2,0},{3,1},{4,6},{5,7},{6,4},{7,5},{8,10},{9,11},{10,... | collective-permute-start | bytes 786440 | tf_op jit(solution)/shard_map/ppermute | solution.py:23
  69.6 5.2 %collective-permute-done.10.refs_5_ = bf16[1,64,2048]{2,1,0:T(8,128)(2,1)S(1)} collective-permute-done((bf16[1,64,2048]{2,1,0:T(8,128)(2,1)S(1)}, bf16[1,64,2048]{2,1,0:T(8,128)(2,1)S(1)}, u32[]{:S(2)}, u32[]{:S(2)}) %collective-permute-start.10) | collective-permute-done | bytes 262176 | tf_op jit(solution)/shard_map/ppermute | solution.py:23
  74.8 0.6 collective-permute-start.6
  75.4 3.0 %collective-permute-done.9.refs_4_ = bf16[1,64,2048]{2,1,0:T(8,128)(2,1)S(1)} collective-permute-done((bf16[1,64,2048]{2,1,0:T(8,128)(2,1)S(1)}, bf16[1,64,2048]{2,1,0:T(8,128)(2,1)S(1)}, u32[]{:S(2)}, u32[]{:S(2)}) %collective-permute-start.9) | collective-permute-done | bytes 262176 | tf_op jit(solution)/shard_map/ppermute | solution.py:23
  78.9 5.2 %collective-permute-done.5.refs_2_ = bf16[1,64,2048]{2,1,0:T(8,128)(2,1)S(1)} collective-permute-done((bf16[1,64,2048]{2,1,0:T(8,128)(2,1)S(1)}, bf16[1,64,2048]{2,1,0:T(8,128)(2,1)S(1)}, u32[]{:S(2)}, u32[]{:S(2)}) %collective-permute-start.5) | collective-permute-done | bytes 262176 | tf_op jit(solution)/shard_map/ppermute | solution.py:23
  84.1 6.5 %collective-permute-done.6.refs_3_ = bf16[1,64,2048]{2,1,0:T(8,128)(2,1)S(1)} collective-permute-done((bf16[1,64,2048]{2,1,0:T(8,128)(2,1)S(1)}, bf16[1,64,2048]{2,1,0:T(8,128)(2,1)S(1)}, u32[]{:S(2)}, u32[]{:S(2)}) %collective-permute-start.6) | collective-permute-done | bytes 262176 | tf_op jit(solution)/shard_map/ppermute | solution.py:23
  90.5 13.4 %orthogonalize.1 = (bf16[1,64,2048]{2,1,0:T(8,128)(2,1)S(1)}, bf16[1,64,2048]{2,1,0:T(8,128)(2,1)S(1)}, bf16[1,64,2048]{2,1,0:T(8,128)(2,1)S(1)}, bf16[1,64,2048...) custom-call(bf16[1,64,2048]{2,1,0:T(8,128)(2,1)S(1)} %get-tuple-elem, ...), custom_call_target="tpu_custom_call" | custom-call | flops 11005853696 | bytes 4194304 | tf_op jit(solution)/shard_map/orthogonalize/pallas_call | solution.py:98
  103.9 2.5 %collective-permute-start.17 = (bf16[1,64,2048]{2,1,0:T(8,128)(2,1)S(1)}, bf16[1,64,2048]{2,1,0:T(8,128)(2,1)S(1)}, u32[]{:S(2)}, u32[]{:S(2)}) collective-permute-start(bf16[1,64,2048]{2,1,0:T(8,128)(2,1)S(1)} %get-tuple-element.13), channel_id=1, source_target_pairs={{0,7},{1,6},{2,5},{3,4},{4,3},{5,2},{6,1},{7,0},{8,15},{9,14},{10,... | collective-permute-start | bytes 786440 | tf_op jit(solution)/shard_map/ppermute | solution.py:23
  106.4 1.3 collective-permute-start.18
  107.8 3.9 %collective-permute-start.20 = (bf16[1,64,2048]{2,1,0:T(8,128)(2,1)S(1)}, bf16[1,64,2048]{2,1,0:T(8,128)(2,1)S(1)}, u32[]{:S(2)}, u32[]{:S(2)}) collective-permute-start(bf16[1,64,2048]{2,1,0:T(8,128)(2,1)S(1)} %get-tuple-element.16), channel_id=1, source_target_pairs={{0,4},{1,5},{2,6},{3,7},{4,0},{5,1},{6,2},{7,3},{8,12},{9,13},{10,... | collective-permute-start | bytes 786440 | tf_op jit(solution)/shard_map/ppermute | solution.py:23
  111.6 4.3 %collective-permute-done.17 = bf16[1,64,2048]{2,1,0:T(8,128)(2,1)S(1)} collective-permute-done((bf16[1,64,2048]{2,1,0:T(8,128)(2,1)S(1)}, bf16[1,64,2048]{2,1,0:T(8,128)(2,1)S(1)}, u32[]{:S(2)}, u32[]{:S(2)}) %collective-permute-start.17) | collective-permute-done | bytes 262176 | tf_op jit(solution)/shard_map/ppermute | solution.py:23
  115.9 20.1 %collective-permute-start.21 = (bf16[1,64,2048]{2,1,0:T(8,128)(2,1)S(1)}, bf16[1,64,2048]{2,1,0:T(8,128)(2,1)S(1)}, u32[]{:S(2)}, u32[]{:S(2)}) collective-permute-start(bf16[1,64,2048]{2,1,0:T(8,128)(2,1)S(1)} %get-tuple-element.17), channel_id=1, source_target_pairs={{0,3},{1,2},{2,1},{3,0},{4,7},{5,6},{6,5},{7,4},{8,11},{9,10},{10,... | collective-permute-start | bytes 786440 | tf_op jit(solution)/shard_map/ppermute | solution.py:23
  136.4 3.7 %add_convert_fusion = bf16[8,1,64,2048]{3,2,1,0:T(8,128)(2,1)S(1)} fusion(bf16[8,1,64,2048]{3,2,1,0:T(8,128)(2,1)} %collective-permute-done.3, bf16[8,1,64,2048]{3,2,1,0:T(8,128)(2,1)} %add_convert_fusion.1, f32[]{:T(128)S(6)} %sub.61, f32[]{:T(128)} %bitcast), kind=kLoop, calls=%fused_computation | loop fusion | flops 6291456 | bytes 6291464 | tf_op jit(solution)/shard_map/convert_element_type | solution.py:166
  140.5 0.6 collective-permute-start.23
  141.2 4.7 %collective-permute-done.19 = bf16[1,64,2048]{2,1,0:T(8,128)(2,1)S(1)} collective-permute-done((bf16[1,64,2048]{2,1,0:T(8,128)(2,1)S(1)}, bf16[1,64,2048]{2,1,0:T(8,128)(2,1)S(1)}, u32[]{:S(2)}, u32[]{:S(2)}) %collective-permute-start.19) | collective-permute-done | bytes 262176 | tf_op jit(solution)/shard_map/ppermute | solution.py:23
  146.0 4.6 %collective-permute-done.20 = bf16[1,64,2048]{2,1,0:T(8,128)(2,1)S(1)} collective-permute-done((bf16[1,64,2048]{2,1,0:T(8,128)(2,1)S(1)}, bf16[1,64,2048]{2,1,0:T(8,128)(2,1)S(1)}, u32[]{:S(2)}, u32[]{:S(2)}) %collective-permute-start.20) | collective-permute-done | bytes 262176 | tf_op jit(solution)/shard_map/ppermute | solution.py:23
  150.7 3.8 %collective-permute-done.21 = bf16[1,64,2048]{2,1,0:T(8,128)(2,1)S(1)} collective-permute-done((bf16[1,64,2048]{2,1,0:T(8,128)(2,1)S(1)}, bf16[1,64,2048]{2,1,0:T(8,128)(2,1)S(1)}, u32[]{:S(2)}, u32[]{:S(2)}) %collective-permute-start.21) | collective-permute-done | bytes 262176 | tf_op jit(solution)/shard_map/ppermute | solution.py:23
  154.7 2.0 %collective-permute-done.22 = bf16[1,64,2048]{2,1,0:T(8,128)(2,1)S(1)} collective-permute-done((bf16[1,64,2048]{2,1,0:T(8,128)(2,1)S(1)}, bf16[1,64,2048]{2,1,0:T(8,128)(2,1)S(1)}, u32[]{:S(2)}, u32[]{:S(2)}) %collective-permute-start.22) | collective-permute-done | bytes 262176 | tf_op jit(solution)/shard_map/ppermute | solution.py:23
  157.0 1.3 copy-done.2
  158.3 0.7 copy-done.3
  (45 shorter events, 2.5 us)
Async XLA Ops:
  0.6 8.1 %copy-start.4 = (bf16[1,8,64,2048]{3,2,1,0:T(8,128)(2,1)S(1)}, bf16[1,8,64,2048]{3,2,1,0:T(8,128)(2,1)}, u32[]{:S(2)}) copy-start(bf16[1,8,64,2048]{3,2,1,0:T(8,128)(2,1)} %param.5) | copy-start | bytes 6291460
  0.7 8.5 %copy-start.7 = (s32[4,2]{0,1:T(2,128)S(1)}, s32[4,2]{0,1:T(2,128)}, u32[]{:S(2)}) copy-start(s32[4,2]{0,1:T(2,128)} %param.9) | copy-start | bytes 100
  2.9 8.2 %collective-permute-start.11 = (bf16[1,1,64,2048]{3,2,1,0:T(8,128)(2,1)}, bf16[1,1,64,2048]{3,2,1,0:T(8,128)(2,1)S(1)}, u32[]{:S(2)}, u32[]{:S(2)}) collective-permute-start(bf16[1,1,64,2048]{3,2,1,0:T(8,128)(2,1)} %get-tuple-element.31), channel_id=1, source_target_pairs={{0,8},{8,0},{16,24},{24,16},{1,9},{9,1},{17,25},{25,17},{2,10},{10... | collective-permute-start | bytes 786440 | tf_op jit(solution)/shard_map/ppermute | solution.py:23
  3.3 7.7 %collective-permute-start.14 = (bf16[1,1,64,2048]{3,2,1,0:T(8,128)(2,1)}, bf16[1,1,64,2048]{3,2,1,0:T(8,128)(2,1)}, u32[]{:S(2)}, u32[]{:S(2)}) collective-permute-start(bf16[1,1,64,2048]{3,2,1,0:T(8,128)(2,1)} %get-tuple-element.32), channel_id=1, source_target_pairs={{0,8},{8,0},{16,24},{24,16},{1,9},{9,1},{17,25},{25,17},{2,10},{10... | collective-permute-start | bytes 786440 | tf_op jit(solution)/shard_map/ppermute | solution.py:23
  5.5 10.6 %collective-permute-start.7 = (bf16[2,1,64,2048]{3,2,1,0:T(8,128)(2,1)}, bf16[2,1,64,2048]{3,2,1,0:T(8,128)(2,1)}, u32[]{:S(2)}, u32[]{:S(2)}) collective-permute-start(bf16[2,1,64,2048]{3,2,1,0:T(8,128)(2,1)} %fusion.3), channel_id=1, source_target_pairs={{0,8},{8,0},{16,24},{24,16},{1,9},{9,1},{17,25},{25,17},{2,10},{10... | collective-permute-start | bytes 1572872 | tf_op jit(solution)/shard_map/ppermute | solution.py:23
  8.6 27.0 %collective-permute-start.1 = (bf16[4,1,64,2048]{3,2,1,0:T(8,128)(2,1)}, bf16[4,1,64,2048]{3,2,1,0:T(8,128)(2,1)S(1)}, u32[]{:S(2)}, u32[]{:S(2)}) collective-permute-start(bf16[4,1,64,2048]{3,2,1,0:T(8,128)(2,1)} %fusion.1), channel_id=1, source_target_pairs={{0,8},{8,0},{16,24},{24,16},{1,9},{9,1},{17,25},{25,17},{2,10},{10... | collective-permute-start | bytes 3145736 | tf_op jit(solution)/shard_map/ppermute | solution.py:23
  8.7 38.2 %collective-permute-start = (bf16[8,1,64,2048]{3,2,1,0:T(8,128)(2,1)S(1)}, bf16[8,1,64,2048]{3,2,1,0:T(8,128)(2,1)}, u32[]{:S(2)}, u32[]{:S(2)}) collective-permute-start(bf16[8,1,64,2048]{3,2,1,0:T(8,128)(2,1)S(1)} %bitcast.136), channel_id=1, source_target_pairs={{0,8},{8,0},{16,24},{24,16},{1,9},{9,1},{17,25},{25,17},{2,10},{10... | collective-permute-start | bytes 6291464 | tf_op jit(solution)/shard_map/ppermute | solution.py:23
  11.1 12.6 %copy-start.6 = (bf16[1,8,64,2048]{3,2,1,0:T(8,128)(2,1)S(1)}, bf16[1,8,64,2048]{3,2,1,0:T(8,128)(2,1)}, u32[]{:S(2)}) copy-start(bf16[1,8,64,2048]{3,2,1,0:T(8,128)(2,1)} %param.7) | copy-start | bytes 6291460
  13.3 9.9 %collective-permute-start.15 = (bf16[1,1,64,2048]{3,2,1,0:T(8,128)(2,1)S(1)}, bf16[1,1,64,2048]{3,2,1,0:T(8,128)(2,1)S(1)}, u32[]{:S(2)}, u32[]{:S(2)}) collective-permute-start(bf16[1,1,64,2048]{3,2,1,0:T(8,128)(2,1)S(1)} %get-tuple-element.30), channel_id=1, source_target_pairs={{0,16},{8,24},{16,0},{24,8},{1,17},{9,25},{17,1},{25,9},{2,18},{10... | collective-permute-start | bytes 786440 | tf_op jit(solution)/shard_map/ppermute | solution.py:23
  16.0 12.8 %collective-permute-start.12 = (bf16[1,1,64,2048]{3,2,1,0:T(8,128)(2,1)S(1)}, bf16[1,1,64,2048]{3,2,1,0:T(8,128)(2,1)S(1)}, u32[]{:S(2)}, u32[]{:S(2)}) collective-permute-start(bf16[1,1,64,2048]{3,2,1,0:T(8,128)(2,1)S(1)} %get-tuple-element.29), channel_id=1, source_target_pairs={{0,16},{8,24},{16,0},{24,8},{1,17},{9,25},{17,1},{25,9},{2,18},{10... | collective-permute-start | bytes 786440 | tf_op jit(solution)/shard_map/ppermute | solution.py:23
  16.1 7.6 %copy-start.5 = (bf16[1,8,64,2048]{3,2,1,0:T(8,128)(2,1)S(1)}, bf16[1,8,64,2048]{3,2,1,0:T(8,128)(2,1)}, u32[]{:S(2)}) copy-start(bf16[1,8,64,2048]{3,2,1,0:T(8,128)(2,1)} %param.8) | copy-start | bytes 6291460
  18.4 5.2 %copy-start = (f32[1,8,64,2048]{3,2,1,0:T(8,128)S(1)}, f32[1,8,64,2048]{3,2,1,0:T(8,128)}, u32[]{:S(2)}) copy-start(f32[1,8,64,2048]{3,2,1,0:T(8,128)} %param.6) | copy-start | bytes 12582916
  18.5 21.6 %collective-permute-start.8 = (bf16[2,1,64,2048]{3,2,1,0:T(8,128)(2,1)S(1)}, bf16[2,1,64,2048]{3,2,1,0:T(8,128)(2,1)S(1)}, u32[]{:S(2)}, u32[]{:S(2)}) collective-permute-start(bf16[2,1,64,2048]{3,2,1,0:T(8,128)(2,1)S(1)} %fusion.2), channel_id=1, source_target_pairs={{0,16},{8,24},{16,0},{24,8},{1,17},{9,25},{17,1},{25,9},{2,18},{10... | collective-permute-start | bytes 1572872 | tf_op jit(solution)/shard_map/ppermute | solution.py:23
  30.3 36.1 %collective-permute-start.13 = (bf16[1,64,2048]{2,1,0:T(8,128)(2,1)S(1)}, bf16[1,64,2048]{2,1,0:T(8,128)(2,1)S(1)}, u32[]{:S(2)}, u32[]{:S(2)}) collective-permute-start(bf16[1,64,2048]{2,1,0:T(8,128)(2,1)S(1)} %bitcast.138), channel_id=1, source_target_pairs={{0,6},{1,7},{2,4},{3,5},{4,2},{5,3},{6,0},{7,1},{8,14},{9,15},{10,... | collective-permute-start | bytes 786440 | tf_op jit(solution)/shard_map/ppermute | solution.py:23
  34.4 33.5 %collective-permute-start.16 = (bf16[1,64,2048]{2,1,0:T(8,128)(2,1)S(1)}, bf16[1,64,2048]{2,1,0:T(8,128)(2,1)S(1)}, u32[]{:S(2)}, u32[]{:S(2)}) collective-permute-start(bf16[1,64,2048]{2,1,0:T(8,128)(2,1)S(1)} %bitcast.137), channel_id=1, source_target_pairs={{0,7},{1,6},{2,5},{3,4},{4,3},{5,2},{6,1},{7,0},{8,15},{9,14},{10,... | collective-permute-start | bytes 786440 | tf_op jit(solution)/shard_map/ppermute | solution.py:23
  36.6 25.6 %collective-permute-start.2 = (bf16[4,1,64,2048]{3,2,1,0:T(8,128)(2,1)S(1)}, bf16[4,1,64,2048]{3,2,1,0:T(8,128)(2,1)S(1)}, u32[]{:S(2)}, u32[]{:S(2)}) collective-permute-start(bf16[4,1,64,2048]{3,2,1,0:T(8,128)(2,1)S(1)} %fusion), channel_id=1, source_target_pairs={{0,16},{8,24},{16,0},{24,8},{1,17},{9,25},{17,1},{25,9},{2,18},{10... | collective-permute-start | bytes 3145736 | tf_op jit(solution)/shard_map/ppermute | solution.py:23
  42.8 32.0 %collective-permute-start.10 = (bf16[1,64,2048]{2,1,0:T(8,128)(2,1)S(1)}, bf16[1,64,2048]{2,1,0:T(8,128)(2,1)S(1)}, u32[]{:S(2)}, u32[]{:S(2)}) collective-permute-start(bf16[1,64,2048]{2,1,0:T(8,128)(2,1)S(1)} %get-tuple-element.37), channel_id=1, source_target_pairs={{0,5},{1,4},{2,7},{3,6},{4,1},{5,0},{6,3},{7,2},{8,13},{9,12},{10,... | collective-permute-start | bytes 786440 | tf_op jit(solution)/shard_map/ppermute | solution.py:23
  46.9 31.5 %collective-permute-start.9 = (bf16[1,64,2048]{2,1,0:T(8,128)(2,1)S(1)}, bf16[1,64,2048]{2,1,0:T(8,128)(2,1)S(1)}, u32[]{:S(2)}, u32[]{:S(2)}) collective-permute-start(bf16[1,64,2048]{2,1,0:T(8,128)(2,1)S(1)} %get-tuple-element.38), channel_id=1, source_target_pairs={{0,4},{1,5},{2,6},{3,7},{4,0},{5,1},{6,2},{7,3},{8,12},{9,13},{10,... | collective-permute-start | bytes 786440 | tf_op jit(solution)/shard_map/ppermute | solution.py:23
  62.2 74.2 %collective-permute-start.3 = (bf16[8,1,64,2048]{3,2,1,0:T(8,128)(2,1)}, bf16[8,1,64,2048]{3,2,1,0:T(8,128)(2,1)}, u32[]{:S(2)}, u32[]{:S(2)}) collective-permute-start(bf16[8,1,64,2048]{3,2,1,0:T(8,128)(2,1)} %add_convert_fusion.1), channel_id=1, source_target_pairs={{0,16},{8,24},{16,0},{24,8},{1,17},{9,25},{17,1},{25,9},{2,18},{10... | collective-permute-start | bytes 6291464 | tf_op jit(solution)/shard_map/ppermute | solution.py:23
  66.2 24.4 %copy-start.1 = (f32[1,8,64,2048]{3,2,1,0:T(8,128)}, f32[1,8,64,2048]{3,2,1,0:T(8,128)S(1)}, u32[]{:S(2)}) copy-start(f32[1,8,64,2048]{3,2,1,0:T(8,128)S(1)} %get-tuple-element.21) | copy-start | bytes 12582916
  66.3 12.6 %collective-permute-start.4 = (bf16[1,64,2048]{2,1,0:T(8,128)(2,1)S(1)}, bf16[1,64,2048]{2,1,0:T(8,128)(2,1)S(1)}, u32[]{:S(2)}, u32[]{:S(2)}) collective-permute-start(bf16[1,64,2048]{2,1,0:T(8,128)(2,1)S(1)} %get-tuple-element.35), channel_id=1, source_target_pairs={{0,1},{1,0},{2,3},{3,2},{4,5},{5,4},{6,7},{7,6},{8,9},{9,8},{10,11... | collective-permute-start | bytes 786440 | tf_op jit(solution)/shard_map/ppermute | solution.py:23
  67.9 16.1 %collective-permute-start.5 = (bf16[1,64,2048]{2,1,0:T(8,128)(2,1)S(1)}, bf16[1,64,2048]{2,1,0:T(8,128)(2,1)S(1)}, u32[]{:S(2)}, u32[]{:S(2)}) collective-permute-start(bf16[1,64,2048]{2,1,0:T(8,128)(2,1)S(1)} %get-tuple-element.34), channel_id=1, source_target_pairs={{0,2},{1,3},{2,0},{3,1},{4,6},{5,7},{6,4},{7,5},{8,10},{9,11},{10,... | collective-permute-start | bytes 786440 | tf_op jit(solution)/shard_map/ppermute | solution.py:23
  74.8 15.7 %collective-permute-start.6 = (bf16[1,64,2048]{2,1,0:T(8,128)(2,1)S(1)}, bf16[1,64,2048]{2,1,0:T(8,128)(2,1)S(1)}, u32[]{:S(2)}, u32[]{:S(2)}) collective-permute-start(bf16[1,64,2048]{2,1,0:T(8,128)(2,1)S(1)} %get-tuple-element.33), channel_id=1, source_target_pairs={{0,3},{1,2},{2,1},{3,0},{4,7},{5,6},{6,5},{7,4},{8,11},{9,10},{10,... | collective-permute-start | bytes 786440 | tf_op jit(solution)/shard_map/ppermute | solution.py:23
  103.9 12.0 %collective-permute-start.17 = (bf16[1,64,2048]{2,1,0:T(8,128)(2,1)S(1)}, bf16[1,64,2048]{2,1,0:T(8,128)(2,1)S(1)}, u32[]{:S(2)}, u32[]{:S(2)}) collective-permute-start(bf16[1,64,2048]{2,1,0:T(8,128)(2,1)S(1)} %get-tuple-element.13), channel_id=1, source_target_pairs={{0,7},{1,6},{2,5},{3,4},{4,3},{5,2},{6,1},{7,0},{8,15},{9,14},{10,... | collective-permute-start | bytes 786440 | tf_op jit(solution)/shard_map/ppermute | solution.py:23
  106.4 34.1 %collective-permute-start.18 = (bf16[1,64,2048]{2,1,0:T(8,128)(2,1)S(1)}, bf16[1,64,2048]{2,1,0:T(8,128)(2,1)S(1)}, u32[]{:S(2)}, u32[]{:S(2)}) collective-permute-start(bf16[1,64,2048]{2,1,0:T(8,128)(2,1)S(1)} %get-tuple-element.14), channel_id=1, source_target_pairs={{0,6},{1,7},{2,4},{3,5},{4,2},{5,3},{6,0},{7,1},{8,14},{9,15},{10,... | collective-permute-start | bytes 786440 | tf_op jit(solution)/shard_map/ppermute | solution.py:23
  107.8 38.2 %collective-permute-start.19 = (bf16[1,64,2048]{2,1,0:T(8,128)(2,1)S(1)}, bf16[1,64,2048]{2,1,0:T(8,128)(2,1)S(1)}, u32[]{:S(2)}, u32[]{:S(2)}) collective-permute-start(bf16[1,64,2048]{2,1,0:T(8,128)(2,1)S(1)} %get-tuple-element.15), channel_id=1, source_target_pairs={{0,5},{1,4},{2,7},{3,6},{4,1},{5,0},{6,3},{7,2},{8,13},{9,12},{10,... | collective-permute-start | bytes 786440 | tf_op jit(solution)/shard_map/ppermute | solution.py:23
  107.8 42.9 %collective-permute-start.20 = (bf16[1,64,2048]{2,1,0:T(8,128)(2,1)S(1)}, bf16[1,64,2048]{2,1,0:T(8,128)(2,1)S(1)}, u32[]{:S(2)}, u32[]{:S(2)}) collective-permute-start(bf16[1,64,2048]{2,1,0:T(8,128)(2,1)S(1)} %get-tuple-element.16), channel_id=1, source_target_pairs={{0,4},{1,5},{2,6},{3,7},{4,0},{5,1},{6,2},{7,3},{8,12},{9,13},{10,... | collective-permute-start | bytes 786440 | tf_op jit(solution)/shard_map/ppermute | solution.py:23
  115.9 38.6 %collective-permute-start.21 = (bf16[1,64,2048]{2,1,0:T(8,128)(2,1)S(1)}, bf16[1,64,2048]{2,1,0:T(8,128)(2,1)S(1)}, u32[]{:S(2)}, u32[]{:S(2)}) collective-permute-start(bf16[1,64,2048]{2,1,0:T(8,128)(2,1)S(1)} %get-tuple-element.17), channel_id=1, source_target_pairs={{0,3},{1,2},{2,1},{3,0},{4,7},{5,6},{6,5},{7,4},{8,11},{9,10},{10,... | collective-permute-start | bytes 786440 | tf_op jit(solution)/shard_map/ppermute | solution.py:23
  136.4 20.3 %collective-permute-start.22 = (bf16[1,64,2048]{2,1,0:T(8,128)(2,1)S(1)}, bf16[1,64,2048]{2,1,0:T(8,128)(2,1)S(1)}, u32[]{:S(2)}, u32[]{:S(2)}) collective-permute-start(bf16[1,64,2048]{2,1,0:T(8,128)(2,1)S(1)} %get-tuple-element.18), channel_id=1, source_target_pairs={{0,2},{1,3},{2,0},{3,1},{4,6},{5,7},{6,4},{7,5},{8,10},{9,11},{10,... | collective-permute-start | bytes 786440 | tf_op jit(solution)/shard_map/ppermute | solution.py:23
  140.5 16.3 %collective-permute-start.23 = (bf16[1,64,2048]{2,1,0:T(8,128)(2,1)S(1)}, bf16[1,64,2048]{2,1,0:T(8,128)(2,1)S(1)}, u32[]{:S(2)}, u32[]{:S(2)}) collective-permute-start(bf16[1,64,2048]{2,1,0:T(8,128)(2,1)S(1)} %get-tuple-element.19), channel_id=1, source_target_pairs={{0,1},{1,0},{2,3},{3,2},{4,5},{5,4},{6,7},{7,6},{8,9},{9,8},{10,11... | collective-permute-start | bytes 786440 | tf_op jit(solution)/shard_map/ppermute | solution.py:23
  157.0 1.3 copy-start.2
  157.0 2.0 %copy-start.3 = (bf16[1,8,64,2048]{3,2,1,0:T(8,128)(2,1)}, bf16[1,8,64,2048]{3,2,1,0:T(8,128)(2,1)S(1)}, u32[]{:S(2)}) copy-start(bf16[1,8,64,2048]{3,2,1,0:T(8,128)(2,1)S(1)} %get-tuple-element.39) | copy-start | bytes 6291460

commit v3 on v2

v3 whole, which is shorter than its diff:
```python
import math

import jax
import jax.numpy as jnp
from jax import lax
from jax.experimental import pallas as pl
from jax.experimental.pallas import tpu as pltpu
from jax.sharding import PartitionSpec as P

NS_STEPS = 5

coeff_a = 3.4445
coeff_b = -4.775
coeff_c = 2.0315
learn_rate = 0.05

F32 = jnp.float32
BF16 = jnp.bfloat16
ANY = pl.BlockSpec(memory_space=pl.ANY)
MIB = 1 << 20


def swapped(values, axis, offset):
    return lax.ppermute(values, axis, [(i, i ^ offset) for i in range(lax.axis_size(axis))])


def cost(flops, moved):
    return pl.CostEstimate(flops=int(flops), bytes_accessed=int(moved), transcendentals=0)


def params(mib):
    return pltpu.CompilerParams(vmem_limit_bytes=mib * MIB)


def split(values):
    high = values.astype(BF16)
    return high, (values - high.astype(F32)).astype(BF16)


def times(left, right):
    return jnp.dot(left, right, preferred_element_type=F32)


def orthogonalize_body(scale, count, here, *refs):
    blocks, out = refs[:count], refs[count]
    held, made, gram_held, poly_held, in_sems, out_sems = refs[count + 1 :]
    rows = blocks[0].shape[1]
    size, columns = held.shape
    matrix = pl.program_id(0)
    copies = []
    for offset, block in enumerate(blocks):
        start = pl.multiple_of((here[0] ^ offset) * rows, rows)
        copies.append(
            pltpu.make_async_copy(
                block.at[matrix], held.at[pl.ds(start, rows), :], in_sems.at[offset]
            )
        )
    for copy in copies:
        copy.start()
    for copy in copies:
        copy.wait()

    gram = lax.dot_general(
        held[...], held[...], (((1,), (1,)), ((), ())), preferred_element_type=F32
    )
    on_diagonal = lax.broadcasted_iota(jnp.int32, (size, size), 0) == lax.broadcasted_iota(
        jnp.int32, (size, size), 1
    )
    square_norm = jnp.sum(
        jnp.sum(jnp.where(on_diagonal, gram, 0.0), axis=0, keepdims=True), axis=1, keepdims=True
    )
    inverse = 1.0 / (jnp.sqrt(square_norm) + 1e-07)
    gram_held[...] = gram * inverse * inverse

    def step(first, last):
        gram = gram_held[...]
        gram_high, gram_low = split(gram)
        shift = (
            coeff_b * gram_high.astype(F32) + coeff_c * times(gram_high, gram_high)
        ).astype(BF16)
        if first:
            poly_held[...] = jnp.where(on_diagonal, coeff_a, 0.0) + shift.astype(F32)
        else:
            poly = poly_held[...]
            poly_high, poly_low = split(poly)
            poly_held[...] = coeff_a * poly + times(shift, poly_high) + times(shift, poly_low)
        if not last:
            half = coeff_a * gram + times(shift, gram_high) + times(shift, gram_low)
            half_high, half_low = split(half)
            gram_held[...] = coeff_a * half + times(half_high, shift) + times(half_low, shift)

    step(True, False)

    @pl.loop(0, NS_STEPS - 2)
    def _(_):
        step(False, False)

    step(False, True)
    high, low = split(poly_held[...] * (scale * inverse))
    parts = out_sems.shape[0]
    width = columns // parts
    copies = []
    for part in range(parts):
        here_columns = pl.ds(part * width, width)
        values = held[:, here_columns]
        made[:, here_columns] = (times(high, values) + times(low, values)).astype(BF16)
        copies.append(
            pltpu.make_async_copy(
                made.at[:, here_columns], out.at[matrix, :, here_columns], out_sems.at[part]
            )
        )
        copies[-1].start()
    for copy in copies:
        copy.wait()


def orthogonalize(blocks, here, scale):
    count = len(blocks)
    each, rows, columns = blocks[0].shape
    size = count * rows
    parts = 4 if columns % 512 == 0 else 1
    flops = 2 * each * size * size * (29 * size + 3 * columns)

    def body(*refs):
        orthogonalize_body(scale, count, *refs)

    return pl.pallas_call(
        body,
        grid_spec=pltpu.PrefetchScalarGridSpec(
            num_scalar_prefetch=1,
            grid=(each,),
            in_specs=[ANY] * count,
            out_specs=ANY,
            scratch_shapes=[
                pltpu.VMEM((size, columns), BF16),
                pltpu.VMEM((size, columns), BF16),
                pltpu.VMEM((size, size), F32),
                pltpu.VMEM((size, size), F32),
                pltpu.SemaphoreType.DMA((count,)),
                pltpu.SemaphoreType.DMA((parts,)),
            ],
        ),
        out_shape=jax.ShapeDtypeStruct((each, size, columns), BF16),
        compiler_params=params(32),
        cost_estimate=cost(flops, 4 * each * size * columns),
        name="orthogonalize",
    )(here.reshape(1), *blocks)


def local(weight, tracker, grad_new, grad_old, mix_keep):
    shards = lax.axis_size("shard")
    _, experts, rows, columns = tracker.shape
    each = experts // shards
    shape = (shards, each, rows, columns)
    weight, tracker, grad_new, grad_old = (
        values.reshape(shape) for values in (weight, tracker, grad_new, grad_old)
    )
    here = lax.axis_index("shard")
    rep_index = lax.axis_index("rep")
    keep = mix_keep.astype(F32) / 16.0
    first, second = keep[rep_index, 0], keep[rep_index, 1]

    unit = shards // 8 if shards % 8 == 0 else 0
    if unit:
        groups = [(low * unit, count * unit) for low, count in ((7, 1), (6, 1), (2, 2), (4, 2), (0, 2))]
        lead = (6 * unit, 2 * unit)
    else:
        groups = [(0, shards)]
        lead = groups[0]

    def place(lowest, length):
        return (here ^ lowest) // length * length

    def taken(values, lowest, length, start=0):
        return lax.dynamic_slice_in_dim(values, place(lowest, length) - start, length, axis=0)

    def blend(own, near):
        return first * own + (1.0 - first) * near.astype(F32)

    own = taken(tracker, *lead)
    lead_mixed = blend(own, swapped(own.astype(BF16), "rep", 1))
    lead_sent = lead_mixed.astype(BF16)
    tracker, lead_sent = lax.optimization_barrier((tracker, lead_sent))
    near = swapped(tracker.astype(BF16), "rep", 1)

    new_tracker = jnp.zeros(shape, F32)
    blocks = [None] * shards
    arrived = []
    for turn, (lowest, length) in enumerate(groups):
        if lead[0] <= lowest < lead[0] + lead[1]:
            mixed = taken(lead_mixed, lowest, length, place(*lead))
            sent = taken(lead_sent, lowest, length, place(*lead))
        else:
            mixed = blend(taken(tracker, lowest, length), taken(near, lowest, length))
            waits = arrived[0] if turn == 2 else blocks[groups[turn - 3][0]]
            sent, _ = lax.optimization_barrier((mixed.astype(BF16), waits))
        far = swapped(sent, "rep", 2)
        arrived.append(far)
        part = second * mixed + (1.0 - second) * far.astype(F32)
        part += taken(grad_new, lowest, length).astype(F32)
        part -= taken(grad_old, lowest, length).astype(F32)
        for offset in reversed(range(lowest, lowest + length)):
            block = lax.dynamic_index_in_dim(part, (here ^ offset) % length, 0, False)
            block = block.astype(BF16)
            blocks[offset] = swapped(block, "shard", offset) if offset else block
        new_tracker = lax.dynamic_update_slice_in_dim(
            new_tracker, part, place(lowest, length), axis=0
        )

    weight, _ = lax.optimization_barrier((weight, arrived[len(groups) // 2]))
    weight_near = swapped(weight, "rep", 1)
    weight_own = blend(weight.astype(F32), weight_near).astype(BF16)
    weight_own, _ = lax.optimization_barrier((weight_own, arrived[-1]))
    weight_far = swapped(weight_own, "rep", 2)
    mixed_weight = (
        second * weight_own.astype(F32) + (1.0 - second) * weight_far.astype(F32)
    ).astype(BF16)

    scale = 0.2 * math.sqrt(max(shards * rows, columns))
    update = orthogonalize(blocks, here, scale)
    update = update.reshape(each, shards, rows, columns).swapaxes(0, 1)
    update = lax.all_to_all(update, "shard", split_axis=0, concat_axis=0, tiled=True)
    new_weight = (mixed_weight.astype(F32) - learn_rate * update.astype(F32)).astype(BF16)
    shape = (1, experts, rows, columns)
    return new_weight.reshape(shape), new_tracker.reshape(shape), update.reshape(shape)


def solution(mesh):
    spec = P("rep", None, "shard", None)
    return jax.shard_map(
        local,
        mesh=mesh,
        in_specs=(spec, spec, spec, spec, P()),
        out_specs=(spec, spec, spec),
        check_vma=False,
    )
```

time: 159 us -> 176 us (1.11)
  waiting for transfers between devices: 57.5 us -> 88.8 us
  starting transfers between devices: 51.8 us -> 26.1 us
  other arithmetic: 23.3 us -> 37.3 us
  local copies, waits for them, and re-layouts: 10.8 us -> 7.51 us
    all_to_all x0 -> x1, waiting for transfers between devices: none -> 38.6 us  [local(): lax.all_to_all(update, 'shard', split_axis=0, concat_axis=0, tiled=True)]
    ppermute x24 -> x16, starting transfers between devices: 51.8 us -> 22.3 us  [swapped(): lax.ppermute(values, axis, [(i, i ^ offset) for i in range(lax.axis_size(...]
    ppermute x24 -> x16, waiting for transfers between devices: 57.5 us -> 50.2 us  [swapped(): lax.ppermute(values, axis, [(i, i ^ offset) for i in range(lax.axis_size(...]
    reshape x0 -> x1, other arithmetic: none -> 5.82 us  [local(): new_weight.reshape(shape)]
    convert_element_type x5 -> x4, local copies, waits for them, and re-layouts: 7.17 us -> 1.39 us  [the longest x1 1.29 us: local(): lead_mixed = blend(own, swapped(own.astype(BF16), 'rep', 1))]
    convert_element_type x5 -> x6, other arithmetic: 13.6 us -> 18.5 us  [the longest x1 5.24 us: local(): weight_own = blend(weight.astype(F32), weight_near).astype(BF16)]
    all_to_all x0 -> x1, starting transfers between devices: none -> 3.8 us  [local(): lax.all_to_all(update, 'shard', split_axis=0, concat_axis=0, tiled=True)]
    dynamic_update_slice x12 -> x3, other arithmetic: 9.7 us -> 12.3 us  [local(): lax.dynamic_update_slice_in_dim(new_tracker, part, place(lowest, length),...]
  transfers between devices with their start and end apart: 24 -> 17, of which waited for: 14 -> 11; matrix products, arithmetic and copies ran while one was open for 19% -> 14% of each run, Pallas kernels for 8% -> 8%
where the time goes in v3:
time: 176 us; the launch traced here: 175 us
  waiting for transfers between devices  88.8 us (50%)
  other arithmetic  37.3 us (21%)
  starting transfers between devices  26.1 us (15%)
  Pallas kernels  13.6 us (8%)
  local copies, waits for them, and re-layouts  7.51 us (4%)
  between operations  2.1 us (1%)
    ppermute x16, waiting for transfers between devices, swapped(): lax.ppermute(values, axis, [(i, i ^ offset) for i in range(lax.axis_size(...  50.2 us
    all_to_all x1, waiting for transfers between devices, local(): lax.all_to_all(update, 'shard', split_axis=0, concat_axis=0, tiled=True)  38.6 us
    ppermute x16, starting transfers between devices, swapped(): lax.ppermute(values, axis, [(i, i ^ offset) for i in range(lax.axis_size(...  22.3 us
    pallas_call x1, Pallas kernels, orthogonalize(): pl.pallas_call(body, grid_spec=pltpu.PrefetchScalarGridSpec(num_scalar_pr...  13.6 us
    dynamic_update_slice x3, other arithmetic, local(): lax.dynamic_update_slice_in_dim(new_tracker, part, place(lowest, length),...  12.3 us
    reshape x1, other arithmetic, local(): new_weight.reshape(shape)  5.82 us
    convert_element_type x1, other arithmetic, local(): weight_own = blend(weight.astype(F32), weight_near).astype(BF16)  5.24 us
    convert_element_type x2, other arithmetic, local(): block = block.astype(BF16)  4.38 us
  transfers between devices with their start and end apart: 17, of which 11 were waited for; matrix products, arithmetic and copies ran while one was open for 14% of the time, Pallas kernels for 8%

profile of v3, /device:TPU:0, one launch (start us, length us, event | category | flops | bytes accessed | tf_op | source)
XLA Modules:
  0.0 175.4 jit_solution(16431778646127194827)
XLA Ops:
  0.7 1.3 fusion.4
  2.0 0.5 collective-permute-start
  2.5 0.7 convert_multiply_fusion
  3.2 0.7 constant_dynamic-slice_fusion.3
  4.5 0.0 collective-permute-done
  4.5 2.9 %fusion.11 = (bf16[2,1,64,2048]{3,2,1,0:T(8,128)(2,1)}, f32[2,1,64,2048]{3,2,1,0:T(8,128)S(1)}) fusion(bf16[2,1,64,2048]{3,2,1,0:T(8,128)(2,1)S(1)} %collective-permute-done, f32[]{:T(128)S(6)} %sub.81, f32[1,8,64,2048]{3,2,1,0:T(8,128)} %param.6, s32[]{:T(128)S(6)} %select_n.140, f32[]{:T(128)} %bitcast.1), kind=kLoop, calls=%fused_computation.45 | loop fusion | flops 1310720 | bytes 3145740 | tf_op jit(solution)/shard_map/convert_element_type | solution.py:182
  7.4 3.8 %convert_element_type.298 = bf16[8,1,64,2048]{3,2,1,0:T(8,128)(2,1)} convert(f32[8,1,64,2048]{3,2,1,0:T(8,128)} %bitcast.64) | non-fusion elementwise | flops 1048576 | bytes 6291456 | tf_op jit(solution)/shard_map/convert_element_type | solution.py:184
  11.2 0.1 collective-permute-start.1
  11.3 1.9 %constant_dynamic-slice_fusion = (bf16[1,1,64,2048]{3,2,1,0:T(8,128)(2,1)}, bf16[1,1,64,2048]{3,2,1,0:T(8,128)(2,1)}) fusion(bf16[2,1,64,2048]{3,2,1,0:T(8,128)(2,1)} %get-tuple-element.11, s32[]{:T(128)S(6)} %select_n.146, s32[]{:T(128)S(6)} %select_n.143), kind=kLoop, calls=%fused_computation.38 | loop fusion | bytes 1048584 | tf_op jit(solution)/shard_map/dynamic_slice | solution.py:175
  13.1 2.9 %collective-permute-start.2 = (bf16[1,1,64,2048]{3,2,1,0:T(8,128)(2,1)}, bf16[1,1,64,2048]{3,2,1,0:T(8,128)(2,1)S(1)}, u32[]{:S(2)}, u32[]{:S(2)}) collective-permute-start(bf16[1,1,64,2048]{3,2,1,0:T(8,128)(2,1)} %get-tuple-element.39), channel_id=1, source_target_pairs={{0,16},{8,24},{16,0},{24,8},{1,17},{9,25},{17,1},{25,9},{2,18},{10... | collective-permute-start | bytes 786440 | tf_op jit(solution)/shard_map/ppermute | solution.py:24
  16.7 0.0 copy-start
  16.7 0.1 collective-permute-start.5
  16.8 6.6 %collective-permute-done.2 = bf16[1,1,64,2048]{3,2,1,0:T(8,128)(2,1)S(1)} collective-permute-done((bf16[1,1,64,2048]{3,2,1,0:T(8,128)(2,1)}, bf16[1,1,64,2048]{3,2,1,0:T(8,128)(2,1)S(1)}, u32[]{:S(2)}, u32[]{:S(2)}) %collective-permute-start.2) | collective-permute-done | bytes 262176 | tf_op jit(solution)/shard_map/ppermute | solution.py:24
  23.4 0.5 reshape.280
  23.9 1.8 %convert_bitcast_fusion = (bf16[1,64,2048]{2,1,0:T(8,128)(2,1)S(1)}, f32[1,8,64,2048]{3,2,1,0:T(8,128)S(1)}) fusion(bf16[1,8,64,2048]{3,2,1,0:T(8,128)(2,1)} %param.8, s32[]{:T(128)S(6)} %select_n.158, bf16[1,8,64,2048]{3,2,1,0:T(8,128)(2,1)} %param.7, bf16[1,1,64,2048]{3,2,1,0:T(8,128)(2,1)S(1)} %collective-permute-done.2, f32[]{:T(128)S(6)} %sub.86, ...), kind=kLoop, calls=%fused_computation.36 | loop fusion | flops 1179648 | bytes 2097168 | tf_op jit(solution)/shard_map/convert_element_type | solution.py:204
  25.7 5.2 %collective-permute-start.12 = (bf16[1,64,2048]{2,1,0:T(8,128)(2,1)S(1)}, bf16[1,64,2048]{2,1,0:T(8,128)(2,1)S(1)}, u32[]{:S(2)}, u32[]{:S(2)}) collective-permute-start(bf16[1,64,2048]{2,1,0:T(8,128)(2,1)S(1)} %get-tuple-element.30), channel_id=1, source_target_pairs={{0,7},{1,6},{2,5},{3,4},{4,3},{5,2},{6,1},{7,0},{8,15},{9,14},{10,... | collective-permute-start | bytes 786440 | tf_op jit(solution)/shard_map/ppermute | solution.py:24
  30.9 0.0 collective-permute-done.1
  30.9 2.2 %fusion.2 = (bf16[2,1,64,2048]{3,2,1,0:T(8,128)(2,1)}, bf16[2,1,64,2048]{3,2,1,0:T(8,128)(2,1)}, bf16[2,1,64,2048]{3,2,1,0:T(8,128)(2,1)}) fusion(f32[8,1,64,2048]{3,2,1,0:T(8,128)S(1)} %bitcast.66, s32[]{:T(128)S(6)} %select_n.145, f32[]{:T(128)S(6)} %sub.81, f32[]{:T(128)} %bitcast.1, bf16[8,1,64,2048]{3,2,1,0:T(8,128)(2,1)S(1)} %collective-permute-done.1, ...), kind=kLoop, calls=%fused_computation.19 | loop fusion | flops 3932160 | bytes 6291476 | tf_op jit(solution)/shard_map/convert_element_type | solution.py:196
  33.1 1.5 collective-permute-start.3
  34.6 2.5 %convert_bitcast_fusion.1 = (bf16[1,64,2048]{2,1,0:T(8,128)(2,1)}, f32[1,8,64,2048]{3,2,1,0:T(8,128)S(1)}) fusion(bf16[1,8,64,2048]{3,2,1,0:T(8,128)(2,1)} %param.8, s32[]{:T(128)S(6)} %select_n.147, bf16[1,8,64,2048]{3,2,1,0:T(8,128)(2,1)} %param.7, bf16[1,1,64,2048]{3,2,1,0:T(8,128)(2,1)S(1)} %collective-permute-done.5, f32[]{:T(128)S(6)} %sub.86, ...), kind=kLoop, calls=%fused_computation.37 | loop fusion | flops 1179648 | bytes 2097168 | tf_op jit(solution)/shard_map/convert_element_type | solution.py:204
  37.2 0.2 collective-permute-start.6
  37.4 0.0 collective-permute-done.12.refs_8_
  37.4 1.8 %copy-done.2 = f32[1,8,64,2048]{3,2,1,0:T(8,128)} copy-done((f32[1,8,64,2048]{3,2,1,0:T(8,128)}, f32[1,8,64,2048]{3,2,1,0:T(8,128)S(1)}, u32[]{:S(2)}) %copy-start.2) | copy-done | bytes 4194328
  39.2 0.5 collective-permute-start.13
  39.7 5.8 %collective-permute-done.6.refs_7_ = bf16[1,64,2048]{2,1,0:T(8,128)(2,1)S(1)} collective-permute-done((bf16[1,64,2048]{2,1,0:T(8,128)(2,1)}, bf16[1,64,2048]{2,1,0:T(8,128)(2,1)S(1)}, u32[]{:S(2)}, u32[]{:S(2)}) %collective-permute-start.6) | collective-permute-done | bytes 262176 | tf_op jit(solution)/shard_map/ppermute | solution.py:24
  45.5 0.5 collective-permute-start.7
  46.1 2.2 %collective-permute-done.3 = bf16[2,1,64,2048]{3,2,1,0:T(8,128)(2,1)} collective-permute-done((bf16[2,1,64,2048]{3,2,1,0:T(8,128)(2,1)}, bf16[2,1,64,2048]{3,2,1,0:T(8,128)(2,1)}, u32[]{:S(2)}, u32[]{:S(2)}) %collective-permute-start.3) | collective-permute-done | bytes 524320 | tf_op jit(solution)/shard_map/ppermute | solution.py:24
  48.3 4.4 %bitcast_dynamic-update-slice_fusion.2 = (f32[1,8,64,2048]{3,2,1,0:T(8,128)}, bf16[2,1,64,2048]{3,2,1,0:T(8,128)(2,1)S(1)}) fusion(f32[1,8,64,2048]{3,2,1,0:T(8,128)} %copy-done.2, s32[]{:T(128)S(6)} %select_n.142, bf16[1,8,64,2048]{3,2,1,0:T(8,128)(2,1)} %param.8, bf16[1,8,64,2048]{3,2,1,0:T(8,128)(2,1)} %param.7, ...), kind=kLoop, calls=%fused_computation.13 | loop fusion | flops 3407872 | bytes 4719628 | tf_op jit(solution)/shard_map/dynamic_update_slice | solution.py:206
  52.7 6.7 %collective-permute-done.13 = bf16[2,1,64,2048]{3,2,1,0:T(8,128)(2,1)S(1)} collective-permute-done((bf16[2,1,64,2048]{3,2,1,0:T(8,128)(2,1)}, bf16[2,1,64,2048]{3,2,1,0:T(8,128)(2,1)S(1)}, u32[]{:S(2)}, u32[]{:S(2)}) %collective-permute-start.13) | collective-permute-done | bytes 524320 | tf_op jit(solution)/shard_map/ppermute | solution.py:24
  59.4 3.9 %bitcast_dynamic-update-slice_fusion.1 = (f32[1,8,64,2048]{3,2,1,0:T(8,128)}, bf16[2,1,64,2048]{3,2,1,0:T(8,128)(2,1)S(1)}) fusion(f32[1,8,64,2048]{3,2,1,0:T(8,128)} %get-tuple-element.21, s32[]{:T(128)S(6)} %select_n.157, bf16[1,8,64,2048]{3,2,1,0:T(8,128)(2,1)} %param.8, bf16[1,8,64,2048]{3,2,1,0:T(8,128)(2,1)} %param.7, ...), kind=kLoop, calls=%fused_computation.12 | loop fusion | flops 3407872 | bytes 4719628 | tf_op jit(solution)/shard_map/dynamic_update_slice | solution.py:206
  63.4 4.2 %collective-permute-done.7 = bf16[2,1,64,2048]{3,2,1,0:T(8,128)(2,1)S(1)} collective-permute-done((bf16[2,1,64,2048]{3,2,1,0:T(8,128)(2,1)}, bf16[2,1,64,2048]{3,2,1,0:T(8,128)(2,1)S(1)}, u32[]{:S(2)}, u32[]{:S(2)}) %collective-permute-start.7) | collective-permute-done | bytes 524320 | tf_op jit(solution)/shard_map/ppermute | solution.py:24
  67.6 3.9 %bitcast_dynamic-update-slice_fusion = (f32[1,8,64,2048]{3,2,1,0:T(8,128)}, bf16[2,1,64,2048]{3,2,1,0:T(8,128)(2,1)S(1)}) fusion(f32[1,8,64,2048]{3,2,1,0:T(8,128)} %get-tuple-element.19, s32[]{:T(128)S(6)} %select_n.145, bf16[1,8,64,2048]{3,2,1,0:T(8,128)(2,1)} %param.8, bf16[1,8,64,2048]{3,2,1,0:T(8,128)(2,1)} %param.7, ...), kind=kLoop, calls=%fused_computation.11 | loop fusion | flops 3407872 | bytes 4719628 | tf_op jit(solution)/shard_map/dynamic_update_slice | solution.py:206
  71.6 0.6 collective-permute-start.9
  72.2 4.2 %collective-permute-start.10 = (bf16[1,64,2048]{2,1,0:T(8,128)(2,1)S(1)}, bf16[1,64,2048]{2,1,0:T(8,128)(2,1)S(1)}, u32[]{:S(2)}, u32[]{:S(2)}) collective-permute-start(bf16[1,64,2048]{2,1,0:T(8,128)(2,1)S(1)} %get-tuple-element.35), channel_id=1, source_target_pairs={{0,2},{1,3},{2,0},{3,1},{4,6},{5,7},{6,4},{7,5},{8,10},{9,11},{10,... | collective-permute-start | bytes 786440 | tf_op jit(solution)/shard_map/ppermute | solution.py:24
  76.4 2.2 %collective-permute-start.14 = (bf16[1,64,2048]{2,1,0:T(8,128)(2,1)S(1)}, bf16[1,64,2048]{2,1,0:T(8,128)(2,1)S(1)}, u32[]{:S(2)}, u32[]{:S(2)}) collective-permute-start(bf16[1,64,2048]{2,1,0:T(8,128)(2,1)S(1)} %get-tuple-element.33), channel_id=1, source_target_pairs={{0,4},{1,5},{2,6},{3,7},{4,0},{5,1},{6,2},{7,3},{8,12},{9,13},{10,... | collective-permute-start | bytes 786440 | tf_op jit(solution)/shard_map/ppermute | solution.py:24
  78.6 1.8 %collective-permute-start.15 = (bf16[1,64,2048]{2,1,0:T(8,128)(2,1)S(1)}, bf16[1,64,2048]{2,1,0:T(8,128)(2,1)S(1)}, u32[]{:S(2)}, u32[]{:S(2)}) collective-permute-start(bf16[1,64,2048]{2,1,0:T(8,128)(2,1)S(1)} %get-tuple-element.32), channel_id=1, source_target_pairs={{0,5},{1,4},{2,7},{3,6},{4,1},{5,0},{6,3},{7,2},{8,13},{9,12},{10,... | collective-permute-start | bytes 786440 | tf_op jit(solution)/shard_map/ppermute | solution.py:24
  80.4 10.0 %collective-permute-done.10.refs_3_ = bf16[1,64,2048]{2,1,0:T(8,128)(2,1)S(1)} collective-permute-done((bf16[1,64,2048]{2,1,0:T(8,128)(2,1)S(1)}, bf16[1,64,2048]{2,1,0:T(8,128)(2,1)S(1)}, u32[]{:S(2)}, u32[]{:S(2)}) %collective-permute-start.10) | collective-permute-done | bytes 262176 | tf_op jit(solution)/shard_map/ppermute | solution.py:24
  90.4 1.7 collective-permute-done.11.refs_4_
  92.1 4.1 %collective-permute-done.14.refs_5_ = bf16[1,64,2048]{2,1,0:T(8,128)(2,1)S(1)} collective-permute-done((bf16[1,64,2048]{2,1,0:T(8,128)(2,1)S(1)}, bf16[1,64,2048]{2,1,0:T(8,128)(2,1)S(1)}, u32[]{:S(2)}, u32[]{:S(2)}) %collective-permute-start.14) | collective-permute-done | bytes 262176 | tf_op jit(solution)/shard_map/ppermute | solution.py:24
  96.2 3.8 %collective-permute-done.15.refs_6_ = bf16[1,64,2048]{2,1,0:T(8,128)(2,1)S(1)} collective-permute-done((bf16[1,64,2048]{2,1,0:T(8,128)(2,1)S(1)}, bf16[1,64,2048]{2,1,0:T(8,128)(2,1)S(1)}, u32[]{:S(2)}, u32[]{:S(2)}) %collective-permute-start.15) | collective-permute-done | bytes 262176 | tf_op jit(solution)/shard_map/ppermute | solution.py:24
  99.9 13.6 %orthogonalize.1 = bf16[1,512,2048]{2,1,0:T(8,128)(2,1)} custom-call(s32[1]{0:T(128)} %bitcast.8.refs_0_, bf16[1,64,2048]{2,1,0:T(8,128)(2,1)S(1)} %get-tuple-element.37.refs_1_, bf16[1,64,2048]{2,1,0:T(8,128)(2,1)S(1)} %collective-permute-done.9.refs_2_, bf16[1,64,2048]{2,1,0:T(8,128)(2,1)S(1)} %collective-permute-done.10.refs_3_, ...), custom_call_target="tpu_custom_call" | custom-call | flops 11005853696 | bytes 4194304 | tf_op jit(solution)/shard_map/orthogonalize/pallas_call | solution.py:127
  113.5 3.8 %all-to-all-start = ((bf16[8,1,64,2048]{3,2,1,0:T(8,128)(2,1)}), bf16[8,1,64,2048]{3,2,1,0:T(8,128)(2,1)S(1)}, u32[]{:S(2)}, u32[]{:S(2)}) async-start(bf16[8,1,64,2048]{3,2,1,0:T(8,128)(2,1)} %bitcast.23), calls=%async_computation | async-start | bytes 4194304 | tf_op jit(solution)/shard_map/all_to_all | solution.py:222
  117.3 5.2 %add_convert_fusion.1 = bf16[8,1,64,2048]{3,2,1,0:T(8,128)(2,1)} fusion(bf16[8,1,64,2048]{3,2,1,0:T(8,128)(2,1)} %collective-permute-done.4, bf16[8,1,64,2048]{3,2,1,0:T(8,128)(2,1)} %bitcast.2, f32[]{:T(128)S(6)} %sub.81, f32[]{:T(128)} %bitcast.1), kind=kLoop, calls=%fused_computation.2 | loop fusion | flops 6291456 | bytes 6291464 | tf_op jit(solution)/shard_map/convert_element_type | solution.py:212
  122.6 2.0 %collective-permute-start.8 = (bf16[8,1,64,2048]{3,2,1,0:T(8,128)(2,1)}, bf16[8,1,64,2048]{3,2,1,0:T(8,128)(2,1)}, u32[]{:S(2)}, u32[]{:S(2)}) collective-permute-start(bf16[8,1,64,2048]{3,2,1,0:T(8,128)(2,1)} %add_convert_fusion.1), channel_id=1, source_target_pairs={{0,16},{8,24},{16,0},{24,8},{1,17},{9,25},{17,1},{25,9},{2,18},{10... | collective-permute-start | bytes 6291464 | tf_op jit(solution)/shard_map/ppermute | solution.py:24
  124.6 38.6 %all-to-all-done = bf16[8,1,64,2048]{3,2,1,0:T(8,128)(2,1)S(1)} async-done(((bf16[8,1,64,2048]{3,2,1,0:T(8,128)(2,1)}), bf16[8,1,64,2048]{3,2,1,0:T(8,128)(2,1)S(1)}, u32[]{:S(2)}, u32[]{:S(2)}) %all-to-all-start) | async-done | bytes 2097184 | tf_op jit(solution)/shard_map/all_to_all | solution.py:222
  163.2 5.1 %collective-permute-done.8 = bf16[8,1,64,2048]{3,2,1,0:T(8,128)(2,1)} collective-permute-done((bf16[8,1,64,2048]{3,2,1,0:T(8,128)(2,1)}, bf16[8,1,64,2048]{3,2,1,0:T(8,128)(2,1)}, u32[]{:S(2)}, u32[]{:S(2)}) %collective-permute-start.8) | collective-permute-done | bytes 2097184 | tf_op jit(solution)/shard_map/ppermute | solution.py:24
  168.3 5.8 %fusion = bf16[1,8,64,2048]{3,2,1,0:T(8,128)(2,1)} fusion(bf16[8,1,64,2048]{3,2,1,0:T(8,128)(2,1)S(1)} %all-to-all-done, bf16[8,1,64,2048]{3,2,1,0:T(8,128)(2,1)} %collective-permute-done.8, bf16[8,1,64,2048]{3,2,1,0:T(8,128)(2,1)} %add_convert_fusion.1, f32[]{:T(128)S(6)} %sub.86, f32[]{:T(128)} %bitcast), kind=kLoop, calls=%fused_computation.3 | loop fusion | flops 11534336 | bytes 8388616 | tf_op jit(solution)/shard_map/reshape | solution.py:225
  174.1 1.3 copy.17
  (12 shorter events, 0.1 us)
Async XLA Ops:
  2.0 2.5 %collective-permute-start = (bf16[2,1,64,2048]{3,2,1,0:T(8,128)(2,1)S(1)}, bf16[2,1,64,2048]{3,2,1,0:T(8,128)(2,1)S(1)}, u32[]{:S(2)}, u32[]{:S(2)}) collective-permute-start(bf16[2,1,64,2048]{3,2,1,0:T(8,128)(2,1)S(1)} %fusion.4), channel_id=1, source_target_pairs={{0,8},{8,0},{16,24},{24,16},{1,9},{9,1},{17,25},{25,17},{2,10},{10... | collective-permute-start | bytes 1572872 | tf_op jit(solution)/shard_map/ppermute | solution.py:24
  11.2 19.7 %collective-permute-start.1 = (bf16[8,1,64,2048]{3,2,1,0:T(8,128)(2,1)}, bf16[8,1,64,2048]{3,2,1,0:T(8,128)(2,1)S(1)}, u32[]{:S(2)}, u32[]{:S(2)}) collective-permute-start(bf16[8,1,64,2048]{3,2,1,0:T(8,128)(2,1)} %convert_element_type.298), channel_id=1, source_target_pairs={{0,8},{8,0},{16,24},{24,16},{1,9},{9,1},{17,25},{25,17},{2,10},{10... | collective-permute-start | bytes 6291464 | tf_op jit(solution)/shard_map/ppermute | solution.py:24
  13.1 10.3 %collective-permute-start.2 = (bf16[1,1,64,2048]{3,2,1,0:T(8,128)(2,1)}, bf16[1,1,64,2048]{3,2,1,0:T(8,128)(2,1)S(1)}, u32[]{:S(2)}, u32[]{:S(2)}) collective-permute-start(bf16[1,1,64,2048]{3,2,1,0:T(8,128)(2,1)} %get-tuple-element.39), channel_id=1, source_target_pairs={{0,16},{8,24},{16,0},{24,8},{1,17},{9,25},{17,1},{25,9},{2,18},{10... | collective-permute-start | bytes 786440 | tf_op jit(solution)/shard_map/ppermute | solution.py:24
  16.7 14.2 %copy-start = (f32[1,8,64,2048]{3,2,1,0:T(8,128)S(1)}, f32[1,8,64,2048]{3,2,1,0:T(8,128)}, u32[]{:S(2)}) copy-start(f32[1,8,64,2048]{3,2,1,0:T(8,128)} %param.6) | copy-start | bytes 12582916
  16.7 17.9 %collective-permute-start.5 = (bf16[1,1,64,2048]{3,2,1,0:T(8,128)(2,1)}, bf16[1,1,64,2048]{3,2,1,0:T(8,128)(2,1)S(1)}, u32[]{:S(2)}, u32[]{:S(2)}) collective-permute-start(bf16[1,1,64,2048]{3,2,1,0:T(8,128)(2,1)} %get-tuple-element.38), channel_id=1, source_target_pairs={{0,16},{8,24},{16,0},{24,8},{1,17},{9,25},{17,1},{25,9},{2,18},{10... | collective-permute-start | bytes 786440 | tf_op jit(solution)/shard_map/ppermute | solution.py:24
  25.7 11.7 %collective-permute-start.12 = (bf16[1,64,2048]{2,1,0:T(8,128)(2,1)S(1)}, bf16[1,64,2048]{2,1,0:T(8,128)(2,1)S(1)}, u32[]{:S(2)}, u32[]{:S(2)}) collective-permute-start(bf16[1,64,2048]{2,1,0:T(8,128)(2,1)S(1)} %get-tuple-element.30), channel_id=1, source_target_pairs={{0,7},{1,6},{2,5},{3,4},{4,3},{5,2},{6,1},{7,0},{8,15},{9,14},{10,... | collective-permute-start | bytes 786440 | tf_op jit(solution)/shard_map/ppermute | solution.py:24
  33.1 15.2 %collective-permute-start.3 = (bf16[2,1,64,2048]{3,2,1,0:T(8,128)(2,1)}, bf16[2,1,64,2048]{3,2,1,0:T(8,128)(2,1)}, u32[]{:S(2)}, u32[]{:S(2)}) collective-permute-start(bf16[2,1,64,2048]{3,2,1,0:T(8,128)(2,1)} %get-tuple-element.12), channel_id=1, source_target_pairs={{0,16},{8,24},{16,0},{24,8},{1,17},{9,25},{17,1},{25,9},{2,18},{10... | collective-permute-start | bytes 1572872 | tf_op jit(solution)/shard_map/ppermute | solution.py:24
  37.1 2.0 %copy-start.2 = (f32[1,8,64,2048]{3,2,1,0:T(8,128)}, f32[1,8,64,2048]{3,2,1,0:T(8,128)S(1)}, u32[]{:S(2)}) copy-start(f32[1,8,64,2048]{3,2,1,0:T(8,128)S(1)} %get-tuple-element.29) | copy-start | bytes 12582916
  37.2 8.4 %collective-permute-start.6 = (bf16[1,64,2048]{2,1,0:T(8,128)(2,1)}, bf16[1,64,2048]{2,1,0:T(8,128)(2,1)S(1)}, u32[]{:S(2)}, u32[]{:S(2)}) collective-permute-start(bf16[1,64,2048]{2,1,0:T(8,128)(2,1)} %get-tuple-element.28), channel_id=1, source_target_pairs={{0,6},{1,7},{2,4},{3,5},{4,2},{5,3},{6,0},{7,1},{8,14},{9,15},{10,... | collective-permute-start | bytes 786440 | tf_op jit(solution)/shard_map/ppermute | solution.py:24
  39.2 20.3 %collective-permute-start.13 = (bf16[2,1,64,2048]{3,2,1,0:T(8,128)(2,1)}, bf16[2,1,64,2048]{3,2,1,0:T(8,128)(2,1)S(1)}, u32[]{:S(2)}, u32[]{:S(2)}) collective-permute-start(bf16[2,1,64,2048]{3,2,1,0:T(8,128)(2,1)} %get-tuple-element.16), channel_id=1, source_target_pairs={{0,16},{8,24},{16,0},{24,8},{1,17},{9,25},{17,1},{25,9},{2,18},{10... | collective-permute-start | bytes 1572872 | tf_op jit(solution)/shard_map/ppermute | solution.py:24
  39.7 19.7 %copy-start.1 = (f32[1,8,64,2048]{3,2,1,0:T(8,128)S(1)}, f32[1,8,64,2048]{3,2,1,0:T(8,128)}, u32[]{:S(2)}) copy-start(f32[1,8,64,2048]{3,2,1,0:T(8,128)} %param.6) | copy-start | bytes 12582916
  45.5 22.1 %collective-permute-start.7 = (bf16[2,1,64,2048]{3,2,1,0:T(8,128)(2,1)}, bf16[2,1,64,2048]{3,2,1,0:T(8,128)(2,1)S(1)}, u32[]{:S(2)}, u32[]{:S(2)}) collective-permute-start(bf16[2,1,64,2048]{3,2,1,0:T(8,128)(2,1)} %get-tuple-element.14), channel_id=1, source_target_pairs={{0,16},{8,24},{16,0},{24,8},{1,17},{9,25},{17,1},{25,9},{2,18},{10... | collective-permute-start | bytes 1572872 | tf_op jit(solution)/shard_map/ppermute | solution.py:24
  71.6 8.8 %collective-permute-start.9 = (bf16[1,64,2048]{2,1,0:T(8,128)(2,1)S(1)}, bf16[1,64,2048]{2,1,0:T(8,128)(2,1)S(1)}, u32[]{:S(2)}, u32[]{:S(2)}) collective-permute-start(bf16[1,64,2048]{2,1,0:T(8,128)(2,1)S(1)} %get-tuple-element.36), channel_id=1, source_target_pairs={{0,1},{1,0},{2,3},{3,2},{4,5},{5,4},{6,7},{7,6},{8,9},{9,8},{10,11... | collective-permute-start | bytes 786440 | tf_op jit(solution)/shard_map/ppermute | solution.py:24
  72.2 18.2 %collective-permute-start.10 = (bf16[1,64,2048]{2,1,0:T(8,128)(2,1)S(1)}, bf16[1,64,2048]{2,1,0:T(8,128)(2,1)S(1)}, u32[]{:S(2)}, u32[]{:S(2)}) collective-permute-start(bf16[1,64,2048]{2,1,0:T(8,128)(2,1)S(1)} %get-tuple-element.35), channel_id=1, source_target_pairs={{0,2},{1,3},{2,0},{3,1},{4,6},{5,7},{6,4},{7,5},{8,10},{9,11},{10,... | collective-permute-start | bytes 786440 | tf_op jit(solution)/shard_map/ppermute | solution.py:24
  76.4 15.7 %collective-permute-start.11 = (bf16[1,64,2048]{2,1,0:T(8,128)(2,1)S(1)}, bf16[1,64,2048]{2,1,0:T(8,128)(2,1)S(1)}, u32[]{:S(2)}, u32[]{:S(2)}) collective-permute-start(bf16[1,64,2048]{2,1,0:T(8,128)(2,1)S(1)} %get-tuple-element.34), channel_id=1, source_target_pairs={{0,3},{1,2},{2,1},{3,0},{4,7},{5,6},{6,5},{7,4},{8,11},{9,10},{10,... | collective-permute-start | bytes 786440 | tf_op jit(solution)/shard_map/ppermute | solution.py:24
  76.4 19.7 %collective-permute-start.14 = (bf16[1,64,2048]{2,1,0:T(8,128)(2,1)S(1)}, bf16[1,64,2048]{2,1,0:T(8,128)(2,1)S(1)}, u32[]{:S(2)}, u32[]{:S(2)}) collective-permute-start(bf16[1,64,2048]{2,1,0:T(8,128)(2,1)S(1)} %get-tuple-element.33), channel_id=1, source_target_pairs={{0,4},{1,5},{2,6},{3,7},{4,0},{5,1},{6,2},{7,3},{8,12},{9,13},{10,... | collective-permute-start | bytes 786440 | tf_op jit(solution)/shard_map/ppermute | solution.py:24
  78.6 21.4 %collective-permute-start.15 = (bf16[1,64,2048]{2,1,0:T(8,128)(2,1)S(1)}, bf16[1,64,2048]{2,1,0:T(8,128)(2,1)S(1)}, u32[]{:S(2)}, u32[]{:S(2)}) collective-permute-start(bf16[1,64,2048]{2,1,0:T(8,128)(2,1)S(1)} %get-tuple-element.32), channel_id=1, source_target_pairs={{0,5},{1,4},{2,7},{3,6},{4,1},{5,0},{6,3},{7,2},{8,13},{9,12},{10,... | collective-permute-start | bytes 786440 | tf_op jit(solution)/shard_map/ppermute | solution.py:24
  80.4 37.0 %collective-permute-start.4 = (bf16[8,1,64,2048]{3,2,1,0:T(8,128)(2,1)}, bf16[8,1,64,2048]{3,2,1,0:T(8,128)(2,1)}, u32[]{:S(2)}, u32[]{:S(2)}) collective-permute-start(bf16[8,1,64,2048]{3,2,1,0:T(8,128)(2,1)} %bitcast.2), channel_id=1, source_target_pairs={{0,8},{8,0},{16,24},{24,16},{1,9},{9,1},{17,25},{25,17},{2,10},{10... | collective-permute-start | bytes 6291464 | tf_op jit(solution)/shard_map/ppermute | solution.py:24
  113.5 49.7 %all-to-all-start = ((bf16[8,1,64,2048]{3,2,1,0:T(8,128)(2,1)}), bf16[8,1,64,2048]{3,2,1,0:T(8,128)(2,1)S(1)}, u32[]{:S(2)}, u32[]{:S(2)}) async-start(bf16[8,1,64,2048]{3,2,1,0:T(8,128)(2,1)} %bitcast.23), calls=%async_computation | async-start | bytes 4194304 | tf_op jit(solution)/shard_map/all_to_all | solution.py:222
  122.6 45.7 %collective-permute-start.8 = (bf16[8,1,64,2048]{3,2,1,0:T(8,128)(2,1)}, bf16[8,1,64,2048]{3,2,1,0:T(8,128)(2,1)}, u32[]{:S(2)}, u32[]{:S(2)}) collective-permute-start(bf16[8,1,64,2048]{3,2,1,0:T(8,128)(2,1)} %add_convert_fusion.1), channel_id=1, source_target_pairs={{0,16},{8,24},{16,0},{24,8},{1,17},{9,25},{17,1},{25,9},{2,18},{10... | collective-permute-start | bytes 6291464 | tf_op jit(solution)/shard_map/ppermute | solution.py:24

commit v4 on v3

--- a/solution.py
+++ b/solution.py
@@ -159,67 +159,77 @@
     rep_index = lax.axis_index("rep")
     keep = mix_keep.astype(F32) / 16.0
     first, second = keep[rep_index, 0], keep[rep_index, 1]
-
-    unit = shards // 8 if shards % 8 == 0 else 0
-    if unit:
-        groups = [(low * unit, count * unit) for low, count in ((7, 1), (6, 1), (2, 2), (4, 2), (0, 2))]
-        lead = (6 * unit, 2 * unit)
-    else:
-        groups = [(0, shards)]
-        lead = groups[0]
-
-    def place(lowest, length):
-        return (here ^ lowest) // length * length
-
-    def taken(values, lowest, length, start=0):
-        return lax.dynamic_slice_in_dim(values, place(lowest, length) - start, length, axis=0)
-
-    def blend(own, near):
-        return first * own + (1.0 - first) * near.astype(F32)
-
-    own = taken(tracker, *lead)
-    lead_mixed = blend(own, swapped(own.astype(BF16), "rep", 1))
-    lead_sent = lead_mixed.astype(BF16)
-    tracker, lead_sent = lax.optimization_barrier((tracker, lead_sent))
-    near = swapped(tracker.astype(BF16), "rep", 1)
+    far_first = keep[rep_index ^ 2, 0]
+
+    count = 8 if shards % 8 == 0 else 1
+    length = shards // count
+    paired = 2 if count > 1 else 1
+
+    def place(group):
+        return (here ^ (group * length)) // length * length
+
+    def taken(values, group):
+        return lax.dynamic_slice_in_dim(values, place(group), length, axis=0)
+
+    def blend(share, own, near):
+        return share * own + (1.0 - share) * near.astype(F32)
+
+    def after(values, *others):
+        return lax.optimization_barrier((values, others))[0]
 
     new_tracker = jnp.zeros(shape, F32)
     blocks = [None] * shards
     arrived = []
-    for turn, (lowest, length) in enumerate(groups):
-        if lead[0] <= lowest < lead[0] + lead[1]:
-            mixed = taken(lead_mixed, lowest, length, place(*lead))
-            sent = taken(lead_sent, lowest, length, place(*lead))
+    for turn, group in enumerate(reversed(range(count))):
+        if turn % paired == 0:
+            size = paired * length
+            base = place(group) // size * size
+            source = after(tracker, arrived[0]) if turn >= 4 else tracker
+            pair = lax.dynamic_slice_in_dim(source, base, size, axis=0)
+            pair_near = swapped(pair.astype(BF16), "rep", 1)
+        own = lax.dynamic_slice_in_dim(pair, place(group) - base, length, axis=0)
+        near = lax.dynamic_slice_in_dim(pair_near, place(group) - base, length, axis=0)
+        mixed = blend(first, own, near)
+        if turn < 2:
+            far = swapped(own.astype(BF16), "rep", 2)
+            far_mixed = blend(far_first, far.astype(F32), swapped(far, "rep", 1))
         else:
-            mixed = blend(taken(tracker, lowest, length), taken(near, lowest, length))
-            waits = arrived[0] if turn == 2 else blocks[groups[turn - 3][0]]
-            sent, _ = lax.optimization_barrier((mixed.astype(BF16), waits))
-        far = swapped(sent, "rep", 2)
+            sent = after(mixed.astype(BF16), arrived[turn - 2])
+            if turn in (3, 5, 7):
+                sent = after(sent, blocks[(8 - (turn - 1) // 2) * length])
+            far = swapped(sent, "rep", 2)
+            if turn == count - 1:
+                far = after(far, blocks[4 * length], blocks[3 * length])
+            far_mixed = far.astype(F32)
         arrived.append(far)
-        part = second * mixed + (1.0 - second) * far.astype(F32)
-        part += taken(grad_new, lowest, length).astype(F32)
-        part -= taken(grad_old, lowest, length).astype(F32)
-        for offset in reversed(range(lowest, lowest + length)):
+        part = second * mixed + (1.0 - second) * far_mixed
+        part += taken(grad_new, group).astype(F32)
+        part -= taken(grad_old, group).astype(F32)
+        for offset in reversed(range(group * length, (group + 1) * length)):
             block = lax.dynamic_index_in_dim(part, (here ^ offset) % length, 0, False)
             block = block.astype(BF16)
             blocks[offset] = swapped(block, "shard", offset) if offset else block
-        new_tracker = lax.dynamic_update_slice_in_dim(
-            new_tracker, part, place(lowest, length), axis=0
-        )
-
-    weight, _ = lax.optimization_barrier((weight, arrived[len(groups) // 2]))
+        new_tracker = lax.dynamic_update_slice_in_dim(new_tracker, part, place(group), axis=0)
+
+    weight = after(weight, arrived[count // 2])
     weight_near = swapped(weight, "rep", 1)
-    weight_own = blend(weight.astype(F32), weight_near).astype(BF16)
-    weight_own, _ = lax.optimization_barrier((weight_own, arrived[-1]))
-    weight_far = swapped(weight_own, "rep", 2)
-    mixed_weight = (
-        second * weight_own.astype(F32) + (1.0 - second) * weight_far.astype(F32)
-    ).astype(BF16)
+    weight_own = blend(first, weight.astype(F32), weight_near).astype(BF16)
+    weight_own = after(weight_own, arrived[-1])
+    halves = jnp.split(weight_own, 2) if shards % 2 == 0 else [weight_own]
+    halves_far = [swapped(half, "rep", 2) for half in halves]
 
     scale = 0.2 * math.sqrt(max(shards * rows, columns))
     update = orthogonalize(blocks, here, scale)
+    update = after(update, halves_far[0])
     update = update.reshape(each, shards, rows, columns).swapaxes(0, 1)
     update = lax.all_to_all(update, "shard", split_axis=0, concat_axis=0, tiled=True)
+    mixed_weight = jnp.concatenate(
+        [
+            blend(second, half.astype(F32), half_far).astype(BF16)
+            for half, half_far in zip(halves, halves_far)
+        ]
+    )
+    mixed_weight = lax.optimization_barrier(mixed_weight)
     new_weight = (mixed_weight.astype(F32) - learn_rate * update.astype(F32)).astype(BF16)
     shape = (1, experts, rows, columns)
     return new_weight.reshape(shape), new_tracker.reshape(shape), update.reshape(shape)

time: 176 us -> 165 us (0.938)
  waiting for transfers between devices: 88.8 us -> 62.9 us
  starting transfers between devices: 26.1 us -> 31.5 us
  other arithmetic: 37.3 us -> 42 us
  local copies, waits for them, and re-layouts: 7.51 us -> 11.6 us
    all_to_all x1, waiting for transfers between devices: 38.6 us -> 19 us  [local(): lax.all_to_all(update, 'shard', split_axis=0, concat_axis=0, tiled=True)]
    dynamic_update_slice x3 -> x7, other arithmetic: 12.3 us -> 24.6 us  [local(): lax.dynamic_update_slice_in_dim(new_tracker, part, place(group), axis=0)]
    convert_element_type x6 -> x4, other arithmetic: 18.5 us -> 11.5 us  [the longest x2 5.52 us: local(): sent = after(mixed.astype(BF16), arrived[turn - 2])]
    ppermute x16 -> x24, waiting for transfers between devices: 50.2 us -> 44 us  [swapped(): lax.ppermute(values, axis, [(i, i ^ offset) for i in range(lax.axis_size(...]
    ppermute x16 -> x24, starting transfers between devices: 22.3 us -> 27.9 us  [swapped(): lax.ppermute(values, axis, [(i, i ^ offset) for i in range(lax.axis_size(...]
    convert_element_type x4 -> x3, local copies, waits for them, and re-layouts: 1.39 us -> 5.56 us  [the longest x2 4.3 us: local(): pair_near = swapped(pair.astype(BF16), 'rep', 1)]
    reshape x1, other arithmetic: 5.82 us -> 3.74 us  [local(): new_weight.reshape(shape)]
    dynamic_slice x1 -> x0, local copies, waits for them, and re-layouts: 1.86 us -> none  [taken(): lax.dynamic_slice_in_dim(values, place(lowest, length) - start, length, a...]
  transfers between devices with their start and end apart: 17 -> 25, of which waited for: 11 -> 11; matrix products, arithmetic and copies ran while one was open for 14% -> 27% of each run, Pallas kernels for 8% -> 8%
where the time goes in v4:
time: 165 us; the launch traced here: 164 us
  waiting for transfers between devices  62.9 us (38%)
  other arithmetic  42 us (25%)
  starting transfers between devices  31.5 us (19%)
  Pallas kernels  13.8 us (8%)
  local copies, waits for them, and re-layouts  11.6 us (7%)
  between operations  2.61 us (2%)
    ppermute x24, waiting for transfers between devices, swapped(): lax.ppermute(values, axis, [(i, i ^ offset) for i in range(lax.axis_size(...  44 us
    ppermute x24, starting transfers between devices, swapped(): lax.ppermute(values, axis, [(i, i ^ offset) for i in range(lax.axis_size(...  27.9 us
    dynamic_update_slice x7, other arithmetic, local(): lax.dynamic_update_slice_in_dim(new_tracker, part, place(group), axis=0)  24.6 us
    all_to_all x1, waiting for transfers between devices, local(): lax.all_to_all(update, 'shard', split_axis=0, concat_axis=0, tiled=True)  19 us
    pallas_call x1, Pallas kernels, orthogonalize(): pl.pallas_call(body, grid_spec=pltpu.PrefetchScalarGridSpec(num_scalar_pr...  13.8 us
    convert_element_type x2, other arithmetic, local(): sent = after(mixed.astype(BF16), arrived[turn - 2])  5.52 us
    convert_element_type x2, local copies, waits for them, and re-layouts, local(): pair_near = swapped(pair.astype(BF16), 'rep', 1)  4.3 us
    reshape x1, other arithmetic, local(): new_weight.reshape(shape)  3.74 us
  transfers between devices with their start and end apart: 25, of which 11 were waited for; matrix products, arithmetic and copies ran while one was open for 27% of the time, Pallas kernels for 8%

profile of v4, /device:TPU:0, one launch (start us, length us, event | category | flops | bytes accessed | tf_op | source)
XLA Modules:
  0.0 164.4 jit_solution(14853086371410040601)
XLA Ops:
  0.7 1.3 dynamic-slice_convert_fusion.4
  2.0 3.0 %collective-permute-start = (bf16[1,1,64,2048]{3,2,1,0:T(8,128)(2,1)S(1)}, bf16[1,1,64,2048]{3,2,1,0:T(8,128)(2,1)S(1)}, u32[]{:S(2)}, u32[]{:S(2)}) collective-permute-start(bf16[1,1,64,2048]{3,2,1,0:T(8,128)(2,1)S(1)} %get-tuple-element.59), channel_id=1, source_target_pairs={{0,16},{8,24},{16,0},{24,8},{1,17},{9,25},{17,1},{25,9},{2,18},{10... | collective-permute-start | bytes 786440 | tf_op jit(solution)/shard_map/ppermute | solution.py:24
  5.0 1.7 %fusion.1 = (bf16[2,1,64,2048]{3,2,1,0:T(8,128)(2,1)S(1)}, bf16[2,1,64,2048]{3,2,1,0:T(8,128)(2,1)S(1)}) fusion(f32[1,8,64,2048]{3,2,1,0:T(8,128)} %param.6, s32[]{:T(128)S(6)} %select_n.214, s32[]{:T(128)S(6)} %select_n.204), kind=kLoop, calls=%fused_computation.10 | loop fusion | bytes 2097160 | tf_op jit(solution)/shard_map/convert_element_type | solution.py:189
  7.3 4.8 %collective-permute-done = bf16[1,1,64,2048]{3,2,1,0:T(8,128)(2,1)S(1)} collective-permute-done((bf16[1,1,64,2048]{3,2,1,0:T(8,128)(2,1)S(1)}, bf16[1,1,64,2048]{3,2,1,0:T(8,128)(2,1)S(1)}, u32[]{:S(2)}, u32[]{:S(2)}) %collective-permute-start) | collective-permute-done | bytes 262176 | tf_op jit(solution)/shard_map/ppermute | solution.py:24
  12.1 0.7 convert_multiply_fusion
  12.8 0.6 constant_dynamic-slice_fusion.1
  15.2 2.6 %dynamic-slice_convert_fusion.1 = (bf16[2,1,64,2048]{3,2,1,0:T(8,128)(2,1)}, bf16[2,1,64,2048]{3,2,1,0:T(8,128)(2,1)S(1)}) fusion(f32[8,1,64,2048]{3,2,1,0:T(8,128)} %bitcast.41, s32[]{:T(128)S(6)} %select_n.219, s32[]{:T(128)S(6)} %select_n.209), kind=kLoop, calls=%fused_computation.7 | loop fusion | bytes 2097160 | tf_op jit(solution)/shard_map/convert_element_type | solution.py:189
  17.8 0.5 collective-permute-start.1
  19.1 3.2 %constant_dynamic-update-slice_fusion.7 = (f32[1,8,64,2048]{3,2,1,0:T(8,128)S(1)}, bf16[1,1,64,2048]{3,2,1,0:T(8,128)(2,1)S(1)}, bf16[1,1,64,2048]{3,2,1,0:T(8,128)(2,1)S(1)}) fusion(f32[1,8,64,2048]{3,2,1,0:T(8,128)S(1)} %reshape.234, s32[]{:T(128)S(6)} %select_n.228, bf16[1,8,64,2048]{3,2,1,0:T(8,128)(2,1)} %param.8, bf16[1,8,64,2048]{3,2,1,0:T(8,128)(2,1)} %param.7, ...), kind=kLoop, calls=%fused_computation.49 | loop fusion | flops 2883584 | bytes 3670060 | tf_op jit(solution)/shard_map/dynamic_update_slice | solution.py:212
  22.3 2.1 %collective-permute-start.3 = (bf16[1,1,64,2048]{3,2,1,0:T(8,128)(2,1)S(1)}, bf16[1,1,64,2048]{3,2,1,0:T(8,128)(2,1)S(1)}, u32[]{:S(2)}, u32[]{:S(2)}) collective-permute-start(bf16[1,1,64,2048]{3,2,1,0:T(8,128)(2,1)S(1)} %get-tuple-element.18), channel_id=1, source_target_pairs={{0,16},{8,24},{16,0},{24,8},{1,17},{9,25},{17,1},{25,9},{2,18},{10... | collective-permute-start | bytes 786440 | tf_op jit(solution)/shard_map/ppermute | solution.py:24
  24.4 4.6 %collective-permute-start.10 = (bf16[1,64,2048]{2,1,0:T(8,128)(2,1)S(1)}, bf16[1,64,2048]{2,1,0:T(8,128)(2,1)S(1)}, u32[]{:S(2)}, u32[]{:S(2)}) collective-permute-start(bf16[1,64,2048]{2,1,0:T(8,128)(2,1)S(1)} %bitcast.50), channel_id=1, source_target_pairs={{0,7},{1,6},{2,5},{3,4},{4,3},{5,2},{6,1},{7,0},{8,15},{9,14},{10,... | collective-permute-start | bytes 786440 | tf_op jit(solution)/shard_map/ppermute | solution.py:24
  29.0 3.9 %constant_dynamic-update-slice_fusion.6 = (f32[1,8,64,2048]{3,2,1,0:T(8,128)S(1)}, bf16[1,1,64,2048]{3,2,1,0:T(8,128)(2,1)}) fusion(f32[1,8,64,2048]{3,2,1,0:T(8,128)S(1)} %get-tuple-element.45, s32[]{:T(128)S(6)} %select_n.229, bf16[1,8,64,2048]{3,2,1,0:T(8,128)(2,1)} %param.8, bf16[1,8,64,2048]{3,2,1,0:T(8,128)(2,1)} %param.7, ...), kind=kLoop, calls=%fused_computation.48 | loop fusion | flops 2228224 | bytes 2621476 | tf_op jit(solution)/shard_map/dynamic_update_slice | solution.py:212
  33.0 1.3 fusion.3
  34.3 0.5 collective-permute-start.4
  34.8 3.3 %constant_dynamic-update-slice_fusion.5 = (f32[1,8,64,2048]{3,2,1,0:T(8,128)S(1)}, bf16[1,1,64,2048]{3,2,1,0:T(8,128)(2,1)}, bf16[1,1,64,2048]{3,2,1,0:T(8,128)(2,1)}) fusion(f32[1,8,64,2048]{3,2,1,0:T(8,128)S(1)} %get-tuple-element.43, s32[]{:T(128)S(6)} %select_n.230, bf16[1,8,64,2048]{3,2,1,0:T(8,128)(2,1)} %param.8, bf16[1,8,64,2048]{3,2,1,0:T(8,128)(2,1)} %param.7, ...), kind=kLoop, calls=%fused_computation.47 | loop fusion | flops 2359296 | bytes 3407908 | tf_op jit(solution)/shard_map/dynamic_update_slice | solution.py:212
  38.1 2.0 %copy-done.2 = f32[1,8,64,2048]{3,2,1,0:T(8,128)} copy-done((f32[1,8,64,2048]{3,2,1,0:T(8,128)}, f32[1,8,64,2048]{3,2,1,0:T(8,128)S(1)}, u32[]{:S(2)}) %copy-start.2) | copy-done | bytes 4194328
  40.1 1.5 collective-permute-start.11
  41.6 1.0 collective-permute-start.13
  42.8 5.5 %collective-permute-done.11 = bf16[1,1,64,2048]{3,2,1,0:T(8,128)(2,1)} collective-permute-done((bf16[1,1,64,2048]{3,2,1,0:T(8,128)(2,1)}, bf16[1,1,64,2048]{3,2,1,0:T(8,128)(2,1)}, u32[]{:S(2)}, u32[]{:S(2)}) %collective-permute-start.11) | collective-permute-done | bytes 262176 | tf_op jit(solution)/shard_map/ppermute | solution.py:24
  48.4 3.5 %constant_dynamic-update-slice_fusion.4 = (f32[1,8,64,2048]{3,2,1,0:T(8,128)}, bf16[1,1,64,2048]{3,2,1,0:T(8,128)(2,1)}) fusion(f32[1,8,64,2048]{3,2,1,0:T(8,128)} %copy-done.2, s32[]{:T(128)S(6)} %select_n.231, bf16[1,8,64,2048]{3,2,1,0:T(8,128)(2,1)} %param.8, bf16[1,8,64,2048]{3,2,1,0:T(8,128)(2,1)} %param.7, ...), kind=kLoop, calls=%fused_computation.46 | loop fusion | flops 1703936 | bytes 2360340 | tf_op jit(solution)/shard_map/dynamic_update_slice | solution.py:212
  51.9 3.8 %constant_dynamic-update-slice_fusion.3 = (f32[1,8,64,2048]{3,2,1,0:T(8,128)}, bf16[1,1,64,2048]{3,2,1,0:T(8,128)(2,1)S(1)}, bf16[1,1,64,2048]{3,2,1,0:T(8,128)(2,1)S(1)}) fusion(f32[1,8,64,2048]{3,2,1,0:T(8,128)} %get-tuple-element.39, s32[]{:T(128)S(6)} %select_n.232, bf16[1,8,64,2048]{3,2,1,0:T(8,128)(2,1)} %param.8, bf16[1,8,64,2048]{3,2,1,0:T(8,128)(2,1)} %param.7, ...), kind=kLoop, calls=%fused_computation.45 | loop fusion | flops 2359296 | bytes 3408924 | tf_op jit(solution)/shard_map/dynamic_update_slice | solution.py:212
  55.7 1.4 collective-permute-start.14
  57.1 2.4 %collective-permute-start.15 = (bf16[1,64,2048]{2,1,0:T(8,128)(2,1)}, bf16[1,64,2048]{2,1,0:T(8,128)(2,1)S(1)}, u32[]{:S(2)}, u32[]{:S(2)}) collective-permute-start(bf16[1,64,2048]{2,1,0:T(8,128)(2,1)} %bitcast.51), channel_id=1, source_target_pairs={{0,5},{1,4},{2,7},{3,6},{4,1},{5,0},{6,3},{7,2},{8,13},{9,12},{10,... | collective-permute-start | bytes 786440 | tf_op jit(solution)/shard_map/ppermute | solution.py:24
  59.5 3.3 %collective-permute-done.14 = bf16[1,1,64,2048]{3,2,1,0:T(8,128)(2,1)} collective-permute-done((bf16[1,1,64,2048]{3,2,1,0:T(8,128)(2,1)S(1)}, bf16[1,1,64,2048]{3,2,1,0:T(8,128)(2,1)}, u32[]{:S(2)}, u32[]{:S(2)}) %collective-permute-start.14) | collective-permute-done | bytes 262176 | tf_op jit(solution)/shard_map/ppermute | solution.py:24
  62.8 4.2 %fusion.5 = (bf16[1,1,64,2048]{3,2,1,0:T(8,128)(2,1)}, bf16[1,1,64,2048]{3,2,1,0:T(8,128)(2,1)}, f32[1,8,64,2048]{3,2,1,0:T(8,128)}, bf16[1,1,64,2048]{3,2,1,0:T(8,128)(2,1)S(1)}) fusion(f32[8,1,64,2048]{3,2,1,0:T(8,128)} %bitcast.43, s32[]{:T(128)S(6)} %dynamic_slice.158, f32[]{:T(128)S(6)} %sub.147, f32[]{:T(128)} %bitcast.1, ...), kind=kLoop, calls=%fused_computation.30 | loop fusion | flops 3014656 | bytes 4457508 | tf_op jit(solution)/shard_map/convert_element_type | solution.py:197
  67.0 1.4 collective-permute-start.21
  68.4 2.4 %collective-permute-start.17 = (bf16[1,64,2048]{2,1,0:T(8,128)(2,1)}, bf16[1,64,2048]{2,1,0:T(8,128)(2,1)S(1)}, u32[]{:S(2)}, u32[]{:S(2)}) collective-permute-start(bf16[1,64,2048]{2,1,0:T(8,128)(2,1)} %bitcast.55), channel_id=1, source_target_pairs={{0,4},{1,5},{2,6},{3,7},{4,0},{5,1},{6,2},{7,3},{8,12},{9,13},{10,... | collective-permute-start | bytes 786440 | tf_op jit(solution)/shard_map/ppermute | solution.py:24
  70.8 0.6 collective-permute-done.15.refs_6_
  71.4 0.9 collective-permute-start.16
  72.3 1.5 collective-permute-done.21
  73.8 2.8 %collective-permute-start.23 = (bf16[1,64,2048]{2,1,0:T(8,128)(2,1)S(1)}, bf16[1,64,2048]{2,1,0:T(8,128)(2,1)S(1)}, u32[]{:S(2)}, u32[]{:S(2)}) collective-permute-start(bf16[1,64,2048]{2,1,0:T(8,128)(2,1)S(1)} %bitcast.54), channel_id=1, source_target_pairs={{0,2},{1,3},{2,0},{3,1},{4,6},{5,7},{6,4},{7,5},{8,10},{9,11},{10,... | collective-permute-start | bytes 786440 | tf_op jit(solution)/shard_map/ppermute | solution.py:24
  76.7 3.5 %constant_dynamic-update-slice_fusion.1 = (f32[1,8,64,2048]{3,2,1,0:T(8,128)}, bf16[1,1,64,2048]{3,2,1,0:T(8,128)(2,1)S(1)}) fusion(f32[1,8,64,2048]{3,2,1,0:T(8,128)} %get-tuple-element.51, s32[]{:T(128)S(6)} %select_n.236, bf16[1,8,64,2048]{3,2,1,0:T(8,128)(2,1)} %param.8, bf16[1,8,64,2048]{3,2,1,0:T(8,128)(2,1)} %param.7, ...), kind=kLoop, calls=%fused_computation.43 | loop fusion | flops 1703936 | bytes 2360340 | tf_op jit(solution)/shard_map/dynamic_update_slice | solution.py:212
  80.1 1.7 %collective-permute-done.17.refs_5_ = bf16[1,64,2048]{2,1,0:T(8,128)(2,1)S(1)} collective-permute-done((bf16[1,64,2048]{2,1,0:T(8,128)(2,1)}, bf16[1,64,2048]{2,1,0:T(8,128)(2,1)S(1)}, u32[]{:S(2)}, u32[]{:S(2)}) %collective-permute-start.17) | collective-permute-done | bytes 262176 | tf_op jit(solution)/shard_map/ppermute | solution.py:24
  81.8 1.5 collective-permute-start.22
  83.3 2.1 %collective-permute-done.18.refs_4_ = bf16[1,64,2048]{2,1,0:T(8,128)(2,1)S(1)} collective-permute-done((bf16[1,64,2048]{2,1,0:T(8,128)(2,1)S(1)}, bf16[1,64,2048]{2,1,0:T(8,128)(2,1)S(1)}, u32[]{:S(2)}, u32[]{:S(2)}) %collective-permute-start.18) | collective-permute-done | bytes 262176 | tf_op jit(solution)/shard_map/ppermute | solution.py:24
  85.4 3.0 %add_convert_fusion = bf16[8,1,64,2048]{3,2,1,0:T(8,128)(2,1)S(1)} fusion(bf16[8,1,64,2048]{3,2,1,0:T(8,128)(2,1)} %collective-permute-done.5, bf16[8,1,64,2048]{3,2,1,0:T(8,128)(2,1)S(1)} %bitcast.49, f32[]{:T(128)S(6)} %sub.147, f32[]{:T(128)} %bitcast.1), kind=kLoop, calls=%fused_computation.1 | loop fusion | flops 6291456 | bytes 6291464 | tf_op jit(solution)/shard_map/convert_element_type | solution.py:216
  88.5 1.3 fusion.9
  89.9 3.4 %constant_dynamic-update-slice_fusion = (f32[1,8,64,2048]{3,2,1,0:T(8,128)}, bf16[1,1,64,2048]{3,2,1,0:T(8,128)(2,1)S(1)}) fusion(f32[1,8,64,2048]{3,2,1,0:T(8,128)} %get-tuple-element.33, s32[]{:T(128)S(6)} %select_n.233, bf16[1,8,64,2048]{3,2,1,0:T(8,128)(2,1)} %param.8, bf16[1,8,64,2048]{3,2,1,0:T(8,128)(2,1)} %param.7, ...), kind=kLoop, calls=%fused_computation.42 | loop fusion | flops 1703936 | bytes 2360340 | tf_op jit(solution)/shard_map/dynamic_update_slice | solution.py:212
  93.3 13.8 %orthogonalize.1 = bf16[1,512,2048]{2,1,0:T(8,128)(2,1)} custom-call(s32[1]{0:T(128)} %bitcast.12.refs_0_, bf16[1,64,2048]{2,1,0:T(8,128)(2,1)S(1)} %bitcast.40, bf16[1,64,2048]{2,1,0:T(8,128)(2,1)S(1)} %collective-permute-done.22.refs_2_, bf16[1,64,2048]{2,1,0:T(8,128)(2,1)S(1)} %collective-permute-done.23.refs_3_, ...), custom_call_target="tpu_custom_call" | custom-call | flops 11005853696 | bytes 4194304 | tf_op jit(solution)/shard_map/orthogonalize/pallas_call | solution.py:127
  107.1 4.3 %collective-permute-done.19 = bf16[4,1,64,2048]{3,2,1,0:T(8,128)(2,1)S(1)} collective-permute-done((bf16[4,1,64,2048]{3,2,1,0:T(8,128)(2,1)S(1)}, bf16[4,1,64,2048]{3,2,1,0:T(8,128)(2,1)S(1)}, u32[]{:S(2)}, u32[]{:S(2)}) %collective-permute-start.19) | collective-permute-done | bytes 1048608 | tf_op jit(solution)/shard_map/ppermute | solution.py:24
  111.4 3.6 %all-to-all-start = ((bf16[8,1,64,2048]{3,2,1,0:T(8,128)(2,1)}), bf16[8,1,64,2048]{3,2,1,0:T(8,128)(2,1)S(1)}, u32[]{:S(2)}, u32[]{:S(2)}) async-start(bf16[8,1,64,2048]{3,2,1,0:T(8,128)(2,1)} %bitcast.17), calls=%async_computation | async-start | bytes 4194304 | tf_op jit(solution)/shard_map/all_to_all | solution.py:225
  115.0 1.0 collective-permute-start.20
  116.0 19.9 %collective-permute-done.20 = bf16[4,1,64,2048]{3,2,1,0:T(8,128)(2,1)S(1)} collective-permute-done((bf16[4,1,64,2048]{3,2,1,0:T(8,128)(2,1)}, bf16[4,1,64,2048]{3,2,1,0:T(8,128)(2,1)S(1)}, u32[]{:S(2)}, u32[]{:S(2)}) %collective-permute-start.20) | collective-permute-done | bytes 1048608 | tf_op jit(solution)/shard_map/ppermute | solution.py:24
  135.9 3.0 %add_convert_fusion.2 = (bf16[4,1,64,2048]{3,2,1,0:T(8,128)(2,1)S(1)}, bf16[4,1,64,2048]{3,2,1,0:T(8,128)(2,1)S(1)}) fusion(bf16[4,1,64,2048]{3,2,1,0:T(8,128)(2,1)S(1)} %collective-permute-done.19, f32[]{:T(128)S(6)} %sub.155, f32[]{:T(128)} %bitcast, bf16[8,1,64,2048]{3,2,1,0:T(8,128)(2,1)} %copy-done.1, bf16[4,1,64,2048]{3,2,1,0:T(8,128)(2,1)S(1)} %collective-permute-done.20), kind=kLoop, calls=%fused_computation.5 | loop fusion | flops 6291456 | bytes 6291464 | tf_op jit(solution)/shard_map/convert_element_type | solution.py:228
  138.9 1.5 pad_maximum_fusion
  140.4 19.0 %all-to-all-done = bf16[8,1,64,2048]{3,2,1,0:T(8,128)(2,1)S(1)} async-done(((bf16[8,1,64,2048]{3,2,1,0:T(8,128)(2,1)}), bf16[8,1,64,2048]{3,2,1,0:T(8,128)(2,1)S(1)}, u32[]{:S(2)}, u32[]{:S(2)}) %all-to-all-start) | async-done | bytes 2097184 | tf_op jit(solution)/shard_map/all_to_all | solution.py:225
  159.4 3.7 %fusion = bf16[1,8,64,2048]{3,2,1,0:T(8,128)(2,1)} fusion(bf16[8,1,64,2048]{3,2,1,0:T(8,128)(2,1)S(1)} %all-to-all-done, bf16[8,1,64,2048]{3,2,1,0:T(8,128)(2,1)} %pad_maximum_fusion), kind=kLoop, calls=%fused_computation.2 | loop fusion | flops 5242880 | bytes 6291456 | tf_op jit(solution)/shard_map/reshape | solution.py:235
  163.1 1.3 copy.18
  (36 shorter events, 1.8 us)
Async XLA Ops:
  2.0 10.1 %collective-permute-start = (bf16[1,1,64,2048]{3,2,1,0:T(8,128)(2,1)S(1)}, bf16[1,1,64,2048]{3,2,1,0:T(8,128)(2,1)S(1)}, u32[]{:S(2)}, u32[]{:S(2)}) collective-permute-start(bf16[1,1,64,2048]{3,2,1,0:T(8,128)(2,1)S(1)} %get-tuple-element.59), channel_id=1, source_target_pairs={{0,16},{8,24},{16,0},{24,8},{1,17},{9,25},{17,1},{25,9},{2,18},{10... | collective-permute-start | bytes 786440 | tf_op jit(solution)/shard_map/ppermute | solution.py:24
  6.7 11.6 %collective-permute-start.2 = (bf16[2,1,64,2048]{3,2,1,0:T(8,128)(2,1)S(1)}, bf16[2,1,64,2048]{3,2,1,0:T(8,128)(2,1)S(1)}, u32[]{:S(2)}, u32[]{:S(2)}) collective-permute-start(bf16[2,1,64,2048]{3,2,1,0:T(8,128)(2,1)S(1)} %get-tuple-element.56), channel_id=1, source_target_pairs={{0,8},{8,0},{16,24},{24,16},{1,9},{9,1},{17,25},{25,17},{2,10},{10... | collective-permute-start | bytes 1572872 | tf_op jit(solution)/shard_map/ppermute | solution.py:24
  6.7 11.6 %collective-permute-start.8 = (bf16[2,1,64,2048]{3,2,1,0:T(8,128)(2,1)S(1)}, bf16[2,1,64,2048]{3,2,1,0:T(8,128)(2,1)S(1)}, u32[]{:S(2)}, u32[]{:S(2)}) collective-permute-start(bf16[2,1,64,2048]{3,2,1,0:T(8,128)(2,1)S(1)} %get-tuple-element.57), channel_id=1, source_target_pairs={{0,8},{8,0},{16,24},{24,16},{1,9},{9,1},{17,25},{25,17},{2,10},{10... | collective-permute-start | bytes 1572872 | tf_op jit(solution)/shard_map/ppermute | solution.py:24
  7.2 11.1 %collective-permute-start.7 = (bf16[1,1,64,2048]{3,2,1,0:T(8,128)(2,1)S(1)}, bf16[1,1,64,2048]{3,2,1,0:T(8,128)(2,1)}, u32[]{:S(2)}, u32[]{:S(2)}) collective-permute-start(bf16[1,1,64,2048]{3,2,1,0:T(8,128)(2,1)S(1)} %get-tuple-element.58), channel_id=1, source_target_pairs={{0,16},{8,24},{16,0},{24,8},{1,17},{9,25},{17,1},{25,9},{2,18},{10... | collective-permute-start | bytes 786440 | tf_op jit(solution)/shard_map/ppermute | solution.py:24
  12.1 6.2 %collective-permute-start.9 = (bf16[1,1,64,2048]{3,2,1,0:T(8,128)(2,1)S(1)}, bf16[1,1,64,2048]{3,2,1,0:T(8,128)(2,1)S(1)}, u32[]{:S(2)}, u32[]{:S(2)}) collective-permute-start(bf16[1,1,64,2048]{3,2,1,0:T(8,128)(2,1)S(1)} %collective-permute-done), channel_id=1, source_target_pairs={{0,8},{8,0},{16,24},{24,16},{1,9},{9,1},{17,25},{25,17},{2,10},{10... | collective-permute-start | bytes 786440 | tf_op jit(solution)/shard_map/ppermute | solution.py:24
  15.1 4.0 %copy-start = (f32[1,8,64,2048]{3,2,1,0:T(8,128)S(1)}, f32[1,8,64,2048]{3,2,1,0:T(8,128)}, u32[]{:S(2)}) copy-start(f32[1,8,64,2048]{3,2,1,0:T(8,128)} %param.6) | copy-start | bytes 12582916
  17.8 15.2 %collective-permute-start.1 = (bf16[2,1,64,2048]{3,2,1,0:T(8,128)(2,1)S(1)}, bf16[2,1,64,2048]{3,2,1,0:T(8,128)(2,1)S(1)}, u32[]{:S(2)}, u32[]{:S(2)}) collective-permute-start(bf16[2,1,64,2048]{3,2,1,0:T(8,128)(2,1)S(1)} %get-tuple-element.54), channel_id=1, source_target_pairs={{0,8},{8,0},{16,24},{24,16},{1,9},{9,1},{17,25},{25,17},{2,10},{10... | collective-permute-start | bytes 1572872 | tf_op jit(solution)/shard_map/ppermute | solution.py:24
  18.3 10.7 %collective-permute-start.12 = (bf16[1,1,64,2048]{3,2,1,0:T(8,128)(2,1)}, bf16[1,1,64,2048]{3,2,1,0:T(8,128)(2,1)S(1)}, u32[]{:S(2)}, u32[]{:S(2)}) collective-permute-start(bf16[1,1,64,2048]{3,2,1,0:T(8,128)(2,1)} %collective-permute-done.7), channel_id=1, source_target_pairs={{0,8},{8,0},{16,24},{24,16},{1,9},{9,1},{17,25},{25,17},{2,10},{10... | collective-permute-start | bytes 786440 | tf_op jit(solution)/shard_map/ppermute | solution.py:24
  18.3 0.8 copy-start.5
  22.3 20.5 %copy-start.3 = (bf16[1,8,64,2048]{3,2,1,0:T(8,128)(2,1)S(1)}, bf16[1,8,64,2048]{3,2,1,0:T(8,128)(2,1)}, u32[]{:S(2)}) copy-start(bf16[1,8,64,2048]{3,2,1,0:T(8,128)(2,1)} %param.5) | copy-start | bytes 6291460
  22.3 12.0 %collective-permute-start.3 = (bf16[1,1,64,2048]{3,2,1,0:T(8,128)(2,1)S(1)}, bf16[1,1,64,2048]{3,2,1,0:T(8,128)(2,1)S(1)}, u32[]{:S(2)}, u32[]{:S(2)}) collective-permute-start(bf16[1,1,64,2048]{3,2,1,0:T(8,128)(2,1)S(1)} %get-tuple-element.18), channel_id=1, source_target_pairs={{0,16},{8,24},{16,0},{24,8},{1,17},{9,25},{17,1},{25,9},{2,18},{10... | collective-permute-start | bytes 786440 | tf_op jit(solution)/shard_map/ppermute | solution.py:24
  24.4 13.7 %collective-permute-start.10 = (bf16[1,64,2048]{2,1,0:T(8,128)(2,1)S(1)}, bf16[1,64,2048]{2,1,0:T(8,128)(2,1)S(1)}, u32[]{:S(2)}, u32[]{:S(2)}) collective-permute-start(bf16[1,64,2048]{2,1,0:T(8,128)(2,1)S(1)} %bitcast.50), channel_id=1, source_target_pairs={{0,7},{1,6},{2,5},{3,4},{4,3},{5,2},{6,1},{7,0},{8,15},{9,14},{10,... | collective-permute-start | bytes 786440 | tf_op jit(solution)/shard_map/ppermute | solution.py:24
  33.0 8.7 %copy-start.4 = (bf16[2,1,64,2048]{3,2,1,0:T(8,128)(2,1)}, bf16[2,1,64,2048]{3,2,1,0:T(8,128)(2,1)S(1)}, u32[]{:S(2)}) copy-start(bf16[2,1,64,2048]{3,2,1,0:T(8,128)(2,1)S(1)} %collective-permute-done.1) | copy-start | bytes 1572868
  34.3 8.5 %collective-permute-start.4 = (bf16[1,1,64,2048]{3,2,1,0:T(8,128)(2,1)}, bf16[1,1,64,2048]{3,2,1,0:T(8,128)(2,1)}, u32[]{:S(2)}, u32[]{:S(2)}) collective-permute-start(bf16[1,1,64,2048]{3,2,1,0:T(8,128)(2,1)} %fusion.3), channel_id=1, source_target_pairs={{0,16},{8,24},{16,0},{24,8},{1,17},{9,25},{17,1},{25,9},{2,18},{10... | collective-permute-start | bytes 786440 | tf_op jit(solution)/shard_map/ppermute | solution.py:24
  38.1 2.0 %copy-start.2 = (f32[1,8,64,2048]{3,2,1,0:T(8,128)}, f32[1,8,64,2048]{3,2,1,0:T(8,128)S(1)}, u32[]{:S(2)}) copy-start(f32[1,8,64,2048]{3,2,1,0:T(8,128)S(1)} %get-tuple-element.41) | copy-start | bytes 12582916
  40.1 8.2 %collective-permute-start.11 = (bf16[1,1,64,2048]{3,2,1,0:T(8,128)(2,1)}, bf16[1,1,64,2048]{3,2,1,0:T(8,128)(2,1)}, u32[]{:S(2)}, u32[]{:S(2)}) collective-permute-start(bf16[1,1,64,2048]{3,2,1,0:T(8,128)(2,1)} %get-tuple-element.22), channel_id=1, source_target_pairs={{0,16},{8,24},{16,0},{24,8},{1,17},{9,25},{17,1},{25,9},{2,18},{10... | collective-permute-start | bytes 786440 | tf_op jit(solution)/shard_map/ppermute | solution.py:24
  41.6 17.9 %collective-permute-start.6 = (bf16[2,1,64,2048]{3,2,1,0:T(8,128)(2,1)}, bf16[2,1,64,2048]{3,2,1,0:T(8,128)(2,1)}, u32[]{:S(2)}, u32[]{:S(2)}) collective-permute-start(bf16[2,1,64,2048]{3,2,1,0:T(8,128)(2,1)} %get-tuple-element.53), channel_id=1, source_target_pairs={{0,8},{8,0},{16,24},{24,16},{1,9},{9,1},{17,25},{25,17},{2,10},{10... | collective-permute-start | bytes 1572872 | tf_op jit(solution)/shard_map/ppermute | solution.py:24
  41.6 14.0 %collective-permute-start.13 = (bf16[1,64,2048]{2,1,0:T(8,128)(2,1)}, bf16[1,64,2048]{2,1,0:T(8,128)(2,1)S(1)}, u32[]{:S(2)}, u32[]{:S(2)}) collective-permute-start(bf16[1,64,2048]{2,1,0:T(8,128)(2,1)} %bitcast.53), channel_id=1, source_target_pairs={{0,6},{1,7},{2,4},{3,5},{4,2},{5,3},{6,0},{7,1},{8,14},{9,15},{10,... | collective-permute-start | bytes 786440 | tf_op jit(solution)/shard_map/ppermute | solution.py:24
  42.8 42.7 %collective-permute-start.5 = (bf16[8,1,64,2048]{3,2,1,0:T(8,128)(2,1)S(1)}, bf16[8,1,64,2048]{3,2,1,0:T(8,128)(2,1)}, u32[]{:S(2)}, u32[]{:S(2)}) collective-permute-start(bf16[8,1,64,2048]{3,2,1,0:T(8,128)(2,1)S(1)} %bitcast.48), channel_id=1, source_target_pairs={{0,8},{8,0},{16,24},{24,16},{1,9},{9,1},{17,25},{25,17},{2,10},{10... | collective-permute-start | bytes 6291464 | tf_op jit(solution)/shard_map/ppermute | solution.py:24
  55.7 7.1 %collective-permute-start.14 = (bf16[1,1,64,2048]{3,2,1,0:T(8,128)(2,1)S(1)}, bf16[1,1,64,2048]{3,2,1,0:T(8,128)(2,1)}, u32[]{:S(2)}, u32[]{:S(2)}) collective-permute-start(bf16[1,1,64,2048]{3,2,1,0:T(8,128)(2,1)S(1)} %get-tuple-element.24), channel_id=1, source_target_pairs={{0,16},{8,24},{16,0},{24,8},{1,17},{9,25},{17,1},{25,9},{2,18},{10... | collective-permute-start | bytes 786440 | tf_op jit(solution)/shard_map/ppermute | solution.py:24
  57.1 14.3 %collective-permute-start.15 = (bf16[1,64,2048]{2,1,0:T(8,128)(2,1)}, bf16[1,64,2048]{2,1,0:T(8,128)(2,1)S(1)}, u32[]{:S(2)}, u32[]{:S(2)}) collective-permute-start(bf16[1,64,2048]{2,1,0:T(8,128)(2,1)} %bitcast.51), channel_id=1, source_target_pairs={{0,5},{1,4},{2,7},{3,6},{4,1},{5,0},{6,3},{7,2},{8,13},{9,12},{10,... | collective-permute-start | bytes 786440 | tf_op jit(solution)/shard_map/ppermute | solution.py:24
  67.0 6.9 %collective-permute-start.21 = (bf16[1,1,64,2048]{3,2,1,0:T(8,128)(2,1)}, bf16[1,1,64,2048]{3,2,1,0:T(8,128)(2,1)}, u32[]{:S(2)}, u32[]{:S(2)}) collective-permute-start(bf16[1,1,64,2048]{3,2,1,0:T(8,128)(2,1)} %get-tuple-element.29), channel_id=1, source_target_pairs={{0,16},{8,24},{16,0},{24,8},{1,17},{9,25},{17,1},{25,9},{2,18},{10... | collective-permute-start | bytes 786440 | tf_op jit(solution)/shard_map/ppermute | solution.py:24
  68.4 13.4 %collective-permute-start.17 = (bf16[1,64,2048]{2,1,0:T(8,128)(2,1)}, bf16[1,64,2048]{2,1,0:T(8,128)(2,1)S(1)}, u32[]{:S(2)}, u32[]{:S(2)}) collective-permute-start(bf16[1,64,2048]{2,1,0:T(8,128)(2,1)} %bitcast.55), channel_id=1, source_target_pairs={{0,4},{1,5},{2,6},{3,7},{4,0},{5,1},{6,2},{7,3},{8,12},{9,13},{10,... | collective-permute-start | bytes 786440 | tf_op jit(solution)/shard_map/ppermute | solution.py:24
  70.8 14.7 %collective-permute-start.18 = (bf16[1,64,2048]{2,1,0:T(8,128)(2,1)S(1)}, bf16[1,64,2048]{2,1,0:T(8,128)(2,1)S(1)}, u32[]{:S(2)}, u32[]{:S(2)}) collective-permute-start(bf16[1,64,2048]{2,1,0:T(8,128)(2,1)S(1)} %bitcast.52), channel_id=1, source_target_pairs={{0,3},{1,2},{2,1},{3,0},{4,7},{5,6},{6,5},{7,4},{8,11},{9,10},{10,... | collective-permute-start | bytes 786440 | tf_op jit(solution)/shard_map/ppermute | solution.py:24
  71.4 14.0 %collective-permute-start.16 = (bf16[1,1,64,2048]{3,2,1,0:T(8,128)(2,1)}, bf16[1,1,64,2048]{3,2,1,0:T(8,128)(2,1)S(1)}, u32[]{:S(2)}, u32[]{:S(2)}) collective-permute-start(bf16[1,1,64,2048]{3,2,1,0:T(8,128)(2,1)} %get-tuple-element.26), channel_id=1, source_target_pairs={{0,16},{8,24},{16,0},{24,8},{1,17},{9,25},{17,1},{25,9},{2,18},{10... | collective-permute-start | bytes 786440 | tf_op jit(solution)/shard_map/ppermute | solution.py:24
  73.8 19.5 %collective-permute-start.23 = (bf16[1,64,2048]{2,1,0:T(8,128)(2,1)S(1)}, bf16[1,64,2048]{2,1,0:T(8,128)(2,1)S(1)}, u32[]{:S(2)}, u32[]{:S(2)}) collective-permute-start(bf16[1,64,2048]{2,1,0:T(8,128)(2,1)S(1)} %bitcast.54), channel_id=1, source_target_pairs={{0,2},{1,3},{2,0},{3,1},{4,6},{5,7},{6,4},{7,5},{8,10},{9,11},{10,... | collective-permute-start | bytes 786440 | tf_op jit(solution)/shard_map/ppermute | solution.py:24
  81.8 11.5 %collective-permute-start.22 = (bf16[1,64,2048]{2,1,0:T(8,128)(2,1)S(1)}, bf16[1,64,2048]{2,1,0:T(8,128)(2,1)S(1)}, u32[]{:S(2)}, u32[]{:S(2)}) collective-permute-start(bf16[1,64,2048]{2,1,0:T(8,128)(2,1)S(1)} %bitcast.56), channel_id=1, source_target_pairs={{0,1},{1,0},{2,3},{3,2},{4,5},{5,4},{6,7},{7,6},{8,9},{9,8},{10,11... | collective-permute-start | bytes 786440 | tf_op jit(solution)/shard_map/ppermute | solution.py:24
  88.5 4.9 %copy-start.1 = (bf16[8,1,64,2048]{3,2,1,0:T(8,128)(2,1)}, bf16[8,1,64,2048]{3,2,1,0:T(8,128)(2,1)S(1)}, u32[]{:S(2)}) copy-start(bf16[8,1,64,2048]{3,2,1,0:T(8,128)(2,1)S(1)} %add_convert_fusion) | copy-start | bytes 6291460
  89.8 21.6 %collective-permute-start.19 = (bf16[4,1,64,2048]{3,2,1,0:T(8,128)(2,1)S(1)}, bf16[4,1,64,2048]{3,2,1,0:T(8,128)(2,1)S(1)}, u32[]{:S(2)}, u32[]{:S(2)}) collective-permute-start(bf16[4,1,64,2048]{3,2,1,0:T(8,128)(2,1)S(1)} %get-tuple-element.63), channel_id=1, source_target_pairs={{0,16},{8,24},{16,0},{24,8},{1,17},{9,25},{17,1},{25,9},{2,18},{10... | collective-permute-start | bytes 3145736 | tf_op jit(solution)/shard_map/ppermute | solution.py:24
  111.4 48.0 %all-to-all-start = ((bf16[8,1,64,2048]{3,2,1,0:T(8,128)(2,1)}), bf16[8,1,64,2048]{3,2,1,0:T(8,128)(2,1)S(1)}, u32[]{:S(2)}, u32[]{:S(2)}) async-start(bf16[8,1,64,2048]{3,2,1,0:T(8,128)(2,1)} %bitcast.17), calls=%async_computation | async-start | bytes 4194304 | tf_op jit(solution)/shard_map/all_to_all | solution.py:225
  115.0 20.9 %collective-permute-start.20 = (bf16[4,1,64,2048]{3,2,1,0:T(8,128)(2,1)}, bf16[4,1,64,2048]{3,2,1,0:T(8,128)(2,1)S(1)}, u32[]{:S(2)}, u32[]{:S(2)}) collective-permute-start(bf16[4,1,64,2048]{3,2,1,0:T(8,128)(2,1)} %get-tuple-element.62), channel_id=1, source_target_pairs={{0,16},{8,24},{16,0},{24,8},{1,17},{9,25},{17,1},{25,9},{2,18},{10... | collective-permute-start | bytes 3145736 | tf_op jit(solution)/shard_map/ppermute | solution.py:24

commit v5 on v3

--- a/solution.py
+++ b/solution.py
@@ -147,11 +147,171 @@
     )(here.reshape(1), *blocks)
 
 
+def block_of(array, index):
+    tail = array.shape[1:]
+    return pl.BlockSpec((1,) + tail, lambda *args: (index(*args),) + (0,) * len(tail))
+
+
+def in_hbm(array):
+    return pltpu.with_memory_space_constraint(array, pltpu.HBM)
+
+
+def run(body, name, steps, picks, operands, outs):
+    return pl.pallas_call(
+        body,
+        grid_spec=pltpu.PrefetchScalarGridSpec(
+            num_scalar_prefetch=1,
+            grid=(steps,),
+            in_specs=[
+                pl.BlockSpec(memory_space=pltpu.SMEM) if index is None else block_of(array, index)
+                for array, index in operands
+            ],
+            out_specs=[block_of(shape, index) for shape, index in outs],
+        ),
+        out_shape=[shape for shape, _ in outs],
+        compiler_params=params(24),
+        cost_estimate=cost(
+            sum(array.size for array, _ in operands),
+            sum(array.size * array.dtype.itemsize for array, _ in operands + outs),
+        ),
+        name=name,
+    )(picks, *(array for array, _ in operands))
+
+
+def by_step(step, picks):
+    return step
+
+
+def by_pick(step, picks):
+    return picks[step]
+
+
+def within(start, length):
+    return lambda step, picks: jnp.clip(step - start, 0, length - 1)
+
+
+def like(array, dtype, leading):
+    return jax.ShapeDtypeStruct((leading,) + array.shape[1:], dtype)
+
+
+def gather_body(picks, own, out):
+    out[...] = own[...].astype(BF16)
+
+
+def gather(picks, tracker):
+    steps = picks.shape[0]
+    return run(
+        gather_body, "gather", steps, picks,
+        [(in_hbm(tracker), by_pick)], [(like(tracker, BF16, steps), by_step)],
+    )[0]
+
+
+def base_body(picks, share, own, near, grad_new, grad_old, base, *sends):
+    mixed = share[0] * own[...] + share[1] * near[...].astype(F32)
+    base[...] = share[3] * mixed + (grad_new[...].astype(F32) - grad_old[...].astype(F32))
+    sent = mixed.astype(BF16)
+    for turn, send in enumerate(sends):
+        @pl.when(pl.program_id(0) // 2 == turn)
+        def _():
+            send[...] = sent
+
+
+def make_base(picks, share, tracker, near, grad_new, grad_old):
+    steps = picks.shape[0]
+    base, *sends = run(
+        base_body, "base", steps, picks,
+        [(share, None), (in_hbm(tracker), by_pick), (near, by_step)]
+        + [(in_hbm(grad_new), by_pick), (in_hbm(grad_old), by_pick)],
+        [(like(tracker, F32, steps), by_step)]
+        + [(like(tracker, BF16, 2), within(start, 2)) for start in range(0, steps, 2)],
+    )
+    return base, sends
+
+
+def place_body(count, picks, share, *refs):
+    *leads, base = refs[: count + 1]
+    fars, out = refs[count + 1 : -1], refs[-1]
+    step = pl.program_id(0)
+    for turn, lead in enumerate(leads):
+        @pl.when(step == turn)
+        def _():
+            out[...] = lead[...]
+    for turn, far in enumerate(fars):
+        @pl.when((step >= count) & ((step - count) // 2 == turn))
+        def _():
+            out[...] = base[...] + share[4] * far[...].astype(F32)
+
+
+def place_tracker(picks, share, leads, base, fars):
+    steps, count = picks.shape[0], len(leads)
+    return run(
+        lambda *refs: place_body(count, *refs), "place", steps, picks,
+        [(share, None)]
+        + [(lead, within(turn, 1)) for turn, lead in enumerate(leads)]
+        + [(base, within(count, steps - count))]
+        + [(far, within(count + 2 * turn, 2)) for turn, far in enumerate(fars)],
+        [(like(base, F32, steps), by_pick)],
+    )[0]
+
+
+def first_weight_body(picks, share, own, near, *outs):
+    mixed = share[0] * own[...].astype(F32) + share[1] * near[...].astype(F32)
+    for turn, out in enumerate(outs):
+        @pl.when(pl.program_id(0) // 4 == turn)
+        def _():
+            out[...] = mixed.astype(BF16)
+
+
+def first_weight(picks, share, weight, near):
+    return run(
+        first_weight_body, "first_weight", 8, picks,
+        [(share, None), (in_hbm(weight), by_step), (near, by_step)],
+        [(like(weight, BF16, 4), within(start, 4)) for start in (0, 4)],
+    )
+
+
+def second_weight_body(picks, share, *refs):
+    out = refs[-1]
+    for turn in range(2):
+        @pl.when(pl.program_id(0) // 4 == turn)
+        def _():
+            own, far = refs[turn][...].astype(F32), refs[2 + turn][...].astype(F32)
+            out[...] = (share[3] * own + share[4] * far).astype(BF16)
+
+
+def second_weight(picks, share, owns, fars):
+    halves = [(half, within(4 * turn, 4)) for turn, half in enumerate(owns)]
+    halves += [(half, within(4 * turn, 4)) for turn, half in enumerate(fars)]
+    return run(
+        second_weight_body, "second_weight", 8, picks,
+        [(share, None)] + halves, [(like(owns[0], BF16, 8), by_step)],
+    )[0]
+
+
+def settle_body(picks, mixed, update, weight_out, update_out):
+    taken = update[...]
+    weight_out[...] = (mixed[...].astype(F32) - learn_rate * taken.astype(F32)).astype(BF16)
+    update_out[...] = taken
+
+
+def settle(picks, mixed, update):
+    kept = like(mixed, BF16, 8)
+    return run(
+        settle_body, "settle", 8, picks,
+        [(mixed, by_step), (update, by_step)], [(kept, by_step), (kept, by_step)],
+    )
+
+
+def after(values, *others):
+    return lax.optimization_barrier((values, others))[0]
+
+
 def local(weight, tracker, grad_new, grad_old, mix_keep):
     shards = lax.axis_size("shard")
     _, experts, rows, columns = tracker.shape
     each = experts // shards
-    shape = (shards, each, rows, columns)
+    length = shards // 8
+    shape = (8, length, each, rows, columns)
     weight, tracker, grad_new, grad_old = (
         values.reshape(shape) for values in (weight, tracker, grad_new, grad_old)
     )
@@ -159,68 +319,76 @@
     rep_index = lax.axis_index("rep")
     keep = mix_keep.astype(F32) / 16.0
     first, second = keep[rep_index, 0], keep[rep_index, 1]
-
-    unit = shards // 8 if shards % 8 == 0 else 0
-    if unit:
-        groups = [(low * unit, count * unit) for low, count in ((7, 1), (6, 1), (2, 2), (4, 2), (0, 2))]
-        lead = (6 * unit, 2 * unit)
-    else:
-        groups = [(0, shards)]
-        lead = groups[0]
-
-    def place(lowest, length):
-        return (here ^ lowest) // length * length
-
-    def taken(values, lowest, length, start=0):
-        return lax.dynamic_slice_in_dim(values, place(lowest, length) - start, length, axis=0)
-
-    def blend(own, near):
-        return first * own + (1.0 - first) * near.astype(F32)
-
-    own = taken(tracker, *lead)
-    lead_mixed = blend(own, swapped(own.astype(BF16), "rep", 1))
-    lead_sent = lead_mixed.astype(BF16)
-    tracker, lead_sent = lax.optimization_barrier((tracker, lead_sent))
-    near = swapped(tracker.astype(BF16), "rep", 1)
-
-    new_tracker = jnp.zeros(shape, F32)
+    far_first = keep[rep_index ^ 2, 0]
+    share = jnp.stack([first, 1.0 - first, far_first, second, 1.0 - second])
+
+    order = (7, 6, 5, 4, 3, 2, 1, 0)
+    picks = jnp.array(order, jnp.int32) ^ (here // length)
+
+    def taken(values, turn):
+        return lax.dynamic_slice_in_dim(values, picks[turn], 1, axis=0)
+
     blocks = [None] * shards
-    arrived = []
-    for turn, (lowest, length) in enumerate(groups):
-        if lead[0] <= lowest < lead[0] + lead[1]:
-            mixed = taken(lead_mixed, lowest, length, place(*lead))
-            sent = taken(lead_sent, lowest, length, place(*lead))
-        else:
-            mixed = blend(taken(tracker, lowest, length), taken(near, lowest, length))
-            waits = arrived[0] if turn == 2 else blocks[groups[turn - 3][0]]
-            sent, _ = lax.optimization_barrier((mixed.astype(BF16), waits))
+    ready = []
+
+    def spread(part, group):
+        part = part.astype(BF16).reshape(shape[1:])
+        ready.append(part)
+        for offset in reversed(range(group * length, (group + 1) * length)):
+            block = part[0]
+            if length > 1:
+                block = lax.dynamic_index_in_dim(part, (here ^ offset) % length, 0, False)
+            blocks[offset] = swapped(block, "shard", offset) if offset else block
+
+    leads = [taken(tracker, turn).astype(BF16) for turn in range(2)]
+    lead_fars = [swapped(lead, "rep", 2) for lead in leads]
+    lead_nears = [swapped(lead, "rep", 1) for lead in leads]
+    near = swapped(gather(picks[2:], after(tracker, leads)), "rep", 1)
+    base, sends = make_base(picks[2:], share, tracker, near, grad_new, grad_old)
+
+    lead_parts = []
+    for turn in range(2):
+        far = lead_fars[turn]
+        mixed = first * taken(tracker, turn) + (1.0 - first) * lead_nears[turn].astype(F32)
+        far_mixed = far_first * far.astype(F32)
+        far_mixed += (1.0 - far_first) * swapped(far, "rep", 1).astype(F32)
+        part = second * mixed + (1.0 - second) * far_mixed
+        part += taken(grad_new, turn).astype(F32) - taken(grad_old, turn).astype(F32)
+        lead_parts.append(part)
+        spread(part, order[turn])
+
+    halves = None
+    arrived = list(lead_fars)
+    fars = []
+    for turn, sent in enumerate(sends):
+        sent = after(sent, arrived[turn])
+        if turn > 0:
+            sent = after(sent, blocks[order[turn - 1] * length], ready[-1])
         far = swapped(sent, "rep", 2)
         arrived.append(far)
-        part = second * mixed + (1.0 - second) * far.astype(F32)
-        part += taken(grad_new, lowest, length).astype(F32)
-        part -= taken(grad_old, lowest, length).astype(F32)
-        for offset in reversed(range(lowest, lowest + length)):
-            block = lax.dynamic_index_in_dim(part, (here ^ offset) % length, 0, False)
-            block = block.astype(BF16)
-            blocks[offset] = swapped(block, "shard", offset) if offset else block
-        new_tracker = lax.dynamic_update_slice_in_dim(
-            new_tracker, part, place(lowest, length), axis=0
-        )
-
-    weight, _ = lax.optimization_barrier((weight, arrived[len(groups) // 2]))
-    weight_near = swapped(weight, "rep", 1)
-    weight_own = blend(weight.astype(F32), weight_near).astype(BF16)
-    weight_own, _ = lax.optimization_barrier((weight_own, arrived[-1]))
-    weight_far = swapped(weight_own, "rep", 2)
-    mixed_weight = (
-        second * weight_own.astype(F32) + (1.0 - second) * weight_far.astype(F32)
-    ).astype(BF16)
+        if turn == 1:
+            weight_near = swapped(after(weight, arrived[1]), "rep", 1)
+            halves = first_weight(picks, share, weight, weight_near)
+        if turn == 2:
+            far = after(far, blocks[order[2] * length], halves[0])
+        if turn > 0:
+            far = after(far, ready[-1])
+        fars.append(far)
+        for step in range(2):
+            part = base[2 * turn + step] + (1.0 - second) * far[step].astype(F32)
+            spread(part, order[2 + 2 * turn + step])
+
+    halves = [after(half, arrived[-1]) for half in halves]
+    halves_far = [swapped(half, "rep", 2) for half in halves]
 
     scale = 0.2 * math.sqrt(max(shards * rows, columns))
     update = orthogonalize(blocks, here, scale)
+    update = after(update, halves_far[0])
     update = update.reshape(each, shards, rows, columns).swapaxes(0, 1)
     update = lax.all_to_all(update, "shard", split_axis=0, concat_axis=0, tiled=True)
-    new_weight = (mixed_weight.astype(F32) - learn_rate * update.astype(F32)).astype(BF16)
+    new_tracker = place_tracker(picks, share, lead_parts, base, fars)
+    mixed_weight = second_weight(picks, share, halves, halves_far)
+    new_weight, update = settle(picks, mixed_weight, update.reshape(shape))
     shape = (1, experts, rows, columns)
     return new_weight.reshape(shape), new_tracker.reshape(shape), update.reshape(shape)
 

time: 176 us -> 184 us (1.045)
  Pallas kernels: 13.6 us -> 44.4 us
  other arithmetic: 37.3 us -> 7.67 us
  waiting for transfers between devices: 88.8 us -> 71.3 us
  local copies, waits for them, and re-layouts: 7.51 us -> 17.7 us
  starting transfers between devices: 26.1 us -> 35.5 us
  between operations: 2.1 us -> 6.7 us
    pallas_call x0 -> x6, Pallas kernels: none -> 30.6 us  [run(): pl.pallas_call(body, grid_spec=pltpu.PrefetchScalarGridSpec(num_scalar_pr...]
    all_to_all x1, waiting for transfers between devices: 38.6 us -> 20.5 us  [local(): lax.all_to_all(update, 'shard', split_axis=0, concat_axis=0, tiled=True)]
    convert_element_type x6 -> x3, other arithmetic: 18.5 us -> 1.52 us  [spread(): part = part.astype(BF16).reshape(shape[1:])]
    dynamic_update_slice x3 -> x0, other arithmetic: 12.3 us -> none  [local(): lax.dynamic_update_slice_in_dim(new_tracker, part, place(lowest, length),...]
    unnamed x7 -> x40, local copies, waits for them, and re-layouts: 3.11 us -> 12.2 us
    ppermute x16 -> x20, starting transfers between devices: 22.3 us -> 31.2 us  [swapped(): lax.ppermute(values, axis, [(i, i ^ offset) for i in range(lax.axis_size(...]
    reshape x1 -> x0, other arithmetic: 5.82 us -> none  [local(): new_weight.reshape(shape)]
    another operation x0 -> x1, other arithmetic: none -> 5.48 us  [spread(): block = part[0]]
  transfers between devices with their start and end apart: 17 -> 21, of which waited for: 11 -> 11; matrix products, arithmetic and copies ran while one was open for 14% -> 5% of each run, Pallas kernels for 8% -> 18%
where the time goes in v5:
time: 184 us; the launch traced here: 183 us
  waiting for transfers between devices  71.3 us (39%)
  Pallas kernels  44.4 us (24%)
  starting transfers between devices  35.5 us (19%)
  local copies, waits for them, and re-layouts  17.7 us (10%)
  other arithmetic  7.67 us (4%)
  between operations  6.7 us (4%)
    ppermute x20, waiting for transfers between devices, swapped(): lax.ppermute(values, axis, [(i, i ^ offset) for i in range(lax.axis_size(...  50.8 us
    ppermute x20, starting transfers between devices, swapped(): lax.ppermute(values, axis, [(i, i ^ offset) for i in range(lax.axis_size(...  31.2 us
    pallas_call x6, Pallas kernels, run(): pl.pallas_call(body, grid_spec=pltpu.PrefetchScalarGridSpec(num_scalar_pr...  30.6 us
    all_to_all x1, waiting for transfers between devices, local(): lax.all_to_all(update, 'shard', split_axis=0, concat_axis=0, tiled=True)  20.5 us
    pallas_call x1, Pallas kernels, orthogonalize(): pl.pallas_call(body, grid_spec=pltpu.PrefetchScalarGridSpec(num_scalar_pr...  13.8 us
    unnamed x40, local copies, waits for them, and re-layouts  12.2 us
    another operation x1, other arithmetic, spread(): block = part[0]  5.48 us
    all_to_all x1, starting transfers between devices, local(): lax.all_to_all(update, 'shard', split_axis=0, concat_axis=0, tiled=True)  4.34 us
  transfers between devices with their start and end apart: 21, of which 11 were waited for; matrix products, arithmetic and copies ran while one was open for 5% of the time, Pallas kernels for 18%

profile of v5, /device:TPU:0, one launch (start us, length us, event | category | flops | bytes accessed | tf_op | source)
XLA Modules:
  0.0 183.3 jit_solution(7516150505447929978)
XLA Ops:
  0.6 0.7 broadcast_xor_fusion.picks.refs_0_
  1.3 0.6 fusion.10
  5.8 2.1 %fusion.5 = (bf16[1,1,1,64,2048]{4,3,2,1,0:T(8,128)(2,1)}, bf16[1,1,1,64,2048]{4,3,2,1,0:T(8,128)(2,1)}) fusion(f32[1,8,64,2048]{3,2,1,0:T(8,128)} %param.7, s32[]{:T(128)S(6)} %select_n.25, s32[]{:T(128)S(6)} %select_n.24), kind=kLoop, calls=%fused_computation.17 | loop fusion | bytes 1048584 | tf_op jit(solution)/shard_map/convert_element_type | solution.py:343
  7.9 4.0 %gather.1 = bf16[6,1,1,64,2048]{4,3,2,1,0:T(8,128)(2,1)S(1)} custom-call(s32[6]{0:T(128)S(1)} %slice.53.picks, f32[8,1,1,64,2048]{4,3,2,1,0:T(8,128)} %bitcast.67), custom_call_target="tpu_custom_call" | custom-call | flops 1048576 | bytes 5767168 | tf_op jit(solution)/shard_map/gather/pallas_call | solution.py:160
  12.5 2.6 %collective-permute-start = (bf16[1,1,1,64,2048]{4,3,2,1,0:T(8,128)(2,1)}, bf16[1,1,1,64,2048]{4,3,2,1,0:T(8,128)(2,1)S(1)}, u32[]{:S(2)}, u32[]{:S(2)}) collective-permute-start(bf16[1,1,1,64,2048]{4,3,2,1,0:T(8,128)(2,1)} %get-tuple-element.52), channel_id=1, source_target_pairs={{0,16},{8,24},{16,0},{24,8},{1,17},{9,25},{17,1},{25,9},{2,18},{10... | collective-permute-start | bytes 786440 | tf_op jit(solution)/shard_map/ppermute | solution.py:24
  15.6 6.8 %collective-permute-done = bf16[1,1,1,64,2048]{4,3,2,1,0:T(8,128)(2,1)S(1)} collective-permute-done((bf16[1,1,1,64,2048]{4,3,2,1,0:T(8,128)(2,1)}, bf16[1,1,1,64,2048]{4,3,2,1,0:T(8,128)(2,1)S(1)}, u32[]{:S(2)}, u32[]{:S(2)}) %collective-permute-start) | collective-permute-done | bytes 262176 | tf_op jit(solution)/shard_map/ppermute | solution.py:24
  22.4 5.5 %collective-permute-done.3 = bf16[1,1,1,64,2048]{4,3,2,1,0:T(8,128)(2,1)} collective-permute-done((bf16[1,1,1,64,2048]{4,3,2,1,0:T(8,128)(2,1)}, bf16[1,1,1,64,2048]{4,3,2,1,0:T(8,128)(2,1)}, u32[]{:S(2)}, u32[]{:S(2)}) %collective-permute-start.3) | collective-permute-done | bytes 262176 | tf_op jit(solution)/shard_map/ppermute | solution.py:24
  27.9 0.7 constant_dynamic-slice_fusion.2
  29.9 2.1 %stack.11.share.refs_1_ = f32[5]{0:T(128)S(1)} concatenate(f32[1]{0:T(128)} %bitcast, f32[1]{0:T(128)} %bitcast.2, f32[1]{0:T(128)} %bitcast.3, f32[1]{0:T(128)} %bitcast.4, f32[1]{0:T(128)} %bitcast.6), dimensions={0} | concatenate | bytes 40 | tf_op jit(solution)/shard_map/stack | solution.py:323
  31.9 1.1 copy-done.7
  33.1 1.4 copy-done.8
  34.5 6.3 %base.1 = (f32[6,1,1,64,2048]{4,3,2,1,0:T(8,128)S(1)}, bf16[2,1,1,64,2048]{4,3,2,1,0:T(8,128)(2,1)}, bf16[2,1,1,64,2048]{4,3,2,1,0:T(8,128)(2,1)S(1)}, bf16[2,1,1,64,2048]{4,3,2,1,0:T(8,128)(2,1)S(1)}) custom-call(s32[6]{0:T(128)S(1)} %slice.53.picks, f32[5]{0:T(128)S(1)} %stack.11.share.refs_1_, f32[8,1,1,64,2048]{4,3,2,1,0:T(8,128)} %bitcast.68, ...), custom_call_target="tpu_custom_call" | custom-call | flops 3932165 | bytes 14680084 | tf_op jit(solution)/shard_map/base/pallas_call | solution.py:160
  40.8 0.8 copy-done.15
  41.6 0.8 copy-done.17
  42.4 1.8 collective-permute-start.4
  45.1 5.5 %convert_bitcast_fusion = (bf16[1,64,2048]{2,1,0:T(8,128)(2,1)S(1)}, f32[1,1,1,64,2048]{4,3,2,1,0:T(8,128)}, bf16[1,64,2048]{2,1,0:T(8,128)(2,1)S(1)}, f32[1,1,1,64,2048]{4,3,2,1,0:T(8,128)}) fusion(bf16[1,8,64,2048]{3,2,1,0:T(8,128)(2,1)} %param.9, s32[]{:T(128)S(6)} %select_n.25, bf16[1,8,64,2048]{3,2,1,0:T(8,128)(2,1)} %param.8, ...), kind=kLoop, calls=%fused_computation.22 | loop fusion | flops 4456448 | bytes 5242912 | tf_op jit(solution)/shard_map/squeeze;reshape | solution.py:338
  50.6 4.6 %collective-permute-start.10 = (bf16[1,64,2048]{2,1,0:T(8,128)(2,1)S(1)}, bf16[1,64,2048]{2,1,0:T(8,128)(2,1)S(1)}, u32[]{:S(2)}, u32[]{:S(2)}) collective-permute-start(bf16[1,64,2048]{2,1,0:T(8,128)(2,1)S(1)} %get-tuple-element.45), channel_id=1, source_target_pairs={{0,7},{1,6},{2,5},{3,4},{4,3},{5,2},{6,1},{7,0},{8,15},{9,14},{10,... | collective-permute-start | bytes 786440 | tf_op jit(solution)/shard_map/ppermute | solution.py:24
  55.2 1.9 %collective-permute-done.4.refs_5_ = bf16[2,1,1,64,2048]{4,3,2,1,0:T(8,128)(2,1)} collective-permute-done((bf16[2,1,1,64,2048]{4,3,2,1,0:T(8,128)(2,1)}, bf16[2,1,1,64,2048]{4,3,2,1,0:T(8,128)(2,1)}, u32[]{:S(2)}, u32[]{:S(2)}) %collective-permute-start.4) | collective-permute-done | bytes 524320 | tf_op jit(solution)/shard_map/ppermute | solution.py:24
  57.0 1.2 fusion.6
  58.3 3.8 %collective-permute-done.10.refs_8_ = bf16[1,64,2048]{2,1,0:T(8,128)(2,1)S(1)} collective-permute-done((bf16[1,64,2048]{2,1,0:T(8,128)(2,1)S(1)}, bf16[1,64,2048]{2,1,0:T(8,128)(2,1)S(1)}, u32[]{:S(2)}, u32[]{:S(2)}) %collective-permute-start.10) | collective-permute-done | bytes 262176 | tf_op jit(solution)/shard_map/ppermute | solution.py:24
  62.0 0.5 collective-permute-start.11
  62.6 3.5 %collective-permute-start.7 = (bf16[1,64,2048]{2,1,0:T(8,128)(2,1)S(1)}, bf16[1,64,2048]{2,1,0:T(8,128)(2,1)S(1)}, u32[]{:S(2)}, u32[]{:S(2)}) collective-permute-start(bf16[1,64,2048]{2,1,0:T(8,128)(2,1)S(1)} %get-tuple-element.49), channel_id=1, source_target_pairs={{0,6},{1,7},{2,4},{3,5},{4,2},{5,3},{6,0},{7,1},{8,14},{9,15},{10,... | collective-permute-start | bytes 786440 | tf_op jit(solution)/shard_map/ppermute | solution.py:24
  66.1 9.4 %collective-permute-done.11.refs_6_ = bf16[2,1,1,64,2048]{4,3,2,1,0:T(8,128)(2,1)S(1)} collective-permute-done((bf16[2,1,1,64,2048]{4,3,2,1,0:T(8,128)(2,1)S(1)}, bf16[2,1,1,64,2048]{4,3,2,1,0:T(8,128)(2,1)S(1)}, u32[]{:S(2)}, u32[]{:S(2)}) %collective-permute-start.11) | collective-permute-done | bytes 524320 | tf_op jit(solution)/shard_map/ppermute | solution.py:24
  75.6 0.8 copy-done.2
  76.4 0.7 collective-permute-start.12
  77.1 6.9 %collective-permute-start.15 = (bf16[1,64,2048]{2,1,0:T(8,128)(2,1)S(1)}, bf16[1,64,2048]{2,1,0:T(8,128)(2,1)S(1)}, u32[]{:S(2)}, u32[]{:S(2)}) collective-permute-start(bf16[1,64,2048]{2,1,0:T(8,128)(2,1)S(1)} %get-tuple-element.57), channel_id=1, source_target_pairs={{0,5},{1,4},{2,7},{3,6},{4,1},{5,0},{6,3},{7,2},{8,13},{9,12},{10,... | collective-permute-start | bytes 786440 | tf_op jit(solution)/shard_map/ppermute | solution.py:24
  84.0 5.3 %first_weight.1 = (bf16[4,1,1,64,2048]{4,3,2,1,0:T(8,128)(2,1)S(1)}, bf16[4,1,1,64,2048]{4,3,2,1,0:T(8,128)(2,1)S(1)}) custom-call(s32[8]{0:T(128)S(1)} %broadcast_xor_fusion.picks.refs_0_, f32[5]{0:T(128)S(1)} %stack.11.share.refs_1_, bf16[8,1,1,64,2048]{4,3,2,1,0:T(8,128)(2,1)} %bitcast.73, bf16[8,1,1,64,2048]{4,3,2,1,0:T(8,128)(2,1)S(1)} %collective-permute-done.1.near), custom_call_target="tpu_custom_call" | custom-call | flops 2097157 | bytes 6291476 | tf_op jit(solution)/shard_map/first_weight/pallas_call | solution.py:160
  89.3 6.3 %collective-permute-start.17 = (bf16[1,64,2048]{2,1,0:T(8,128)(2,1)S(1)}, bf16[1,64,2048]{2,1,0:T(8,128)(2,1)S(1)}, u32[]{:S(2)}, u32[]{:S(2)}) collective-permute-start(bf16[1,64,2048]{2,1,0:T(8,128)(2,1)S(1)} %bitcast.75), channel_id=1, source_target_pairs={{0,2},{1,3},{2,0},{3,1},{4,6},{5,7},{6,4},{7,5},{8,10},{9,11},{10,... | collective-permute-start | bytes 786440 | tf_op jit(solution)/shard_map/ppermute | solution.py:24
  95.6 5.7 %collective-permute-done.15.refs_6_ = bf16[1,64,2048]{2,1,0:T(8,128)(2,1)S(1)} collective-permute-done((bf16[1,64,2048]{2,1,0:T(8,128)(2,1)S(1)}, bf16[1,64,2048]{2,1,0:T(8,128)(2,1)S(1)}, u32[]{:S(2)}, u32[]{:S(2)}) %collective-permute-start.15) | collective-permute-done | bytes 262176 | tf_op jit(solution)/shard_map/ppermute | solution.py:24
  101.4 0.8 copy-done.4
  102.2 1.5 collective-permute-start.13
  103.7 1.9 %collective-permute-done.17.refs_3_ = bf16[1,64,2048]{2,1,0:T(8,128)(2,1)S(1)} collective-permute-done((bf16[1,64,2048]{2,1,0:T(8,128)(2,1)S(1)}, bf16[1,64,2048]{2,1,0:T(8,128)(2,1)S(1)}, u32[]{:S(2)}, u32[]{:S(2)}) %collective-permute-start.17) | collective-permute-done | bytes 262176 | tf_op jit(solution)/shard_map/ppermute | solution.py:24
  105.6 5.8 %collective-permute-done.18.refs_4_ = bf16[1,64,2048]{2,1,0:T(8,128)(2,1)S(1)} collective-permute-done((bf16[1,64,2048]{2,1,0:T(8,128)(2,1)S(1)}, bf16[1,64,2048]{2,1,0:T(8,128)(2,1)S(1)}, u32[]{:S(2)}, u32[]{:S(2)}) %collective-permute-start.18) | collective-permute-done | bytes 262176 | tf_op jit(solution)/shard_map/ppermute | solution.py:24
  111.4 0.9 collective-permute-done.16.refs_2_
  112.3 13.8 %orthogonalize.1 = bf16[1,512,2048]{2,1,0:T(8,128)(2,1)S(1)} custom-call(s32[1]{0:T(128)} %bitcast.24.refs_0_, bf16[1,64,2048]{2,1,0:T(8,128)(2,1)S(1)} %get-tuple-element.56.refs_1_, bf16[1,64,2048]{2,1,0:T(8,128)(2,1)S(1)} %collective-permute-done.16.refs_2_, bf16[1,64,2048]{2,1,0:T(8,128)(2,1)S(1)} %collective-permute-done.17.refs_3_, ...), custom_call_target="tpu_custom_call" | custom-call | flops 11005853696 | bytes 4194304 | tf_op jit(solution)/shard_map/orthogonalize/pallas_call | solution.py:127
  126.2 1.3 copy-done.6
  127.5 1.0 copy-done.13
  128.5 4.3 %all-to-all-start = ((bf16[8,1,64,2048]{3,2,1,0:T(8,128)(2,1)}), bf16[8,1,64,2048]{3,2,1,0:T(8,128)(2,1)}, u32[]{:S(2)}, u32[]{:S(2)}) async-start(bf16[8,1,64,2048]{3,2,1,0:T(8,128)(2,1)} %bitcast.66), calls=%async_computation | async-start | bytes 4194304 | tf_op jit(solution)/shard_map/all_to_all | solution.py:388
  132.8 1.5 collective-permute-start.14
  134.3 1.0 copy-done
  135.3 1.0 copy-done.1
  136.4 1.0 copy-done.3
  137.4 1.0 copy-done.5
  138.4 6.3 %place.1 = f32[8,1,1,64,2048]{4,3,2,1,0:T(8,128)} custom-call(s32[8]{0:T(128)S(1)} %broadcast_xor_fusion.picks.refs_0_, f32[5]{0:T(128)S(1)} %stack.11.share.refs_1_, f32[1,1,1,64,2048]{4,3,2,1,0:T(8,128)S(1)} %copy-done, f32[1,1,1,64,2048]{4,3,2,1,0:T(8,128)S(1)} %copy-done.1, f32[6,1,1,64,2048]{4,3,2,1,0:T(8,128)S(1)} %get-tuple-element.31.refs_4_, ...), custom_call_target="tpu_custom_call" | custom-call | flops 1835013 | bytes 9961492 | tf_op jit(solution)/shard_map/place/pallas_call | solution.py:160
  144.8 9.3 %collective-permute-done.14.refs_3_ = bf16[4,1,1,64,2048]{4,3,2,1,0:T(8,128)(2,1)S(1)} collective-permute-done((bf16[4,1,1,64,2048]{4,3,2,1,0:T(8,128)(2,1)}, bf16[4,1,1,64,2048]{4,3,2,1,0:T(8,128)(2,1)S(1)}, u32[]{:S(2)}, u32[]{:S(2)}) %collective-permute-start.14) | collective-permute-done | bytes 1048608 | tf_op jit(solution)/shard_map/ppermute | solution.py:24
  154.1 2.2 %second_weight.1.mixed = bf16[8,1,1,64,2048]{4,3,2,1,0:T(8,128)(2,1)S(1)} custom-call(s32[8]{0:T(128)S(1)} %broadcast_xor_fusion.picks.refs_0_, f32[5]{0:T(128)S(1)} %stack.11.share.refs_1_, bf16[4,1,1,64,2048]{4,3,2,1,0:T(8,128)(2,1)S(1)} %copy-done.10, bf16[4,1,1,64,2048]{4,3,2,1,0:T(8,128)(2,1)S(1)} %copy-done.12, ...), custom_call_target="tpu_custom_call" | custom-call | flops 2097157 | bytes 6291476 | tf_op jit(solution)/shard_map/second_weight/pallas_call | solution.py:160
  156.3 20.5 %all-to-all-done = bf16[8,1,64,2048]{3,2,1,0:T(8,128)(2,1)} async-done(((bf16[8,1,64,2048]{3,2,1,0:T(8,128)(2,1)}), bf16[8,1,64,2048]{3,2,1,0:T(8,128)(2,1)}, u32[]{:S(2)}, u32[]{:S(2)}) %all-to-all-start) | async-done | bytes 2097184 | tf_op jit(solution)/shard_map/all_to_all | solution.py:388
  176.8 6.6 %settle.1 = (bf16[8,1,1,64,2048]{4,3,2,1,0:T(8,128)(2,1)}, bf16[8,1,1,64,2048]{4,3,2,1,0:T(8,128)(2,1)}) custom-call(s32[8]{0:T(128)S(1)} %broadcast_xor_fusion.picks.refs_0_, bf16[8,1,1,64,2048]{4,3,2,1,0:T(8,128)(2,1)S(1)} %second_weight.1.mixed, bf16[8,1,1,64,2048]{4,3,2,1,0:T(8,128)(2,1)} %bitcast.33.update), custom_call_target="tpu_custom_call" | custom-call | flops 2097152 | bytes 8388608 | tf_op jit(solution)/shard_map/settle/pallas_call | solution.py:160
  (52 shorter events, 1.9 us)
Async XLA Ops:
  7.9 20.0 %copy-start.19 = (s32[4,2]{0,1:T(2,128)S(1)}, s32[4,2]{0,1:T(2,128)}, u32[]{:S(2)}) copy-start(s32[4,2]{0,1:T(2,128)} %param.10) | copy-start | bytes 100
  11.9 20.0 %collective-permute-start.2 = (bf16[6,1,1,64,2048]{4,3,2,1,0:T(8,128)(2,1)S(1)}, bf16[6,1,1,64,2048]{4,3,2,1,0:T(8,128)(2,1)S(1)}, u32[]{:S(2)}, u32[]{:S(2)}) collective-permute-start(bf16[6,1,1,64,2048]{4,3,2,1,0:T(8,128)(2,1)S(1)} %gather.1), channel_id=1, source_target_pairs={{0,8},{8,0},{16,24},{24,16},{1,9},{9,1},{17,25},{25,17},{2,10},{10... | collective-permute-start | bytes 4718600 | tf_op jit(solution)/shard_map/ppermute | solution.py:24
  12.5 9.9 %collective-permute-start = (bf16[1,1,1,64,2048]{4,3,2,1,0:T(8,128)(2,1)}, bf16[1,1,1,64,2048]{4,3,2,1,0:T(8,128)(2,1)S(1)}, u32[]{:S(2)}, u32[]{:S(2)}) collective-permute-start(bf16[1,1,1,64,2048]{4,3,2,1,0:T(8,128)(2,1)} %get-tuple-element.52), channel_id=1, source_target_pairs={{0,16},{8,24},{16,0},{24,8},{1,17},{9,25},{17,1},{25,9},{2,18},{10... | collective-permute-start | bytes 786440 | tf_op jit(solution)/shard_map/ppermute | solution.py:24
  15.0 12.8 %collective-permute-start.3 = (bf16[1,1,1,64,2048]{4,3,2,1,0:T(8,128)(2,1)}, bf16[1,1,1,64,2048]{4,3,2,1,0:T(8,128)(2,1)}, u32[]{:S(2)}, u32[]{:S(2)}) collective-permute-start(bf16[1,1,1,64,2048]{4,3,2,1,0:T(8,128)(2,1)} %get-tuple-element.51), channel_id=1, source_target_pairs={{0,16},{8,24},{16,0},{24,8},{1,17},{9,25},{17,1},{25,9},{2,18},{10... | collective-permute-start | bytes 786440 | tf_op jit(solution)/shard_map/ppermute | solution.py:24
  15.1 29.7 %collective-permute-start.5 = (bf16[1,1,1,64,2048]{4,3,2,1,0:T(8,128)(2,1)}, bf16[1,1,1,64,2048]{4,3,2,1,0:T(8,128)(2,1)}, u32[]{:S(2)}, u32[]{:S(2)}) collective-permute-start(bf16[1,1,1,64,2048]{4,3,2,1,0:T(8,128)(2,1)} %get-tuple-element.52), channel_id=1, source_target_pairs={{0,8},{8,0},{16,24},{24,16},{1,9},{9,1},{17,25},{25,17},{2,10},{10... | collective-permute-start | bytes 786440 | tf_op jit(solution)/shard_map/ppermute | solution.py:24
  15.2 29.9 %collective-permute-start.8 = (bf16[1,1,1,64,2048]{4,3,2,1,0:T(8,128)(2,1)}, bf16[1,1,1,64,2048]{4,3,2,1,0:T(8,128)(2,1)}, u32[]{:S(2)}, u32[]{:S(2)}) collective-permute-start(bf16[1,1,1,64,2048]{4,3,2,1,0:T(8,128)(2,1)} %get-tuple-element.51), channel_id=1, source_target_pairs={{0,8},{8,0},{16,24},{24,16},{1,9},{9,1},{17,25},{25,17},{2,10},{10... | collective-permute-start | bytes 786440 | tf_op jit(solution)/shard_map/ppermute | solution.py:24
  22.4 22.7 %collective-permute-start.6 = (bf16[1,1,1,64,2048]{4,3,2,1,0:T(8,128)(2,1)S(1)}, bf16[1,1,1,64,2048]{4,3,2,1,0:T(8,128)(2,1)}, u32[]{:S(2)}, u32[]{:S(2)}) collective-permute-start(bf16[1,1,1,64,2048]{4,3,2,1,0:T(8,128)(2,1)S(1)} %collective-permute-done), channel_id=1, source_target_pairs={{0,8},{8,0},{16,24},{24,16},{1,9},{9,1},{17,25},{25,17},{2,10},{10... | collective-permute-start | bytes 786440 | tf_op jit(solution)/shard_map/ppermute | solution.py:24
  27.9 17.3 %collective-permute-start.9 = (bf16[1,1,1,64,2048]{4,3,2,1,0:T(8,128)(2,1)}, bf16[1,1,1,64,2048]{4,3,2,1,0:T(8,128)(2,1)}, u32[]{:S(2)}, u32[]{:S(2)}) collective-permute-start(bf16[1,1,1,64,2048]{4,3,2,1,0:T(8,128)(2,1)} %collective-permute-done.3), channel_id=1, source_target_pairs={{0,8},{8,0},{16,24},{24,16},{1,9},{9,1},{17,25},{25,17},{2,10},{10... | collective-permute-start | bytes 786440 | tf_op jit(solution)/shard_map/ppermute | solution.py:24
  31.9 1.1 copy-start.7
  33.1 1.4 copy-start.8
  40.8 0.8 copy-start.15
  41.6 0.8 copy-start.17
  42.4 14.7 %collective-permute-start.4 = (bf16[2,1,1,64,2048]{4,3,2,1,0:T(8,128)(2,1)}, bf16[2,1,1,64,2048]{4,3,2,1,0:T(8,128)(2,1)}, u32[]{:S(2)}, u32[]{:S(2)}) collective-permute-start(bf16[2,1,1,64,2048]{4,3,2,1,0:T(8,128)(2,1)} %get-tuple-element.29), channel_id=1, source_target_pairs={{0,16},{8,24},{16,0},{24,8},{1,17},{9,25},{17,1},{25,9},{2,18},{10... | collective-permute-start | bytes 1572872 | tf_op jit(solution)/shard_map/ppermute | solution.py:24
  44.8 39.2 %collective-permute-start.1 = (bf16[8,1,1,64,2048]{4,3,2,1,0:T(8,128)(2,1)}, bf16[8,1,1,64,2048]{4,3,2,1,0:T(8,128)(2,1)S(1)}, u32[]{:S(2)}, u32[]{:S(2)}) collective-permute-start(bf16[8,1,1,64,2048]{4,3,2,1,0:T(8,128)(2,1)} %bitcast.72), channel_id=1, source_target_pairs={{0,8},{8,0},{16,24},{24,16},{1,9},{9,1},{17,25},{25,17},{2,10},{10... | collective-permute-start | bytes 6291464 | tf_op jit(solution)/shard_map/ppermute | solution.py:24
  50.6 11.4 %copy-start.18 = (bf16[2,1,1,64,2048]{4,3,2,1,0:T(8,128)(2,1)S(1)}, bf16[2,1,1,64,2048]{4,3,2,1,0:T(8,128)(2,1)}, u32[]{:S(2)}) copy-start(bf16[2,1,1,64,2048]{4,3,2,1,0:T(8,128)(2,1)} %copy-done.17) | copy-start | bytes 1572868
  50.6 11.4 %collective-permute-start.10 = (bf16[1,64,2048]{2,1,0:T(8,128)(2,1)S(1)}, bf16[1,64,2048]{2,1,0:T(8,128)(2,1)S(1)}, u32[]{:S(2)}, u32[]{:S(2)}) collective-permute-start(bf16[1,64,2048]{2,1,0:T(8,128)(2,1)S(1)} %get-tuple-element.45), channel_id=1, source_target_pairs={{0,7},{1,6},{2,5},{3,4},{4,3},{5,2},{6,1},{7,0},{8,15},{9,14},{10,... | collective-permute-start | bytes 786440 | tf_op jit(solution)/shard_map/ppermute | solution.py:24
  57.0 19.4 %copy-start.16 = (bf16[2,1,1,64,2048]{4,3,2,1,0:T(8,128)(2,1)S(1)}, bf16[2,1,1,64,2048]{4,3,2,1,0:T(8,128)(2,1)}, u32[]{:S(2)}) copy-start(bf16[2,1,1,64,2048]{4,3,2,1,0:T(8,128)(2,1)} %copy-done.15) | copy-start | bytes 1572868
  62.0 13.4 %collective-permute-start.11 = (bf16[2,1,1,64,2048]{4,3,2,1,0:T(8,128)(2,1)S(1)}, bf16[2,1,1,64,2048]{4,3,2,1,0:T(8,128)(2,1)S(1)}, u32[]{:S(2)}, u32[]{:S(2)}) collective-permute-start(bf16[2,1,1,64,2048]{4,3,2,1,0:T(8,128)(2,1)S(1)} %copy-done.18), channel_id=1, source_target_pairs={{0,16},{8,24},{16,0},{24,8},{1,17},{9,25},{17,1},{25,9},{2,18},{10... | collective-permute-start | bytes 1572872 | tf_op jit(solution)/shard_map/ppermute | solution.py:24
  62.6 13.8 %collective-permute-start.7 = (bf16[1,64,2048]{2,1,0:T(8,128)(2,1)S(1)}, bf16[1,64,2048]{2,1,0:T(8,128)(2,1)S(1)}, u32[]{:S(2)}, u32[]{:S(2)}) collective-permute-start(bf16[1,64,2048]{2,1,0:T(8,128)(2,1)S(1)} %get-tuple-element.49), channel_id=1, source_target_pairs={{0,6},{1,7},{2,4},{3,5},{4,2},{5,3},{6,0},{7,1},{8,14},{9,15},{10,... | collective-permute-start | bytes 786440 | tf_op jit(solution)/shard_map/ppermute | solution.py:24
  75.6 0.8 copy-start.2
  76.4 24.9 %collective-permute-start.12 = (bf16[2,1,1,64,2048]{4,3,2,1,0:T(8,128)(2,1)S(1)}, bf16[2,1,1,64,2048]{4,3,2,1,0:T(8,128)(2,1)S(1)}, u32[]{:S(2)}, u32[]{:S(2)}) collective-permute-start(bf16[2,1,1,64,2048]{4,3,2,1,0:T(8,128)(2,1)S(1)} %copy-done.16), channel_id=1, source_target_pairs={{0,16},{8,24},{16,0},{24,8},{1,17},{9,25},{17,1},{25,9},{2,18},{10... | collective-permute-start | bytes 1572872 | tf_op jit(solution)/shard_map/ppermute | solution.py:24
  77.1 24.2 %collective-permute-start.15 = (bf16[1,64,2048]{2,1,0:T(8,128)(2,1)S(1)}, bf16[1,64,2048]{2,1,0:T(8,128)(2,1)S(1)}, u32[]{:S(2)}, u32[]{:S(2)}) collective-permute-start(bf16[1,64,2048]{2,1,0:T(8,128)(2,1)S(1)} %get-tuple-element.57), channel_id=1, source_target_pairs={{0,5},{1,4},{2,7},{3,6},{4,1},{5,0},{6,3},{7,2},{8,13},{9,12},{10,... | collective-permute-start | bytes 786440 | tf_op jit(solution)/shard_map/ppermute | solution.py:24
  84.0 19.7 %collective-permute-start.19 = (bf16[1,64,2048]{2,1,0:T(8,128)(2,1)S(1)}, bf16[1,64,2048]{2,1,0:T(8,128)(2,1)S(1)}, u32[]{:S(2)}, u32[]{:S(2)}) collective-permute-start(bf16[1,64,2048]{2,1,0:T(8,128)(2,1)S(1)} %bitcast.74), channel_id=1, source_target_pairs={{0,4},{1,5},{2,6},{3,7},{4,0},{5,1},{6,2},{7,3},{8,12},{9,13},{10,... | collective-permute-start | bytes 786440 | tf_op jit(solution)/shard_map/ppermute | solution.py:24
  89.3 23.0 %copy-start.11 = (bf16[4,1,1,64,2048]{4,3,2,1,0:T(8,128)(2,1)}, bf16[4,1,1,64,2048]{4,3,2,1,0:T(8,128)(2,1)S(1)}, u32[]{:S(2)}) copy-start(bf16[4,1,1,64,2048]{4,3,2,1,0:T(8,128)(2,1)S(1)} %get-tuple-element.39.refs_1_) | copy-start | bytes 3145732
  89.3 36.9 %copy-start.9 = (bf16[4,1,1,64,2048]{4,3,2,1,0:T(8,128)(2,1)}, bf16[4,1,1,64,2048]{4,3,2,1,0:T(8,128)(2,1)S(1)}, u32[]{:S(2)}) copy-start(bf16[4,1,1,64,2048]{4,3,2,1,0:T(8,128)(2,1)S(1)} %get-tuple-element.37.refs_0_) | copy-start | bytes 3145732
  89.3 16.3 %collective-permute-start.17 = (bf16[1,64,2048]{2,1,0:T(8,128)(2,1)S(1)}, bf16[1,64,2048]{2,1,0:T(8,128)(2,1)S(1)}, u32[]{:S(2)}, u32[]{:S(2)}) collective-permute-start(bf16[1,64,2048]{2,1,0:T(8,128)(2,1)S(1)} %bitcast.75), channel_id=1, source_target_pairs={{0,2},{1,3},{2,0},{3,1},{4,6},{5,7},{6,4},{7,5},{8,10},{9,11},{10,... | collective-permute-start | bytes 786440 | tf_op jit(solution)/shard_map/ppermute | solution.py:24
  95.6 15.8 %collective-permute-start.18 = (bf16[1,64,2048]{2,1,0:T(8,128)(2,1)S(1)}, bf16[1,64,2048]{2,1,0:T(8,128)(2,1)S(1)}, u32[]{:S(2)}, u32[]{:S(2)}) collective-permute-start(bf16[1,64,2048]{2,1,0:T(8,128)(2,1)S(1)} %get-tuple-element.53), channel_id=1, source_target_pairs={{0,3},{1,2},{2,1},{3,0},{4,7},{5,6},{6,5},{7,4},{8,11},{9,10},{10,... | collective-permute-start | bytes 786440 | tf_op jit(solution)/shard_map/ppermute | solution.py:24
  101.4 0.8 copy-start.4
  102.2 10.1 %collective-permute-start.16 = (bf16[1,64,2048]{2,1,0:T(8,128)(2,1)S(1)}, bf16[1,64,2048]{2,1,0:T(8,128)(2,1)S(1)}, u32[]{:S(2)}, u32[]{:S(2)}) collective-permute-start(bf16[1,64,2048]{2,1,0:T(8,128)(2,1)S(1)} %get-tuple-element.55), channel_id=1, source_target_pairs={{0,1},{1,0},{2,3},{3,2},{4,5},{5,4},{6,7},{7,6},{8,9},{9,8},{10,11... | collective-permute-start | bytes 786440 | tf_op jit(solution)/shard_map/ppermute | solution.py:24
  102.2 25.2 %collective-permute-start.13 = (bf16[4,1,1,64,2048]{4,3,2,1,0:T(8,128)(2,1)S(1)}, bf16[4,1,1,64,2048]{4,3,2,1,0:T(8,128)(2,1)S(1)}, u32[]{:S(2)}, u32[]{:S(2)}) collective-permute-start(bf16[4,1,1,64,2048]{4,3,2,1,0:T(8,128)(2,1)S(1)} %get-tuple-element.37.refs_0_), channel_id=1, source_target_pairs={{0,16},{8,24},{16,0},{24,8},{1,17},{9,25},{17,1},{25,9},{2,18},{10... | collective-permute-start | bytes 3145736 | tf_op jit(solution)/shard_map/ppermute | solution.py:24
  126.2 1.3 copy-start.6
  127.5 1.0 copy-start.13
  128.5 48.3 %all-to-all-start = ((bf16[8,1,64,2048]{3,2,1,0:T(8,128)(2,1)}), bf16[8,1,64,2048]{3,2,1,0:T(8,128)(2,1)}, u32[]{:S(2)}, u32[]{:S(2)}) async-start(bf16[8,1,64,2048]{3,2,1,0:T(8,128)(2,1)} %bitcast.66), calls=%async_computation | async-start | bytes 4194304 | tf_op jit(solution)/shard_map/all_to_all | solution.py:388
  132.8 21.3 %collective-permute-start.14 = (bf16[4,1,1,64,2048]{4,3,2,1,0:T(8,128)(2,1)}, bf16[4,1,1,64,2048]{4,3,2,1,0:T(8,128)(2,1)S(1)}, u32[]{:S(2)}, u32[]{:S(2)}) collective-permute-start(bf16[4,1,1,64,2048]{4,3,2,1,0:T(8,128)(2,1)} %copy-done.11), channel_id=1, source_target_pairs={{0,16},{8,24},{16,0},{24,8},{1,17},{9,25},{17,1},{25,9},{2,18},{10... | collective-permute-start | bytes 3145736 | tf_op jit(solution)/shard_map/ppermute | solution.py:24
  134.3 1.0 copy-start
  135.3 1.0 copy-start.1
  136.4 1.0 copy-start.3
  137.4 1.0 copy-start.5
  138.4 15.7 %copy-start.10 = (bf16[4,1,1,64,2048]{4,3,2,1,0:T(8,128)(2,1)S(1)}, bf16[4,1,1,64,2048]{4,3,2,1,0:T(8,128)(2,1)}, u32[]{:S(2)}) copy-start(bf16[4,1,1,64,2048]{4,3,2,1,0:T(8,128)(2,1)} %copy-done.9) | copy-start | bytes 3145732
  138.4 15.7 %copy-start.12 = (bf16[4,1,1,64,2048]{4,3,2,1,0:T(8,128)(2,1)S(1)}, bf16[4,1,1,64,2048]{4,3,2,1,0:T(8,128)(2,1)}, u32[]{:S(2)}) copy-start(bf16[4,1,1,64,2048]{4,3,2,1,0:T(8,128)(2,1)} %copy-done.11) | copy-start | bytes 3145732
  138.4 15.7 %copy-start.14 = (bf16[4,1,1,64,2048]{4,3,2,1,0:T(8,128)(2,1)S(1)}, bf16[4,1,1,64,2048]{4,3,2,1,0:T(8,128)(2,1)}, u32[]{:S(2)}) copy-start(bf16[4,1,1,64,2048]{4,3,2,1,0:T(8,128)(2,1)} %copy-done.13) | copy-start | bytes 3145732

commit v6 on v2

--- a/solution.py
+++ b/solution.py
@@ -58,27 +58,31 @@
     )
     inverse = 1.0 / (jnp.sqrt(square_norm) + 1e-07)
     gram_held[...] = gram * inverse * inverse
-    poly_held[...] = jnp.where(on_diagonal, 1.0, 0.0)
-
-    def step(last):
+
+    def step(first, last):
         gram = gram_held[...]
         gram_high, gram_low = split(gram)
         shift = (
             coeff_b * gram_high.astype(F32) + coeff_c * times(gram_high, gram_high)
         ).astype(BF16)
-        poly = poly_held[...]
-        poly_high, poly_low = split(poly)
-        poly_held[...] = coeff_a * poly + times(shift, poly_high) + times(shift, poly_low)
+        if first:
+            poly_held[...] = jnp.where(on_diagonal, coeff_a, 0.0) + shift.astype(F32)
+        else:
+            poly = poly_held[...]
+            poly_high, poly_low = split(poly)
+            poly_held[...] = coeff_a * poly + times(shift, poly_high) + times(shift, poly_low)
         if not last:
             half = coeff_a * gram + times(shift, gram_high) + times(shift, gram_low)
             half_high, half_low = split(half)
             gram_held[...] = coeff_a * half + times(half_high, shift) + times(half_low, shift)
 
-    @pl.loop(0, NS_STEPS - 1)
+    step(True, False)
+
+    @pl.loop(0, NS_STEPS - 2)
     def _(_):
-        step(False)
-
-    step(True)
+        step(False, False)
+
+    step(False, True)
     high, low = split(poly_held[...] * (scale * inverse))
     update = (times(high, held[...]) + times(low, held[...])).astype(BF16)
     for place, out in enumerate(outs):
@@ -122,6 +126,10 @@
     return groups if top == 0 else [(0, shards)]
 
 
+def after(values, *others):
+    return lax.optimization_barrier((values, others))[0]
+
+
 def local(weight, tracker, grad_new, grad_old, mix_keep):
     shards = lax.axis_size("shard")
     _, experts, rows, columns = tracker.shape
@@ -140,13 +148,15 @@
 
     new_tracker = jnp.zeros(shape, F32)
     blocks = [None] * shards
-    far = None
-    for lowest, length in grouped(shards):
+    for turn, (lowest, length) in enumerate(grouped(shards)):
+        if turn == 2:
+            tracker = after(tracker, sent)
         start = (here ^ lowest) // length * length
         own = taken(tracker, start, length)
         near = swapped(own.astype(BF16), "rep", 1)
         mixed = first * own + (1.0 - first) * near.astype(F32)
-        far = swapped(mixed.astype(BF16), "rep", 2)
+        sent = mixed.astype(BF16)
+        far = swapped(sent, "rep", 2)
         group = second * mixed + (1.0 - second) * far.astype(F32)
         group += taken(grad_new, start, length).astype(F32)
         group -= taken(grad_old, start, length).astype(F32)
@@ -159,7 +169,7 @@
     weight_own = (
         first * weight.astype(F32) + (1.0 - first) * weight_near.astype(F32)
     ).astype(BF16)
-    weight_own, _ = lax.optimization_barrier((weight_own, far))
+    weight_own = after(weight_own, far, blocks[1])
     weight_far = swapped(weight_own, "rep", 2)
     mixed_weight = (
         second * weight_own.astype(F32) + (1.0 - second) * weight_far.astype(F32)
@@ -169,9 +179,14 @@
     updates = orthogonalize(blocks, scale)
     update = jnp.zeros(shape, BF16)
     new_weight = jnp.zeros(shape, BF16)
-    for offset in reversed(range(shards)):
-        block = updates[offset]
-        block = swapped(block, "shard", offset) if offset else block
+    half = shards // 2
+    order = list(range(1, half)) + list(reversed(range(half, shards))) + [0]
+    received = [
+        swapped(block, "shard", offset) if offset else block for offset, block in enumerate(updates)
+    ]
+    mixed_weight = after(mixed_weight, received[-1])
+    for offset in order:
+        block = received[offset]
         place = here ^ offset
         kept = taken(mixed_weight, place, 1)[0]
         settled = (kept.astype(F32) - learn_rate * block.astype(F32)).astype(BF16)

time: 159 us -> 164 us (1.031)
  waiting for transfers between devices: 57.5 us -> 71.5 us
  starting transfers between devices: 51.8 us -> 41.5 us
  other arithmetic: 23.3 us -> 25.6 us
    ppermute x24, waiting for transfers between devices: 57.5 us -> 71.5 us  [swapped(): lax.ppermute(values, axis, [(i, i ^ offset) for i in range(lax.axis_size(...]
    ppermute x24, starting transfers between devices: 51.8 us -> 41.5 us  [swapped(): lax.ppermute(values, axis, [(i, i ^ offset) for i in range(lax.axis_size(...]
    convert_element_type x3, other arithmetic: 5.51 us -> 8.03 us  [local(): sent = mixed.astype(BF16)]
  transfers between devices with their start and end apart: 24 -> 24, of which waited for: 14 -> 12; matrix products, arithmetic and copies ran while one was open for 19% -> 16% of each run, Pallas kernels for 8% -> 8%
where the time goes in v6:
time: 164 us
  waiting for transfers between devices  71.5 us (44%)
  starting transfers between devices  41.5 us (25%)
  other arithmetic  25.6 us (16%)
  Pallas kernels  12.8 us (8%)
  local copies, waits for them, and re-layouts  10 us (6%)
  between operations  2.23 us (1%)
    ppermute x24, waiting for transfers between devices, swapped(): lax.ppermute(values, axis, [(i, i ^ offset) for i in range(lax.axis_size(...  71.5 us
    ppermute x24, starting transfers between devices, swapped(): lax.ppermute(values, axis, [(i, i ^ offset) for i in range(lax.axis_size(...  41.5 us
    pallas_call x1, Pallas kernels, orthogonalize(): pl.pallas_call(body, grid=(each,), in_specs=[block] * count, out_specs=[b...  12.8 us
    convert_element_type x3, other arithmetic, local(): sent = mixed.astype(BF16)  8.03 us
    dynamic_update_slice x4, other arithmetic, local(): lax.dynamic_update_slice_in_dim(new_tracker, group, start, axis=0)  8.01 us
    convert_element_type x3, local copies, waits for them, and re-layouts, local(): near = swapped(own.astype(BF16), 'rep', 1)  6.21 us
    convert_element_type x1, other arithmetic, local(): weight_own = (first * weight.astype(F32) + (1.0 - first) * weight_near.as...  4.4 us
    convert_element_type x1, other arithmetic, local(): mixed_weight = (second * weight_own.astype(F32) + (1.0 - second) * weight...  3.71 us
  transfers between devices with their start and end apart: 24, of which 12 were waited for; matrix products, arithmetic and copies ran while one was open for 16% of the time, Pallas kernels for 8%

profile of v6, /device:TPU:0, one launch (start us, length us, event | category | flops | bytes accessed | tf_op | source)
XLA Modules:
  0.0 163.5 jit_solution(14276105216233946500)
XLA Ops:
  0.6 1.3 dynamic-slice_convert_fusion.9
  1.9 0.5 collective-permute-start.1
  2.5 0.7 convert_multiply_fusion
  3.2 0.6 constant_dynamic-slice_fusion.1
  4.5 2.8 %fusion.10 = (bf16[1,1,64,2048]{3,2,1,0:T(8,128)(2,1)}, bf16[1,1,64,2048]{3,2,1,0:T(8,128)(2,1)}) fusion(bf16[1,1,64,2048]{3,2,1,0:T(8,128)(2,1)S(1)} %collective-permute-done.1, f32[1,8,64,2048]{3,2,1,0:T(8,128)} %param.6, s32[]{:T(128)S(6)} %select_n.125, f32[]{:T(128)S(6)} %sub.59, f32[]{:T(128)} %bitcast.1, ...), kind=kLoop, calls=%fused_computation.42 | loop fusion | flops 1310720 | bytes 2097168 | tf_op jit(solution)/shard_map/convert_element_type | solution.py:158
  7.2 2.9 %dynamic-slice_convert_fusion = bf16[4,1,64,2048]{3,2,1,0:T(8,128)(2,1)} fusion(f32[8,1,64,2048]{3,2,1,0:T(8,128)} %bitcast.115, s32[]{:T(128)S(6)} %select_n.127), kind=kLoop, calls=%fused_computation.6 | loop fusion | bytes 2097156 | tf_op jit(solution)/shard_map/convert_element_type | solution.py:156
  10.1 0.4 collective-permute-start.2
  10.5 2.1 %dynamic-slice_convert_fusion.1 = bf16[2,1,64,2048]{3,2,1,0:T(8,128)(2,1)} fusion(f32[8,1,64,2048]{3,2,1,0:T(8,128)} %bitcast.116, s32[]{:T(128)S(6)} %select_n.137), kind=kLoop, calls=%fused_computation.12 | loop fusion | bytes 1048580 | tf_op jit(solution)/shard_map/convert_element_type | solution.py:156
  12.7 0.4 collective-permute-start
  13.8 2.6 %collective-permute-start.12 = (bf16[1,1,64,2048]{3,2,1,0:T(8,128)(2,1)}, bf16[1,1,64,2048]{3,2,1,0:T(8,128)(2,1)S(1)}, u32[]{:S(2)}, u32[]{:S(2)}) collective-permute-start(bf16[1,1,64,2048]{3,2,1,0:T(8,128)(2,1)} %get-tuple-element.33), channel_id=1, source_target_pairs={{0,16},{8,24},{16,0},{24,8},{1,17},{9,25},{17,1},{25,9},{2,18},{10... | collective-permute-start | bytes 786440 | tf_op jit(solution)/shard_map/ppermute | solution.py:23
  16.5 2.2 %fusion.1 = bf16[2,1,64,2048]{3,2,1,0:T(8,128)(2,1)S(1)} fusion(bf16[2,1,64,2048]{3,2,1,0:T(8,128)(2,1)} %collective-permute-done.8, f32[8,1,64,2048]{3,2,1,0:T(8,128)} %bitcast.117, s32[]{:T(128)S(6)} %select_n.137, f32[]{:T(128)S(6)} %sub.59, f32[]{:T(128)} %bitcast.1), kind=kLoop, calls=%fused_computation.13 | loop fusion | flops 1310720 | bytes 2097164 | tf_op jit(solution)/shard_map/convert_element_type | solution.py:158
  18.7 2.0 %collective-permute-start.9 = (bf16[2,1,64,2048]{3,2,1,0:T(8,128)(2,1)S(1)}, bf16[2,1,64,2048]{3,2,1,0:T(8,128)(2,1)S(1)}, u32[]{:S(2)}, u32[]{:S(2)}) collective-permute-start(bf16[2,1,64,2048]{3,2,1,0:T(8,128)(2,1)S(1)} %fusion.1), channel_id=1, source_target_pairs={{0,16},{8,24},{16,0},{24,8},{1,17},{9,25},{17,1},{25,9},{2,18},{10... | collective-permute-start | bytes 1572872 | tf_op jit(solution)/shard_map/ppermute | solution.py:23
  20.7 3.1 %fusion = bf16[4,1,64,2048]{3,2,1,0:T(8,128)(2,1)S(1)} fusion(bf16[4,1,64,2048]{3,2,1,0:T(8,128)(2,1)S(1)} %collective-permute-done.2, f32[8,1,64,2048]{3,2,1,0:T(8,128)} %bitcast.118, s32[]{:T(128)S(6)} %select_n.127, f32[]{:T(128)S(6)} %sub.59, f32[]{:T(128)} %bitcast.1), kind=kLoop, calls=%fused_computation.7 | loop fusion | flops 2621440 | bytes 4194316 | tf_op jit(solution)/shard_map/convert_element_type | solution.py:158
  24.0 5.4 %collective-permute-done.15 = bf16[1,1,64,2048]{3,2,1,0:T(8,128)(2,1)S(1)} collective-permute-done((bf16[1,1,64,2048]{3,2,1,0:T(8,128)(2,1)}, bf16[1,1,64,2048]{3,2,1,0:T(8,128)(2,1)S(1)}, u32[]{:S(2)}, u32[]{:S(2)}) %collective-permute-start.15) | collective-permute-done | bytes 262176 | tf_op jit(solution)/shard_map/ppermute | solution.py:23
  29.4 0.5 reshape.374
  29.9 1.5 constant_dynamic-update-slice_fusion.1
  31.4 1.5 constant_dynamic-update-slice_fusion
  32.9 4.1 %collective-permute-start.13 = (bf16[1,64,2048]{2,1,0:T(8,128)(2,1)S(1)}, bf16[1,64,2048]{2,1,0:T(8,128)(2,1)S(1)}, u32[]{:S(2)}, u32[]{:S(2)}) collective-permute-start(bf16[1,64,2048]{2,1,0:T(8,128)(2,1)S(1)} %bitcast.123), channel_id=1, source_target_pairs={{0,6},{1,7},{2,4},{3,5},{4,2},{5,3},{6,0},{7,1},{8,14},{9,15},{10,... | collective-permute-start | bytes 786440 | tf_op jit(solution)/shard_map/ppermute | solution.py:23
  37.0 1.2 collective-permute-start.16
  38.2 2.4 %collective-permute-done.9 = bf16[2,1,64,2048]{3,2,1,0:T(8,128)(2,1)S(1)} collective-permute-done((bf16[2,1,64,2048]{3,2,1,0:T(8,128)(2,1)S(1)}, bf16[2,1,64,2048]{3,2,1,0:T(8,128)(2,1)S(1)}, u32[]{:S(2)}, u32[]{:S(2)}) %collective-permute-start.9) | collective-permute-done | bytes 524320 | tf_op jit(solution)/shard_map/ppermute | solution.py:23
  40.6 2.8 %bitcast_dynamic-update-slice_fusion.1 = (f32[1,8,64,2048]{3,2,1,0:T(8,128)S(1)}, bf16[2,1,64,2048]{3,2,1,0:T(8,128)(2,1)S(1)}) fusion(f32[1,8,64,2048]{3,2,1,0:T(8,128)S(1)} %get-tuple-element.29, s32[]{:T(128)S(6)} %select_n.137, bf16[1,8,64,2048]{3,2,1,0:T(8,128)(2,1)S(1)} %copy-done.5, bf16[1,8,64,2048]{3,2,1,0:T(8,128)(2,1)S(1)} %copy-done.6, ...), kind=kLoop, calls=%fused_computation.10 | loop fusion | flops 3407872 | bytes 4718612 | tf_op jit(solution)/shard_map/dynamic_update_slice | solution.py:166
  43.4 19.4 %collective-permute-done.3 = bf16[4,1,64,2048]{3,2,1,0:T(8,128)(2,1)S(1)} collective-permute-done((bf16[4,1,64,2048]{3,2,1,0:T(8,128)(2,1)S(1)}, bf16[4,1,64,2048]{3,2,1,0:T(8,128)(2,1)S(1)}, u32[]{:S(2)}, u32[]{:S(2)}) %collective-permute-start.3) | collective-permute-done | bytes 1048608 | tf_op jit(solution)/shard_map/ppermute | solution.py:23
  62.8 2.3 %bitcast_dynamic-update-slice_fusion = (f32[1,8,64,2048]{3,2,1,0:T(8,128)S(1)}, bf16[4,1,64,2048]{3,2,1,0:T(8,128)(2,1)S(1)}) fusion(f32[1,8,64,2048]{3,2,1,0:T(8,128)S(1)} %get-tuple-element.27, s32[]{:T(128)S(6)} %select_n.127, bf16[1,8,64,2048]{3,2,1,0:T(8,128)(2,1)S(1)} %copy-done.5, bf16[1,8,64,2048]{3,2,1,0:T(8,128)(2,1)S(1)} %copy-done.6, ...), kind=kLoop, calls=%fused_computation.4 | loop fusion | flops 6815744 | bytes 9437204 | tf_op jit(solution)/shard_map/dynamic_update_slice | solution.py:166
  65.3 1.8 %collective-permute-start.4 = (bf16[1,64,2048]{2,1,0:T(8,128)(2,1)S(1)}, bf16[1,64,2048]{2,1,0:T(8,128)(2,1)S(1)}, u32[]{:S(2)}, u32[]{:S(2)}) collective-permute-start(bf16[1,64,2048]{2,1,0:T(8,128)(2,1)S(1)} %get-tuple-element.40), channel_id=1, source_target_pairs={{0,1},{1,0},{2,3},{3,2},{4,5},{5,4},{6,7},{7,6},{8,9},{9,8},{10,11... | collective-permute-start | bytes 786440 | tf_op jit(solution)/shard_map/ppermute | solution.py:23
  67.1 4.4 %add_convert_fusion.1 = bf16[8,1,64,2048]{3,2,1,0:T(8,128)(2,1)} fusion(bf16[8,1,64,2048]{3,2,1,0:T(8,128)(2,1)} %collective-permute-done, f32[]{:T(128)S(6)} %sub.59, f32[]{:T(128)} %bitcast.1, bf16[1,8,64,2048]{3,2,1,0:T(8,128)(2,1)S(1)} %copy-done.4), kind=kLoop, calls=%fused_computation.1 | loop fusion | flops 6291456 | bytes 6291464 | tf_op jit(solution)/shard_map/convert_element_type | solution.py:171
  71.5 1.9 %collective-permute-done.4.refs_1_ = bf16[1,64,2048]{2,1,0:T(8,128)(2,1)S(1)} collective-permute-done((bf16[1,64,2048]{2,1,0:T(8,128)(2,1)S(1)}, bf16[1,64,2048]{2,1,0:T(8,128)(2,1)S(1)}, u32[]{:S(2)}, u32[]{:S(2)}) %collective-permute-start.4) | collective-permute-done | bytes 262176 | tf_op jit(solution)/shard_map/ppermute | solution.py:23
  73.4 1.6 collective-permute-start.5
  75.0 2.7 %collective-permute-start.10 = (bf16[1,64,2048]{2,1,0:T(8,128)(2,1)S(1)}, bf16[1,64,2048]{2,1,0:T(8,128)(2,1)S(1)}, u32[]{:S(2)}, u32[]{:S(2)}) collective-permute-start(bf16[1,64,2048]{2,1,0:T(8,128)(2,1)S(1)} %get-tuple-element.42), channel_id=1, source_target_pairs={{0,4},{1,5},{2,6},{3,7},{4,0},{5,1},{6,2},{7,3},{8,12},{9,13},{10,... | collective-permute-start | bytes 786440 | tf_op jit(solution)/shard_map/ppermute | solution.py:23
  77.7 1.3 collective-permute-start.11
  79.0 1.6 collective-permute-start.6
  80.5 0.4 collective-permute-start.7
  80.9 14.2 %collective-permute-done.10.refs_4_ = bf16[1,64,2048]{2,1,0:T(8,128)(2,1)S(1)} collective-permute-done((bf16[1,64,2048]{2,1,0:T(8,128)(2,1)S(1)}, bf16[1,64,2048]{2,1,0:T(8,128)(2,1)S(1)}, u32[]{:S(2)}, u32[]{:S(2)}) %collective-permute-start.10) | collective-permute-done | bytes 262176 | tf_op jit(solution)/shard_map/ppermute | solution.py:23
  95.2 5.4 %collective-permute-done.11.refs_5_ = bf16[1,64,2048]{2,1,0:T(8,128)(2,1)S(1)} collective-permute-done((bf16[1,64,2048]{2,1,0:T(8,128)(2,1)S(1)}, bf16[1,64,2048]{2,1,0:T(8,128)(2,1)S(1)}, u32[]{:S(2)}, u32[]{:S(2)}) %collective-permute-start.11) | collective-permute-done | bytes 262176 | tf_op jit(solution)/shard_map/ppermute | solution.py:23
  100.8 12.8 %orthogonalize.1 = (bf16[1,64,2048]{2,1,0:T(8,128)(2,1)S(1)}, bf16[1,64,2048]{2,1,0:T(8,128)(2,1)S(1)}, bf16[1,64,2048]{2,1,0:T(8,128)(2,1)S(1)}, bf16[1,64,2048...) custom-call(bf16[1,64,2048]{2,1,0:T(8,128)(2,1)S(1)} %get-tuple-elem, ...), custom_call_target="tpu_custom_call" | custom-call | flops 11005853696 | bytes 4194304 | tf_op jit(solution)/shard_map/orthogonalize/pallas_call | solution.py:102
  113.6 1.6 collective-permute-start.18
  115.2 4.5 %collective-permute-start.17 = (bf16[1,64,2048]{2,1,0:T(8,128)(2,1)S(1)}, bf16[1,64,2048]{2,1,0:T(8,128)(2,1)S(1)}, u32[]{:S(2)}, u32[]{:S(2)}) collective-permute-start(bf16[1,64,2048]{2,1,0:T(8,128)(2,1)S(1)} %get-tuple-element.16), channel_id=1, source_target_pairs={{0,7},{1,6},{2,5},{3,4},{4,3},{5,2},{6,1},{7,0},{8,15},{9,14},{10,... | collective-permute-start | bytes 786440 | tf_op jit(solution)/shard_map/ppermute | solution.py:23
  119.7 3.0 %collective-permute-start.20 = (bf16[1,64,2048]{2,1,0:T(8,128)(2,1)S(1)}, bf16[1,64,2048]{2,1,0:T(8,128)(2,1)S(1)}, u32[]{:S(2)}, u32[]{:S(2)}) collective-permute-start(bf16[1,64,2048]{2,1,0:T(8,128)(2,1)S(1)} %get-tuple-element.20), channel_id=1, source_target_pairs={{0,3},{1,2},{2,1},{3,0},{4,7},{5,6},{6,5},{7,4},{8,11},{9,10},{10,... | collective-permute-start | bytes 786440 | tf_op jit(solution)/shard_map/ppermute | solution.py:23
  122.7 2.5 %collective-permute-done.18 = bf16[1,64,2048]{2,1,0:T(8,128)(2,1)S(1)} collective-permute-done((bf16[1,64,2048]{2,1,0:T(8,128)(2,1)S(1)}, bf16[1,64,2048]{2,1,0:T(8,128)(2,1)S(1)}, u32[]{:S(2)}, u32[]{:S(2)}) %collective-permute-start.18) | collective-permute-done | bytes 262176 | tf_op jit(solution)/shard_map/ppermute | solution.py:23
  125.2 6.2 %collective-permute-start.21 = (bf16[1,64,2048]{2,1,0:T(8,128)(2,1)S(1)}, bf16[1,64,2048]{2,1,0:T(8,128)(2,1)S(1)}, u32[]{:S(2)}, u32[]{:S(2)}) collective-permute-start(bf16[1,64,2048]{2,1,0:T(8,128)(2,1)S(1)} %get-tuple-element.21), channel_id=1, source_target_pairs={{0,6},{1,7},{2,4},{3,5},{4,2},{5,3},{6,0},{7,1},{8,14},{9,15},{10,... | collective-permute-start | bytes 786440 | tf_op jit(solution)/shard_map/ppermute | solution.py:23
  131.4 0.2 reshape.371.clone
  131.8 3.7 %add_convert_fusion = bf16[8,1,64,2048]{3,2,1,0:T(8,128)(2,1)S(1)} fusion(bf16[8,1,64,2048]{3,2,1,0:T(8,128)(2,1)} %collective-permute-done.5, bf16[8,1,64,2048]{3,2,1,0:T(8,128)(2,1)} %add_convert_fusion.1, f32[]{:T(128)S(6)} %sub.61, f32[]{:T(128)} %bitcast), kind=kLoop, calls=%fused_computation | loop fusion | flops 6291456 | bytes 6291464 | tf_op jit(solution)/shard_map/convert_element_type | solution.py:176
  135.5 5.0 %collective-permute-start.23 = (bf16[1,64,2048]{2,1,0:T(8,128)(2,1)S(1)}, bf16[1,64,2048]{2,1,0:T(8,128)(2,1)S(1)}, u32[]{:S(2)}, u32[]{:S(2)}) collective-permute-start(bf16[1,64,2048]{2,1,0:T(8,128)(2,1)S(1)} %get-tuple-element.23), channel_id=1, source_target_pairs={{0,4},{1,5},{2,6},{3,7},{4,0},{5,1},{6,2},{7,3},{8,12},{9,13},{10,... | collective-permute-start | bytes 786440 | tf_op jit(solution)/shard_map/ppermute | solution.py:23
  141.0 1.4 collective-permute-done.20
  142.6 1.3 collective-permute-done.21
  144.0 14.4 %collective-permute-done.22 = bf16[1,64,2048]{2,1,0:T(8,128)(2,1)S(1)} collective-permute-done((bf16[1,64,2048]{2,1,0:T(8,128)(2,1)S(1)}, bf16[1,64,2048]{2,1,0:T(8,128)(2,1)S(1)}, u32[]{:S(2)}, u32[]{:S(2)}) %collective-permute-start.22) | collective-permute-done | bytes 262176 | tf_op jit(solution)/shard_map/ppermute | solution.py:23
  158.5 2.8 %collective-permute-done.23 = bf16[1,64,2048]{2,1,0:T(8,128)(2,1)S(1)} collective-permute-done((bf16[1,64,2048]{2,1,0:T(8,128)(2,1)S(1)}, bf16[1,64,2048]{2,1,0:T(8,128)(2,1)S(1)}, u32[]{:S(2)}, u32[]{:S(2)}) %collective-permute-start.23) | collective-permute-done | bytes 262176 | tf_op jit(solution)/shard_map/ppermute | solution.py:23
  161.5 1.3 copy-done.2
  162.8 0.7 copy-done.3
  (47 shorter events, 1.9 us)
Async XLA Ops:
  1.9 2.5 %collective-permute-start.1 = (bf16[1,1,64,2048]{3,2,1,0:T(8,128)(2,1)S(1)}, bf16[1,1,64,2048]{3,2,1,0:T(8,128)(2,1)S(1)}, u32[]{:S(2)}, u32[]{:S(2)}) collective-permute-start(bf16[1,1,64,2048]{3,2,1,0:T(8,128)(2,1)S(1)} %get-tuple-element.35), channel_id=1, source_target_pairs={{0,8},{8,0},{16,24},{24,16},{1,9},{9,1},{17,25},{25,17},{2,10},{10... | collective-permute-start | bytes 786440 | tf_op jit(solution)/shard_map/ppermute | solution.py:23
  2.4 2.0 %collective-permute-start.14 = (bf16[1,1,64,2048]{3,2,1,0:T(8,128)(2,1)S(1)}, bf16[1,1,64,2048]{3,2,1,0:T(8,128)(2,1)S(1)}, u32[]{:S(2)}, u32[]{:S(2)}) collective-permute-start(bf16[1,1,64,2048]{3,2,1,0:T(8,128)(2,1)S(1)} %get-tuple-element.36), channel_id=1, source_target_pairs={{0,8},{8,0},{16,24},{24,16},{1,9},{9,1},{17,25},{25,17},{2,10},{10... | collective-permute-start | bytes 786440 | tf_op jit(solution)/shard_map/ppermute | solution.py:23
  4.5 2.8 %copy-start.7 = (bf16[1,1,64,2048]{3,2,1,0:T(8,128)(2,1)}, bf16[1,1,64,2048]{3,2,1,0:T(8,128)(2,1)S(1)}, u32[]{:S(2)}) copy-start(bf16[1,1,64,2048]{3,2,1,0:T(8,128)(2,1)S(1)} %collective-permute-done.14) | copy-start | bytes 786436
  7.2 5.5 %copy-start.4 = (bf16[1,8,64,2048]{3,2,1,0:T(8,128)(2,1)S(1)}, bf16[1,8,64,2048]{3,2,1,0:T(8,128)(2,1)}, u32[]{:S(2)}) copy-start(bf16[1,8,64,2048]{3,2,1,0:T(8,128)(2,1)} %param.5) | copy-start | bytes 6291460
  10.1 10.6 %collective-permute-start.2 = (bf16[4,1,64,2048]{3,2,1,0:T(8,128)(2,1)}, bf16[4,1,64,2048]{3,2,1,0:T(8,128)(2,1)S(1)}, u32[]{:S(2)}, u32[]{:S(2)}) collective-permute-start(bf16[4,1,64,2048]{3,2,1,0:T(8,128)(2,1)} %dynamic-slice_convert_fusion), channel_id=1, source_target_pairs={{0,8},{8,0},{16,24},{24,16},{1,9},{9,1},{17,25},{25,17},{2,10},{10... | collective-permute-start | bytes 3145736 | tf_op jit(solution)/shard_map/ppermute | solution.py:23
  12.6 3.9 %collective-permute-start.8 = (bf16[2,1,64,2048]{3,2,1,0:T(8,128)(2,1)}, bf16[2,1,64,2048]{3,2,1,0:T(8,128)(2,1)}, u32[]{:S(2)}, u32[]{:S(2)}) collective-permute-start(bf16[2,1,64,2048]{3,2,1,0:T(8,128)(2,1)} %dynamic-slice_convert_fusion.1), channel_id=1, source_target_pairs={{0,8},{8,0},{16,24},{24,16},{1,9},{9,1},{17,25},{25,17},{2,10},{10... | collective-permute-start | bytes 1572872 | tf_op jit(solution)/shard_map/ppermute | solution.py:23
  12.7 54.4 %collective-permute-start = (bf16[8,1,64,2048]{3,2,1,0:T(8,128)(2,1)S(1)}, bf16[8,1,64,2048]{3,2,1,0:T(8,128)(2,1)}, u32[]{:S(2)}, u32[]{:S(2)}) collective-permute-start(bf16[8,1,64,2048]{3,2,1,0:T(8,128)(2,1)S(1)} %bitcast.121), channel_id=1, source_target_pairs={{0,8},{8,0},{16,24},{24,16},{1,9},{9,1},{17,25},{25,17},{2,10},{10... | collective-permute-start | bytes 6291464 | tf_op jit(solution)/shard_map/ppermute | solution.py:23
  13.8 17.6 %collective-permute-start.12 = (bf16[1,1,64,2048]{3,2,1,0:T(8,128)(2,1)}, bf16[1,1,64,2048]{3,2,1,0:T(8,128)(2,1)S(1)}, u32[]{:S(2)}, u32[]{:S(2)}) collective-permute-start(bf16[1,1,64,2048]{3,2,1,0:T(8,128)(2,1)} %get-tuple-element.33), channel_id=1, source_target_pairs={{0,16},{8,24},{16,0},{24,8},{1,17},{9,25},{17,1},{25,9},{2,18},{10... | collective-permute-start | bytes 786440 | tf_op jit(solution)/shard_map/ppermute | solution.py:23
  16.4 13.0 %collective-permute-start.15 = (bf16[1,1,64,2048]{3,2,1,0:T(8,128)(2,1)}, bf16[1,1,64,2048]{3,2,1,0:T(8,128)(2,1)S(1)}, u32[]{:S(2)}, u32[]{:S(2)}) collective-permute-start(bf16[1,1,64,2048]{3,2,1,0:T(8,128)(2,1)} %get-tuple-element.34), channel_id=1, source_target_pairs={{0,16},{8,24},{16,0},{24,8},{1,17},{9,25},{17,1},{25,9},{2,18},{10... | collective-permute-start | bytes 786440 | tf_op jit(solution)/shard_map/ppermute | solution.py:23
  16.5 13.4 %copy-start.8 = (bf16[1,1,64,2048]{3,2,1,0:T(8,128)(2,1)S(1)}, bf16[1,1,64,2048]{3,2,1,0:T(8,128)(2,1)}, u32[]{:S(2)}) copy-start(bf16[1,1,64,2048]{3,2,1,0:T(8,128)(2,1)} %copy-done.7) | copy-start | bytes 786436
  18.7 21.9 %collective-permute-start.9 = (bf16[2,1,64,2048]{3,2,1,0:T(8,128)(2,1)S(1)}, bf16[2,1,64,2048]{3,2,1,0:T(8,128)(2,1)S(1)}, u32[]{:S(2)}, u32[]{:S(2)}) collective-permute-start(bf16[2,1,64,2048]{3,2,1,0:T(8,128)(2,1)S(1)} %fusion.1), channel_id=1, source_target_pairs={{0,16},{8,24},{16,0},{24,8},{1,17},{9,25},{17,1},{25,9},{2,18},{10... | collective-permute-start | bytes 1572872 | tf_op jit(solution)/shard_map/ppermute | solution.py:23
  20.7 9.2 %copy-start.5 = (bf16[1,8,64,2048]{3,2,1,0:T(8,128)(2,1)S(1)}, bf16[1,8,64,2048]{3,2,1,0:T(8,128)(2,1)}, u32[]{:S(2)}) copy-start(bf16[1,8,64,2048]{3,2,1,0:T(8,128)(2,1)} %param.8) | copy-start | bytes 6291460
  20.7 9.2 %copy-start.6 = (bf16[1,8,64,2048]{3,2,1,0:T(8,128)(2,1)S(1)}, bf16[1,8,64,2048]{3,2,1,0:T(8,128)(2,1)}, u32[]{:S(2)}) copy-start(bf16[1,8,64,2048]{3,2,1,0:T(8,128)(2,1)} %param.7) | copy-start | bytes 6291460
  23.8 6.1 %copy-start = (f32[1,8,64,2048]{3,2,1,0:T(8,128)S(1)}, f32[1,8,64,2048]{3,2,1,0:T(8,128)}, u32[]{:S(2)}) copy-start(f32[1,8,64,2048]{3,2,1,0:T(8,128)} %param.6) | copy-start | bytes 12582916
  23.8 39.0 %collective-permute-start.3 = (bf16[4,1,64,2048]{3,2,1,0:T(8,128)(2,1)S(1)}, bf16[4,1,64,2048]{3,2,1,0:T(8,128)(2,1)S(1)}, u32[]{:S(2)}, u32[]{:S(2)}) collective-permute-start(bf16[4,1,64,2048]{3,2,1,0:T(8,128)(2,1)S(1)} %fusion), channel_id=1, source_target_pairs={{0,16},{8,24},{16,0},{24,8},{1,17},{9,25},{17,1},{25,9},{2,18},{10... | collective-permute-start | bytes 3145736 | tf_op jit(solution)/shard_map/ppermute | solution.py:23
  32.9 46.0 %collective-permute-start.13 = (bf16[1,64,2048]{2,1,0:T(8,128)(2,1)S(1)}, bf16[1,64,2048]{2,1,0:T(8,128)(2,1)S(1)}, u32[]{:S(2)}, u32[]{:S(2)}) collective-permute-start(bf16[1,64,2048]{2,1,0:T(8,128)(2,1)S(1)} %bitcast.123), channel_id=1, source_target_pairs={{0,6},{1,7},{2,4},{3,5},{4,2},{5,3},{6,0},{7,1},{8,14},{9,15},{10,... | collective-permute-start | bytes 786440 | tf_op jit(solution)/shard_map/ppermute | solution.py:23
  37.0 43.5 %collective-permute-start.16 = (bf16[1,64,2048]{2,1,0:T(8,128)(2,1)S(1)}, bf16[1,64,2048]{2,1,0:T(8,128)(2,1)S(1)}, u32[]{:S(2)}, u32[]{:S(2)}) collective-permute-start(bf16[1,64,2048]{2,1,0:T(8,128)(2,1)S(1)} %bitcast.122), channel_id=1, source_target_pairs={{0,7},{1,6},{2,5},{3,4},{4,3},{5,2},{6,1},{7,0},{8,15},{9,14},{10,... | collective-permute-start | bytes 786440 | tf_op jit(solution)/shard_map/ppermute | solution.py:23
  65.1 6.4 %copy-start.1 = (f32[1,8,64,2048]{3,2,1,0:T(8,128)}, f32[1,8,64,2048]{3,2,1,0:T(8,128)S(1)}, u32[]{:S(2)}) copy-start(f32[1,8,64,2048]{3,2,1,0:T(8,128)S(1)} %get-tuple-element.25) | copy-start | bytes 12582916
  65.3 8.1 %collective-permute-start.4 = (bf16[1,64,2048]{2,1,0:T(8,128)(2,1)S(1)}, bf16[1,64,2048]{2,1,0:T(8,128)(2,1)S(1)}, u32[]{:S(2)}, u32[]{:S(2)}) collective-permute-start(bf16[1,64,2048]{2,1,0:T(8,128)(2,1)S(1)} %get-tuple-element.40), channel_id=1, source_target_pairs={{0,1},{1,0},{2,3},{3,2},{4,5},{5,4},{6,7},{7,6},{8,9},{9,8},{10,11... | collective-permute-start | bytes 786440 | tf_op jit(solution)/shard_map/ppermute | solution.py:23
  73.4 58.3 %collective-permute-start.5 = (bf16[8,1,64,2048]{3,2,1,0:T(8,128)(2,1)}, bf16[8,1,64,2048]{3,2,1,0:T(8,128)(2,1)}, u32[]{:S(2)}, u32[]{:S(2)}) collective-permute-start(bf16[8,1,64,2048]{3,2,1,0:T(8,128)(2,1)} %add_convert_fusion.1), channel_id=1, source_target_pairs={{0,16},{8,24},{16,0},{24,8},{1,17},{9,25},{17,1},{25,9},{2,18},{10... | collective-permute-start | bytes 6291464 | tf_op jit(solution)/shard_map/ppermute | solution.py:23
  75.0 20.2 %collective-permute-start.10 = (bf16[1,64,2048]{2,1,0:T(8,128)(2,1)S(1)}, bf16[1,64,2048]{2,1,0:T(8,128)(2,1)S(1)}, u32[]{:S(2)}, u32[]{:S(2)}) collective-permute-start(bf16[1,64,2048]{2,1,0:T(8,128)(2,1)S(1)} %get-tuple-element.42), channel_id=1, source_target_pairs={{0,4},{1,5},{2,6},{3,7},{4,0},{5,1},{6,2},{7,3},{8,12},{9,13},{10,... | collective-permute-start | bytes 786440 | tf_op jit(solution)/shard_map/ppermute | solution.py:23
  77.7 22.9 %collective-permute-start.11 = (bf16[1,64,2048]{2,1,0:T(8,128)(2,1)S(1)}, bf16[1,64,2048]{2,1,0:T(8,128)(2,1)S(1)}, u32[]{:S(2)}, u32[]{:S(2)}) collective-permute-start(bf16[1,64,2048]{2,1,0:T(8,128)(2,1)S(1)} %get-tuple-element.41), channel_id=1, source_target_pairs={{0,5},{1,4},{2,7},{3,6},{4,1},{5,0},{6,3},{7,2},{8,13},{9,12},{10,... | collective-permute-start | bytes 786440 | tf_op jit(solution)/shard_map/ppermute | solution.py:23
  79.0 21.6 %collective-permute-start.6 = (bf16[1,64,2048]{2,1,0:T(8,128)(2,1)S(1)}, bf16[1,64,2048]{2,1,0:T(8,128)(2,1)S(1)}, u32[]{:S(2)}, u32[]{:S(2)}) collective-permute-start(bf16[1,64,2048]{2,1,0:T(8,128)(2,1)S(1)} %get-tuple-element.38), channel_id=1, source_target_pairs={{0,2},{1,3},{2,0},{3,1},{4,6},{5,7},{6,4},{7,5},{8,10},{9,11},{10,... | collective-permute-start | bytes 786440 | tf_op jit(solution)/shard_map/ppermute | solution.py:23
  80.5 20.3 %collective-permute-start.7 = (bf16[1,64,2048]{2,1,0:T(8,128)(2,1)S(1)}, bf16[1,64,2048]{2,1,0:T(8,128)(2,1)S(1)}, u32[]{:S(2)}, u32[]{:S(2)}) collective-permute-start(bf16[1,64,2048]{2,1,0:T(8,128)(2,1)S(1)} %get-tuple-element.37), channel_id=1, source_target_pairs={{0,3},{1,2},{2,1},{3,0},{4,7},{5,6},{6,5},{7,4},{8,11},{9,10},{10,... | collective-permute-start | bytes 786440 | tf_op jit(solution)/shard_map/ppermute | solution.py:23
  113.6 11.6 %collective-permute-start.18 = (bf16[1,64,2048]{2,1,0:T(8,128)(2,1)S(1)}, bf16[1,64,2048]{2,1,0:T(8,128)(2,1)S(1)}, u32[]{:S(2)}, u32[]{:S(2)}) collective-permute-start(bf16[1,64,2048]{2,1,0:T(8,128)(2,1)S(1)} %get-tuple-element.18), channel_id=1, source_target_pairs={{0,1},{1,0},{2,3},{3,2},{4,5},{5,4},{6,7},{7,6},{8,9},{9,8},{10,11... | collective-permute-start | bytes 786440 | tf_op jit(solution)/shard_map/ppermute | solution.py:23
  115.2 20.3 %collective-permute-start.17 = (bf16[1,64,2048]{2,1,0:T(8,128)(2,1)S(1)}, bf16[1,64,2048]{2,1,0:T(8,128)(2,1)S(1)}, u32[]{:S(2)}, u32[]{:S(2)}) collective-permute-start(bf16[1,64,2048]{2,1,0:T(8,128)(2,1)S(1)} %get-tuple-element.16), channel_id=1, source_target_pairs={{0,7},{1,6},{2,5},{3,4},{4,3},{5,2},{6,1},{7,0},{8,15},{9,14},{10,... | collective-permute-start | bytes 786440 | tf_op jit(solution)/shard_map/ppermute | solution.py:23
  119.7 21.2 %collective-permute-start.19 = (bf16[1,64,2048]{2,1,0:T(8,128)(2,1)S(1)}, bf16[1,64,2048]{2,1,0:T(8,128)(2,1)S(1)}, u32[]{:S(2)}, u32[]{:S(2)}) collective-permute-start(bf16[1,64,2048]{2,1,0:T(8,128)(2,1)S(1)} %get-tuple-element.19), channel_id=1, source_target_pairs={{0,2},{1,3},{2,0},{3,1},{4,6},{5,7},{6,4},{7,5},{8,10},{9,11},{10,... | collective-permute-start | bytes 786440 | tf_op jit(solution)/shard_map/ppermute | solution.py:23
  119.7 22.7 %collective-permute-start.20 = (bf16[1,64,2048]{2,1,0:T(8,128)(2,1)S(1)}, bf16[1,64,2048]{2,1,0:T(8,128)(2,1)S(1)}, u32[]{:S(2)}, u32[]{:S(2)}) collective-permute-start(bf16[1,64,2048]{2,1,0:T(8,128)(2,1)S(1)} %get-tuple-element.20), channel_id=1, source_target_pairs={{0,3},{1,2},{2,1},{3,0},{4,7},{5,6},{6,5},{7,4},{8,11},{9,10},{10,... | collective-permute-start | bytes 786440 | tf_op jit(solution)/shard_map/ppermute | solution.py:23
  125.2 18.8 %collective-permute-start.21 = (bf16[1,64,2048]{2,1,0:T(8,128)(2,1)S(1)}, bf16[1,64,2048]{2,1,0:T(8,128)(2,1)S(1)}, u32[]{:S(2)}, u32[]{:S(2)}) collective-permute-start(bf16[1,64,2048]{2,1,0:T(8,128)(2,1)S(1)} %get-tuple-element.21), channel_id=1, source_target_pairs={{0,6},{1,7},{2,4},{3,5},{4,2},{5,3},{6,0},{7,1},{8,14},{9,15},{10,... | collective-permute-start | bytes 786440 | tf_op jit(solution)/shard_map/ppermute | solution.py:23
  131.7 26.7 %collective-permute-start.22 = (bf16[1,64,2048]{2,1,0:T(8,128)(2,1)S(1)}, bf16[1,64,2048]{2,1,0:T(8,128)(2,1)S(1)}, u32[]{:S(2)}, u32[]{:S(2)}) collective-permute-start(bf16[1,64,2048]{2,1,0:T(8,128)(2,1)S(1)} %get-tuple-element.22), channel_id=1, source_target_pairs={{0,5},{1,4},{2,7},{3,6},{4,1},{5,0},{6,3},{7,2},{8,13},{9,12},{10,... | collective-permute-start | bytes 786440 | tf_op jit(solution)/shard_map/ppermute | solution.py:23
  135.5 25.8 %collective-permute-start.23 = (bf16[1,64,2048]{2,1,0:T(8,128)(2,1)S(1)}, bf16[1,64,2048]{2,1,0:T(8,128)(2,1)S(1)}, u32[]{:S(2)}, u32[]{:S(2)}) collective-permute-start(bf16[1,64,2048]{2,1,0:T(8,128)(2,1)S(1)} %get-tuple-element.23), channel_id=1, source_target_pairs={{0,4},{1,5},{2,6},{3,7},{4,0},{5,1},{6,2},{7,3},{8,12},{9,13},{10,... | collective-permute-start | bytes 786440 | tf_op jit(solution)/shard_map/ppermute | solution.py:23
  161.5 1.3 copy-start.2
  161.5 2.0 %copy-start.3 = (bf16[1,8,64,2048]{3,2,1,0:T(8,128)(2,1)}, bf16[1,8,64,2048]{3,2,1,0:T(8,128)(2,1)S(1)}, u32[]{:S(2)}) copy-start(bf16[1,8,64,2048]{3,2,1,0:T(8,128)(2,1)S(1)} %get-tuple-element.43) | copy-start | bytes 6291460

commit v7 on v6

--- a/solution.py
+++ b/solution.py
@@ -119,7 +119,7 @@
 def grouped(shards):
     groups = []
     top = shards
-    for length in (shards // 8, shards // 8, shards // 4, shards // 2):
+    for length in (shards // 4,) * 4:
         if length:
             top -= length
             groups.append((top, length))
@@ -148,20 +148,32 @@
 
     new_tracker = jnp.zeros(shape, F32)
     blocks = [None] * shards
+    unit = shards // 8
+    arrived = []
+    ready = None
     for turn, (lowest, length) in enumerate(grouped(shards)):
         if turn == 2:
-            tracker = after(tracker, sent)
+            tracker = after(tracker, ready)
         start = (here ^ lowest) // length * length
         own = taken(tracker, start, length)
         near = swapped(own.astype(BF16), "rep", 1)
         mixed = first * own + (1.0 - first) * near.astype(F32)
         sent = mixed.astype(BF16)
+        if turn == 2:
+            sent = after(sent, arrived[1])
+        elif turn == 3:
+            sent = after(sent, blocks[7 * unit], blocks[6 * unit])
         far = swapped(sent, "rep", 2)
+        arrived.append(far)
+        if turn == 3:
+            far = after(far, blocks[5 * unit], blocks[4 * unit])
         group = second * mixed + (1.0 - second) * far.astype(F32)
         group += taken(grad_new, start, length).astype(F32)
         group -= taken(grad_old, start, length).astype(F32)
         for offset in reversed(range(lowest, lowest + length)):
             block = taken(group, (here ^ offset) % length, 1)[0].astype(BF16)
+            if ready is None:
+                ready = block
             blocks[offset] = swapped(block, "shard", offset) if offset else block
         new_tracker = lax.dynamic_update_slice_in_dim(new_tracker, group, start, axis=0)
 
@@ -169,7 +181,7 @@
     weight_own = (
         first * weight.astype(F32) + (1.0 - first) * weight_near.astype(F32)
     ).astype(BF16)
-    weight_own = after(weight_own, far, blocks[1])
+    weight_own = after(weight_own, arrived[-1], blocks[1:])
     weight_far = swapped(weight_own, "rep", 2)
     mixed_weight = (
         second * weight_own.astype(F32) + (1.0 - second) * weight_far.astype(F32)

time: 164 us -> 194 us (1.18)
  waiting for transfers between devices: 71.5 us -> 92.3 us
  other arithmetic: 25.6 us -> 35 us
  starting transfers between devices: 41.5 us -> 37.7 us
  local copies, waits for them, and re-layouts: 10 us -> 13.1 us
    ppermute x24, waiting for transfers between devices: 71.5 us -> 92.3 us  [swapped(): lax.ppermute(values, axis, [(i, i ^ offset) for i in range(lax.axis_size(...]
    dynamic_update_slice x4, other arithmetic: 8.01 us -> 16.7 us  [local(): lax.dynamic_update_slice_in_dim(new_tracker, group, start, axis=0)]
    ppermute x24, starting transfers between devices: 41.5 us -> 37.7 us  [swapped(): lax.ppermute(values, axis, [(i, i ^ offset) for i in range(lax.axis_size(...]
    reshape x1, local copies, waits for them, and re-layouts: 0.49 us -> 2.53 us  [local(): new_tracker.reshape(shape)]
  transfers between devices with their start and end apart: 24 -> 24, of which waited for: 12 -> 14; matrix products, arithmetic and copies ran while one was open for 16% -> 16% of each run, Pallas kernels for 8% -> 7%
where the time goes in v7:
time: 194 us; the launch traced here: 193 us
  waiting for transfers between devices  92.3 us (48%)
  starting transfers between devices  37.7 us (19%)
  other arithmetic  35 us (18%)
  local copies, waits for them, and re-layouts  13.1 us (7%)
  Pallas kernels  12.8 us (7%)
  between operations  2.18 us (1%)
    ppermute x24, waiting for transfers between devices, swapped(): lax.ppermute(values, axis, [(i, i ^ offset) for i in range(lax.axis_size(...  92.3 us
    ppermute x24, starting transfers between devices, swapped(): lax.ppermute(values, axis, [(i, i ^ offset) for i in range(lax.axis_size(...  37.7 us
    dynamic_update_slice x4, other arithmetic, local(): lax.dynamic_update_slice_in_dim(new_tracker, group, start, axis=0)  16.7 us
    pallas_call x1, Pallas kernels, orthogonalize(): pl.pallas_call(body, grid=(each,), in_specs=[block] * count, out_specs=[b...  12.8 us
    convert_element_type x3, other arithmetic, local(): sent = mixed.astype(BF16)  9.4 us
    convert_element_type x3, local copies, waits for them, and re-layouts, local(): near = swapped(own.astype(BF16), 'rep', 1)  5.86 us
    convert_element_type x1, other arithmetic, local(): weight_own = (first * weight.astype(F32) + (1.0 - first) * weight_near.as...  4.42 us
  transfers between devices with their start and end apart: 24, of which 14 were waited for; matrix products, arithmetic and copies ran while one was open for 16% of the time, Pallas kernels for 7%

profile of v7, /device:TPU:0, one launch (start us, length us, event | category | flops | bytes accessed | tf_op | source)
XLA Modules:
  0.0 193.1 jit_solution(612158322640507846)
XLA Ops:
  0.7 1.7 fusion.7
  2.4 0.5 collective-permute-start.1
  3.0 0.6 constant_dynamic-slice_fusion.1
  4.5 0.7 collective-permute-done.7
  5.2 3.5 %fusion.5 = (bf16[2,1,64,2048]{3,2,1,0:T(8,128)(2,1)}, bf16[2,1,64,2048]{3,2,1,0:T(8,128)(2,1)}) fusion(bf16[2,1,64,2048]{3,2,1,0:T(8,128)(2,1)S(1)} %collective-permute-done.7, f32[1,8,64,2048]{3,2,1,0:T(8,128)} %param.6, s32[]{:T(128)S(6)} %select_n.150, f32[]{:T(128)S(6)} %sub.63, f32[]{:T(128)} %bitcast.1, ...), kind=kLoop, calls=%fused_computation.28 | loop fusion | flops 2621440 | bytes 4194320 | tf_op jit(solution)/shard_map/convert_element_type | solution.py:161
  8.7 2.9 %collective-permute-start.2 = (bf16[2,1,64,2048]{3,2,1,0:T(8,128)(2,1)}, bf16[2,1,64,2048]{3,2,1,0:T(8,128)(2,1)S(1)}, u32[]{:S(2)}, u32[]{:S(2)}) collective-permute-start(bf16[2,1,64,2048]{3,2,1,0:T(8,128)(2,1)} %get-tuple-element.40), channel_id=1, source_target_pairs={{0,16},{8,24},{16,0},{24,8},{1,17},{9,25},{17,1},{25,9},{2,18},{10... | collective-permute-start | bytes 1572872 | tf_op jit(solution)/shard_map/ppermute | solution.py:23
  12.2 11.8 %collective-permute-done.2 = bf16[2,1,64,2048]{3,2,1,0:T(8,128)(2,1)S(1)} collective-permute-done((bf16[2,1,64,2048]{3,2,1,0:T(8,128)(2,1)}, bf16[2,1,64,2048]{3,2,1,0:T(8,128)(2,1)S(1)}, u32[]{:S(2)}, u32[]{:S(2)}) %collective-permute-start.2) | collective-permute-done | bytes 524320 | tf_op jit(solution)/shard_map/ppermute | solution.py:23
  24.0 2.5 %reshape.480 = f32[1,8,64,2048]{3,2,1,0:T(8,128)} broadcast(f32[]{:T(128)} %constant.135.clone.1), dimensions={} | broadcast | bytes 4194308 | tf_op jit(solution)/shard_map/reshape | solution.py:208
  26.5 4.0 %bitcast_dynamic-update-slice_fusion.3 = (f32[1,8,64,2048]{3,2,1,0:T(8,128)}, bf16[2,1,64,2048]{3,2,1,0:T(8,128)(2,1)S(1)}) fusion(f32[1,8,64,2048]{3,2,1,0:T(8,128)} %reshape.480, s32[]{:T(128)S(6)} %select_n.142, bf16[1,8,64,2048]{3,2,1,0:T(8,128)(2,1)S(1)} %copy-done, bf16[1,8,64,2048]{3,2,1,0:T(8,128)(2,1)} %param.7, ...), kind=kLoop, calls=%fused_computation.18 | loop fusion | flops 3407872 | bytes 4719628 | tf_op jit(solution)/shard_map/dynamic_update_slice | solution.py:178
  30.6 0.8 fusion.17
  31.3 2.1 %dynamic-slice_convert_fusion.2 = bf16[2,1,64,2048]{3,2,0,1:T(8,128)(2,1)} fusion(f32[8,1,64,2048]{3,2,0,1:T(8,128)} %bitcast.196, s32[]{:T(128)S(6)} %select_n.146), kind=kLoop, calls=%fused_computation.23 | loop fusion | bytes 1048580 | tf_op jit(solution)/shard_map/convert_element_type | solution.py:159
  33.4 2.1 %dynamic-slice_convert_fusion = bf16[2,1,64,2048]{3,2,1,0:T(8,128)(2,1)} fusion(f32[8,1,64,2048]{3,2,1,0:T(8,128)} %bitcast.197, s32[]{:T(128)S(6)} %select_n.158), kind=kLoop, calls=%fused_computation.21 | loop fusion | bytes 1048580 | tf_op jit(solution)/shard_map/convert_element_type | solution.py:159
  35.5 0.5 collective-permute-start.12
  36.0 1.7 collective-permute-start.8
  37.8 4.6 %collective-permute-start.4 = (bf16[1,64,2048]{2,1,0:T(8,128)(2,1)}, bf16[1,64,2048]{2,1,0:T(8,128)(2,1)S(1)}, u32[]{:S(2)}, u32[]{:S(2)}) collective-permute-start(bf16[1,64,2048]{2,1,0:T(8,128)(2,1)} %get-tuple-element.50), channel_id=1, source_target_pairs={{0,7},{1,6},{2,5},{3,4},{4,3},{5,2},{6,1},{7,0},{8,15},{9,14},{10,... | collective-permute-start | bytes 786440 | tf_op jit(solution)/shard_map/ppermute | solution.py:23
  42.5 2.9 %fusion.2 = bf16[2,1,64,2048]{3,2,1,0:T(8,128)(2,1)} fusion(bf16[2,1,64,2048]{3,2,0,1:T(8,128)(2,1)S(1)} %collective-permute-done.3, f32[8,1,64,2048]{3,2,0,1:T(8,128)} %bitcast.198, s32[]{:T(128)S(6)} %select_n.146, f32[]{:T(128)S(6)} %sub.63, f32[]{:T(128)} %bitcast.1), kind=kLoop, calls=%fused_computation.25 | loop fusion | flops 1310720 | bytes 2097164 | tf_op jit(solution)/shard_map/convert_element_type | solution.py:161
  45.5 4.4 %collective-permute-done.4.refs_7_ = bf16[1,64,2048]{2,1,0:T(8,128)(2,1)S(1)} collective-permute-done((bf16[1,64,2048]{2,1,0:T(8,128)(2,1)}, bf16[1,64,2048]{2,1,0:T(8,128)(2,1)S(1)}, u32[]{:S(2)}, u32[]{:S(2)}) %collective-permute-start.4) | collective-permute-done | bytes 262176 | tf_op jit(solution)/shard_map/ppermute | solution.py:23
  49.9 5.0 %collective-permute-done.5.refs_6_ = bf16[1,64,2048]{2,1,0:T(8,128)(2,1)S(1)} collective-permute-done((bf16[1,64,2048]{2,1,0:T(8,128)(2,1)S(1)}, bf16[1,64,2048]{2,1,0:T(8,128)(2,1)S(1)}, u32[]{:S(2)}, u32[]{:S(2)}) %collective-permute-start.5) | collective-permute-done | bytes 262176 | tf_op jit(solution)/shard_map/ppermute | solution.py:23
  54.9 0.5 collective-permute-start.6
  55.4 3.0 %fusion.4 = bf16[2,1,64,2048]{3,2,1,0:T(8,128)(2,1)} fusion(bf16[2,1,64,2048]{3,2,1,0:T(8,128)(2,1)} %collective-permute-done.12, f32[8,1,64,2048]{3,2,1,0:T(8,128)} %bitcast.199, s32[]{:T(128)S(6)} %select_n.158, f32[]{:T(128)S(6)} %sub.63, f32[]{:T(128)} %bitcast.1), kind=kLoop, calls=%fused_computation.27 | loop fusion | flops 1310720 | bytes 2097164 | tf_op jit(solution)/shard_map/convert_element_type | solution.py:161
  58.4 1.5 collective-permute-start.13
  59.9 4.1 %bitcast_dynamic-update-slice_fusion.2 = (f32[1,8,64,2048]{3,2,1,0:T(8,128)}, bf16[2,1,64,2048]{3,2,1,0:T(8,128)(2,1)S(1)}) fusion(f32[1,8,64,2048]{3,2,1,0:T(8,128)} %get-tuple-element.37, s32[]{:T(128)S(6)} %select_n.150, bf16[1,8,64,2048]{3,2,1,0:T(8,128)(2,1)S(1)} %copy-done, bf16[1,8,64,2048]{3,2,1,0:T(8,128)(2,1)} %param.7, ...), kind=kLoop, calls=%fused_computation.17 | loop fusion | flops 3407872 | bytes 4719628 | tf_op jit(solution)/shard_map/dynamic_update_slice | solution.py:178
  64.0 0.7 fusion.19
  64.7 11.9 %collective-permute-start.10 = (bf16[1,64,2048]{2,1,0:T(8,128)(2,1)}, bf16[1,64,2048]{2,1,0:T(8,128)(2,1)S(1)}, u32[]{:S(2)}, u32[]{:S(2)}) collective-permute-start(bf16[1,64,2048]{2,1,0:T(8,128)(2,1)} %get-tuple-element.47), channel_id=1, source_target_pairs={{0,4},{1,5},{2,6},{3,7},{4,0},{5,1},{6,2},{7,3},{8,12},{9,13},{10,... | collective-permute-start | bytes 786440 | tf_op jit(solution)/shard_map/ppermute | solution.py:23
  76.6 18.0 %collective-permute-done.10.refs_4_ = bf16[1,64,2048]{2,1,0:T(8,128)(2,1)S(1)} collective-permute-done((bf16[1,64,2048]{2,1,0:T(8,128)(2,1)}, bf16[1,64,2048]{2,1,0:T(8,128)(2,1)S(1)}, u32[]{:S(2)}, u32[]{:S(2)}) %collective-permute-start.10) | collective-permute-done | bytes 262176 | tf_op jit(solution)/shard_map/ppermute | solution.py:23
  94.6 4.3 %collective-permute-done.9.refs_5_ = bf16[1,64,2048]{2,1,0:T(8,128)(2,1)S(1)} collective-permute-done((bf16[1,64,2048]{2,1,0:T(8,128)(2,1)S(1)}, bf16[1,64,2048]{2,1,0:T(8,128)(2,1)S(1)}, u32[]{:S(2)}, u32[]{:S(2)}) %collective-permute-start.9) | collective-permute-done | bytes 262176 | tf_op jit(solution)/shard_map/ppermute | solution.py:23
  99.0 4.4 %bitcast_dynamic-update-slice_fusion.1 = (f32[1,8,64,2048]{3,2,1,0:T(8,128)}, bf16[2,1,64,2048]{3,2,1,0:T(8,128)(2,1)S(1)}) fusion(f32[1,8,64,2048]{3,2,1,0:T(8,128)} %get-tuple-element.35, s32[]{:T(128)S(6)} %select_n.158, bf16[1,8,64,2048]{3,2,1,0:T(8,128)(2,1)S(1)} %copy-done, bf16[1,8,64,2048]{3,2,1,0:T(8,128)(2,1)} %param.7, ...), kind=kLoop, calls=%fused_computation.16 | loop fusion | flops 3407872 | bytes 4719628 | tf_op jit(solution)/shard_map/dynamic_update_slice | solution.py:178
  103.4 4.2 %bitcast_dynamic-update-slice_fusion = (f32[1,8,64,2048]{3,2,1,0:T(8,128)}, bf16[2,1,64,2048]{3,2,1,0:T(8,128)(2,1)S(1)}) fusion(f32[1,8,64,2048]{3,2,1,0:T(8,128)} %get-tuple-element.33, s32[]{:T(128)S(6)} %select_n.146, bf16[1,8,64,2048]{3,2,1,0:T(8,128)(2,1)S(1)} %copy-done, bf16[1,8,64,2048]{3,2,1,0:T(8,128)(2,1)} %param.7, ...), kind=kLoop, calls=%fused_computation.15 | loop fusion | flops 3407872 | bytes 4719628 | tf_op jit(solution)/shard_map/dynamic_update_slice | solution.py:178
  107.6 1.6 collective-permute-start.11
  109.3 2.0 %collective-permute-start.15 = (bf16[1,64,2048]{2,1,0:T(8,128)(2,1)S(1)}, bf16[1,64,2048]{2,1,0:T(8,128)(2,1)S(1)}, u32[]{:S(2)}, u32[]{:S(2)}) collective-permute-start(bf16[1,64,2048]{2,1,0:T(8,128)(2,1)S(1)} %get-tuple-element.43), channel_id=1, source_target_pairs={{0,3},{1,2},{2,1},{3,0},{4,7},{5,6},{6,5},{7,4},{8,11},{9,10},{10,... | collective-permute-start | bytes 786440 | tf_op jit(solution)/shard_map/ppermute | solution.py:23
  111.3 4.4 %add_convert_fusion.1 = bf16[8,1,64,2048]{3,2,1,0:T(8,128)(2,1)} fusion(bf16[8,1,64,2048]{3,2,1,0:T(8,128)(2,1)} %collective-permute-done, f32[]{:T(128)S(6)} %sub.63, f32[]{:T(128)} %bitcast.1, bf16[1,8,64,2048]{3,2,1,0:T(8,128)(2,1)S(1)} %copy-done.3), kind=kLoop, calls=%fused_computation.1 | loop fusion | flops 6291456 | bytes 6291464 | tf_op jit(solution)/shard_map/convert_element_type | solution.py:183
  115.9 2.6 %collective-permute-done.14.refs_2_ = bf16[1,64,2048]{2,1,0:T(8,128)(2,1)S(1)} collective-permute-done((bf16[1,64,2048]{2,1,0:T(8,128)(2,1)S(1)}, bf16[1,64,2048]{2,1,0:T(8,128)(2,1)S(1)}, u32[]{:S(2)}, u32[]{:S(2)}) %collective-permute-start.14) | collective-permute-done | bytes 262176 | tf_op jit(solution)/shard_map/ppermute | solution.py:23
  118.6 3.1 %collective-permute-done.15.refs_3_ = bf16[1,64,2048]{2,1,0:T(8,128)(2,1)S(1)} collective-permute-done((bf16[1,64,2048]{2,1,0:T(8,128)(2,1)S(1)}, bf16[1,64,2048]{2,1,0:T(8,128)(2,1)S(1)}, u32[]{:S(2)}, u32[]{:S(2)}) %collective-permute-start.15) | collective-permute-done | bytes 262176 | tf_op jit(solution)/shard_map/ppermute | solution.py:23
  121.7 0.5 collective-permute-start.16
  122.2 12.8 %orthogonalize.1 = (bf16[1,64,2048]{2,1,0:T(8,128)(2,1)S(1)}, bf16[1,64,2048]{2,1,0:T(8,128)(2,1)S(1)}, bf16[1,64,2048]{2,1,0:T(8,128)(2,1)S(1)}, bf16[1,64,2048...) custom-call(bf16[1,64,2048]{2,1,0:T(8,128)(2,1)S(1)} %get-tuple-elem, ...), custom_call_target="tpu_custom_call" | custom-call | flops 11005853696 | bytes 4194304 | tf_op jit(solution)/shard_map/orthogonalize/pallas_call | solution.py:102
  135.0 1.6 collective-permute-start.18
  136.6 0.6 collective-permute-start.17
  137.2 3.0 %collective-permute-start.20 = (bf16[1,64,2048]{2,1,0:T(8,128)(2,1)S(1)}, bf16[1,64,2048]{2,1,0:T(8,128)(2,1)S(1)}, u32[]{:S(2)}, u32[]{:S(2)}) collective-permute-start(bf16[1,64,2048]{2,1,0:T(8,128)(2,1)S(1)} %get-tuple-element.26), channel_id=1, source_target_pairs={{0,3},{1,2},{2,1},{3,0},{4,7},{5,6},{6,5},{7,4},{8,11},{9,10},{10,... | collective-permute-start | bytes 786440 | tf_op jit(solution)/shard_map/ppermute | solution.py:23
  140.2 8.6 %collective-permute-done.18 = bf16[1,64,2048]{2,1,0:T(8,128)(2,1)S(1)} collective-permute-done((bf16[1,64,2048]{2,1,0:T(8,128)(2,1)S(1)}, bf16[1,64,2048]{2,1,0:T(8,128)(2,1)S(1)}, u32[]{:S(2)}, u32[]{:S(2)}) %collective-permute-start.18) | collective-permute-done | bytes 262176 | tf_op jit(solution)/shard_map/ppermute | solution.py:23
  148.8 0.2 reshape.477.clone
  149.1 18.1 %collective-permute-done.16 = bf16[8,1,64,2048]{3,2,1,0:T(8,128)(2,1)} collective-permute-done((bf16[8,1,64,2048]{3,2,1,0:T(8,128)(2,1)}, bf16[8,1,64,2048]{3,2,1,0:T(8,128)(2,1)}, u32[]{:S(2)}, u32[]{:S(2)}) %collective-permute-start.16) | collective-permute-done | bytes 2097184 | tf_op jit(solution)/shard_map/ppermute | solution.py:23
  167.2 3.7 %add_convert_fusion = bf16[8,1,64,2048]{3,2,1,0:T(8,128)(2,1)S(1)} fusion(bf16[8,1,64,2048]{3,2,1,0:T(8,128)(2,1)} %collective-permute-done.16, bf16[8,1,64,2048]{3,2,1,0:T(8,128)(2,1)} %add_convert_fusion.1, f32[]{:T(128)S(6)} %sub.65, f32[]{:T(128)} %bitcast), kind=kLoop, calls=%fused_computation | loop fusion | flops 6291456 | bytes 6291464 | tf_op jit(solution)/shard_map/convert_element_type | solution.py:188
  171.0 3.9 %collective-permute-start.23 = (bf16[1,64,2048]{2,1,0:T(8,128)(2,1)S(1)}, bf16[1,64,2048]{2,1,0:T(8,128)(2,1)S(1)}, u32[]{:S(2)}, u32[]{:S(2)}) collective-permute-start(bf16[1,64,2048]{2,1,0:T(8,128)(2,1)S(1)} %get-tuple-element.29), channel_id=1, source_target_pairs={{0,4},{1,5},{2,6},{3,7},{4,0},{5,1},{6,2},{7,3},{8,12},{9,13},{10,... | collective-permute-start | bytes 786440 | tf_op jit(solution)/shard_map/ppermute | solution.py:23
  174.9 0.2 reshape.477.clone.1
  175.7 11.0 %collective-permute-done.22 = bf16[1,64,2048]{2,1,0:T(8,128)(2,1)S(1)} collective-permute-done((bf16[1,64,2048]{2,1,0:T(8,128)(2,1)S(1)}, bf16[1,64,2048]{2,1,0:T(8,128)(2,1)S(1)}, u32[]{:S(2)}, u32[]{:S(2)}) %collective-permute-start.22) | collective-permute-done | bytes 262176 | tf_op jit(solution)/shard_map/ppermute | solution.py:23
  186.8 4.1 %collective-permute-done.23 = bf16[1,64,2048]{2,1,0:T(8,128)(2,1)S(1)} collective-permute-done((bf16[1,64,2048]{2,1,0:T(8,128)(2,1)S(1)}, bf16[1,64,2048]{2,1,0:T(8,128)(2,1)S(1)}, u32[]{:S(2)}, u32[]{:S(2)}) %collective-permute-start.23) | collective-permute-done | bytes 262176 | tf_op jit(solution)/shard_map/ppermute | solution.py:23
  191.1 1.3 copy-done.1
  192.4 0.7 copy-done.2
  (49 shorter events, 1.7 us)
Async XLA Ops:
  0.6 2.4 %copy-start.8 = (s32[4,2]{0,1:T(2,128)S(1)}, s32[4,2]{0,1:T(2,128)}, u32[]{:S(2)}) copy-start(s32[4,2]{0,1:T(2,128)} %param.9) | copy-start | bytes 100
  2.4 2.1 %collective-permute-start.1 = (bf16[2,1,64,2048]{3,2,0,1:T(8,128)(2,1)S(1)}, bf16[2,1,64,2048]{3,2,0,1:T(8,128)(2,1)S(1)}, u32[]{:S(2)}, u32[]{:S(2)}) collective-permute-start(bf16[2,1,64,2048]{3,2,0,1:T(8,128)(2,1)S(1)} %get-tuple-element.42), channel_id=1, source_target_pairs={{0,8},{8,0},{16,24},{24,16},{1,9},{9,1},{17,25},{25,17},{2,10},{10... | collective-permute-start | bytes 1572872 | tf_op jit(solution)/shard_map/ppermute | solution.py:23
  2.9 2.3 %collective-permute-start.7 = (bf16[2,1,64,2048]{3,2,1,0:T(8,128)(2,1)S(1)}, bf16[2,1,64,2048]{3,2,1,0:T(8,128)(2,1)S(1)}, u32[]{:S(2)}, u32[]{:S(2)}) collective-permute-start(bf16[2,1,64,2048]{3,2,1,0:T(8,128)(2,1)S(1)} %get-tuple-element.41), channel_id=1, source_target_pairs={{0,8},{8,0},{16,24},{24,16},{1,9},{9,1},{17,25},{25,17},{2,10},{10... | collective-permute-start | bytes 1572872 | tf_op jit(solution)/shard_map/ppermute | solution.py:23
  5.2 3.5 %copy-start.6 = (bf16[2,1,64,2048]{3,2,1,0:T(8,128)(2,1)}, bf16[2,1,64,2048]{3,2,1,0:T(8,128)(2,1)S(1)}, u32[]{:S(2)}) copy-start(bf16[2,1,64,2048]{3,2,1,0:T(8,128)(2,1)S(1)} %collective-permute-done.7) | copy-start | bytes 1572868
  8.7 15.3 %collective-permute-start.2 = (bf16[2,1,64,2048]{3,2,1,0:T(8,128)(2,1)}, bf16[2,1,64,2048]{3,2,1,0:T(8,128)(2,1)S(1)}, u32[]{:S(2)}, u32[]{:S(2)}) collective-permute-start(bf16[2,1,64,2048]{3,2,1,0:T(8,128)(2,1)} %get-tuple-element.40), channel_id=1, source_target_pairs={{0,16},{8,24},{16,0},{24,8},{1,17},{9,25},{17,1},{25,9},{2,18},{10... | collective-permute-start | bytes 1572872 | tf_op jit(solution)/shard_map/ppermute | solution.py:23
  12.2 14.3 %copy-start = (bf16[1,8,64,2048]{3,2,1,0:T(8,128)(2,1)S(1)}, bf16[1,8,64,2048]{3,2,1,0:T(8,128)(2,1)}, u32[]{:S(2)}) copy-start(bf16[1,8,64,2048]{3,2,1,0:T(8,128)(2,1)} %param.8) | copy-start | bytes 6291460
  33.4 8.9 %collective-permute-start.3 = (bf16[2,1,64,2048]{3,2,0,1:T(8,128)(2,1)}, bf16[2,1,64,2048]{3,2,0,1:T(8,128)(2,1)S(1)}, u32[]{:S(2)}, u32[]{:S(2)}) collective-permute-start(bf16[2,1,64,2048]{3,2,0,1:T(8,128)(2,1)} %dynamic-slice_convert_fusion.2), channel_id=1, source_target_pairs={{0,8},{8,0},{16,24},{24,16},{1,9},{9,1},{17,25},{25,17},{2,10},{10... | collective-permute-start | bytes 1572872 | tf_op jit(solution)/shard_map/ppermute | solution.py:23
  35.5 19.9 %collective-permute-start.12 = (bf16[2,1,64,2048]{3,2,1,0:T(8,128)(2,1)}, bf16[2,1,64,2048]{3,2,1,0:T(8,128)(2,1)}, u32[]{:S(2)}, u32[]{:S(2)}) collective-permute-start(bf16[2,1,64,2048]{3,2,1,0:T(8,128)(2,1)} %dynamic-slice_convert_fusion), channel_id=1, source_target_pairs={{0,8},{8,0},{16,24},{24,16},{1,9},{9,1},{17,25},{25,17},{2,10},{10... | collective-permute-start | bytes 1572872 | tf_op jit(solution)/shard_map/ppermute | solution.py:23
  36.0 75.3 %collective-permute-start = (bf16[8,1,64,2048]{3,2,1,0:T(8,128)(2,1)}, bf16[8,1,64,2048]{3,2,1,0:T(8,128)(2,1)}, u32[]{:S(2)}, u32[]{:S(2)}) collective-permute-start(bf16[8,1,64,2048]{3,2,1,0:T(8,128)(2,1)} %bitcast.202), channel_id=1, source_target_pairs={{0,8},{8,0},{16,24},{24,16},{1,9},{9,1},{17,25},{25,17},{2,10},{10... | collective-permute-start | bytes 6291464 | tf_op jit(solution)/shard_map/ppermute | solution.py:23
  36.0 22.4 %collective-permute-start.8 = (bf16[2,1,64,2048]{3,2,1,0:T(8,128)(2,1)}, bf16[2,1,64,2048]{3,2,1,0:T(8,128)(2,1)S(1)}, u32[]{:S(2)}, u32[]{:S(2)}) collective-permute-start(bf16[2,1,64,2048]{3,2,1,0:T(8,128)(2,1)} %get-tuple-element.39), channel_id=1, source_target_pairs={{0,16},{8,24},{16,0},{24,8},{1,17},{9,25},{17,1},{25,9},{2,18},{10... | collective-permute-start | bytes 1572872 | tf_op jit(solution)/shard_map/ppermute | solution.py:23
  37.8 12.1 %collective-permute-start.4 = (bf16[1,64,2048]{2,1,0:T(8,128)(2,1)}, bf16[1,64,2048]{2,1,0:T(8,128)(2,1)S(1)}, u32[]{:S(2)}, u32[]{:S(2)}) collective-permute-start(bf16[1,64,2048]{2,1,0:T(8,128)(2,1)} %get-tuple-element.50), channel_id=1, source_target_pairs={{0,7},{1,6},{2,5},{3,4},{4,3},{5,2},{6,1},{7,0},{8,15},{9,14},{10,... | collective-permute-start | bytes 786440 | tf_op jit(solution)/shard_map/ppermute | solution.py:23
  42.3 16.1 %copy-start.4 = (bf16[2,1,64,2048]{3,2,0,1:T(8,128)(2,1)}, bf16[2,1,64,2048]{3,2,0,1:T(8,128)(2,1)S(1)}, u32[]{:S(2)}) copy-start(bf16[2,1,64,2048]{3,2,0,1:T(8,128)(2,1)S(1)} %collective-permute-done.3) | copy-start | bytes 1572868
  42.3 17.6 %copy-start.7 = (bf16[2,1,64,2048]{3,2,1,0:T(8,128)(2,1)S(1)}, bf16[2,1,64,2048]{3,2,1,0:T(8,128)(2,1)}, u32[]{:S(2)}) copy-start(bf16[2,1,64,2048]{3,2,1,0:T(8,128)(2,1)} %copy-done.6) | copy-start | bytes 1572868
  42.3 12.6 %collective-permute-start.5 = (bf16[1,64,2048]{2,1,0:T(8,128)(2,1)S(1)}, bf16[1,64,2048]{2,1,0:T(8,128)(2,1)S(1)}, u32[]{:S(2)}, u32[]{:S(2)}) collective-permute-start(bf16[1,64,2048]{2,1,0:T(8,128)(2,1)S(1)} %get-tuple-element.49), channel_id=1, source_target_pairs={{0,6},{1,7},{2,4},{3,5},{4,2},{5,3},{6,0},{7,1},{8,14},{9,15},{10,... | collective-permute-start | bytes 786440 | tf_op jit(solution)/shard_map/ppermute | solution.py:23
  54.9 44.1 %collective-permute-start.6 = (bf16[2,1,64,2048]{3,2,1,0:T(8,128)(2,1)}, bf16[2,1,64,2048]{3,2,1,0:T(8,128)(2,1)}, u32[]{:S(2)}, u32[]{:S(2)}) collective-permute-start(bf16[2,1,64,2048]{3,2,1,0:T(8,128)(2,1)} %fusion.2), channel_id=1, source_target_pairs={{0,16},{8,24},{16,0},{24,8},{1,17},{9,25},{17,1},{25,9},{2,18},{10... | collective-permute-start | bytes 1572872 | tf_op jit(solution)/shard_map/ppermute | solution.py:23
  58.4 40.6 %collective-permute-start.13 = (bf16[2,1,64,2048]{3,2,1,0:T(8,128)(2,1)}, bf16[2,1,64,2048]{3,2,1,0:T(8,128)(2,1)}, u32[]{:S(2)}, u32[]{:S(2)}) collective-permute-start(bf16[2,1,64,2048]{3,2,1,0:T(8,128)(2,1)} %fusion.4), channel_id=1, source_target_pairs={{0,16},{8,24},{16,0},{24,8},{1,17},{9,25},{17,1},{25,9},{2,18},{10... | collective-permute-start | bytes 1572872 | tf_op jit(solution)/shard_map/ppermute | solution.py:23
  64.7 29.9 %collective-permute-start.10 = (bf16[1,64,2048]{2,1,0:T(8,128)(2,1)}, bf16[1,64,2048]{2,1,0:T(8,128)(2,1)S(1)}, u32[]{:S(2)}, u32[]{:S(2)}) collective-permute-start(bf16[1,64,2048]{2,1,0:T(8,128)(2,1)} %get-tuple-element.47), channel_id=1, source_target_pairs={{0,4},{1,5},{2,6},{3,7},{4,0},{5,1},{6,2},{7,3},{8,12},{9,13},{10,... | collective-permute-start | bytes 786440 | tf_op jit(solution)/shard_map/ppermute | solution.py:23
  76.6 22.3 %collective-permute-start.9 = (bf16[1,64,2048]{2,1,0:T(8,128)(2,1)S(1)}, bf16[1,64,2048]{2,1,0:T(8,128)(2,1)S(1)}, u32[]{:S(2)}, u32[]{:S(2)}) collective-permute-start(bf16[1,64,2048]{2,1,0:T(8,128)(2,1)S(1)} %get-tuple-element.48), channel_id=1, source_target_pairs={{0,5},{1,4},{2,7},{3,6},{4,1},{5,0},{6,3},{7,2},{8,13},{9,12},{10,... | collective-permute-start | bytes 786440 | tf_op jit(solution)/shard_map/ppermute | solution.py:23
  99.0 4.4 %copy-start.5 = (bf16[2,1,64,2048]{3,2,0,1:T(8,128)(2,1)S(1)}, bf16[2,1,64,2048]{3,2,0,1:T(8,128)(2,1)}, u32[]{:S(2)}) copy-start(bf16[2,1,64,2048]{3,2,0,1:T(8,128)(2,1)} %copy-done.4) | copy-start | bytes 1572868
  107.6 3.7 %copy-start.3 = (bf16[1,8,64,2048]{3,2,1,0:T(8,128)(2,1)S(1)}, bf16[1,8,64,2048]{3,2,1,0:T(8,128)(2,1)}, u32[]{:S(2)}) copy-start(bf16[1,8,64,2048]{3,2,1,0:T(8,128)(2,1)} %param.5) | copy-start | bytes 6291460
  107.6 8.3 %collective-permute-start.11 = (bf16[1,64,2048]{2,1,0:T(8,128)(2,1)S(1)}, bf16[1,64,2048]{2,1,0:T(8,128)(2,1)S(1)}, u32[]{:S(2)}, u32[]{:S(2)}) collective-permute-start(bf16[1,64,2048]{2,1,0:T(8,128)(2,1)S(1)} %get-tuple-element.45), channel_id=1, source_target_pairs={{0,1},{1,0},{2,3},{3,2},{4,5},{5,4},{6,7},{7,6},{8,9},{9,8},{10,11... | collective-permute-start | bytes 786440 | tf_op jit(solution)/shard_map/ppermute | solution.py:23
  109.3 9.3 %collective-permute-start.14 = (bf16[1,64,2048]{2,1,0:T(8,128)(2,1)S(1)}, bf16[1,64,2048]{2,1,0:T(8,128)(2,1)S(1)}, u32[]{:S(2)}, u32[]{:S(2)}) collective-permute-start(bf16[1,64,2048]{2,1,0:T(8,128)(2,1)S(1)} %get-tuple-element.44), channel_id=1, source_target_pairs={{0,2},{1,3},{2,0},{3,1},{4,6},{5,7},{6,4},{7,5},{8,10},{9,11},{10,... | collective-permute-start | bytes 786440 | tf_op jit(solution)/shard_map/ppermute | solution.py:23
  109.3 12.4 %collective-permute-start.15 = (bf16[1,64,2048]{2,1,0:T(8,128)(2,1)S(1)}, bf16[1,64,2048]{2,1,0:T(8,128)(2,1)S(1)}, u32[]{:S(2)}, u32[]{:S(2)}) collective-permute-start(bf16[1,64,2048]{2,1,0:T(8,128)(2,1)S(1)} %get-tuple-element.43), channel_id=1, source_target_pairs={{0,3},{1,2},{2,1},{3,0},{4,7},{5,6},{6,5},{7,4},{8,11},{9,10},{10,... | collective-permute-start | bytes 786440 | tf_op jit(solution)/shard_map/ppermute | solution.py:23
  121.7 45.5 %collective-permute-start.16 = (bf16[8,1,64,2048]{3,2,1,0:T(8,128)(2,1)}, bf16[8,1,64,2048]{3,2,1,0:T(8,128)(2,1)}, u32[]{:S(2)}, u32[]{:S(2)}) collective-permute-start(bf16[8,1,64,2048]{3,2,1,0:T(8,128)(2,1)} %add_convert_fusion.1), channel_id=1, source_target_pairs={{0,16},{8,24},{16,0},{24,8},{1,17},{9,25},{17,1},{25,9},{2,18},{10... | collective-permute-start | bytes 6291464 | tf_op jit(solution)/shard_map/ppermute | solution.py:23
  135.0 13.8 %collective-permute-start.18 = (bf16[1,64,2048]{2,1,0:T(8,128)(2,1)S(1)}, bf16[1,64,2048]{2,1,0:T(8,128)(2,1)S(1)}, u32[]{:S(2)}, u32[]{:S(2)}) collective-permute-start(bf16[1,64,2048]{2,1,0:T(8,128)(2,1)S(1)} %get-tuple-element.24), channel_id=1, source_target_pairs={{0,1},{1,0},{2,3},{3,2},{4,5},{5,4},{6,7},{7,6},{8,9},{9,8},{10,11... | collective-permute-start | bytes 786440 | tf_op jit(solution)/shard_map/ppermute | solution.py:23
  136.6 34.4 %collective-permute-start.17 = (bf16[1,64,2048]{2,1,0:T(8,128)(2,1)S(1)}, bf16[1,64,2048]{2,1,0:T(8,128)(2,1)S(1)}, u32[]{:S(2)}, u32[]{:S(2)}) collective-permute-start(bf16[1,64,2048]{2,1,0:T(8,128)(2,1)S(1)} %get-tuple-element.22), channel_id=1, source_target_pairs={{0,7},{1,6},{2,5},{3,4},{4,3},{5,2},{6,1},{7,0},{8,15},{9,14},{10,... | collective-permute-start | bytes 786440 | tf_op jit(solution)/shard_map/ppermute | solution.py:23
  137.2 38.0 %collective-permute-start.19 = (bf16[1,64,2048]{2,1,0:T(8,128)(2,1)S(1)}, bf16[1,64,2048]{2,1,0:T(8,128)(2,1)S(1)}, u32[]{:S(2)}, u32[]{:S(2)}) collective-permute-start(bf16[1,64,2048]{2,1,0:T(8,128)(2,1)S(1)} %get-tuple-element.25), channel_id=1, source_target_pairs={{0,2},{1,3},{2,0},{3,1},{4,6},{5,7},{6,4},{7,5},{8,10},{9,11},{10,... | collective-permute-start | bytes 786440 | tf_op jit(solution)/shard_map/ppermute | solution.py:23
  137.2 38.1 %collective-permute-start.20 = (bf16[1,64,2048]{2,1,0:T(8,128)(2,1)S(1)}, bf16[1,64,2048]{2,1,0:T(8,128)(2,1)S(1)}, u32[]{:S(2)}, u32[]{:S(2)}) collective-permute-start(bf16[1,64,2048]{2,1,0:T(8,128)(2,1)S(1)} %get-tuple-element.26), channel_id=1, source_target_pairs={{0,3},{1,2},{2,1},{3,0},{4,7},{5,6},{6,5},{7,4},{8,11},{9,10},{10,... | collective-permute-start | bytes 786440 | tf_op jit(solution)/shard_map/ppermute | solution.py:23
  148.8 26.7 %collective-permute-start.21 = (bf16[1,64,2048]{2,1,0:T(8,128)(2,1)S(1)}, bf16[1,64,2048]{2,1,0:T(8,128)(2,1)S(1)}, u32[]{:S(2)}, u32[]{:S(2)}) collective-permute-start(bf16[1,64,2048]{2,1,0:T(8,128)(2,1)S(1)} %get-tuple-element.27), channel_id=1, source_target_pairs={{0,6},{1,7},{2,4},{3,5},{4,2},{5,3},{6,0},{7,1},{8,14},{9,15},{10,... | collective-permute-start | bytes 786440 | tf_op jit(solution)/shard_map/ppermute | solution.py:23
  167.2 19.5 %collective-permute-start.22 = (bf16[1,64,2048]{2,1,0:T(8,128)(2,1)S(1)}, bf16[1,64,2048]{2,1,0:T(8,128)(2,1)S(1)}, u32[]{:S(2)}, u32[]{:S(2)}) collective-permute-start(bf16[1,64,2048]{2,1,0:T(8,128)(2,1)S(1)} %get-tuple-element.28), channel_id=1, source_target_pairs={{0,5},{1,4},{2,7},{3,6},{4,1},{5,0},{6,3},{7,2},{8,13},{9,12},{10,... | collective-permute-start | bytes 786440 | tf_op jit(solution)/shard_map/ppermute | solution.py:23
  171.0 20.0 %collective-permute-start.23 = (bf16[1,64,2048]{2,1,0:T(8,128)(2,1)S(1)}, bf16[1,64,2048]{2,1,0:T(8,128)(2,1)S(1)}, u32[]{:S(2)}, u32[]{:S(2)}) collective-permute-start(bf16[1,64,2048]{2,1,0:T(8,128)(2,1)S(1)} %get-tuple-element.29), channel_id=1, source_target_pairs={{0,4},{1,5},{2,6},{3,7},{4,0},{5,1},{6,2},{7,3},{8,12},{9,13},{10,... | collective-permute-start | bytes 786440 | tf_op jit(solution)/shard_map/ppermute | solution.py:23
  191.1 1.3 copy-start.1
  191.1 2.0 %copy-start.2 = (bf16[1,8,64,2048]{3,2,1,0:T(8,128)(2,1)}, bf16[1,8,64,2048]{3,2,1,0:T(8,128)(2,1)S(1)}, u32[]{:S(2)}) copy-start(bf16[1,8,64,2048]{3,2,1,0:T(8,128)(2,1)S(1)} %get-tuple-element.51) | copy-start | bytes 6291460

commit v8 on v6

--- a/solution.py
+++ b/solution.py
@@ -146,18 +146,25 @@
     def taken(values, start, length):
         return lax.dynamic_slice_in_dim(values, start, length, axis=0)
 
+    far_first = keep[rep_index ^ 2, 0]
+
+    def blend(share, own, near):
+        return share * own + (1.0 - share) * near.astype(F32)
+
     new_tracker = jnp.zeros(shape, F32)
     blocks = [None] * shards
     for turn, (lowest, length) in enumerate(grouped(shards)):
-        if turn == 2:
-            tracker = after(tracker, sent)
         start = (here ^ lowest) // length * length
         own = taken(tracker, start, length)
-        near = swapped(own.astype(BF16), "rep", 1)
-        mixed = first * own + (1.0 - first) * near.astype(F32)
-        sent = mixed.astype(BF16)
-        far = swapped(sent, "rep", 2)
-        group = second * mixed + (1.0 - second) * far.astype(F32)
+        rounded = own.astype(BF16)
+        mixed = blend(first, own, swapped(rounded, "rep", 1))
+        if turn < 2:
+            far = swapped(rounded, "rep", 2)
+            far_mixed = blend(far_first, far.astype(F32), swapped(far, "rep", 1))
+        else:
+            far = swapped(mixed.astype(BF16), "rep", 2)
+            far_mixed = far.astype(F32)
+        group = second * mixed + (1.0 - second) * far_mixed
         group += taken(grad_new, start, length).astype(F32)
         group -= taken(grad_old, start, length).astype(F32)
         for offset in reversed(range(lowest, lowest + length)):
@@ -169,7 +176,7 @@
     weight_own = (
         first * weight.astype(F32) + (1.0 - first) * weight_near.astype(F32)
     ).astype(BF16)
-    weight_own = after(weight_own, far, blocks[1])
+    weight_own = after(weight_own, far)
     weight_far = swapped(weight_own, "rep", 2)
     mixed_weight = (
         second * weight_own.astype(F32) + (1.0 - second) * weight_far.astype(F32)

time: 164 us -> 152 us (0.927)
  starting transfers between devices: 41.5 us -> 32.8 us
  other arithmetic: 25.6 us -> 21.2 us
    ppermute x24 -> x26, starting transfers between devices: 41.5 us -> 32.8 us  [swapped(): lax.ppermute(values, axis, [(i, i ^ offset) for i in range(lax.axis_size(...]
    convert_element_type x3 -> x2, other arithmetic: 8.03 us -> 3.16 us  [local(): far = swapped(mixed.astype(BF16), 'rep', 2)]
    dynamic_update_slice x4, other arithmetic: 8.01 us -> 10.5 us  [local(): lax.dynamic_update_slice_in_dim(new_tracker, group, start, axis=0)]
    ppermute x24 -> x26, waiting for transfers between devices: 71.5 us -> 72.9 us  [swapped(): lax.ppermute(values, axis, [(i, i ^ offset) for i in range(lax.axis_size(...]
  transfers between devices with their start and end apart: 24 -> 26, of which waited for: 12 -> 11; matrix products, arithmetic and copies ran while one was open for 16% -> 18% of each run, Pallas kernels for 8% -> 8%
where the time goes in v8:
time: 152 us
  waiting for transfers between devices  72.9 us (48%)
  starting transfers between devices  32.8 us (22%)
  other arithmetic  21.2 us (14%)
  Pallas kernels  12.8 us (8%)
  local copies, waits for them, and re-layouts  9.12 us (6%)
  between operations  3.08 us (2%)
    ppermute x26, waiting for transfers between devices, swapped(): lax.ppermute(values, axis, [(i, i ^ offset) for i in range(lax.axis_size(...  72.9 us
    ppermute x26, starting transfers between devices, swapped(): lax.ppermute(values, axis, [(i, i ^ offset) for i in range(lax.axis_size(...  32.8 us
    pallas_call x1, Pallas kernels, orthogonalize(): pl.pallas_call(body, grid=(each,), in_specs=[block] * count, out_specs=[b...  12.8 us
    dynamic_update_slice x4, other arithmetic, local(): lax.dynamic_update_slice_in_dim(new_tracker, group, start, axis=0)  10.5 us
    convert_element_type x3, local copies, waits for them, and re-layouts, local(): rounded = own.astype(BF16)  5.29 us
    convert_element_type x1, other arithmetic, local(): mixed_weight = (second * weight_own.astype(F32) + (1.0 - second) * weight...  3.7 us
    convert_element_type x2, other arithmetic, local(): far = swapped(mixed.astype(BF16), 'rep', 2)  3.16 us
  transfers between devices with their start and end apart: 26, of which 11 were waited for; matrix products, arithmetic and copies ran while one was open for 18% of the time, Pallas kernels for 8%

profile of v8, /device:TPU:0, one launch (start us, length us, event | category | flops | bytes accessed | tf_op | source)
XLA Modules:
  0.0 151.8 jit_solution(14723988307765877812)
XLA Ops:
  0.7 1.4 fusion.3
  2.1 0.5 collective-permute-start.7
  2.7 2.0 %dynamic-slice_convert_fusion.9 = (bf16[1,1,64,2048]{3,2,1,0:T(8,128)(2,1)S(1)}, bf16[1,1,64,2048]{3,2,1,0:T(8,128)(2,1)}) fusion(f32[1,8,64,2048]{3,2,1,0:T(8,128)} %param.6, s32[]{:T(128)S(6)} %select_n.144, s32[]{:T(128)S(6)} %select_n.146), kind=kLoop, calls=%fused_computation.41 | loop fusion | bytes 1048584 | tf_op jit(solution)/shard_map/convert_element_type | solution.py:159
  4.6 2.5 %collective-permute-start.16 = (bf16[1,1,64,2048]{3,2,1,0:T(8,128)(2,1)}, bf16[1,1,64,2048]{3,2,1,0:T(8,128)(2,1)}, u32[]{:S(2)}, u32[]{:S(2)}) collective-permute-start(bf16[1,1,64,2048]{3,2,1,0:T(8,128)(2,1)} %get-tuple-element.32), channel_id=1, source_target_pairs={{0,16},{8,24},{16,0},{24,8},{1,17},{9,25},{17,1},{25,9},{2,18},{10... | collective-permute-start | bytes 786440 | tf_op jit(solution)/shard_map/ppermute | solution.py:23
  7.1 0.2 collective-permute-start.15
  7.3 0.3 collective-permute-start.12
  7.8 0.6 constant_dynamic-slice_fusion.1
  10.4 1.9 %fusion.1 = bf16[4,1,64,2048]{3,2,1,0:T(8,128)(2,1)S(1)} fusion(f32[1,8,64,2048]{3,2,1,0:T(8,128)} %param.6, s32[]{:T(128)S(6)} %select_n.129), kind=kLoop, calls=%fused_computation.8 | loop fusion | bytes 2097156 | tf_op jit(solution)/shard_map/convert_element_type | solution.py:159
  12.3 2.3 %collective-permute-done.16 = bf16[1,1,64,2048]{3,2,1,0:T(8,128)(2,1)} collective-permute-done((bf16[1,1,64,2048]{3,2,1,0:T(8,128)(2,1)}, bf16[1,1,64,2048]{3,2,1,0:T(8,128)(2,1)}, u32[]{:S(2)}, u32[]{:S(2)}) %collective-permute-start.16) | collective-permute-done | bytes 262176 | tf_op jit(solution)/shard_map/ppermute | solution.py:23
  14.6 0.5 collective-permute-start.17
  15.1 2.2 %fusion.2 = bf16[2,1,64,2048]{3,2,1,0:T(8,128)(2,1)S(1)} fusion(bf16[2,1,64,2048]{3,2,1,0:T(8,128)(2,1)S(1)} %collective-permute-done.7, f32[1,8,64,2048]{3,2,1,0:T(8,128)} %param.6, s32[]{:T(128)S(6)} %select_n.139, f32[]{:T(128)S(6)} %sub.63, f32[]{:T(128)} %bitcast.1), kind=kLoop, calls=%fused_computation.14 | loop fusion | flops 1310720 | bytes 2097164 | tf_op jit(solution)/shard_map/convert_element_type | solution.py:165
  17.4 2.6 %collective-permute-done.12 = bf16[1,1,64,2048]{3,2,1,0:T(8,128)(2,1)} collective-permute-done((bf16[1,1,64,2048]{3,2,1,0:T(8,128)(2,1)S(1)}, bf16[1,1,64,2048]{3,2,1,0:T(8,128)(2,1)}, u32[]{:S(2)}, u32[]{:S(2)}) %collective-permute-start.12) | collective-permute-done | bytes 262176 | tf_op jit(solution)/shard_map/ppermute | solution.py:23
  20.0 1.7 %collective-permute-start.8 = (bf16[2,1,64,2048]{3,2,1,0:T(8,128)(2,1)S(1)}, bf16[2,1,64,2048]{3,2,1,0:T(8,128)(2,1)S(1)}, u32[]{:S(2)}, u32[]{:S(2)}) collective-permute-start(bf16[2,1,64,2048]{3,2,1,0:T(8,128)(2,1)S(1)} %fusion.2), channel_id=1, source_target_pairs={{0,16},{8,24},{16,0},{24,8},{1,17},{9,25},{17,1},{25,9},{2,18},{10... | collective-permute-start | bytes 1572872 | tf_op jit(solution)/shard_map/ppermute | solution.py:23
  21.8 0.5 reshape.427
  22.3 3.2 %constant_dynamic-update-slice_fusion.1 = (f32[1,8,64,2048]{3,2,1,0:T(8,128)S(1)}, bf16[1,1,64,2048]{3,2,1,0:T(8,128)(2,1)S(1)}) fusion(f32[1,8,64,2048]{3,2,1,0:T(8,128)S(1)} %reshape.427, s32[]{:T(128)S(6)} %select_n.146, bf16[1,8,64,2048]{3,2,1,0:T(8,128)(2,1)S(1)} %copy-done.5, bf16[1,8,64,2048]{3,2,1,0:T(8,128)(2,1)S(1)} %copy-done.6, ...), kind=kLoop, calls=%fused_computation.75 | loop fusion | flops 2228224 | bytes 2621468 | tf_op jit(solution)/shard_map/dynamic_update_slice | solution.py:173
  25.6 3.2 %constant_dynamic-update-slice_fusion = (f32[1,8,64,2048]{3,2,1,0:T(8,128)S(1)}, bf16[1,1,64,2048]{3,2,1,0:T(8,128)(2,1)S(1)}) fusion(f32[1,8,64,2048]{3,2,1,0:T(8,128)S(1)} %get-tuple-element.29, s32[]{:T(128)S(6)} %select_n.144, bf16[1,8,64,2048]{3,2,1,0:T(8,128)(2,1)S(1)} %copy-done.5, bf16[1,8,64,2048]{3,2,1,0:T(8,128)(2,1)S(1)} %copy-done.6, ...), kind=kLoop, calls=%fused_computation.74 | loop fusion | flops 2228224 | bytes 2621468 | tf_op jit(solution)/shard_map/dynamic_update_slice | solution.py:173
  28.8 3.7 %collective-permute-start.14 = (bf16[1,64,2048]{2,1,0:T(8,128)(2,1)S(1)}, bf16[1,64,2048]{2,1,0:T(8,128)(2,1)S(1)}, u32[]{:S(2)}, u32[]{:S(2)}) collective-permute-start(bf16[1,64,2048]{2,1,0:T(8,128)(2,1)S(1)} %bitcast.139), channel_id=1, source_target_pairs={{0,6},{1,7},{2,4},{3,5},{4,2},{5,3},{6,0},{7,1},{8,14},{9,15},{10,... | collective-permute-start | bytes 786440 | tf_op jit(solution)/shard_map/ppermute | solution.py:23
  32.5 1.2 collective-permute-start.18
  33.7 1.0 fusion
  34.6 0.6 collective-permute-start.2
  35.2 1.7 %bitcast_dynamic-update-slice_fusion.1 = (f32[1,8,64,2048]{3,2,1,0:T(8,128)S(1)}, bf16[2,1,64,2048]{3,2,1,0:T(8,128)(2,1)S(1)}) fusion(f32[1,8,64,2048]{3,2,1,0:T(8,128)S(1)} %get-tuple-element.27, s32[]{:T(128)S(6)} %select_n.139, bf16[1,8,64,2048]{3,2,1,0:T(8,128)(2,1)S(1)} %copy-done.5, bf16[1,8,64,2048]{3,2,1,0:T(8,128)(2,1)S(1)} %copy-done.6, ...), kind=kLoop, calls=%fused_computation.12 | loop fusion | flops 3407872 | bytes 4718612 | tf_op jit(solution)/shard_map/dynamic_update_slice | solution.py:173
  37.1 3.4 %collective-permute-start.10 = (bf16[1,64,2048]{2,1,0:T(8,128)(2,1)S(1)}, bf16[1,64,2048]{2,1,0:T(8,128)(2,1)S(1)}, u32[]{:S(2)}, u32[]{:S(2)}) collective-permute-start(bf16[1,64,2048]{2,1,0:T(8,128)(2,1)S(1)} %get-tuple-element.37), channel_id=1, source_target_pairs={{0,5},{1,4},{2,7},{3,6},{4,1},{5,0},{6,3},{7,2},{8,13},{9,12},{10,... | collective-permute-start | bytes 786440 | tf_op jit(solution)/shard_map/ppermute | solution.py:23
  40.4 3.0 %add_convert_fusion.1 = bf16[8,1,64,2048]{3,2,1,0:T(8,128)(2,1)} fusion(bf16[8,1,64,2048]{3,2,1,0:T(8,128)(2,1)S(1)} %collective-permute-done, f32[]{:T(128)S(6)} %sub.63, f32[]{:T(128)} %bitcast.1, bf16[1,8,64,2048]{3,2,1,0:T(8,128)(2,1)S(1)} %copy-done.4), kind=kLoop, calls=%fused_computation.1 | loop fusion | flops 6291456 | bytes 6291464 | tf_op jit(solution)/shard_map/convert_element_type | solution.py:178
  43.4 16.2 %collective-permute-done.2 = bf16[4,1,64,2048]{3,2,1,0:T(8,128)(2,1)S(1)} collective-permute-done((bf16[4,1,64,2048]{3,2,1,0:T(8,128)(2,1)S(1)}, bf16[4,1,64,2048]{3,2,1,0:T(8,128)(2,1)S(1)}, u32[]{:S(2)}, u32[]{:S(2)}) %collective-permute-start.2) | collective-permute-done | bytes 1048608 | tf_op jit(solution)/shard_map/ppermute | solution.py:23
  59.6 0.5 collective-permute-start.3
  60.1 2.3 %bitcast_dynamic-update-slice_fusion = (f32[1,8,64,2048]{3,2,1,0:T(8,128)S(1)}, bf16[4,1,64,2048]{3,2,1,0:T(8,128)(2,1)S(1)}) fusion(f32[1,8,64,2048]{3,2,1,0:T(8,128)S(1)} %get-tuple-element.25, s32[]{:T(128)S(6)} %select_n.129, bf16[1,8,64,2048]{3,2,1,0:T(8,128)(2,1)S(1)} %copy-done.5, bf16[1,8,64,2048]{3,2,1,0:T(8,128)(2,1)S(1)} %copy-done.6, ...), kind=kLoop, calls=%fused_computation.5 | loop fusion | flops 6815744 | bytes 9437204 | tf_op jit(solution)/shard_map/dynamic_update_slice | solution.py:173
  62.4 0.1 fusion.15
  62.6 0.6 collective-permute-start.4
  63.1 5.5 %collective-permute-start.5 = (bf16[1,64,2048]{2,1,0:T(8,128)(2,1)S(1)}, bf16[1,64,2048]{2,1,0:T(8,128)(2,1)S(1)}, u32[]{:S(2)}, u32[]{:S(2)}) collective-permute-start(bf16[1,64,2048]{2,1,0:T(8,128)(2,1)S(1)} %get-tuple-element.34), channel_id=1, source_target_pairs={{0,2},{1,3},{2,0},{3,1},{4,6},{5,7},{6,4},{7,5},{8,10},{9,11},{10,... | collective-permute-start | bytes 786440 | tf_op jit(solution)/shard_map/ppermute | solution.py:23
  68.7 5.2 %collective-permute-done.10.refs_5_ = bf16[1,64,2048]{2,1,0:T(8,128)(2,1)S(1)} collective-permute-done((bf16[1,64,2048]{2,1,0:T(8,128)(2,1)S(1)}, bf16[1,64,2048]{2,1,0:T(8,128)(2,1)S(1)}, u32[]{:S(2)}, u32[]{:S(2)}) %collective-permute-start.10) | collective-permute-done | bytes 262176 | tf_op jit(solution)/shard_map/ppermute | solution.py:23
  73.8 4.0 %collective-permute-done.9.refs_4_ = bf16[1,64,2048]{2,1,0:T(8,128)(2,1)S(1)} collective-permute-done((bf16[1,64,2048]{2,1,0:T(8,128)(2,1)S(1)}, bf16[1,64,2048]{2,1,0:T(8,128)(2,1)S(1)}, u32[]{:S(2)}, u32[]{:S(2)}) %collective-permute-start.9) | collective-permute-done | bytes 262176 | tf_op jit(solution)/shard_map/ppermute | solution.py:23
  77.8 5.6 %collective-permute-done.5.refs_2_ = bf16[1,64,2048]{2,1,0:T(8,128)(2,1)S(1)} collective-permute-done((bf16[1,64,2048]{2,1,0:T(8,128)(2,1)S(1)}, bf16[1,64,2048]{2,1,0:T(8,128)(2,1)S(1)}, u32[]{:S(2)}, u32[]{:S(2)}) %collective-permute-start.5) | collective-permute-done | bytes 262176 | tf_op jit(solution)/shard_map/ppermute | solution.py:23
  83.4 6.5 %collective-permute-done.6.refs_3_ = bf16[1,64,2048]{2,1,0:T(8,128)(2,1)S(1)} collective-permute-done((bf16[1,64,2048]{2,1,0:T(8,128)(2,1)S(1)}, bf16[1,64,2048]{2,1,0:T(8,128)(2,1)S(1)}, u32[]{:S(2)}, u32[]{:S(2)}) %collective-permute-start.6) | collective-permute-done | bytes 262176 | tf_op jit(solution)/shard_map/ppermute | solution.py:23
  89.9 12.8 %orthogonalize.1 = (bf16[1,64,2048]{2,1,0:T(8,128)(2,1)S(1)}, bf16[1,64,2048]{2,1,0:T(8,128)(2,1)S(1)}, bf16[1,64,2048]{2,1,0:T(8,128)(2,1)S(1)}, bf16[1,64,2048...) custom-call(bf16[1,64,2048]{2,1,0:T(8,128)(2,1)S(1)} %get-tuple-elem, ...), custom_call_target="tpu_custom_call" | custom-call | flops 11005853696 | bytes 4194304 | tf_op jit(solution)/shard_map/orthogonalize/pallas_call | solution.py:102
  102.7 0.6 collective-permute-start.20
  103.3 3.4 %collective-permute-start.19 = (bf16[1,64,2048]{2,1,0:T(8,128)(2,1)S(1)}, bf16[1,64,2048]{2,1,0:T(8,128)(2,1)S(1)}, u32[]{:S(2)}, u32[]{:S(2)}) collective-permute-start(bf16[1,64,2048]{2,1,0:T(8,128)(2,1)S(1)} %get-tuple-element.14), channel_id=1, source_target_pairs={{0,7},{1,6},{2,5},{3,4},{4,3},{5,2},{6,1},{7,0},{8,15},{9,14},{10,... | collective-permute-start | bytes 786440 | tf_op jit(solution)/shard_map/ppermute | solution.py:23
  106.7 2.0 %collective-permute-start.22 = (bf16[1,64,2048]{2,1,0:T(8,128)(2,1)S(1)}, bf16[1,64,2048]{2,1,0:T(8,128)(2,1)S(1)}, u32[]{:S(2)}, u32[]{:S(2)}) collective-permute-start(bf16[1,64,2048]{2,1,0:T(8,128)(2,1)S(1)} %get-tuple-element.18), channel_id=1, source_target_pairs={{0,3},{1,2},{2,1},{3,0},{4,7},{5,6},{6,5},{7,4},{8,11},{9,10},{10,... | collective-permute-start | bytes 786440 | tf_op jit(solution)/shard_map/ppermute | solution.py:23
  108.7 7.9 %collective-permute-done.20 = bf16[1,64,2048]{2,1,0:T(8,128)(2,1)S(1)} collective-permute-done((bf16[1,64,2048]{2,1,0:T(8,128)(2,1)S(1)}, bf16[1,64,2048]{2,1,0:T(8,128)(2,1)S(1)}, u32[]{:S(2)}, u32[]{:S(2)}) %collective-permute-start.20) | collective-permute-done | bytes 262176 | tf_op jit(solution)/shard_map/ppermute | solution.py:23
  116.6 2.5 %collective-permute-start.23 = (bf16[1,64,2048]{2,1,0:T(8,128)(2,1)S(1)}, bf16[1,64,2048]{2,1,0:T(8,128)(2,1)S(1)}, u32[]{:S(2)}, u32[]{:S(2)}) collective-permute-start(bf16[1,64,2048]{2,1,0:T(8,128)(2,1)S(1)} %get-tuple-element.19), channel_id=1, source_target_pairs={{0,6},{1,7},{2,4},{3,5},{4,2},{5,3},{6,0},{7,1},{8,14},{9,15},{10,... | collective-permute-start | bytes 786440 | tf_op jit(solution)/shard_map/ppermute | solution.py:23
  119.1 0.2 reshape.425.clone
  119.4 3.7 %add_convert_fusion = bf16[8,1,64,2048]{3,2,1,0:T(8,128)(2,1)S(1)} fusion(bf16[8,1,64,2048]{3,2,1,0:T(8,128)(2,1)} %collective-permute-done.3, bf16[8,1,64,2048]{3,2,1,0:T(8,128)(2,1)} %add_convert_fusion.1, f32[]{:T(128)S(6)} %sub.65, f32[]{:T(128)} %bitcast), kind=kLoop, calls=%fused_computation | loop fusion | flops 6291456 | bytes 6291464 | tf_op jit(solution)/shard_map/convert_element_type | solution.py:183
  123.2 2.9 %collective-permute-start.25 = (bf16[1,64,2048]{2,1,0:T(8,128)(2,1)S(1)}, bf16[1,64,2048]{2,1,0:T(8,128)(2,1)S(1)}, u32[]{:S(2)}, u32[]{:S(2)}) collective-permute-start(bf16[1,64,2048]{2,1,0:T(8,128)(2,1)S(1)} %get-tuple-element.21), channel_id=1, source_target_pairs={{0,4},{1,5},{2,6},{3,7},{4,0},{5,1},{6,2},{7,3},{8,12},{9,13},{10,... | collective-permute-start | bytes 786440 | tf_op jit(solution)/shard_map/ppermute | solution.py:23
  126.1 0.2 reshape.425.clone.1
  126.5 6.9 %collective-permute-done.22 = bf16[1,64,2048]{2,1,0:T(8,128)(2,1)S(1)} collective-permute-done((bf16[1,64,2048]{2,1,0:T(8,128)(2,1)S(1)}, bf16[1,64,2048]{2,1,0:T(8,128)(2,1)S(1)}, u32[]{:S(2)}, u32[]{:S(2)}) %collective-permute-start.22) | collective-permute-done | bytes 262176 | tf_op jit(solution)/shard_map/ppermute | solution.py:23
  133.7 13.2 %collective-permute-done.24 = bf16[1,64,2048]{2,1,0:T(8,128)(2,1)S(1)} collective-permute-done((bf16[1,64,2048]{2,1,0:T(8,128)(2,1)S(1)}, bf16[1,64,2048]{2,1,0:T(8,128)(2,1)S(1)}, u32[]{:S(2)}, u32[]{:S(2)}) %collective-permute-start.24) | collective-permute-done | bytes 262176 | tf_op jit(solution)/shard_map/ppermute | solution.py:23
  147.0 2.6 %collective-permute-done.25 = bf16[1,64,2048]{2,1,0:T(8,128)(2,1)S(1)} collective-permute-done((bf16[1,64,2048]{2,1,0:T(8,128)(2,1)S(1)}, bf16[1,64,2048]{2,1,0:T(8,128)(2,1)S(1)}, u32[]{:S(2)}, u32[]{:S(2)}) %collective-permute-start.25) | collective-permute-done | bytes 262176 | tf_op jit(solution)/shard_map/ppermute | solution.py:23
  149.8 1.3 copy-done.2
  151.1 0.7 copy-done.3
  (48 shorter events, 1.1 us)
Async XLA Ops:
  0.6 7.0 %copy-start.7 = (s32[4,2]{0,1:T(2,128)S(1)}, s32[4,2]{0,1:T(2,128)}, u32[]{:S(2)}) copy-start(s32[4,2]{0,1:T(2,128)} %param.9) | copy-start | bytes 100
  0.7 21.6 %copy-start.6 = (bf16[1,8,64,2048]{3,2,1,0:T(8,128)(2,1)S(1)}, bf16[1,8,64,2048]{3,2,1,0:T(8,128)(2,1)}, u32[]{:S(2)}) copy-start(bf16[1,8,64,2048]{3,2,1,0:T(8,128)(2,1)} %param.7) | copy-start | bytes 6291460
  2.1 12.5 %collective-permute-start.7 = (bf16[2,1,64,2048]{3,2,1,0:T(8,128)(2,1)S(1)}, bf16[2,1,64,2048]{3,2,1,0:T(8,128)(2,1)S(1)}, u32[]{:S(2)}, u32[]{:S(2)}) collective-permute-start(bf16[2,1,64,2048]{3,2,1,0:T(8,128)(2,1)S(1)} %fusion.3), channel_id=1, source_target_pairs={{0,8},{8,0},{16,24},{24,16},{1,9},{9,1},{17,25},{25,17},{2,10},{10... | collective-permute-start | bytes 1572872 | tf_op jit(solution)/shard_map/ppermute | solution.py:23
  4.6 10.0 %collective-permute-start.16 = (bf16[1,1,64,2048]{3,2,1,0:T(8,128)(2,1)}, bf16[1,1,64,2048]{3,2,1,0:T(8,128)(2,1)}, u32[]{:S(2)}, u32[]{:S(2)}) collective-permute-start(bf16[1,1,64,2048]{3,2,1,0:T(8,128)(2,1)} %get-tuple-element.32), channel_id=1, source_target_pairs={{0,16},{8,24},{16,0},{24,8},{1,17},{9,25},{17,1},{25,9},{2,18},{10... | collective-permute-start | bytes 786440 | tf_op jit(solution)/shard_map/ppermute | solution.py:23
  7.1 10.2 %collective-permute-start.15 = (bf16[1,1,64,2048]{3,2,1,0:T(8,128)(2,1)}, bf16[1,1,64,2048]{3,2,1,0:T(8,128)(2,1)}, u32[]{:S(2)}, u32[]{:S(2)}) collective-permute-start(bf16[1,1,64,2048]{3,2,1,0:T(8,128)(2,1)} %get-tuple-element.32), channel_id=1, source_target_pairs={{0,8},{8,0},{16,24},{24,16},{1,9},{9,1},{17,25},{25,17},{2,10},{10... | collective-permute-start | bytes 786440 | tf_op jit(solution)/shard_map/ppermute | solution.py:23
  7.3 12.7 %collective-permute-start.12 = (bf16[1,1,64,2048]{3,2,1,0:T(8,128)(2,1)S(1)}, bf16[1,1,64,2048]{3,2,1,0:T(8,128)(2,1)}, u32[]{:S(2)}, u32[]{:S(2)}) collective-permute-start(bf16[1,1,64,2048]{3,2,1,0:T(8,128)(2,1)S(1)} %get-tuple-element.31), channel_id=1, source_target_pairs={{0,16},{8,24},{16,0},{24,8},{1,17},{9,25},{17,1},{25,9},{2,18},{10... | collective-permute-start | bytes 786440 | tf_op jit(solution)/shard_map/ppermute | solution.py:23
  7.6 17.9 %collective-permute-start.11 = (bf16[1,1,64,2048]{3,2,1,0:T(8,128)(2,1)S(1)}, bf16[1,1,64,2048]{3,2,1,0:T(8,128)(2,1)}, u32[]{:S(2)}, u32[]{:S(2)}) collective-permute-start(bf16[1,1,64,2048]{3,2,1,0:T(8,128)(2,1)S(1)} %get-tuple-element.31), channel_id=1, source_target_pairs={{0,8},{8,0},{16,24},{24,16},{1,9},{9,1},{17,25},{25,17},{2,10},{10... | collective-permute-start | bytes 786440 | tf_op jit(solution)/shard_map/ppermute | solution.py:23
  10.4 6.9 %copy-start.4 = (bf16[1,8,64,2048]{3,2,1,0:T(8,128)(2,1)S(1)}, bf16[1,8,64,2048]{3,2,1,0:T(8,128)(2,1)}, u32[]{:S(2)}) copy-start(bf16[1,8,64,2048]{3,2,1,0:T(8,128)(2,1)} %param.5) | copy-start | bytes 6291460
  14.6 19.0 %collective-permute-start.1 = (bf16[4,1,64,2048]{3,2,1,0:T(8,128)(2,1)S(1)}, bf16[4,1,64,2048]{3,2,1,0:T(8,128)(2,1)S(1)}, u32[]{:S(2)}, u32[]{:S(2)}) collective-permute-start(bf16[4,1,64,2048]{3,2,1,0:T(8,128)(2,1)S(1)} %fusion.1), channel_id=1, source_target_pairs={{0,8},{8,0},{16,24},{24,16},{1,9},{9,1},{17,25},{25,17},{2,10},{10... | collective-permute-start | bytes 3145736 | tf_op jit(solution)/shard_map/ppermute | solution.py:23
  14.6 5.4 %collective-permute-start.17 = (bf16[1,1,64,2048]{3,2,1,0:T(8,128)(2,1)}, bf16[1,1,64,2048]{3,2,1,0:T(8,128)(2,1)S(1)}, u32[]{:S(2)}, u32[]{:S(2)}) collective-permute-start(bf16[1,1,64,2048]{3,2,1,0:T(8,128)(2,1)} %collective-permute-done.16), channel_id=1, source_target_pairs={{0,8},{8,0},{16,24},{24,16},{1,9},{9,1},{17,25},{25,17},{2,10},{10... | collective-permute-start | bytes 786440 | tf_op jit(solution)/shard_map/ppermute | solution.py:23
  15.1 7.2 %copy-start.5 = (bf16[1,8,64,2048]{3,2,1,0:T(8,128)(2,1)S(1)}, bf16[1,8,64,2048]{3,2,1,0:T(8,128)(2,1)}, u32[]{:S(2)}) copy-start(bf16[1,8,64,2048]{3,2,1,0:T(8,128)(2,1)} %param.8) | copy-start | bytes 6291460
  17.3 5.0 %copy-start = (f32[1,8,64,2048]{3,2,1,0:T(8,128)S(1)}, f32[1,8,64,2048]{3,2,1,0:T(8,128)}, u32[]{:S(2)}) copy-start(f32[1,8,64,2048]{3,2,1,0:T(8,128)} %param.6) | copy-start | bytes 12582916
  17.3 23.1 %collective-permute-start = (bf16[8,1,64,2048]{3,2,1,0:T(8,128)(2,1)S(1)}, bf16[8,1,64,2048]{3,2,1,0:T(8,128)(2,1)S(1)}, u32[]{:S(2)}, u32[]{:S(2)}) collective-permute-start(bf16[8,1,64,2048]{3,2,1,0:T(8,128)(2,1)S(1)} %bitcast.137), channel_id=1, source_target_pairs={{0,8},{8,0},{16,24},{24,16},{1,9},{9,1},{17,25},{25,17},{2,10},{10... | collective-permute-start | bytes 6291464 | tf_op jit(solution)/shard_map/ppermute | solution.py:23
  20.0 5.5 %collective-permute-start.13 = (bf16[1,1,64,2048]{3,2,1,0:T(8,128)(2,1)}, bf16[1,1,64,2048]{3,2,1,0:T(8,128)(2,1)S(1)}, u32[]{:S(2)}, u32[]{:S(2)}) collective-permute-start(bf16[1,1,64,2048]{3,2,1,0:T(8,128)(2,1)} %collective-permute-done.12), channel_id=1, source_target_pairs={{0,8},{8,0},{16,24},{24,16},{1,9},{9,1},{17,25},{25,17},{2,10},{10... | collective-permute-start | bytes 786440 | tf_op jit(solution)/shard_map/ppermute | solution.py:23
  20.0 15.2 %collective-permute-start.8 = (bf16[2,1,64,2048]{3,2,1,0:T(8,128)(2,1)S(1)}, bf16[2,1,64,2048]{3,2,1,0:T(8,128)(2,1)S(1)}, u32[]{:S(2)}, u32[]{:S(2)}) collective-permute-start(bf16[2,1,64,2048]{3,2,1,0:T(8,128)(2,1)S(1)} %fusion.2), channel_id=1, source_target_pairs={{0,16},{8,24},{16,0},{24,8},{1,17},{9,25},{17,1},{25,9},{2,18},{10... | collective-permute-start | bytes 1572872 | tf_op jit(solution)/shard_map/ppermute | solution.py:23
  28.8 33.8 %collective-permute-start.14 = (bf16[1,64,2048]{2,1,0:T(8,128)(2,1)S(1)}, bf16[1,64,2048]{2,1,0:T(8,128)(2,1)S(1)}, u32[]{:S(2)}, u32[]{:S(2)}) collective-permute-start(bf16[1,64,2048]{2,1,0:T(8,128)(2,1)S(1)} %bitcast.139), channel_id=1, source_target_pairs={{0,6},{1,7},{2,4},{3,5},{4,2},{5,3},{6,0},{7,1},{8,14},{9,15},{10,... | collective-permute-start | bytes 786440 | tf_op jit(solution)/shard_map/ppermute | solution.py:23
  32.5 30.7 %collective-permute-start.18 = (bf16[1,64,2048]{2,1,0:T(8,128)(2,1)S(1)}, bf16[1,64,2048]{2,1,0:T(8,128)(2,1)S(1)}, u32[]{:S(2)}, u32[]{:S(2)}) collective-permute-start(bf16[1,64,2048]{2,1,0:T(8,128)(2,1)S(1)} %bitcast.138), channel_id=1, source_target_pairs={{0,7},{1,6},{2,5},{3,4},{4,3},{5,2},{6,1},{7,0},{8,15},{9,14},{10,... | collective-permute-start | bytes 786440 | tf_op jit(solution)/shard_map/ppermute | solution.py:23
  34.6 24.9 %collective-permute-start.2 = (bf16[4,1,64,2048]{3,2,1,0:T(8,128)(2,1)S(1)}, bf16[4,1,64,2048]{3,2,1,0:T(8,128)(2,1)S(1)}, u32[]{:S(2)}, u32[]{:S(2)}) collective-permute-start(bf16[4,1,64,2048]{3,2,1,0:T(8,128)(2,1)S(1)} %fusion), channel_id=1, source_target_pairs={{0,16},{8,24},{16,0},{24,8},{1,17},{9,25},{17,1},{25,9},{2,18},{10... | collective-permute-start | bytes 3145736 | tf_op jit(solution)/shard_map/ppermute | solution.py:23
  37.1 36.8 %collective-permute-start.10 = (bf16[1,64,2048]{2,1,0:T(8,128)(2,1)S(1)}, bf16[1,64,2048]{2,1,0:T(8,128)(2,1)S(1)}, u32[]{:S(2)}, u32[]{:S(2)}) collective-permute-start(bf16[1,64,2048]{2,1,0:T(8,128)(2,1)S(1)} %get-tuple-element.37), channel_id=1, source_target_pairs={{0,5},{1,4},{2,7},{3,6},{4,1},{5,0},{6,3},{7,2},{8,13},{9,12},{10,... | collective-permute-start | bytes 786440 | tf_op jit(solution)/shard_map/ppermute | solution.py:23
  40.4 37.4 %collective-permute-start.9 = (bf16[1,64,2048]{2,1,0:T(8,128)(2,1)S(1)}, bf16[1,64,2048]{2,1,0:T(8,128)(2,1)S(1)}, u32[]{:S(2)}, u32[]{:S(2)}) collective-permute-start(bf16[1,64,2048]{2,1,0:T(8,128)(2,1)S(1)} %get-tuple-element.38), channel_id=1, source_target_pairs={{0,4},{1,5},{2,6},{3,7},{4,0},{5,1},{6,2},{7,3},{8,12},{9,13},{10,... | collective-permute-start | bytes 786440 | tf_op jit(solution)/shard_map/ppermute | solution.py:23
  59.6 59.8 %collective-permute-start.3 = (bf16[8,1,64,2048]{3,2,1,0:T(8,128)(2,1)}, bf16[8,1,64,2048]{3,2,1,0:T(8,128)(2,1)}, u32[]{:S(2)}, u32[]{:S(2)}) collective-permute-start(bf16[8,1,64,2048]{3,2,1,0:T(8,128)(2,1)} %add_convert_fusion.1), channel_id=1, source_target_pairs={{0,16},{8,24},{16,0},{24,8},{1,17},{9,25},{17,1},{25,9},{2,18},{10... | collective-permute-start | bytes 6291464 | tf_op jit(solution)/shard_map/ppermute | solution.py:23
  62.4 27.5 %copy-start.1 = (f32[1,8,64,2048]{3,2,1,0:T(8,128)}, f32[1,8,64,2048]{3,2,1,0:T(8,128)S(1)}, u32[]{:S(2)}) copy-start(f32[1,8,64,2048]{3,2,1,0:T(8,128)S(1)} %get-tuple-element.23) | copy-start | bytes 12582916
  62.6 15.2 %collective-permute-start.4 = (bf16[1,64,2048]{2,1,0:T(8,128)(2,1)S(1)}, bf16[1,64,2048]{2,1,0:T(8,128)(2,1)S(1)}, u32[]{:S(2)}, u32[]{:S(2)}) collective-permute-start(bf16[1,64,2048]{2,1,0:T(8,128)(2,1)S(1)} %get-tuple-element.35), channel_id=1, source_target_pairs={{0,1},{1,0},{2,3},{3,2},{4,5},{5,4},{6,7},{7,6},{8,9},{9,8},{10,11... | collective-permute-start | bytes 786440 | tf_op jit(solution)/shard_map/ppermute | solution.py:23
  63.1 20.3 %collective-permute-start.5 = (bf16[1,64,2048]{2,1,0:T(8,128)(2,1)S(1)}, bf16[1,64,2048]{2,1,0:T(8,128)(2,1)S(1)}, u32[]{:S(2)}, u32[]{:S(2)}) collective-permute-start(bf16[1,64,2048]{2,1,0:T(8,128)(2,1)S(1)} %get-tuple-element.34), channel_id=1, source_target_pairs={{0,2},{1,3},{2,0},{3,1},{4,6},{5,7},{6,4},{7,5},{8,10},{9,11},{10,... | collective-permute-start | bytes 786440 | tf_op jit(solution)/shard_map/ppermute | solution.py:23
  73.8 16.1 %collective-permute-start.6 = (bf16[1,64,2048]{2,1,0:T(8,128)(2,1)S(1)}, bf16[1,64,2048]{2,1,0:T(8,128)(2,1)S(1)}, u32[]{:S(2)}, u32[]{:S(2)}) collective-permute-start(bf16[1,64,2048]{2,1,0:T(8,128)(2,1)S(1)} %get-tuple-element.33), channel_id=1, source_target_pairs={{0,3},{1,2},{2,1},{3,0},{4,7},{5,6},{6,5},{7,4},{8,11},{9,10},{10,... | collective-permute-start | bytes 786440 | tf_op jit(solution)/shard_map/ppermute | solution.py:23
  102.7 13.9 %collective-permute-start.20 = (bf16[1,64,2048]{2,1,0:T(8,128)(2,1)S(1)}, bf16[1,64,2048]{2,1,0:T(8,128)(2,1)S(1)}, u32[]{:S(2)}, u32[]{:S(2)}) collective-permute-start(bf16[1,64,2048]{2,1,0:T(8,128)(2,1)S(1)} %get-tuple-element.16), channel_id=1, source_target_pairs={{0,1},{1,0},{2,3},{3,2},{4,5},{5,4},{6,7},{7,6},{8,9},{9,8},{10,11... | collective-permute-start | bytes 786440 | tf_op jit(solution)/shard_map/ppermute | solution.py:23
  103.3 19.9 %collective-permute-start.19 = (bf16[1,64,2048]{2,1,0:T(8,128)(2,1)S(1)}, bf16[1,64,2048]{2,1,0:T(8,128)(2,1)S(1)}, u32[]{:S(2)}, u32[]{:S(2)}) collective-permute-start(bf16[1,64,2048]{2,1,0:T(8,128)(2,1)S(1)} %get-tuple-element.14), channel_id=1, source_target_pairs={{0,7},{1,6},{2,5},{3,4},{4,3},{5,2},{6,1},{7,0},{8,15},{9,14},{10,... | collective-permute-start | bytes 786440 | tf_op jit(solution)/shard_map/ppermute | solution.py:23
  106.7 19.7 %collective-permute-start.21 = (bf16[1,64,2048]{2,1,0:T(8,128)(2,1)S(1)}, bf16[1,64,2048]{2,1,0:T(8,128)(2,1)S(1)}, u32[]{:S(2)}, u32[]{:S(2)}) collective-permute-start(bf16[1,64,2048]{2,1,0:T(8,128)(2,1)S(1)} %get-tuple-element.17), channel_id=1, source_target_pairs={{0,2},{1,3},{2,0},{3,1},{4,6},{5,7},{6,4},{7,5},{8,10},{9,11},{10,... | collective-permute-start | bytes 786440 | tf_op jit(solution)/shard_map/ppermute | solution.py:23
  106.7 26.7 %collective-permute-start.22 = (bf16[1,64,2048]{2,1,0:T(8,128)(2,1)S(1)}, bf16[1,64,2048]{2,1,0:T(8,128)(2,1)S(1)}, u32[]{:S(2)}, u32[]{:S(2)}) collective-permute-start(bf16[1,64,2048]{2,1,0:T(8,128)(2,1)S(1)} %get-tuple-element.18), channel_id=1, source_target_pairs={{0,3},{1,2},{2,1},{3,0},{4,7},{5,6},{6,5},{7,4},{8,11},{9,10},{10,... | collective-permute-start | bytes 786440 | tf_op jit(solution)/shard_map/ppermute | solution.py:23
  116.6 17.0 %collective-permute-start.23 = (bf16[1,64,2048]{2,1,0:T(8,128)(2,1)S(1)}, bf16[1,64,2048]{2,1,0:T(8,128)(2,1)S(1)}, u32[]{:S(2)}, u32[]{:S(2)}) collective-permute-start(bf16[1,64,2048]{2,1,0:T(8,128)(2,1)S(1)} %get-tuple-element.19), channel_id=1, source_target_pairs={{0,6},{1,7},{2,4},{3,5},{4,2},{5,3},{6,0},{7,1},{8,14},{9,15},{10,... | collective-permute-start | bytes 786440 | tf_op jit(solution)/shard_map/ppermute | solution.py:23
  119.4 27.6 %collective-permute-start.24 = (bf16[1,64,2048]{2,1,0:T(8,128)(2,1)S(1)}, bf16[1,64,2048]{2,1,0:T(8,128)(2,1)S(1)}, u32[]{:S(2)}, u32[]{:S(2)}) collective-permute-start(bf16[1,64,2048]{2,1,0:T(8,128)(2,1)S(1)} %get-tuple-element.20), channel_id=1, source_target_pairs={{0,5},{1,4},{2,7},{3,6},{4,1},{5,0},{6,3},{7,2},{8,13},{9,12},{10,... | collective-permute-start | bytes 786440 | tf_op jit(solution)/shard_map/ppermute | solution.py:23
  123.2 26.4 %collective-permute-start.25 = (bf16[1,64,2048]{2,1,0:T(8,128)(2,1)S(1)}, bf16[1,64,2048]{2,1,0:T(8,128)(2,1)S(1)}, u32[]{:S(2)}, u32[]{:S(2)}) collective-permute-start(bf16[1,64,2048]{2,1,0:T(8,128)(2,1)S(1)} %get-tuple-element.21), channel_id=1, source_target_pairs={{0,4},{1,5},{2,6},{3,7},{4,0},{5,1},{6,2},{7,3},{8,12},{9,13},{10,... | collective-permute-start | bytes 786440 | tf_op jit(solution)/shard_map/ppermute | solution.py:23
  149.8 1.3 copy-start.2
  149.8 2.0 %copy-start.3 = (bf16[1,8,64,2048]{3,2,1,0:T(8,128)(2,1)}, bf16[1,8,64,2048]{3,2,1,0:T(8,128)(2,1)S(1)}, u32[]{:S(2)}) copy-start(bf16[1,8,64,2048]{3,2,1,0:T(8,128)(2,1)S(1)} %get-tuple-element.39) | copy-start | bytes 6291460

commit v9 on v8

--- a/solution.py
+++ b/solution.py
@@ -117,13 +117,10 @@
 
 
 def grouped(shards):
-    groups = []
-    top = shards
-    for length in (shards // 8, shards // 8, shards // 4, shards // 2):
-        if length:
-            top -= length
-            groups.append((top, length))
-    return groups if top == 0 else [(0, shards)]
+    unit = shards // 8
+    if shards % 8:
+        return [(0, shards)]
+    return [(low * unit, count * unit) for low, count in ((7, 1), (6, 1), (2, 2), (4, 2), (0, 2))]
 
 
 def after(values, *others):
@@ -153,10 +150,14 @@
 
     new_tracker = jnp.zeros(shape, F32)
     blocks = [None] * shards
+    leads = []
     for turn, (lowest, length) in enumerate(grouped(shards)):
+        if turn == 2:
+            tracker = after(tracker, leads)
         start = (here ^ lowest) // length * length
         own = taken(tracker, start, length)
         rounded = own.astype(BF16)
+        leads.append(rounded)
         mixed = blend(first, own, swapped(rounded, "rep", 1))
         if turn < 2:
             far = swapped(rounded, "rep", 2)
@@ -164,9 +165,12 @@
         else:
             far = swapped(mixed.astype(BF16), "rep", 2)
             far_mixed = far.astype(F32)
-        group = second * mixed + (1.0 - second) * far_mixed
-        group += taken(grad_new, start, length).astype(F32)
-        group -= taken(grad_old, start, length).astype(F32)
+        base = second * mixed + (
+            taken(grad_new, start, length).astype(F32) - taken(grad_old, start, length).astype(F32)
+        )
+        if turn < 2:
+            base = lax.optimization_barrier(base)
+        group = base + (1.0 - second) * far_mixed
         for offset in reversed(range(lowest, lowest + length)):
             block = taken(group, (here ^ offset) % length, 1)[0].astype(BF16)
             blocks[offset] = swapped(block, "shard", offset) if offset else block

time: 152 us -> 162 us (1.066)
  starting transfers between devices: 32.8 us -> 42.7 us
    ppermute x26 -> x28, starting transfers between devices: 32.8 us -> 42.7 us  [swapped(): lax.ppermute(values, axis, [(i, i ^ offset) for i in range(lax.axis_size(...]
    dynamic_update_slice x4 -> x3, other arithmetic: 10.5 us -> 6.32 us  [local(): lax.dynamic_update_slice_in_dim(new_tracker, group, start, axis=0)]
    add x0 -> x1, other arithmetic: none -> 3.08 us  [local(): second * mixed]
    convert_element_type x0 -> x2, other arithmetic: none -> 2.1 us  [local(): block = taken(group, (here ^ offset) % length, 1)[0].astype(BF16)]
    ppermute x26 -> x28, waiting for transfers between devices: 72.9 us -> 72.6 us  [swapped(): lax.ppermute(values, axis, [(i, i ^ offset) for i in range(lax.axis_size(...]
    convert_element_type x3 -> x2, local copies, waits for them, and re-layouts: 5.29 us -> 5.18 us  [local(): rounded = own.astype(BF16)]
  transfers between devices with their start and end apart: 26 -> 28, of which waited for: 11 -> 12; matrix products, arithmetic and copies ran while one was open for 18% -> 16% of each run, Pallas kernels for 8% -> 8%
where the time goes in v9:
time: 162 us
  waiting for transfers between devices  72.6 us (45%)
  starting transfers between devices  42.7 us (26%)
  other arithmetic  22 us (14%)
  Pallas kernels  12.8 us (8%)
  local copies, waits for them, and re-layouts  9.05 us (6%)
  between operations  2.87 us (2%)
    ppermute x28, waiting for transfers between devices, swapped(): lax.ppermute(values, axis, [(i, i ^ offset) for i in range(lax.axis_size(...  72.6 us
    ppermute x28, starting transfers between devices, swapped(): lax.ppermute(values, axis, [(i, i ^ offset) for i in range(lax.axis_size(...  42.7 us
    pallas_call x1, Pallas kernels, orthogonalize(): pl.pallas_call(body, grid=(each,), in_specs=[block] * count, out_specs=[b...  12.8 us
    dynamic_update_slice x3, other arithmetic, local(): lax.dynamic_update_slice_in_dim(new_tracker, group, start, axis=0)  6.32 us
    convert_element_type x2, local copies, waits for them, and re-layouts, local(): rounded = own.astype(BF16)  5.18 us
    convert_element_type x1, other arithmetic, local(): mixed_weight = (second * weight_own.astype(F32) + (1.0 - second) * weight...  3.71 us
  transfers between devices with their start and end apart: 28, of which 12 were waited for; matrix products, arithmetic and copies ran while one was open for 16% of the time, Pallas kernels for 8%

profile of v9, /device:TPU:0, one launch (start us, length us, event | category | flops | bytes accessed | tf_op | source)
XLA Modules:
  0.0 162.0 jit_solution(13897913399732728268)
XLA Ops:
  0.7 2.1 %dynamic-slice_convert_fusion.9 = (bf16[1,1,64,2048]{3,2,1,0:T(8,128)(2,1)S(1)}, bf16[1,1,64,2048]{3,2,1,0:T(8,128)(2,1)}) fusion(f32[1,8,64,2048]{3,2,1,0:T(8,128)} %param.6, s32[]{:T(128)S(6)} %select_n.138, s32[]{:T(128)S(6)} %select_n.137), kind=kLoop, calls=%fused_computation.46 | loop fusion | bytes 1048584 | tf_op jit(solution)/shard_map/convert_element_type | solution.py:159
  2.8 0.5 collective-permute-start.13
  3.3 3.1 %dynamic-slice_convert_fusion.2 = (bf16[2,1,64,2048]{3,2,1,0:T(8,128)(2,1)}, bf16[2,1,64,2048]{3,2,1,0:T(8,128)(2,1)}, bf16[2,1,64,2048]{3,2,1,0:T(8,128)(2,1)}) fusion(f32[8,1,64,2048]{3,2,1,0:T(8,128)} %bitcast.115, s32[]{:T(128)S(6)} %select_n.140, s32[]{:T(128)S(6)} %select_n.146, s32[]{:T(128)S(6)} %select_n.152), kind=kLoop, calls=%fused_computation.16 | loop fusion | bytes 3145740 | tf_op jit(solution)/shard_map/convert_element_type | solution.py:159
  6.4 0.5 collective-permute-start.1
  6.9 0.5 collective-permute-start.9
  7.3 0.7 constant_dynamic-slice_fusion
  9.9 2.7 %collective-permute-start.18 = (bf16[1,1,64,2048]{3,2,1,0:T(8,128)(2,1)}, bf16[1,1,64,2048]{3,2,1,0:T(8,128)(2,1)S(1)}, u32[]{:S(2)}, u32[]{:S(2)}) collective-permute-start(bf16[1,1,64,2048]{3,2,1,0:T(8,128)(2,1)} %get-tuple-element.40), channel_id=1, source_target_pairs={{0,16},{8,24},{16,0},{24,8},{1,17},{9,25},{17,1},{25,9},{2,18},{10... | collective-permute-start | bytes 786440 | tf_op jit(solution)/shard_map/ppermute | solution.py:23
  12.7 3.1 %subtract_add_fusion.1 = (f32[1,1,64,2048]{3,2,1,0:T(8,128)S(1)}, f32[1,1,64,2048]{3,2,1,0:T(8,128)S(1)}) fusion(bf16[1,1,64,2048]{3,2,1,0:T(8,128)(2,1)} %collective-permute-done.13, f32[1,8,64,2048]{3,2,1,0:T(8,128)} %param.6, s32[]{:T(128)S(6)} %select_n.138, bf16[1,8,64,2048]{3,2,1,0:T(8,128)(2,1)S(1)} %copy-done.2, bf16[1,8,64,2048]{3,2,1,0:T(8,128)(2,1)} %param.7, ...), kind=kLoop, calls=%fused_computation.39 | loop fusion | flops 2359296 | bytes 3670036 | tf_op jit(solution)/shard_map/add | solution.py:168
  15.8 4.2 %collective-permute-done.18 = bf16[1,1,64,2048]{3,2,1,0:T(8,128)(2,1)S(1)} collective-permute-done((bf16[1,1,64,2048]{3,2,1,0:T(8,128)(2,1)}, bf16[1,1,64,2048]{3,2,1,0:T(8,128)(2,1)S(1)}, u32[]{:S(2)}, u32[]{:S(2)}) %collective-permute-start.18) | collective-permute-done | bytes 262176 | tf_op jit(solution)/shard_map/ppermute | solution.py:23
  20.0 5.3 %collective-permute-done.14 = bf16[1,1,64,2048]{3,2,1,0:T(8,128)(2,1)S(1)} collective-permute-done((bf16[1,1,64,2048]{3,2,1,0:T(8,128)(2,1)S(1)}, bf16[1,1,64,2048]{3,2,1,0:T(8,128)(2,1)S(1)}, u32[]{:S(2)}, u32[]{:S(2)}) %collective-permute-start.14) | collective-permute-done | bytes 262176 | tf_op jit(solution)/shard_map/ppermute | solution.py:23
  25.3 0.5 collective-permute-start.15
  25.8 3.2 %fusion.3 = (bf16[2,1,64,2048]{3,2,1,0:T(8,128)(2,1)S(1)}, bf16[2,1,64,2048]{3,2,1,0:T(8,128)(2,1)S(1)}, bf16[2,1,64,2048]{3,2,1,0:T(8,128)(2,1)S(1)}) fusion(bf16[2,1,64,2048]{3,2,1,0:T(8,128)(2,1)S(1)} %collective-permute-done.1, f32[8,1,64,2048]{3,2,1,0:T(8,128)} %bitcast.116, s32[]{:T(128)S(6)} %select_n.140, f32[]{:T(128)S(6)} %sub.108, f32[]{:T(128)} %bitcast.1, ...), kind=kLoop, calls=%fused_computation.17 | loop fusion | flops 3932160 | bytes 6291476 | tf_op jit(solution)/shard_map/convert_element_type | solution.py:166
  29.0 1.8 %collective-permute-start.6 = (bf16[2,1,64,2048]{3,2,1,0:T(8,128)(2,1)S(1)}, bf16[2,1,64,2048]{3,2,1,0:T(8,128)(2,1)S(1)}, u32[]{:S(2)}, u32[]{:S(2)}) collective-permute-start(bf16[2,1,64,2048]{3,2,1,0:T(8,128)(2,1)S(1)} %get-tuple-element.35), channel_id=1, source_target_pairs={{0,16},{8,24},{16,0},{24,8},{1,17},{9,25},{17,1},{25,9},{2,18},{10... | collective-permute-start | bytes 1572872 | tf_op jit(solution)/shard_map/ppermute | solution.py:23
  31.1 1.7 %collective-permute-start.2 = (bf16[2,1,64,2048]{3,2,1,0:T(8,128)(2,1)S(1)}, bf16[2,1,64,2048]{3,2,1,0:T(8,128)(2,1)S(1)}, u32[]{:S(2)}, u32[]{:S(2)}) collective-permute-start(bf16[2,1,64,2048]{3,2,1,0:T(8,128)(2,1)S(1)} %get-tuple-element.33), channel_id=1, source_target_pairs={{0,16},{8,24},{16,0},{24,8},{1,17},{9,25},{17,1},{25,9},{2,18},{10... | collective-permute-start | bytes 1572872 | tf_op jit(solution)/shard_map/ppermute | solution.py:23
  32.8 0.5 reshape.419
  33.3 1.0 convert_bitcast_fusion
  34.4 1.1 convert_bitcast_fusion.1
  35.5 3.7 %collective-permute-start.16 = (bf16[1,64,2048]{2,1,0:T(8,128)(2,1)S(1)}, bf16[1,64,2048]{2,1,0:T(8,128)(2,1)S(1)}, u32[]{:S(2)}, u32[]{:S(2)}) collective-permute-start(bf16[1,64,2048]{2,1,0:T(8,128)(2,1)S(1)} %get-tuple-element.43), channel_id=1, source_target_pairs={{0,6},{1,7},{2,4},{3,5},{4,2},{5,3},{6,0},{7,1},{8,14},{9,15},{10,... | collective-permute-start | bytes 786440 | tf_op jit(solution)/shard_map/ppermute | solution.py:23
  39.1 4.7 %collective-permute-done.6 = bf16[2,1,64,2048]{3,2,1,0:T(8,128)(2,1)S(1)} collective-permute-done((bf16[2,1,64,2048]{3,2,1,0:T(8,128)(2,1)S(1)}, bf16[2,1,64,2048]{3,2,1,0:T(8,128)(2,1)S(1)}, u32[]{:S(2)}, u32[]{:S(2)}) %collective-permute-start.6) | collective-permute-done | bytes 524320 | tf_op jit(solution)/shard_map/ppermute | solution.py:23
  43.8 4.8 %collective-permute-start.20 = (bf16[1,64,2048]{2,1,0:T(8,128)(2,1)S(1)}, bf16[1,64,2048]{2,1,0:T(8,128)(2,1)S(1)}, u32[]{:S(2)}, u32[]{:S(2)}) collective-permute-start(bf16[1,64,2048]{2,1,0:T(8,128)(2,1)S(1)} %get-tuple-element.41), channel_id=1, source_target_pairs={{0,7},{1,6},{2,5},{3,4},{4,3},{5,2},{6,1},{7,0},{8,15},{9,14},{10,... | collective-permute-start | bytes 786440 | tf_op jit(solution)/shard_map/ppermute | solution.py:23
  48.7 2.8 %bitcast_dynamic-update-slice_fusion.2 = (f32[1,8,64,2048]{3,2,1,0:T(8,128)S(1)}, bf16[2,1,64,2048]{3,2,1,0:T(8,128)(2,1)S(1)}) fusion(f32[1,8,64,2048]{3,2,1,0:T(8,128)S(1)} %get-tuple-element.44, s32[]{:T(128)S(6)} %select_n.146, bf16[2,1,64,2048]{3,2,1,0:T(8,128)(2,1)S(1)} %collective-permute-done.6, f32[]{:T(128)S(6)} %sub.110, ...), kind=kLoop, calls=%fused_computation.4 | loop fusion | flops 3407872 | bytes 4718612 | tf_op jit(solution)/shard_map/dynamic_update_slice | solution.py:177
  51.5 3.6 %collective-permute-done.10 = bf16[2,1,64,2048]{3,2,1,0:T(8,128)(2,1)S(1)} collective-permute-done((bf16[2,1,64,2048]{3,2,1,0:T(8,128)(2,1)S(1)}, bf16[2,1,64,2048]{3,2,1,0:T(8,128)(2,1)S(1)}, u32[]{:S(2)}, u32[]{:S(2)}) %collective-permute-start.10) | collective-permute-done | bytes 524320 | tf_op jit(solution)/shard_map/ppermute | solution.py:23
  55.1 1.8 %bitcast_dynamic-update-slice_fusion.1 = (f32[1,8,64,2048]{3,2,1,0:T(8,128)S(1)}, bf16[2,1,64,2048]{3,2,1,0:T(8,128)(2,1)S(1)}) fusion(f32[1,8,64,2048]{3,2,1,0:T(8,128)S(1)} %get-tuple-element.29, s32[]{:T(128)S(6)} %select_n.152, bf16[2,1,64,2048]{3,2,1,0:T(8,128)(2,1)S(1)} %collective-permute-done.10, f32[]{:T(128)S(6)} %sub.110, ...), kind=kLoop, calls=%fused_computation.3 | loop fusion | flops 3407872 | bytes 4718612 | tf_op jit(solution)/shard_map/dynamic_update_slice | solution.py:177
  56.8 8.5 %collective-permute-done.2 = bf16[2,1,64,2048]{3,2,1,0:T(8,128)(2,1)S(1)} collective-permute-done((bf16[2,1,64,2048]{3,2,1,0:T(8,128)(2,1)S(1)}, bf16[2,1,64,2048]{3,2,1,0:T(8,128)(2,1)S(1)}, u32[]{:S(2)}, u32[]{:S(2)}) %collective-permute-start.2) | collective-permute-done | bytes 524320 | tf_op jit(solution)/shard_map/ppermute | solution.py:23
  65.4 1.8 %bitcast_dynamic-update-slice_fusion = (f32[1,8,64,2048]{3,2,1,0:T(8,128)S(1)}, bf16[2,1,64,2048]{3,2,1,0:T(8,128)(2,1)S(1)}) fusion(f32[1,8,64,2048]{3,2,1,0:T(8,128)S(1)} %get-tuple-element.27, s32[]{:T(128)S(6)} %select_n.140, bf16[2,1,64,2048]{3,2,1,0:T(8,128)(2,1)S(1)} %collective-permute-done.2, f32[]{:T(128)S(6)} %sub.110, ...), kind=kLoop, calls=%fused_computation.2 | loop fusion | flops 3407872 | bytes 4718612 | tf_op jit(solution)/shard_map/dynamic_update_slice | solution.py:177
  67.2 1.8 %collective-permute-start.4 = (bf16[1,64,2048]{2,1,0:T(8,128)(2,1)S(1)}, bf16[1,64,2048]{2,1,0:T(8,128)(2,1)S(1)}, u32[]{:S(2)}, u32[]{:S(2)}) collective-permute-start(bf16[1,64,2048]{2,1,0:T(8,128)(2,1)S(1)} %get-tuple-element.49), channel_id=1, source_target_pairs={{0,1},{1,0},{2,3},{3,2},{4,5},{5,4},{6,7},{7,6},{8,9},{9,8},{10,11... | collective-permute-start | bytes 786440 | tf_op jit(solution)/shard_map/ppermute | solution.py:23
  69.1 2.8 %collective-permute-start.11 = (bf16[1,64,2048]{2,1,0:T(8,128)(2,1)S(1)}, bf16[1,64,2048]{2,1,0:T(8,128)(2,1)S(1)}, u32[]{:S(2)}, u32[]{:S(2)}) collective-permute-start(bf16[1,64,2048]{2,1,0:T(8,128)(2,1)S(1)} %get-tuple-element.46), channel_id=1, source_target_pairs={{0,4},{1,5},{2,6},{3,7},{4,0},{5,1},{6,2},{7,3},{8,12},{9,13},{10,... | collective-permute-start | bytes 786440 | tf_op jit(solution)/shard_map/ppermute | solution.py:23
  72.0 2.9 %add_convert_fusion.1 = bf16[8,1,64,2048]{3,2,1,0:T(8,128)(2,1)} fusion(bf16[8,1,64,2048]{3,2,1,0:T(8,128)(2,1)S(1)} %collective-permute-done, f32[]{:T(128)S(6)} %sub.108, f32[]{:T(128)} %bitcast.1, bf16[1,8,64,2048]{3,2,1,0:T(8,128)(2,1)S(1)} %copy-done.6), kind=kLoop, calls=%fused_computation.1 | loop fusion | flops 6291456 | bytes 6291464 | tf_op jit(solution)/shard_map/convert_element_type | solution.py:182
  74.9 1.5 collective-permute-start.3
  76.4 1.4 collective-permute-start.12
  77.8 1.6 collective-permute-start.7
  79.3 0.4 collective-permute-start.8
  79.7 10.5 %collective-permute-done.11.refs_4_ = bf16[1,64,2048]{2,1,0:T(8,128)(2,1)S(1)} collective-permute-done((bf16[1,64,2048]{2,1,0:T(8,128)(2,1)S(1)}, bf16[1,64,2048]{2,1,0:T(8,128)(2,1)S(1)}, u32[]{:S(2)}, u32[]{:S(2)}) %collective-permute-start.11) | collective-permute-done | bytes 262176 | tf_op jit(solution)/shard_map/ppermute | solution.py:23
  90.2 5.4 %collective-permute-done.12.refs_5_ = bf16[1,64,2048]{2,1,0:T(8,128)(2,1)S(1)} collective-permute-done((bf16[1,64,2048]{2,1,0:T(8,128)(2,1)S(1)}, bf16[1,64,2048]{2,1,0:T(8,128)(2,1)S(1)}, u32[]{:S(2)}, u32[]{:S(2)}) %collective-permute-start.12) | collective-permute-done | bytes 262176 | tf_op jit(solution)/shard_map/ppermute | solution.py:23
  95.6 4.5 %collective-permute-done.8.refs_3_ = bf16[1,64,2048]{2,1,0:T(8,128)(2,1)S(1)} collective-permute-done((bf16[1,64,2048]{2,1,0:T(8,128)(2,1)S(1)}, bf16[1,64,2048]{2,1,0:T(8,128)(2,1)S(1)}, u32[]{:S(2)}, u32[]{:S(2)}) %collective-permute-start.8) | collective-permute-done | bytes 262176 | tf_op jit(solution)/shard_map/ppermute | solution.py:23
  100.1 12.8 %orthogonalize.1 = (bf16[1,64,2048]{2,1,0:T(8,128)(2,1)S(1)}, bf16[1,64,2048]{2,1,0:T(8,128)(2,1)S(1)}, bf16[1,64,2048]{2,1,0:T(8,128)(2,1)S(1)}, bf16[1,64,2048...) custom-call(bf16[1,64,2048]{2,1,0:T(8,128)(2,1)S(1)} %get-tuple-elem, ...), custom_call_target="tpu_custom_call" | custom-call | flops 11005853696 | bytes 4194304 | tf_op jit(solution)/shard_map/orthogonalize/pallas_call | solution.py:102
  112.9 1.4 collective-permute-start.22
  114.3 4.6 %collective-permute-start.21 = (bf16[1,64,2048]{2,1,0:T(8,128)(2,1)S(1)}, bf16[1,64,2048]{2,1,0:T(8,128)(2,1)S(1)}, u32[]{:S(2)}, u32[]{:S(2)}) collective-permute-start(bf16[1,64,2048]{2,1,0:T(8,128)(2,1)S(1)} %get-tuple-element.16), channel_id=1, source_target_pairs={{0,7},{1,6},{2,5},{3,4},{4,3},{5,2},{6,1},{7,0},{8,15},{9,14},{10,... | collective-permute-start | bytes 786440 | tf_op jit(solution)/shard_map/ppermute | solution.py:23
  118.9 3.0 %collective-permute-start.24 = (bf16[1,64,2048]{2,1,0:T(8,128)(2,1)S(1)}, bf16[1,64,2048]{2,1,0:T(8,128)(2,1)S(1)}, u32[]{:S(2)}, u32[]{:S(2)}) collective-permute-start(bf16[1,64,2048]{2,1,0:T(8,128)(2,1)S(1)} %get-tuple-element.20), channel_id=1, source_target_pairs={{0,3},{1,2},{2,1},{3,0},{4,7},{5,6},{6,5},{7,4},{8,11},{9,10},{10,... | collective-permute-start | bytes 786440 | tf_op jit(solution)/shard_map/ppermute | solution.py:23
  121.9 3.0 %collective-permute-done.22 = bf16[1,64,2048]{2,1,0:T(8,128)(2,1)S(1)} collective-permute-done((bf16[1,64,2048]{2,1,0:T(8,128)(2,1)S(1)}, bf16[1,64,2048]{2,1,0:T(8,128)(2,1)S(1)}, u32[]{:S(2)}, u32[]{:S(2)}) %collective-permute-start.22) | collective-permute-done | bytes 262176 | tf_op jit(solution)/shard_map/ppermute | solution.py:23
  124.9 3.1 %collective-permute-start.25 = (bf16[1,64,2048]{2,1,0:T(8,128)(2,1)S(1)}, bf16[1,64,2048]{2,1,0:T(8,128)(2,1)S(1)}, u32[]{:S(2)}, u32[]{:S(2)}) collective-permute-start(bf16[1,64,2048]{2,1,0:T(8,128)(2,1)S(1)} %get-tuple-element.21), channel_id=1, source_target_pairs={{0,6},{1,7},{2,4},{3,5},{4,2},{5,3},{6,0},{7,1},{8,14},{9,15},{10,... | collective-permute-start | bytes 786440 | tf_op jit(solution)/shard_map/ppermute | solution.py:23
  128.3 3.7 %add_convert_fusion = bf16[8,1,64,2048]{3,2,1,0:T(8,128)(2,1)S(1)} fusion(bf16[8,1,64,2048]{3,2,1,0:T(8,128)(2,1)} %collective-permute-done.3, bf16[8,1,64,2048]{3,2,1,0:T(8,128)(2,1)} %add_convert_fusion.1, f32[]{:T(128)S(6)} %sub.110, f32[]{:T(128)} %bitcast), kind=kLoop, calls=%fused_computation | loop fusion | flops 6291456 | bytes 6291464 | tf_op jit(solution)/shard_map/convert_element_type | solution.py:187
  132.1 3.9 %collective-permute-start.27 = (bf16[1,64,2048]{2,1,0:T(8,128)(2,1)S(1)}, bf16[1,64,2048]{2,1,0:T(8,128)(2,1)S(1)}, u32[]{:S(2)}, u32[]{:S(2)}) collective-permute-start(bf16[1,64,2048]{2,1,0:T(8,128)(2,1)S(1)} %get-tuple-element.23), channel_id=1, source_target_pairs={{0,4},{1,5},{2,6},{3,7},{4,0},{5,1},{6,2},{7,3},{8,12},{9,13},{10,... | collective-permute-start | bytes 786440 | tf_op jit(solution)/shard_map/ppermute | solution.py:23
  136.5 7.6 %collective-permute-done.24 = bf16[1,64,2048]{2,1,0:T(8,128)(2,1)S(1)} collective-permute-done((bf16[1,64,2048]{2,1,0:T(8,128)(2,1)S(1)}, bf16[1,64,2048]{2,1,0:T(8,128)(2,1)S(1)}, u32[]{:S(2)}, u32[]{:S(2)}) %collective-permute-start.24) | collective-permute-done | bytes 262176 | tf_op jit(solution)/shard_map/ppermute | solution.py:23
  144.3 13.0 %collective-permute-done.26 = bf16[1,64,2048]{2,1,0:T(8,128)(2,1)S(1)} collective-permute-done((bf16[1,64,2048]{2,1,0:T(8,128)(2,1)S(1)}, bf16[1,64,2048]{2,1,0:T(8,128)(2,1)S(1)}, u32[]{:S(2)}, u32[]{:S(2)}) %collective-permute-start.26) | collective-permute-done | bytes 262176 | tf_op jit(solution)/shard_map/ppermute | solution.py:23
  157.5 2.3 %collective-permute-done.27 = bf16[1,64,2048]{2,1,0:T(8,128)(2,1)S(1)} collective-permute-done((bf16[1,64,2048]{2,1,0:T(8,128)(2,1)S(1)}, bf16[1,64,2048]{2,1,0:T(8,128)(2,1)S(1)}, u32[]{:S(2)}, u32[]{:S(2)}) %collective-permute-start.27) | collective-permute-done | bytes 262176 | tf_op jit(solution)/shard_map/ppermute | solution.py:23
  160.0 1.3 copy-done.4
  161.3 0.7 copy-done.5
  (53 shorter events, 2.1 us)
Async XLA Ops:
  0.6 6.7 %copy-start.7 = (s32[4,2]{0,1:T(2,128)S(1)}, s32[4,2]{0,1:T(2,128)}, u32[]{:S(2)}) copy-start(s32[4,2]{0,1:T(2,128)} %param.9) | copy-start | bytes 100
  0.7 12.1 %copy-start.2 = (bf16[1,8,64,2048]{3,2,1,0:T(8,128)(2,1)S(1)}, bf16[1,8,64,2048]{3,2,1,0:T(8,128)(2,1)}, u32[]{:S(2)}) copy-start(bf16[1,8,64,2048]{3,2,1,0:T(8,128)(2,1)} %param.8) | copy-start | bytes 6291460
  2.8 7.1 %collective-permute-start.13 = (bf16[1,1,64,2048]{3,2,1,0:T(8,128)(2,1)S(1)}, bf16[1,1,64,2048]{3,2,1,0:T(8,128)(2,1)}, u32[]{:S(2)}, u32[]{:S(2)}) collective-permute-start(bf16[1,1,64,2048]{3,2,1,0:T(8,128)(2,1)S(1)} %get-tuple-element.39), channel_id=1, source_target_pairs={{0,8},{8,0},{16,24},{24,16},{1,9},{9,1},{17,25},{25,17},{2,10},{10... | collective-permute-start | bytes 786440 | tf_op jit(solution)/shard_map/ppermute | solution.py:23
  3.2 9.4 %collective-permute-start.17 = (bf16[1,1,64,2048]{3,2,1,0:T(8,128)(2,1)}, bf16[1,1,64,2048]{3,2,1,0:T(8,128)(2,1)}, u32[]{:S(2)}, u32[]{:S(2)}) collective-permute-start(bf16[1,1,64,2048]{3,2,1,0:T(8,128)(2,1)} %get-tuple-element.40), channel_id=1, source_target_pairs={{0,8},{8,0},{16,24},{24,16},{1,9},{9,1},{17,25},{25,17},{2,10},{10... | collective-permute-start | bytes 786440 | tf_op jit(solution)/shard_map/ppermute | solution.py:23
  6.4 18.9 %collective-permute-start.1 = (bf16[2,1,64,2048]{3,2,1,0:T(8,128)(2,1)}, bf16[2,1,64,2048]{3,2,1,0:T(8,128)(2,1)S(1)}, u32[]{:S(2)}, u32[]{:S(2)}) collective-permute-start(bf16[2,1,64,2048]{3,2,1,0:T(8,128)(2,1)} %get-tuple-element.36), channel_id=1, source_target_pairs={{0,8},{8,0},{16,24},{24,16},{1,9},{9,1},{17,25},{25,17},{2,10},{10... | collective-permute-start | bytes 1572872 | tf_op jit(solution)/shard_map/ppermute | solution.py:23
  6.8 19.0 %collective-permute-start.5 = (bf16[2,1,64,2048]{3,2,1,0:T(8,128)(2,1)}, bf16[2,1,64,2048]{3,2,1,0:T(8,128)(2,1)}, u32[]{:S(2)}, u32[]{:S(2)}) collective-permute-start(bf16[2,1,64,2048]{3,2,1,0:T(8,128)(2,1)} %get-tuple-element.37), channel_id=1, source_target_pairs={{0,8},{8,0},{16,24},{24,16},{1,9},{9,1},{17,25},{25,17},{2,10},{10... | collective-permute-start | bytes 1572872 | tf_op jit(solution)/shard_map/ppermute | solution.py:23
  6.9 18.9 %collective-permute-start.9 = (bf16[2,1,64,2048]{3,2,1,0:T(8,128)(2,1)}, bf16[2,1,64,2048]{3,2,1,0:T(8,128)(2,1)S(1)}, u32[]{:S(2)}, u32[]{:S(2)}) collective-permute-start(bf16[2,1,64,2048]{3,2,1,0:T(8,128)(2,1)} %get-tuple-element.38), channel_id=1, source_target_pairs={{0,8},{8,0},{16,24},{24,16},{1,9},{9,1},{17,25},{25,17},{2,10},{10... | collective-permute-start | bytes 1572872 | tf_op jit(solution)/shard_map/ppermute | solution.py:23
  9.9 10.1 %copy-start.6 = (bf16[1,8,64,2048]{3,2,1,0:T(8,128)(2,1)S(1)}, bf16[1,8,64,2048]{3,2,1,0:T(8,128)(2,1)}, u32[]{:S(2)}) copy-start(bf16[1,8,64,2048]{3,2,1,0:T(8,128)(2,1)} %param.5) | copy-start | bytes 6291460
  9.9 10.1 %collective-permute-start.18 = (bf16[1,1,64,2048]{3,2,1,0:T(8,128)(2,1)}, bf16[1,1,64,2048]{3,2,1,0:T(8,128)(2,1)S(1)}, u32[]{:S(2)}, u32[]{:S(2)}) collective-permute-start(bf16[1,1,64,2048]{3,2,1,0:T(8,128)(2,1)} %get-tuple-element.40), channel_id=1, source_target_pairs={{0,16},{8,24},{16,0},{24,8},{1,17},{9,25},{17,1},{25,9},{2,18},{10... | collective-permute-start | bytes 786440 | tf_op jit(solution)/shard_map/ppermute | solution.py:23
  12.6 12.7 %collective-permute-start.14 = (bf16[1,1,64,2048]{3,2,1,0:T(8,128)(2,1)S(1)}, bf16[1,1,64,2048]{3,2,1,0:T(8,128)(2,1)S(1)}, u32[]{:S(2)}, u32[]{:S(2)}) collective-permute-start(bf16[1,1,64,2048]{3,2,1,0:T(8,128)(2,1)S(1)} %get-tuple-element.39), channel_id=1, source_target_pairs={{0,16},{8,24},{16,0},{24,8},{1,17},{9,25},{17,1},{25,9},{2,18},{10... | collective-permute-start | bytes 786440 | tf_op jit(solution)/shard_map/ppermute | solution.py:23
  20.0 52.0 %collective-permute-start = (bf16[8,1,64,2048]{3,2,1,0:T(8,128)(2,1)S(1)}, bf16[8,1,64,2048]{3,2,1,0:T(8,128)(2,1)S(1)}, u32[]{:S(2)}, u32[]{:S(2)}) collective-permute-start(bf16[8,1,64,2048]{3,2,1,0:T(8,128)(2,1)S(1)} %bitcast.120), channel_id=1, source_target_pairs={{0,8},{8,0},{16,24},{24,16},{1,9},{9,1},{17,25},{25,17},{2,10},{10... | collective-permute-start | bytes 6291464 | tf_op jit(solution)/shard_map/ppermute | solution.py:23
  25.3 5.8 %collective-permute-start.19 = (bf16[1,1,64,2048]{3,2,1,0:T(8,128)(2,1)S(1)}, bf16[1,1,64,2048]{3,2,1,0:T(8,128)(2,1)S(1)}, u32[]{:S(2)}, u32[]{:S(2)}) collective-permute-start(bf16[1,1,64,2048]{3,2,1,0:T(8,128)(2,1)S(1)} %collective-permute-done.18), channel_id=1, source_target_pairs={{0,8},{8,0},{16,24},{24,16},{1,9},{9,1},{17,25},{25,17},{2,10},{10... | collective-permute-start | bytes 786440 | tf_op jit(solution)/shard_map/ppermute | solution.py:23
  25.3 9.1 %collective-permute-start.15 = (bf16[1,1,64,2048]{3,2,1,0:T(8,128)(2,1)S(1)}, bf16[1,1,64,2048]{3,2,1,0:T(8,128)(2,1)S(1)}, u32[]{:S(2)}, u32[]{:S(2)}) collective-permute-start(bf16[1,1,64,2048]{3,2,1,0:T(8,128)(2,1)S(1)} %collective-permute-done.14), channel_id=1, source_target_pairs={{0,8},{8,0},{16,24},{24,16},{1,9},{9,1},{17,25},{25,17},{2,10},{10... | collective-permute-start | bytes 786440 | tf_op jit(solution)/shard_map/ppermute | solution.py:23
  29.0 14.9 %collective-permute-start.6 = (bf16[2,1,64,2048]{3,2,1,0:T(8,128)(2,1)S(1)}, bf16[2,1,64,2048]{3,2,1,0:T(8,128)(2,1)S(1)}, u32[]{:S(2)}, u32[]{:S(2)}) collective-permute-start(bf16[2,1,64,2048]{3,2,1,0:T(8,128)(2,1)S(1)} %get-tuple-element.35), channel_id=1, source_target_pairs={{0,16},{8,24},{16,0},{24,8},{1,17},{9,25},{17,1},{25,9},{2,18},{10... | collective-permute-start | bytes 1572872 | tf_op jit(solution)/shard_map/ppermute | solution.py:23
  30.8 24.3 %collective-permute-start.10 = (bf16[2,1,64,2048]{3,2,1,0:T(8,128)(2,1)S(1)}, bf16[2,1,64,2048]{3,2,1,0:T(8,128)(2,1)S(1)}, u32[]{:S(2)}, u32[]{:S(2)}) collective-permute-start(bf16[2,1,64,2048]{3,2,1,0:T(8,128)(2,1)S(1)} %get-tuple-element.34), channel_id=1, source_target_pairs={{0,16},{8,24},{16,0},{24,8},{1,17},{9,25},{17,1},{25,9},{2,18},{10... | collective-permute-start | bytes 1572872 | tf_op jit(solution)/shard_map/ppermute | solution.py:23
  31.1 34.3 %collective-permute-start.2 = (bf16[2,1,64,2048]{3,2,1,0:T(8,128)(2,1)S(1)}, bf16[2,1,64,2048]{3,2,1,0:T(8,128)(2,1)S(1)}, u32[]{:S(2)}, u32[]{:S(2)}) collective-permute-start(bf16[2,1,64,2048]{3,2,1,0:T(8,128)(2,1)S(1)} %get-tuple-element.33), channel_id=1, source_target_pairs={{0,16},{8,24},{16,0},{24,8},{1,17},{9,25},{17,1},{25,9},{2,18},{10... | collective-permute-start | bytes 1572872 | tf_op jit(solution)/shard_map/ppermute | solution.py:23
  32.8 15.8 %copy-start = (f32[1,8,64,2048]{3,2,1,0:T(8,128)S(1)}, f32[1,8,64,2048]{3,2,1,0:T(8,128)}, u32[]{:S(2)}) copy-start(f32[1,8,64,2048]{3,2,1,0:T(8,128)} %param.6) | copy-start | bytes 12582916
  33.3 15.3 %copy-start.3 = (bf16[1,8,64,2048]{3,2,1,0:T(8,128)(2,1)S(1)}, bf16[1,8,64,2048]{3,2,1,0:T(8,128)(2,1)}, u32[]{:S(2)}) copy-start(bf16[1,8,64,2048]{3,2,1,0:T(8,128)(2,1)} %param.7) | copy-start | bytes 6291460
  35.5 40.9 %collective-permute-start.16 = (bf16[1,64,2048]{2,1,0:T(8,128)(2,1)S(1)}, bf16[1,64,2048]{2,1,0:T(8,128)(2,1)S(1)}, u32[]{:S(2)}, u32[]{:S(2)}) collective-permute-start(bf16[1,64,2048]{2,1,0:T(8,128)(2,1)S(1)} %get-tuple-element.43), channel_id=1, source_target_pairs={{0,6},{1,7},{2,4},{3,5},{4,2},{5,3},{6,0},{7,1},{8,14},{9,15},{10,... | collective-permute-start | bytes 786440 | tf_op jit(solution)/shard_map/ppermute | solution.py:23
  43.8 33.9 %collective-permute-start.20 = (bf16[1,64,2048]{2,1,0:T(8,128)(2,1)S(1)}, bf16[1,64,2048]{2,1,0:T(8,128)(2,1)S(1)}, u32[]{:S(2)}, u32[]{:S(2)}) collective-permute-start(bf16[1,64,2048]{2,1,0:T(8,128)(2,1)S(1)} %get-tuple-element.41), channel_id=1, source_target_pairs={{0,7},{1,6},{2,5},{3,4},{4,3},{5,2},{6,1},{7,0},{8,15},{9,14},{10,... | collective-permute-start | bytes 786440 | tf_op jit(solution)/shard_map/ppermute | solution.py:23
  67.1 2.0 %copy-start.1 = (f32[1,8,64,2048]{3,2,1,0:T(8,128)}, f32[1,8,64,2048]{3,2,1,0:T(8,128)S(1)}, u32[]{:S(2)}) copy-start(f32[1,8,64,2048]{3,2,1,0:T(8,128)S(1)} %get-tuple-element.25) | copy-start | bytes 12582916
  67.2 12.2 %collective-permute-start.4 = (bf16[1,64,2048]{2,1,0:T(8,128)(2,1)S(1)}, bf16[1,64,2048]{2,1,0:T(8,128)(2,1)S(1)}, u32[]{:S(2)}, u32[]{:S(2)}) collective-permute-start(bf16[1,64,2048]{2,1,0:T(8,128)(2,1)S(1)} %get-tuple-element.49), channel_id=1, source_target_pairs={{0,1},{1,0},{2,3},{3,2},{4,5},{5,4},{6,7},{7,6},{8,9},{9,8},{10,11... | collective-permute-start | bytes 786440 | tf_op jit(solution)/shard_map/ppermute | solution.py:23
  69.1 21.1 %collective-permute-start.11 = (bf16[1,64,2048]{2,1,0:T(8,128)(2,1)S(1)}, bf16[1,64,2048]{2,1,0:T(8,128)(2,1)S(1)}, u32[]{:S(2)}, u32[]{:S(2)}) collective-permute-start(bf16[1,64,2048]{2,1,0:T(8,128)(2,1)S(1)} %get-tuple-element.46), channel_id=1, source_target_pairs={{0,4},{1,5},{2,6},{3,7},{4,0},{5,1},{6,2},{7,3},{8,12},{9,13},{10,... | collective-permute-start | bytes 786440 | tf_op jit(solution)/shard_map/ppermute | solution.py:23
  74.9 53.4 %collective-permute-start.3 = (bf16[8,1,64,2048]{3,2,1,0:T(8,128)(2,1)}, bf16[8,1,64,2048]{3,2,1,0:T(8,128)(2,1)}, u32[]{:S(2)}, u32[]{:S(2)}) collective-permute-start(bf16[8,1,64,2048]{3,2,1,0:T(8,128)(2,1)} %add_convert_fusion.1), channel_id=1, source_target_pairs={{0,16},{8,24},{16,0},{24,8},{1,17},{9,25},{17,1},{25,9},{2,18},{10... | collective-permute-start | bytes 6291464 | tf_op jit(solution)/shard_map/ppermute | solution.py:23
  76.4 19.2 %collective-permute-start.12 = (bf16[1,64,2048]{2,1,0:T(8,128)(2,1)S(1)}, bf16[1,64,2048]{2,1,0:T(8,128)(2,1)S(1)}, u32[]{:S(2)}, u32[]{:S(2)}) collective-permute-start(bf16[1,64,2048]{2,1,0:T(8,128)(2,1)S(1)} %get-tuple-element.45), channel_id=1, source_target_pairs={{0,5},{1,4},{2,7},{3,6},{4,1},{5,0},{6,3},{7,2},{8,13},{9,12},{10,... | collective-permute-start | bytes 786440 | tf_op jit(solution)/shard_map/ppermute | solution.py:23
  77.8 17.8 %collective-permute-start.7 = (bf16[1,64,2048]{2,1,0:T(8,128)(2,1)S(1)}, bf16[1,64,2048]{2,1,0:T(8,128)(2,1)S(1)}, u32[]{:S(2)}, u32[]{:S(2)}) collective-permute-start(bf16[1,64,2048]{2,1,0:T(8,128)(2,1)S(1)} %get-tuple-element.48), channel_id=1, source_target_pairs={{0,2},{1,3},{2,0},{3,1},{4,6},{5,7},{6,4},{7,5},{8,10},{9,11},{10,... | collective-permute-start | bytes 786440 | tf_op jit(solution)/shard_map/ppermute | solution.py:23
  79.3 20.7 %collective-permute-start.8 = (bf16[1,64,2048]{2,1,0:T(8,128)(2,1)S(1)}, bf16[1,64,2048]{2,1,0:T(8,128)(2,1)S(1)}, u32[]{:S(2)}, u32[]{:S(2)}) collective-permute-start(bf16[1,64,2048]{2,1,0:T(8,128)(2,1)S(1)} %get-tuple-element.47), channel_id=1, source_target_pairs={{0,3},{1,2},{2,1},{3,0},{4,7},{5,6},{6,5},{7,4},{8,11},{9,10},{10,... | collective-permute-start | bytes 786440 | tf_op jit(solution)/shard_map/ppermute | solution.py:23
  112.9 12.0 %collective-permute-start.22 = (bf16[1,64,2048]{2,1,0:T(8,128)(2,1)S(1)}, bf16[1,64,2048]{2,1,0:T(8,128)(2,1)S(1)}, u32[]{:S(2)}, u32[]{:S(2)}) collective-permute-start(bf16[1,64,2048]{2,1,0:T(8,128)(2,1)S(1)} %get-tuple-element.18), channel_id=1, source_target_pairs={{0,1},{1,0},{2,3},{3,2},{4,5},{5,4},{6,7},{7,6},{8,9},{9,8},{10,11... | collective-permute-start | bytes 786440 | tf_op jit(solution)/shard_map/ppermute | solution.py:23
  114.3 17.7 %collective-permute-start.21 = (bf16[1,64,2048]{2,1,0:T(8,128)(2,1)S(1)}, bf16[1,64,2048]{2,1,0:T(8,128)(2,1)S(1)}, u32[]{:S(2)}, u32[]{:S(2)}) collective-permute-start(bf16[1,64,2048]{2,1,0:T(8,128)(2,1)S(1)} %get-tuple-element.16), channel_id=1, source_target_pairs={{0,7},{1,6},{2,5},{3,4},{4,3},{5,2},{6,1},{7,0},{8,15},{9,14},{10,... | collective-permute-start | bytes 786440 | tf_op jit(solution)/shard_map/ppermute | solution.py:23
  118.9 17.4 %collective-permute-start.23 = (bf16[1,64,2048]{2,1,0:T(8,128)(2,1)S(1)}, bf16[1,64,2048]{2,1,0:T(8,128)(2,1)S(1)}, u32[]{:S(2)}, u32[]{:S(2)}) collective-permute-start(bf16[1,64,2048]{2,1,0:T(8,128)(2,1)S(1)} %get-tuple-element.19), channel_id=1, source_target_pairs={{0,2},{1,3},{2,0},{3,1},{4,6},{5,7},{6,4},{7,5},{8,10},{9,11},{10,... | collective-permute-start | bytes 786440 | tf_op jit(solution)/shard_map/ppermute | solution.py:23
  118.9 25.1 %collective-permute-start.24 = (bf16[1,64,2048]{2,1,0:T(8,128)(2,1)S(1)}, bf16[1,64,2048]{2,1,0:T(8,128)(2,1)S(1)}, u32[]{:S(2)}, u32[]{:S(2)}) collective-permute-start(bf16[1,64,2048]{2,1,0:T(8,128)(2,1)S(1)} %get-tuple-element.20), channel_id=1, source_target_pairs={{0,3},{1,2},{2,1},{3,0},{4,7},{5,6},{6,5},{7,4},{8,11},{9,10},{10,... | collective-permute-start | bytes 786440 | tf_op jit(solution)/shard_map/ppermute | solution.py:23
  124.9 19.3 %collective-permute-start.25 = (bf16[1,64,2048]{2,1,0:T(8,128)(2,1)S(1)}, bf16[1,64,2048]{2,1,0:T(8,128)(2,1)S(1)}, u32[]{:S(2)}, u32[]{:S(2)}) collective-permute-start(bf16[1,64,2048]{2,1,0:T(8,128)(2,1)S(1)} %get-tuple-element.21), channel_id=1, source_target_pairs={{0,6},{1,7},{2,4},{3,5},{4,2},{5,3},{6,0},{7,1},{8,14},{9,15},{10,... | collective-permute-start | bytes 786440 | tf_op jit(solution)/shard_map/ppermute | solution.py:23
  128.3 29.1 %collective-permute-start.26 = (bf16[1,64,2048]{2,1,0:T(8,128)(2,1)S(1)}, bf16[1,64,2048]{2,1,0:T(8,128)(2,1)S(1)}, u32[]{:S(2)}, u32[]{:S(2)}) collective-permute-start(bf16[1,64,2048]{2,1,0:T(8,128)(2,1)S(1)} %get-tuple-element.22), channel_id=1, source_target_pairs={{0,5},{1,4},{2,7},{3,6},{4,1},{5,0},{6,3},{7,2},{8,13},{9,12},{10,... | collective-permute-start | bytes 786440 | tf_op jit(solution)/shard_map/ppermute | solution.py:23
  132.1 27.7 %collective-permute-start.27 = (bf16[1,64,2048]{2,1,0:T(8,128)(2,1)S(1)}, bf16[1,64,2048]{2,1,0:T(8,128)(2,1)S(1)}, u32[]{:S(2)}, u32[]{:S(2)}) collective-permute-start(bf16[1,64,2048]{2,1,0:T(8,128)(2,1)S(1)} %get-tuple-element.23), channel_id=1, source_target_pairs={{0,4},{1,5},{2,6},{3,7},{4,0},{5,1},{6,2},{7,3},{8,12},{9,13},{10,... | collective-permute-start | bytes 786440 | tf_op jit(solution)/shard_map/ppermute | solution.py:23
  160.0 1.3 copy-start.4
  160.0 2.0 %copy-start.5 = (bf16[1,8,64,2048]{3,2,1,0:T(8,128)(2,1)}, bf16[1,8,64,2048]{3,2,1,0:T(8,128)(2,1)S(1)}, u32[]{:S(2)}) copy-start(bf16[1,8,64,2048]{3,2,1,0:T(8,128)(2,1)S(1)} %get-tuple-element.51) | copy-start | bytes 6291460

commit v10 on v8

--- a/solution.py
+++ b/solution.py
@@ -164,10 +164,14 @@
         else:
             far = swapped(mixed.astype(BF16), "rep", 2)
             far_mixed = far.astype(F32)
-        group = second * mixed + (1.0 - second) * far_mixed
-        group += taken(grad_new, start, length).astype(F32)
-        group -= taken(grad_old, start, length).astype(F32)
-        for offset in reversed(range(lowest, lowest + length)):
+        base = second * mixed + (
+            taken(grad_new, start, length).astype(F32) - taken(grad_old, start, length).astype(F32)
+        )
+        if turn < 2:
+            base = lax.optimization_barrier(base)
+        group = base + (1.0 - second) * far_mixed
+        offsets = range(lowest, lowest + length)
+        for offset in offsets if lowest == 0 else reversed(offsets):
             block = taken(group, (here ^ offset) % length, 1)[0].astype(BF16)
             blocks[offset] = swapped(block, "shard", offset) if offset else block
         new_tracker = lax.dynamic_update_slice_in_dim(new_tracker, group, start, axis=0)

time: 152 us -> 150 us (0.987)
  waiting for transfers between devices: 72.9 us -> 68.5 us
  starting transfers between devices: 32.8 us -> 34.4 us
    dynamic_update_slice x4 -> x2, other arithmetic: 10.5 us -> 3.99 us  [local(): lax.dynamic_update_slice_in_dim(new_tracker, group, start, axis=0)]
    ppermute x26, waiting for transfers between devices: 72.9 us -> 68.5 us  [swapped(): lax.ppermute(values, axis, [(i, i ^ offset) for i in range(lax.axis_size(...]
    convert_element_type x0 -> x2, other arithmetic: none -> 3.75 us  [local(): block = taken(group, (here ^ offset) % length, 1)[0].astype(BF16)]
    add x0 -> x1, other arithmetic: none -> 3.18 us  [local(): second * mixed]
    ppermute x26, starting transfers between devices: 32.8 us -> 34.4 us  [swapped(): lax.ppermute(values, axis, [(i, i ^ offset) for i in range(lax.axis_size(...]
  transfers between devices with their start and end apart: 26 -> 26, of which waited for: 11 -> 11; matrix products, arithmetic and copies ran while one was open for 18% -> 18% of each run, Pallas kernels for 8% -> 9%
where the time goes in v10:
time: 150 us
  waiting for transfers between devices  68.5 us (46%)
  starting transfers between devices  34.4 us (23%)
  other arithmetic  21.4 us (14%)
  Pallas kernels  12.8 us (9%)
  local copies, waits for them, and re-layouts  9.91 us (7%)
  between operations  2.85 us (2%)
    ppermute x26, waiting for transfers between devices, swapped(): lax.ppermute(values, axis, [(i, i ^ offset) for i in range(lax.axis_size(...  68.5 us
    ppermute x26, starting transfers between devices, swapped(): lax.ppermute(values, axis, [(i, i ^ offset) for i in range(lax.axis_size(...  34.4 us
    pallas_call x1, Pallas kernels, orthogonalize(): pl.pallas_call(body, grid=(each,), in_specs=[block] * count, out_specs=[b...  12.8 us
    convert_element_type x3, local copies, waits for them, and re-layouts, local(): rounded = own.astype(BF16)  6.13 us
    dynamic_update_slice x2, other arithmetic, local(): lax.dynamic_update_slice_in_dim(new_tracker, group, start, axis=0)  3.99 us
    convert_element_type x2, other arithmetic, local(): block = taken(group, (here ^ offset) % length, 1)[0].astype(BF16)  3.75 us
    convert_element_type x1, other arithmetic, local(): mixed_weight = (second * weight_own.astype(F32) + (1.0 - second) * weight...  3.65 us
    add x1, other arithmetic, local(): second * mixed  3.18 us
  transfers between devices with their start and end apart: 26, of which 11 were waited for; matrix products, arithmetic and copies ran while one was open for 18% of the time, Pallas kernels for 9%

profile of v10, /device:TPU:0, one launch (start us, length us, event | category | flops | bytes accessed | tf_op | source)
XLA Modules:
  0.0 149.8 jit_solution(16187644147894316663)
XLA Ops:
  0.7 2.1 %dynamic-slice_convert_fusion.9 = (bf16[1,1,64,2048]{3,2,1,0:T(8,128)(2,1)S(1)}, bf16[1,1,64,2048]{3,2,1,0:T(8,128)(2,1)}) fusion(f32[1,8,64,2048]{3,2,1,0:T(8,128)} %param.6, s32[]{:T(128)S(6)} %select_n.144, s32[]{:T(128)S(6)} %select_n.146), kind=kLoop, calls=%fused_computation.43 | loop fusion | bytes 1048584 | tf_op jit(solution)/shard_map/convert_element_type | solution.py:159
  2.8 0.5 collective-permute-start.15
  3.2 2.5 %collective-permute-start.16 = (bf16[1,1,64,2048]{3,2,1,0:T(8,128)(2,1)}, bf16[1,1,64,2048]{3,2,1,0:T(8,128)(2,1)}, u32[]{:S(2)}, u32[]{:S(2)}) collective-permute-start(bf16[1,1,64,2048]{3,2,1,0:T(8,128)(2,1)} %get-tuple-element.30), channel_id=1, source_target_pairs={{0,16},{8,24},{16,0},{24,8},{1,17},{9,25},{17,1},{25,9},{2,18},{10... | collective-permute-start | bytes 786440 | tf_op jit(solution)/shard_map/ppermute | solution.py:23
  6.0 0.3 collective-permute-start.12
  6.2 1.3 fusion.5
  7.6 2.7 %fusion.2 = bf16[4,1,64,2048]{3,2,1,0:T(8,128)(2,1)} fusion(f32[1,8,64,2048]{3,2,1,0:T(8,128)} %param.6, s32[]{:T(128)S(6)} %select_n.129), kind=kLoop, calls=%fused_computation.8 | loop fusion | bytes 2097156 | tf_op jit(solution)/shard_map/convert_element_type | solution.py:159
  10.4 0.6 constant_dynamic-slice_fusion
  12.9 0.5 collective-permute-start.1
  13.5 3.2 %subtract_add_fusion.1 = (f32[1,1,64,2048]{3,2,1,0:T(8,128)S(1)}, f32[1,1,64,2048]{3,2,1,0:T(8,128)S(1)}) fusion(bf16[1,1,64,2048]{3,2,1,0:T(8,128)(2,1)} %collective-permute-done.11, f32[1,8,64,2048]{3,2,1,0:T(8,128)} %param.6, s32[]{:T(128)S(6)} %select_n.144, bf16[1,8,64,2048]{3,2,1,0:T(8,128)(2,1)} %param.8, bf16[1,8,64,2048]{3,2,1,0:T(8,128)(2,1)} %param.7, ...), kind=kLoop, calls=%fused_computation.35 | loop fusion | flops 2359296 | bytes 3670036 | tf_op jit(solution)/shard_map/add | solution.py:167
  16.7 0.5 collective-permute-start.17
  17.2 1.5 collective-permute-done.12
  18.6 2.0 %fusion.4 = bf16[2,1,64,2048]{3,2,1,0:T(8,128)(2,1)S(1)} fusion(bf16[2,1,64,2048]{3,2,1,0:T(8,128)(2,1)S(1)} %collective-permute-done.7, f32[1,8,64,2048]{3,2,1,0:T(8,128)} %param.6, s32[]{:T(128)S(6)} %select_n.139, f32[]{:T(128)S(6)} %sub.89, f32[]{:T(128)} %bitcast.1), kind=kLoop, calls=%fused_computation.14 | loop fusion | flops 1310720 | bytes 2097164 | tf_op jit(solution)/shard_map/convert_element_type | solution.py:165
  20.7 1.8 %collective-permute-start.8 = (bf16[2,1,64,2048]{3,2,1,0:T(8,128)(2,1)S(1)}, bf16[2,1,64,2048]{3,2,1,0:T(8,128)(2,1)S(1)}, u32[]{:S(2)}, u32[]{:S(2)}) collective-permute-start(bf16[2,1,64,2048]{3,2,1,0:T(8,128)(2,1)S(1)} %fusion.4), channel_id=1, source_target_pairs={{0,16},{8,24},{16,0},{24,8},{1,17},{9,25},{17,1},{25,9},{2,18},{10... | collective-permute-start | bytes 1572872 | tf_op jit(solution)/shard_map/ppermute | solution.py:23
  22.5 0.5 reshape.435
  23.0 2.0 %convert_bitcast_fusion = (bf16[1,64,2048]{2,1,0:T(8,128)(2,1)S(1)}, f32[1,8,64,2048]{3,2,1,0:T(8,128)S(1)}) fusion(f32[1,1,64,2048]{3,2,1,0:T(8,128)S(1)} %get-tuple-element.28, bf16[1,1,64,2048]{3,2,1,0:T(8,128)(2,1)S(1)} %collective-permute-done.17, f32[]{:T(128)S(6)} %sub.98, bf16[1,1,64,2048]{3,2,1,0:T(8,128)(2,1)} %collective-permute-done.16, ...), kind=kLoop, calls=%fused_computation.74 | loop fusion | flops 1048576 | bytes 1835024 | tf_op jit(solution)/shard_map/convert_element_type | solution.py:175
  25.0 1.7 %convert_bitcast_fusion.1 = (bf16[1,64,2048]{2,1,0:T(8,128)(2,1)S(1)}, f32[1,8,64,2048]{3,2,1,0:T(8,128)S(1)}) fusion(f32[1,1,64,2048]{3,2,1,0:T(8,128)S(1)} %get-tuple-element.27, bf16[1,1,64,2048]{3,2,1,0:T(8,128)(2,1)S(1)} %collective-permute-done.13, f32[]{:T(128)S(6)} %sub.98, bf16[1,1,64,2048]{3,2,1,0:T(8,128)(2,1)} %collective-permute-done.12, ...), kind=kLoop, calls=%fused_computation.75 | loop fusion | flops 1048576 | bytes 1835024 | tf_op jit(solution)/shard_map/convert_element_type | solution.py:175
  26.8 3.7 %collective-permute-start.14 = (bf16[1,64,2048]{2,1,0:T(8,128)(2,1)S(1)}, bf16[1,64,2048]{2,1,0:T(8,128)(2,1)S(1)}, u32[]{:S(2)}, u32[]{:S(2)}) collective-permute-start(bf16[1,64,2048]{2,1,0:T(8,128)(2,1)S(1)} %get-tuple-element.37), channel_id=1, source_target_pairs={{0,6},{1,7},{2,4},{3,5},{4,2},{5,3},{6,0},{7,1},{8,14},{9,15},{10,... | collective-permute-start | bytes 786440 | tf_op jit(solution)/shard_map/ppermute | solution.py:23
  30.4 1.2 collective-permute-start.18
  31.6 1.0 fusion.1
  32.7 0.6 collective-permute-start.2
  33.3 1.8 %collective-permute-done.8 = bf16[2,1,64,2048]{3,2,1,0:T(8,128)(2,1)S(1)} collective-permute-done((bf16[2,1,64,2048]{3,2,1,0:T(8,128)(2,1)S(1)}, bf16[2,1,64,2048]{3,2,1,0:T(8,128)(2,1)S(1)}, u32[]{:S(2)}, u32[]{:S(2)}) %collective-permute-start.8) | collective-permute-done | bytes 524320 | tf_op jit(solution)/shard_map/ppermute | solution.py:23
  35.1 1.7 %bitcast_dynamic-update-slice_fusion.1 = (f32[1,8,64,2048]{3,2,1,0:T(8,128)S(1)}, bf16[2,1,64,2048]{3,2,1,0:T(8,128)(2,1)S(1)}) fusion(f32[1,8,64,2048]{3,2,1,0:T(8,128)S(1)} %get-tuple-element.38, s32[]{:T(128)S(6)} %select_n.139, bf16[2,1,64,2048]{3,2,1,0:T(8,128)(2,1)S(1)} %collective-permute-done.8, f32[]{:T(128)S(6)} %sub.91, ...), kind=kLoop, calls=%fused_computation.10 | loop fusion | flops 3407872 | bytes 4718612 | tf_op jit(solution)/shard_map/dynamic_update_slice | solution.py:177
  36.8 4.2 %collective-permute-start.10 = (bf16[1,64,2048]{2,1,0:T(8,128)(2,1)S(1)}, bf16[1,64,2048]{2,1,0:T(8,128)(2,1)S(1)}, u32[]{:S(2)}, u32[]{:S(2)}) collective-permute-start(bf16[1,64,2048]{2,1,0:T(8,128)(2,1)S(1)} %get-tuple-element.39), channel_id=1, source_target_pairs={{0,5},{1,4},{2,7},{3,6},{4,1},{5,0},{6,3},{7,2},{8,13},{9,12},{10,... | collective-permute-start | bytes 786440 | tf_op jit(solution)/shard_map/ppermute | solution.py:23
  41.1 0.3 collective-permute-start.9
  41.4 3.0 %add_convert_fusion.1 = bf16[8,1,64,2048]{3,2,1,0:T(8,128)(2,1)} fusion(bf16[8,1,64,2048]{3,2,1,0:T(8,128)(2,1)S(1)} %collective-permute-done, f32[]{:T(128)S(6)} %sub.89, f32[]{:T(128)} %bitcast.1, bf16[1,8,64,2048]{3,2,1,0:T(8,128)(2,1)S(1)} %copy-done.4), kind=kLoop, calls=%fused_computation.1 | loop fusion | flops 6291456 | bytes 6291464 | tf_op jit(solution)/shard_map/convert_element_type | solution.py:182
  44.4 13.3 %collective-permute-done.2 = bf16[4,1,64,2048]{3,2,1,0:T(8,128)(2,1)S(1)} collective-permute-done((bf16[4,1,64,2048]{3,2,1,0:T(8,128)(2,1)S(1)}, bf16[4,1,64,2048]{3,2,1,0:T(8,128)(2,1)S(1)}, u32[]{:S(2)}, u32[]{:S(2)}) %collective-permute-start.2) | collective-permute-done | bytes 1048608 | tf_op jit(solution)/shard_map/ppermute | solution.py:23
  57.7 1.6 %collective-permute-start.3 = (bf16[8,1,64,2048]{3,2,1,0:T(8,128)(2,1)}, bf16[8,1,64,2048]{3,2,1,0:T(8,128)(2,1)}, u32[]{:S(2)}, u32[]{:S(2)}) collective-permute-start(bf16[8,1,64,2048]{3,2,1,0:T(8,128)(2,1)} %add_convert_fusion.1), channel_id=1, source_target_pairs={{0,16},{8,24},{16,0},{24,8},{1,17},{9,25},{17,1},{25,9},{2,18},{10... | collective-permute-start | bytes 6291464 | tf_op jit(solution)/shard_map/ppermute | solution.py:23
  59.3 2.3 %bitcast_dynamic-update-slice_fusion = (f32[1,8,64,2048]{3,2,1,0:T(8,128)S(1)}, bf16[4,1,64,2048]{3,2,1,0:T(8,128)(2,1)S(1)}) fusion(f32[1,8,64,2048]{3,2,1,0:T(8,128)S(1)} %get-tuple-element.25, s32[]{:T(128)S(6)} %select_n.129, bf16[4,1,64,2048]{3,2,1,0:T(8,128)(2,1)S(1)} %collective-permute-done.2, f32[]{:T(128)S(6)} %sub.91, ...), kind=kLoop, calls=%fused_computation.3 | loop fusion | flops 6815744 | bytes 9437204 | tf_op jit(solution)/shard_map/dynamic_update_slice | solution.py:177
  61.7 1.6 %collective-permute-start.4 = (bf16[1,64,2048]{2,1,0:T(8,128)(2,1)S(1)}, bf16[1,64,2048]{2,1,0:T(8,128)(2,1)S(1)}, u32[]{:S(2)}, u32[]{:S(2)}) collective-permute-start(bf16[1,64,2048]{2,1,0:T(8,128)(2,1)S(1)} %get-tuple-element.33), channel_id=1, source_target_pairs={{0,1},{1,0},{2,3},{3,2},{4,5},{5,4},{6,7},{7,6},{8,9},{9,8},{10,11... | collective-permute-start | bytes 786440 | tf_op jit(solution)/shard_map/ppermute | solution.py:23
  63.3 3.2 %collective-permute-start.5 = (bf16[1,64,2048]{2,1,0:T(8,128)(2,1)S(1)}, bf16[1,64,2048]{2,1,0:T(8,128)(2,1)S(1)}, u32[]{:S(2)}, u32[]{:S(2)}) collective-permute-start(bf16[1,64,2048]{2,1,0:T(8,128)(2,1)S(1)} %get-tuple-element.32), channel_id=1, source_target_pairs={{0,2},{1,3},{2,0},{3,1},{4,6},{5,7},{6,4},{7,5},{8,10},{9,11},{10,... | collective-permute-start | bytes 786440 | tf_op jit(solution)/shard_map/ppermute | solution.py:23
  66.6 5.2 %collective-permute-done.10.refs_5_ = bf16[1,64,2048]{2,1,0:T(8,128)(2,1)S(1)} collective-permute-done((bf16[1,64,2048]{2,1,0:T(8,128)(2,1)S(1)}, bf16[1,64,2048]{2,1,0:T(8,128)(2,1)S(1)}, u32[]{:S(2)}, u32[]{:S(2)}) %collective-permute-start.10) | collective-permute-done | bytes 262176 | tf_op jit(solution)/shard_map/ppermute | solution.py:23
  71.7 4.0 %collective-permute-done.9.refs_4_ = bf16[1,64,2048]{2,1,0:T(8,128)(2,1)S(1)} collective-permute-done((bf16[1,64,2048]{2,1,0:T(8,128)(2,1)S(1)}, bf16[1,64,2048]{2,1,0:T(8,128)(2,1)S(1)}, u32[]{:S(2)}, u32[]{:S(2)}) %collective-permute-start.9) | collective-permute-done | bytes 262176 | tf_op jit(solution)/shard_map/ppermute | solution.py:23
  75.7 5.6 %collective-permute-done.5.refs_2_ = bf16[1,64,2048]{2,1,0:T(8,128)(2,1)S(1)} collective-permute-done((bf16[1,64,2048]{2,1,0:T(8,128)(2,1)S(1)}, bf16[1,64,2048]{2,1,0:T(8,128)(2,1)S(1)}, u32[]{:S(2)}, u32[]{:S(2)}) %collective-permute-start.5) | collective-permute-done | bytes 262176 | tf_op jit(solution)/shard_map/ppermute | solution.py:23
  81.4 6.4 %collective-permute-done.6.refs_3_ = bf16[1,64,2048]{2,1,0:T(8,128)(2,1)S(1)} collective-permute-done((bf16[1,64,2048]{2,1,0:T(8,128)(2,1)S(1)}, bf16[1,64,2048]{2,1,0:T(8,128)(2,1)S(1)}, u32[]{:S(2)}, u32[]{:S(2)}) %collective-permute-start.6) | collective-permute-done | bytes 262176 | tf_op jit(solution)/shard_map/ppermute | solution.py:23
  87.8 12.8 %orthogonalize.1 = (bf16[1,64,2048]{2,1,0:T(8,128)(2,1)S(1)}, bf16[1,64,2048]{2,1,0:T(8,128)(2,1)S(1)}, bf16[1,64,2048]{2,1,0:T(8,128)(2,1)S(1)}, bf16[1,64,2048...) custom-call(bf16[1,64,2048]{2,1,0:T(8,128)(2,1)S(1)} %get-tuple-elem, ...), custom_call_target="tpu_custom_call" | custom-call | flops 11005853696 | bytes 4194304 | tf_op jit(solution)/shard_map/orthogonalize/pallas_call | solution.py:102
  100.6 0.6 collective-permute-start.20
  101.2 3.4 %collective-permute-start.19 = (bf16[1,64,2048]{2,1,0:T(8,128)(2,1)S(1)}, bf16[1,64,2048]{2,1,0:T(8,128)(2,1)S(1)}, u32[]{:S(2)}, u32[]{:S(2)}) collective-permute-start(bf16[1,64,2048]{2,1,0:T(8,128)(2,1)S(1)} %get-tuple-element.14), channel_id=1, source_target_pairs={{0,7},{1,6},{2,5},{3,4},{4,3},{5,2},{6,1},{7,0},{8,15},{9,14},{10,... | collective-permute-start | bytes 786440 | tf_op jit(solution)/shard_map/ppermute | solution.py:23
  104.6 2.0 %collective-permute-start.22 = (bf16[1,64,2048]{2,1,0:T(8,128)(2,1)S(1)}, bf16[1,64,2048]{2,1,0:T(8,128)(2,1)S(1)}, u32[]{:S(2)}, u32[]{:S(2)}) collective-permute-start(bf16[1,64,2048]{2,1,0:T(8,128)(2,1)S(1)} %get-tuple-element.18), channel_id=1, source_target_pairs={{0,3},{1,2},{2,1},{3,0},{4,7},{5,6},{6,5},{7,4},{8,11},{9,10},{10,... | collective-permute-start | bytes 786440 | tf_op jit(solution)/shard_map/ppermute | solution.py:23
  106.6 7.9 %collective-permute-done.20 = bf16[1,64,2048]{2,1,0:T(8,128)(2,1)S(1)} collective-permute-done((bf16[1,64,2048]{2,1,0:T(8,128)(2,1)S(1)}, bf16[1,64,2048]{2,1,0:T(8,128)(2,1)S(1)}, u32[]{:S(2)}, u32[]{:S(2)}) %collective-permute-start.20) | collective-permute-done | bytes 262176 | tf_op jit(solution)/shard_map/ppermute | solution.py:23
  114.5 2.5 %collective-permute-start.23 = (bf16[1,64,2048]{2,1,0:T(8,128)(2,1)S(1)}, bf16[1,64,2048]{2,1,0:T(8,128)(2,1)S(1)}, u32[]{:S(2)}, u32[]{:S(2)}) collective-permute-start(bf16[1,64,2048]{2,1,0:T(8,128)(2,1)S(1)} %get-tuple-element.19), channel_id=1, source_target_pairs={{0,6},{1,7},{2,4},{3,5},{4,2},{5,3},{6,0},{7,1},{8,14},{9,15},{10,... | collective-permute-start | bytes 786440 | tf_op jit(solution)/shard_map/ppermute | solution.py:23
  117.0 0.2 reshape.433.clone
  117.3 3.6 %add_convert_fusion = bf16[8,1,64,2048]{3,2,1,0:T(8,128)(2,1)S(1)} fusion(bf16[8,1,64,2048]{3,2,1,0:T(8,128)(2,1)} %collective-permute-done.3, bf16[8,1,64,2048]{3,2,1,0:T(8,128)(2,1)} %add_convert_fusion.1, f32[]{:T(128)S(6)} %sub.91, f32[]{:T(128)} %bitcast), kind=kLoop, calls=%fused_computation | loop fusion | flops 6291456 | bytes 6291464 | tf_op jit(solution)/shard_map/convert_element_type | solution.py:187
  121.0 3.0 %collective-permute-start.25 = (bf16[1,64,2048]{2,1,0:T(8,128)(2,1)S(1)}, bf16[1,64,2048]{2,1,0:T(8,128)(2,1)S(1)}, u32[]{:S(2)}, u32[]{:S(2)}) collective-permute-start(bf16[1,64,2048]{2,1,0:T(8,128)(2,1)S(1)} %get-tuple-element.21), channel_id=1, source_target_pairs={{0,4},{1,5},{2,6},{3,7},{4,0},{5,1},{6,2},{7,3},{8,12},{9,13},{10,... | collective-permute-start | bytes 786440 | tf_op jit(solution)/shard_map/ppermute | solution.py:23
  124.4 7.0 %collective-permute-done.22 = bf16[1,64,2048]{2,1,0:T(8,128)(2,1)S(1)} collective-permute-done((bf16[1,64,2048]{2,1,0:T(8,128)(2,1)S(1)}, bf16[1,64,2048]{2,1,0:T(8,128)(2,1)S(1)}, u32[]{:S(2)}, u32[]{:S(2)}) %collective-permute-start.22) | collective-permute-done | bytes 262176 | tf_op jit(solution)/shard_map/ppermute | solution.py:23
  131.7 13.1 %collective-permute-done.24 = bf16[1,64,2048]{2,1,0:T(8,128)(2,1)S(1)} collective-permute-done((bf16[1,64,2048]{2,1,0:T(8,128)(2,1)S(1)}, bf16[1,64,2048]{2,1,0:T(8,128)(2,1)S(1)}, u32[]{:S(2)}, u32[]{:S(2)}) %collective-permute-start.24) | collective-permute-done | bytes 262176 | tf_op jit(solution)/shard_map/ppermute | solution.py:23
  145.0 2.6 %collective-permute-done.25 = bf16[1,64,2048]{2,1,0:T(8,128)(2,1)S(1)} collective-permute-done((bf16[1,64,2048]{2,1,0:T(8,128)(2,1)S(1)}, bf16[1,64,2048]{2,1,0:T(8,128)(2,1)S(1)}, u32[]{:S(2)}, u32[]{:S(2)}) %collective-permute-start.25) | collective-permute-done | bytes 262176 | tf_op jit(solution)/shard_map/ppermute | solution.py:23
  147.8 1.3 copy-done.2
  149.1 0.7 copy-done.3
  (49 shorter events, 1.7 us)
Async XLA Ops:
  0.6 9.7 %copy-start.7 = (s32[4,2]{0,1:T(2,128)S(1)}, s32[4,2]{0,1:T(2,128)}, u32[]{:S(2)}) copy-start(s32[4,2]{0,1:T(2,128)} %param.9) | copy-start | bytes 100
  0.7 12.8 %copy-start.4 = (bf16[1,8,64,2048]{3,2,1,0:T(8,128)(2,1)S(1)}, bf16[1,8,64,2048]{3,2,1,0:T(8,128)(2,1)}, u32[]{:S(2)}) copy-start(bf16[1,8,64,2048]{3,2,1,0:T(8,128)(2,1)} %param.5) | copy-start | bytes 6291460
  2.8 10.6 %collective-permute-start.15 = (bf16[1,1,64,2048]{3,2,1,0:T(8,128)(2,1)}, bf16[1,1,64,2048]{3,2,1,0:T(8,128)(2,1)}, u32[]{:S(2)}, u32[]{:S(2)}) collective-permute-start(bf16[1,1,64,2048]{3,2,1,0:T(8,128)(2,1)} %get-tuple-element.30), channel_id=1, source_target_pairs={{0,8},{8,0},{16,24},{24,16},{1,9},{9,1},{17,25},{25,17},{2,10},{10... | collective-permute-start | bytes 786440 | tf_op jit(solution)/shard_map/ppermute | solution.py:23
  3.2 13.4 %collective-permute-start.16 = (bf16[1,1,64,2048]{3,2,1,0:T(8,128)(2,1)}, bf16[1,1,64,2048]{3,2,1,0:T(8,128)(2,1)}, u32[]{:S(2)}, u32[]{:S(2)}) collective-permute-start(bf16[1,1,64,2048]{3,2,1,0:T(8,128)(2,1)} %get-tuple-element.30), channel_id=1, source_target_pairs={{0,16},{8,24},{16,0},{24,8},{1,17},{9,25},{17,1},{25,9},{2,18},{10... | collective-permute-start | bytes 786440 | tf_op jit(solution)/shard_map/ppermute | solution.py:23
  5.7 7.1 %collective-permute-start.11 = (bf16[1,1,64,2048]{3,2,1,0:T(8,128)(2,1)S(1)}, bf16[1,1,64,2048]{3,2,1,0:T(8,128)(2,1)}, u32[]{:S(2)}, u32[]{:S(2)}) collective-permute-start(bf16[1,1,64,2048]{3,2,1,0:T(8,128)(2,1)S(1)} %get-tuple-element.29), channel_id=1, source_target_pairs={{0,8},{8,0},{16,24},{24,16},{1,9},{9,1},{17,25},{25,17},{2,10},{10... | collective-permute-start | bytes 786440 | tf_op jit(solution)/shard_map/ppermute | solution.py:23
  6.0 12.7 %collective-permute-start.12 = (bf16[1,1,64,2048]{3,2,1,0:T(8,128)(2,1)S(1)}, bf16[1,1,64,2048]{3,2,1,0:T(8,128)(2,1)}, u32[]{:S(2)}, u32[]{:S(2)}) collective-permute-start(bf16[1,1,64,2048]{3,2,1,0:T(8,128)(2,1)S(1)} %get-tuple-element.29), channel_id=1, source_target_pairs={{0,16},{8,24},{16,0},{24,8},{1,17},{9,25},{17,1},{25,9},{2,18},{10... | collective-permute-start | bytes 786440 | tf_op jit(solution)/shard_map/ppermute | solution.py:23
  7.5 11.1 %collective-permute-start.7 = (bf16[2,1,64,2048]{3,2,1,0:T(8,128)(2,1)S(1)}, bf16[2,1,64,2048]{3,2,1,0:T(8,128)(2,1)S(1)}, u32[]{:S(2)}, u32[]{:S(2)}) collective-permute-start(bf16[2,1,64,2048]{3,2,1,0:T(8,128)(2,1)S(1)} %fusion.5), channel_id=1, source_target_pairs={{0,8},{8,0},{16,24},{24,16},{1,9},{9,1},{17,25},{25,17},{2,10},{10... | collective-permute-start | bytes 1572872 | tf_op jit(solution)/shard_map/ppermute | solution.py:23
  12.9 18.7 %collective-permute-start.1 = (bf16[4,1,64,2048]{3,2,1,0:T(8,128)(2,1)}, bf16[4,1,64,2048]{3,2,1,0:T(8,128)(2,1)S(1)}, u32[]{:S(2)}, u32[]{:S(2)}) collective-permute-start(bf16[4,1,64,2048]{3,2,1,0:T(8,128)(2,1)} %fusion.2), channel_id=1, source_target_pairs={{0,8},{8,0},{16,24},{24,16},{1,9},{9,1},{17,25},{25,17},{2,10},{10... | collective-permute-start | bytes 3145736 | tf_op jit(solution)/shard_map/ppermute | solution.py:23
  13.4 27.7 %collective-permute-start = (bf16[8,1,64,2048]{3,2,1,0:T(8,128)(2,1)S(1)}, bf16[8,1,64,2048]{3,2,1,0:T(8,128)(2,1)S(1)}, u32[]{:S(2)}, u32[]{:S(2)}) collective-permute-start(bf16[8,1,64,2048]{3,2,1,0:T(8,128)(2,1)S(1)} %bitcast.129), channel_id=1, source_target_pairs={{0,8},{8,0},{16,24},{24,16},{1,9},{9,1},{17,25},{25,17},{2,10},{10... | collective-permute-start | bytes 6291464 | tf_op jit(solution)/shard_map/ppermute | solution.py:23
  16.7 5.8 %collective-permute-start.17 = (bf16[1,1,64,2048]{3,2,1,0:T(8,128)(2,1)}, bf16[1,1,64,2048]{3,2,1,0:T(8,128)(2,1)S(1)}, u32[]{:S(2)}, u32[]{:S(2)}) collective-permute-start(bf16[1,1,64,2048]{3,2,1,0:T(8,128)(2,1)} %collective-permute-done.16), channel_id=1, source_target_pairs={{0,8},{8,0},{16,24},{24,16},{1,9},{9,1},{17,25},{25,17},{2,10},{10... | collective-permute-start | bytes 786440 | tf_op jit(solution)/shard_map/ppermute | solution.py:23
  18.6 6.4 %collective-permute-start.13 = (bf16[1,1,64,2048]{3,2,1,0:T(8,128)(2,1)}, bf16[1,1,64,2048]{3,2,1,0:T(8,128)(2,1)S(1)}, u32[]{:S(2)}, u32[]{:S(2)}) collective-permute-start(bf16[1,1,64,2048]{3,2,1,0:T(8,128)(2,1)} %collective-permute-done.12), channel_id=1, source_target_pairs={{0,8},{8,0},{16,24},{24,16},{1,9},{9,1},{17,25},{25,17},{2,10},{10... | collective-permute-start | bytes 786440 | tf_op jit(solution)/shard_map/ppermute | solution.py:23
  20.7 14.4 %collective-permute-start.8 = (bf16[2,1,64,2048]{3,2,1,0:T(8,128)(2,1)S(1)}, bf16[2,1,64,2048]{3,2,1,0:T(8,128)(2,1)S(1)}, u32[]{:S(2)}, u32[]{:S(2)}) collective-permute-start(bf16[2,1,64,2048]{3,2,1,0:T(8,128)(2,1)S(1)} %fusion.4), channel_id=1, source_target_pairs={{0,16},{8,24},{16,0},{24,8},{1,17},{9,25},{17,1},{25,9},{2,18},{10... | collective-permute-start | bytes 1572872 | tf_op jit(solution)/shard_map/ppermute | solution.py:23
  22.5 9.1 %copy-start = (f32[1,8,64,2048]{3,2,1,0:T(8,128)S(1)}, f32[1,8,64,2048]{3,2,1,0:T(8,128)}, u32[]{:S(2)}) copy-start(f32[1,8,64,2048]{3,2,1,0:T(8,128)} %param.6) | copy-start | bytes 12582916
  26.8 35.0 %collective-permute-start.14 = (bf16[1,64,2048]{2,1,0:T(8,128)(2,1)S(1)}, bf16[1,64,2048]{2,1,0:T(8,128)(2,1)S(1)}, u32[]{:S(2)}, u32[]{:S(2)}) collective-permute-start(bf16[1,64,2048]{2,1,0:T(8,128)(2,1)S(1)} %get-tuple-element.37), channel_id=1, source_target_pairs={{0,6},{1,7},{2,4},{3,5},{4,2},{5,3},{6,0},{7,1},{8,14},{9,15},{10,... | collective-permute-start | bytes 786440 | tf_op jit(solution)/shard_map/ppermute | solution.py:23
  30.4 4.7 %copy-start.5 = (bf16[1,8,64,2048]{3,2,1,0:T(8,128)(2,1)S(1)}, bf16[1,8,64,2048]{3,2,1,0:T(8,128)(2,1)}, u32[]{:S(2)}) copy-start(bf16[1,8,64,2048]{3,2,1,0:T(8,128)(2,1)} %param.8) | copy-start | bytes 6291460
  30.4 4.7 %copy-start.6 = (bf16[1,8,64,2048]{3,2,1,0:T(8,128)(2,1)S(1)}, bf16[1,8,64,2048]{3,2,1,0:T(8,128)(2,1)}, u32[]{:S(2)}) copy-start(bf16[1,8,64,2048]{3,2,1,0:T(8,128)(2,1)} %param.7) | copy-start | bytes 6291460
  30.4 32.9 %collective-permute-start.18 = (bf16[1,64,2048]{2,1,0:T(8,128)(2,1)S(1)}, bf16[1,64,2048]{2,1,0:T(8,128)(2,1)S(1)}, u32[]{:S(2)}, u32[]{:S(2)}) collective-permute-start(bf16[1,64,2048]{2,1,0:T(8,128)(2,1)S(1)} %get-tuple-element.35), channel_id=1, source_target_pairs={{0,7},{1,6},{2,5},{3,4},{4,3},{5,2},{6,1},{7,0},{8,15},{9,14},{10,... | collective-permute-start | bytes 786440 | tf_op jit(solution)/shard_map/ppermute | solution.py:23
  32.7 25.1 %collective-permute-start.2 = (bf16[4,1,64,2048]{3,2,1,0:T(8,128)(2,1)S(1)}, bf16[4,1,64,2048]{3,2,1,0:T(8,128)(2,1)S(1)}, u32[]{:S(2)}, u32[]{:S(2)}) collective-permute-start(bf16[4,1,64,2048]{3,2,1,0:T(8,128)(2,1)S(1)} %fusion.1), channel_id=1, source_target_pairs={{0,16},{8,24},{16,0},{24,8},{1,17},{9,25},{17,1},{25,9},{2,18},{10... | collective-permute-start | bytes 3145736 | tf_op jit(solution)/shard_map/ppermute | solution.py:23
  36.8 34.9 %collective-permute-start.10 = (bf16[1,64,2048]{2,1,0:T(8,128)(2,1)S(1)}, bf16[1,64,2048]{2,1,0:T(8,128)(2,1)S(1)}, u32[]{:S(2)}, u32[]{:S(2)}) collective-permute-start(bf16[1,64,2048]{2,1,0:T(8,128)(2,1)S(1)} %get-tuple-element.39), channel_id=1, source_target_pairs={{0,5},{1,4},{2,7},{3,6},{4,1},{5,0},{6,3},{7,2},{8,13},{9,12},{10,... | collective-permute-start | bytes 786440 | tf_op jit(solution)/shard_map/ppermute | solution.py:23
  41.1 34.7 %collective-permute-start.9 = (bf16[1,64,2048]{2,1,0:T(8,128)(2,1)S(1)}, bf16[1,64,2048]{2,1,0:T(8,128)(2,1)S(1)}, u32[]{:S(2)}, u32[]{:S(2)}) collective-permute-start(bf16[1,64,2048]{2,1,0:T(8,128)(2,1)S(1)} %get-tuple-element.40), channel_id=1, source_target_pairs={{0,4},{1,5},{2,6},{3,7},{4,0},{5,1},{6,2},{7,3},{8,12},{9,13},{10,... | collective-permute-start | bytes 786440 | tf_op jit(solution)/shard_map/ppermute | solution.py:23
  57.7 59.5 %collective-permute-start.3 = (bf16[8,1,64,2048]{3,2,1,0:T(8,128)(2,1)}, bf16[8,1,64,2048]{3,2,1,0:T(8,128)(2,1)}, u32[]{:S(2)}, u32[]{:S(2)}) collective-permute-start(bf16[8,1,64,2048]{3,2,1,0:T(8,128)(2,1)} %add_convert_fusion.1), channel_id=1, source_target_pairs={{0,16},{8,24},{16,0},{24,8},{1,17},{9,25},{17,1},{25,9},{2,18},{10... | collective-permute-start | bytes 6291464 | tf_op jit(solution)/shard_map/ppermute | solution.py:23
  61.6 26.2 %copy-start.1 = (f32[1,8,64,2048]{3,2,1,0:T(8,128)}, f32[1,8,64,2048]{3,2,1,0:T(8,128)S(1)}, u32[]{:S(2)}) copy-start(f32[1,8,64,2048]{3,2,1,0:T(8,128)S(1)} %get-tuple-element.23) | copy-start | bytes 12582916
  61.7 14.0 %collective-permute-start.4 = (bf16[1,64,2048]{2,1,0:T(8,128)(2,1)S(1)}, bf16[1,64,2048]{2,1,0:T(8,128)(2,1)S(1)}, u32[]{:S(2)}, u32[]{:S(2)}) collective-permute-start(bf16[1,64,2048]{2,1,0:T(8,128)(2,1)S(1)} %get-tuple-element.33), channel_id=1, source_target_pairs={{0,1},{1,0},{2,3},{3,2},{4,5},{5,4},{6,7},{7,6},{8,9},{9,8},{10,11... | collective-permute-start | bytes 786440 | tf_op jit(solution)/shard_map/ppermute | solution.py:23
  63.3 18.0 %collective-permute-start.5 = (bf16[1,64,2048]{2,1,0:T(8,128)(2,1)S(1)}, bf16[1,64,2048]{2,1,0:T(8,128)(2,1)S(1)}, u32[]{:S(2)}, u32[]{:S(2)}) collective-permute-start(bf16[1,64,2048]{2,1,0:T(8,128)(2,1)S(1)} %get-tuple-element.32), channel_id=1, source_target_pairs={{0,2},{1,3},{2,0},{3,1},{4,6},{5,7},{6,4},{7,5},{8,10},{9,11},{10,... | collective-permute-start | bytes 786440 | tf_op jit(solution)/shard_map/ppermute | solution.py:23
  71.7 16.1 %collective-permute-start.6 = (bf16[1,64,2048]{2,1,0:T(8,128)(2,1)S(1)}, bf16[1,64,2048]{2,1,0:T(8,128)(2,1)S(1)}, u32[]{:S(2)}, u32[]{:S(2)}) collective-permute-start(bf16[1,64,2048]{2,1,0:T(8,128)(2,1)S(1)} %get-tuple-element.31), channel_id=1, source_target_pairs={{0,3},{1,2},{2,1},{3,0},{4,7},{5,6},{6,5},{7,4},{8,11},{9,10},{10,... | collective-permute-start | bytes 786440 | tf_op jit(solution)/shard_map/ppermute | solution.py:23
  100.6 13.9 %collective-permute-start.20 = (bf16[1,64,2048]{2,1,0:T(8,128)(2,1)S(1)}, bf16[1,64,2048]{2,1,0:T(8,128)(2,1)S(1)}, u32[]{:S(2)}, u32[]{:S(2)}) collective-permute-start(bf16[1,64,2048]{2,1,0:T(8,128)(2,1)S(1)} %get-tuple-element.16), channel_id=1, source_target_pairs={{0,1},{1,0},{2,3},{3,2},{4,5},{5,4},{6,7},{7,6},{8,9},{9,8},{10,11... | collective-permute-start | bytes 786440 | tf_op jit(solution)/shard_map/ppermute | solution.py:23
  101.2 19.8 %collective-permute-start.19 = (bf16[1,64,2048]{2,1,0:T(8,128)(2,1)S(1)}, bf16[1,64,2048]{2,1,0:T(8,128)(2,1)S(1)}, u32[]{:S(2)}, u32[]{:S(2)}) collective-permute-start(bf16[1,64,2048]{2,1,0:T(8,128)(2,1)S(1)} %get-tuple-element.14), channel_id=1, source_target_pairs={{0,7},{1,6},{2,5},{3,4},{4,3},{5,2},{6,1},{7,0},{8,15},{9,14},{10,... | collective-permute-start | bytes 786440 | tf_op jit(solution)/shard_map/ppermute | solution.py:23
  104.6 19.7 %collective-permute-start.21 = (bf16[1,64,2048]{2,1,0:T(8,128)(2,1)S(1)}, bf16[1,64,2048]{2,1,0:T(8,128)(2,1)S(1)}, u32[]{:S(2)}, u32[]{:S(2)}) collective-permute-start(bf16[1,64,2048]{2,1,0:T(8,128)(2,1)S(1)} %get-tuple-element.17), channel_id=1, source_target_pairs={{0,2},{1,3},{2,0},{3,1},{4,6},{5,7},{6,4},{7,5},{8,10},{9,11},{10,... | collective-permute-start | bytes 786440 | tf_op jit(solution)/shard_map/ppermute | solution.py:23
  104.6 26.8 %collective-permute-start.22 = (bf16[1,64,2048]{2,1,0:T(8,128)(2,1)S(1)}, bf16[1,64,2048]{2,1,0:T(8,128)(2,1)S(1)}, u32[]{:S(2)}, u32[]{:S(2)}) collective-permute-start(bf16[1,64,2048]{2,1,0:T(8,128)(2,1)S(1)} %get-tuple-element.18), channel_id=1, source_target_pairs={{0,3},{1,2},{2,1},{3,0},{4,7},{5,6},{6,5},{7,4},{8,11},{9,10},{10,... | collective-permute-start | bytes 786440 | tf_op jit(solution)/shard_map/ppermute | solution.py:23
  114.5 17.1 %collective-permute-start.23 = (bf16[1,64,2048]{2,1,0:T(8,128)(2,1)S(1)}, bf16[1,64,2048]{2,1,0:T(8,128)(2,1)S(1)}, u32[]{:S(2)}, u32[]{:S(2)}) collective-permute-start(bf16[1,64,2048]{2,1,0:T(8,128)(2,1)S(1)} %get-tuple-element.19), channel_id=1, source_target_pairs={{0,6},{1,7},{2,4},{3,5},{4,2},{5,3},{6,0},{7,1},{8,14},{9,15},{10,... | collective-permute-start | bytes 786440 | tf_op jit(solution)/shard_map/ppermute | solution.py:23
  117.3 27.6 %collective-permute-start.24 = (bf16[1,64,2048]{2,1,0:T(8,128)(2,1)S(1)}, bf16[1,64,2048]{2,1,0:T(8,128)(2,1)S(1)}, u32[]{:S(2)}, u32[]{:S(2)}) collective-permute-start(bf16[1,64,2048]{2,1,0:T(8,128)(2,1)S(1)} %get-tuple-element.20), channel_id=1, source_target_pairs={{0,5},{1,4},{2,7},{3,6},{4,1},{5,0},{6,3},{7,2},{8,13},{9,12},{10,... | collective-permute-start | bytes 786440 | tf_op jit(solution)/shard_map/ppermute | solution.py:23
  121.0 26.5 %collective-permute-start.25 = (bf16[1,64,2048]{2,1,0:T(8,128)(2,1)S(1)}, bf16[1,64,2048]{2,1,0:T(8,128)(2,1)S(1)}, u32[]{:S(2)}, u32[]{:S(2)}) collective-permute-start(bf16[1,64,2048]{2,1,0:T(8,128)(2,1)S(1)} %get-tuple-element.21), channel_id=1, source_target_pairs={{0,4},{1,5},{2,6},{3,7},{4,0},{5,1},{6,2},{7,3},{8,12},{9,13},{10,... | collective-permute-start | bytes 786440 | tf_op jit(solution)/shard_map/ppermute | solution.py:23
  147.7 1.3 copy-start.2
  147.8 2.0 %copy-start.3 = (bf16[1,8,64,2048]{3,2,1,0:T(8,128)(2,1)}, bf16[1,8,64,2048]{3,2,1,0:T(8,128)(2,1)S(1)}, u32[]{:S(2)}) copy-start(bf16[1,8,64,2048]{3,2,1,0:T(8,128)(2,1)S(1)} %get-tuple-element.41) | copy-start | bytes 6291460

commit v11 on v10

--- a/solution.py
+++ b/solution.py
@@ -187,10 +187,13 @@
     ).astype(BF16)
 
     scale = 0.2 * math.sqrt(max(shards * rows, columns))
-    updates = orthogonalize(blocks, scale)
+    half = shards // 2
+    rows_order = [0] + list(reversed(range(1, half))) + list(range(half, shards))
+    updates = [None] * shards
+    for offset, block in zip(rows_order, orthogonalize([blocks[k] for k in rows_order], scale)):
+        updates[offset] = block
     update = jnp.zeros(shape, BF16)
     new_weight = jnp.zeros(shape, BF16)
-    half = shards // 2
     order = list(range(1, half)) + list(reversed(range(half, shards))) + [0]
     received = [
         swapped(block, "shard", offset) if offset else block for offset, block in enumerate(updates)

time: 150 us -> 151 us (level)
  starting transfers between devices: 34.4 us -> 37.1 us
  waiting for transfers between devices: 68.5 us -> 66.1 us
    ppermute x26, starting transfers between devices: 34.4 us -> 37.1 us  [swapped(): lax.ppermute(values, axis, [(i, i ^ offset) for i in range(lax.axis_size(...]
    ppermute x26, waiting for transfers between devices: 68.5 us -> 66.1 us  [swapped(): lax.ppermute(values, axis, [(i, i ^ offset) for i in range(lax.axis_size(...]
where the time goes in v11:
time: 151 us; the launch traced here: 150 us
  waiting for transfers between devices  66.1 us (44%)
  starting transfers between devices  37.1 us (25%)
  other arithmetic  21.4 us (14%)
  Pallas kernels  12.8 us (8%)
  local copies, waits for them, and re-layouts  9.91 us (7%)
  between operations  2.85 us (2%)
    ppermute x26, waiting for transfers between devices, swapped(): lax.ppermute(values, axis, [(i, i ^ offset) for i in range(lax.axis_size(...  66.1 us
    ppermute x26, starting transfers between devices, swapped(): lax.ppermute(values, axis, [(i, i ^ offset) for i in range(lax.axis_size(...  37.1 us
    pallas_call x1, Pallas kernels, orthogonalize(): pl.pallas_call(body, grid=(each,), in_specs=[block] * count, out_specs=[b...  12.8 us
    convert_element_type x3, local copies, waits for them, and re-layouts, local(): rounded = own.astype(BF16)  6.13 us
    dynamic_update_slice x2, other arithmetic, local(): lax.dynamic_update_slice_in_dim(new_tracker, group, start, axis=0)  3.99 us
    convert_element_type x2, other arithmetic, local(): block = taken(group, (here ^ offset) % length, 1)[0].astype(BF16)  3.75 us
    convert_element_type x1, other arithmetic, local(): mixed_weight = (second * weight_own.astype(F32) + (1.0 - second) * weight...  3.65 us
    add x1, other arithmetic, local(): second * mixed  3.18 us
  transfers between devices with their start and end apart: 26, of which 11 were waited for; matrix products, arithmetic and copies ran while one was open for 18% of the time, Pallas kernels for 9%

profile of v11, /device:TPU:0, one launch (start us, length us, event | category | flops | bytes accessed | tf_op | source)
XLA Modules:
  0.0 150.1 jit_solution(2871626394626104619)
XLA Ops:
  0.7 2.1 %dynamic-slice_convert_fusion.9 = (bf16[1,1,64,2048]{3,2,1,0:T(8,128)(2,1)S(1)}, bf16[1,1,64,2048]{3,2,1,0:T(8,128)(2,1)}) fusion(f32[1,8,64,2048]{3,2,1,0:T(8,128)} %param.6, s32[]{:T(128)S(6)} %select_n.144, s32[]{:T(128)S(6)} %select_n.146), kind=kLoop, calls=%fused_computation.43 | loop fusion | bytes 1048584 | tf_op jit(solution)/shard_map/convert_element_type | solution.py:159
  2.8 0.5 collective-permute-start.15
  3.2 2.5 %collective-permute-start.16 = (bf16[1,1,64,2048]{3,2,1,0:T(8,128)(2,1)}, bf16[1,1,64,2048]{3,2,1,0:T(8,128)(2,1)}, u32[]{:S(2)}, u32[]{:S(2)}) collective-permute-start(bf16[1,1,64,2048]{3,2,1,0:T(8,128)(2,1)} %get-tuple-element.30), channel_id=1, source_target_pairs={{0,16},{8,24},{16,0},{24,8},{1,17},{9,25},{17,1},{25,9},{2,18},{10... | collective-permute-start | bytes 786440 | tf_op jit(solution)/shard_map/ppermute | solution.py:23
  6.0 0.3 collective-permute-start.12
  6.2 1.3 fusion.5
  7.6 2.7 %fusion.2 = bf16[4,1,64,2048]{3,2,1,0:T(8,128)(2,1)} fusion(f32[1,8,64,2048]{3,2,1,0:T(8,128)} %param.6, s32[]{:T(128)S(6)} %select_n.129), kind=kLoop, calls=%fused_computation.8 | loop fusion | bytes 2097156 | tf_op jit(solution)/shard_map/convert_element_type | solution.py:159
  10.4 0.6 constant_dynamic-slice_fusion
  12.9 0.5 collective-permute-start.1
  13.5 3.2 %subtract_add_fusion.1 = (f32[1,1,64,2048]{3,2,1,0:T(8,128)S(1)}, f32[1,1,64,2048]{3,2,1,0:T(8,128)S(1)}) fusion(bf16[1,1,64,2048]{3,2,1,0:T(8,128)(2,1)} %collective-permute-done.11, f32[1,8,64,2048]{3,2,1,0:T(8,128)} %param.6, s32[]{:T(128)S(6)} %select_n.144, bf16[1,8,64,2048]{3,2,1,0:T(8,128)(2,1)} %param.8, bf16[1,8,64,2048]{3,2,1,0:T(8,128)(2,1)} %param.7, ...), kind=kLoop, calls=%fused_computation.35 | loop fusion | flops 2359296 | bytes 3670036 | tf_op jit(solution)/shard_map/add | solution.py:167
  16.7 0.5 collective-permute-start.17
  17.2 1.5 collective-permute-done.12
  18.6 2.0 %fusion.4 = bf16[2,1,64,2048]{3,2,1,0:T(8,128)(2,1)S(1)} fusion(bf16[2,1,64,2048]{3,2,1,0:T(8,128)(2,1)S(1)} %collective-permute-done.7, f32[1,8,64,2048]{3,2,1,0:T(8,128)} %param.6, s32[]{:T(128)S(6)} %select_n.139, f32[]{:T(128)S(6)} %sub.89, f32[]{:T(128)} %bitcast.1), kind=kLoop, calls=%fused_computation.14 | loop fusion | flops 1310720 | bytes 2097164 | tf_op jit(solution)/shard_map/convert_element_type | solution.py:165
  20.7 1.8 %collective-permute-start.8 = (bf16[2,1,64,2048]{3,2,1,0:T(8,128)(2,1)S(1)}, bf16[2,1,64,2048]{3,2,1,0:T(8,128)(2,1)S(1)}, u32[]{:S(2)}, u32[]{:S(2)}) collective-permute-start(bf16[2,1,64,2048]{3,2,1,0:T(8,128)(2,1)S(1)} %fusion.4), channel_id=1, source_target_pairs={{0,16},{8,24},{16,0},{24,8},{1,17},{9,25},{17,1},{25,9},{2,18},{10... | collective-permute-start | bytes 1572872 | tf_op jit(solution)/shard_map/ppermute | solution.py:23
  22.5 0.5 reshape.435
  23.0 2.0 %convert_bitcast_fusion = (bf16[1,64,2048]{2,1,0:T(8,128)(2,1)S(1)}, f32[1,8,64,2048]{3,2,1,0:T(8,128)S(1)}) fusion(f32[1,1,64,2048]{3,2,1,0:T(8,128)S(1)} %get-tuple-element.28, bf16[1,1,64,2048]{3,2,1,0:T(8,128)(2,1)S(1)} %collective-permute-done.17, f32[]{:T(128)S(6)} %sub.98, bf16[1,1,64,2048]{3,2,1,0:T(8,128)(2,1)} %collective-permute-done.16, ...), kind=kLoop, calls=%fused_computation.74 | loop fusion | flops 1048576 | bytes 1835024 | tf_op jit(solution)/shard_map/convert_element_type | solution.py:175
  25.0 1.7 %convert_bitcast_fusion.1 = (bf16[1,64,2048]{2,1,0:T(8,128)(2,1)S(1)}, f32[1,8,64,2048]{3,2,1,0:T(8,128)S(1)}) fusion(f32[1,1,64,2048]{3,2,1,0:T(8,128)S(1)} %get-tuple-element.27, bf16[1,1,64,2048]{3,2,1,0:T(8,128)(2,1)S(1)} %collective-permute-done.13, f32[]{:T(128)S(6)} %sub.98, bf16[1,1,64,2048]{3,2,1,0:T(8,128)(2,1)} %collective-permute-done.12, ...), kind=kLoop, calls=%fused_computation.75 | loop fusion | flops 1048576 | bytes 1835024 | tf_op jit(solution)/shard_map/convert_element_type | solution.py:175
  26.8 3.7 %collective-permute-start.14 = (bf16[1,64,2048]{2,1,0:T(8,128)(2,1)S(1)}, bf16[1,64,2048]{2,1,0:T(8,128)(2,1)S(1)}, u32[]{:S(2)}, u32[]{:S(2)}) collective-permute-start(bf16[1,64,2048]{2,1,0:T(8,128)(2,1)S(1)} %get-tuple-element.37), channel_id=1, source_target_pairs={{0,6},{1,7},{2,4},{3,5},{4,2},{5,3},{6,0},{7,1},{8,14},{9,15},{10,... | collective-permute-start | bytes 786440 | tf_op jit(solution)/shard_map/ppermute | solution.py:23
  30.4 1.2 collective-permute-start.18
  31.6 1.0 fusion.1
  32.7 0.6 collective-permute-start.2
  33.3 1.8 %collective-permute-done.8 = bf16[2,1,64,2048]{3,2,1,0:T(8,128)(2,1)S(1)} collective-permute-done((bf16[2,1,64,2048]{3,2,1,0:T(8,128)(2,1)S(1)}, bf16[2,1,64,2048]{3,2,1,0:T(8,128)(2,1)S(1)}, u32[]{:S(2)}, u32[]{:S(2)}) %collective-permute-start.8) | collective-permute-done | bytes 524320 | tf_op jit(solution)/shard_map/ppermute | solution.py:23
  35.1 1.7 %bitcast_dynamic-update-slice_fusion.1 = (f32[1,8,64,2048]{3,2,1,0:T(8,128)S(1)}, bf16[2,1,64,2048]{3,2,1,0:T(8,128)(2,1)S(1)}) fusion(f32[1,8,64,2048]{3,2,1,0:T(8,128)S(1)} %get-tuple-element.38, s32[]{:T(128)S(6)} %select_n.139, bf16[2,1,64,2048]{3,2,1,0:T(8,128)(2,1)S(1)} %collective-permute-done.8, f32[]{:T(128)S(6)} %sub.91, ...), kind=kLoop, calls=%fused_computation.10 | loop fusion | flops 3407872 | bytes 4718612 | tf_op jit(solution)/shard_map/dynamic_update_slice | solution.py:177
  36.8 4.2 %collective-permute-start.10 = (bf16[1,64,2048]{2,1,0:T(8,128)(2,1)S(1)}, bf16[1,64,2048]{2,1,0:T(8,128)(2,1)S(1)}, u32[]{:S(2)}, u32[]{:S(2)}) collective-permute-start(bf16[1,64,2048]{2,1,0:T(8,128)(2,1)S(1)} %get-tuple-element.39), channel_id=1, source_target_pairs={{0,5},{1,4},{2,7},{3,6},{4,1},{5,0},{6,3},{7,2},{8,13},{9,12},{10,... | collective-permute-start | bytes 786440 | tf_op jit(solution)/shard_map/ppermute | solution.py:23
  41.1 0.3 collective-permute-start.9
  41.4 3.0 %add_convert_fusion.1 = bf16[8,1,64,2048]{3,2,1,0:T(8,128)(2,1)} fusion(bf16[8,1,64,2048]{3,2,1,0:T(8,128)(2,1)S(1)} %collective-permute-done, f32[]{:T(128)S(6)} %sub.89, f32[]{:T(128)} %bitcast.1, bf16[1,8,64,2048]{3,2,1,0:T(8,128)(2,1)S(1)} %copy-done.4), kind=kLoop, calls=%fused_computation.1 | loop fusion | flops 6291456 | bytes 6291464 | tf_op jit(solution)/shard_map/convert_element_type | solution.py:182
  44.4 13.3 %collective-permute-done.2 = bf16[4,1,64,2048]{3,2,1,0:T(8,128)(2,1)S(1)} collective-permute-done((bf16[4,1,64,2048]{3,2,1,0:T(8,128)(2,1)S(1)}, bf16[4,1,64,2048]{3,2,1,0:T(8,128)(2,1)S(1)}, u32[]{:S(2)}, u32[]{:S(2)}) %collective-permute-start.2) | collective-permute-done | bytes 1048608 | tf_op jit(solution)/shard_map/ppermute | solution.py:23
  57.7 1.6 %collective-permute-start.3 = (bf16[8,1,64,2048]{3,2,1,0:T(8,128)(2,1)}, bf16[8,1,64,2048]{3,2,1,0:T(8,128)(2,1)}, u32[]{:S(2)}, u32[]{:S(2)}) collective-permute-start(bf16[8,1,64,2048]{3,2,1,0:T(8,128)(2,1)} %add_convert_fusion.1), channel_id=1, source_target_pairs={{0,16},{8,24},{16,0},{24,8},{1,17},{9,25},{17,1},{25,9},{2,18},{10... | collective-permute-start | bytes 6291464 | tf_op jit(solution)/shard_map/ppermute | solution.py:23
  59.3 2.3 %bitcast_dynamic-update-slice_fusion = (f32[1,8,64,2048]{3,2,1,0:T(8,128)S(1)}, bf16[4,1,64,2048]{3,2,1,0:T(8,128)(2,1)S(1)}) fusion(f32[1,8,64,2048]{3,2,1,0:T(8,128)S(1)} %get-tuple-element.25, s32[]{:T(128)S(6)} %select_n.129, bf16[4,1,64,2048]{3,2,1,0:T(8,128)(2,1)S(1)} %collective-permute-done.2, f32[]{:T(128)S(6)} %sub.91, ...), kind=kLoop, calls=%fused_computation.3 | loop fusion | flops 6815744 | bytes 9437204 | tf_op jit(solution)/shard_map/dynamic_update_slice | solution.py:177
  61.7 2.6 %collective-permute-start.4 = (bf16[1,64,2048]{2,1,0:T(8,128)(2,1)S(1)}, bf16[1,64,2048]{2,1,0:T(8,128)(2,1)S(1)}, u32[]{:S(2)}, u32[]{:S(2)}) collective-permute-start(bf16[1,64,2048]{2,1,0:T(8,128)(2,1)S(1)} %get-tuple-element.33), channel_id=1, source_target_pairs={{0,3},{1,2},{2,1},{3,0},{4,7},{5,6},{6,5},{7,4},{8,11},{9,10},{10,... | collective-permute-start | bytes 786440 | tf_op jit(solution)/shard_map/ppermute | solution.py:23
  64.3 2.4 %collective-permute-start.5 = (bf16[1,64,2048]{2,1,0:T(8,128)(2,1)S(1)}, bf16[1,64,2048]{2,1,0:T(8,128)(2,1)S(1)}, u32[]{:S(2)}, u32[]{:S(2)}) collective-permute-start(bf16[1,64,2048]{2,1,0:T(8,128)(2,1)S(1)} %get-tuple-element.32), channel_id=1, source_target_pairs={{0,2},{1,3},{2,0},{3,1},{4,6},{5,7},{6,4},{7,5},{8,10},{9,11},{10,... | collective-permute-start | bytes 786440 | tf_op jit(solution)/shard_map/ppermute | solution.py:23
  66.7 5.0 %collective-permute-done.10.refs_5_ = bf16[1,64,2048]{2,1,0:T(8,128)(2,1)S(1)} collective-permute-done((bf16[1,64,2048]{2,1,0:T(8,128)(2,1)S(1)}, bf16[1,64,2048]{2,1,0:T(8,128)(2,1)S(1)}, u32[]{:S(2)}, u32[]{:S(2)}) %collective-permute-start.10) | collective-permute-done | bytes 262176 | tf_op jit(solution)/shard_map/ppermute | solution.py:23
  71.7 0.5 collective-permute-start.6
  72.2 3.5 %collective-permute-done.9.refs_4_ = bf16[1,64,2048]{2,1,0:T(8,128)(2,1)S(1)} collective-permute-done((bf16[1,64,2048]{2,1,0:T(8,128)(2,1)S(1)}, bf16[1,64,2048]{2,1,0:T(8,128)(2,1)S(1)}, u32[]{:S(2)}, u32[]{:S(2)}) %collective-permute-start.9) | collective-permute-done | bytes 262176 | tf_op jit(solution)/shard_map/ppermute | solution.py:23
  75.7 6.7 %collective-permute-done.4.refs_1_ = bf16[1,64,2048]{2,1,0:T(8,128)(2,1)S(1)} collective-permute-done((bf16[1,64,2048]{2,1,0:T(8,128)(2,1)S(1)}, bf16[1,64,2048]{2,1,0:T(8,128)(2,1)S(1)}, u32[]{:S(2)}, u32[]{:S(2)}) %collective-permute-start.4) | collective-permute-done | bytes 262176 | tf_op jit(solution)/shard_map/ppermute | solution.py:23
  82.4 4.4 %collective-permute-done.5.refs_2_ = bf16[1,64,2048]{2,1,0:T(8,128)(2,1)S(1)} collective-permute-done((bf16[1,64,2048]{2,1,0:T(8,128)(2,1)S(1)}, bf16[1,64,2048]{2,1,0:T(8,128)(2,1)S(1)}, u32[]{:S(2)}, u32[]{:S(2)}) %collective-permute-start.5) | collective-permute-done | bytes 262176 | tf_op jit(solution)/shard_map/ppermute | solution.py:23
  86.8 12.8 %orthogonalize.1 = (bf16[1,64,2048]{2,1,0:T(8,128)(2,1)S(1)}, bf16[1,64,2048]{2,1,0:T(8,128)(2,1)S(1)}, bf16[1,64,2048]{2,1,0:T(8,128)(2,1)S(1)}, bf16[1,64,2048...) custom-call(bf16[1,64,2048]{2,1,0:T(8,128)(2,1)S(1)} %get-tuple-elem, ...), custom_call_target="tpu_custom_call" | custom-call | flops 11005853696 | bytes 4194304 | tf_op jit(solution)/shard_map/orthogonalize/pallas_call | solution.py:102
  99.6 1.1 collective-permute-start.20
  100.6 3.1 %collective-permute-start.19 = (bf16[1,64,2048]{2,1,0:T(8,128)(2,1)S(1)}, bf16[1,64,2048]{2,1,0:T(8,128)(2,1)S(1)}, u32[]{:S(2)}, u32[]{:S(2)}) collective-permute-start(bf16[1,64,2048]{2,1,0:T(8,128)(2,1)S(1)} %get-tuple-element.14), channel_id=1, source_target_pairs={{0,7},{1,6},{2,5},{3,4},{4,3},{5,2},{6,1},{7,0},{8,15},{9,14},{10,... | collective-permute-start | bytes 786440 | tf_op jit(solution)/shard_map/ppermute | solution.py:23
  103.7 2.9 %collective-permute-start.22 = (bf16[1,64,2048]{2,1,0:T(8,128)(2,1)S(1)}, bf16[1,64,2048]{2,1,0:T(8,128)(2,1)S(1)}, u32[]{:S(2)}, u32[]{:S(2)}) collective-permute-start(bf16[1,64,2048]{2,1,0:T(8,128)(2,1)S(1)} %get-tuple-element.18), channel_id=1, source_target_pairs={{0,3},{1,2},{2,1},{3,0},{4,7},{5,6},{6,5},{7,4},{8,11},{9,10},{10,... | collective-permute-start | bytes 786440 | tf_op jit(solution)/shard_map/ppermute | solution.py:23
  106.6 6.8 %collective-permute-done.20 = bf16[1,64,2048]{2,1,0:T(8,128)(2,1)S(1)} collective-permute-done((bf16[1,64,2048]{2,1,0:T(8,128)(2,1)S(1)}, bf16[1,64,2048]{2,1,0:T(8,128)(2,1)S(1)}, u32[]{:S(2)}, u32[]{:S(2)}) %collective-permute-start.20) | collective-permute-done | bytes 262176 | tf_op jit(solution)/shard_map/ppermute | solution.py:23
  113.4 3.0 %collective-permute-start.23 = (bf16[1,64,2048]{2,1,0:T(8,128)(2,1)S(1)}, bf16[1,64,2048]{2,1,0:T(8,128)(2,1)S(1)}, u32[]{:S(2)}, u32[]{:S(2)}) collective-permute-start(bf16[1,64,2048]{2,1,0:T(8,128)(2,1)S(1)} %get-tuple-element.19), channel_id=1, source_target_pairs={{0,6},{1,7},{2,4},{3,5},{4,2},{5,3},{6,0},{7,1},{8,14},{9,15},{10,... | collective-permute-start | bytes 786440 | tf_op jit(solution)/shard_map/ppermute | solution.py:23
  116.8 3.6 %add_convert_fusion = bf16[8,1,64,2048]{3,2,1,0:T(8,128)(2,1)S(1)} fusion(bf16[8,1,64,2048]{3,2,1,0:T(8,128)(2,1)} %collective-permute-done.3, bf16[8,1,64,2048]{3,2,1,0:T(8,128)(2,1)} %add_convert_fusion.1, f32[]{:T(128)S(6)} %sub.91, f32[]{:T(128)} %bitcast), kind=kLoop, calls=%fused_computation | loop fusion | flops 6291456 | bytes 6291464 | tf_op jit(solution)/shard_map/convert_element_type | solution.py:187
  120.4 3.6 %collective-permute-start.25 = (bf16[1,64,2048]{2,1,0:T(8,128)(2,1)S(1)}, bf16[1,64,2048]{2,1,0:T(8,128)(2,1)S(1)}, u32[]{:S(2)}, u32[]{:S(2)}) collective-permute-start(bf16[1,64,2048]{2,1,0:T(8,128)(2,1)S(1)} %get-tuple-element.21), channel_id=1, source_target_pairs={{0,4},{1,5},{2,6},{3,7},{4,0},{5,1},{6,2},{7,3},{8,12},{9,13},{10,... | collective-permute-start | bytes 786440 | tf_op jit(solution)/shard_map/ppermute | solution.py:23
  124.5 5.4 %collective-permute-done.22 = bf16[1,64,2048]{2,1,0:T(8,128)(2,1)S(1)} collective-permute-done((bf16[1,64,2048]{2,1,0:T(8,128)(2,1)S(1)}, bf16[1,64,2048]{2,1,0:T(8,128)(2,1)S(1)}, u32[]{:S(2)}, u32[]{:S(2)}) %collective-permute-start.22) | collective-permute-done | bytes 262176 | tf_op jit(solution)/shard_map/ppermute | solution.py:23
  130.2 13.5 %collective-permute-done.24 = bf16[1,64,2048]{2,1,0:T(8,128)(2,1)S(1)} collective-permute-done((bf16[1,64,2048]{2,1,0:T(8,128)(2,1)S(1)}, bf16[1,64,2048]{2,1,0:T(8,128)(2,1)S(1)}, u32[]{:S(2)}, u32[]{:S(2)}) %collective-permute-start.24) | collective-permute-done | bytes 262176 | tf_op jit(solution)/shard_map/ppermute | solution.py:23
  143.7 4.2 %collective-permute-done.25 = bf16[1,64,2048]{2,1,0:T(8,128)(2,1)S(1)} collective-permute-done((bf16[1,64,2048]{2,1,0:T(8,128)(2,1)S(1)}, bf16[1,64,2048]{2,1,0:T(8,128)(2,1)S(1)}, u32[]{:S(2)}, u32[]{:S(2)}) %collective-permute-start.25) | collective-permute-done | bytes 262176 | tf_op jit(solution)/shard_map/ppermute | solution.py:23
  148.1 1.3 copy-done.2
  149.4 0.7 copy-done.3
  (49 shorter events, 2.0 us)
Async XLA Ops:
  0.6 9.7 %copy-start.7 = (s32[4,2]{0,1:T(2,128)S(1)}, s32[4,2]{0,1:T(2,128)}, u32[]{:S(2)}) copy-start(s32[4,2]{0,1:T(2,128)} %param.9) | copy-start | bytes 100
  0.7 12.8 %copy-start.4 = (bf16[1,8,64,2048]{3,2,1,0:T(8,128)(2,1)S(1)}, bf16[1,8,64,2048]{3,2,1,0:T(8,128)(2,1)}, u32[]{:S(2)}) copy-start(bf16[1,8,64,2048]{3,2,1,0:T(8,128)(2,1)} %param.5) | copy-start | bytes 6291460
  2.8 10.6 %collective-permute-start.15 = (bf16[1,1,64,2048]{3,2,1,0:T(8,128)(2,1)}, bf16[1,1,64,2048]{3,2,1,0:T(8,128)(2,1)}, u32[]{:S(2)}, u32[]{:S(2)}) collective-permute-start(bf16[1,1,64,2048]{3,2,1,0:T(8,128)(2,1)} %get-tuple-element.30), channel_id=1, source_target_pairs={{0,8},{8,0},{16,24},{24,16},{1,9},{9,1},{17,25},{25,17},{2,10},{10... | collective-permute-start | bytes 786440 | tf_op jit(solution)/shard_map/ppermute | solution.py:23
  3.2 13.4 %collective-permute-start.16 = (bf16[1,1,64,2048]{3,2,1,0:T(8,128)(2,1)}, bf16[1,1,64,2048]{3,2,1,0:T(8,128)(2,1)}, u32[]{:S(2)}, u32[]{:S(2)}) collective-permute-start(bf16[1,1,64,2048]{3,2,1,0:T(8,128)(2,1)} %get-tuple-element.30), channel_id=1, source_target_pairs={{0,16},{8,24},{16,0},{24,8},{1,17},{9,25},{17,1},{25,9},{2,18},{10... | collective-permute-start | bytes 786440 | tf_op jit(solution)/shard_map/ppermute | solution.py:23
  5.7 7.1 %collective-permute-start.11 = (bf16[1,1,64,2048]{3,2,1,0:T(8,128)(2,1)S(1)}, bf16[1,1,64,2048]{3,2,1,0:T(8,128)(2,1)}, u32[]{:S(2)}, u32[]{:S(2)}) collective-permute-start(bf16[1,1,64,2048]{3,2,1,0:T(8,128)(2,1)S(1)} %get-tuple-element.29), channel_id=1, source_target_pairs={{0,8},{8,0},{16,24},{24,16},{1,9},{9,1},{17,25},{25,17},{2,10},{10... | collective-permute-start | bytes 786440 | tf_op jit(solution)/shard_map/ppermute | solution.py:23
  6.0 12.7 %collective-permute-start.12 = (bf16[1,1,64,2048]{3,2,1,0:T(8,128)(2,1)S(1)}, bf16[1,1,64,2048]{3,2,1,0:T(8,128)(2,1)}, u32[]{:S(2)}, u32[]{:S(2)}) collective-permute-start(bf16[1,1,64,2048]{3,2,1,0:T(8,128)(2,1)S(1)} %get-tuple-element.29), channel_id=1, source_target_pairs={{0,16},{8,24},{16,0},{24,8},{1,17},{9,25},{17,1},{25,9},{2,18},{10... | collective-permute-start | bytes 786440 | tf_op jit(solution)/shard_map/ppermute | solution.py:23
  7.5 11.1 %collective-permute-start.7 = (bf16[2,1,64,2048]{3,2,1,0:T(8,128)(2,1)S(1)}, bf16[2,1,64,2048]{3,2,1,0:T(8,128)(2,1)S(1)}, u32[]{:S(2)}, u32[]{:S(2)}) collective-permute-start(bf16[2,1,64,2048]{3,2,1,0:T(8,128)(2,1)S(1)} %fusion.5), channel_id=1, source_target_pairs={{0,8},{8,0},{16,24},{24,16},{1,9},{9,1},{17,25},{25,17},{2,10},{10... | collective-permute-start | bytes 1572872 | tf_op jit(solution)/shard_map/ppermute | solution.py:23
  12.9 18.7 %collective-permute-start.1 = (bf16[4,1,64,2048]{3,2,1,0:T(8,128)(2,1)}, bf16[4,1,64,2048]{3,2,1,0:T(8,128)(2,1)S(1)}, u32[]{:S(2)}, u32[]{:S(2)}) collective-permute-start(bf16[4,1,64,2048]{3,2,1,0:T(8,128)(2,1)} %fusion.2), channel_id=1, source_target_pairs={{0,8},{8,0},{16,24},{24,16},{1,9},{9,1},{17,25},{25,17},{2,10},{10... | collective-permute-start | bytes 3145736 | tf_op jit(solution)/shard_map/ppermute | solution.py:23
  13.4 27.7 %collective-permute-start = (bf16[8,1,64,2048]{3,2,1,0:T(8,128)(2,1)S(1)}, bf16[8,1,64,2048]{3,2,1,0:T(8,128)(2,1)S(1)}, u32[]{:S(2)}, u32[]{:S(2)}) collective-permute-start(bf16[8,1,64,2048]{3,2,1,0:T(8,128)(2,1)S(1)} %bitcast.129), channel_id=1, source_target_pairs={{0,8},{8,0},{16,24},{24,16},{1,9},{9,1},{17,25},{25,17},{2,10},{10... | collective-permute-start | bytes 6291464 | tf_op jit(solution)/shard_map/ppermute | solution.py:23
  16.7 5.8 %collective-permute-start.17 = (bf16[1,1,64,2048]{3,2,1,0:T(8,128)(2,1)}, bf16[1,1,64,2048]{3,2,1,0:T(8,128)(2,1)S(1)}, u32[]{:S(2)}, u32[]{:S(2)}) collective-permute-start(bf16[1,1,64,2048]{3,2,1,0:T(8,128)(2,1)} %collective-permute-done.16), channel_id=1, source_target_pairs={{0,8},{8,0},{16,24},{24,16},{1,9},{9,1},{17,25},{25,17},{2,10},{10... | collective-permute-start | bytes 786440 | tf_op jit(solution)/shard_map/ppermute | solution.py:23
  18.6 6.4 %collective-permute-start.13 = (bf16[1,1,64,2048]{3,2,1,0:T(8,128)(2,1)}, bf16[1,1,64,2048]{3,2,1,0:T(8,128)(2,1)S(1)}, u32[]{:S(2)}, u32[]{:S(2)}) collective-permute-start(bf16[1,1,64,2048]{3,2,1,0:T(8,128)(2,1)} %collective-permute-done.12), channel_id=1, source_target_pairs={{0,8},{8,0},{16,24},{24,16},{1,9},{9,1},{17,25},{25,17},{2,10},{10... | collective-permute-start | bytes 786440 | tf_op jit(solution)/shard_map/ppermute | solution.py:23
  20.7 14.4 %collective-permute-start.8 = (bf16[2,1,64,2048]{3,2,1,0:T(8,128)(2,1)S(1)}, bf16[2,1,64,2048]{3,2,1,0:T(8,128)(2,1)S(1)}, u32[]{:S(2)}, u32[]{:S(2)}) collective-permute-start(bf16[2,1,64,2048]{3,2,1,0:T(8,128)(2,1)S(1)} %fusion.4), channel_id=1, source_target_pairs={{0,16},{8,24},{16,0},{24,8},{1,17},{9,25},{17,1},{25,9},{2,18},{10... | collective-permute-start | bytes 1572872 | tf_op jit(solution)/shard_map/ppermute | solution.py:23
  22.5 9.1 %copy-start = (f32[1,8,64,2048]{3,2,1,0:T(8,128)S(1)}, f32[1,8,64,2048]{3,2,1,0:T(8,128)}, u32[]{:S(2)}) copy-start(f32[1,8,64,2048]{3,2,1,0:T(8,128)} %param.6) | copy-start | bytes 12582916
  26.8 35.0 %collective-permute-start.14 = (bf16[1,64,2048]{2,1,0:T(8,128)(2,1)S(1)}, bf16[1,64,2048]{2,1,0:T(8,128)(2,1)S(1)}, u32[]{:S(2)}, u32[]{:S(2)}) collective-permute-start(bf16[1,64,2048]{2,1,0:T(8,128)(2,1)S(1)} %get-tuple-element.37), channel_id=1, source_target_pairs={{0,6},{1,7},{2,4},{3,5},{4,2},{5,3},{6,0},{7,1},{8,14},{9,15},{10,... | collective-permute-start | bytes 786440 | tf_op jit(solution)/shard_map/ppermute | solution.py:23
  30.4 4.7 %copy-start.5 = (bf16[1,8,64,2048]{3,2,1,0:T(8,128)(2,1)S(1)}, bf16[1,8,64,2048]{3,2,1,0:T(8,128)(2,1)}, u32[]{:S(2)}) copy-start(bf16[1,8,64,2048]{3,2,1,0:T(8,128)(2,1)} %param.8) | copy-start | bytes 6291460
  30.4 4.7 %copy-start.6 = (bf16[1,8,64,2048]{3,2,1,0:T(8,128)(2,1)S(1)}, bf16[1,8,64,2048]{3,2,1,0:T(8,128)(2,1)}, u32[]{:S(2)}) copy-start(bf16[1,8,64,2048]{3,2,1,0:T(8,128)(2,1)} %param.7) | copy-start | bytes 6291460
  30.4 33.9 %collective-permute-start.18 = (bf16[1,64,2048]{2,1,0:T(8,128)(2,1)S(1)}, bf16[1,64,2048]{2,1,0:T(8,128)(2,1)S(1)}, u32[]{:S(2)}, u32[]{:S(2)}) collective-permute-start(bf16[1,64,2048]{2,1,0:T(8,128)(2,1)S(1)} %get-tuple-element.35), channel_id=1, source_target_pairs={{0,7},{1,6},{2,5},{3,4},{4,3},{5,2},{6,1},{7,0},{8,15},{9,14},{10,... | collective-permute-start | bytes 786440 | tf_op jit(solution)/shard_map/ppermute | solution.py:23
  32.7 25.1 %collective-permute-start.2 = (bf16[4,1,64,2048]{3,2,1,0:T(8,128)(2,1)S(1)}, bf16[4,1,64,2048]{3,2,1,0:T(8,128)(2,1)S(1)}, u32[]{:S(2)}, u32[]{:S(2)}) collective-permute-start(bf16[4,1,64,2048]{3,2,1,0:T(8,128)(2,1)S(1)} %fusion.1), channel_id=1, source_target_pairs={{0,16},{8,24},{16,0},{24,8},{1,17},{9,25},{17,1},{25,9},{2,18},{10... | collective-permute-start | bytes 3145736 | tf_op jit(solution)/shard_map/ppermute | solution.py:23
  36.8 34.9 %collective-permute-start.10 = (bf16[1,64,2048]{2,1,0:T(8,128)(2,1)S(1)}, bf16[1,64,2048]{2,1,0:T(8,128)(2,1)S(1)}, u32[]{:S(2)}, u32[]{:S(2)}) collective-permute-start(bf16[1,64,2048]{2,1,0:T(8,128)(2,1)S(1)} %get-tuple-element.39), channel_id=1, source_target_pairs={{0,5},{1,4},{2,7},{3,6},{4,1},{5,0},{6,3},{7,2},{8,13},{9,12},{10,... | collective-permute-start | bytes 786440 | tf_op jit(solution)/shard_map/ppermute | solution.py:23
  41.1 34.6 %collective-permute-start.9 = (bf16[1,64,2048]{2,1,0:T(8,128)(2,1)S(1)}, bf16[1,64,2048]{2,1,0:T(8,128)(2,1)S(1)}, u32[]{:S(2)}, u32[]{:S(2)}) collective-permute-start(bf16[1,64,2048]{2,1,0:T(8,128)(2,1)S(1)} %get-tuple-element.40), channel_id=1, source_target_pairs={{0,4},{1,5},{2,6},{3,7},{4,0},{5,1},{6,2},{7,3},{8,12},{9,13},{10,... | collective-permute-start | bytes 786440 | tf_op jit(solution)/shard_map/ppermute | solution.py:23
  57.7 58.9 %collective-permute-start.3 = (bf16[8,1,64,2048]{3,2,1,0:T(8,128)(2,1)}, bf16[8,1,64,2048]{3,2,1,0:T(8,128)(2,1)}, u32[]{:S(2)}, u32[]{:S(2)}) collective-permute-start(bf16[8,1,64,2048]{3,2,1,0:T(8,128)(2,1)} %add_convert_fusion.1), channel_id=1, source_target_pairs={{0,16},{8,24},{16,0},{24,8},{1,17},{9,25},{17,1},{25,9},{2,18},{10... | collective-permute-start | bytes 6291464 | tf_op jit(solution)/shard_map/ppermute | solution.py:23
  61.6 25.1 %copy-start.1 = (f32[1,8,64,2048]{3,2,1,0:T(8,128)}, f32[1,8,64,2048]{3,2,1,0:T(8,128)S(1)}, u32[]{:S(2)}) copy-start(f32[1,8,64,2048]{3,2,1,0:T(8,128)S(1)} %get-tuple-element.23) | copy-start | bytes 12582916
  61.7 20.6 %collective-permute-start.4 = (bf16[1,64,2048]{2,1,0:T(8,128)(2,1)S(1)}, bf16[1,64,2048]{2,1,0:T(8,128)(2,1)S(1)}, u32[]{:S(2)}, u32[]{:S(2)}) collective-permute-start(bf16[1,64,2048]{2,1,0:T(8,128)(2,1)S(1)} %get-tuple-element.33), channel_id=1, source_target_pairs={{0,3},{1,2},{2,1},{3,0},{4,7},{5,6},{6,5},{7,4},{8,11},{9,10},{10,... | collective-permute-start | bytes 786440 | tf_op jit(solution)/shard_map/ppermute | solution.py:23
  64.3 22.4 %collective-permute-start.5 = (bf16[1,64,2048]{2,1,0:T(8,128)(2,1)S(1)}, bf16[1,64,2048]{2,1,0:T(8,128)(2,1)S(1)}, u32[]{:S(2)}, u32[]{:S(2)}) collective-permute-start(bf16[1,64,2048]{2,1,0:T(8,128)(2,1)S(1)} %get-tuple-element.32), channel_id=1, source_target_pairs={{0,2},{1,3},{2,0},{3,1},{4,6},{5,7},{6,4},{7,5},{8,10},{9,11},{10,... | collective-permute-start | bytes 786440 | tf_op jit(solution)/shard_map/ppermute | solution.py:23
  71.7 15.0 %collective-permute-start.6 = (bf16[1,64,2048]{2,1,0:T(8,128)(2,1)S(1)}, bf16[1,64,2048]{2,1,0:T(8,128)(2,1)S(1)}, u32[]{:S(2)}, u32[]{:S(2)}) collective-permute-start(bf16[1,64,2048]{2,1,0:T(8,128)(2,1)S(1)} %get-tuple-element.31), channel_id=1, source_target_pairs={{0,1},{1,0},{2,3},{3,2},{4,5},{5,4},{6,7},{7,6},{8,9},{9,8},{10,11... | collective-permute-start | bytes 786440 | tf_op jit(solution)/shard_map/ppermute | solution.py:23
  99.6 13.9 %collective-permute-start.20 = (bf16[1,64,2048]{2,1,0:T(8,128)(2,1)S(1)}, bf16[1,64,2048]{2,1,0:T(8,128)(2,1)S(1)}, u32[]{:S(2)}, u32[]{:S(2)}) collective-permute-start(bf16[1,64,2048]{2,1,0:T(8,128)(2,1)S(1)} %get-tuple-element.16), channel_id=1, source_target_pairs={{0,1},{1,0},{2,3},{3,2},{4,5},{5,4},{6,7},{7,6},{8,9},{9,8},{10,11... | collective-permute-start | bytes 786440 | tf_op jit(solution)/shard_map/ppermute | solution.py:23
  100.6 19.8 %collective-permute-start.19 = (bf16[1,64,2048]{2,1,0:T(8,128)(2,1)S(1)}, bf16[1,64,2048]{2,1,0:T(8,128)(2,1)S(1)}, u32[]{:S(2)}, u32[]{:S(2)}) collective-permute-start(bf16[1,64,2048]{2,1,0:T(8,128)(2,1)S(1)} %get-tuple-element.14), channel_id=1, source_target_pairs={{0,7},{1,6},{2,5},{3,4},{4,3},{5,2},{6,1},{7,0},{8,15},{9,14},{10,... | collective-permute-start | bytes 786440 | tf_op jit(solution)/shard_map/ppermute | solution.py:23
  103.7 20.7 %collective-permute-start.21 = (bf16[1,64,2048]{2,1,0:T(8,128)(2,1)S(1)}, bf16[1,64,2048]{2,1,0:T(8,128)(2,1)S(1)}, u32[]{:S(2)}, u32[]{:S(2)}) collective-permute-start(bf16[1,64,2048]{2,1,0:T(8,128)(2,1)S(1)} %get-tuple-element.17), channel_id=1, source_target_pairs={{0,2},{1,3},{2,0},{3,1},{4,6},{5,7},{6,4},{7,5},{8,10},{9,11},{10,... | collective-permute-start | bytes 786440 | tf_op jit(solution)/shard_map/ppermute | solution.py:23
  103.7 26.2 %collective-permute-start.22 = (bf16[1,64,2048]{2,1,0:T(8,128)(2,1)S(1)}, bf16[1,64,2048]{2,1,0:T(8,128)(2,1)S(1)}, u32[]{:S(2)}, u32[]{:S(2)}) collective-permute-start(bf16[1,64,2048]{2,1,0:T(8,128)(2,1)S(1)} %get-tuple-element.18), channel_id=1, source_target_pairs={{0,3},{1,2},{2,1},{3,0},{4,7},{5,6},{6,5},{7,4},{8,11},{9,10},{10,... | collective-permute-start | bytes 786440 | tf_op jit(solution)/shard_map/ppermute | solution.py:23
  113.4 16.6 %collective-permute-start.23 = (bf16[1,64,2048]{2,1,0:T(8,128)(2,1)S(1)}, bf16[1,64,2048]{2,1,0:T(8,128)(2,1)S(1)}, u32[]{:S(2)}, u32[]{:S(2)}) collective-permute-start(bf16[1,64,2048]{2,1,0:T(8,128)(2,1)S(1)} %get-tuple-element.19), channel_id=1, source_target_pairs={{0,6},{1,7},{2,4},{3,5},{4,2},{5,3},{6,0},{7,1},{8,14},{9,15},{10,... | collective-permute-start | bytes 786440 | tf_op jit(solution)/shard_map/ppermute | solution.py:23
  116.7 27.0 %collective-permute-start.24 = (bf16[1,64,2048]{2,1,0:T(8,128)(2,1)S(1)}, bf16[1,64,2048]{2,1,0:T(8,128)(2,1)S(1)}, u32[]{:S(2)}, u32[]{:S(2)}) collective-permute-start(bf16[1,64,2048]{2,1,0:T(8,128)(2,1)S(1)} %get-tuple-element.20), channel_id=1, source_target_pairs={{0,5},{1,4},{2,7},{3,6},{4,1},{5,0},{6,3},{7,2},{8,13},{9,12},{10,... | collective-permute-start | bytes 786440 | tf_op jit(solution)/shard_map/ppermute | solution.py:23
  120.4 27.5 %collective-permute-start.25 = (bf16[1,64,2048]{2,1,0:T(8,128)(2,1)S(1)}, bf16[1,64,2048]{2,1,0:T(8,128)(2,1)S(1)}, u32[]{:S(2)}, u32[]{:S(2)}) collective-permute-start(bf16[1,64,2048]{2,1,0:T(8,128)(2,1)S(1)} %get-tuple-element.21), channel_id=1, source_target_pairs={{0,4},{1,5},{2,6},{3,7},{4,0},{5,1},{6,2},{7,3},{8,12},{9,13},{10,... | collective-permute-start | bytes 786440 | tf_op jit(solution)/shard_map/ppermute | solution.py:23
  148.1 1.3 copy-start.2
  148.1 2.0 %copy-start.3 = (bf16[1,8,64,2048]{3,2,1,0:T(8,128)(2,1)}, bf16[1,8,64,2048]{3,2,1,0:T(8,128)(2,1)S(1)}, u32[]{:S(2)}) copy-start(bf16[1,8,64,2048]{3,2,1,0:T(8,128)(2,1)S(1)} %get-tuple-element.41) | copy-start | bytes 6291460

commit v12 on v9

--- a/solution.py
+++ b/solution.py
@@ -119,8 +119,9 @@
 def grouped(shards):
     unit = shards // 8
     if shards % 8:
-        return [(0, shards)]
-    return [(low * unit, count * unit) for low, count in ((7, 1), (6, 1), (2, 2), (4, 2), (0, 2))]
+        return [[(0, shards)]]
+    groups = [[(7, 1)], [(6, 1)], [(2, 2)], [(4, 2)], [(0, 2)]]
+    return [[(low * unit, count * unit) for low, count in group] for group in groups]
 
 
 def after(values, *others):
@@ -148,35 +149,45 @@
     def blend(share, own, near):
         return share * own + (1.0 - share) * near.astype(F32)
 
+    weight_near = swapped(weight, "rep", 1)
+    arrived = []
     new_tracker = jnp.zeros(shape, F32)
     blocks = [None] * shards
-    leads = []
-    for turn, (lowest, length) in enumerate(grouped(shards)):
-        if turn == 2:
-            tracker = after(tracker, leads)
-        start = (here ^ lowest) // length * length
-        own = taken(tracker, start, length)
+    for turn, runs in enumerate(grouped(shards)):
+        places = [((here ^ lowest) // length * length, length) for lowest, length in runs]
+
+        def part_of(values):
+            parts = [taken(values, start, length) for start, length in places]
+            return parts[0] if len(parts) == 1 else jnp.concatenate(parts)
+
+        own = part_of(tracker)
         rounded = own.astype(BF16)
-        leads.append(rounded)
         mixed = blend(first, own, swapped(rounded, "rep", 1))
         if turn < 2:
             far = swapped(rounded, "rep", 2)
             far_mixed = blend(far_first, far.astype(F32), swapped(far, "rep", 1))
         else:
-            far = swapped(mixed.astype(BF16), "rep", 2)
+            sent = mixed.astype(BF16)
+            if turn == 2:
+                sent = after(sent, weight_near)
+            elif turn == 4:
+                sent = after(sent, arrived[turn - 2], blocks[7 * shards // 8])
+            far = swapped(sent, "rep", 2)
             far_mixed = far.astype(F32)
-        base = second * mixed + (
-            taken(grad_new, start, length).astype(F32) - taken(grad_old, start, length).astype(F32)
-        )
+        arrived.append(far)
+        base = second * mixed + (part_of(grad_new).astype(F32) - part_of(grad_old).astype(F32))
         if turn < 2:
             base = lax.optimization_barrier(base)
-        group = base + (1.0 - second) * far_mixed
-        for offset in reversed(range(lowest, lowest + length)):
-            block = taken(group, (here ^ offset) % length, 1)[0].astype(BF16)
-            blocks[offset] = swapped(block, "shard", offset) if offset else block
-        new_tracker = lax.dynamic_update_slice_in_dim(new_tracker, group, start, axis=0)
-
-    weight_near = swapped(weight, "rep", 1)
+        whole = base + (1.0 - second) * far_mixed
+        passed = 0
+        for (lowest, length), (start, _) in zip(runs, places):
+            group = whole[passed : passed + length]
+            passed += length
+            for offset in reversed(range(lowest, lowest + length)):
+                block = taken(group, (here ^ offset) % length, 1)[0].astype(BF16)
+                blocks[offset] = swapped(block, "shard", offset) if offset else block
+            new_tracker = lax.dynamic_update_slice_in_dim(new_tracker, group, start, axis=0)
+
     weight_own = (
         first * weight.astype(F32) + (1.0 - first) * weight_near.astype(F32)
     ).astype(BF16)

time: 162 us -> 151 us (0.932)
  starting transfers between devices: 42.7 us -> 26.7 us
  waiting for transfers between devices: 72.6 us -> 79 us
    ppermute x28, starting transfers between devices: 42.7 us -> 26.7 us  [swapped(): lax.ppermute(values, axis, [(i, i ^ offset) for i in range(lax.axis_size(...]
    ppermute x28, waiting for transfers between devices: 72.6 us -> 79 us  [swapped(): lax.ppermute(values, axis, [(i, i ^ offset) for i in range(lax.axis_size(...]
  transfers between devices with their start and end apart: 28 -> 28, of which waited for: 12 -> 12; matrix products, arithmetic and copies ran while one was open for 16% -> 17% of each run, Pallas kernels for 8% -> 8%
where the time goes in v12:
time: 151 us
  waiting for transfers between devices  79 us (52%)
  starting transfers between devices  26.7 us (18%)
  other arithmetic  20.6 us (14%)
  Pallas kernels  12.8 us (8%)
  local copies, waits for them, and re-layouts  8.99 us (6%)
  between operations  2.84 us (2%)
    ppermute x28, waiting for transfers between devices, swapped(): lax.ppermute(values, axis, [(i, i ^ offset) for i in range(lax.axis_size(...  79 us
    ppermute x28, starting transfers between devices, swapped(): lax.ppermute(values, axis, [(i, i ^ offset) for i in range(lax.axis_size(...  26.7 us
    pallas_call x1, Pallas kernels, orthogonalize(): pl.pallas_call(body, grid=(each,), in_specs=[block] * count, out_specs=[b...  12.8 us
    convert_element_type x2, local copies, waits for them, and re-layouts, local(): rounded = own.astype(BF16)  5.18 us
    dynamic_update_slice x3, other arithmetic, local(): lax.dynamic_update_slice_in_dim(new_tracker, group, start, axis=0)  4.98 us
    convert_element_type x2, other arithmetic, local(): block = taken(group, (here ^ offset) % length, 1)[0].astype(BF16)  3.68 us
    convert_element_type x1, other arithmetic, local(): mixed_weight = (second * weight_own.astype(F32) + (1.0 - second) * weight...  3.64 us
  transfers between devices with their start and end apart: 28, of which 12 were waited for; matrix products, arithmetic and copies ran while one was open for 17% of the time, Pallas kernels for 8%

profile of v12, /device:TPU:0, one launch (start us, length us, event | category | flops | bytes accessed | tf_op | source)
XLA Modules:
  0.0 150.9 jit_solution(14781238227938976359)
XLA Ops:
  0.7 2.1 %dynamic-slice_convert_fusion.9 = (bf16[1,1,64,2048]{3,2,1,0:T(8,128)(2,1)S(1)}, bf16[1,1,64,2048]{3,2,1,0:T(8,128)(2,1)}) fusion(f32[1,8,64,2048]{3,2,1,0:T(8,128)} %param.6, s32[]{:T(128)S(6)} %select_n.157, s32[]{:T(128)S(6)} %select_n.141), kind=kLoop, calls=%fused_computation.53 | loop fusion | bytes 1048584 | tf_op jit(solution)/shard_map/convert_element_type | solution.py:164
  2.8 0.5 collective-permute-start.4
  3.2 2.5 %collective-permute-start.5 = (bf16[1,1,64,2048]{3,2,1,0:T(8,128)(2,1)}, bf16[1,1,64,2048]{3,2,1,0:T(8,128)(2,1)}, u32[]{:S(2)}, u32[]{:S(2)}) collective-permute-start(bf16[1,1,64,2048]{3,2,1,0:T(8,128)(2,1)} %get-tuple-element.41), channel_id=1, source_target_pairs={{0,16},{8,24},{16,0},{24,8},{1,17},{9,25},{17,1},{25,9},{2,18},{10... | collective-permute-start | bytes 786440 | tf_op jit(solution)/shard_map/ppermute | solution.py:23
  6.0 0.3 collective-permute-start.18
  6.2 3.1 %fusion.6 = (bf16[2,1,64,2048]{3,2,0,1:T(8,128)(2,1)S(1)}, bf16[2,1,64,2048]{3,2,1,0:T(8,128)(2,1)}, bf16[2,1,64,2048]{3,2,0,1:T(8,128)(2,1)}) fusion(f32[1,8,64,2048]{3,2,1,0:T(8,128)} %param.6, s32[]{:T(128)S(6)} %select_n.138, s32[]{:T(128)S(6)} %select_n.140, s32[]{:T(128)S(6)} %select_n.152), kind=kLoop, calls=%fused_computation.24 | loop fusion | bytes 3145740 | tf_op jit(solution)/shard_map/convert_element_type | solution.py:164
  9.3 0.7 constant_dynamic-slice_fusion
  11.8 0.6 collective-permute-start.2
  12.5 0.7 collective-permute-done.5
  13.2 3.0 %subtract_add_fusion = (f32[1,1,64,2048]{3,2,1,0:T(8,128)S(1)}, f32[1,1,64,2048]{3,2,1,0:T(8,128)S(1)}) fusion(bf16[1,1,64,2048]{3,2,1,0:T(8,128)(2,1)} %collective-permute-done.17, f32[1,8,64,2048]{3,2,1,0:T(8,128)} %param.6, s32[]{:T(128)S(6)} %select_n.157, bf16[1,8,64,2048]{3,2,1,0:T(8,128)(2,1)S(1)} %copy-done.2, bf16[1,8,64,2048]{3,2,1,0:T(8,128)(2,1)} %param.7, ...), kind=kLoop, calls=%fused_computation.44 | loop fusion | flops 2359296 | bytes 3670036 | tf_op jit(solution)/shard_map/add | solution.py:178
  16.2 2.4 %collective-permute-done.18 = bf16[1,1,64,2048]{3,2,1,0:T(8,128)(2,1)} collective-permute-done((bf16[1,1,64,2048]{3,2,1,0:T(8,128)(2,1)S(1)}, bf16[1,1,64,2048]{3,2,1,0:T(8,128)(2,1)}, u32[]{:S(2)}, u32[]{:S(2)}) %collective-permute-start.18) | collective-permute-done | bytes 262176 | tf_op jit(solution)/shard_map/ppermute | solution.py:23
  18.7 0.5 collective-permute-start.19
  19.2 0.5 reshape.500
  19.7 2.0 %convert_bitcast_fusion.1 = (bf16[1,64,2048]{2,1,0:T(8,128)(2,1)S(1)}, f32[1,8,64,2048]{3,2,1,0:T(8,128)S(1)}) fusion(f32[1,1,64,2048]{3,2,1,0:T(8,128)S(1)} %get-tuple-element.34, bf16[1,1,64,2048]{3,2,1,0:T(8,128)(2,1)S(1)} %collective-permute-done.6, f32[]{:T(128)S(6)} %sub.113, bf16[1,1,64,2048]{3,2,1,0:T(8,128)(2,1)} %collective-permute-done.5, ...), kind=kLoop, calls=%fused_computation.86 | loop fusion | flops 1048576 | bytes 1835024 | tf_op jit(solution)/shard_map/convert_element_type | solution.py:187
  21.6 4.9 %collective-permute-start.7 = (bf16[1,64,2048]{2,1,0:T(8,128)(2,1)S(1)}, bf16[1,64,2048]{2,1,0:T(8,128)(2,1)S(1)}, u32[]{:S(2)}, u32[]{:S(2)}) collective-permute-start(bf16[1,64,2048]{2,1,0:T(8,128)(2,1)S(1)} %get-tuple-element.50), channel_id=1, source_target_pairs={{0,7},{1,6},{2,5},{3,4},{4,3},{5,2},{6,1},{7,0},{8,15},{9,14},{10,... | collective-permute-start | bytes 786440 | tf_op jit(solution)/shard_map/ppermute | solution.py:23
  26.5 1.0 fusion.5
  27.5 1.6 %collective-permute-start.14 = (bf16[2,1,64,2048]{3,2,1,0:T(8,128)(2,1)S(1)}, bf16[2,1,64,2048]{3,2,1,0:T(8,128)(2,1)S(1)}, u32[]{:S(2)}, u32[]{:S(2)}) collective-permute-start(bf16[2,1,64,2048]{3,2,1,0:T(8,128)(2,1)S(1)} %get-tuple-element.38), channel_id=1, source_target_pairs={{0,16},{8,24},{16,0},{24,8},{1,17},{9,25},{17,1},{25,9},{2,18},{10... | collective-permute-start | bytes 1572872 | tf_op jit(solution)/shard_map/ppermute | solution.py:23
  29.1 1.7 %convert_bitcast_fusion = (bf16[1,64,2048]{2,1,0:T(8,128)(2,1)S(1)}, f32[1,8,64,2048]{3,2,1,0:T(8,128)S(1)}) fusion(f32[1,1,64,2048]{3,2,1,0:T(8,128)S(1)} %get-tuple-element.33, bf16[1,1,64,2048]{3,2,1,0:T(8,128)(2,1)S(1)} %collective-permute-done.19, f32[]{:T(128)S(6)} %sub.113, bf16[1,1,64,2048]{3,2,1,0:T(8,128)(2,1)} %collective-permute-done.18, ...), kind=kLoop, calls=%fused_computation.85 | loop fusion | flops 1048576 | bytes 1835024 | tf_op jit(solution)/shard_map/convert_element_type | solution.py:187
  30.8 0.3 collective-permute-start.20
  31.1 0.8 fusion.3
  31.9 0.6 collective-permute-start.3
  32.5 2.8 %add_convert_fusion.1 = bf16[8,1,64,2048]{3,2,1,0:T(8,128)(2,1)} fusion(bf16[8,1,64,2048]{3,2,1,0:T(8,128)(2,1)S(1)} %collective-permute-done, f32[]{:T(128)S(6)} %sub.108, f32[]{:T(128)} %bitcast.1, bf16[1,8,64,2048]{3,2,1,0:T(8,128)(2,1)S(1)} %copy-done.6), kind=kLoop, calls=%fused_computation.1 | loop fusion | flops 6291456 | bytes 6291464 | tf_op jit(solution)/shard_map/convert_element_type | solution.py:193
  35.3 16.8 %collective-permute-done.3 = bf16[2,1,64,2048]{3,2,1,0:T(8,128)(2,1)S(1)} collective-permute-done((bf16[2,1,64,2048]{3,2,1,0:T(8,128)(2,1)S(1)}, bf16[2,1,64,2048]{3,2,1,0:T(8,128)(2,1)S(1)}, u32[]{:S(2)}, u32[]{:S(2)}) %collective-permute-start.3) | collective-permute-done | bytes 524320 | tf_op jit(solution)/shard_map/ppermute | solution.py:23
  52.2 1.5 collective-permute-start.8
  53.7 1.7 %bitcast_dynamic-update-slice_fusion.2 = (f32[1,8,64,2048]{3,2,1,0:T(8,128)S(1)}, bf16[2,1,64,2048]{3,2,1,0:T(8,128)(2,1)S(1)}) fusion(f32[1,8,64,2048]{3,2,1,0:T(8,128)S(1)} %get-tuple-element.43, s32[]{:T(128)S(6)} %select_n.140, bf16[2,1,64,2048]{3,2,1,0:T(8,128)(2,1)S(1)} %collective-permute-done.3, f32[]{:T(128)S(6)} %sub.112, ...), kind=kLoop, calls=%fused_computation.10 | loop fusion | flops 3407872 | bytes 4718612 | tf_op jit(solution)/shard_map/dynamic_update_slice | solution.py:189
  55.4 1.7 %bitcast_dynamic-update-slice_fusion.1 = (f32[1,8,64,2048]{3,2,1,0:T(8,128)S(1)}, bf16[2,1,64,2048]{3,2,1,0:T(8,128)(2,1)S(1)}) fusion(f32[1,8,64,2048]{3,2,1,0:T(8,128)S(1)} %get-tuple-element.31, s32[]{:T(128)S(6)} %select_n.152, bf16[2,1,64,2048]{3,2,1,0:T(8,128)(2,1)S(1)} %collective-permute-done.14, f32[]{:T(128)S(6)} %sub.112, ...), kind=kLoop, calls=%fused_computation.9 | loop fusion | flops 3407872 | bytes 4718612 | tf_op jit(solution)/shard_map/dynamic_update_slice | solution.py:189
  57.2 2.9 %collective-permute-start.16 = (bf16[1,64,2048]{2,1,0:T(8,128)(2,1)S(1)}, bf16[1,64,2048]{2,1,0:T(8,128)(2,1)S(1)}, u32[]{:S(2)}, u32[]{:S(2)}) collective-permute-start(bf16[1,64,2048]{2,1,0:T(8,128)(2,1)S(1)} %get-tuple-element.44), channel_id=1, source_target_pairs={{0,5},{1,4},{2,7},{3,6},{4,1},{5,0},{6,3},{7,2},{8,13},{9,12},{10,... | collective-permute-start | bytes 786440 | tf_op jit(solution)/shard_map/ppermute | solution.py:23
  60.1 4.5 %collective-permute-done.8 = bf16[2,1,64,2048]{3,2,0,1:T(8,128)(2,1)S(1)} collective-permute-done((bf16[2,1,64,2048]{3,2,0,1:T(8,128)(2,1)S(1)}, bf16[2,1,64,2048]{3,2,0,1:T(8,128)(2,1)S(1)}, u32[]{:S(2)}, u32[]{:S(2)}) %collective-permute-start.8) | collective-permute-done | bytes 524320 | tf_op jit(solution)/shard_map/ppermute | solution.py:23
  64.6 1.5 collective-permute-start.9
  66.1 1.7 %bitcast_dynamic-update-slice_fusion = (f32[1,8,64,2048]{3,2,1,0:T(8,128)S(1)}, bf16[2,1,64,2048]{3,2,0,1:T(8,128)(2,1)S(1)}) fusion(f32[1,8,64,2048]{3,2,1,0:T(8,128)S(1)} %get-tuple-element.29, s32[]{:T(128)S(6)} %select_n.138, bf16[2,1,64,2048]{3,2,0,1:T(8,128)(2,1)S(1)} %collective-permute-done.8, f32[]{:T(128)S(6)} %sub.112, ...), kind=kLoop, calls=%fused_computation.8 | loop fusion | flops 3407872 | bytes 4718612 | tf_op jit(solution)/shard_map/dynamic_update_slice | solution.py:189
  68.0 7.1 %collective-permute-done.15.refs_4_ = bf16[1,64,2048]{2,1,0:T(8,128)(2,1)S(1)} collective-permute-done((bf16[1,64,2048]{2,1,0:T(8,128)(2,1)S(1)}, bf16[1,64,2048]{2,1,0:T(8,128)(2,1)S(1)}, u32[]{:S(2)}, u32[]{:S(2)}) %collective-permute-start.15) | collective-permute-done | bytes 262176 | tf_op jit(solution)/shard_map/ppermute | solution.py:23
  75.0 0.5 collective-permute-start.10
  75.5 5.1 %collective-permute-done.16.refs_5_ = bf16[1,64,2048]{2,1,0:T(8,128)(2,1)S(1)} collective-permute-done((bf16[1,64,2048]{2,1,0:T(8,128)(2,1)S(1)}, bf16[1,64,2048]{2,1,0:T(8,128)(2,1)S(1)}, u32[]{:S(2)}, u32[]{:S(2)}) %collective-permute-start.16) | collective-permute-done | bytes 262176 | tf_op jit(solution)/shard_map/ppermute | solution.py:23
  80.6 4.0 %collective-permute-done.12.refs_3_ = bf16[1,64,2048]{2,1,0:T(8,128)(2,1)S(1)} collective-permute-done((bf16[1,64,2048]{2,1,0:T(8,128)(2,1)S(1)}, bf16[1,64,2048]{2,1,0:T(8,128)(2,1)S(1)}, u32[]{:S(2)}, u32[]{:S(2)}) %collective-permute-start.12) | collective-permute-done | bytes 262176 | tf_op jit(solution)/shard_map/ppermute | solution.py:23
  84.6 5.5 %collective-permute-done.10.refs_1_ = bf16[1,64,2048]{2,1,0:T(8,128)(2,1)S(1)} collective-permute-done((bf16[1,64,2048]{2,1,0:T(8,128)(2,1)S(1)}, bf16[1,64,2048]{2,1,0:T(8,128)(2,1)S(1)}, u32[]{:S(2)}, u32[]{:S(2)}) %collective-permute-start.10) | collective-permute-done | bytes 262176 | tf_op jit(solution)/shard_map/ppermute | solution.py:23
  90.1 12.8 %orthogonalize.1 = (bf16[1,64,2048]{2,1,0:T(8,128)(2,1)S(1)}, bf16[1,64,2048]{2,1,0:T(8,128)(2,1)S(1)}, bf16[1,64,2048]{2,1,0:T(8,128)(2,1)S(1)}, bf16[1,64,2048...) custom-call(bf16[1,64,2048]{2,1,0:T(8,128)(2,1)S(1)} %get-tuple-elem, ...), custom_call_target="tpu_custom_call" | custom-call | flops 11005853696 | bytes 4194304 | tf_op jit(solution)/shard_map/orthogonalize/pallas_call | solution.py:102
  102.9 1.1 collective-permute-start.22
  104.0 1.1 collective-permute-start.21
  105.1 2.1 %collective-permute-start.24 = (bf16[1,64,2048]{2,1,0:T(8,128)(2,1)S(1)}, bf16[1,64,2048]{2,1,0:T(8,128)(2,1)S(1)}, u32[]{:S(2)}, u32[]{:S(2)}) collective-permute-start(bf16[1,64,2048]{2,1,0:T(8,128)(2,1)S(1)} %get-tuple-element.22), channel_id=1, source_target_pairs={{0,3},{1,2},{2,1},{3,0},{4,7},{5,6},{6,5},{7,4},{8,11},{9,10},{10,... | collective-permute-start | bytes 786440 | tf_op jit(solution)/shard_map/ppermute | solution.py:23
  107.3 9.7 %collective-permute-done.22 = bf16[1,64,2048]{2,1,0:T(8,128)(2,1)S(1)} collective-permute-done((bf16[1,64,2048]{2,1,0:T(8,128)(2,1)S(1)}, bf16[1,64,2048]{2,1,0:T(8,128)(2,1)S(1)}, u32[]{:S(2)}, u32[]{:S(2)}) %collective-permute-start.22) | collective-permute-done | bytes 262176 | tf_op jit(solution)/shard_map/ppermute | solution.py:23
  117.0 0.7 collective-permute-start.25
  117.6 0.2 reshape.498.clone
  118.0 3.6 %add_convert_fusion = bf16[8,1,64,2048]{3,2,1,0:T(8,128)(2,1)S(1)} fusion(bf16[8,1,64,2048]{3,2,1,0:T(8,128)(2,1)} %collective-permute-done.9, bf16[8,1,64,2048]{3,2,1,0:T(8,128)(2,1)} %add_convert_fusion.1, f32[]{:T(128)S(6)} %sub.112, f32[]{:T(128)} %bitcast), kind=kLoop, calls=%fused_computation | loop fusion | flops 6291456 | bytes 6291464 | tf_op jit(solution)/shard_map/convert_element_type | solution.py:198
  121.6 3.1 %collective-permute-start.27 = (bf16[1,64,2048]{2,1,0:T(8,128)(2,1)S(1)}, bf16[1,64,2048]{2,1,0:T(8,128)(2,1)S(1)}, u32[]{:S(2)}, u32[]{:S(2)}) collective-permute-start(bf16[1,64,2048]{2,1,0:T(8,128)(2,1)S(1)} %get-tuple-element.25), channel_id=1, source_target_pairs={{0,4},{1,5},{2,6},{3,7},{4,0},{5,1},{6,2},{7,3},{8,12},{9,13},{10,... | collective-permute-start | bytes 786440 | tf_op jit(solution)/shard_map/ppermute | solution.py:23
  125.2 9.4 %collective-permute-done.24 = bf16[1,64,2048]{2,1,0:T(8,128)(2,1)S(1)} collective-permute-done((bf16[1,64,2048]{2,1,0:T(8,128)(2,1)S(1)}, bf16[1,64,2048]{2,1,0:T(8,128)(2,1)S(1)}, u32[]{:S(2)}, u32[]{:S(2)}) %collective-permute-start.24) | collective-permute-done | bytes 262176 | tf_op jit(solution)/shard_map/ppermute | solution.py:23
  134.8 11.0 %collective-permute-done.26 = bf16[1,64,2048]{2,1,0:T(8,128)(2,1)S(1)} collective-permute-done((bf16[1,64,2048]{2,1,0:T(8,128)(2,1)S(1)}, bf16[1,64,2048]{2,1,0:T(8,128)(2,1)S(1)}, u32[]{:S(2)}, u32[]{:S(2)}) %collective-permute-start.26) | collective-permute-done | bytes 262176 | tf_op jit(solution)/shard_map/ppermute | solution.py:23
  146.0 2.7 %collective-permute-done.27 = bf16[1,64,2048]{2,1,0:T(8,128)(2,1)S(1)} collective-permute-done((bf16[1,64,2048]{2,1,0:T(8,128)(2,1)S(1)}, bf16[1,64,2048]{2,1,0:T(8,128)(2,1)S(1)}, u32[]{:S(2)}, u32[]{:S(2)}) %collective-permute-start.27) | collective-permute-done | bytes 262176 | tf_op jit(solution)/shard_map/ppermute | solution.py:23
  148.9 1.3 copy-done.4
  150.2 0.7 copy-done.5
  (54 shorter events, 1.8 us)
Async XLA Ops:
  0.6 8.7 %copy-start.7 = (s32[4,2]{0,1:T(2,128)S(1)}, s32[4,2]{0,1:T(2,128)}, u32[]{:S(2)}) copy-start(s32[4,2]{0,1:T(2,128)} %param.9) | copy-start | bytes 100
  0.7 12.6 %copy-start.2 = (bf16[1,8,64,2048]{3,2,1,0:T(8,128)(2,1)S(1)}, bf16[1,8,64,2048]{3,2,1,0:T(8,128)(2,1)}, u32[]{:S(2)}) copy-start(bf16[1,8,64,2048]{3,2,1,0:T(8,128)(2,1)} %param.8) | copy-start | bytes 6291460
  2.8 9.6 %collective-permute-start.4 = (bf16[1,1,64,2048]{3,2,1,0:T(8,128)(2,1)}, bf16[1,1,64,2048]{3,2,1,0:T(8,128)(2,1)}, u32[]{:S(2)}, u32[]{:S(2)}) collective-permute-start(bf16[1,1,64,2048]{3,2,1,0:T(8,128)(2,1)} %get-tuple-element.41), channel_id=1, source_target_pairs={{0,8},{8,0},{16,24},{24,16},{1,9},{9,1},{17,25},{25,17},{2,10},{10... | collective-permute-start | bytes 786440 | tf_op jit(solution)/shard_map/ppermute | solution.py:23
  3.2 10.0 %collective-permute-start.5 = (bf16[1,1,64,2048]{3,2,1,0:T(8,128)(2,1)}, bf16[1,1,64,2048]{3,2,1,0:T(8,128)(2,1)}, u32[]{:S(2)}, u32[]{:S(2)}) collective-permute-start(bf16[1,1,64,2048]{3,2,1,0:T(8,128)(2,1)} %get-tuple-element.41), channel_id=1, source_target_pairs={{0,16},{8,24},{16,0},{24,8},{1,17},{9,25},{17,1},{25,9},{2,18},{10... | collective-permute-start | bytes 786440 | tf_op jit(solution)/shard_map/ppermute | solution.py:23
  5.7 6.1 %collective-permute-start.17 = (bf16[1,1,64,2048]{3,2,1,0:T(8,128)(2,1)S(1)}, bf16[1,1,64,2048]{3,2,1,0:T(8,128)(2,1)}, u32[]{:S(2)}, u32[]{:S(2)}) collective-permute-start(bf16[1,1,64,2048]{3,2,1,0:T(8,128)(2,1)S(1)} %get-tuple-element.40), channel_id=1, source_target_pairs={{0,8},{8,0},{16,24},{24,16},{1,9},{9,1},{17,25},{25,17},{2,10},{10... | collective-permute-start | bytes 786440 | tf_op jit(solution)/shard_map/ppermute | solution.py:23
  6.0 12.7 %collective-permute-start.18 = (bf16[1,1,64,2048]{3,2,1,0:T(8,128)(2,1)S(1)}, bf16[1,1,64,2048]{3,2,1,0:T(8,128)(2,1)}, u32[]{:S(2)}, u32[]{:S(2)}) collective-permute-start(bf16[1,1,64,2048]{3,2,1,0:T(8,128)(2,1)S(1)} %get-tuple-element.40), channel_id=1, source_target_pairs={{0,16},{8,24},{16,0},{24,8},{1,17},{9,25},{17,1},{25,9},{2,18},{10... | collective-permute-start | bytes 786440 | tf_op jit(solution)/shard_map/ppermute | solution.py:23
  9.3 12.3 %collective-permute-start.13 = (bf16[2,1,64,2048]{3,2,0,1:T(8,128)(2,1)}, bf16[2,1,64,2048]{3,2,0,1:T(8,128)(2,1)S(1)}, u32[]{:S(2)}, u32[]{:S(2)}) collective-permute-start(bf16[2,1,64,2048]{3,2,0,1:T(8,128)(2,1)} %get-tuple-element.37), channel_id=1, source_target_pairs={{0,8},{8,0},{16,24},{24,16},{1,9},{9,1},{17,25},{25,17},{2,10},{10... | collective-permute-start | bytes 1572872 | tf_op jit(solution)/shard_map/ppermute | solution.py:23
  11.8 14.7 %collective-permute-start.2 = (bf16[2,1,64,2048]{3,2,1,0:T(8,128)(2,1)}, bf16[2,1,64,2048]{3,2,1,0:T(8,128)(2,1)S(1)}, u32[]{:S(2)}, u32[]{:S(2)}) collective-permute-start(bf16[2,1,64,2048]{3,2,1,0:T(8,128)(2,1)} %get-tuple-element.36), channel_id=1, source_target_pairs={{0,8},{8,0},{16,24},{24,16},{1,9},{9,1},{17,25},{25,17},{2,10},{10... | collective-permute-start | bytes 1572872 | tf_op jit(solution)/shard_map/ppermute | solution.py:23
  12.4 19.5 %collective-permute-start = (bf16[8,1,64,2048]{3,2,1,0:T(8,128)(2,1)}, bf16[8,1,64,2048]{3,2,1,0:T(8,128)(2,1)S(1)}, u32[]{:S(2)}, u32[]{:S(2)}) collective-permute-start(bf16[8,1,64,2048]{3,2,1,0:T(8,128)(2,1)} %bitcast.175), channel_id=1, source_target_pairs={{0,8},{8,0},{16,24},{24,16},{1,9},{9,1},{17,25},{25,17},{2,10},{10... | collective-permute-start | bytes 6291464 | tf_op jit(solution)/shard_map/ppermute | solution.py:23
  13.2 5.4 %collective-permute-start.6 = (bf16[1,1,64,2048]{3,2,1,0:T(8,128)(2,1)}, bf16[1,1,64,2048]{3,2,1,0:T(8,128)(2,1)S(1)}, u32[]{:S(2)}, u32[]{:S(2)}) collective-permute-start(bf16[1,1,64,2048]{3,2,1,0:T(8,128)(2,1)} %collective-permute-done.5), channel_id=1, source_target_pairs={{0,8},{8,0},{16,24},{24,16},{1,9},{9,1},{17,25},{25,17},{2,10},{10... | collective-permute-start | bytes 786440 | tf_op jit(solution)/shard_map/ppermute | solution.py:23
  18.6 7.9 %copy-start = (f32[1,8,64,2048]{3,2,1,0:T(8,128)S(1)}, f32[1,8,64,2048]{3,2,1,0:T(8,128)}, u32[]{:S(2)}) copy-start(f32[1,8,64,2048]{3,2,1,0:T(8,128)} %param.6) | copy-start | bytes 12582916
  18.6 12.4 %collective-permute-start.1 = (bf16[2,1,64,2048]{3,2,0,1:T(8,128)(2,1)S(1)}, bf16[2,1,64,2048]{3,2,0,1:T(8,128)(2,1)S(1)}, u32[]{:S(2)}, u32[]{:S(2)}) collective-permute-start(bf16[2,1,64,2048]{3,2,0,1:T(8,128)(2,1)S(1)} %get-tuple-element.35), channel_id=1, source_target_pairs={{0,8},{8,0},{16,24},{24,16},{1,9},{9,1},{17,25},{25,17},{2,10},{10... | collective-permute-start | bytes 1572872 | tf_op jit(solution)/shard_map/ppermute | solution.py:23
  18.7 10.4 %collective-permute-start.19 = (bf16[1,1,64,2048]{3,2,1,0:T(8,128)(2,1)}, bf16[1,1,64,2048]{3,2,1,0:T(8,128)(2,1)S(1)}, u32[]{:S(2)}, u32[]{:S(2)}) collective-permute-start(bf16[1,1,64,2048]{3,2,1,0:T(8,128)(2,1)} %collective-permute-done.18), channel_id=1, source_target_pairs={{0,8},{8,0},{16,24},{24,16},{1,9},{9,1},{17,25},{25,17},{2,10},{10... | collective-permute-start | bytes 786440 | tf_op jit(solution)/shard_map/ppermute | solution.py:23
  21.6 13.7 %collective-permute-start.7 = (bf16[1,64,2048]{2,1,0:T(8,128)(2,1)S(1)}, bf16[1,64,2048]{2,1,0:T(8,128)(2,1)S(1)}, u32[]{:S(2)}, u32[]{:S(2)}) collective-permute-start(bf16[1,64,2048]{2,1,0:T(8,128)(2,1)S(1)} %get-tuple-element.50), channel_id=1, source_target_pairs={{0,7},{1,6},{2,5},{3,4},{4,3},{5,2},{6,1},{7,0},{8,15},{9,14},{10,... | collective-permute-start | bytes 786440 | tf_op jit(solution)/shard_map/ppermute | solution.py:23
  27.5 5.0 %copy-start.6 = (bf16[1,8,64,2048]{3,2,1,0:T(8,128)(2,1)S(1)}, bf16[1,8,64,2048]{3,2,1,0:T(8,128)(2,1)}, u32[]{:S(2)}) copy-start(bf16[1,8,64,2048]{3,2,1,0:T(8,128)(2,1)} %param.5) | copy-start | bytes 6291460
  27.5 27.8 %collective-permute-start.14 = (bf16[2,1,64,2048]{3,2,1,0:T(8,128)(2,1)S(1)}, bf16[2,1,64,2048]{3,2,1,0:T(8,128)(2,1)S(1)}, u32[]{:S(2)}, u32[]{:S(2)}) collective-permute-start(bf16[2,1,64,2048]{3,2,1,0:T(8,128)(2,1)S(1)} %get-tuple-element.38), channel_id=1, source_target_pairs={{0,16},{8,24},{16,0},{24,8},{1,17},{9,25},{17,1},{25,9},{2,18},{10... | collective-permute-start | bytes 1572872 | tf_op jit(solution)/shard_map/ppermute | solution.py:23
  30.8 37.1 %collective-permute-start.20 = (bf16[1,64,2048]{2,1,0:T(8,128)(2,1)S(1)}, bf16[1,64,2048]{2,1,0:T(8,128)(2,1)S(1)}, u32[]{:S(2)}, u32[]{:S(2)}) collective-permute-start(bf16[1,64,2048]{2,1,0:T(8,128)(2,1)S(1)} %get-tuple-element.42), channel_id=1, source_target_pairs={{0,6},{1,7},{2,4},{3,5},{4,2},{5,3},{6,0},{7,1},{8,14},{9,15},{10,... | collective-permute-start | bytes 786440 | tf_op jit(solution)/shard_map/ppermute | solution.py:23
  31.9 21.8 %copy-start.3 = (bf16[1,8,64,2048]{3,2,1,0:T(8,128)(2,1)S(1)}, bf16[1,8,64,2048]{3,2,1,0:T(8,128)(2,1)}, u32[]{:S(2)}) copy-start(bf16[1,8,64,2048]{3,2,1,0:T(8,128)(2,1)} %param.7) | copy-start | bytes 6291460
  31.9 20.3 %collective-permute-start.3 = (bf16[2,1,64,2048]{3,2,1,0:T(8,128)(2,1)S(1)}, bf16[2,1,64,2048]{3,2,1,0:T(8,128)(2,1)S(1)}, u32[]{:S(2)}, u32[]{:S(2)}) collective-permute-start(bf16[2,1,64,2048]{3,2,1,0:T(8,128)(2,1)S(1)} %get-tuple-element.15), channel_id=1, source_target_pairs={{0,16},{8,24},{16,0},{24,8},{1,17},{9,25},{17,1},{25,9},{2,18},{10... | collective-permute-start | bytes 1572872 | tf_op jit(solution)/shard_map/ppermute | solution.py:23
  52.2 12.5 %collective-permute-start.8 = (bf16[2,1,64,2048]{3,2,0,1:T(8,128)(2,1)S(1)}, bf16[2,1,64,2048]{3,2,0,1:T(8,128)(2,1)S(1)}, u32[]{:S(2)}, u32[]{:S(2)}) collective-permute-start(bf16[2,1,64,2048]{3,2,0,1:T(8,128)(2,1)S(1)} %fusion.3), channel_id=1, source_target_pairs={{0,16},{8,24},{16,0},{24,8},{1,17},{9,25},{17,1},{25,9},{2,18},{10... | collective-permute-start | bytes 1572872 | tf_op jit(solution)/shard_map/ppermute | solution.py:23
  57.1 18.0 %collective-permute-start.15 = (bf16[1,64,2048]{2,1,0:T(8,128)(2,1)S(1)}, bf16[1,64,2048]{2,1,0:T(8,128)(2,1)S(1)}, u32[]{:S(2)}, u32[]{:S(2)}) collective-permute-start(bf16[1,64,2048]{2,1,0:T(8,128)(2,1)S(1)} %get-tuple-element.45), channel_id=1, source_target_pairs={{0,4},{1,5},{2,6},{3,7},{4,0},{5,1},{6,2},{7,3},{8,12},{9,13},{10,... | collective-permute-start | bytes 786440 | tf_op jit(solution)/shard_map/ppermute | solution.py:23
  57.2 23.4 %collective-permute-start.16 = (bf16[1,64,2048]{2,1,0:T(8,128)(2,1)S(1)}, bf16[1,64,2048]{2,1,0:T(8,128)(2,1)S(1)}, u32[]{:S(2)}, u32[]{:S(2)}) collective-permute-start(bf16[1,64,2048]{2,1,0:T(8,128)(2,1)S(1)} %get-tuple-element.44), channel_id=1, source_target_pairs={{0,5},{1,4},{2,7},{3,6},{4,1},{5,0},{6,3},{7,2},{8,13},{9,12},{10,... | collective-permute-start | bytes 786440 | tf_op jit(solution)/shard_map/ppermute | solution.py:23
  60.1 20.5 %collective-permute-start.11 = (bf16[1,64,2048]{2,1,0:T(8,128)(2,1)S(1)}, bf16[1,64,2048]{2,1,0:T(8,128)(2,1)S(1)}, u32[]{:S(2)}, u32[]{:S(2)}) collective-permute-start(bf16[1,64,2048]{2,1,0:T(8,128)(2,1)S(1)} %get-tuple-element.47), channel_id=1, source_target_pairs={{0,2},{1,3},{2,0},{3,1},{4,6},{5,7},{6,4},{7,5},{8,10},{9,11},{10,... | collective-permute-start | bytes 786440 | tf_op jit(solution)/shard_map/ppermute | solution.py:23
  64.6 53.3 %collective-permute-start.9 = (bf16[8,1,64,2048]{3,2,1,0:T(8,128)(2,1)}, bf16[8,1,64,2048]{3,2,1,0:T(8,128)(2,1)}, u32[]{:S(2)}, u32[]{:S(2)}) collective-permute-start(bf16[8,1,64,2048]{3,2,1,0:T(8,128)(2,1)} %add_convert_fusion.1), channel_id=1, source_target_pairs={{0,16},{8,24},{16,0},{24,8},{1,17},{9,25},{17,1},{25,9},{2,18},{10... | collective-permute-start | bytes 6291464 | tf_op jit(solution)/shard_map/ppermute | solution.py:23
  67.8 22.3 %copy-start.1 = (f32[1,8,64,2048]{3,2,1,0:T(8,128)}, f32[1,8,64,2048]{3,2,1,0:T(8,128)S(1)}, u32[]{:S(2)}) copy-start(f32[1,8,64,2048]{3,2,1,0:T(8,128)S(1)} %get-tuple-element.27) | copy-start | bytes 12582916
  67.9 16.7 %collective-permute-start.12 = (bf16[1,64,2048]{2,1,0:T(8,128)(2,1)S(1)}, bf16[1,64,2048]{2,1,0:T(8,128)(2,1)S(1)}, u32[]{:S(2)}, u32[]{:S(2)}) collective-permute-start(bf16[1,64,2048]{2,1,0:T(8,128)(2,1)S(1)} %get-tuple-element.46), channel_id=1, source_target_pairs={{0,3},{1,2},{2,1},{3,0},{4,7},{5,6},{6,5},{7,4},{8,11},{9,10},{10,... | collective-permute-start | bytes 786440 | tf_op jit(solution)/shard_map/ppermute | solution.py:23
  75.0 15.1 %collective-permute-start.10 = (bf16[1,64,2048]{2,1,0:T(8,128)(2,1)S(1)}, bf16[1,64,2048]{2,1,0:T(8,128)(2,1)S(1)}, u32[]{:S(2)}, u32[]{:S(2)}) collective-permute-start(bf16[1,64,2048]{2,1,0:T(8,128)(2,1)S(1)} %get-tuple-element.48), channel_id=1, source_target_pairs={{0,1},{1,0},{2,3},{3,2},{4,5},{5,4},{6,7},{7,6},{8,9},{9,8},{10,11... | collective-permute-start | bytes 786440 | tf_op jit(solution)/shard_map/ppermute | solution.py:23
  102.9 14.0 %collective-permute-start.22 = (bf16[1,64,2048]{2,1,0:T(8,128)(2,1)S(1)}, bf16[1,64,2048]{2,1,0:T(8,128)(2,1)S(1)}, u32[]{:S(2)}, u32[]{:S(2)}) collective-permute-start(bf16[1,64,2048]{2,1,0:T(8,128)(2,1)S(1)} %get-tuple-element.20), channel_id=1, source_target_pairs={{0,1},{1,0},{2,3},{3,2},{4,5},{5,4},{6,7},{7,6},{8,9},{9,8},{10,11... | collective-permute-start | bytes 786440 | tf_op jit(solution)/shard_map/ppermute | solution.py:23
  104.0 17.6 %collective-permute-start.21 = (bf16[1,64,2048]{2,1,0:T(8,128)(2,1)S(1)}, bf16[1,64,2048]{2,1,0:T(8,128)(2,1)S(1)}, u32[]{:S(2)}, u32[]{:S(2)}) collective-permute-start(bf16[1,64,2048]{2,1,0:T(8,128)(2,1)S(1)} %get-tuple-element.18), channel_id=1, source_target_pairs={{0,7},{1,6},{2,5},{3,4},{4,3},{5,2},{6,1},{7,0},{8,15},{9,14},{10,... | collective-permute-start | bytes 786440 | tf_op jit(solution)/shard_map/ppermute | solution.py:23
  105.1 19.9 %collective-permute-start.23 = (bf16[1,64,2048]{2,1,0:T(8,128)(2,1)S(1)}, bf16[1,64,2048]{2,1,0:T(8,128)(2,1)S(1)}, u32[]{:S(2)}, u32[]{:S(2)}) collective-permute-start(bf16[1,64,2048]{2,1,0:T(8,128)(2,1)S(1)} %get-tuple-element.21), channel_id=1, source_target_pairs={{0,2},{1,3},{2,0},{3,1},{4,6},{5,7},{6,4},{7,5},{8,10},{9,11},{10,... | collective-permute-start | bytes 786440 | tf_op jit(solution)/shard_map/ppermute | solution.py:23
  105.1 29.4 %collective-permute-start.24 = (bf16[1,64,2048]{2,1,0:T(8,128)(2,1)S(1)}, bf16[1,64,2048]{2,1,0:T(8,128)(2,1)S(1)}, u32[]{:S(2)}, u32[]{:S(2)}) collective-permute-start(bf16[1,64,2048]{2,1,0:T(8,128)(2,1)S(1)} %get-tuple-element.22), channel_id=1, source_target_pairs={{0,3},{1,2},{2,1},{3,0},{4,7},{5,6},{6,5},{7,4},{8,11},{9,10},{10,... | collective-permute-start | bytes 786440 | tf_op jit(solution)/shard_map/ppermute | solution.py:23
  117.0 17.8 %collective-permute-start.25 = (bf16[1,64,2048]{2,1,0:T(8,128)(2,1)S(1)}, bf16[1,64,2048]{2,1,0:T(8,128)(2,1)S(1)}, u32[]{:S(2)}, u32[]{:S(2)}) collective-permute-start(bf16[1,64,2048]{2,1,0:T(8,128)(2,1)S(1)} %get-tuple-element.23), channel_id=1, source_target_pairs={{0,6},{1,7},{2,4},{3,5},{4,2},{5,3},{6,0},{7,1},{8,14},{9,15},{10,... | collective-permute-start | bytes 786440 | tf_op jit(solution)/shard_map/ppermute | solution.py:23
  117.9 28.0 %collective-permute-start.26 = (bf16[1,64,2048]{2,1,0:T(8,128)(2,1)S(1)}, bf16[1,64,2048]{2,1,0:T(8,128)(2,1)S(1)}, u32[]{:S(2)}, u32[]{:S(2)}) collective-permute-start(bf16[1,64,2048]{2,1,0:T(8,128)(2,1)S(1)} %get-tuple-element.24), channel_id=1, source_target_pairs={{0,5},{1,4},{2,7},{3,6},{4,1},{5,0},{6,3},{7,2},{8,13},{9,12},{10,... | collective-permute-start | bytes 786440 | tf_op jit(solution)/shard_map/ppermute | solution.py:23
  121.6 27.0 %collective-permute-start.27 = (bf16[1,64,2048]{2,1,0:T(8,128)(2,1)S(1)}, bf16[1,64,2048]{2,1,0:T(8,128)(2,1)S(1)}, u32[]{:S(2)}, u32[]{:S(2)}) collective-permute-start(bf16[1,64,2048]{2,1,0:T(8,128)(2,1)S(1)} %get-tuple-element.25), channel_id=1, source_target_pairs={{0,4},{1,5},{2,6},{3,7},{4,0},{5,1},{6,2},{7,3},{8,12},{9,13},{10,... | collective-permute-start | bytes 786440 | tf_op jit(solution)/shard_map/ppermute | solution.py:23
  148.9 1.3 copy-start.4
  148.9 2.0 %copy-start.5 = (bf16[1,8,64,2048]{3,2,1,0:T(8,128)(2,1)}, bf16[1,8,64,2048]{3,2,1,0:T(8,128)(2,1)S(1)}, u32[]{:S(2)}) copy-start(bf16[1,8,64,2048]{3,2,1,0:T(8,128)(2,1)S(1)} %get-tuple-element.52) | copy-start | bytes 6291460

commit v13 on v12

--- a/solution.py
+++ b/solution.py
@@ -151,6 +151,7 @@
 
     weight_near = swapped(weight, "rep", 1)
     arrived = []
+    mixes = []
     new_tracker = jnp.zeros(shape, F32)
     blocks = [None] * shards
     for turn, runs in enumerate(grouped(shards)):
@@ -171,7 +172,7 @@
             if turn == 2:
                 sent = after(sent, weight_near)
             elif turn == 4:
-                sent = after(sent, arrived[turn - 2], blocks[7 * shards // 8])
+                sent = after(sent, arrived[2], blocks[7 * shards // 8])
             far = swapped(sent, "rep", 2)
             far_mixed = far.astype(F32)
         arrived.append(far)
@@ -186,7 +187,11 @@
             for offset in reversed(range(lowest, lowest + length)):
                 block = taken(group, (here ^ offset) % length, 1)[0].astype(BF16)
                 blocks[offset] = swapped(block, "shard", offset) if offset else block
-            new_tracker = lax.dynamic_update_slice_in_dim(new_tracker, group, start, axis=0)
+            mixes.append((group, start))
+
+    for turn in (0, 1, 3, 2, 4):
+        group, start = mixes[turn]
+        new_tracker = lax.dynamic_update_slice_in_dim(new_tracker, group, start, axis=0)
 
     weight_own = (
         first * weight.astype(F32) + (1.0 - first) * weight_near.astype(F32)

time: 151 us -> 146 us (0.967)
  waiting for transfers between devices: 79 us -> 70.7 us
  starting transfers between devices: 26.7 us -> 29.3 us
    ppermute x28, waiting for transfers between devices: 79 us -> 70.7 us  [swapped(): lax.ppermute(values, axis, [(i, i ^ offset) for i in range(lax.axis_size(...]
    ppermute x28, starting transfers between devices: 26.7 us -> 29.3 us  [swapped(): lax.ppermute(values, axis, [(i, i ^ offset) for i in range(lax.axis_size(...]
  transfers between devices with their start and end apart: 28 -> 28, of which waited for: 12 -> 13; matrix products, arithmetic and copies ran while one was open for 17% -> 17% of each run, Pallas kernels for 8% -> 9%
where the time goes in v13:
time: 146 us; the launch traced here: 145 us
  waiting for transfers between devices  70.7 us (48%)
  starting transfers between devices  29.3 us (20%)
  other arithmetic  20.8 us (14%)
  Pallas kernels  12.8 us (9%)
  local copies, waits for them, and re-layouts  8.99 us (6%)
  between operations  2.8 us (2%)
    ppermute x28, waiting for transfers between devices, swapped(): lax.ppermute(values, axis, [(i, i ^ offset) for i in range(lax.axis_size(...  70.7 us
    ppermute x28, starting transfers between devices, swapped(): lax.ppermute(values, axis, [(i, i ^ offset) for i in range(lax.axis_size(...  29.3 us
    pallas_call x1, Pallas kernels, orthogonalize(): pl.pallas_call(body, grid=(each,), in_specs=[block] * count, out_specs=[b...  12.8 us
    convert_element_type x2, local copies, waits for them, and re-layouts, local(): rounded = own.astype(BF16)  5.18 us
    dynamic_update_slice x3, other arithmetic, local(): lax.dynamic_update_slice_in_dim(new_tracker, group, start, axis=0)  5.13 us
    convert_element_type x2, other arithmetic, local(): block = taken(group, (here ^ offset) % length, 1)[0].astype(BF16)  3.67 us
    convert_element_type x1, other arithmetic, local(): mixed_weight = (second * weight_own.astype(F32) + (1.0 - second) * weight...  3.64 us
    add x1, other arithmetic, local(): second * mixed  3 us
  transfers between devices with their start and end apart: 28, of which 13 were waited for; matrix products, arithmetic and copies ran while one was open for 17% of the time, Pallas kernels for 9%

profile of v13, /device:TPU:0, one launch (start us, length us, event | category | flops | bytes accessed | tf_op | source)
XLA Modules:
  0.0 145.4 jit_solution(6978720992207935478)
XLA Ops:
  0.7 2.1 %dynamic-slice_convert_fusion.9 = (bf16[1,1,64,2048]{3,2,1,0:T(8,128)(2,1)S(1)}, bf16[1,1,64,2048]{3,2,1,0:T(8,128)(2,1)}) fusion(f32[1,8,64,2048]{3,2,1,0:T(8,128)} %param.6, s32[]{:T(128)S(6)} %select_n.157, s32[]{:T(128)S(6)} %select_n.141), kind=kLoop, calls=%fused_computation.53 | loop fusion | bytes 1048584 | tf_op jit(solution)/shard_map/convert_element_type | solution.py:165
  2.8 0.5 collective-permute-start.4
  3.2 2.5 %collective-permute-start.5 = (bf16[1,1,64,2048]{3,2,1,0:T(8,128)(2,1)}, bf16[1,1,64,2048]{3,2,1,0:T(8,128)(2,1)}, u32[]{:S(2)}, u32[]{:S(2)}) collective-permute-start(bf16[1,1,64,2048]{3,2,1,0:T(8,128)(2,1)} %get-tuple-element.41), channel_id=1, source_target_pairs={{0,16},{8,24},{16,0},{24,8},{1,17},{9,25},{17,1},{25,9},{2,18},{10... | collective-permute-start | bytes 786440 | tf_op jit(solution)/shard_map/ppermute | solution.py:23
  6.2 3.1 %fusion.6 = (bf16[2,1,64,2048]{3,2,0,1:T(8,128)(2,1)S(1)}, bf16[2,1,64,2048]{3,2,1,0:T(8,128)(2,1)}, bf16[2,1,64,2048]{3,2,0,1:T(8,128)(2,1)}) fusion(f32[1,8,64,2048]{3,2,1,0:T(8,128)} %param.6, s32[]{:T(128)S(6)} %select_n.138, s32[]{:T(128)S(6)} %select_n.140, s32[]{:T(128)S(6)} %select_n.152), kind=kLoop, calls=%fused_computation.24 | loop fusion | bytes 3145740 | tf_op jit(solution)/shard_map/convert_element_type | solution.py:165
  9.3 0.7 constant_dynamic-slice_fusion
  11.8 0.6 collective-permute-start.2
  12.5 0.7 collective-permute-done.5
  13.2 3.0 %subtract_add_fusion = (f32[1,1,64,2048]{3,2,1,0:T(8,128)S(1)}, f32[1,1,64,2048]{3,2,1,0:T(8,128)S(1)}) fusion(bf16[1,1,64,2048]{3,2,1,0:T(8,128)(2,1)} %collective-permute-done.17, f32[1,8,64,2048]{3,2,1,0:T(8,128)} %param.6, s32[]{:T(128)S(6)} %select_n.157, bf16[1,8,64,2048]{3,2,1,0:T(8,128)(2,1)S(1)} %copy-done.2, bf16[1,8,64,2048]{3,2,1,0:T(8,128)(2,1)} %param.7, ...), kind=kLoop, calls=%fused_computation.44 | loop fusion | flops 2359296 | bytes 3670036 | tf_op jit(solution)/shard_map/add | solution.py:179
  16.2 2.4 %collective-permute-done.18 = bf16[1,1,64,2048]{3,2,1,0:T(8,128)(2,1)} collective-permute-done((bf16[1,1,64,2048]{3,2,1,0:T(8,128)(2,1)S(1)}, bf16[1,1,64,2048]{3,2,1,0:T(8,128)(2,1)}, u32[]{:S(2)}, u32[]{:S(2)}) %collective-permute-start.18) | collective-permute-done | bytes 262176 | tf_op jit(solution)/shard_map/ppermute | solution.py:23
  18.7 0.5 collective-permute-start.19
  19.2 0.5 reshape.500
  19.7 2.0 %convert_bitcast_fusion.1 = (bf16[1,64,2048]{2,1,0:T(8,128)(2,1)S(1)}, f32[1,8,64,2048]{3,2,1,0:T(8,128)S(1)}) fusion(f32[1,1,64,2048]{3,2,1,0:T(8,128)S(1)} %get-tuple-element.34, bf16[1,1,64,2048]{3,2,1,0:T(8,128)(2,1)S(1)} %collective-permute-done.6, f32[]{:T(128)S(6)} %sub.113, bf16[1,1,64,2048]{3,2,1,0:T(8,128)(2,1)} %collective-permute-done.5, ...), kind=kLoop, calls=%fused_computation.86 | loop fusion | flops 1048576 | bytes 1835024 | tf_op jit(solution)/shard_map/convert_element_type | solution.py:188
  21.6 4.9 %collective-permute-start.7 = (bf16[1,64,2048]{2,1,0:T(8,128)(2,1)S(1)}, bf16[1,64,2048]{2,1,0:T(8,128)(2,1)S(1)}, u32[]{:S(2)}, u32[]{:S(2)}) collective-permute-start(bf16[1,64,2048]{2,1,0:T(8,128)(2,1)S(1)} %get-tuple-element.50), channel_id=1, source_target_pairs={{0,7},{1,6},{2,5},{3,4},{4,3},{5,2},{6,1},{7,0},{8,15},{9,14},{10,... | collective-permute-start | bytes 786440 | tf_op jit(solution)/shard_map/ppermute | solution.py:23
  26.5 1.0 fusion.4
  27.5 1.6 %collective-permute-start.14 = (bf16[2,1,64,2048]{3,2,1,0:T(8,128)(2,1)S(1)}, bf16[2,1,64,2048]{3,2,1,0:T(8,128)(2,1)S(1)}, u32[]{:S(2)}, u32[]{:S(2)}) collective-permute-start(bf16[2,1,64,2048]{3,2,1,0:T(8,128)(2,1)S(1)} %get-tuple-element.39), channel_id=1, source_target_pairs={{0,16},{8,24},{16,0},{24,8},{1,17},{9,25},{17,1},{25,9},{2,18},{10... | collective-permute-start | bytes 1572872 | tf_op jit(solution)/shard_map/ppermute | solution.py:23
  29.1 1.7 %convert_bitcast_fusion = (bf16[1,64,2048]{2,1,0:T(8,128)(2,1)S(1)}, f32[1,8,64,2048]{3,2,1,0:T(8,128)S(1)}) fusion(f32[1,1,64,2048]{3,2,1,0:T(8,128)S(1)} %get-tuple-element.33, bf16[1,1,64,2048]{3,2,1,0:T(8,128)(2,1)S(1)} %collective-permute-done.19, f32[]{:T(128)S(6)} %sub.113, bf16[1,1,64,2048]{3,2,1,0:T(8,128)(2,1)} %collective-permute-done.18, ...), kind=kLoop, calls=%fused_computation.85 | loop fusion | flops 1048576 | bytes 1835024 | tf_op jit(solution)/shard_map/convert_element_type | solution.py:188
  30.8 0.3 collective-permute-start.20
  31.1 0.8 fusion.3
  31.9 9.1 %collective-permute-done.14 = bf16[2,1,64,2048]{3,2,1,0:T(8,128)(2,1)S(1)} collective-permute-done((bf16[2,1,64,2048]{3,2,1,0:T(8,128)(2,1)S(1)}, bf16[2,1,64,2048]{3,2,1,0:T(8,128)(2,1)S(1)}, u32[]{:S(2)}, u32[]{:S(2)}) %collective-permute-start.14) | collective-permute-done | bytes 524320 | tf_op jit(solution)/shard_map/ppermute | solution.py:23
  40.9 1.8 %bitcast_dynamic-update-slice_fusion.2 = (f32[1,8,64,2048]{3,2,1,0:T(8,128)S(1)}, bf16[2,1,64,2048]{3,2,1,0:T(8,128)(2,1)S(1)}) fusion(f32[1,8,64,2048]{3,2,1,0:T(8,128)S(1)} %get-tuple-element.43, s32[]{:T(128)S(6)} %select_n.152, bf16[2,1,64,2048]{3,2,1,0:T(8,128)(2,1)S(1)} %collective-permute-done.14, f32[]{:T(128)S(6)} %sub.112, ...), kind=kLoop, calls=%fused_computation.10 | loop fusion | flops 3407872 | bytes 4718612 | tf_op jit(solution)/shard_map/dynamic_update_slice | solution.py:194
  42.9 2.9 %collective-permute-start.16 = (bf16[1,64,2048]{2,1,0:T(8,128)(2,1)S(1)}, bf16[1,64,2048]{2,1,0:T(8,128)(2,1)S(1)}, u32[]{:S(2)}, u32[]{:S(2)}) collective-permute-start(bf16[1,64,2048]{2,1,0:T(8,128)(2,1)S(1)} %get-tuple-element.44), channel_id=1, source_target_pairs={{0,5},{1,4},{2,7},{3,6},{4,1},{5,0},{6,3},{7,2},{8,13},{9,12},{10,... | collective-permute-start | bytes 786440 | tf_op jit(solution)/shard_map/ppermute | solution.py:23
  45.8 1.5 %collective-permute-start.3 = (bf16[2,1,64,2048]{3,2,1,0:T(8,128)(2,1)S(1)}, bf16[2,1,64,2048]{3,2,1,0:T(8,128)(2,1)S(1)}, u32[]{:S(2)}, u32[]{:S(2)}) collective-permute-start(bf16[2,1,64,2048]{3,2,1,0:T(8,128)(2,1)S(1)} %get-tuple-element.15), channel_id=1, source_target_pairs={{0,16},{8,24},{16,0},{24,8},{1,17},{9,25},{17,1},{25,9},{2,18},{10... | collective-permute-start | bytes 1572872 | tf_op jit(solution)/shard_map/ppermute | solution.py:23
  47.2 2.8 %add_convert_fusion.1 = bf16[8,1,64,2048]{3,2,1,0:T(8,128)(2,1)} fusion(bf16[8,1,64,2048]{3,2,1,0:T(8,128)(2,1)S(1)} %collective-permute-done, f32[]{:T(128)S(6)} %sub.108, f32[]{:T(128)} %bitcast.1, bf16[1,8,64,2048]{3,2,1,0:T(8,128)(2,1)S(1)} %copy-done.6), kind=kLoop, calls=%fused_computation.1 | loop fusion | flops 6291456 | bytes 6291464 | tf_op jit(solution)/shard_map/convert_element_type | solution.py:198
  50.1 7.8 %collective-permute-done.3 = bf16[2,1,64,2048]{3,2,1,0:T(8,128)(2,1)S(1)} collective-permute-done((bf16[2,1,64,2048]{3,2,1,0:T(8,128)(2,1)S(1)}, bf16[2,1,64,2048]{3,2,1,0:T(8,128)(2,1)S(1)}, u32[]{:S(2)}, u32[]{:S(2)}) %collective-permute-start.3) | collective-permute-done | bytes 524320 | tf_op jit(solution)/shard_map/ppermute | solution.py:23
  57.8 1.5 %collective-permute-start.8 = (bf16[2,1,64,2048]{3,2,0,1:T(8,128)(2,1)S(1)}, bf16[2,1,64,2048]{3,2,0,1:T(8,128)(2,1)S(1)}, u32[]{:S(2)}, u32[]{:S(2)}) collective-permute-start(bf16[2,1,64,2048]{3,2,0,1:T(8,128)(2,1)S(1)} %fusion.3), channel_id=1, source_target_pairs={{0,16},{8,24},{16,0},{24,8},{1,17},{9,25},{17,1},{25,9},{2,18},{10... | collective-permute-start | bytes 1572872 | tf_op jit(solution)/shard_map/ppermute | solution.py:23
  59.3 1.7 %bitcast_dynamic-update-slice_fusion.1 = (f32[1,8,64,2048]{3,2,1,0:T(8,128)S(1)}, bf16[2,1,64,2048]{3,2,1,0:T(8,128)(2,1)S(1)}) fusion(f32[1,8,64,2048]{3,2,1,0:T(8,128)S(1)} %get-tuple-element.31, s32[]{:T(128)S(6)} %select_n.140, bf16[2,1,64,2048]{3,2,1,0:T(8,128)(2,1)S(1)} %collective-permute-done.3, f32[]{:T(128)S(6)} %sub.112, ...), kind=kLoop, calls=%fused_computation.9 | loop fusion | flops 3407872 | bytes 4718612 | tf_op jit(solution)/shard_map/dynamic_update_slice | solution.py:194
  61.1 8.6 %collective-permute-done.8 = bf16[2,1,64,2048]{3,2,0,1:T(8,128)(2,1)S(1)} collective-permute-done((bf16[2,1,64,2048]{3,2,0,1:T(8,128)(2,1)S(1)}, bf16[2,1,64,2048]{3,2,0,1:T(8,128)(2,1)S(1)}, u32[]{:S(2)}, u32[]{:S(2)}) %collective-permute-start.8) | collective-permute-done | bytes 524320 | tf_op jit(solution)/shard_map/ppermute | solution.py:23
  69.7 1.5 %collective-permute-start.9 = (bf16[8,1,64,2048]{3,2,1,0:T(8,128)(2,1)}, bf16[8,1,64,2048]{3,2,1,0:T(8,128)(2,1)}, u32[]{:S(2)}, u32[]{:S(2)}) collective-permute-start(bf16[8,1,64,2048]{3,2,1,0:T(8,128)(2,1)} %add_convert_fusion.1), channel_id=1, source_target_pairs={{0,16},{8,24},{16,0},{24,8},{1,17},{9,25},{17,1},{25,9},{2,18},{10... | collective-permute-start | bytes 6291464 | tf_op jit(solution)/shard_map/ppermute | solution.py:23
  71.2 1.7 %bitcast_dynamic-update-slice_fusion = (f32[1,8,64,2048]{3,2,1,0:T(8,128)S(1)}, bf16[2,1,64,2048]{3,2,0,1:T(8,128)(2,1)S(1)}) fusion(f32[1,8,64,2048]{3,2,1,0:T(8,128)S(1)} %get-tuple-element.29, s32[]{:T(128)S(6)} %select_n.138, bf16[2,1,64,2048]{3,2,0,1:T(8,128)(2,1)S(1)} %collective-permute-done.8, f32[]{:T(128)S(6)} %sub.112, ...), kind=kLoop, calls=%fused_computation.8 | loop fusion | flops 3407872 | bytes 4718612 | tf_op jit(solution)/shard_map/dynamic_update_slice | solution.py:194
  73.0 0.6 collective-permute-start.12
  73.5 1.1 collective-permute-start.10
  74.6 2.4 %collective-permute-done.11.refs_2_ = bf16[1,64,2048]{2,1,0:T(8,128)(2,1)S(1)} collective-permute-done((bf16[1,64,2048]{2,1,0:T(8,128)(2,1)S(1)}, bf16[1,64,2048]{2,1,0:T(8,128)(2,1)S(1)}, u32[]{:S(2)}, u32[]{:S(2)}) %collective-permute-start.11) | collective-permute-done | bytes 262176 | tf_op jit(solution)/shard_map/ppermute | solution.py:23
  77.1 5.5 %collective-permute-done.12.refs_3_ = bf16[1,64,2048]{2,1,0:T(8,128)(2,1)S(1)} collective-permute-done((bf16[1,64,2048]{2,1,0:T(8,128)(2,1)S(1)}, bf16[1,64,2048]{2,1,0:T(8,128)(2,1)S(1)}, u32[]{:S(2)}, u32[]{:S(2)}) %collective-permute-start.12) | collective-permute-done | bytes 262176 | tf_op jit(solution)/shard_map/ppermute | solution.py:23
  82.6 2.7 %collective-permute-done.10.refs_1_ = bf16[1,64,2048]{2,1,0:T(8,128)(2,1)S(1)} collective-permute-done((bf16[1,64,2048]{2,1,0:T(8,128)(2,1)S(1)}, bf16[1,64,2048]{2,1,0:T(8,128)(2,1)S(1)}, u32[]{:S(2)}, u32[]{:S(2)}) %collective-permute-start.10) | collective-permute-done | bytes 262176 | tf_op jit(solution)/shard_map/ppermute | solution.py:23
  85.3 12.8 %orthogonalize.1 = (bf16[1,64,2048]{2,1,0:T(8,128)(2,1)S(1)}, bf16[1,64,2048]{2,1,0:T(8,128)(2,1)S(1)}, bf16[1,64,2048]{2,1,0:T(8,128)(2,1)S(1)}, bf16[1,64,2048...) custom-call(bf16[1,64,2048]{2,1,0:T(8,128)(2,1)S(1)} %get-tuple-elem, ...), custom_call_target="tpu_custom_call" | custom-call | flops 11005853696 | bytes 4194304 | tf_op jit(solution)/shard_map/orthogonalize/pallas_call | solution.py:102
  98.1 1.1 collective-permute-start.22
  99.2 1.8 %collective-permute-start.21 = (bf16[1,64,2048]{2,1,0:T(8,128)(2,1)S(1)}, bf16[1,64,2048]{2,1,0:T(8,128)(2,1)S(1)}, u32[]{:S(2)}, u32[]{:S(2)}) collective-permute-start(bf16[1,64,2048]{2,1,0:T(8,128)(2,1)S(1)} %get-tuple-element.18), channel_id=1, source_target_pairs={{0,7},{1,6},{2,5},{3,4},{4,3},{5,2},{6,1},{7,0},{8,15},{9,14},{10,... | collective-permute-start | bytes 786440 | tf_op jit(solution)/shard_map/ppermute | solution.py:23
  101.0 2.0 %collective-permute-start.24 = (bf16[1,64,2048]{2,1,0:T(8,128)(2,1)S(1)}, bf16[1,64,2048]{2,1,0:T(8,128)(2,1)S(1)}, u32[]{:S(2)}, u32[]{:S(2)}) collective-permute-start(bf16[1,64,2048]{2,1,0:T(8,128)(2,1)S(1)} %get-tuple-element.22), channel_id=1, source_target_pairs={{0,3},{1,2},{2,1},{3,0},{4,7},{5,6},{6,5},{7,4},{8,11},{9,10},{10,... | collective-permute-start | bytes 786440 | tf_op jit(solution)/shard_map/ppermute | solution.py:23
  103.0 6.7 %collective-permute-done.22 = bf16[1,64,2048]{2,1,0:T(8,128)(2,1)S(1)} collective-permute-done((bf16[1,64,2048]{2,1,0:T(8,128)(2,1)S(1)}, bf16[1,64,2048]{2,1,0:T(8,128)(2,1)S(1)}, u32[]{:S(2)}, u32[]{:S(2)}) %collective-permute-start.22) | collective-permute-done | bytes 262176 | tf_op jit(solution)/shard_map/ppermute | solution.py:23
  109.9 4.0 %collective-permute-done.9 = bf16[8,1,64,2048]{3,2,1,0:T(8,128)(2,1)} collective-permute-done((bf16[8,1,64,2048]{3,2,1,0:T(8,128)(2,1)}, bf16[8,1,64,2048]{3,2,1,0:T(8,128)(2,1)}, u32[]{:S(2)}, u32[]{:S(2)}) %collective-permute-start.9) | collective-permute-done | bytes 2097184 | tf_op jit(solution)/shard_map/ppermute | solution.py:23
  113.9 1.3 collective-permute-start.26
  115.3 3.6 %add_convert_fusion = bf16[8,1,64,2048]{3,2,1,0:T(8,128)(2,1)S(1)} fusion(bf16[8,1,64,2048]{3,2,1,0:T(8,128)(2,1)} %collective-permute-done.9, bf16[8,1,64,2048]{3,2,1,0:T(8,128)(2,1)} %add_convert_fusion.1, f32[]{:T(128)S(6)} %sub.112, f32[]{:T(128)} %bitcast), kind=kLoop, calls=%fused_computation | loop fusion | flops 6291456 | bytes 6291464 | tf_op jit(solution)/shard_map/convert_element_type | solution.py:203
  118.9 2.6 %collective-permute-start.27 = (bf16[1,64,2048]{2,1,0:T(8,128)(2,1)S(1)}, bf16[1,64,2048]{2,1,0:T(8,128)(2,1)S(1)}, u32[]{:S(2)}, u32[]{:S(2)}) collective-permute-start(bf16[1,64,2048]{2,1,0:T(8,128)(2,1)S(1)} %get-tuple-element.25), channel_id=1, source_target_pairs={{0,4},{1,5},{2,6},{3,7},{4,0},{5,1},{6,2},{7,3},{8,12},{9,13},{10,... | collective-permute-start | bytes 786440 | tf_op jit(solution)/shard_map/ppermute | solution.py:23
  122.2 5.4 %collective-permute-done.25 = bf16[1,64,2048]{2,1,0:T(8,128)(2,1)S(1)} collective-permute-done((bf16[1,64,2048]{2,1,0:T(8,128)(2,1)S(1)}, bf16[1,64,2048]{2,1,0:T(8,128)(2,1)S(1)}, u32[]{:S(2)}, u32[]{:S(2)}) %collective-permute-start.25) | collective-permute-done | bytes 262176 | tf_op jit(solution)/shard_map/ppermute | solution.py:23
  127.7 11.0 %collective-permute-done.26 = bf16[1,64,2048]{2,1,0:T(8,128)(2,1)S(1)} collective-permute-done((bf16[1,64,2048]{2,1,0:T(8,128)(2,1)S(1)}, bf16[1,64,2048]{2,1,0:T(8,128)(2,1)S(1)}, u32[]{:S(2)}, u32[]{:S(2)}) %collective-permute-start.26) | collective-permute-done | bytes 262176 | tf_op jit(solution)/shard_map/ppermute | solution.py:23
  138.8 4.4 %collective-permute-done.27 = bf16[1,64,2048]{2,1,0:T(8,128)(2,1)S(1)} collective-permute-done((bf16[1,64,2048]{2,1,0:T(8,128)(2,1)S(1)}, bf16[1,64,2048]{2,1,0:T(8,128)(2,1)S(1)}, u32[]{:S(2)}, u32[]{:S(2)}) %collective-permute-start.27) | collective-permute-done | bytes 262176 | tf_op jit(solution)/shard_map/ppermute | solution.py:23
  143.4 1.3 copy-done.4
  144.7 0.7 copy-done.5
  (54 shorter events, 2.2 us)
Async XLA Ops:
  0.6 8.7 %copy-start.7 = (s32[4,2]{0,1:T(2,128)S(1)}, s32[4,2]{0,1:T(2,128)}, u32[]{:S(2)}) copy-start(s32[4,2]{0,1:T(2,128)} %param.9) | copy-start | bytes 100
  0.7 12.6 %copy-start.2 = (bf16[1,8,64,2048]{3,2,1,0:T(8,128)(2,1)S(1)}, bf16[1,8,64,2048]{3,2,1,0:T(8,128)(2,1)}, u32[]{:S(2)}) copy-start(bf16[1,8,64,2048]{3,2,1,0:T(8,128)(2,1)} %param.8) | copy-start | bytes 6291460
  2.8 9.6 %collective-permute-start.4 = (bf16[1,1,64,2048]{3,2,1,0:T(8,128)(2,1)}, bf16[1,1,64,2048]{3,2,1,0:T(8,128)(2,1)}, u32[]{:S(2)}, u32[]{:S(2)}) collective-permute-start(bf16[1,1,64,2048]{3,2,1,0:T(8,128)(2,1)} %get-tuple-element.41), channel_id=1, source_target_pairs={{0,8},{8,0},{16,24},{24,16},{1,9},{9,1},{17,25},{25,17},{2,10},{10... | collective-permute-start | bytes 786440 | tf_op jit(solution)/shard_map/ppermute | solution.py:23
  3.2 10.0 %collective-permute-start.5 = (bf16[1,1,64,2048]{3,2,1,0:T(8,128)(2,1)}, bf16[1,1,64,2048]{3,2,1,0:T(8,128)(2,1)}, u32[]{:S(2)}, u32[]{:S(2)}) collective-permute-start(bf16[1,1,64,2048]{3,2,1,0:T(8,128)(2,1)} %get-tuple-element.41), channel_id=1, source_target_pairs={{0,16},{8,24},{16,0},{24,8},{1,17},{9,25},{17,1},{25,9},{2,18},{10... | collective-permute-start | bytes 786440 | tf_op jit(solution)/shard_map/ppermute | solution.py:23
  5.7 6.1 %collective-permute-start.17 = (bf16[1,1,64,2048]{3,2,1,0:T(8,128)(2,1)S(1)}, bf16[1,1,64,2048]{3,2,1,0:T(8,128)(2,1)}, u32[]{:S(2)}, u32[]{:S(2)}) collective-permute-start(bf16[1,1,64,2048]{3,2,1,0:T(8,128)(2,1)S(1)} %get-tuple-element.40), channel_id=1, source_target_pairs={{0,8},{8,0},{16,24},{24,16},{1,9},{9,1},{17,25},{25,17},{2,10},{10... | collective-permute-start | bytes 786440 | tf_op jit(solution)/shard_map/ppermute | solution.py:23
  6.0 12.7 %collective-permute-start.18 = (bf16[1,1,64,2048]{3,2,1,0:T(8,128)(2,1)S(1)}, bf16[1,1,64,2048]{3,2,1,0:T(8,128)(2,1)}, u32[]{:S(2)}, u32[]{:S(2)}) collective-permute-start(bf16[1,1,64,2048]{3,2,1,0:T(8,128)(2,1)S(1)} %get-tuple-element.40), channel_id=1, source_target_pairs={{0,16},{8,24},{16,0},{24,8},{1,17},{9,25},{17,1},{25,9},{2,18},{10... | collective-permute-start | bytes 786440 | tf_op jit(solution)/shard_map/ppermute | solution.py:23
  9.3 12.3 %collective-permute-start.13 = (bf16[2,1,64,2048]{3,2,0,1:T(8,128)(2,1)}, bf16[2,1,64,2048]{3,2,0,1:T(8,128)(2,1)S(1)}, u32[]{:S(2)}, u32[]{:S(2)}) collective-permute-start(bf16[2,1,64,2048]{3,2,0,1:T(8,128)(2,1)} %get-tuple-element.37), channel_id=1, source_target_pairs={{0,8},{8,0},{16,24},{24,16},{1,9},{9,1},{17,25},{25,17},{2,10},{10... | collective-permute-start | bytes 1572872 | tf_op jit(solution)/shard_map/ppermute | solution.py:23
  11.8 14.7 %collective-permute-start.2 = (bf16[2,1,64,2048]{3,2,1,0:T(8,128)(2,1)}, bf16[2,1,64,2048]{3,2,1,0:T(8,128)(2,1)S(1)}, u32[]{:S(2)}, u32[]{:S(2)}) collective-permute-start(bf16[2,1,64,2048]{3,2,1,0:T(8,128)(2,1)} %get-tuple-element.36), channel_id=1, source_target_pairs={{0,8},{8,0},{16,24},{24,16},{1,9},{9,1},{17,25},{25,17},{2,10},{10... | collective-permute-start | bytes 1572872 | tf_op jit(solution)/shard_map/ppermute | solution.py:23
  12.4 33.4 %collective-permute-start = (bf16[8,1,64,2048]{3,2,1,0:T(8,128)(2,1)}, bf16[8,1,64,2048]{3,2,1,0:T(8,128)(2,1)S(1)}, u32[]{:S(2)}, u32[]{:S(2)}) collective-permute-start(bf16[8,1,64,2048]{3,2,1,0:T(8,128)(2,1)} %bitcast.175), channel_id=1, source_target_pairs={{0,8},{8,0},{16,24},{24,16},{1,9},{9,1},{17,25},{25,17},{2,10},{10... | collective-permute-start | bytes 6291464 | tf_op jit(solution)/shard_map/ppermute | solution.py:23
  13.2 5.4 %collective-permute-start.6 = (bf16[1,1,64,2048]{3,2,1,0:T(8,128)(2,1)}, bf16[1,1,64,2048]{3,2,1,0:T(8,128)(2,1)S(1)}, u32[]{:S(2)}, u32[]{:S(2)}) collective-permute-start(bf16[1,1,64,2048]{3,2,1,0:T(8,128)(2,1)} %collective-permute-done.5), channel_id=1, source_target_pairs={{0,8},{8,0},{16,24},{24,16},{1,9},{9,1},{17,25},{25,17},{2,10},{10... | collective-permute-start | bytes 786440 | tf_op jit(solution)/shard_map/ppermute | solution.py:23
  18.6 7.9 %copy-start = (f32[1,8,64,2048]{3,2,1,0:T(8,128)S(1)}, f32[1,8,64,2048]{3,2,1,0:T(8,128)}, u32[]{:S(2)}) copy-start(f32[1,8,64,2048]{3,2,1,0:T(8,128)} %param.6) | copy-start | bytes 12582916
  18.6 12.4 %collective-permute-start.1 = (bf16[2,1,64,2048]{3,2,0,1:T(8,128)(2,1)S(1)}, bf16[2,1,64,2048]{3,2,0,1:T(8,128)(2,1)S(1)}, u32[]{:S(2)}, u32[]{:S(2)}) collective-permute-start(bf16[2,1,64,2048]{3,2,0,1:T(8,128)(2,1)S(1)} %get-tuple-element.35), channel_id=1, source_target_pairs={{0,8},{8,0},{16,24},{24,16},{1,9},{9,1},{17,25},{25,17},{2,10},{10... | collective-permute-start | bytes 1572872 | tf_op jit(solution)/shard_map/ppermute | solution.py:23
  18.7 10.4 %collective-permute-start.19 = (bf16[1,1,64,2048]{3,2,1,0:T(8,128)(2,1)}, bf16[1,1,64,2048]{3,2,1,0:T(8,128)(2,1)S(1)}, u32[]{:S(2)}, u32[]{:S(2)}) collective-permute-start(bf16[1,1,64,2048]{3,2,1,0:T(8,128)(2,1)} %collective-permute-done.18), channel_id=1, source_target_pairs={{0,8},{8,0},{16,24},{24,16},{1,9},{9,1},{17,25},{25,17},{2,10},{10... | collective-permute-start | bytes 786440 | tf_op jit(solution)/shard_map/ppermute | solution.py:23
  21.6 28.4 %collective-permute-start.7 = (bf16[1,64,2048]{2,1,0:T(8,128)(2,1)S(1)}, bf16[1,64,2048]{2,1,0:T(8,128)(2,1)S(1)}, u32[]{:S(2)}, u32[]{:S(2)}) collective-permute-start(bf16[1,64,2048]{2,1,0:T(8,128)(2,1)S(1)} %get-tuple-element.50), channel_id=1, source_target_pairs={{0,7},{1,6},{2,5},{3,4},{4,3},{5,2},{6,1},{7,0},{8,15},{9,14},{10,... | collective-permute-start | bytes 786440 | tf_op jit(solution)/shard_map/ppermute | solution.py:23
  27.5 13.5 %copy-start.3 = (bf16[1,8,64,2048]{3,2,1,0:T(8,128)(2,1)S(1)}, bf16[1,8,64,2048]{3,2,1,0:T(8,128)(2,1)}, u32[]{:S(2)}) copy-start(bf16[1,8,64,2048]{3,2,1,0:T(8,128)(2,1)} %param.7) | copy-start | bytes 6291460
  27.5 13.4 %collective-permute-start.14 = (bf16[2,1,64,2048]{3,2,1,0:T(8,128)(2,1)S(1)}, bf16[2,1,64,2048]{3,2,1,0:T(8,128)(2,1)S(1)}, u32[]{:S(2)}, u32[]{:S(2)}) collective-permute-start(bf16[2,1,64,2048]{3,2,1,0:T(8,128)(2,1)S(1)} %get-tuple-element.39), channel_id=1, source_target_pairs={{0,16},{8,24},{16,0},{24,8},{1,17},{9,25},{17,1},{25,9},{2,18},{10... | collective-permute-start | bytes 1572872 | tf_op jit(solution)/shard_map/ppermute | solution.py:23
  30.8 42.2 %collective-permute-start.20 = (bf16[1,64,2048]{2,1,0:T(8,128)(2,1)S(1)}, bf16[1,64,2048]{2,1,0:T(8,128)(2,1)S(1)}, u32[]{:S(2)}, u32[]{:S(2)}) collective-permute-start(bf16[1,64,2048]{2,1,0:T(8,128)(2,1)S(1)} %get-tuple-element.42), channel_id=1, source_target_pairs={{0,6},{1,7},{2,4},{3,5},{4,2},{5,3},{6,0},{7,1},{8,14},{9,15},{10,... | collective-permute-start | bytes 786440 | tf_op jit(solution)/shard_map/ppermute | solution.py:23
  40.9 6.3 %copy-start.6 = (bf16[1,8,64,2048]{3,2,1,0:T(8,128)(2,1)S(1)}, bf16[1,8,64,2048]{3,2,1,0:T(8,128)(2,1)}, u32[]{:S(2)}) copy-start(bf16[1,8,64,2048]{3,2,1,0:T(8,128)(2,1)} %param.5) | copy-start | bytes 6291460
  42.8 30.7 %collective-permute-start.15 = (bf16[1,64,2048]{2,1,0:T(8,128)(2,1)S(1)}, bf16[1,64,2048]{2,1,0:T(8,128)(2,1)S(1)}, u32[]{:S(2)}, u32[]{:S(2)}) collective-permute-start(bf16[1,64,2048]{2,1,0:T(8,128)(2,1)S(1)} %get-tuple-element.45), channel_id=1, source_target_pairs={{0,4},{1,5},{2,6},{3,7},{4,0},{5,1},{6,2},{7,3},{8,12},{9,13},{10,... | collective-permute-start | bytes 786440 | tf_op jit(solution)/shard_map/ppermute | solution.py:23
  42.9 31.7 %collective-permute-start.16 = (bf16[1,64,2048]{2,1,0:T(8,128)(2,1)S(1)}, bf16[1,64,2048]{2,1,0:T(8,128)(2,1)S(1)}, u32[]{:S(2)}, u32[]{:S(2)}) collective-permute-start(bf16[1,64,2048]{2,1,0:T(8,128)(2,1)S(1)} %get-tuple-element.44), channel_id=1, source_target_pairs={{0,5},{1,4},{2,7},{3,6},{4,1},{5,0},{6,3},{7,2},{8,13},{9,12},{10,... | collective-permute-start | bytes 786440 | tf_op jit(solution)/shard_map/ppermute | solution.py:23
  45.8 12.1 %collective-permute-start.3 = (bf16[2,1,64,2048]{3,2,1,0:T(8,128)(2,1)S(1)}, bf16[2,1,64,2048]{3,2,1,0:T(8,128)(2,1)S(1)}, u32[]{:S(2)}, u32[]{:S(2)}) collective-permute-start(bf16[2,1,64,2048]{3,2,1,0:T(8,128)(2,1)S(1)} %get-tuple-element.15), channel_id=1, source_target_pairs={{0,16},{8,24},{16,0},{24,8},{1,17},{9,25},{17,1},{25,9},{2,18},{10... | collective-permute-start | bytes 1572872 | tf_op jit(solution)/shard_map/ppermute | solution.py:23
  57.8 11.9 %collective-permute-start.8 = (bf16[2,1,64,2048]{3,2,0,1:T(8,128)(2,1)S(1)}, bf16[2,1,64,2048]{3,2,0,1:T(8,128)(2,1)S(1)}, u32[]{:S(2)}, u32[]{:S(2)}) collective-permute-start(bf16[2,1,64,2048]{3,2,0,1:T(8,128)(2,1)S(1)} %fusion.3), channel_id=1, source_target_pairs={{0,16},{8,24},{16,0},{24,8},{1,17},{9,25},{17,1},{25,9},{2,18},{10... | collective-permute-start | bytes 1572872 | tf_op jit(solution)/shard_map/ppermute | solution.py:23
  61.1 16.0 %collective-permute-start.11 = (bf16[1,64,2048]{2,1,0:T(8,128)(2,1)S(1)}, bf16[1,64,2048]{2,1,0:T(8,128)(2,1)S(1)}, u32[]{:S(2)}, u32[]{:S(2)}) collective-permute-start(bf16[1,64,2048]{2,1,0:T(8,128)(2,1)S(1)} %get-tuple-element.47), channel_id=1, source_target_pairs={{0,2},{1,3},{2,0},{3,1},{4,6},{5,7},{6,4},{7,5},{8,10},{9,11},{10,... | collective-permute-start | bytes 786440 | tf_op jit(solution)/shard_map/ppermute | solution.py:23
  69.7 44.2 %collective-permute-start.9 = (bf16[8,1,64,2048]{3,2,1,0:T(8,128)(2,1)}, bf16[8,1,64,2048]{3,2,1,0:T(8,128)(2,1)}, u32[]{:S(2)}, u32[]{:S(2)}) collective-permute-start(bf16[8,1,64,2048]{3,2,1,0:T(8,128)(2,1)} %add_convert_fusion.1), channel_id=1, source_target_pairs={{0,16},{8,24},{16,0},{24,8},{1,17},{9,25},{17,1},{25,9},{2,18},{10... | collective-permute-start | bytes 6291464 | tf_op jit(solution)/shard_map/ppermute | solution.py:23
  72.9 12.4 %copy-start.1 = (f32[1,8,64,2048]{3,2,1,0:T(8,128)}, f32[1,8,64,2048]{3,2,1,0:T(8,128)S(1)}, u32[]{:S(2)}) copy-start(f32[1,8,64,2048]{3,2,1,0:T(8,128)S(1)} %get-tuple-element.27) | copy-start | bytes 12582916
  73.0 9.6 %collective-permute-start.12 = (bf16[1,64,2048]{2,1,0:T(8,128)(2,1)S(1)}, bf16[1,64,2048]{2,1,0:T(8,128)(2,1)S(1)}, u32[]{:S(2)}, u32[]{:S(2)}) collective-permute-start(bf16[1,64,2048]{2,1,0:T(8,128)(2,1)S(1)} %get-tuple-element.46), channel_id=1, source_target_pairs={{0,3},{1,2},{2,1},{3,0},{4,7},{5,6},{6,5},{7,4},{8,11},{9,10},{10,... | collective-permute-start | bytes 786440 | tf_op jit(solution)/shard_map/ppermute | solution.py:23
  73.5 11.7 %collective-permute-start.10 = (bf16[1,64,2048]{2,1,0:T(8,128)(2,1)S(1)}, bf16[1,64,2048]{2,1,0:T(8,128)(2,1)S(1)}, u32[]{:S(2)}, u32[]{:S(2)}) collective-permute-start(bf16[1,64,2048]{2,1,0:T(8,128)(2,1)S(1)} %get-tuple-element.48), channel_id=1, source_target_pairs={{0,1},{1,0},{2,3},{3,2},{4,5},{5,4},{6,7},{7,6},{8,9},{9,8},{10,11... | collective-permute-start | bytes 786440 | tf_op jit(solution)/shard_map/ppermute | solution.py:23
  98.1 11.6 %collective-permute-start.22 = (bf16[1,64,2048]{2,1,0:T(8,128)(2,1)S(1)}, bf16[1,64,2048]{2,1,0:T(8,128)(2,1)S(1)}, u32[]{:S(2)}, u32[]{:S(2)}) collective-permute-start(bf16[1,64,2048]{2,1,0:T(8,128)(2,1)S(1)} %get-tuple-element.20), channel_id=1, source_target_pairs={{0,1},{1,0},{2,3},{3,2},{4,5},{5,4},{6,7},{7,6},{8,9},{9,8},{10,11... | collective-permute-start | bytes 786440 | tf_op jit(solution)/shard_map/ppermute | solution.py:23
  99.2 19.7 %collective-permute-start.21 = (bf16[1,64,2048]{2,1,0:T(8,128)(2,1)S(1)}, bf16[1,64,2048]{2,1,0:T(8,128)(2,1)S(1)}, u32[]{:S(2)}, u32[]{:S(2)}) collective-permute-start(bf16[1,64,2048]{2,1,0:T(8,128)(2,1)S(1)} %get-tuple-element.18), channel_id=1, source_target_pairs={{0,7},{1,6},{2,5},{3,4},{4,3},{5,2},{6,1},{7,0},{8,15},{9,14},{10,... | collective-permute-start | bytes 786440 | tf_op jit(solution)/shard_map/ppermute | solution.py:23
  101.0 20.9 %collective-permute-start.23 = (bf16[1,64,2048]{2,1,0:T(8,128)(2,1)S(1)}, bf16[1,64,2048]{2,1,0:T(8,128)(2,1)S(1)}, u32[]{:S(2)}, u32[]{:S(2)}) collective-permute-start(bf16[1,64,2048]{2,1,0:T(8,128)(2,1)S(1)} %get-tuple-element.21), channel_id=1, source_target_pairs={{0,2},{1,3},{2,0},{3,1},{4,6},{5,7},{6,4},{7,5},{8,10},{9,11},{10,... | collective-permute-start | bytes 786440 | tf_op jit(solution)/shard_map/ppermute | solution.py:23
  101.0 21.0 %collective-permute-start.24 = (bf16[1,64,2048]{2,1,0:T(8,128)(2,1)S(1)}, bf16[1,64,2048]{2,1,0:T(8,128)(2,1)S(1)}, u32[]{:S(2)}, u32[]{:S(2)}) collective-permute-start(bf16[1,64,2048]{2,1,0:T(8,128)(2,1)S(1)} %get-tuple-element.22), channel_id=1, source_target_pairs={{0,3},{1,2},{2,1},{3,0},{4,7},{5,6},{6,5},{7,4},{8,11},{9,10},{10,... | collective-permute-start | bytes 786440 | tf_op jit(solution)/shard_map/ppermute | solution.py:23
  109.6 18.0 %collective-permute-start.25 = (bf16[1,64,2048]{2,1,0:T(8,128)(2,1)S(1)}, bf16[1,64,2048]{2,1,0:T(8,128)(2,1)S(1)}, u32[]{:S(2)}, u32[]{:S(2)}) collective-permute-start(bf16[1,64,2048]{2,1,0:T(8,128)(2,1)S(1)} %get-tuple-element.23), channel_id=1, source_target_pairs={{0,6},{1,7},{2,4},{3,5},{4,2},{5,3},{6,0},{7,1},{8,14},{9,15},{10,... | collective-permute-start | bytes 786440 | tf_op jit(solution)/shard_map/ppermute | solution.py:23
  113.9 24.7 %collective-permute-start.26 = (bf16[1,64,2048]{2,1,0:T(8,128)(2,1)S(1)}, bf16[1,64,2048]{2,1,0:T(8,128)(2,1)S(1)}, u32[]{:S(2)}, u32[]{:S(2)}) collective-permute-start(bf16[1,64,2048]{2,1,0:T(8,128)(2,1)S(1)} %get-tuple-element.24), channel_id=1, source_target_pairs={{0,5},{1,4},{2,7},{3,6},{4,1},{5,0},{6,3},{7,2},{8,13},{9,12},{10,... | collective-permute-start | bytes 786440 | tf_op jit(solution)/shard_map/ppermute | solution.py:23
  118.9 24.2 %collective-permute-start.27 = (bf16[1,64,2048]{2,1,0:T(8,128)(2,1)S(1)}, bf16[1,64,2048]{2,1,0:T(8,128)(2,1)S(1)}, u32[]{:S(2)}, u32[]{:S(2)}) collective-permute-start(bf16[1,64,2048]{2,1,0:T(8,128)(2,1)S(1)} %get-tuple-element.25), channel_id=1, source_target_pairs={{0,4},{1,5},{2,6},{3,7},{4,0},{5,1},{6,2},{7,3},{8,12},{9,13},{10,... | collective-permute-start | bytes 786440 | tf_op jit(solution)/shard_map/ppermute | solution.py:23
  143.4 1.3 copy-start.4
  143.4 2.0 %copy-start.5 = (bf16[1,8,64,2048]{3,2,1,0:T(8,128)(2,1)}, bf16[1,8,64,2048]{3,2,1,0:T(8,128)(2,1)S(1)}, u32[]{:S(2)}) copy-start(bf16[1,8,64,2048]{3,2,1,0:T(8,128)(2,1)S(1)} %get-tuple-element.52) | copy-start | bytes 6291460

commit v14 on v13

--- a/solution.py
+++ b/solution.py
@@ -172,7 +172,7 @@
             if turn == 2:
                 sent = after(sent, weight_near)
             elif turn == 4:
-                sent = after(sent, arrived[2], blocks[7 * shards // 8])
+                sent = after(sent, arrived[2], blocks[7 * shards // 8], blocks[6 * shards // 8])
             far = swapped(sent, "rep", 2)
             far_mixed = far.astype(F32)
         arrived.append(far)

time: 146 us -> 152 us (1.041)
  starting transfers between devices: 29.3 us -> 45.9 us
  waiting for transfers between devices: 70.7 us -> 59.7 us
    ppermute x28, starting transfers between devices: 29.3 us -> 45.9 us  [swapped(): lax.ppermute(values, axis, [(i, i ^ offset) for i in range(lax.axis_size(...]
    ppermute x28, waiting for transfers between devices: 70.7 us -> 59.7 us  [swapped(): lax.ppermute(values, axis, [(i, i ^ offset) for i in range(lax.axis_size(...]
  transfers between devices with their start and end apart: 28 -> 28, of which waited for: 13 -> 10; matrix products, arithmetic and copies ran while one was open for 17% -> 17% of each run, Pallas kernels for 9% -> 8%
where the time goes in v14:
time: 152 us
  waiting for transfers between devices  59.7 us (39%)
  starting transfers between devices  45.9 us (30%)
  other arithmetic  21.7 us (14%)
  Pallas kernels  12.8 us (8%)
  local copies, waits for them, and re-layouts  9.01 us (6%)
  between operations  2.86 us (2%)
    ppermute x28, waiting for transfers between devices, swapped(): lax.ppermute(values, axis, [(i, i ^ offset) for i in range(lax.axis_size(...  59.7 us
    ppermute x28, starting transfers between devices, swapped(): lax.ppermute(values, axis, [(i, i ^ offset) for i in range(lax.axis_size(...  45.9 us
    pallas_call x1, Pallas kernels, orthogonalize(): pl.pallas_call(body, grid=(each,), in_specs=[block] * count, out_specs=[b...  12.8 us
    dynamic_update_slice x3, other arithmetic, local(): lax.dynamic_update_slice_in_dim(new_tracker, group, start, axis=0)  5.34 us
    convert_element_type x2, local copies, waits for them, and re-layouts, local(): rounded = own.astype(BF16)  5.17 us
    convert_element_type x1, other arithmetic, local(): mixed_weight = (second * weight_own.astype(F32) + (1.0 - second) * weight...  3.77 us
    convert_element_type x2, other arithmetic, local(): sent = mixed.astype(BF16)  3.16 us
    add x1, other arithmetic, local(): second * mixed  3.07 us
  transfers between devices with their start and end apart: 28, of which 10 were waited for; matrix products, arithmetic and copies ran while one was open for 17% of the time, Pallas kernels for 8%

profile of v14, /device:TPU:0, one launch (start us, length us, event | category | flops | bytes accessed | tf_op | source)
XLA Modules:
  0.0 152.0 jit_solution(9259587631916464217)
XLA Ops:
  0.7 2.1 %dynamic-slice_convert_fusion.9 = (bf16[1,1,64,2048]{3,2,1,0:T(8,128)(2,1)S(1)}, bf16[1,1,64,2048]{3,2,1,0:T(8,128)(2,1)}) fusion(f32[1,8,64,2048]{3,2,1,0:T(8,128)} %param.6, s32[]{:T(128)S(6)} %select_n.143, s32[]{:T(128)S(6)} %select_n.141), kind=kLoop, calls=%fused_computation.53 | loop fusion | bytes 1048584 | tf_op jit(solution)/shard_map/convert_element_type | solution.py:165
  2.8 0.5 collective-permute-start.4
  3.2 2.5 %collective-permute-start.5 = (bf16[1,1,64,2048]{3,2,1,0:T(8,128)(2,1)}, bf16[1,1,64,2048]{3,2,1,0:T(8,128)(2,1)}, u32[]{:S(2)}, u32[]{:S(2)}) collective-permute-start(bf16[1,1,64,2048]{3,2,1,0:T(8,128)(2,1)} %get-tuple-element.41), channel_id=1, source_target_pairs={{0,16},{8,24},{16,0},{24,8},{1,17},{9,25},{17,1},{25,9},{2,18},{10... | collective-permute-start | bytes 786440 | tf_op jit(solution)/shard_map/ppermute | solution.py:23
  5.9 3.1 %fusion.6 = (bf16[2,1,64,2048]{3,2,0,1:T(8,128)(2,1)}, bf16[2,1,64,2048]{3,2,1,0:T(8,128)(2,1)}, bf16[2,1,64,2048]{3,2,0,1:T(8,128)(2,1)}) fusion(f32[1,8,64,2048]{3,2,1,0:T(8,128)} %param.6, s32[]{:T(128)S(6)} %select_n.138, s32[]{:T(128)S(6)} %select_n.140, s32[]{:T(128)S(6)} %select_n.153), kind=kLoop, calls=%fused_computation.24 | loop fusion | bytes 3145740 | tf_op jit(solution)/shard_map/convert_element_type | solution.py:165
  9.0 0.3 collective-permute-start.17
  9.5 0.7 constant_dynamic-slice_fusion
  12.1 0.3 collective-permute-start.9
  12.6 3.1 %subtract_add_fusion = (f32[1,1,64,2048]{3,2,1,0:T(8,128)S(1)}, f32[1,1,64,2048]{3,2,1,0:T(8,128)S(1)}) fusion(bf16[1,1,64,2048]{3,2,1,0:T(8,128)(2,1)} %collective-permute-done.8, f32[1,8,64,2048]{3,2,1,0:T(8,128)} %param.6, s32[]{:T(128)S(6)} %select_n.143, bf16[1,8,64,2048]{3,2,1,0:T(8,128)(2,1)S(1)} %copy-done.2, bf16[1,8,64,2048]{3,2,1,0:T(8,128)(2,1)} %param.7, ...), kind=kLoop, calls=%fused_computation.50 | loop fusion | flops 2359296 | bytes 3670036 | tf_op jit(solution)/shard_map/add | solution.py:179
  15.7 0.5 collective-permute-start.1
  16.1 4.5 %collective-permute-done.9 = bf16[1,1,64,2048]{3,2,1,0:T(8,128)(2,1)S(1)} collective-permute-done((bf16[1,1,64,2048]{3,2,1,0:T(8,128)(2,1)S(1)}, bf16[1,1,64,2048]{3,2,1,0:T(8,128)(2,1)S(1)}, u32[]{:S(2)}, u32[]{:S(2)}) %collective-permute-start.9) | collective-permute-done | bytes 262176 | tf_op jit(solution)/shard_map/ppermute | solution.py:23
  20.7 0.5 collective-permute-start.10
  21.2 2.4 %fusion.4 = (bf16[2,1,64,2048]{3,2,1,0:T(8,128)(2,1)S(1)}, bf16[2,1,64,2048]{3,2,1,0:T(8,128)(2,1)S(1)}) fusion(bf16[2,1,64,2048]{3,2,1,0:T(8,128)(2,1)S(1)} %collective-permute-done.2, f32[1,8,64,2048]{3,2,1,0:T(8,128)} %param.6, s32[]{:T(128)S(6)} %select_n.140, f32[]{:T(128)S(6)} %sub.108, f32[]{:T(128)} %bitcast.1, ...), kind=kLoop, calls=%fused_computation.22 | loop fusion | flops 2621440 | bytes 4194320 | tf_op jit(solution)/shard_map/convert_element_type | solution.py:171
  23.6 0.4 collective-permute-start.18
  24.0 0.5 reshape.500
  24.5 2.0 %convert_bitcast_fusion.1 = (bf16[1,64,2048]{2,1,0:T(8,128)(2,1)S(1)}, f32[1,8,64,2048]{3,2,1,0:T(8,128)S(1)}) fusion(f32[1,1,64,2048]{3,2,1,0:T(8,128)S(1)} %get-tuple-element.34, bf16[1,1,64,2048]{3,2,1,0:T(8,128)(2,1)S(1)} %collective-permute-done.6, f32[]{:T(128)S(6)} %sub.113, bf16[1,1,64,2048]{3,2,1,0:T(8,128)(2,1)} %collective-permute-done.5, ...), kind=kLoop, calls=%fused_computation.86 | loop fusion | flops 1048576 | bytes 1835024 | tf_op jit(solution)/shard_map/convert_element_type | solution.py:188
  26.5 0.9 convert_bitcast_fusion
  27.4 3.9 %collective-permute-start.11 = (bf16[1,64,2048]{2,1,0:T(8,128)(2,1)S(1)}, bf16[1,64,2048]{2,1,0:T(8,128)(2,1)S(1)}, u32[]{:S(2)}, u32[]{:S(2)}) collective-permute-start(bf16[1,64,2048]{2,1,0:T(8,128)(2,1)S(1)} %get-tuple-element.48), channel_id=1, source_target_pairs={{0,6},{1,7},{2,4},{3,5},{4,2},{5,3},{6,0},{7,1},{8,14},{9,15},{10,... | collective-permute-start | bytes 786440 | tf_op jit(solution)/shard_map/ppermute | solution.py:23
  31.3 1.2 collective-permute-start.7
  32.5 0.7 fusion.3
  33.2 4.3 %collective-permute-done.18 = bf16[2,1,64,2048]{3,2,1,0:T(8,128)(2,1)S(1)} collective-permute-done((bf16[2,1,64,2048]{3,2,1,0:T(8,128)(2,1)S(1)}, bf16[2,1,64,2048]{3,2,1,0:T(8,128)(2,1)S(1)}, u32[]{:S(2)}, u32[]{:S(2)}) %collective-permute-start.18) | collective-permute-done | bytes 524320 | tf_op jit(solution)/shard_map/ppermute | solution.py:23
  37.5 1.9 %bitcast_dynamic-update-slice_fusion.2 = (f32[1,8,64,2048]{3,2,1,0:T(8,128)S(1)}, bf16[2,1,64,2048]{3,2,1,0:T(8,128)(2,1)S(1)}) fusion(f32[1,8,64,2048]{3,2,1,0:T(8,128)S(1)} %get-tuple-element.49, s32[]{:T(128)S(6)} %select_n.153, bf16[2,1,64,2048]{3,2,1,0:T(8,128)(2,1)S(1)} %collective-permute-done.18, f32[]{:T(128)S(6)} %sub.112, ...), kind=kLoop, calls=%fused_computation.10 | loop fusion | flops 3407872 | bytes 4718612 | tf_op jit(solution)/shard_map/dynamic_update_slice | solution.py:194
  39.5 2.7 %collective-permute-start.19 = (bf16[1,64,2048]{2,1,0:T(8,128)(2,1)S(1)}, bf16[1,64,2048]{2,1,0:T(8,128)(2,1)S(1)}, u32[]{:S(2)}, u32[]{:S(2)}) collective-permute-start(bf16[1,64,2048]{2,1,0:T(8,128)(2,1)S(1)} %get-tuple-element.43), channel_id=1, source_target_pairs={{0,4},{1,5},{2,6},{3,7},{4,0},{5,1},{6,2},{7,3},{8,12},{9,13},{10,... | collective-permute-start | bytes 786440 | tf_op jit(solution)/shard_map/ppermute | solution.py:23
  42.1 1.3 collective-permute-start.20
  43.4 0.5 collective-permute-start.3
  44.0 2.8 %add_convert_fusion.1 = bf16[8,1,64,2048]{3,2,1,0:T(8,128)(2,1)} fusion(bf16[8,1,64,2048]{3,2,1,0:T(8,128)(2,1)S(1)} %collective-permute-done, f32[]{:T(128)S(6)} %sub.108, f32[]{:T(128)} %bitcast.1, bf16[1,8,64,2048]{3,2,1,0:T(8,128)(2,1)S(1)} %copy-done.6), kind=kLoop, calls=%fused_computation.1 | loop fusion | flops 6291456 | bytes 6291464 | tf_op jit(solution)/shard_map/convert_element_type | solution.py:198
  46.7 9.1 %collective-permute-done.3 = bf16[2,1,64,2048]{3,2,1,0:T(8,128)(2,1)S(1)} collective-permute-done((bf16[2,1,64,2048]{3,2,1,0:T(8,128)(2,1)S(1)}, bf16[2,1,64,2048]{3,2,1,0:T(8,128)(2,1)S(1)}, u32[]{:S(2)}, u32[]{:S(2)}) %collective-permute-start.3) | collective-permute-done | bytes 524320 | tf_op jit(solution)/shard_map/ppermute | solution.py:23
  55.9 0.5 collective-permute-start.12
  56.4 1.7 %bitcast_dynamic-update-slice_fusion.1 = (f32[1,8,64,2048]{3,2,1,0:T(8,128)S(1)}, bf16[2,1,64,2048]{3,2,1,0:T(8,128)(2,1)S(1)}) fusion(f32[1,8,64,2048]{3,2,1,0:T(8,128)S(1)} %get-tuple-element.31, s32[]{:T(128)S(6)} %select_n.140, bf16[2,1,64,2048]{3,2,1,0:T(8,128)(2,1)S(1)} %collective-permute-done.3, f32[]{:T(128)S(6)} %sub.112, ...), kind=kLoop, calls=%fused_computation.9 | loop fusion | flops 3407872 | bytes 4718612 | tf_op jit(solution)/shard_map/dynamic_update_slice | solution.py:194
  58.2 12.4 %collective-permute-start.15 = (bf16[1,64,2048]{2,1,0:T(8,128)(2,1)S(1)}, bf16[1,64,2048]{2,1,0:T(8,128)(2,1)S(1)}, u32[]{:S(2)}, u32[]{:S(2)}) collective-permute-start(bf16[1,64,2048]{2,1,0:T(8,128)(2,1)S(1)} %get-tuple-element.45), channel_id=1, source_target_pairs={{0,2},{1,3},{2,0},{3,1},{4,6},{5,7},{6,4},{7,5},{8,10},{9,11},{10,... | collective-permute-start | bytes 786440 | tf_op jit(solution)/shard_map/ppermute | solution.py:23
  70.6 0.5 collective-permute-start.13
  71.2 1.7 %bitcast_dynamic-update-slice_fusion = (f32[1,8,64,2048]{3,2,1,0:T(8,128)S(1)}, bf16[2,1,64,2048]{3,2,0,1:T(8,128)(2,1)S(1)}) fusion(f32[1,8,64,2048]{3,2,1,0:T(8,128)S(1)} %get-tuple-element.29, s32[]{:T(128)S(6)} %select_n.138, bf16[2,1,64,2048]{3,2,0,1:T(8,128)(2,1)S(1)} %collective-permute-done.12, f32[]{:T(128)S(6)} %sub.112, ...), kind=kLoop, calls=%fused_computation.8 | loop fusion | flops 3407872 | bytes 4718612 | tf_op jit(solution)/shard_map/dynamic_update_slice | solution.py:194
  73.0 1.6 %collective-permute-start.14 = (bf16[1,64,2048]{2,1,0:T(8,128)(2,1)S(1)}, bf16[1,64,2048]{2,1,0:T(8,128)(2,1)S(1)}, u32[]{:S(2)}, u32[]{:S(2)}) collective-permute-start(bf16[1,64,2048]{2,1,0:T(8,128)(2,1)S(1)} %get-tuple-element.46), channel_id=1, source_target_pairs={{0,1},{1,0},{2,3},{3,2},{4,5},{5,4},{6,7},{7,6},{8,9},{9,8},{10,11... | collective-permute-start | bytes 786440 | tf_op jit(solution)/shard_map/ppermute | solution.py:23
  74.5 2.6 %collective-permute-done.20.refs_5_ = bf16[1,64,2048]{2,1,0:T(8,128)(2,1)S(1)} collective-permute-done((bf16[1,64,2048]{2,1,0:T(8,128)(2,1)S(1)}, bf16[1,64,2048]{2,1,0:T(8,128)(2,1)S(1)}, u32[]{:S(2)}, u32[]{:S(2)}) %collective-permute-start.20) | collective-permute-done | bytes 262176 | tf_op jit(solution)/shard_map/ppermute | solution.py:23
  77.1 4.6 %collective-permute-done.15.refs_2_ = bf16[1,64,2048]{2,1,0:T(8,128)(2,1)S(1)} collective-permute-done((bf16[1,64,2048]{2,1,0:T(8,128)(2,1)S(1)}, bf16[1,64,2048]{2,1,0:T(8,128)(2,1)S(1)}, u32[]{:S(2)}, u32[]{:S(2)}) %collective-permute-start.15) | collective-permute-done | bytes 262176 | tf_op jit(solution)/shard_map/ppermute | solution.py:23
  81.7 6.6 %collective-permute-done.16.refs_3_ = bf16[1,64,2048]{2,1,0:T(8,128)(2,1)S(1)} collective-permute-done((bf16[1,64,2048]{2,1,0:T(8,128)(2,1)S(1)}, bf16[1,64,2048]{2,1,0:T(8,128)(2,1)S(1)}, u32[]{:S(2)}, u32[]{:S(2)}) %collective-permute-start.16) | collective-permute-done | bytes 262176 | tf_op jit(solution)/shard_map/ppermute | solution.py:23
  88.3 12.8 %orthogonalize.1 = (bf16[1,64,2048]{2,1,0:T(8,128)(2,1)S(1)}, bf16[1,64,2048]{2,1,0:T(8,128)(2,1)S(1)}, bf16[1,64,2048]{2,1,0:T(8,128)(2,1)S(1)}, bf16[1,64,2048...) custom-call(bf16[1,64,2048]{2,1,0:T(8,128)(2,1)S(1)} %get-tuple-elem, ...), custom_call_target="tpu_custom_call" | custom-call | flops 11005853696 | bytes 4194304 | tf_op jit(solution)/shard_map/orthogonalize/pallas_call | solution.py:102
  101.1 0.6 collective-permute-start.22
  101.6 3.4 %collective-permute-start.21 = (bf16[1,64,2048]{2,1,0:T(8,128)(2,1)S(1)}, bf16[1,64,2048]{2,1,0:T(8,128)(2,1)S(1)}, u32[]{:S(2)}, u32[]{:S(2)}) collective-permute-start(bf16[1,64,2048]{2,1,0:T(8,128)(2,1)S(1)} %get-tuple-element.18), channel_id=1, source_target_pairs={{0,7},{1,6},{2,5},{3,4},{4,3},{5,2},{6,1},{7,0},{8,15},{9,14},{10,... | collective-permute-start | bytes 786440 | tf_op jit(solution)/shard_map/ppermute | solution.py:23
  105.1 2.0 %collective-permute-start.24 = (bf16[1,64,2048]{2,1,0:T(8,128)(2,1)S(1)}, bf16[1,64,2048]{2,1,0:T(8,128)(2,1)S(1)}, u32[]{:S(2)}, u32[]{:S(2)}) collective-permute-start(bf16[1,64,2048]{2,1,0:T(8,128)(2,1)S(1)} %get-tuple-element.22), channel_id=1, source_target_pairs={{0,3},{1,2},{2,1},{3,0},{4,7},{5,6},{6,5},{7,4},{8,11},{9,10},{10,... | collective-permute-start | bytes 786440 | tf_op jit(solution)/shard_map/ppermute | solution.py:23
  107.0 7.9 %collective-permute-done.22 = bf16[1,64,2048]{2,1,0:T(8,128)(2,1)S(1)} collective-permute-done((bf16[1,64,2048]{2,1,0:T(8,128)(2,1)S(1)}, bf16[1,64,2048]{2,1,0:T(8,128)(2,1)S(1)}, u32[]{:S(2)}, u32[]{:S(2)}) %collective-permute-start.22) | collective-permute-done | bytes 262176 | tf_op jit(solution)/shard_map/ppermute | solution.py:23
  114.9 2.5 %collective-permute-start.25 = (bf16[1,64,2048]{2,1,0:T(8,128)(2,1)S(1)}, bf16[1,64,2048]{2,1,0:T(8,128)(2,1)S(1)}, u32[]{:S(2)}, u32[]{:S(2)}) collective-permute-start(bf16[1,64,2048]{2,1,0:T(8,128)(2,1)S(1)} %get-tuple-element.23), channel_id=1, source_target_pairs={{0,6},{1,7},{2,4},{3,5},{4,2},{5,3},{6,0},{7,1},{8,14},{9,15},{10,... | collective-permute-start | bytes 786440 | tf_op jit(solution)/shard_map/ppermute | solution.py:23
  117.7 7.3 %collective-permute-start.26 = (bf16[1,64,2048]{2,1,0:T(8,128)(2,1)S(1)}, bf16[1,64,2048]{2,1,0:T(8,128)(2,1)S(1)}, u32[]{:S(2)}, u32[]{:S(2)}) collective-permute-start(bf16[1,64,2048]{2,1,0:T(8,128)(2,1)S(1)} %get-tuple-element.24), channel_id=1, source_target_pairs={{0,5},{1,4},{2,7},{3,6},{4,1},{5,0},{6,3},{7,2},{8,13},{9,12},{10,... | collective-permute-start | bytes 786440 | tf_op jit(solution)/shard_map/ppermute | solution.py:23
  124.9 3.8 %add_convert_fusion = bf16[8,1,64,2048]{3,2,1,0:T(8,128)(2,1)S(1)} fusion(bf16[8,1,64,2048]{3,2,1,0:T(8,128)(2,1)} %collective-permute-done.13, bf16[8,1,64,2048]{3,2,1,0:T(8,128)(2,1)} %add_convert_fusion.1, f32[]{:T(128)S(6)} %sub.112, f32[]{:T(128)} %bitcast), kind=kLoop, calls=%fused_computation | loop fusion | flops 6291456 | bytes 6291464 | tf_op jit(solution)/shard_map/convert_element_type | solution.py:203
  129.3 1.8 %collective-permute-done.24 = bf16[1,64,2048]{2,1,0:T(8,128)(2,1)S(1)} collective-permute-done((bf16[1,64,2048]{2,1,0:T(8,128)(2,1)S(1)}, bf16[1,64,2048]{2,1,0:T(8,128)(2,1)S(1)}, u32[]{:S(2)}, u32[]{:S(2)}) %collective-permute-start.24) | collective-permute-done | bytes 262176 | tf_op jit(solution)/shard_map/ppermute | solution.py:23
  131.4 14.7 %collective-permute-done.26 = bf16[1,64,2048]{2,1,0:T(8,128)(2,1)S(1)} collective-permute-done((bf16[1,64,2048]{2,1,0:T(8,128)(2,1)S(1)}, bf16[1,64,2048]{2,1,0:T(8,128)(2,1)S(1)}, u32[]{:S(2)}, u32[]{:S(2)}) %collective-permute-start.26) | collective-permute-done | bytes 262176 | tf_op jit(solution)/shard_map/ppermute | solution.py:23
  146.2 3.6 %collective-permute-done.27 = bf16[1,64,2048]{2,1,0:T(8,128)(2,1)S(1)} collective-permute-done((bf16[1,64,2048]{2,1,0:T(8,128)(2,1)S(1)}, bf16[1,64,2048]{2,1,0:T(8,128)(2,1)S(1)}, u32[]{:S(2)}, u32[]{:S(2)}) %collective-permute-start.27) | collective-permute-done | bytes 262176 | tf_op jit(solution)/shard_map/ppermute | solution.py:23
  150.0 1.3 copy-done.4
  151.3 0.7 copy-done.5
  (56 shorter events, 2.2 us)
Async XLA Ops:
  0.6 8.9 %copy-start.8 = (s32[4,2]{0,1:T(2,128)S(1)}, s32[4,2]{0,1:T(2,128)}, u32[]{:S(2)}) copy-start(s32[4,2]{0,1:T(2,128)} %param.9) | copy-start | bytes 100
  0.7 11.9 %copy-start.2 = (bf16[1,8,64,2048]{3,2,1,0:T(8,128)(2,1)S(1)}, bf16[1,8,64,2048]{3,2,1,0:T(8,128)(2,1)}, u32[]{:S(2)}) copy-start(bf16[1,8,64,2048]{3,2,1,0:T(8,128)(2,1)} %param.8) | copy-start | bytes 6291460
  2.8 9.3 %collective-permute-start.4 = (bf16[1,1,64,2048]{3,2,1,0:T(8,128)(2,1)}, bf16[1,1,64,2048]{3,2,1,0:T(8,128)(2,1)}, u32[]{:S(2)}, u32[]{:S(2)}) collective-permute-start(bf16[1,1,64,2048]{3,2,1,0:T(8,128)(2,1)} %get-tuple-element.41), channel_id=1, source_target_pairs={{0,8},{8,0},{16,24},{24,16},{1,9},{9,1},{17,25},{25,17},{2,10},{10... | collective-permute-start | bytes 786440 | tf_op jit(solution)/shard_map/ppermute | solution.py:23
  3.2 12.4 %collective-permute-start.5 = (bf16[1,1,64,2048]{3,2,1,0:T(8,128)(2,1)}, bf16[1,1,64,2048]{3,2,1,0:T(8,128)(2,1)}, u32[]{:S(2)}, u32[]{:S(2)}) collective-permute-start(bf16[1,1,64,2048]{3,2,1,0:T(8,128)(2,1)} %get-tuple-element.41), channel_id=1, source_target_pairs={{0,16},{8,24},{16,0},{24,8},{1,17},{9,25},{17,1},{25,9},{2,18},{10... | collective-permute-start | bytes 786440 | tf_op jit(solution)/shard_map/ppermute | solution.py:23
  5.7 6.7 %collective-permute-start.8 = (bf16[1,1,64,2048]{3,2,1,0:T(8,128)(2,1)S(1)}, bf16[1,1,64,2048]{3,2,1,0:T(8,128)(2,1)}, u32[]{:S(2)}, u32[]{:S(2)}) collective-permute-start(bf16[1,1,64,2048]{3,2,1,0:T(8,128)(2,1)S(1)} %get-tuple-element.40), channel_id=1, source_target_pairs={{0,8},{8,0},{16,24},{24,16},{1,9},{9,1},{17,25},{25,17},{2,10},{10... | collective-permute-start | bytes 786440 | tf_op jit(solution)/shard_map/ppermute | solution.py:23
  9.0 11.7 %collective-permute-start.17 = (bf16[2,1,64,2048]{3,2,0,1:T(8,128)(2,1)}, bf16[2,1,64,2048]{3,2,0,1:T(8,128)(2,1)S(1)}, u32[]{:S(2)}, u32[]{:S(2)}) collective-permute-start(bf16[2,1,64,2048]{3,2,0,1:T(8,128)(2,1)} %get-tuple-element.37), channel_id=1, source_target_pairs={{0,8},{8,0},{16,24},{24,16},{1,9},{9,1},{17,25},{25,17},{2,10},{10... | collective-permute-start | bytes 1572872 | tf_op jit(solution)/shard_map/ppermute | solution.py:23
  9.3 11.9 %collective-permute-start.2 = (bf16[2,1,64,2048]{3,2,1,0:T(8,128)(2,1)}, bf16[2,1,64,2048]{3,2,1,0:T(8,128)(2,1)S(1)}, u32[]{:S(2)}, u32[]{:S(2)}) collective-permute-start(bf16[2,1,64,2048]{3,2,1,0:T(8,128)(2,1)} %get-tuple-element.36), channel_id=1, source_target_pairs={{0,8},{8,0},{16,24},{24,16},{1,9},{9,1},{17,25},{25,17},{2,10},{10... | collective-permute-start | bytes 1572872 | tf_op jit(solution)/shard_map/ppermute | solution.py:23
  12.1 3.6 %copy-start.7 = (bf16[2,1,64,2048]{3,2,0,1:T(8,128)(2,1)S(1)}, bf16[2,1,64,2048]{3,2,0,1:T(8,128)(2,1)}, u32[]{:S(2)}) copy-start(bf16[2,1,64,2048]{3,2,0,1:T(8,128)(2,1)} %get-tuple-element.35) | copy-start | bytes 1572868
  12.1 8.6 %collective-permute-start.9 = (bf16[1,1,64,2048]{3,2,1,0:T(8,128)(2,1)S(1)}, bf16[1,1,64,2048]{3,2,1,0:T(8,128)(2,1)S(1)}, u32[]{:S(2)}, u32[]{:S(2)}) collective-permute-start(bf16[1,1,64,2048]{3,2,1,0:T(8,128)(2,1)S(1)} %get-tuple-element.40), channel_id=1, source_target_pairs={{0,16},{8,24},{16,0},{24,8},{1,17},{9,25},{17,1},{25,9},{2,18},{10... | collective-permute-start | bytes 786440 | tf_op jit(solution)/shard_map/ppermute | solution.py:23
  12.5 31.0 %collective-permute-start = (bf16[8,1,64,2048]{3,2,1,0:T(8,128)(2,1)}, bf16[8,1,64,2048]{3,2,1,0:T(8,128)(2,1)S(1)}, u32[]{:S(2)}, u32[]{:S(2)}) collective-permute-start(bf16[8,1,64,2048]{3,2,1,0:T(8,128)(2,1)} %bitcast.175), channel_id=1, source_target_pairs={{0,8},{8,0},{16,24},{24,16},{1,9},{9,1},{17,25},{25,17},{2,10},{10... | collective-permute-start | bytes 6291464 | tf_op jit(solution)/shard_map/ppermute | solution.py:23
  15.7 16.8 %collective-permute-start.1 = (bf16[2,1,64,2048]{3,2,0,1:T(8,128)(2,1)S(1)}, bf16[2,1,64,2048]{3,2,0,1:T(8,128)(2,1)S(1)}, u32[]{:S(2)}, u32[]{:S(2)}) collective-permute-start(bf16[2,1,64,2048]{3,2,0,1:T(8,128)(2,1)S(1)} %copy-done.7), channel_id=1, source_target_pairs={{0,8},{8,0},{16,24},{24,16},{1,9},{9,1},{17,25},{25,17},{2,10},{10... | collective-permute-start | bytes 1572872 | tf_op jit(solution)/shard_map/ppermute | solution.py:23
  20.7 3.3 %collective-permute-start.6 = (bf16[1,1,64,2048]{3,2,1,0:T(8,128)(2,1)}, bf16[1,1,64,2048]{3,2,1,0:T(8,128)(2,1)S(1)}, u32[]{:S(2)}, u32[]{:S(2)}) collective-permute-start(bf16[1,1,64,2048]{3,2,1,0:T(8,128)(2,1)} %collective-permute-done.5), channel_id=1, source_target_pairs={{0,8},{8,0},{16,24},{24,16},{1,9},{9,1},{17,25},{25,17},{2,10},{10... | collective-permute-start | bytes 786440 | tf_op jit(solution)/shard_map/ppermute | solution.py:23
  20.7 5.8 %collective-permute-start.10 = (bf16[1,1,64,2048]{3,2,1,0:T(8,128)(2,1)S(1)}, bf16[1,1,64,2048]{3,2,1,0:T(8,128)(2,1)S(1)}, u32[]{:S(2)}, u32[]{:S(2)}) collective-permute-start(bf16[1,1,64,2048]{3,2,1,0:T(8,128)(2,1)S(1)} %collective-permute-done.9), channel_id=1, source_target_pairs={{0,8},{8,0},{16,24},{24,16},{1,9},{9,1},{17,25},{25,17},{2,10},{10... | collective-permute-start | bytes 786440 | tf_op jit(solution)/shard_map/ppermute | solution.py:23
  23.6 13.9 %collective-permute-start.18 = (bf16[2,1,64,2048]{3,2,1,0:T(8,128)(2,1)S(1)}, bf16[2,1,64,2048]{3,2,1,0:T(8,128)(2,1)S(1)}, u32[]{:S(2)}, u32[]{:S(2)}) collective-permute-start(bf16[2,1,64,2048]{3,2,1,0:T(8,128)(2,1)S(1)} %get-tuple-element.39), channel_id=1, source_target_pairs={{0,16},{8,24},{16,0},{24,8},{1,17},{9,25},{17,1},{25,9},{2,18},{10... | collective-permute-start | bytes 1572872 | tf_op jit(solution)/shard_map/ppermute | solution.py:23
  24.0 8.5 %copy-start = (f32[1,8,64,2048]{3,2,1,0:T(8,128)S(1)}, f32[1,8,64,2048]{3,2,1,0:T(8,128)}, u32[]{:S(2)}) copy-start(f32[1,8,64,2048]{3,2,1,0:T(8,128)} %param.6) | copy-start | bytes 12582916
  26.5 11.1 %copy-start.3 = (bf16[1,8,64,2048]{3,2,1,0:T(8,128)(2,1)S(1)}, bf16[1,8,64,2048]{3,2,1,0:T(8,128)(2,1)}, u32[]{:S(2)}) copy-start(bf16[1,8,64,2048]{3,2,1,0:T(8,128)(2,1)} %param.7) | copy-start | bytes 6291460
  27.4 19.4 %collective-permute-start.11 = (bf16[1,64,2048]{2,1,0:T(8,128)(2,1)S(1)}, bf16[1,64,2048]{2,1,0:T(8,128)(2,1)S(1)}, u32[]{:S(2)}, u32[]{:S(2)}) collective-permute-start(bf16[1,64,2048]{2,1,0:T(8,128)(2,1)S(1)} %get-tuple-element.48), channel_id=1, source_target_pairs={{0,6},{1,7},{2,4},{3,5},{4,2},{5,3},{6,0},{7,1},{8,14},{9,15},{10,... | collective-permute-start | bytes 786440 | tf_op jit(solution)/shard_map/ppermute | solution.py:23
  31.3 15.4 %collective-permute-start.7 = (bf16[1,64,2048]{2,1,0:T(8,128)(2,1)S(1)}, bf16[1,64,2048]{2,1,0:T(8,128)(2,1)S(1)}, u32[]{:S(2)}, u32[]{:S(2)}) collective-permute-start(bf16[1,64,2048]{2,1,0:T(8,128)(2,1)S(1)} %get-tuple-element.50), channel_id=1, source_target_pairs={{0,7},{1,6},{2,5},{3,4},{4,3},{5,2},{6,1},{7,0},{8,15},{9,14},{10,... | collective-permute-start | bytes 786440 | tf_op jit(solution)/shard_map/ppermute | solution.py:23
  37.5 6.4 %copy-start.6 = (bf16[1,8,64,2048]{3,2,1,0:T(8,128)(2,1)S(1)}, bf16[1,8,64,2048]{3,2,1,0:T(8,128)(2,1)}, u32[]{:S(2)}) copy-start(bf16[1,8,64,2048]{3,2,1,0:T(8,128)(2,1)} %param.5) | copy-start | bytes 6291460
  39.5 33.5 %collective-permute-start.19 = (bf16[1,64,2048]{2,1,0:T(8,128)(2,1)S(1)}, bf16[1,64,2048]{2,1,0:T(8,128)(2,1)S(1)}, u32[]{:S(2)}, u32[]{:S(2)}) collective-permute-start(bf16[1,64,2048]{2,1,0:T(8,128)(2,1)S(1)} %get-tuple-element.43), channel_id=1, source_target_pairs={{0,4},{1,5},{2,6},{3,7},{4,0},{5,1},{6,2},{7,3},{8,12},{9,13},{10,... | collective-permute-start | bytes 786440 | tf_op jit(solution)/shard_map/ppermute | solution.py:23
  42.1 35.0 %collective-permute-start.20 = (bf16[1,64,2048]{2,1,0:T(8,128)(2,1)S(1)}, bf16[1,64,2048]{2,1,0:T(8,128)(2,1)S(1)}, u32[]{:S(2)}, u32[]{:S(2)}) collective-permute-start(bf16[1,64,2048]{2,1,0:T(8,128)(2,1)S(1)} %get-tuple-element.42), channel_id=1, source_target_pairs={{0,5},{1,4},{2,7},{3,6},{4,1},{5,0},{6,3},{7,2},{8,13},{9,12},{10,... | collective-permute-start | bytes 786440 | tf_op jit(solution)/shard_map/ppermute | solution.py:23
  43.4 12.4 %collective-permute-start.3 = (bf16[2,1,64,2048]{3,2,1,0:T(8,128)(2,1)S(1)}, bf16[2,1,64,2048]{3,2,1,0:T(8,128)(2,1)S(1)}, u32[]{:S(2)}, u32[]{:S(2)}) collective-permute-start(bf16[2,1,64,2048]{3,2,1,0:T(8,128)(2,1)S(1)} %get-tuple-element.15), channel_id=1, source_target_pairs={{0,16},{8,24},{16,0},{24,8},{1,17},{9,25},{17,1},{25,9},{2,18},{10... | collective-permute-start | bytes 1572872 | tf_op jit(solution)/shard_map/ppermute | solution.py:23
  55.9 14.7 %collective-permute-start.12 = (bf16[2,1,64,2048]{3,2,0,1:T(8,128)(2,1)S(1)}, bf16[2,1,64,2048]{3,2,0,1:T(8,128)(2,1)S(1)}, u32[]{:S(2)}, u32[]{:S(2)}) collective-permute-start(bf16[2,1,64,2048]{3,2,0,1:T(8,128)(2,1)S(1)} %fusion.3), channel_id=1, source_target_pairs={{0,16},{8,24},{16,0},{24,8},{1,17},{9,25},{17,1},{25,9},{2,18},{10... | collective-permute-start | bytes 1572872 | tf_op jit(solution)/shard_map/ppermute | solution.py:23
  58.2 23.5 %collective-permute-start.15 = (bf16[1,64,2048]{2,1,0:T(8,128)(2,1)S(1)}, bf16[1,64,2048]{2,1,0:T(8,128)(2,1)S(1)}, u32[]{:S(2)}, u32[]{:S(2)}) collective-permute-start(bf16[1,64,2048]{2,1,0:T(8,128)(2,1)S(1)} %get-tuple-element.45), channel_id=1, source_target_pairs={{0,2},{1,3},{2,0},{3,1},{4,6},{5,7},{6,4},{7,5},{8,10},{9,11},{10,... | collective-permute-start | bytes 786440 | tf_op jit(solution)/shard_map/ppermute | solution.py:23
  70.6 17.7 %collective-permute-start.16 = (bf16[1,64,2048]{2,1,0:T(8,128)(2,1)S(1)}, bf16[1,64,2048]{2,1,0:T(8,128)(2,1)S(1)}, u32[]{:S(2)}, u32[]{:S(2)}) collective-permute-start(bf16[1,64,2048]{2,1,0:T(8,128)(2,1)S(1)} %get-tuple-element.44), channel_id=1, source_target_pairs={{0,3},{1,2},{2,1},{3,0},{4,7},{5,6},{6,5},{7,4},{8,11},{9,10},{10,... | collective-permute-start | bytes 786440 | tf_op jit(solution)/shard_map/ppermute | solution.py:23
  70.6 47.0 %collective-permute-start.13 = (bf16[8,1,64,2048]{3,2,1,0:T(8,128)(2,1)}, bf16[8,1,64,2048]{3,2,1,0:T(8,128)(2,1)}, u32[]{:S(2)}, u32[]{:S(2)}) collective-permute-start(bf16[8,1,64,2048]{3,2,1,0:T(8,128)(2,1)} %add_convert_fusion.1), channel_id=1, source_target_pairs={{0,16},{8,24},{16,0},{24,8},{1,17},{9,25},{17,1},{25,9},{2,18},{10... | collective-permute-start | bytes 6291464 | tf_op jit(solution)/shard_map/ppermute | solution.py:23
  72.9 15.4 %copy-start.1 = (f32[1,8,64,2048]{3,2,1,0:T(8,128)}, f32[1,8,64,2048]{3,2,1,0:T(8,128)S(1)}, u32[]{:S(2)}) copy-start(f32[1,8,64,2048]{3,2,1,0:T(8,128)S(1)} %get-tuple-element.27) | copy-start | bytes 12582916
  73.0 15.3 %collective-permute-start.14 = (bf16[1,64,2048]{2,1,0:T(8,128)(2,1)S(1)}, bf16[1,64,2048]{2,1,0:T(8,128)(2,1)S(1)}, u32[]{:S(2)}, u32[]{:S(2)}) collective-permute-start(bf16[1,64,2048]{2,1,0:T(8,128)(2,1)S(1)} %get-tuple-element.46), channel_id=1, source_target_pairs={{0,1},{1,0},{2,3},{3,2},{4,5},{5,4},{6,7},{7,6},{8,9},{9,8},{10,11... | collective-permute-start | bytes 786440 | tf_op jit(solution)/shard_map/ppermute | solution.py:23
  101.1 13.8 %collective-permute-start.22 = (bf16[1,64,2048]{2,1,0:T(8,128)(2,1)S(1)}, bf16[1,64,2048]{2,1,0:T(8,128)(2,1)S(1)}, u32[]{:S(2)}, u32[]{:S(2)}) collective-permute-start(bf16[1,64,2048]{2,1,0:T(8,128)(2,1)S(1)} %get-tuple-element.20), channel_id=1, source_target_pairs={{0,1},{1,0},{2,3},{3,2},{4,5},{5,4},{6,7},{7,6},{8,9},{9,8},{10,11... | collective-permute-start | bytes 786440 | tf_op jit(solution)/shard_map/ppermute | solution.py:23
  101.6 27.1 %collective-permute-start.21 = (bf16[1,64,2048]{2,1,0:T(8,128)(2,1)S(1)}, bf16[1,64,2048]{2,1,0:T(8,128)(2,1)S(1)}, u32[]{:S(2)}, u32[]{:S(2)}) collective-permute-start(bf16[1,64,2048]{2,1,0:T(8,128)(2,1)S(1)} %get-tuple-element.18), channel_id=1, source_target_pairs={{0,7},{1,6},{2,5},{3,4},{4,3},{5,2},{6,1},{7,0},{8,15},{9,14},{10,... | collective-permute-start | bytes 786440 | tf_op jit(solution)/shard_map/ppermute | solution.py:23
  105.0 24.1 %collective-permute-start.23 = (bf16[1,64,2048]{2,1,0:T(8,128)(2,1)S(1)}, bf16[1,64,2048]{2,1,0:T(8,128)(2,1)S(1)}, u32[]{:S(2)}, u32[]{:S(2)}) collective-permute-start(bf16[1,64,2048]{2,1,0:T(8,128)(2,1)S(1)} %get-tuple-element.21), channel_id=1, source_target_pairs={{0,2},{1,3},{2,0},{3,1},{4,6},{5,7},{6,4},{7,5},{8,10},{9,11},{10,... | collective-permute-start | bytes 786440 | tf_op jit(solution)/shard_map/ppermute | solution.py:23
  105.1 26.1 %collective-permute-start.24 = (bf16[1,64,2048]{2,1,0:T(8,128)(2,1)S(1)}, bf16[1,64,2048]{2,1,0:T(8,128)(2,1)S(1)}, u32[]{:S(2)}, u32[]{:S(2)}) collective-permute-start(bf16[1,64,2048]{2,1,0:T(8,128)(2,1)S(1)} %get-tuple-element.22), channel_id=1, source_target_pairs={{0,3},{1,2},{2,1},{3,0},{4,7},{5,6},{6,5},{7,4},{8,11},{9,10},{10,... | collective-permute-start | bytes 786440 | tf_op jit(solution)/shard_map/ppermute | solution.py:23
  114.9 16.4 %collective-permute-start.25 = (bf16[1,64,2048]{2,1,0:T(8,128)(2,1)S(1)}, bf16[1,64,2048]{2,1,0:T(8,128)(2,1)S(1)}, u32[]{:S(2)}, u32[]{:S(2)}) collective-permute-start(bf16[1,64,2048]{2,1,0:T(8,128)(2,1)S(1)} %get-tuple-element.23), channel_id=1, source_target_pairs={{0,6},{1,7},{2,4},{3,5},{4,2},{5,3},{6,0},{7,1},{8,14},{9,15},{10,... | collective-permute-start | bytes 786440 | tf_op jit(solution)/shard_map/ppermute | solution.py:23
  117.7 28.4 %collective-permute-start.26 = (bf16[1,64,2048]{2,1,0:T(8,128)(2,1)S(1)}, bf16[1,64,2048]{2,1,0:T(8,128)(2,1)S(1)}, u32[]{:S(2)}, u32[]{:S(2)}) collective-permute-start(bf16[1,64,2048]{2,1,0:T(8,128)(2,1)S(1)} %get-tuple-element.24), channel_id=1, source_target_pairs={{0,5},{1,4},{2,7},{3,6},{4,1},{5,0},{6,3},{7,2},{8,13},{9,12},{10,... | collective-permute-start | bytes 786440 | tf_op jit(solution)/shard_map/ppermute | solution.py:23
  128.7 21.0 %collective-permute-start.27 = (bf16[1,64,2048]{2,1,0:T(8,128)(2,1)S(1)}, bf16[1,64,2048]{2,1,0:T(8,128)(2,1)S(1)}, u32[]{:S(2)}, u32[]{:S(2)}) collective-permute-start(bf16[1,64,2048]{2,1,0:T(8,128)(2,1)S(1)} %get-tuple-element.25), channel_id=1, source_target_pairs={{0,4},{1,5},{2,6},{3,7},{4,0},{5,1},{6,2},{7,3},{8,12},{9,13},{10,... | collective-permute-start | bytes 786440 | tf_op jit(solution)/shard_map/ppermute | solution.py:23
  150.0 1.3 copy-start.4
  150.0 2.0 %copy-start.5 = (bf16[1,8,64,2048]{3,2,1,0:T(8,128)(2,1)}, bf16[1,8,64,2048]{3,2,1,0:T(8,128)(2,1)S(1)}, u32[]{:S(2)}) copy-start(bf16[1,8,64,2048]{3,2,1,0:T(8,128)(2,1)S(1)} %get-tuple-element.52) | copy-start | bytes 6291460

commit v15 on v14

--- a/solution.py
+++ b/solution.py
@@ -170,9 +170,9 @@
         else:
             sent = mixed.astype(BF16)
             if turn == 2:
-                sent = after(sent, weight_near)
+                sent = after(sent)
             elif turn == 4:
-                sent = after(sent, arrived[2], blocks[7 * shards // 8], blocks[6 * shards // 8])
+                sent = after(sent, arrived[2], blocks[7 * shards // 8], weight_near, blocks[6 * shards // 8])
             far = swapped(sent, "rep", 2)
             far_mixed = far.astype(F32)
         arrived.append(far)

time: 152 us -> 145 us (0.954)
  starting transfers between devices: 45.9 us -> 35.6 us
  waiting for transfers between devices: 59.7 us -> 63.1 us
    ppermute x28, starting transfers between devices: 45.9 us -> 35.6 us  [swapped(): lax.ppermute(values, axis, [(i, i ^ offset) for i in range(lax.axis_size(...]
    ppermute x28, waiting for transfers between devices: 59.7 us -> 63.1 us  [swapped(): lax.ppermute(values, axis, [(i, i ^ offset) for i in range(lax.axis_size(...]
  transfers between devices with their start and end apart: 28 -> 28, of which waited for: 10 -> 12; matrix products, arithmetic and copies ran while one was open for 17% -> 18% of each run, Pallas kernels for 8% -> 9%
where the time goes in v15:
time: 145 us
  waiting for transfers between devices  63.1 us (44%)
  starting transfers between devices  35.6 us (25%)
  other arithmetic  21.6 us (15%)
  Pallas kernels  12.8 us (9%)
  local copies, waits for them, and re-layouts  9 us (6%)
  between operations  2.81 us (2%)
    ppermute x28, waiting for transfers between devices, swapped(): lax.ppermute(values, axis, [(i, i ^ offset) for i in range(lax.axis_size(...  63.1 us
    ppermute x28, starting transfers between devices, swapped(): lax.ppermute(values, axis, [(i, i ^ offset) for i in range(lax.axis_size(...  35.6 us
    pallas_call x1, Pallas kernels, orthogonalize(): pl.pallas_call(body, grid=(each,), in_specs=[block] * count, out_specs=[b...  12.8 us
    convert_element_type x2, local copies, waits for them, and re-layouts, local(): rounded = own.astype(BF16)  5.18 us
    dynamic_update_slice x3, other arithmetic, local(): lax.dynamic_update_slice_in_dim(new_tracker, group, start, axis=0)  4.98 us
    convert_element_type x1, other arithmetic, local(): mixed_weight = (second * weight_own.astype(F32) + (1.0 - second) * weight...  3.64 us
    convert_element_type x2, other arithmetic, local(): sent = mixed.astype(BF16)  3.29 us
    add x1, other arithmetic, local(): second * mixed  3.17 us
  transfers between devices with their start and end apart: 28, of which 12 were waited for; matrix products, arithmetic and copies ran while one was open for 18% of the time, Pallas kernels for 9%

profile of v15, /device:TPU:0, one launch (start us, length us, event | category | flops | bytes accessed | tf_op | source)
XLA Modules:
  0.0 144.9 jit_solution(13157386604527405)
XLA Ops:
  0.7 2.1 %dynamic-slice_convert_fusion.9 = (bf16[1,1,64,2048]{3,2,1,0:T(8,128)(2,1)S(1)}, bf16[1,1,64,2048]{3,2,1,0:T(8,128)(2,1)}) fusion(f32[1,8,64,2048]{3,2,1,0:T(8,128)} %param.6, s32[]{:T(128)S(6)} %select_n.143, s32[]{:T(128)S(6)} %select_n.141), kind=kLoop, calls=%fused_computation.53 | loop fusion | bytes 1048584 | tf_op jit(solution)/shard_map/convert_element_type | solution.py:165
  2.8 0.5 collective-permute-start.4
  3.2 2.5 %collective-permute-start.5 = (bf16[1,1,64,2048]{3,2,1,0:T(8,128)(2,1)}, bf16[1,1,64,2048]{3,2,1,0:T(8,128)(2,1)}, u32[]{:S(2)}, u32[]{:S(2)}) collective-permute-start(bf16[1,1,64,2048]{3,2,1,0:T(8,128)(2,1)} %get-tuple-element.39), channel_id=1, source_target_pairs={{0,16},{8,24},{16,0},{24,8},{1,17},{9,25},{17,1},{25,9},{2,18},{10... | collective-permute-start | bytes 786440 | tf_op jit(solution)/shard_map/ppermute | solution.py:23
  6.0 3.1 %fusion.6 = (bf16[2,1,64,2048]{3,2,0,1:T(8,128)(2,1)}, bf16[2,1,64,2048]{3,2,1,0:T(8,128)(2,1)}, bf16[2,1,64,2048]{3,2,0,1:T(8,128)(2,1)}) fusion(f32[1,8,64,2048]{3,2,1,0:T(8,128)} %param.6, s32[]{:T(128)S(6)} %select_n.138, s32[]{:T(128)S(6)} %select_n.140, s32[]{:T(128)S(6)} %select_n.153), kind=kLoop, calls=%fused_computation.24 | loop fusion | bytes 3145740 | tf_op jit(solution)/shard_map/convert_element_type | solution.py:165
  9.5 0.7 constant_dynamic-slice_fusion
  12.5 3.2 %subtract_add_fusion = (f32[1,1,64,2048]{3,2,1,0:T(8,128)S(1)}, f32[1,1,64,2048]{3,2,1,0:T(8,128)S(1)}) fusion(bf16[1,1,64,2048]{3,2,1,0:T(8,128)(2,1)} %collective-permute-done.8, f32[1,8,64,2048]{3,2,1,0:T(8,128)} %param.6, s32[]{:T(128)S(6)} %select_n.143, bf16[1,8,64,2048]{3,2,1,0:T(8,128)(2,1)S(1)} %copy-done.2, bf16[1,8,64,2048]{3,2,1,0:T(8,128)(2,1)} %param.7, ...), kind=kLoop, calls=%fused_computation.50 | loop fusion | flops 2359296 | bytes 3670036 | tf_op jit(solution)/shard_map/add | solution.py:179
  15.7 0.4 collective-permute-start
  16.1 4.6 %collective-permute-done.9 = bf16[1,1,64,2048]{3,2,1,0:T(8,128)(2,1)S(1)} collective-permute-done((bf16[1,1,64,2048]{3,2,1,0:T(8,128)(2,1)S(1)}, bf16[1,1,64,2048]{3,2,1,0:T(8,128)(2,1)S(1)}, u32[]{:S(2)}, u32[]{:S(2)}) %collective-permute-start.9) | collective-permute-done | bytes 262176 | tf_op jit(solution)/shard_map/ppermute | solution.py:23
  20.6 0.5 collective-permute-start.10
  21.1 2.5 %fusion.4 = (bf16[2,1,64,2048]{3,2,1,0:T(8,128)(2,1)S(1)}, bf16[2,1,64,2048]{3,2,1,0:T(8,128)(2,1)S(1)}) fusion(bf16[2,1,64,2048]{3,2,1,0:T(8,128)(2,1)S(1)} %collective-permute-done.2, f32[1,8,64,2048]{3,2,1,0:T(8,128)} %param.6, s32[]{:T(128)S(6)} %select_n.140, f32[]{:T(128)S(6)} %sub.108, f32[]{:T(128)} %bitcast.1, ...), kind=kLoop, calls=%fused_computation.22 | loop fusion | flops 2621440 | bytes 4194320 | tf_op jit(solution)/shard_map/convert_element_type | solution.py:171
  24.0 0.5 reshape.500
  24.5 2.0 %convert_bitcast_fusion.1 = (bf16[1,64,2048]{2,1,0:T(8,128)(2,1)S(1)}, f32[1,8,64,2048]{3,2,1,0:T(8,128)S(1)}) fusion(f32[1,1,64,2048]{3,2,1,0:T(8,128)S(1)} %get-tuple-element.32, bf16[1,1,64,2048]{3,2,1,0:T(8,128)(2,1)S(1)} %collective-permute-done.6, f32[]{:T(128)S(6)} %sub.113, bf16[1,1,64,2048]{3,2,1,0:T(8,128)(2,1)} %collective-permute-done.5, ...), kind=kLoop, calls=%fused_computation.86 | loop fusion | flops 1048576 | bytes 1835024 | tf_op jit(solution)/shard_map/convert_element_type | solution.py:188
  26.5 0.9 convert_bitcast_fusion
  27.4 3.9 %collective-permute-start.11 = (bf16[1,64,2048]{2,1,0:T(8,128)(2,1)S(1)}, bf16[1,64,2048]{2,1,0:T(8,128)(2,1)S(1)}, u32[]{:S(2)}, u32[]{:S(2)}) collective-permute-start(bf16[1,64,2048]{2,1,0:T(8,128)(2,1)S(1)} %get-tuple-element.46), channel_id=1, source_target_pairs={{0,6},{1,7},{2,4},{3,5},{4,2},{5,3},{6,0},{7,1},{8,14},{9,15},{10,... | collective-permute-start | bytes 786440 | tf_op jit(solution)/shard_map/ppermute | solution.py:23
  31.3 1.2 collective-permute-start.7
  32.5 1.5 %collective-permute-start.3 = (bf16[2,1,64,2048]{3,2,1,0:T(8,128)(2,1)S(1)}, bf16[2,1,64,2048]{3,2,1,0:T(8,128)(2,1)S(1)}, u32[]{:S(2)}, u32[]{:S(2)}) collective-permute-start(bf16[2,1,64,2048]{3,2,1,0:T(8,128)(2,1)S(1)} %get-tuple-element.36), channel_id=1, source_target_pairs={{0,16},{8,24},{16,0},{24,8},{1,17},{9,25},{17,1},{25,9},{2,18},{10... | collective-permute-start | bytes 1572872 | tf_op jit(solution)/shard_map/ppermute | solution.py:23
  34.0 0.8 fusion.3
  34.8 3.7 %collective-permute-done.18 = bf16[2,1,64,2048]{3,2,1,0:T(8,128)(2,1)S(1)} collective-permute-done((bf16[2,1,64,2048]{3,2,1,0:T(8,128)(2,1)S(1)}, bf16[2,1,64,2048]{3,2,1,0:T(8,128)(2,1)S(1)}, u32[]{:S(2)}, u32[]{:S(2)}) %collective-permute-start.18) | collective-permute-done | bytes 524320 | tf_op jit(solution)/shard_map/ppermute | solution.py:23
  38.5 1.7 %bitcast_dynamic-update-slice_fusion.2 = (f32[1,8,64,2048]{3,2,1,0:T(8,128)S(1)}, bf16[2,1,64,2048]{3,2,1,0:T(8,128)(2,1)S(1)}) fusion(f32[1,8,64,2048]{3,2,1,0:T(8,128)S(1)} %get-tuple-element.47, s32[]{:T(128)S(6)} %select_n.153, bf16[2,1,64,2048]{3,2,1,0:T(8,128)(2,1)S(1)} %collective-permute-done.18, f32[]{:T(128)S(6)} %sub.112, ...), kind=kLoop, calls=%fused_computation.10 | loop fusion | flops 3407872 | bytes 4718612 | tf_op jit(solution)/shard_map/dynamic_update_slice | solution.py:194
  40.2 8.6 %collective-permute-done.3 = bf16[2,1,64,2048]{3,2,1,0:T(8,128)(2,1)S(1)} collective-permute-done((bf16[2,1,64,2048]{3,2,1,0:T(8,128)(2,1)S(1)}, bf16[2,1,64,2048]{3,2,1,0:T(8,128)(2,1)S(1)}, u32[]{:S(2)}, u32[]{:S(2)}) %collective-permute-start.3) | collective-permute-done | bytes 524320 | tf_op jit(solution)/shard_map/ppermute | solution.py:23
  48.8 1.7 %bitcast_dynamic-update-slice_fusion.1 = (f32[1,8,64,2048]{3,2,1,0:T(8,128)S(1)}, bf16[2,1,64,2048]{3,2,1,0:T(8,128)(2,1)S(1)}) fusion(f32[1,8,64,2048]{3,2,1,0:T(8,128)S(1)} %get-tuple-element.29, s32[]{:T(128)S(6)} %select_n.140, bf16[2,1,64,2048]{3,2,1,0:T(8,128)(2,1)S(1)} %collective-permute-done.3, f32[]{:T(128)S(6)} %sub.112, ...), kind=kLoop, calls=%fused_computation.9 | loop fusion | flops 3407872 | bytes 4718612 | tf_op jit(solution)/shard_map/dynamic_update_slice | solution.py:194
  50.5 1.6 %collective-permute-start.15 = (bf16[1,64,2048]{2,1,0:T(8,128)(2,1)S(1)}, bf16[1,64,2048]{2,1,0:T(8,128)(2,1)S(1)}, u32[]{:S(2)}, u32[]{:S(2)}) collective-permute-start(bf16[1,64,2048]{2,1,0:T(8,128)(2,1)S(1)} %get-tuple-element.43), channel_id=1, source_target_pairs={{0,2},{1,3},{2,0},{3,1},{4,6},{5,7},{6,4},{7,5},{8,10},{9,11},{10,... | collective-permute-start | bytes 786440 | tf_op jit(solution)/shard_map/ppermute | solution.py:23
  52.2 1.4 collective-permute-start.16
  53.6 2.7 %collective-permute-start.19 = (bf16[1,64,2048]{2,1,0:T(8,128)(2,1)S(1)}, bf16[1,64,2048]{2,1,0:T(8,128)(2,1)S(1)}, u32[]{:S(2)}, u32[]{:S(2)}) collective-permute-start(bf16[1,64,2048]{2,1,0:T(8,128)(2,1)S(1)} %get-tuple-element.41), channel_id=1, source_target_pairs={{0,4},{1,5},{2,6},{3,7},{4,0},{5,1},{6,2},{7,3},{8,12},{9,13},{10,... | collective-permute-start | bytes 786440 | tf_op jit(solution)/shard_map/ppermute | solution.py:23
  56.6 1.0 collective-permute-start.12
  57.5 2.8 %add_convert_fusion.1 = bf16[8,1,64,2048]{3,2,1,0:T(8,128)(2,1)} fusion(bf16[8,1,64,2048]{3,2,1,0:T(8,128)(2,1)S(1)} %collective-permute-done, f32[]{:T(128)S(6)} %sub.108, f32[]{:T(128)} %bitcast.1, bf16[1,8,64,2048]{3,2,1,0:T(8,128)(2,1)S(1)} %copy-done.6), kind=kLoop, calls=%fused_computation.1 | loop fusion | flops 6291456 | bytes 6291464 | tf_op jit(solution)/shard_map/convert_element_type | solution.py:198
  60.3 8.1 %collective-permute-done.12 = bf16[2,1,64,2048]{3,2,0,1:T(8,128)(2,1)S(1)} collective-permute-done((bf16[2,1,64,2048]{3,2,0,1:T(8,128)(2,1)S(1)}, bf16[2,1,64,2048]{3,2,0,1:T(8,128)(2,1)S(1)}, u32[]{:S(2)}, u32[]{:S(2)}) %collective-permute-start.12) | collective-permute-done | bytes 524320 | tf_op jit(solution)/shard_map/ppermute | solution.py:23
  68.5 1.4 collective-permute-start.13
  69.9 1.7 %bitcast_dynamic-update-slice_fusion = (f32[1,8,64,2048]{3,2,1,0:T(8,128)S(1)}, bf16[2,1,64,2048]{3,2,0,1:T(8,128)(2,1)S(1)}) fusion(f32[1,8,64,2048]{3,2,1,0:T(8,128)S(1)} %get-tuple-element.27, s32[]{:T(128)S(6)} %select_n.138, bf16[2,1,64,2048]{3,2,0,1:T(8,128)(2,1)S(1)} %collective-permute-done.12, f32[]{:T(128)S(6)} %sub.112, ...), kind=kLoop, calls=%fused_computation.8 | loop fusion | flops 3407872 | bytes 4718612 | tf_op jit(solution)/shard_map/dynamic_update_slice | solution.py:194
  71.6 1.6 %collective-permute-start.14 = (bf16[1,64,2048]{2,1,0:T(8,128)(2,1)S(1)}, bf16[1,64,2048]{2,1,0:T(8,128)(2,1)S(1)}, u32[]{:S(2)}, u32[]{:S(2)}) collective-permute-start(bf16[1,64,2048]{2,1,0:T(8,128)(2,1)S(1)} %get-tuple-element.44), channel_id=1, source_target_pairs={{0,1},{1,0},{2,3},{3,2},{4,5},{5,4},{6,7},{7,6},{8,9},{9,8},{10,11... | collective-permute-start | bytes 786440 | tf_op jit(solution)/shard_map/ppermute | solution.py:23
  73.2 2.3 %collective-permute-done.16.refs_3_ = bf16[1,64,2048]{2,1,0:T(8,128)(2,1)S(1)} collective-permute-done((bf16[1,64,2048]{2,1,0:T(8,128)(2,1)S(1)}, bf16[1,64,2048]{2,1,0:T(8,128)(2,1)S(1)}, u32[]{:S(2)}, u32[]{:S(2)}) %collective-permute-start.16) | collective-permute-done | bytes 262176 | tf_op jit(solution)/shard_map/ppermute | solution.py:23
  75.6 2.8 %collective-permute-done.20.refs_5_ = bf16[1,64,2048]{2,1,0:T(8,128)(2,1)S(1)} collective-permute-done((bf16[1,64,2048]{2,1,0:T(8,128)(2,1)S(1)}, bf16[1,64,2048]{2,1,0:T(8,128)(2,1)S(1)}, u32[]{:S(2)}, u32[]{:S(2)}) %collective-permute-start.20) | collective-permute-done | bytes 262176 | tf_op jit(solution)/shard_map/ppermute | solution.py:23
  78.3 3.0 %collective-permute-done.14.refs_1_ = bf16[1,64,2048]{2,1,0:T(8,128)(2,1)S(1)} collective-permute-done((bf16[1,64,2048]{2,1,0:T(8,128)(2,1)S(1)}, bf16[1,64,2048]{2,1,0:T(8,128)(2,1)S(1)}, u32[]{:S(2)}, u32[]{:S(2)}) %collective-permute-start.14) | collective-permute-done | bytes 262176 | tf_op jit(solution)/shard_map/ppermute | solution.py:23
  81.4 12.8 %orthogonalize.1 = (bf16[1,64,2048]{2,1,0:T(8,128)(2,1)S(1)}, bf16[1,64,2048]{2,1,0:T(8,128)(2,1)S(1)}, bf16[1,64,2048]{2,1,0:T(8,128)(2,1)S(1)}, bf16[1,64,2048...) custom-call(bf16[1,64,2048]{2,1,0:T(8,128)(2,1)S(1)} %get-tuple-elem, ...), custom_call_target="tpu_custom_call" | custom-call | flops 11005853696 | bytes 4194304 | tf_op jit(solution)/shard_map/orthogonalize/pallas_call | solution.py:102
  94.2 0.6 collective-permute-start.22
  94.7 4.6 %collective-permute-start.21 = (bf16[1,64,2048]{2,1,0:T(8,128)(2,1)S(1)}, bf16[1,64,2048]{2,1,0:T(8,128)(2,1)S(1)}, u32[]{:S(2)}, u32[]{:S(2)}) collective-permute-start(bf16[1,64,2048]{2,1,0:T(8,128)(2,1)S(1)} %get-tuple-element.16), channel_id=1, source_target_pairs={{0,7},{1,6},{2,5},{3,4},{4,3},{5,2},{6,1},{7,0},{8,15},{9,14},{10,... | collective-permute-start | bytes 786440 | tf_op jit(solution)/shard_map/ppermute | solution.py:23
  99.3 2.1 %collective-permute-start.24 = (bf16[1,64,2048]{2,1,0:T(8,128)(2,1)S(1)}, bf16[1,64,2048]{2,1,0:T(8,128)(2,1)S(1)}, u32[]{:S(2)}, u32[]{:S(2)}) collective-permute-start(bf16[1,64,2048]{2,1,0:T(8,128)(2,1)S(1)} %get-tuple-element.20), channel_id=1, source_target_pairs={{0,3},{1,2},{2,1},{3,0},{4,7},{5,6},{6,5},{7,4},{8,11},{9,10},{10,... | collective-permute-start | bytes 786440 | tf_op jit(solution)/shard_map/ppermute | solution.py:23
  101.5 6.7 %collective-permute-done.22 = bf16[1,64,2048]{2,1,0:T(8,128)(2,1)S(1)} collective-permute-done((bf16[1,64,2048]{2,1,0:T(8,128)(2,1)S(1)}, bf16[1,64,2048]{2,1,0:T(8,128)(2,1)S(1)}, u32[]{:S(2)}, u32[]{:S(2)}) %collective-permute-start.22) | collective-permute-done | bytes 262176 | tf_op jit(solution)/shard_map/ppermute | solution.py:23
  108.2 2.5 %collective-permute-start.25 = (bf16[1,64,2048]{2,1,0:T(8,128)(2,1)S(1)}, bf16[1,64,2048]{2,1,0:T(8,128)(2,1)S(1)}, u32[]{:S(2)}, u32[]{:S(2)}) collective-permute-start(bf16[1,64,2048]{2,1,0:T(8,128)(2,1)S(1)} %get-tuple-element.21), channel_id=1, source_target_pairs={{0,6},{1,7},{2,4},{3,5},{4,2},{5,3},{6,0},{7,1},{8,14},{9,15},{10,... | collective-permute-start | bytes 786440 | tf_op jit(solution)/shard_map/ppermute | solution.py:23
  111.0 2.7 %collective-permute-done.13 = bf16[8,1,64,2048]{3,2,1,0:T(8,128)(2,1)} collective-permute-done((bf16[8,1,64,2048]{3,2,1,0:T(8,128)(2,1)}, bf16[8,1,64,2048]{3,2,1,0:T(8,128)(2,1)}, u32[]{:S(2)}, u32[]{:S(2)}) %collective-permute-start.13) | collective-permute-done | bytes 2097184 | tf_op jit(solution)/shard_map/ppermute | solution.py:23
  113.6 3.4 %collective-permute-start.26 = (bf16[1,64,2048]{2,1,0:T(8,128)(2,1)S(1)}, bf16[1,64,2048]{2,1,0:T(8,128)(2,1)S(1)}, u32[]{:S(2)}, u32[]{:S(2)}) collective-permute-start(bf16[1,64,2048]{2,1,0:T(8,128)(2,1)S(1)} %get-tuple-element.22), channel_id=1, source_target_pairs={{0,5},{1,4},{2,7},{3,6},{4,1},{5,0},{6,3},{7,2},{8,13},{9,12},{10,... | collective-permute-start | bytes 786440 | tf_op jit(solution)/shard_map/ppermute | solution.py:23
  117.0 3.6 %add_convert_fusion = bf16[8,1,64,2048]{3,2,1,0:T(8,128)(2,1)S(1)} fusion(bf16[8,1,64,2048]{3,2,1,0:T(8,128)(2,1)} %collective-permute-done.13, bf16[8,1,64,2048]{3,2,1,0:T(8,128)(2,1)} %add_convert_fusion.1, f32[]{:T(128)S(6)} %sub.112, f32[]{:T(128)} %bitcast), kind=kLoop, calls=%fused_computation | loop fusion | flops 6291456 | bytes 6291464 | tf_op jit(solution)/shard_map/convert_element_type | solution.py:203
  120.7 0.6 collective-permute-start.27
  121.7 2.3 %collective-permute-done.24 = bf16[1,64,2048]{2,1,0:T(8,128)(2,1)S(1)} collective-permute-done((bf16[1,64,2048]{2,1,0:T(8,128)(2,1)S(1)}, bf16[1,64,2048]{2,1,0:T(8,128)(2,1)S(1)}, u32[]{:S(2)}, u32[]{:S(2)}) %collective-permute-start.24) | collective-permute-done | bytes 262176 | tf_op jit(solution)/shard_map/ppermute | solution.py:23
  124.3 15.1 %collective-permute-done.26 = bf16[1,64,2048]{2,1,0:T(8,128)(2,1)S(1)} collective-permute-done((bf16[1,64,2048]{2,1,0:T(8,128)(2,1)S(1)}, bf16[1,64,2048]{2,1,0:T(8,128)(2,1)S(1)}, u32[]{:S(2)}, u32[]{:S(2)}) %collective-permute-start.26) | collective-permute-done | bytes 262176 | tf_op jit(solution)/shard_map/ppermute | solution.py:23
  139.4 3.2 %collective-permute-done.27 = bf16[1,64,2048]{2,1,0:T(8,128)(2,1)S(1)} collective-permute-done((bf16[1,64,2048]{2,1,0:T(8,128)(2,1)S(1)}, bf16[1,64,2048]{2,1,0:T(8,128)(2,1)S(1)}, u32[]{:S(2)}, u32[]{:S(2)}) %collective-permute-start.27) | collective-permute-done | bytes 262176 | tf_op jit(solution)/shard_map/ppermute | solution.py:23
  142.9 1.3 copy-done.4
  144.2 0.7 copy-done.5
  (54 shorter events, 3.3 us)
Async XLA Ops:
  0.6 8.9 %copy-start.7 = (s32[4,2]{0,1:T(2,128)S(1)}, s32[4,2]{0,1:T(2,128)}, u32[]{:S(2)}) copy-start(s32[4,2]{0,1:T(2,128)} %param.9) | copy-start | bytes 100
  0.7 11.8 %copy-start.2 = (bf16[1,8,64,2048]{3,2,1,0:T(8,128)(2,1)S(1)}, bf16[1,8,64,2048]{3,2,1,0:T(8,128)(2,1)}, u32[]{:S(2)}) copy-start(bf16[1,8,64,2048]{3,2,1,0:T(8,128)(2,1)} %param.8) | copy-start | bytes 6291460
  2.8 9.3 %collective-permute-start.4 = (bf16[1,1,64,2048]{3,2,1,0:T(8,128)(2,1)}, bf16[1,1,64,2048]{3,2,1,0:T(8,128)(2,1)}, u32[]{:S(2)}, u32[]{:S(2)}) collective-permute-start(bf16[1,1,64,2048]{3,2,1,0:T(8,128)(2,1)} %get-tuple-element.39), channel_id=1, source_target_pairs={{0,8},{8,0},{16,24},{24,16},{1,9},{9,1},{17,25},{25,17},{2,10},{10... | collective-permute-start | bytes 786440 | tf_op jit(solution)/shard_map/ppermute | solution.py:23
  3.2 12.4 %collective-permute-start.5 = (bf16[1,1,64,2048]{3,2,1,0:T(8,128)(2,1)}, bf16[1,1,64,2048]{3,2,1,0:T(8,128)(2,1)}, u32[]{:S(2)}, u32[]{:S(2)}) collective-permute-start(bf16[1,1,64,2048]{3,2,1,0:T(8,128)(2,1)} %get-tuple-element.39), channel_id=1, source_target_pairs={{0,16},{8,24},{16,0},{24,8},{1,17},{9,25},{17,1},{25,9},{2,18},{10... | collective-permute-start | bytes 786440 | tf_op jit(solution)/shard_map/ppermute | solution.py:23
  5.7 6.7 %collective-permute-start.8 = (bf16[1,1,64,2048]{3,2,1,0:T(8,128)(2,1)S(1)}, bf16[1,1,64,2048]{3,2,1,0:T(8,128)(2,1)}, u32[]{:S(2)}, u32[]{:S(2)}) collective-permute-start(bf16[1,1,64,2048]{3,2,1,0:T(8,128)(2,1)S(1)} %get-tuple-element.38), channel_id=1, source_target_pairs={{0,8},{8,0},{16,24},{24,16},{1,9},{9,1},{17,25},{25,17},{2,10},{10... | collective-permute-start | bytes 786440 | tf_op jit(solution)/shard_map/ppermute | solution.py:23
  9.0 11.6 %collective-permute-start.17 = (bf16[2,1,64,2048]{3,2,0,1:T(8,128)(2,1)}, bf16[2,1,64,2048]{3,2,0,1:T(8,128)(2,1)S(1)}, u32[]{:S(2)}, u32[]{:S(2)}) collective-permute-start(bf16[2,1,64,2048]{3,2,0,1:T(8,128)(2,1)} %get-tuple-element.35), channel_id=1, source_target_pairs={{0,8},{8,0},{16,24},{24,16},{1,9},{9,1},{17,25},{25,17},{2,10},{10... | collective-permute-start | bytes 1572872 | tf_op jit(solution)/shard_map/ppermute | solution.py:23
  9.3 11.8 %collective-permute-start.2 = (bf16[2,1,64,2048]{3,2,1,0:T(8,128)(2,1)}, bf16[2,1,64,2048]{3,2,1,0:T(8,128)(2,1)S(1)}, u32[]{:S(2)}, u32[]{:S(2)}) collective-permute-start(bf16[2,1,64,2048]{3,2,1,0:T(8,128)(2,1)} %get-tuple-element.34), channel_id=1, source_target_pairs={{0,8},{8,0},{16,24},{24,16},{1,9},{9,1},{17,25},{25,17},{2,10},{10... | collective-permute-start | bytes 1572872 | tf_op jit(solution)/shard_map/ppermute | solution.py:23
  12.0 3.7 %copy-start.6 = (bf16[1,8,64,2048]{3,2,1,0:T(8,128)(2,1)S(1)}, bf16[1,8,64,2048]{3,2,1,0:T(8,128)(2,1)}, u32[]{:S(2)}) copy-start(bf16[1,8,64,2048]{3,2,1,0:T(8,128)(2,1)} %param.5) | copy-start | bytes 6291460
  12.1 8.6 %collective-permute-start.9 = (bf16[1,1,64,2048]{3,2,1,0:T(8,128)(2,1)S(1)}, bf16[1,1,64,2048]{3,2,1,0:T(8,128)(2,1)S(1)}, u32[]{:S(2)}, u32[]{:S(2)}) collective-permute-start(bf16[1,1,64,2048]{3,2,1,0:T(8,128)(2,1)S(1)} %get-tuple-element.38), channel_id=1, source_target_pairs={{0,16},{8,24},{16,0},{24,8},{1,17},{9,25},{17,1},{25,9},{2,18},{10... | collective-permute-start | bytes 786440 | tf_op jit(solution)/shard_map/ppermute | solution.py:23
  12.4 20.1 %collective-permute-start.1 = (bf16[2,1,64,2048]{3,2,0,1:T(8,128)(2,1)}, bf16[2,1,64,2048]{3,2,0,1:T(8,128)(2,1)S(1)}, u32[]{:S(2)}, u32[]{:S(2)}) collective-permute-start(bf16[2,1,64,2048]{3,2,0,1:T(8,128)(2,1)} %get-tuple-element.33), channel_id=1, source_target_pairs={{0,8},{8,0},{16,24},{24,16},{1,9},{9,1},{17,25},{25,17},{2,10},{10... | collective-permute-start | bytes 1572872 | tf_op jit(solution)/shard_map/ppermute | solution.py:23
  15.7 40.9 %collective-permute-start = (bf16[8,1,64,2048]{3,2,1,0:T(8,128)(2,1)S(1)}, bf16[8,1,64,2048]{3,2,1,0:T(8,128)(2,1)S(1)}, u32[]{:S(2)}, u32[]{:S(2)}) collective-permute-start(bf16[8,1,64,2048]{3,2,1,0:T(8,128)(2,1)S(1)} %bitcast.175), channel_id=1, source_target_pairs={{0,8},{8,0},{16,24},{24,16},{1,9},{9,1},{17,25},{25,17},{2,10},{10... | collective-permute-start | bytes 6291464 | tf_op jit(solution)/shard_map/ppermute | solution.py:23
  20.6 3.4 %collective-permute-start.6 = (bf16[1,1,64,2048]{3,2,1,0:T(8,128)(2,1)}, bf16[1,1,64,2048]{3,2,1,0:T(8,128)(2,1)S(1)}, u32[]{:S(2)}, u32[]{:S(2)}) collective-permute-start(bf16[1,1,64,2048]{3,2,1,0:T(8,128)(2,1)} %collective-permute-done.5), channel_id=1, source_target_pairs={{0,8},{8,0},{16,24},{24,16},{1,9},{9,1},{17,25},{25,17},{2,10},{10... | collective-permute-start | bytes 786440 | tf_op jit(solution)/shard_map/ppermute | solution.py:23
  20.6 5.9 %collective-permute-start.10 = (bf16[1,1,64,2048]{3,2,1,0:T(8,128)(2,1)S(1)}, bf16[1,1,64,2048]{3,2,1,0:T(8,128)(2,1)S(1)}, u32[]{:S(2)}, u32[]{:S(2)}) collective-permute-start(bf16[1,1,64,2048]{3,2,1,0:T(8,128)(2,1)S(1)} %collective-permute-done.9), channel_id=1, source_target_pairs={{0,8},{8,0},{16,24},{24,16},{1,9},{9,1},{17,25},{25,17},{2,10},{10... | collective-permute-start | bytes 786440 | tf_op jit(solution)/shard_map/ppermute | solution.py:23
  23.7 14.9 %collective-permute-start.18 = (bf16[2,1,64,2048]{3,2,1,0:T(8,128)(2,1)S(1)}, bf16[2,1,64,2048]{3,2,1,0:T(8,128)(2,1)S(1)}, u32[]{:S(2)}, u32[]{:S(2)}) collective-permute-start(bf16[2,1,64,2048]{3,2,1,0:T(8,128)(2,1)S(1)} %get-tuple-element.37), channel_id=1, source_target_pairs={{0,16},{8,24},{16,0},{24,8},{1,17},{9,25},{17,1},{25,9},{2,18},{10... | collective-permute-start | bytes 1572872 | tf_op jit(solution)/shard_map/ppermute | solution.py:23
  24.0 10.0 %copy-start = (f32[1,8,64,2048]{3,2,1,0:T(8,128)S(1)}, f32[1,8,64,2048]{3,2,1,0:T(8,128)}, u32[]{:S(2)}) copy-start(f32[1,8,64,2048]{3,2,1,0:T(8,128)} %param.6) | copy-start | bytes 12582916
  26.5 12.0 %copy-start.3 = (bf16[1,8,64,2048]{3,2,1,0:T(8,128)(2,1)S(1)}, bf16[1,8,64,2048]{3,2,1,0:T(8,128)(2,1)}, u32[]{:S(2)}) copy-start(bf16[1,8,64,2048]{3,2,1,0:T(8,128)(2,1)} %param.7) | copy-start | bytes 6291460
  27.4 26.2 %collective-permute-start.11 = (bf16[1,64,2048]{2,1,0:T(8,128)(2,1)S(1)}, bf16[1,64,2048]{2,1,0:T(8,128)(2,1)S(1)}, u32[]{:S(2)}, u32[]{:S(2)}) collective-permute-start(bf16[1,64,2048]{2,1,0:T(8,128)(2,1)S(1)} %get-tuple-element.46), channel_id=1, source_target_pairs={{0,6},{1,7},{2,4},{3,5},{4,2},{5,3},{6,0},{7,1},{8,14},{9,15},{10,... | collective-permute-start | bytes 786440 | tf_op jit(solution)/shard_map/ppermute | solution.py:23
  31.3 24.9 %collective-permute-start.7 = (bf16[1,64,2048]{2,1,0:T(8,128)(2,1)S(1)}, bf16[1,64,2048]{2,1,0:T(8,128)(2,1)S(1)}, u32[]{:S(2)}, u32[]{:S(2)}) collective-permute-start(bf16[1,64,2048]{2,1,0:T(8,128)(2,1)S(1)} %get-tuple-element.48), channel_id=1, source_target_pairs={{0,7},{1,6},{2,5},{3,4},{4,3},{5,2},{6,1},{7,0},{8,15},{9,14},{10,... | collective-permute-start | bytes 786440 | tf_op jit(solution)/shard_map/ppermute | solution.py:23
  32.5 16.3 %collective-permute-start.3 = (bf16[2,1,64,2048]{3,2,1,0:T(8,128)(2,1)S(1)}, bf16[2,1,64,2048]{3,2,1,0:T(8,128)(2,1)S(1)}, u32[]{:S(2)}, u32[]{:S(2)}) collective-permute-start(bf16[2,1,64,2048]{3,2,1,0:T(8,128)(2,1)S(1)} %get-tuple-element.36), channel_id=1, source_target_pairs={{0,16},{8,24},{16,0},{24,8},{1,17},{9,25},{17,1},{25,9},{2,18},{10... | collective-permute-start | bytes 1572872 | tf_op jit(solution)/shard_map/ppermute | solution.py:23
  50.5 21.1 %collective-permute-start.15 = (bf16[1,64,2048]{2,1,0:T(8,128)(2,1)S(1)}, bf16[1,64,2048]{2,1,0:T(8,128)(2,1)S(1)}, u32[]{:S(2)}, u32[]{:S(2)}) collective-permute-start(bf16[1,64,2048]{2,1,0:T(8,128)(2,1)S(1)} %get-tuple-element.43), channel_id=1, source_target_pairs={{0,2},{1,3},{2,0},{3,1},{4,6},{5,7},{6,4},{7,5},{8,10},{9,11},{10,... | collective-permute-start | bytes 786440 | tf_op jit(solution)/shard_map/ppermute | solution.py:23
  52.2 23.4 %collective-permute-start.16 = (bf16[1,64,2048]{2,1,0:T(8,128)(2,1)S(1)}, bf16[1,64,2048]{2,1,0:T(8,128)(2,1)S(1)}, u32[]{:S(2)}, u32[]{:S(2)}) collective-permute-start(bf16[1,64,2048]{2,1,0:T(8,128)(2,1)S(1)} %get-tuple-element.42), channel_id=1, source_target_pairs={{0,3},{1,2},{2,1},{3,0},{4,7},{5,6},{6,5},{7,4},{8,11},{9,10},{10,... | collective-permute-start | bytes 786440 | tf_op jit(solution)/shard_map/ppermute | solution.py:23
  53.6 21.9 %collective-permute-start.19 = (bf16[1,64,2048]{2,1,0:T(8,128)(2,1)S(1)}, bf16[1,64,2048]{2,1,0:T(8,128)(2,1)S(1)}, u32[]{:S(2)}, u32[]{:S(2)}) collective-permute-start(bf16[1,64,2048]{2,1,0:T(8,128)(2,1)S(1)} %get-tuple-element.41), channel_id=1, source_target_pairs={{0,4},{1,5},{2,6},{3,7},{4,0},{5,1},{6,2},{7,3},{8,12},{9,13},{10,... | collective-permute-start | bytes 786440 | tf_op jit(solution)/shard_map/ppermute | solution.py:23
  56.3 22.1 %collective-permute-start.20 = (bf16[1,64,2048]{2,1,0:T(8,128)(2,1)S(1)}, bf16[1,64,2048]{2,1,0:T(8,128)(2,1)S(1)}, u32[]{:S(2)}, u32[]{:S(2)}) collective-permute-start(bf16[1,64,2048]{2,1,0:T(8,128)(2,1)S(1)} %get-tuple-element.40), channel_id=1, source_target_pairs={{0,5},{1,4},{2,7},{3,6},{4,1},{5,0},{6,3},{7,2},{8,13},{9,12},{10,... | collective-permute-start | bytes 786440 | tf_op jit(solution)/shard_map/ppermute | solution.py:23
  56.6 11.9 %collective-permute-start.12 = (bf16[2,1,64,2048]{3,2,0,1:T(8,128)(2,1)S(1)}, bf16[2,1,64,2048]{3,2,0,1:T(8,128)(2,1)S(1)}, u32[]{:S(2)}, u32[]{:S(2)}) collective-permute-start(bf16[2,1,64,2048]{3,2,0,1:T(8,128)(2,1)S(1)} %fusion.3), channel_id=1, source_target_pairs={{0,16},{8,24},{16,0},{24,8},{1,17},{9,25},{17,1},{25,9},{2,18},{10... | collective-permute-start | bytes 1572872 | tf_op jit(solution)/shard_map/ppermute | solution.py:23
  68.5 45.2 %collective-permute-start.13 = (bf16[8,1,64,2048]{3,2,1,0:T(8,128)(2,1)}, bf16[8,1,64,2048]{3,2,1,0:T(8,128)(2,1)}, u32[]{:S(2)}, u32[]{:S(2)}) collective-permute-start(bf16[8,1,64,2048]{3,2,1,0:T(8,128)(2,1)} %add_convert_fusion.1), channel_id=1, source_target_pairs={{0,16},{8,24},{16,0},{24,8},{1,17},{9,25},{17,1},{25,9},{2,18},{10... | collective-permute-start | bytes 6291464 | tf_op jit(solution)/shard_map/ppermute | solution.py:23
  71.6 9.8 %copy-start.1 = (f32[1,8,64,2048]{3,2,1,0:T(8,128)}, f32[1,8,64,2048]{3,2,1,0:T(8,128)S(1)}, u32[]{:S(2)}) copy-start(f32[1,8,64,2048]{3,2,1,0:T(8,128)S(1)} %get-tuple-element.25) | copy-start | bytes 12582916
  71.6 9.7 %collective-permute-start.14 = (bf16[1,64,2048]{2,1,0:T(8,128)(2,1)S(1)}, bf16[1,64,2048]{2,1,0:T(8,128)(2,1)S(1)}, u32[]{:S(2)}, u32[]{:S(2)}) collective-permute-start(bf16[1,64,2048]{2,1,0:T(8,128)(2,1)S(1)} %get-tuple-element.44), channel_id=1, source_target_pairs={{0,1},{1,0},{2,3},{3,2},{4,5},{5,4},{6,7},{7,6},{8,9},{9,8},{10,11... | collective-permute-start | bytes 786440 | tf_op jit(solution)/shard_map/ppermute | solution.py:23
  94.2 14.0 %collective-permute-start.22 = (bf16[1,64,2048]{2,1,0:T(8,128)(2,1)S(1)}, bf16[1,64,2048]{2,1,0:T(8,128)(2,1)S(1)}, u32[]{:S(2)}, u32[]{:S(2)}) collective-permute-start(bf16[1,64,2048]{2,1,0:T(8,128)(2,1)S(1)} %get-tuple-element.18), channel_id=1, source_target_pairs={{0,1},{1,0},{2,3},{3,2},{4,5},{5,4},{6,7},{7,6},{8,9},{9,8},{10,11... | collective-permute-start | bytes 786440 | tf_op jit(solution)/shard_map/ppermute | solution.py:23
  94.7 25.9 %collective-permute-start.21 = (bf16[1,64,2048]{2,1,0:T(8,128)(2,1)S(1)}, bf16[1,64,2048]{2,1,0:T(8,128)(2,1)S(1)}, u32[]{:S(2)}, u32[]{:S(2)}) collective-permute-start(bf16[1,64,2048]{2,1,0:T(8,128)(2,1)S(1)} %get-tuple-element.16), channel_id=1, source_target_pairs={{0,7},{1,6},{2,5},{3,4},{4,3},{5,2},{6,1},{7,0},{8,15},{9,14},{10,... | collective-permute-start | bytes 786440 | tf_op jit(solution)/shard_map/ppermute | solution.py:23
  99.3 22.3 %collective-permute-start.23 = (bf16[1,64,2048]{2,1,0:T(8,128)(2,1)S(1)}, bf16[1,64,2048]{2,1,0:T(8,128)(2,1)S(1)}, u32[]{:S(2)}, u32[]{:S(2)}) collective-permute-start(bf16[1,64,2048]{2,1,0:T(8,128)(2,1)S(1)} %get-tuple-element.19), channel_id=1, source_target_pairs={{0,2},{1,3},{2,0},{3,1},{4,6},{5,7},{6,4},{7,5},{8,10},{9,11},{10,... | collective-permute-start | bytes 786440 | tf_op jit(solution)/shard_map/ppermute | solution.py:23
  99.3 24.7 %collective-permute-start.24 = (bf16[1,64,2048]{2,1,0:T(8,128)(2,1)S(1)}, bf16[1,64,2048]{2,1,0:T(8,128)(2,1)S(1)}, u32[]{:S(2)}, u32[]{:S(2)}) collective-permute-start(bf16[1,64,2048]{2,1,0:T(8,128)(2,1)S(1)} %get-tuple-element.20), channel_id=1, source_target_pairs={{0,3},{1,2},{2,1},{3,0},{4,7},{5,6},{6,5},{7,4},{8,11},{9,10},{10,... | collective-permute-start | bytes 786440 | tf_op jit(solution)/shard_map/ppermute | solution.py:23
  108.2 16.0 %collective-permute-start.25 = (bf16[1,64,2048]{2,1,0:T(8,128)(2,1)S(1)}, bf16[1,64,2048]{2,1,0:T(8,128)(2,1)S(1)}, u32[]{:S(2)}, u32[]{:S(2)}) collective-permute-start(bf16[1,64,2048]{2,1,0:T(8,128)(2,1)S(1)} %get-tuple-element.21), channel_id=1, source_target_pairs={{0,6},{1,7},{2,4},{3,5},{4,2},{5,3},{6,0},{7,1},{8,14},{9,15},{10,... | collective-permute-start | bytes 786440 | tf_op jit(solution)/shard_map/ppermute | solution.py:23
  113.6 25.7 %collective-permute-start.26 = (bf16[1,64,2048]{2,1,0:T(8,128)(2,1)S(1)}, bf16[1,64,2048]{2,1,0:T(8,128)(2,1)S(1)}, u32[]{:S(2)}, u32[]{:S(2)}) collective-permute-start(bf16[1,64,2048]{2,1,0:T(8,128)(2,1)S(1)} %get-tuple-element.22), channel_id=1, source_target_pairs={{0,5},{1,4},{2,7},{3,6},{4,1},{5,0},{6,3},{7,2},{8,13},{9,12},{10,... | collective-permute-start | bytes 786440 | tf_op jit(solution)/shard_map/ppermute | solution.py:23
  120.7 22.0 %collective-permute-start.27 = (bf16[1,64,2048]{2,1,0:T(8,128)(2,1)S(1)}, bf16[1,64,2048]{2,1,0:T(8,128)(2,1)S(1)}, u32[]{:S(2)}, u32[]{:S(2)}) collective-permute-start(bf16[1,64,2048]{2,1,0:T(8,128)(2,1)S(1)} %get-tuple-element.23), channel_id=1, source_target_pairs={{0,4},{1,5},{2,6},{3,7},{4,0},{5,1},{6,2},{7,3},{8,12},{9,13},{10,... | collective-permute-start | bytes 786440 | tf_op jit(solution)/shard_map/ppermute | solution.py:23
  142.8 1.3 copy-start.4
  142.9 2.0 %copy-start.5 = (bf16[1,8,64,2048]{3,2,1,0:T(8,128)(2,1)}, bf16[1,8,64,2048]{3,2,1,0:T(8,128)(2,1)S(1)}, u32[]{:S(2)}) copy-start(bf16[1,8,64,2048]{3,2,1,0:T(8,128)(2,1)S(1)} %get-tuple-element.50) | copy-start | bytes 6291460

commit v16 on v15

--- a/solution.py
+++ b/solution.py
@@ -207,7 +207,7 @@
     update = jnp.zeros(shape, BF16)
     new_weight = jnp.zeros(shape, BF16)
     half = shards // 2
-    order = list(range(1, half)) + list(reversed(range(half, shards))) + [0]
+    order = [1, shards - 1, shards - 2, *range(2, half), *reversed(range(half, shards - 2)), 0]
     received = [
         swapped(block, "shard", offset) if offset else block for offset, block in enumerate(updates)
     ]

time: 145 us -> 145 us (level)
  starting transfers between devices: 35.6 us -> 31.1 us
  waiting for transfers between devices: 63.1 us -> 67.3 us
    ppermute x28, starting transfers between devices: 35.6 us -> 31.1 us  [swapped(): lax.ppermute(values, axis, [(i, i ^ offset) for i in range(lax.axis_size(...]
    ppermute x28, waiting for transfers between devices: 63.1 us -> 67.3 us  [swapped(): lax.ppermute(values, axis, [(i, i ^ offset) for i in range(lax.axis_size(...]
where the time goes in v16:
time: 145 us
  waiting for transfers between devices  67.3 us (46%)
  starting transfers between devices  31.1 us (21%)
  other arithmetic  21.6 us (15%)
  Pallas kernels  12.8 us (9%)
  local copies, waits for them, and re-layouts  9 us (6%)
  between operations  2.81 us (2%)
    ppermute x28, waiting for transfers between devices, swapped(): lax.ppermute(values, axis, [(i, i ^ offset) for i in range(lax.axis_size(...  67.3 us
    ppermute x28, starting transfers between devices, swapped(): lax.ppermute(values, axis, [(i, i ^ offset) for i in range(lax.axis_size(...  31.1 us
    pallas_call x1, Pallas kernels, orthogonalize(): pl.pallas_call(body, grid=(each,), in_specs=[block] * count, out_specs=[b...  12.8 us
    convert_element_type x2, local copies, waits for them, and re-layouts, local(): rounded = own.astype(BF16)  5.18 us
    dynamic_update_slice x3, other arithmetic, local(): lax.dynamic_update_slice_in_dim(new_tracker, group, start, axis=0)  4.98 us
    convert_element_type x1, other arithmetic, local(): mixed_weight = (second * weight_own.astype(F32) + (1.0 - second) * weight...  3.64 us
    convert_element_type x2, other arithmetic, local(): sent = mixed.astype(BF16)  3.29 us
    add x1, other arithmetic, local(): second * mixed  3.17 us
  transfers between devices with their start and end apart: 28, of which 12 were waited for; matrix products, arithmetic and copies ran while one was open for 18% of the time, Pallas kernels for 9%

profile of v16, /device:TPU:0, one launch (start us, length us, event | category | flops | bytes accessed | tf_op | source)
XLA Modules:
  0.0 144.6 jit_solution(3735283057306477940)
XLA Ops:
  0.7 2.1 %dynamic-slice_convert_fusion.9 = (bf16[1,1,64,2048]{3,2,1,0:T(8,128)(2,1)S(1)}, bf16[1,1,64,2048]{3,2,1,0:T(8,128)(2,1)}) fusion(f32[1,8,64,2048]{3,2,1,0:T(8,128)} %param.6, s32[]{:T(128)S(6)} %select_n.143, s32[]{:T(128)S(6)} %select_n.141), kind=kLoop, calls=%fused_computation.53 | loop fusion | bytes 1048584 | tf_op jit(solution)/shard_map/convert_element_type | solution.py:165
  2.8 0.5 collective-permute-start.4
  3.2 2.5 %collective-permute-start.5 = (bf16[1,1,64,2048]{3,2,1,0:T(8,128)(2,1)}, bf16[1,1,64,2048]{3,2,1,0:T(8,128)(2,1)}, u32[]{:S(2)}, u32[]{:S(2)}) collective-permute-start(bf16[1,1,64,2048]{3,2,1,0:T(8,128)(2,1)} %get-tuple-element.39), channel_id=1, source_target_pairs={{0,16},{8,24},{16,0},{24,8},{1,17},{9,25},{17,1},{25,9},{2,18},{10... | collective-permute-start | bytes 786440 | tf_op jit(solution)/shard_map/ppermute | solution.py:23
  6.0 3.1 %fusion.6 = (bf16[2,1,64,2048]{3,2,0,1:T(8,128)(2,1)}, bf16[2,1,64,2048]{3,2,1,0:T(8,128)(2,1)}, bf16[2,1,64,2048]{3,2,0,1:T(8,128)(2,1)}) fusion(f32[1,8,64,2048]{3,2,1,0:T(8,128)} %param.6, s32[]{:T(128)S(6)} %select_n.138, s32[]{:T(128)S(6)} %select_n.140, s32[]{:T(128)S(6)} %select_n.153), kind=kLoop, calls=%fused_computation.24 | loop fusion | bytes 3145740 | tf_op jit(solution)/shard_map/convert_element_type | solution.py:165
  9.5 0.7 constant_dynamic-slice_fusion
  12.1 0.3 collective-permute-start.9
  12.5 3.2 %subtract_add_fusion = (f32[1,1,64,2048]{3,2,1,0:T(8,128)S(1)}, f32[1,1,64,2048]{3,2,1,0:T(8,128)S(1)}) fusion(bf16[1,1,64,2048]{3,2,1,0:T(8,128)(2,1)} %collective-permute-done.8, f32[1,8,64,2048]{3,2,1,0:T(8,128)} %param.6, s32[]{:T(128)S(6)} %select_n.143, bf16[1,8,64,2048]{3,2,1,0:T(8,128)(2,1)S(1)} %copy-done.2, bf16[1,8,64,2048]{3,2,1,0:T(8,128)(2,1)} %param.7, ...), kind=kLoop, calls=%fused_computation.50 | loop fusion | flops 2359296 | bytes 3670036 | tf_op jit(solution)/shard_map/add | solution.py:179
  15.7 0.4 collective-permute-start
  16.1 4.6 %collective-permute-done.9 = bf16[1,1,64,2048]{3,2,1,0:T(8,128)(2,1)S(1)} collective-permute-done((bf16[1,1,64,2048]{3,2,1,0:T(8,128)(2,1)S(1)}, bf16[1,1,64,2048]{3,2,1,0:T(8,128)(2,1)S(1)}, u32[]{:S(2)}, u32[]{:S(2)}) %collective-permute-start.9) | collective-permute-done | bytes 262176 | tf_op jit(solution)/shard_map/ppermute | solution.py:23
  20.6 0.5 collective-permute-start.10
  21.1 2.5 %fusion.4 = (bf16[2,1,64,2048]{3,2,1,0:T(8,128)(2,1)S(1)}, bf16[2,1,64,2048]{3,2,1,0:T(8,128)(2,1)S(1)}) fusion(bf16[2,1,64,2048]{3,2,1,0:T(8,128)(2,1)S(1)} %collective-permute-done.2, f32[1,8,64,2048]{3,2,1,0:T(8,128)} %param.6, s32[]{:T(128)S(6)} %select_n.140, f32[]{:T(128)S(6)} %sub.108, f32[]{:T(128)} %bitcast.1, ...), kind=kLoop, calls=%fused_computation.22 | loop fusion | flops 2621440 | bytes 4194320 | tf_op jit(solution)/shard_map/convert_element_type | solution.py:171
  23.7 0.4 collective-permute-start.18
  24.0 0.5 reshape.500
  24.5 2.0 %convert_bitcast_fusion.1 = (bf16[1,64,2048]{2,1,0:T(8,128)(2,1)S(1)}, f32[1,8,64,2048]{3,2,1,0:T(8,128)S(1)}) fusion(f32[1,1,64,2048]{3,2,1,0:T(8,128)S(1)} %get-tuple-element.32, bf16[1,1,64,2048]{3,2,1,0:T(8,128)(2,1)S(1)} %collective-permute-done.6, f32[]{:T(128)S(6)} %sub.113, bf16[1,1,64,2048]{3,2,1,0:T(8,128)(2,1)} %collective-permute-done.5, ...), kind=kLoop, calls=%fused_computation.86 | loop fusion | flops 1048576 | bytes 1835024 | tf_op jit(solution)/shard_map/convert_element_type | solution.py:188
  26.5 0.9 convert_bitcast_fusion
  27.4 3.9 %collective-permute-start.11 = (bf16[1,64,2048]{2,1,0:T(8,128)(2,1)S(1)}, bf16[1,64,2048]{2,1,0:T(8,128)(2,1)S(1)}, u32[]{:S(2)}, u32[]{:S(2)}) collective-permute-start(bf16[1,64,2048]{2,1,0:T(8,128)(2,1)S(1)} %get-tuple-element.46), channel_id=1, source_target_pairs={{0,6},{1,7},{2,4},{3,5},{4,2},{5,3},{6,0},{7,1},{8,14},{9,15},{10,... | collective-permute-start | bytes 786440 | tf_op jit(solution)/shard_map/ppermute | solution.py:23
  31.3 1.2 collective-permute-start.7
  32.5 1.5 %collective-permute-start.3 = (bf16[2,1,64,2048]{3,2,1,0:T(8,128)(2,1)S(1)}, bf16[2,1,64,2048]{3,2,1,0:T(8,128)(2,1)S(1)}, u32[]{:S(2)}, u32[]{:S(2)}) collective-permute-start(bf16[2,1,64,2048]{3,2,1,0:T(8,128)(2,1)S(1)} %get-tuple-element.36), channel_id=1, source_target_pairs={{0,16},{8,24},{16,0},{24,8},{1,17},{9,25},{17,1},{25,9},{2,18},{10... | collective-permute-start | bytes 1572872 | tf_op jit(solution)/shard_map/ppermute | solution.py:23
  34.0 0.8 fusion.3
  34.8 3.7 %collective-permute-done.18 = bf16[2,1,64,2048]{3,2,1,0:T(8,128)(2,1)S(1)} collective-permute-done((bf16[2,1,64,2048]{3,2,1,0:T(8,128)(2,1)S(1)}, bf16[2,1,64,2048]{3,2,1,0:T(8,128)(2,1)S(1)}, u32[]{:S(2)}, u32[]{:S(2)}) %collective-permute-start.18) | collective-permute-done | bytes 524320 | tf_op jit(solution)/shard_map/ppermute | solution.py:23
  38.5 1.7 %bitcast_dynamic-update-slice_fusion.2 = (f32[1,8,64,2048]{3,2,1,0:T(8,128)S(1)}, bf16[2,1,64,2048]{3,2,1,0:T(8,128)(2,1)S(1)}) fusion(f32[1,8,64,2048]{3,2,1,0:T(8,128)S(1)} %get-tuple-element.47, s32[]{:T(128)S(6)} %select_n.153, bf16[2,1,64,2048]{3,2,1,0:T(8,128)(2,1)S(1)} %collective-permute-done.18, f32[]{:T(128)S(6)} %sub.112, ...), kind=kLoop, calls=%fused_computation.10 | loop fusion | flops 3407872 | bytes 4718612 | tf_op jit(solution)/shard_map/dynamic_update_slice | solution.py:194
  40.2 8.6 %collective-permute-done.3 = bf16[2,1,64,2048]{3,2,1,0:T(8,128)(2,1)S(1)} collective-permute-done((bf16[2,1,64,2048]{3,2,1,0:T(8,128)(2,1)S(1)}, bf16[2,1,64,2048]{3,2,1,0:T(8,128)(2,1)S(1)}, u32[]{:S(2)}, u32[]{:S(2)}) %collective-permute-start.3) | collective-permute-done | bytes 524320 | tf_op jit(solution)/shard_map/ppermute | solution.py:23
  48.8 1.7 %bitcast_dynamic-update-slice_fusion.1 = (f32[1,8,64,2048]{3,2,1,0:T(8,128)S(1)}, bf16[2,1,64,2048]{3,2,1,0:T(8,128)(2,1)S(1)}) fusion(f32[1,8,64,2048]{3,2,1,0:T(8,128)S(1)} %get-tuple-element.29, s32[]{:T(128)S(6)} %select_n.140, bf16[2,1,64,2048]{3,2,1,0:T(8,128)(2,1)S(1)} %collective-permute-done.3, f32[]{:T(128)S(6)} %sub.112, ...), kind=kLoop, calls=%fused_computation.9 | loop fusion | flops 3407872 | bytes 4718612 | tf_op jit(solution)/shard_map/dynamic_update_slice | solution.py:194
  50.5 1.6 %collective-permute-start.15 = (bf16[1,64,2048]{2,1,0:T(8,128)(2,1)S(1)}, bf16[1,64,2048]{2,1,0:T(8,128)(2,1)S(1)}, u32[]{:S(2)}, u32[]{:S(2)}) collective-permute-start(bf16[1,64,2048]{2,1,0:T(8,128)(2,1)S(1)} %get-tuple-element.43), channel_id=1, source_target_pairs={{0,2},{1,3},{2,0},{3,1},{4,6},{5,7},{6,4},{7,5},{8,10},{9,11},{10,... | collective-permute-start | bytes 786440 | tf_op jit(solution)/shard_map/ppermute | solution.py:23
  52.2 1.4 collective-permute-start.16
  53.6 2.7 %collective-permute-start.19 = (bf16[1,64,2048]{2,1,0:T(8,128)(2,1)S(1)}, bf16[1,64,2048]{2,1,0:T(8,128)(2,1)S(1)}, u32[]{:S(2)}, u32[]{:S(2)}) collective-permute-start(bf16[1,64,2048]{2,1,0:T(8,128)(2,1)S(1)} %get-tuple-element.41), channel_id=1, source_target_pairs={{0,4},{1,5},{2,6},{3,7},{4,0},{5,1},{6,2},{7,3},{8,12},{9,13},{10,... | collective-permute-start | bytes 786440 | tf_op jit(solution)/shard_map/ppermute | solution.py:23
  56.6 1.0 collective-permute-start.12
  57.5 2.8 %add_convert_fusion.1 = bf16[8,1,64,2048]{3,2,1,0:T(8,128)(2,1)} fusion(bf16[8,1,64,2048]{3,2,1,0:T(8,128)(2,1)S(1)} %collective-permute-done, f32[]{:T(128)S(6)} %sub.108, f32[]{:T(128)} %bitcast.1, bf16[1,8,64,2048]{3,2,1,0:T(8,128)(2,1)S(1)} %copy-done.6), kind=kLoop, calls=%fused_computation.1 | loop fusion | flops 6291456 | bytes 6291464 | tf_op jit(solution)/shard_map/convert_element_type | solution.py:198
  60.3 8.1 %collective-permute-done.12 = bf16[2,1,64,2048]{3,2,0,1:T(8,128)(2,1)S(1)} collective-permute-done((bf16[2,1,64,2048]{3,2,0,1:T(8,128)(2,1)S(1)}, bf16[2,1,64,2048]{3,2,0,1:T(8,128)(2,1)S(1)}, u32[]{:S(2)}, u32[]{:S(2)}) %collective-permute-start.12) | collective-permute-done | bytes 524320 | tf_op jit(solution)/shard_map/ppermute | solution.py:23
  68.5 1.4 collective-permute-start.13
  69.9 1.7 %bitcast_dynamic-update-slice_fusion = (f32[1,8,64,2048]{3,2,1,0:T(8,128)S(1)}, bf16[2,1,64,2048]{3,2,0,1:T(8,128)(2,1)S(1)}) fusion(f32[1,8,64,2048]{3,2,1,0:T(8,128)S(1)} %get-tuple-element.27, s32[]{:T(128)S(6)} %select_n.138, bf16[2,1,64,2048]{3,2,0,1:T(8,128)(2,1)S(1)} %collective-permute-done.12, f32[]{:T(128)S(6)} %sub.112, ...), kind=kLoop, calls=%fused_computation.8 | loop fusion | flops 3407872 | bytes 4718612 | tf_op jit(solution)/shard_map/dynamic_update_slice | solution.py:194
  71.6 1.6 %collective-permute-start.14 = (bf16[1,64,2048]{2,1,0:T(8,128)(2,1)S(1)}, bf16[1,64,2048]{2,1,0:T(8,128)(2,1)S(1)}, u32[]{:S(2)}, u32[]{:S(2)}) collective-permute-start(bf16[1,64,2048]{2,1,0:T(8,128)(2,1)S(1)} %get-tuple-element.44), channel_id=1, source_target_pairs={{0,1},{1,0},{2,3},{3,2},{4,5},{5,4},{6,7},{7,6},{8,9},{9,8},{10,11... | collective-permute-start | bytes 786440 | tf_op jit(solution)/shard_map/ppermute | solution.py:23
  73.2 2.3 %collective-permute-done.16.refs_3_ = bf16[1,64,2048]{2,1,0:T(8,128)(2,1)S(1)} collective-permute-done((bf16[1,64,2048]{2,1,0:T(8,128)(2,1)S(1)}, bf16[1,64,2048]{2,1,0:T(8,128)(2,1)S(1)}, u32[]{:S(2)}, u32[]{:S(2)}) %collective-permute-start.16) | collective-permute-done | bytes 262176 | tf_op jit(solution)/shard_map/ppermute | solution.py:23
  75.6 2.8 %collective-permute-done.20.refs_5_ = bf16[1,64,2048]{2,1,0:T(8,128)(2,1)S(1)} collective-permute-done((bf16[1,64,2048]{2,1,0:T(8,128)(2,1)S(1)}, bf16[1,64,2048]{2,1,0:T(8,128)(2,1)S(1)}, u32[]{:S(2)}, u32[]{:S(2)}) %collective-permute-start.20) | collective-permute-done | bytes 262176 | tf_op jit(solution)/shard_map/ppermute | solution.py:23
  78.3 3.0 %collective-permute-done.14.refs_1_ = bf16[1,64,2048]{2,1,0:T(8,128)(2,1)S(1)} collective-permute-done((bf16[1,64,2048]{2,1,0:T(8,128)(2,1)S(1)}, bf16[1,64,2048]{2,1,0:T(8,128)(2,1)S(1)}, u32[]{:S(2)}, u32[]{:S(2)}) %collective-permute-start.14) | collective-permute-done | bytes 262176 | tf_op jit(solution)/shard_map/ppermute | solution.py:23
  81.4 12.8 %orthogonalize.1 = (bf16[1,64,2048]{2,1,0:T(8,128)(2,1)S(1)}, bf16[1,64,2048]{2,1,0:T(8,128)(2,1)S(1)}, bf16[1,64,2048]{2,1,0:T(8,128)(2,1)S(1)}, bf16[1,64,2048...) custom-call(bf16[1,64,2048]{2,1,0:T(8,128)(2,1)S(1)} %get-tuple-elem, ...), custom_call_target="tpu_custom_call" | custom-call | flops 11005853696 | bytes 4194304 | tf_op jit(solution)/shard_map/orthogonalize/pallas_call | solution.py:102
  94.2 0.6 collective-permute-start.22
  94.7 4.6 %collective-permute-start.21 = (bf16[1,64,2048]{2,1,0:T(8,128)(2,1)S(1)}, bf16[1,64,2048]{2,1,0:T(8,128)(2,1)S(1)}, u32[]{:S(2)}, u32[]{:S(2)}) collective-permute-start(bf16[1,64,2048]{2,1,0:T(8,128)(2,1)S(1)} %get-tuple-element.16), channel_id=1, source_target_pairs={{0,7},{1,6},{2,5},{3,4},{4,3},{5,2},{6,1},{7,0},{8,15},{9,14},{10,... | collective-permute-start | bytes 786440 | tf_op jit(solution)/shard_map/ppermute | solution.py:23
  99.5 8.7 %collective-permute-done.22 = bf16[1,64,2048]{2,1,0:T(8,128)(2,1)S(1)} collective-permute-done((bf16[1,64,2048]{2,1,0:T(8,128)(2,1)S(1)}, bf16[1,64,2048]{2,1,0:T(8,128)(2,1)S(1)}, u32[]{:S(2)}, u32[]{:S(2)}) %collective-permute-start.22) | collective-permute-done | bytes 262176 | tf_op jit(solution)/shard_map/ppermute | solution.py:23
  108.5 5.2 %collective-permute-done.13 = bf16[8,1,64,2048]{3,2,1,0:T(8,128)(2,1)} collective-permute-done((bf16[8,1,64,2048]{3,2,1,0:T(8,128)(2,1)}, bf16[8,1,64,2048]{3,2,1,0:T(8,128)(2,1)}, u32[]{:S(2)}, u32[]{:S(2)}) %collective-permute-start.13) | collective-permute-done | bytes 2097184 | tf_op jit(solution)/shard_map/ppermute | solution.py:23
  113.6 3.4 %collective-permute-start.26 = (bf16[1,64,2048]{2,1,0:T(8,128)(2,1)S(1)}, bf16[1,64,2048]{2,1,0:T(8,128)(2,1)S(1)}, u32[]{:S(2)}, u32[]{:S(2)}) collective-permute-start(bf16[1,64,2048]{2,1,0:T(8,128)(2,1)S(1)} %get-tuple-element.22), channel_id=1, source_target_pairs={{0,5},{1,4},{2,7},{3,6},{4,1},{5,0},{6,3},{7,2},{8,13},{9,12},{10,... | collective-permute-start | bytes 786440 | tf_op jit(solution)/shard_map/ppermute | solution.py:23
  117.0 3.6 %add_convert_fusion = bf16[8,1,64,2048]{3,2,1,0:T(8,128)(2,1)S(1)} fusion(bf16[8,1,64,2048]{3,2,1,0:T(8,128)(2,1)} %collective-permute-done.13, bf16[8,1,64,2048]{3,2,1,0:T(8,128)(2,1)} %add_convert_fusion.1, f32[]{:T(128)S(6)} %sub.112, f32[]{:T(128)} %bitcast), kind=kLoop, calls=%fused_computation | loop fusion | flops 6291456 | bytes 6291464 | tf_op jit(solution)/shard_map/convert_element_type | solution.py:203
  120.7 0.6 collective-permute-start.27
  121.9 2.0 %collective-permute-done.25 = bf16[1,64,2048]{2,1,0:T(8,128)(2,1)S(1)} collective-permute-done((bf16[1,64,2048]{2,1,0:T(8,128)(2,1)S(1)}, bf16[1,64,2048]{2,1,0:T(8,128)(2,1)S(1)}, u32[]{:S(2)}, u32[]{:S(2)}) %collective-permute-start.25) | collective-permute-done | bytes 262176 | tf_op jit(solution)/shard_map/ppermute | solution.py:23
  124.1 15.2 %collective-permute-done.26 = bf16[1,64,2048]{2,1,0:T(8,128)(2,1)S(1)} collective-permute-done((bf16[1,64,2048]{2,1,0:T(8,128)(2,1)S(1)}, bf16[1,64,2048]{2,1,0:T(8,128)(2,1)S(1)}, u32[]{:S(2)}, u32[]{:S(2)}) %collective-permute-start.26) | collective-permute-done | bytes 262176 | tf_op jit(solution)/shard_map/ppermute | solution.py:23
  139.3 3.0 %collective-permute-done.27 = bf16[1,64,2048]{2,1,0:T(8,128)(2,1)S(1)} collective-permute-done((bf16[1,64,2048]{2,1,0:T(8,128)(2,1)S(1)}, bf16[1,64,2048]{2,1,0:T(8,128)(2,1)S(1)}, u32[]{:S(2)}, u32[]{:S(2)}) %collective-permute-start.27) | collective-permute-done | bytes 262176 | tf_op jit(solution)/shard_map/ppermute | solution.py:23
  142.6 1.3 copy-done.4
  143.9 0.7 copy-done.5
  (54 shorter events, 2.8 us)
Async XLA Ops:
  0.6 8.9 %copy-start.7 = (s32[4,2]{0,1:T(2,128)S(1)}, s32[4,2]{0,1:T(2,128)}, u32[]{:S(2)}) copy-start(s32[4,2]{0,1:T(2,128)} %param.9) | copy-start | bytes 100
  0.7 11.8 %copy-start.2 = (bf16[1,8,64,2048]{3,2,1,0:T(8,128)(2,1)S(1)}, bf16[1,8,64,2048]{3,2,1,0:T(8,128)(2,1)}, u32[]{:S(2)}) copy-start(bf16[1,8,64,2048]{3,2,1,0:T(8,128)(2,1)} %param.8) | copy-start | bytes 6291460
  2.8 9.3 %collective-permute-start.4 = (bf16[1,1,64,2048]{3,2,1,0:T(8,128)(2,1)}, bf16[1,1,64,2048]{3,2,1,0:T(8,128)(2,1)}, u32[]{:S(2)}, u32[]{:S(2)}) collective-permute-start(bf16[1,1,64,2048]{3,2,1,0:T(8,128)(2,1)} %get-tuple-element.39), channel_id=1, source_target_pairs={{0,8},{8,0},{16,24},{24,16},{1,9},{9,1},{17,25},{25,17},{2,10},{10... | collective-permute-start | bytes 786440 | tf_op jit(solution)/shard_map/ppermute | solution.py:23
  3.2 12.4 %collective-permute-start.5 = (bf16[1,1,64,2048]{3,2,1,0:T(8,128)(2,1)}, bf16[1,1,64,2048]{3,2,1,0:T(8,128)(2,1)}, u32[]{:S(2)}, u32[]{:S(2)}) collective-permute-start(bf16[1,1,64,2048]{3,2,1,0:T(8,128)(2,1)} %get-tuple-element.39), channel_id=1, source_target_pairs={{0,16},{8,24},{16,0},{24,8},{1,17},{9,25},{17,1},{25,9},{2,18},{10... | collective-permute-start | bytes 786440 | tf_op jit(solution)/shard_map/ppermute | solution.py:23
  5.7 6.7 %collective-permute-start.8 = (bf16[1,1,64,2048]{3,2,1,0:T(8,128)(2,1)S(1)}, bf16[1,1,64,2048]{3,2,1,0:T(8,128)(2,1)}, u32[]{:S(2)}, u32[]{:S(2)}) collective-permute-start(bf16[1,1,64,2048]{3,2,1,0:T(8,128)(2,1)S(1)} %get-tuple-element.38), channel_id=1, source_target_pairs={{0,8},{8,0},{16,24},{24,16},{1,9},{9,1},{17,25},{25,17},{2,10},{10... | collective-permute-start | bytes 786440 | tf_op jit(solution)/shard_map/ppermute | solution.py:23
  9.0 11.6 %collective-permute-start.17 = (bf16[2,1,64,2048]{3,2,0,1:T(8,128)(2,1)}, bf16[2,1,64,2048]{3,2,0,1:T(8,128)(2,1)S(1)}, u32[]{:S(2)}, u32[]{:S(2)}) collective-permute-start(bf16[2,1,64,2048]{3,2,0,1:T(8,128)(2,1)} %get-tuple-element.35), channel_id=1, source_target_pairs={{0,8},{8,0},{16,24},{24,16},{1,9},{9,1},{17,25},{25,17},{2,10},{10... | collective-permute-start | bytes 1572872 | tf_op jit(solution)/shard_map/ppermute | solution.py:23
  9.3 11.8 %collective-permute-start.2 = (bf16[2,1,64,2048]{3,2,1,0:T(8,128)(2,1)}, bf16[2,1,64,2048]{3,2,1,0:T(8,128)(2,1)S(1)}, u32[]{:S(2)}, u32[]{:S(2)}) collective-permute-start(bf16[2,1,64,2048]{3,2,1,0:T(8,128)(2,1)} %get-tuple-element.34), channel_id=1, source_target_pairs={{0,8},{8,0},{16,24},{24,16},{1,9},{9,1},{17,25},{25,17},{2,10},{10... | collective-permute-start | bytes 1572872 | tf_op jit(solution)/shard_map/ppermute | solution.py:23
  12.0 3.7 %copy-start.6 = (bf16[1,8,64,2048]{3,2,1,0:T(8,128)(2,1)S(1)}, bf16[1,8,64,2048]{3,2,1,0:T(8,128)(2,1)}, u32[]{:S(2)}) copy-start(bf16[1,8,64,2048]{3,2,1,0:T(8,128)(2,1)} %param.5) | copy-start | bytes 6291460
  12.1 8.6 %collective-permute-start.9 = (bf16[1,1,64,2048]{3,2,1,0:T(8,128)(2,1)S(1)}, bf16[1,1,64,2048]{3,2,1,0:T(8,128)(2,1)S(1)}, u32[]{:S(2)}, u32[]{:S(2)}) collective-permute-start(bf16[1,1,64,2048]{3,2,1,0:T(8,128)(2,1)S(1)} %get-tuple-element.38), channel_id=1, source_target_pairs={{0,16},{8,24},{16,0},{24,8},{1,17},{9,25},{17,1},{25,9},{2,18},{10... | collective-permute-start | bytes 786440 | tf_op jit(solution)/shard_map/ppermute | solution.py:23
  12.4 20.1 %collective-permute-start.1 = (bf16[2,1,64,2048]{3,2,0,1:T(8,128)(2,1)}, bf16[2,1,64,2048]{3,2,0,1:T(8,128)(2,1)S(1)}, u32[]{:S(2)}, u32[]{:S(2)}) collective-permute-start(bf16[2,1,64,2048]{3,2,0,1:T(8,128)(2,1)} %get-tuple-element.33), channel_id=1, source_target_pairs={{0,8},{8,0},{16,24},{24,16},{1,9},{9,1},{17,25},{25,17},{2,10},{10... | collective-permute-start | bytes 1572872 | tf_op jit(solution)/shard_map/ppermute | solution.py:23
  15.7 40.9 %collective-permute-start = (bf16[8,1,64,2048]{3,2,1,0:T(8,128)(2,1)S(1)}, bf16[8,1,64,2048]{3,2,1,0:T(8,128)(2,1)S(1)}, u32[]{:S(2)}, u32[]{:S(2)}) collective-permute-start(bf16[8,1,64,2048]{3,2,1,0:T(8,128)(2,1)S(1)} %bitcast.175), channel_id=1, source_target_pairs={{0,8},{8,0},{16,24},{24,16},{1,9},{9,1},{17,25},{25,17},{2,10},{10... | collective-permute-start | bytes 6291464 | tf_op jit(solution)/shard_map/ppermute | solution.py:23
  20.6 3.4 %collective-permute-start.6 = (bf16[1,1,64,2048]{3,2,1,0:T(8,128)(2,1)}, bf16[1,1,64,2048]{3,2,1,0:T(8,128)(2,1)S(1)}, u32[]{:S(2)}, u32[]{:S(2)}) collective-permute-start(bf16[1,1,64,2048]{3,2,1,0:T(8,128)(2,1)} %collective-permute-done.5), channel_id=1, source_target_pairs={{0,8},{8,0},{16,24},{24,16},{1,9},{9,1},{17,25},{25,17},{2,10},{10... | collective-permute-start | bytes 786440 | tf_op jit(solution)/shard_map/ppermute | solution.py:23
  20.6 5.9 %collective-permute-start.10 = (bf16[1,1,64,2048]{3,2,1,0:T(8,128)(2,1)S(1)}, bf16[1,1,64,2048]{3,2,1,0:T(8,128)(2,1)S(1)}, u32[]{:S(2)}, u32[]{:S(2)}) collective-permute-start(bf16[1,1,64,2048]{3,2,1,0:T(8,128)(2,1)S(1)} %collective-permute-done.9), channel_id=1, source_target_pairs={{0,8},{8,0},{16,24},{24,16},{1,9},{9,1},{17,25},{25,17},{2,10},{10... | collective-permute-start | bytes 786440 | tf_op jit(solution)/shard_map/ppermute | solution.py:23
  23.7 14.9 %collective-permute-start.18 = (bf16[2,1,64,2048]{3,2,1,0:T(8,128)(2,1)S(1)}, bf16[2,1,64,2048]{3,2,1,0:T(8,128)(2,1)S(1)}, u32[]{:S(2)}, u32[]{:S(2)}) collective-permute-start(bf16[2,1,64,2048]{3,2,1,0:T(8,128)(2,1)S(1)} %get-tuple-element.37), channel_id=1, source_target_pairs={{0,16},{8,24},{16,0},{24,8},{1,17},{9,25},{17,1},{25,9},{2,18},{10... | collective-permute-start | bytes 1572872 | tf_op jit(solution)/shard_map/ppermute | solution.py:23
  24.0 10.0 %copy-start = (f32[1,8,64,2048]{3,2,1,0:T(8,128)S(1)}, f32[1,8,64,2048]{3,2,1,0:T(8,128)}, u32[]{:S(2)}) copy-start(f32[1,8,64,2048]{3,2,1,0:T(8,128)} %param.6) | copy-start | bytes 12582916
  26.5 12.0 %copy-start.3 = (bf16[1,8,64,2048]{3,2,1,0:T(8,128)(2,1)S(1)}, bf16[1,8,64,2048]{3,2,1,0:T(8,128)(2,1)}, u32[]{:S(2)}) copy-start(bf16[1,8,64,2048]{3,2,1,0:T(8,128)(2,1)} %param.7) | copy-start | bytes 6291460
  27.4 26.2 %collective-permute-start.11 = (bf16[1,64,2048]{2,1,0:T(8,128)(2,1)S(1)}, bf16[1,64,2048]{2,1,0:T(8,128)(2,1)S(1)}, u32[]{:S(2)}, u32[]{:S(2)}) collective-permute-start(bf16[1,64,2048]{2,1,0:T(8,128)(2,1)S(1)} %get-tuple-element.46), channel_id=1, source_target_pairs={{0,6},{1,7},{2,4},{3,5},{4,2},{5,3},{6,0},{7,1},{8,14},{9,15},{10,... | collective-permute-start | bytes 786440 | tf_op jit(solution)/shard_map/ppermute | solution.py:23
  31.3 24.9 %collective-permute-start.7 = (bf16[1,64,2048]{2,1,0:T(8,128)(2,1)S(1)}, bf16[1,64,2048]{2,1,0:T(8,128)(2,1)S(1)}, u32[]{:S(2)}, u32[]{:S(2)}) collective-permute-start(bf16[1,64,2048]{2,1,0:T(8,128)(2,1)S(1)} %get-tuple-element.48), channel_id=1, source_target_pairs={{0,7},{1,6},{2,5},{3,4},{4,3},{5,2},{6,1},{7,0},{8,15},{9,14},{10,... | collective-permute-start | bytes 786440 | tf_op jit(solution)/shard_map/ppermute | solution.py:23
  32.5 16.3 %collective-permute-start.3 = (bf16[2,1,64,2048]{3,2,1,0:T(8,128)(2,1)S(1)}, bf16[2,1,64,2048]{3,2,1,0:T(8,128)(2,1)S(1)}, u32[]{:S(2)}, u32[]{:S(2)}) collective-permute-start(bf16[2,1,64,2048]{3,2,1,0:T(8,128)(2,1)S(1)} %get-tuple-element.36), channel_id=1, source_target_pairs={{0,16},{8,24},{16,0},{24,8},{1,17},{9,25},{17,1},{25,9},{2,18},{10... | collective-permute-start | bytes 1572872 | tf_op jit(solution)/shard_map/ppermute | solution.py:23
  50.5 21.1 %collective-permute-start.15 = (bf16[1,64,2048]{2,1,0:T(8,128)(2,1)S(1)}, bf16[1,64,2048]{2,1,0:T(8,128)(2,1)S(1)}, u32[]{:S(2)}, u32[]{:S(2)}) collective-permute-start(bf16[1,64,2048]{2,1,0:T(8,128)(2,1)S(1)} %get-tuple-element.43), channel_id=1, source_target_pairs={{0,2},{1,3},{2,0},{3,1},{4,6},{5,7},{6,4},{7,5},{8,10},{9,11},{10,... | collective-permute-start | bytes 786440 | tf_op jit(solution)/shard_map/ppermute | solution.py:23
  52.2 23.4 %collective-permute-start.16 = (bf16[1,64,2048]{2,1,0:T(8,128)(2,1)S(1)}, bf16[1,64,2048]{2,1,0:T(8,128)(2,1)S(1)}, u32[]{:S(2)}, u32[]{:S(2)}) collective-permute-start(bf16[1,64,2048]{2,1,0:T(8,128)(2,1)S(1)} %get-tuple-element.42), channel_id=1, source_target_pairs={{0,3},{1,2},{2,1},{3,0},{4,7},{5,6},{6,5},{7,4},{8,11},{9,10},{10,... | collective-permute-start | bytes 786440 | tf_op jit(solution)/shard_map/ppermute | solution.py:23
  53.6 21.9 %collective-permute-start.19 = (bf16[1,64,2048]{2,1,0:T(8,128)(2,1)S(1)}, bf16[1,64,2048]{2,1,0:T(8,128)(2,1)S(1)}, u32[]{:S(2)}, u32[]{:S(2)}) collective-permute-start(bf16[1,64,2048]{2,1,0:T(8,128)(2,1)S(1)} %get-tuple-element.41), channel_id=1, source_target_pairs={{0,4},{1,5},{2,6},{3,7},{4,0},{5,1},{6,2},{7,3},{8,12},{9,13},{10,... | collective-permute-start | bytes 786440 | tf_op jit(solution)/shard_map/ppermute | solution.py:23
  56.3 22.1 %collective-permute-start.20 = (bf16[1,64,2048]{2,1,0:T(8,128)(2,1)S(1)}, bf16[1,64,2048]{2,1,0:T(8,128)(2,1)S(1)}, u32[]{:S(2)}, u32[]{:S(2)}) collective-permute-start(bf16[1,64,2048]{2,1,0:T(8,128)(2,1)S(1)} %get-tuple-element.40), channel_id=1, source_target_pairs={{0,5},{1,4},{2,7},{3,6},{4,1},{5,0},{6,3},{7,2},{8,13},{9,12},{10,... | collective-permute-start | bytes 786440 | tf_op jit(solution)/shard_map/ppermute | solution.py:23
  56.6 11.9 %collective-permute-start.12 = (bf16[2,1,64,2048]{3,2,0,1:T(8,128)(2,1)S(1)}, bf16[2,1,64,2048]{3,2,0,1:T(8,128)(2,1)S(1)}, u32[]{:S(2)}, u32[]{:S(2)}) collective-permute-start(bf16[2,1,64,2048]{3,2,0,1:T(8,128)(2,1)S(1)} %fusion.3), channel_id=1, source_target_pairs={{0,16},{8,24},{16,0},{24,8},{1,17},{9,25},{17,1},{25,9},{2,18},{10... | collective-permute-start | bytes 1572872 | tf_op jit(solution)/shard_map/ppermute | solution.py:23
  68.5 45.2 %collective-permute-start.13 = (bf16[8,1,64,2048]{3,2,1,0:T(8,128)(2,1)}, bf16[8,1,64,2048]{3,2,1,0:T(8,128)(2,1)}, u32[]{:S(2)}, u32[]{:S(2)}) collective-permute-start(bf16[8,1,64,2048]{3,2,1,0:T(8,128)(2,1)} %add_convert_fusion.1), channel_id=1, source_target_pairs={{0,16},{8,24},{16,0},{24,8},{1,17},{9,25},{17,1},{25,9},{2,18},{10... | collective-permute-start | bytes 6291464 | tf_op jit(solution)/shard_map/ppermute | solution.py:23
  71.6 9.8 %copy-start.1 = (f32[1,8,64,2048]{3,2,1,0:T(8,128)}, f32[1,8,64,2048]{3,2,1,0:T(8,128)S(1)}, u32[]{:S(2)}) copy-start(f32[1,8,64,2048]{3,2,1,0:T(8,128)S(1)} %get-tuple-element.25) | copy-start | bytes 12582916
  71.6 9.7 %collective-permute-start.14 = (bf16[1,64,2048]{2,1,0:T(8,128)(2,1)S(1)}, bf16[1,64,2048]{2,1,0:T(8,128)(2,1)S(1)}, u32[]{:S(2)}, u32[]{:S(2)}) collective-permute-start(bf16[1,64,2048]{2,1,0:T(8,128)(2,1)S(1)} %get-tuple-element.44), channel_id=1, source_target_pairs={{0,1},{1,0},{2,3},{3,2},{4,5},{5,4},{6,7},{7,6},{8,9},{9,8},{10,11... | collective-permute-start | bytes 786440 | tf_op jit(solution)/shard_map/ppermute | solution.py:23
  94.2 14.0 %collective-permute-start.22 = (bf16[1,64,2048]{2,1,0:T(8,128)(2,1)S(1)}, bf16[1,64,2048]{2,1,0:T(8,128)(2,1)S(1)}, u32[]{:S(2)}, u32[]{:S(2)}) collective-permute-start(bf16[1,64,2048]{2,1,0:T(8,128)(2,1)S(1)} %get-tuple-element.18), channel_id=1, source_target_pairs={{0,1},{1,0},{2,3},{3,2},{4,5},{5,4},{6,7},{7,6},{8,9},{9,8},{10,11... | collective-permute-start | bytes 786440 | tf_op jit(solution)/shard_map/ppermute | solution.py:23
  94.7 25.9 %collective-permute-start.21 = (bf16[1,64,2048]{2,1,0:T(8,128)(2,1)S(1)}, bf16[1,64,2048]{2,1,0:T(8,128)(2,1)S(1)}, u32[]{:S(2)}, u32[]{:S(2)}) collective-permute-start(bf16[1,64,2048]{2,1,0:T(8,128)(2,1)S(1)} %get-tuple-element.16), channel_id=1, source_target_pairs={{0,7},{1,6},{2,5},{3,4},{4,3},{5,2},{6,1},{7,0},{8,15},{9,14},{10,... | collective-permute-start | bytes 786440 | tf_op jit(solution)/shard_map/ppermute | solution.py:23
  99.3 22.4 %collective-permute-start.23 = (bf16[1,64,2048]{2,1,0:T(8,128)(2,1)S(1)}, bf16[1,64,2048]{2,1,0:T(8,128)(2,1)S(1)}, u32[]{:S(2)}, u32[]{:S(2)}) collective-permute-start(bf16[1,64,2048]{2,1,0:T(8,128)(2,1)S(1)} %get-tuple-element.19), channel_id=1, source_target_pairs={{0,6},{1,7},{2,4},{3,5},{4,2},{5,3},{6,0},{7,1},{8,14},{9,15},{10,... | collective-permute-start | bytes 786440 | tf_op jit(solution)/shard_map/ppermute | solution.py:23
  99.5 22.3 %collective-permute-start.24 = (bf16[1,64,2048]{2,1,0:T(8,128)(2,1)S(1)}, bf16[1,64,2048]{2,1,0:T(8,128)(2,1)S(1)}, u32[]{:S(2)}, u32[]{:S(2)}) collective-permute-start(bf16[1,64,2048]{2,1,0:T(8,128)(2,1)S(1)} %get-tuple-element.20), channel_id=1, source_target_pairs={{0,2},{1,3},{2,0},{3,1},{4,6},{5,7},{6,4},{7,5},{8,10},{9,11},{10,... | collective-permute-start | bytes 786440 | tf_op jit(solution)/shard_map/ppermute | solution.py:23
  108.2 15.8 %collective-permute-start.25 = (bf16[1,64,2048]{2,1,0:T(8,128)(2,1)S(1)}, bf16[1,64,2048]{2,1,0:T(8,128)(2,1)S(1)}, u32[]{:S(2)}, u32[]{:S(2)}) collective-permute-start(bf16[1,64,2048]{2,1,0:T(8,128)(2,1)S(1)} %get-tuple-element.21), channel_id=1, source_target_pairs={{0,3},{1,2},{2,1},{3,0},{4,7},{5,6},{6,5},{7,4},{8,11},{9,10},{10,... | collective-permute-start | bytes 786440 | tf_op jit(solution)/shard_map/ppermute | solution.py:23
  113.6 25.6 %collective-permute-start.26 = (bf16[1,64,2048]{2,1,0:T(8,128)(2,1)S(1)}, bf16[1,64,2048]{2,1,0:T(8,128)(2,1)S(1)}, u32[]{:S(2)}, u32[]{:S(2)}) collective-permute-start(bf16[1,64,2048]{2,1,0:T(8,128)(2,1)S(1)} %get-tuple-element.22), channel_id=1, source_target_pairs={{0,5},{1,4},{2,7},{3,6},{4,1},{5,0},{6,3},{7,2},{8,13},{9,12},{10,... | collective-permute-start | bytes 786440 | tf_op jit(solution)/shard_map/ppermute | solution.py:23
  120.7 21.7 %collective-permute-start.27 = (bf16[1,64,2048]{2,1,0:T(8,128)(2,1)S(1)}, bf16[1,64,2048]{2,1,0:T(8,128)(2,1)S(1)}, u32[]{:S(2)}, u32[]{:S(2)}) collective-permute-start(bf16[1,64,2048]{2,1,0:T(8,128)(2,1)S(1)} %get-tuple-element.23), channel_id=1, source_target_pairs={{0,4},{1,5},{2,6},{3,7},{4,0},{5,1},{6,2},{7,3},{8,12},{9,13},{10,... | collective-permute-start | bytes 786440 | tf_op jit(solution)/shard_map/ppermute | solution.py:23
  142.6 1.3 copy-start.4
  142.6 2.0 %copy-start.5 = (bf16[1,8,64,2048]{3,2,1,0:T(8,128)(2,1)}, bf16[1,8,64,2048]{3,2,1,0:T(8,128)(2,1)S(1)}, u32[]{:S(2)}) copy-start(bf16[1,8,64,2048]{3,2,1,0:T(8,128)(2,1)S(1)} %get-tuple-element.50) | copy-start | bytes 6291460

commit v17 on v16

--- a/solution.py
+++ b/solution.py
@@ -150,6 +150,9 @@
         return share * own + (1.0 - share) * near.astype(F32)
 
     weight_near = swapped(weight, "rep", 1)
+    weight_own = (
+        first * weight.astype(F32) + (1.0 - first) * weight_near.astype(F32)
+    ).astype(BF16)
     arrived = []
     mixes = []
     new_tracker = jnp.zeros(shape, F32)
@@ -172,8 +175,12 @@
             if turn == 2:
                 sent = after(sent)
             elif turn == 4:
-                sent = after(sent, arrived[2], blocks[7 * shards // 8], weight_near, blocks[6 * shards // 8])
+                sent = after(sent, arrived[2], weight_near)
             far = swapped(sent, "rep", 2)
+            if turn == 2:
+                far = after(far, weight_own)
+            if turn == 4:
+                far = after(far, blocks[7 * shards // 8], blocks[6 * shards // 8])
             far_mixed = far.astype(F32)
         arrived.append(far)
         base = second * mixed + (part_of(grad_new).astype(F32) - part_of(grad_old).astype(F32))
@@ -193,9 +200,6 @@
         group, start = mixes[turn]
         new_tracker = lax.dynamic_update_slice_in_dim(new_tracker, group, start, axis=0)
 
-    weight_own = (
-        first * weight.astype(F32) + (1.0 - first) * weight_near.astype(F32)
-    ).astype(BF16)
     weight_own = after(weight_own, far)
     weight_far = swapped(weight_own, "rep", 2)
     mixed_weight = (

time: 145 us -> 145 us (level)
  starting transfers between devices: 31.1 us -> 44.5 us
  waiting for transfers between devices: 67.3 us -> 53.9 us
    ppermute x28, waiting for transfers between devices: 67.3 us -> 53.9 us  [swapped(): lax.ppermute(values, axis, [(i, i ^ offset) for i in range(lax.axis_size(...]
    ppermute x28, starting transfers between devices: 31.1 us -> 44.5 us  [swapped(): lax.ppermute(values, axis, [(i, i ^ offset) for i in range(lax.axis_size(...]
  transfers between devices with their start and end apart: 28 -> 28, of which waited for: 12 -> 11; matrix products, arithmetic and copies ran while one was open for 18% -> 18% of each run, Pallas kernels for 9% -> 9%
where the time goes in v17:
time: 145 us
  waiting for transfers between devices  53.9 us (37%)
  starting transfers between devices  44.5 us (31%)
  other arithmetic  21.7 us (15%)
  Pallas kernels  12.8 us (9%)
  local copies, waits for them, and re-layouts  9.02 us (6%)
  between operations  2.86 us (2%)
    ppermute x28, waiting for transfers between devices, swapped(): lax.ppermute(values, axis, [(i, i ^ offset) for i in range(lax.axis_size(...  53.9 us
    ppermute x28, starting transfers between devices, swapped(): lax.ppermute(values, axis, [(i, i ^ offset) for i in range(lax.axis_size(...  44.5 us
    pallas_call x1, Pallas kernels, orthogonalize(): pl.pallas_call(body, grid=(each,), in_specs=[block] * count, out_specs=[b...  12.8 us
    dynamic_update_slice x3, other arithmetic, local(): lax.dynamic_update_slice_in_dim(new_tracker, group, start, axis=0)  5.34 us
    convert_element_type x2, local copies, waits for them, and re-layouts, local(): rounded = own.astype(BF16)  5.17 us
    convert_element_type x1, other arithmetic, local(): mixed_weight = (second * weight_own.astype(F32) + (1.0 - second) * weight...  3.77 us
    convert_element_type x2, other arithmetic, local(): sent = mixed.astype(BF16)  3.16 us
    add x1, other arithmetic, local(): second * mixed  3.07 us
  transfers between devices with their start and end apart: 28, of which 11 were waited for; matrix products, arithmetic and copies ran while one was open for 18% of the time, Pallas kernels for 9%

profile of v17, /device:TPU:0, one launch (start us, length us, event | category | flops | bytes accessed | tf_op | source)
XLA Modules:
  0.0 144.7 jit_solution(6335985432492992761)
XLA Ops:
  0.7 2.1 %dynamic-slice_convert_fusion.9 = (bf16[1,1,64,2048]{3,2,1,0:T(8,128)(2,1)S(1)}, bf16[1,1,64,2048]{3,2,1,0:T(8,128)(2,1)}) fusion(f32[1,8,64,2048]{3,2,1,0:T(8,128)} %param.6, s32[]{:T(128)S(6)} %select_n.143, s32[]{:T(128)S(6)} %select_n.141), kind=kLoop, calls=%fused_computation.53 | loop fusion | bytes 1048584 | tf_op jit(solution)/shard_map/convert_element_type | solution.py:168
  2.8 0.5 collective-permute-start.5
  3.2 2.5 %collective-permute-start.6 = (bf16[1,1,64,2048]{3,2,1,0:T(8,128)(2,1)}, bf16[1,1,64,2048]{3,2,1,0:T(8,128)(2,1)}, u32[]{:S(2)}, u32[]{:S(2)}) collective-permute-start(bf16[1,1,64,2048]{3,2,1,0:T(8,128)(2,1)} %get-tuple-element.43), channel_id=1, source_target_pairs={{0,16},{8,24},{16,0},{24,8},{1,17},{9,25},{17,1},{25,9},{2,18},{10... | collective-permute-start | bytes 786440 | tf_op jit(solution)/shard_map/ppermute | solution.py:23
  5.9 3.1 %fusion.6 = (bf16[2,1,64,2048]{3,2,0,1:T(8,128)(2,1)}, bf16[2,1,64,2048]{3,2,1,0:T(8,128)(2,1)}, bf16[2,1,64,2048]{3,2,0,1:T(8,128)(2,1)}) fusion(f32[1,8,64,2048]{3,2,1,0:T(8,128)} %param.6, s32[]{:T(128)S(6)} %select_n.138, s32[]{:T(128)S(6)} %select_n.140, s32[]{:T(128)S(6)} %select_n.153), kind=kLoop, calls=%fused_computation.24 | loop fusion | bytes 3145740 | tf_op jit(solution)/shard_map/convert_element_type | solution.py:168
  9.5 0.7 constant_dynamic-slice_fusion
  12.1 0.3 collective-permute-start.10
  12.6 3.1 %subtract_add_fusion = (f32[1,1,64,2048]{3,2,1,0:T(8,128)S(1)}, f32[1,1,64,2048]{3,2,1,0:T(8,128)S(1)}) fusion(bf16[1,1,64,2048]{3,2,1,0:T(8,128)(2,1)} %collective-permute-done.9, f32[1,8,64,2048]{3,2,1,0:T(8,128)} %param.6, s32[]{:T(128)S(6)} %select_n.143, bf16[1,8,64,2048]{3,2,1,0:T(8,128)(2,1)S(1)} %copy-done.2, bf16[1,8,64,2048]{3,2,1,0:T(8,128)(2,1)} %param.7, ...), kind=kLoop, calls=%fused_computation.50 | loop fusion | flops 2359296 | bytes 3670036 | tf_op jit(solution)/shard_map/add | solution.py:186
  15.7 0.5 collective-permute-start.1
  16.1 4.5 %collective-permute-done.10 = bf16[1,1,64,2048]{3,2,1,0:T(8,128)(2,1)S(1)} collective-permute-done((bf16[1,1,64,2048]{3,2,1,0:T(8,128)(2,1)S(1)}, bf16[1,1,64,2048]{3,2,1,0:T(8,128)(2,1)S(1)}, u32[]{:S(2)}, u32[]{:S(2)}) %collective-permute-start.10) | collective-permute-done | bytes 262176 | tf_op jit(solution)/shard_map/ppermute | solution.py:23
  20.7 0.5 collective-permute-start.11
  21.2 2.4 %fusion.4 = (bf16[2,1,64,2048]{3,2,1,0:T(8,128)(2,1)S(1)}, bf16[2,1,64,2048]{3,2,1,0:T(8,128)(2,1)S(1)}) fusion(bf16[2,1,64,2048]{3,2,1,0:T(8,128)(2,1)S(1)} %collective-permute-done.2, f32[1,8,64,2048]{3,2,1,0:T(8,128)} %param.6, s32[]{:T(128)S(6)} %select_n.140, f32[]{:T(128)S(6)} %sub.108, f32[]{:T(128)} %bitcast.1, ...), kind=kLoop, calls=%fused_computation.22 | loop fusion | flops 2621440 | bytes 4194320 | tf_op jit(solution)/shard_map/convert_element_type | solution.py:174
  23.6 0.4 collective-permute-start.18
  24.0 0.5 reshape.500
  24.5 2.0 %convert_bitcast_fusion.1 = (bf16[1,64,2048]{2,1,0:T(8,128)(2,1)S(1)}, f32[1,8,64,2048]{3,2,1,0:T(8,128)S(1)}) fusion(f32[1,1,64,2048]{3,2,1,0:T(8,128)S(1)} %get-tuple-element.36, bf16[1,1,64,2048]{3,2,1,0:T(8,128)(2,1)S(1)} %collective-permute-done.7, f32[]{:T(128)S(6)} %sub.113, bf16[1,1,64,2048]{3,2,1,0:T(8,128)(2,1)} %collective-permute-done.6, ...), kind=kLoop, calls=%fused_computation.86 | loop fusion | flops 1048576 | bytes 1835024 | tf_op jit(solution)/shard_map/convert_element_type | solution.py:195
  26.5 0.9 convert_bitcast_fusion
  27.4 3.9 %collective-permute-start.12 = (bf16[1,64,2048]{2,1,0:T(8,128)(2,1)S(1)}, bf16[1,64,2048]{2,1,0:T(8,128)(2,1)S(1)}, u32[]{:S(2)}, u32[]{:S(2)}) collective-permute-start(bf16[1,64,2048]{2,1,0:T(8,128)(2,1)S(1)} %get-tuple-element.50), channel_id=1, source_target_pairs={{0,6},{1,7},{2,4},{3,5},{4,2},{5,3},{6,0},{7,1},{8,14},{9,15},{10,... | collective-permute-start | bytes 786440 | tf_op jit(solution)/shard_map/ppermute | solution.py:23
  31.3 1.5 %collective-permute-start.3 = (bf16[2,1,64,2048]{3,2,1,0:T(8,128)(2,1)S(1)}, bf16[2,1,64,2048]{3,2,1,0:T(8,128)(2,1)S(1)}, u32[]{:S(2)}, u32[]{:S(2)}) collective-permute-start(bf16[2,1,64,2048]{3,2,1,0:T(8,128)(2,1)S(1)} %get-tuple-element.40), channel_id=1, source_target_pairs={{0,16},{8,24},{16,0},{24,8},{1,17},{9,25},{17,1},{25,9},{2,18},{10... | collective-permute-start | bytes 1572872 | tf_op jit(solution)/shard_map/ppermute | solution.py:23
  32.8 1.2 collective-permute-start.8
  34.0 0.7 fusion.3
  34.7 3.8 %collective-permute-done.18 = bf16[2,1,64,2048]{3,2,1,0:T(8,128)(2,1)S(1)} collective-permute-done((bf16[2,1,64,2048]{3,2,1,0:T(8,128)(2,1)S(1)}, bf16[2,1,64,2048]{3,2,1,0:T(8,128)(2,1)S(1)}, u32[]{:S(2)}, u32[]{:S(2)}) %collective-permute-start.18) | collective-permute-done | bytes 524320 | tf_op jit(solution)/shard_map/ppermute | solution.py:23
  38.5 1.9 %bitcast_dynamic-update-slice_fusion.2 = (f32[1,8,64,2048]{3,2,1,0:T(8,128)S(1)}, bf16[2,1,64,2048]{3,2,1,0:T(8,128)(2,1)S(1)}) fusion(f32[1,8,64,2048]{3,2,1,0:T(8,128)S(1)} %get-tuple-element.51, s32[]{:T(128)S(6)} %select_n.153, bf16[2,1,64,2048]{3,2,1,0:T(8,128)(2,1)S(1)} %collective-permute-done.18, f32[]{:T(128)S(6)} %sub.112, ...), kind=kLoop, calls=%fused_computation.10 | loop fusion | flops 3407872 | bytes 4718612 | tf_op jit(solution)/shard_map/dynamic_update_slice | solution.py:201
  40.4 2.7 %collective-permute-start.19 = (bf16[1,64,2048]{2,1,0:T(8,128)(2,1)S(1)}, bf16[1,64,2048]{2,1,0:T(8,128)(2,1)S(1)}, u32[]{:S(2)}, u32[]{:S(2)}) collective-permute-start(bf16[1,64,2048]{2,1,0:T(8,128)(2,1)S(1)} %get-tuple-element.45), channel_id=1, source_target_pairs={{0,4},{1,5},{2,6},{3,7},{4,0},{5,1},{6,2},{7,3},{8,12},{9,13},{10,... | collective-permute-start | bytes 786440 | tf_op jit(solution)/shard_map/ppermute | solution.py:23
  43.1 1.3 collective-permute-start.20
  44.4 2.8 %add_convert_fusion.1 = bf16[8,1,64,2048]{3,2,1,0:T(8,128)(2,1)} fusion(bf16[8,1,64,2048]{3,2,1,0:T(8,128)(2,1)S(1)} %collective-permute-done, f32[]{:T(128)S(6)} %sub.108, f32[]{:T(128)} %bitcast.1, bf16[1,8,64,2048]{3,2,1,0:T(8,128)(2,1)S(1)} %copy-done.6), kind=kLoop, calls=%fused_computation.1 | loop fusion | flops 6291456 | bytes 6291464 | tf_op jit(solution)/shard_map/convert_element_type | solution.py:155
  47.2 1.6 %collective-permute-done.3 = bf16[2,1,64,2048]{3,2,1,0:T(8,128)(2,1)S(1)} collective-permute-done((bf16[2,1,64,2048]{3,2,1,0:T(8,128)(2,1)S(1)}, bf16[2,1,64,2048]{3,2,1,0:T(8,128)(2,1)S(1)}, u32[]{:S(2)}, u32[]{:S(2)}) %collective-permute-start.3) | collective-permute-done | bytes 524320 | tf_op jit(solution)/shard_map/ppermute | solution.py:23
  49.1 1.7 %bitcast_dynamic-update-slice_fusion.1 = (f32[1,8,64,2048]{3,2,1,0:T(8,128)S(1)}, bf16[2,1,64,2048]{3,2,1,0:T(8,128)(2,1)S(1)}) fusion(f32[1,8,64,2048]{3,2,1,0:T(8,128)S(1)} %get-tuple-element.33, s32[]{:T(128)S(6)} %select_n.140, bf16[2,1,64,2048]{3,2,1,0:T(8,128)(2,1)S(1)} %collective-permute-done.3, f32[]{:T(128)S(6)} %sub.112, ...), kind=kLoop, calls=%fused_computation.9 | loop fusion | flops 3407872 | bytes 4718612 | tf_op jit(solution)/shard_map/dynamic_update_slice | solution.py:201
  50.9 9.8 %collective-permute-start.15 = (bf16[1,64,2048]{2,1,0:T(8,128)(2,1)S(1)}, bf16[1,64,2048]{2,1,0:T(8,128)(2,1)S(1)}, u32[]{:S(2)}, u32[]{:S(2)}) collective-permute-start(bf16[1,64,2048]{2,1,0:T(8,128)(2,1)S(1)} %get-tuple-element.47), channel_id=1, source_target_pairs={{0,2},{1,3},{2,0},{3,1},{4,6},{5,7},{6,4},{7,5},{8,10},{9,11},{10,... | collective-permute-start | bytes 786440 | tf_op jit(solution)/shard_map/ppermute | solution.py:23
  60.7 6.5 %collective-permute-start.16 = (bf16[1,64,2048]{2,1,0:T(8,128)(2,1)S(1)}, bf16[1,64,2048]{2,1,0:T(8,128)(2,1)S(1)}, u32[]{:S(2)}, u32[]{:S(2)}) collective-permute-start(bf16[1,64,2048]{2,1,0:T(8,128)(2,1)S(1)} %get-tuple-element.46), channel_id=1, source_target_pairs={{0,3},{1,2},{2,1},{3,0},{4,7},{5,6},{6,5},{7,4},{8,11},{9,10},{10,... | collective-permute-start | bytes 786440 | tf_op jit(solution)/shard_map/ppermute | solution.py:23
  67.2 1.5 %collective-permute-start.13 = (bf16[8,1,64,2048]{3,2,1,0:T(8,128)(2,1)}, bf16[8,1,64,2048]{3,2,1,0:T(8,128)(2,1)}, u32[]{:S(2)}, u32[]{:S(2)}) collective-permute-start(bf16[8,1,64,2048]{3,2,1,0:T(8,128)(2,1)} %add_convert_fusion.1), channel_id=1, source_target_pairs={{0,16},{8,24},{16,0},{24,8},{1,17},{9,25},{17,1},{25,9},{2,18},{10... | collective-permute-start | bytes 6291464 | tf_op jit(solution)/shard_map/ppermute | solution.py:23
  68.7 1.7 %bitcast_dynamic-update-slice_fusion = (f32[1,8,64,2048]{3,2,1,0:T(8,128)S(1)}, bf16[2,1,64,2048]{3,2,0,1:T(8,128)(2,1)S(1)}) fusion(f32[1,8,64,2048]{3,2,1,0:T(8,128)S(1)} %get-tuple-element.31, s32[]{:T(128)S(6)} %select_n.138, bf16[2,1,64,2048]{3,2,0,1:T(8,128)(2,1)S(1)} %collective-permute-done.4, f32[]{:T(128)S(6)} %sub.112, ...), kind=kLoop, calls=%fused_computation.8 | loop fusion | flops 3407872 | bytes 4718612 | tf_op jit(solution)/shard_map/dynamic_update_slice | solution.py:201
  70.5 1.0 collective-permute-done.19.refs_4_
  71.4 1.5 %collective-permute-start.14 = (bf16[1,64,2048]{2,1,0:T(8,128)(2,1)S(1)}, bf16[1,64,2048]{2,1,0:T(8,128)(2,1)S(1)}, u32[]{:S(2)}, u32[]{:S(2)}) collective-permute-start(bf16[1,64,2048]{2,1,0:T(8,128)(2,1)S(1)} %get-tuple-element.48), channel_id=1, source_target_pairs={{0,1},{1,0},{2,3},{3,2},{4,5},{5,4},{6,7},{7,6},{8,9},{9,8},{10,11... | collective-permute-start | bytes 786440 | tf_op jit(solution)/shard_map/ppermute | solution.py:23
  73.0 4.2 %collective-permute-done.20.refs_5_ = bf16[1,64,2048]{2,1,0:T(8,128)(2,1)S(1)} collective-permute-done((bf16[1,64,2048]{2,1,0:T(8,128)(2,1)S(1)}, bf16[1,64,2048]{2,1,0:T(8,128)(2,1)S(1)}, u32[]{:S(2)}, u32[]{:S(2)}) %collective-permute-start.20) | collective-permute-done | bytes 262176 | tf_op jit(solution)/shard_map/ppermute | solution.py:23
  77.1 6.1 %collective-permute-done.16.refs_3_ = bf16[1,64,2048]{2,1,0:T(8,128)(2,1)S(1)} collective-permute-done((bf16[1,64,2048]{2,1,0:T(8,128)(2,1)S(1)}, bf16[1,64,2048]{2,1,0:T(8,128)(2,1)S(1)}, u32[]{:S(2)}, u32[]{:S(2)}) %collective-permute-start.16) | collective-permute-done | bytes 262176 | tf_op jit(solution)/shard_map/ppermute | solution.py:23
  83.2 4.8 %collective-permute-done.14.refs_1_ = bf16[1,64,2048]{2,1,0:T(8,128)(2,1)S(1)} collective-permute-done((bf16[1,64,2048]{2,1,0:T(8,128)(2,1)S(1)}, bf16[1,64,2048]{2,1,0:T(8,128)(2,1)S(1)}, u32[]{:S(2)}, u32[]{:S(2)}) %collective-permute-start.14) | collective-permute-done | bytes 262176 | tf_op jit(solution)/shard_map/ppermute | solution.py:23
  88.0 12.8 %orthogonalize.1 = (bf16[1,64,2048]{2,1,0:T(8,128)(2,1)S(1)}, bf16[1,64,2048]{2,1,0:T(8,128)(2,1)S(1)}, bf16[1,64,2048]{2,1,0:T(8,128)(2,1)S(1)}, bf16[1,64,2048...) custom-call(bf16[1,64,2048]{2,1,0:T(8,128)(2,1)S(1)} %get-tuple-elem, ...), custom_call_target="tpu_custom_call" | custom-call | flops 11005853696 | bytes 4194304 | tf_op jit(solution)/shard_map/orthogonalize/pallas_call | solution.py:102
  100.8 0.9 collective-permute-start.22
  101.6 2.7 %collective-permute-start.21 = (bf16[1,64,2048]{2,1,0:T(8,128)(2,1)S(1)}, bf16[1,64,2048]{2,1,0:T(8,128)(2,1)S(1)}, u32[]{:S(2)}, u32[]{:S(2)}) collective-permute-start(bf16[1,64,2048]{2,1,0:T(8,128)(2,1)S(1)} %get-tuple-element.20), channel_id=1, source_target_pairs={{0,7},{1,6},{2,5},{3,4},{4,3},{5,2},{6,1},{7,0},{8,15},{9,14},{10,... | collective-permute-start | bytes 786440 | tf_op jit(solution)/shard_map/ppermute | solution.py:23
  104.4 1.8 %collective-permute-start.23 = (bf16[1,64,2048]{2,1,0:T(8,128)(2,1)S(1)}, bf16[1,64,2048]{2,1,0:T(8,128)(2,1)S(1)}, u32[]{:S(2)}, u32[]{:S(2)}) collective-permute-start(bf16[1,64,2048]{2,1,0:T(8,128)(2,1)S(1)} %get-tuple-element.23), channel_id=1, source_target_pairs={{0,6},{1,7},{2,4},{3,5},{4,2},{5,3},{6,0},{7,1},{8,14},{9,15},{10,... | collective-permute-start | bytes 786440 | tf_op jit(solution)/shard_map/ppermute | solution.py:23
  106.1 8.5 %collective-permute-done.22 = bf16[1,64,2048]{2,1,0:T(8,128)(2,1)S(1)} collective-permute-done((bf16[1,64,2048]{2,1,0:T(8,128)(2,1)S(1)}, bf16[1,64,2048]{2,1,0:T(8,128)(2,1)S(1)}, u32[]{:S(2)}, u32[]{:S(2)}) %collective-permute-start.22) | collective-permute-done | bytes 262176 | tf_op jit(solution)/shard_map/ppermute | solution.py:23
  115.0 3.2 %collective-permute-start.26 = (bf16[1,64,2048]{2,1,0:T(8,128)(2,1)S(1)}, bf16[1,64,2048]{2,1,0:T(8,128)(2,1)S(1)}, u32[]{:S(2)}, u32[]{:S(2)}) collective-permute-start(bf16[1,64,2048]{2,1,0:T(8,128)(2,1)S(1)} %get-tuple-element.26), channel_id=1, source_target_pairs={{0,5},{1,4},{2,7},{3,6},{4,1},{5,0},{6,3},{7,2},{8,13},{9,12},{10,... | collective-permute-start | bytes 786440 | tf_op jit(solution)/shard_map/ppermute | solution.py:23
  118.2 3.8 %add_convert_fusion = bf16[8,1,64,2048]{3,2,1,0:T(8,128)(2,1)S(1)} fusion(bf16[8,1,64,2048]{3,2,1,0:T(8,128)(2,1)} %collective-permute-done.13, bf16[8,1,64,2048]{3,2,1,0:T(8,128)(2,1)} %add_convert_fusion.1, f32[]{:T(128)S(6)} %sub.112, f32[]{:T(128)} %bitcast), kind=kLoop, calls=%fused_computation | loop fusion | flops 6291456 | bytes 6291464 | tf_op jit(solution)/shard_map/convert_element_type | solution.py:207
  121.9 0.3 collective-permute-start.27
  122.8 9.7 %collective-permute-done.24 = bf16[1,64,2048]{2,1,0:T(8,128)(2,1)S(1)} collective-permute-done((bf16[1,64,2048]{2,1,0:T(8,128)(2,1)S(1)}, bf16[1,64,2048]{2,1,0:T(8,128)(2,1)S(1)}, u32[]{:S(2)}, u32[]{:S(2)}) %collective-permute-start.24) | collective-permute-done | bytes 262176 | tf_op jit(solution)/shard_map/ppermute | solution.py:23
  132.6 5.5 %collective-permute-done.25 = bf16[1,64,2048]{2,1,0:T(8,128)(2,1)S(1)} collective-permute-done((bf16[1,64,2048]{2,1,0:T(8,128)(2,1)S(1)}, bf16[1,64,2048]{2,1,0:T(8,128)(2,1)S(1)}, u32[]{:S(2)}, u32[]{:S(2)}) %collective-permute-start.25) | collective-permute-done | bytes 262176 | tf_op jit(solution)/shard_map/ppermute | solution.py:23
  138.3 4.2 %collective-permute-done.27 = bf16[1,64,2048]{2,1,0:T(8,128)(2,1)S(1)} collective-permute-done((bf16[1,64,2048]{2,1,0:T(8,128)(2,1)S(1)}, bf16[1,64,2048]{2,1,0:T(8,128)(2,1)S(1)}, u32[]{:S(2)}, u32[]{:S(2)}) %collective-permute-start.27) | collective-permute-done | bytes 262176 | tf_op jit(solution)/shard_map/ppermute | solution.py:23
  142.7 1.3 copy-done.4
  144.0 0.7 copy-done.5
  (56 shorter events, 2.6 us)
Async XLA Ops:
  0.6 8.9 %copy-start.8 = (s32[4,2]{0,1:T(2,128)S(1)}, s32[4,2]{0,1:T(2,128)}, u32[]{:S(2)}) copy-start(s32[4,2]{0,1:T(2,128)} %param.9) | copy-start | bytes 100
  0.7 11.9 %copy-start.2 = (bf16[1,8,64,2048]{3,2,1,0:T(8,128)(2,1)S(1)}, bf16[1,8,64,2048]{3,2,1,0:T(8,128)(2,1)}, u32[]{:S(2)}) copy-start(bf16[1,8,64,2048]{3,2,1,0:T(8,128)(2,1)} %param.8) | copy-start | bytes 6291460
  2.8 9.3 %collective-permute-start.5 = (bf16[1,1,64,2048]{3,2,1,0:T(8,128)(2,1)}, bf16[1,1,64,2048]{3,2,1,0:T(8,128)(2,1)}, u32[]{:S(2)}, u32[]{:S(2)}) collective-permute-start(bf16[1,1,64,2048]{3,2,1,0:T(8,128)(2,1)} %get-tuple-element.43), channel_id=1, source_target_pairs={{0,8},{8,0},{16,24},{24,16},{1,9},{9,1},{17,25},{25,17},{2,10},{10... | collective-permute-start | bytes 786440 | tf_op jit(solution)/shard_map/ppermute | solution.py:23
  3.2 12.4 %collective-permute-start.6 = (bf16[1,1,64,2048]{3,2,1,0:T(8,128)(2,1)}, bf16[1,1,64,2048]{3,2,1,0:T(8,128)(2,1)}, u32[]{:S(2)}, u32[]{:S(2)}) collective-permute-start(bf16[1,1,64,2048]{3,2,1,0:T(8,128)(2,1)} %get-tuple-element.43), channel_id=1, source_target_pairs={{0,16},{8,24},{16,0},{24,8},{1,17},{9,25},{17,1},{25,9},{2,18},{10... | collective-permute-start | bytes 786440 | tf_op jit(solution)/shard_map/ppermute | solution.py:23
  5.7 6.7 %collective-permute-start.9 = (bf16[1,1,64,2048]{3,2,1,0:T(8,128)(2,1)S(1)}, bf16[1,1,64,2048]{3,2,1,0:T(8,128)(2,1)}, u32[]{:S(2)}, u32[]{:S(2)}) collective-permute-start(bf16[1,1,64,2048]{3,2,1,0:T(8,128)(2,1)S(1)} %get-tuple-element.42), channel_id=1, source_target_pairs={{0,8},{8,0},{16,24},{24,16},{1,9},{9,1},{17,25},{25,17},{2,10},{10... | collective-permute-start | bytes 786440 | tf_op jit(solution)/shard_map/ppermute | solution.py:23
  9.0 11.7 %collective-permute-start.17 = (bf16[2,1,64,2048]{3,2,0,1:T(8,128)(2,1)}, bf16[2,1,64,2048]{3,2,0,1:T(8,128)(2,1)S(1)}, u32[]{:S(2)}, u32[]{:S(2)}) collective-permute-start(bf16[2,1,64,2048]{3,2,0,1:T(8,128)(2,1)} %get-tuple-element.39), channel_id=1, source_target_pairs={{0,8},{8,0},{16,24},{24,16},{1,9},{9,1},{17,25},{25,17},{2,10},{10... | collective-permute-start | bytes 1572872 | tf_op jit(solution)/shard_map/ppermute | solution.py:23
  9.3 11.9 %collective-permute-start.2 = (bf16[2,1,64,2048]{3,2,1,0:T(8,128)(2,1)}, bf16[2,1,64,2048]{3,2,1,0:T(8,128)(2,1)S(1)}, u32[]{:S(2)}, u32[]{:S(2)}) collective-permute-start(bf16[2,1,64,2048]{3,2,1,0:T(8,128)(2,1)} %get-tuple-element.38), channel_id=1, source_target_pairs={{0,8},{8,0},{16,24},{24,16},{1,9},{9,1},{17,25},{25,17},{2,10},{10... | collective-permute-start | bytes 1572872 | tf_op jit(solution)/shard_map/ppermute | solution.py:23
  12.1 3.6 %copy-start.7 = (bf16[2,1,64,2048]{3,2,0,1:T(8,128)(2,1)S(1)}, bf16[2,1,64,2048]{3,2,0,1:T(8,128)(2,1)}, u32[]{:S(2)}) copy-start(bf16[2,1,64,2048]{3,2,0,1:T(8,128)(2,1)} %get-tuple-element.37) | copy-start | bytes 1572868
  12.1 8.6 %collective-permute-start.10 = (bf16[1,1,64,2048]{3,2,1,0:T(8,128)(2,1)S(1)}, bf16[1,1,64,2048]{3,2,1,0:T(8,128)(2,1)S(1)}, u32[]{:S(2)}, u32[]{:S(2)}) collective-permute-start(bf16[1,1,64,2048]{3,2,1,0:T(8,128)(2,1)S(1)} %get-tuple-element.42), channel_id=1, source_target_pairs={{0,16},{8,24},{16,0},{24,8},{1,17},{9,25},{17,1},{25,9},{2,18},{10... | collective-permute-start | bytes 786440 | tf_op jit(solution)/shard_map/ppermute | solution.py:23
  12.5 30.6 %collective-permute-start = (bf16[8,1,64,2048]{3,2,1,0:T(8,128)(2,1)}, bf16[8,1,64,2048]{3,2,1,0:T(8,128)(2,1)S(1)}, u32[]{:S(2)}, u32[]{:S(2)}) collective-permute-start(bf16[8,1,64,2048]{3,2,1,0:T(8,128)(2,1)} %bitcast.175), channel_id=1, source_target_pairs={{0,8},{8,0},{16,24},{24,16},{1,9},{9,1},{17,25},{25,17},{2,10},{10... | collective-permute-start | bytes 6291464 | tf_op jit(solution)/shard_map/ppermute | solution.py:23
  15.7 17.1 %collective-permute-start.1 = (bf16[2,1,64,2048]{3,2,0,1:T(8,128)(2,1)S(1)}, bf16[2,1,64,2048]{3,2,0,1:T(8,128)(2,1)S(1)}, u32[]{:S(2)}, u32[]{:S(2)}) collective-permute-start(bf16[2,1,64,2048]{3,2,0,1:T(8,128)(2,1)S(1)} %copy-done.7), channel_id=1, source_target_pairs={{0,8},{8,0},{16,24},{24,16},{1,9},{9,1},{17,25},{25,17},{2,10},{10... | collective-permute-start | bytes 1572872 | tf_op jit(solution)/shard_map/ppermute | solution.py:23
  20.7 3.3 %collective-permute-start.7 = (bf16[1,1,64,2048]{3,2,1,0:T(8,128)(2,1)}, bf16[1,1,64,2048]{3,2,1,0:T(8,128)(2,1)S(1)}, u32[]{:S(2)}, u32[]{:S(2)}) collective-permute-start(bf16[1,1,64,2048]{3,2,1,0:T(8,128)(2,1)} %collective-permute-done.6), channel_id=1, source_target_pairs={{0,8},{8,0},{16,24},{24,16},{1,9},{9,1},{17,25},{25,17},{2,10},{10... | collective-permute-start | bytes 786440 | tf_op jit(solution)/shard_map/ppermute | solution.py:23
  20.7 5.8 %collective-permute-start.11 = (bf16[1,1,64,2048]{3,2,1,0:T(8,128)(2,1)S(1)}, bf16[1,1,64,2048]{3,2,1,0:T(8,128)(2,1)S(1)}, u32[]{:S(2)}, u32[]{:S(2)}) collective-permute-start(bf16[1,1,64,2048]{3,2,1,0:T(8,128)(2,1)S(1)} %collective-permute-done.10), channel_id=1, source_target_pairs={{0,8},{8,0},{16,24},{24,16},{1,9},{9,1},{17,25},{25,17},{2,10},{10... | collective-permute-start | bytes 786440 | tf_op jit(solution)/shard_map/ppermute | solution.py:23
  23.6 14.9 %collective-permute-start.18 = (bf16[2,1,64,2048]{3,2,1,0:T(8,128)(2,1)S(1)}, bf16[2,1,64,2048]{3,2,1,0:T(8,128)(2,1)S(1)}, u32[]{:S(2)}, u32[]{:S(2)}) collective-permute-start(bf16[2,1,64,2048]{3,2,1,0:T(8,128)(2,1)S(1)} %get-tuple-element.41), channel_id=1, source_target_pairs={{0,16},{8,24},{16,0},{24,8},{1,17},{9,25},{17,1},{25,9},{2,18},{10... | collective-permute-start | bytes 1572872 | tf_op jit(solution)/shard_map/ppermute | solution.py:23
  24.0 10.0 %copy-start = (f32[1,8,64,2048]{3,2,1,0:T(8,128)S(1)}, f32[1,8,64,2048]{3,2,1,0:T(8,128)}, u32[]{:S(2)}) copy-start(f32[1,8,64,2048]{3,2,1,0:T(8,128)} %param.6) | copy-start | bytes 12582916
  26.5 12.0 %copy-start.3 = (bf16[1,8,64,2048]{3,2,1,0:T(8,128)(2,1)S(1)}, bf16[1,8,64,2048]{3,2,1,0:T(8,128)(2,1)}, u32[]{:S(2)}) copy-start(bf16[1,8,64,2048]{3,2,1,0:T(8,128)(2,1)} %param.7) | copy-start | bytes 6291460
  27.4 23.5 %collective-permute-start.12 = (bf16[1,64,2048]{2,1,0:T(8,128)(2,1)S(1)}, bf16[1,64,2048]{2,1,0:T(8,128)(2,1)S(1)}, u32[]{:S(2)}, u32[]{:S(2)}) collective-permute-start(bf16[1,64,2048]{2,1,0:T(8,128)(2,1)S(1)} %get-tuple-element.50), channel_id=1, source_target_pairs={{0,6},{1,7},{2,4},{3,5},{4,2},{5,3},{6,0},{7,1},{8,14},{9,15},{10,... | collective-permute-start | bytes 786440 | tf_op jit(solution)/shard_map/ppermute | solution.py:23
  31.3 17.5 %collective-permute-start.3 = (bf16[2,1,64,2048]{3,2,1,0:T(8,128)(2,1)S(1)}, bf16[2,1,64,2048]{3,2,1,0:T(8,128)(2,1)S(1)}, u32[]{:S(2)}, u32[]{:S(2)}) collective-permute-start(bf16[2,1,64,2048]{3,2,1,0:T(8,128)(2,1)S(1)} %get-tuple-element.40), channel_id=1, source_target_pairs={{0,16},{8,24},{16,0},{24,8},{1,17},{9,25},{17,1},{25,9},{2,18},{10... | collective-permute-start | bytes 1572872 | tf_op jit(solution)/shard_map/ppermute | solution.py:23
  32.8 27.9 %collective-permute-start.8 = (bf16[1,64,2048]{2,1,0:T(8,128)(2,1)S(1)}, bf16[1,64,2048]{2,1,0:T(8,128)(2,1)S(1)}, u32[]{:S(2)}, u32[]{:S(2)}) collective-permute-start(bf16[1,64,2048]{2,1,0:T(8,128)(2,1)S(1)} %get-tuple-element.52), channel_id=1, source_target_pairs={{0,7},{1,6},{2,5},{3,4},{4,3},{5,2},{6,1},{7,0},{8,15},{9,14},{10,... | collective-permute-start | bytes 786440 | tf_op jit(solution)/shard_map/ppermute | solution.py:23
  38.5 5.9 %copy-start.6 = (bf16[1,8,64,2048]{3,2,1,0:T(8,128)(2,1)S(1)}, bf16[1,8,64,2048]{3,2,1,0:T(8,128)(2,1)}, u32[]{:S(2)}) copy-start(bf16[1,8,64,2048]{3,2,1,0:T(8,128)(2,1)} %param.5) | copy-start | bytes 6291460
  40.4 31.0 %collective-permute-start.19 = (bf16[1,64,2048]{2,1,0:T(8,128)(2,1)S(1)}, bf16[1,64,2048]{2,1,0:T(8,128)(2,1)S(1)}, u32[]{:S(2)}, u32[]{:S(2)}) collective-permute-start(bf16[1,64,2048]{2,1,0:T(8,128)(2,1)S(1)} %get-tuple-element.45), channel_id=1, source_target_pairs={{0,4},{1,5},{2,6},{3,7},{4,0},{5,1},{6,2},{7,3},{8,12},{9,13},{10,... | collective-permute-start | bytes 786440 | tf_op jit(solution)/shard_map/ppermute | solution.py:23
  43.1 34.0 %collective-permute-start.20 = (bf16[1,64,2048]{2,1,0:T(8,128)(2,1)S(1)}, bf16[1,64,2048]{2,1,0:T(8,128)(2,1)S(1)}, u32[]{:S(2)}, u32[]{:S(2)}) collective-permute-start(bf16[1,64,2048]{2,1,0:T(8,128)(2,1)S(1)} %get-tuple-element.44), channel_id=1, source_target_pairs={{0,5},{1,4},{2,7},{3,6},{4,1},{5,0},{6,3},{7,2},{8,13},{9,12},{10,... | collective-permute-start | bytes 786440 | tf_op jit(solution)/shard_map/ppermute | solution.py:23
  48.8 18.4 %collective-permute-start.4 = (bf16[2,1,64,2048]{3,2,0,1:T(8,128)(2,1)S(1)}, bf16[2,1,64,2048]{3,2,0,1:T(8,128)(2,1)S(1)}, u32[]{:S(2)}, u32[]{:S(2)}) collective-permute-start(bf16[2,1,64,2048]{3,2,0,1:T(8,128)(2,1)S(1)} %fusion.3), channel_id=1, source_target_pairs={{0,16},{8,24},{16,0},{24,8},{1,17},{9,25},{17,1},{25,9},{2,18},{10... | collective-permute-start | bytes 1572872 | tf_op jit(solution)/shard_map/ppermute | solution.py:23
  50.9 26.3 %collective-permute-start.15 = (bf16[1,64,2048]{2,1,0:T(8,128)(2,1)S(1)}, bf16[1,64,2048]{2,1,0:T(8,128)(2,1)S(1)}, u32[]{:S(2)}, u32[]{:S(2)}) collective-permute-start(bf16[1,64,2048]{2,1,0:T(8,128)(2,1)S(1)} %get-tuple-element.47), channel_id=1, source_target_pairs={{0,2},{1,3},{2,0},{3,1},{4,6},{5,7},{6,4},{7,5},{8,10},{9,11},{10,... | collective-permute-start | bytes 786440 | tf_op jit(solution)/shard_map/ppermute | solution.py:23
  60.7 22.5 %collective-permute-start.16 = (bf16[1,64,2048]{2,1,0:T(8,128)(2,1)S(1)}, bf16[1,64,2048]{2,1,0:T(8,128)(2,1)S(1)}, u32[]{:S(2)}, u32[]{:S(2)}) collective-permute-start(bf16[1,64,2048]{2,1,0:T(8,128)(2,1)S(1)} %get-tuple-element.46), channel_id=1, source_target_pairs={{0,3},{1,2},{2,1},{3,0},{4,7},{5,6},{6,5},{7,4},{8,11},{9,10},{10,... | collective-permute-start | bytes 786440 | tf_op jit(solution)/shard_map/ppermute | solution.py:23
  67.2 47.8 %collective-permute-start.13 = (bf16[8,1,64,2048]{3,2,1,0:T(8,128)(2,1)}, bf16[8,1,64,2048]{3,2,1,0:T(8,128)(2,1)}, u32[]{:S(2)}, u32[]{:S(2)}) collective-permute-start(bf16[8,1,64,2048]{3,2,1,0:T(8,128)(2,1)} %add_convert_fusion.1), channel_id=1, source_target_pairs={{0,16},{8,24},{16,0},{24,8},{1,17},{9,25},{17,1},{25,9},{2,18},{10... | collective-permute-start | bytes 6291464 | tf_op jit(solution)/shard_map/ppermute | solution.py:23
  70.4 17.6 %copy-start.1 = (f32[1,8,64,2048]{3,2,1,0:T(8,128)}, f32[1,8,64,2048]{3,2,1,0:T(8,128)S(1)}, u32[]{:S(2)}) copy-start(f32[1,8,64,2048]{3,2,1,0:T(8,128)S(1)} %get-tuple-element.29) | copy-start | bytes 12582916
  71.4 16.6 %collective-permute-start.14 = (bf16[1,64,2048]{2,1,0:T(8,128)(2,1)S(1)}, bf16[1,64,2048]{2,1,0:T(8,128)(2,1)S(1)}, u32[]{:S(2)}, u32[]{:S(2)}) collective-permute-start(bf16[1,64,2048]{2,1,0:T(8,128)(2,1)S(1)} %get-tuple-element.48), channel_id=1, source_target_pairs={{0,1},{1,0},{2,3},{3,2},{4,5},{5,4},{6,7},{7,6},{8,9},{9,8},{10,11... | collective-permute-start | bytes 786440 | tf_op jit(solution)/shard_map/ppermute | solution.py:23
  100.8 13.9 %collective-permute-start.22 = (bf16[1,64,2048]{2,1,0:T(8,128)(2,1)S(1)}, bf16[1,64,2048]{2,1,0:T(8,128)(2,1)S(1)}, u32[]{:S(2)}, u32[]{:S(2)}) collective-permute-start(bf16[1,64,2048]{2,1,0:T(8,128)(2,1)S(1)} %get-tuple-element.22), channel_id=1, source_target_pairs={{0,1},{1,0},{2,3},{3,2},{4,5},{5,4},{6,7},{7,6},{8,9},{9,8},{10,11... | collective-permute-start | bytes 786440 | tf_op jit(solution)/shard_map/ppermute | solution.py:23
  101.6 20.3 %collective-permute-start.21 = (bf16[1,64,2048]{2,1,0:T(8,128)(2,1)S(1)}, bf16[1,64,2048]{2,1,0:T(8,128)(2,1)S(1)}, u32[]{:S(2)}, u32[]{:S(2)}) collective-permute-start(bf16[1,64,2048]{2,1,0:T(8,128)(2,1)S(1)} %get-tuple-element.20), channel_id=1, source_target_pairs={{0,7},{1,6},{2,5},{3,4},{4,3},{5,2},{6,1},{7,0},{8,15},{9,14},{10,... | collective-permute-start | bytes 786440 | tf_op jit(solution)/shard_map/ppermute | solution.py:23
  104.4 18.3 %collective-permute-start.23 = (bf16[1,64,2048]{2,1,0:T(8,128)(2,1)S(1)}, bf16[1,64,2048]{2,1,0:T(8,128)(2,1)S(1)}, u32[]{:S(2)}, u32[]{:S(2)}) collective-permute-start(bf16[1,64,2048]{2,1,0:T(8,128)(2,1)S(1)} %get-tuple-element.23), channel_id=1, source_target_pairs={{0,6},{1,7},{2,4},{3,5},{4,2},{5,3},{6,0},{7,1},{8,14},{9,15},{10,... | collective-permute-start | bytes 786440 | tf_op jit(solution)/shard_map/ppermute | solution.py:23
  106.1 26.4 %collective-permute-start.24 = (bf16[1,64,2048]{2,1,0:T(8,128)(2,1)S(1)}, bf16[1,64,2048]{2,1,0:T(8,128)(2,1)S(1)}, u32[]{:S(2)}, u32[]{:S(2)}) collective-permute-start(bf16[1,64,2048]{2,1,0:T(8,128)(2,1)S(1)} %get-tuple-element.24), channel_id=1, source_target_pairs={{0,2},{1,3},{2,0},{3,1},{4,6},{5,7},{6,4},{7,5},{8,10},{9,11},{10,... | collective-permute-start | bytes 786440 | tf_op jit(solution)/shard_map/ppermute | solution.py:23
  114.7 23.4 %collective-permute-start.25 = (bf16[1,64,2048]{2,1,0:T(8,128)(2,1)S(1)}, bf16[1,64,2048]{2,1,0:T(8,128)(2,1)S(1)}, u32[]{:S(2)}, u32[]{:S(2)}) collective-permute-start(bf16[1,64,2048]{2,1,0:T(8,128)(2,1)S(1)} %get-tuple-element.25), channel_id=1, source_target_pairs={{0,3},{1,2},{2,1},{3,0},{4,7},{5,6},{6,5},{7,4},{8,11},{9,10},{10,... | collective-permute-start | bytes 786440 | tf_op jit(solution)/shard_map/ppermute | solution.py:23
  115.0 23.2 %collective-permute-start.26 = (bf16[1,64,2048]{2,1,0:T(8,128)(2,1)S(1)}, bf16[1,64,2048]{2,1,0:T(8,128)(2,1)S(1)}, u32[]{:S(2)}, u32[]{:S(2)}) collective-permute-start(bf16[1,64,2048]{2,1,0:T(8,128)(2,1)S(1)} %get-tuple-element.26), channel_id=1, source_target_pairs={{0,5},{1,4},{2,7},{3,6},{4,1},{5,0},{6,3},{7,2},{8,13},{9,12},{10,... | collective-permute-start | bytes 786440 | tf_op jit(solution)/shard_map/ppermute | solution.py:23
  121.9 20.5 %collective-permute-start.27 = (bf16[1,64,2048]{2,1,0:T(8,128)(2,1)S(1)}, bf16[1,64,2048]{2,1,0:T(8,128)(2,1)S(1)}, u32[]{:S(2)}, u32[]{:S(2)}) collective-permute-start(bf16[1,64,2048]{2,1,0:T(8,128)(2,1)S(1)} %get-tuple-element.27), channel_id=1, source_target_pairs={{0,4},{1,5},{2,6},{3,7},{4,0},{5,1},{6,2},{7,3},{8,12},{9,13},{10,... | collective-permute-start | bytes 786440 | tf_op jit(solution)/shard_map/ppermute | solution.py:23
  142.7 1.3 copy-start.4
  142.7 2.0 %copy-start.5 = (bf16[1,8,64,2048]{3,2,1,0:T(8,128)(2,1)}, bf16[1,8,64,2048]{3,2,1,0:T(8,128)(2,1)S(1)}, u32[]{:S(2)}) copy-start(bf16[1,8,64,2048]{3,2,1,0:T(8,128)(2,1)S(1)} %get-tuple-element.54) | copy-start | bytes 6291460

commit v18 on v17

--- a/solution.py
+++ b/solution.py
@@ -177,7 +177,7 @@
             elif turn == 4:
                 sent = after(sent, arrived[2], weight_near)
             far = swapped(sent, "rep", 2)
-            if turn == 2:
+            if turn == 3:
                 far = after(far, weight_own)
             if turn == 4:
                 far = after(far, blocks[7 * shards // 8], blocks[6 * shards // 8])

time: 145 us -> 141 us (0.972)
  starting transfers between devices: 44.5 us -> 29.8 us
  waiting for transfers between devices: 53.9 us -> 64.5 us
    ppermute x28, starting transfers between devices: 44.5 us -> 29.8 us  [swapped(): lax.ppermute(values, axis, [(i, i ^ offset) for i in range(lax.axis_size(...]
    ppermute x28, waiting for transfers between devices: 53.9 us -> 64.5 us  [swapped(): lax.ppermute(values, axis, [(i, i ^ offset) for i in range(lax.axis_size(...]
  transfers between devices with their start and end apart: 28 -> 28, of which waited for: 11 -> 14; matrix products, arithmetic and copies ran while one was open for 18% -> 19% of each run, Pallas kernels for 9% -> 9%
where the time goes in v18:
time: 141 us; the launch traced here: 140 us
  waiting for transfers between devices  64.5 us (46%)
  starting transfers between devices  29.8 us (21%)
  other arithmetic  21.5 us (15%)
  Pallas kernels  12.8 us (9%)
  local copies, waits for them, and re-layouts  9.01 us (6%)
  between operations  2.85 us (2%)
    ppermute x28, waiting for transfers between devices, swapped(): lax.ppermute(values, axis, [(i, i ^ offset) for i in range(lax.axis_size(...  64.5 us
    ppermute x28, starting transfers between devices, swapped(): lax.ppermute(values, axis, [(i, i ^ offset) for i in range(lax.axis_size(...  29.8 us
    pallas_call x1, Pallas kernels, orthogonalize(): pl.pallas_call(body, grid=(each,), in_specs=[block] * count, out_specs=[b...  12.8 us
    dynamic_update_slice x3, other arithmetic, local(): lax.dynamic_update_slice_in_dim(new_tracker, group, start, axis=0)  5.18 us
    convert_element_type x2, local copies, waits for them, and re-layouts, local(): rounded = own.astype(BF16)  5.17 us
    convert_element_type x1, other arithmetic, local(): mixed_weight = (second * weight_own.astype(F32) + (1.0 - second) * weight...  3.77 us
    convert_element_type x2, other arithmetic, local(): sent = mixed.astype(BF16)  3.16 us
    add x1, other arithmetic, local(): second * mixed  3.07 us
  transfers between devices with their start and end apart: 28, of which 14 were waited for; matrix products, arithmetic and copies ran while one was open for 19% of the time, Pallas kernels for 9%

profile of v18, /device:TPU:0, one launch (start us, length us, event | category | flops | bytes accessed | tf_op | source)
XLA Modules:
  0.0 140.5 jit_solution(3957720806929509601)
XLA Ops:
  0.7 2.1 %dynamic-slice_convert_fusion.9 = (bf16[1,1,64,2048]{3,2,1,0:T(8,128)(2,1)S(1)}, bf16[1,1,64,2048]{3,2,1,0:T(8,128)(2,1)}) fusion(f32[1,8,64,2048]{3,2,1,0:T(8,128)} %param.6, s32[]{:T(128)S(6)} %select_n.143, s32[]{:T(128)S(6)} %select_n.141), kind=kLoop, calls=%fused_computation.53 | loop fusion | bytes 1048584 | tf_op jit(solution)/shard_map/convert_element_type | solution.py:168
  2.8 0.5 collective-permute-start.5
  3.2 2.5 %collective-permute-start.6 = (bf16[1,1,64,2048]{3,2,1,0:T(8,128)(2,1)}, bf16[1,1,64,2048]{3,2,1,0:T(8,128)(2,1)}, u32[]{:S(2)}, u32[]{:S(2)}) collective-permute-start(bf16[1,1,64,2048]{3,2,1,0:T(8,128)(2,1)} %get-tuple-element.43), channel_id=1, source_target_pairs={{0,16},{8,24},{16,0},{24,8},{1,17},{9,25},{17,1},{25,9},{2,18},{10... | collective-permute-start | bytes 786440 | tf_op jit(solution)/shard_map/ppermute | solution.py:23
  5.9 3.1 %fusion.6 = (bf16[2,1,64,2048]{3,2,0,1:T(8,128)(2,1)}, bf16[2,1,64,2048]{3,2,1,0:T(8,128)(2,1)}, bf16[2,1,64,2048]{3,2,0,1:T(8,128)(2,1)}) fusion(f32[1,8,64,2048]{3,2,1,0:T(8,128)} %param.6, s32[]{:T(128)S(6)} %select_n.138, s32[]{:T(128)S(6)} %select_n.140, s32[]{:T(128)S(6)} %select_n.153), kind=kLoop, calls=%fused_computation.24 | loop fusion | bytes 3145740 | tf_op jit(solution)/shard_map/convert_element_type | solution.py:168
  9.5 0.7 constant_dynamic-slice_fusion
  12.6 3.1 %subtract_add_fusion = (f32[1,1,64,2048]{3,2,1,0:T(8,128)S(1)}, f32[1,1,64,2048]{3,2,1,0:T(8,128)S(1)}) fusion(bf16[1,1,64,2048]{3,2,1,0:T(8,128)(2,1)} %collective-permute-done.9, f32[1,8,64,2048]{3,2,1,0:T(8,128)} %param.6, s32[]{:T(128)S(6)} %select_n.143, bf16[1,8,64,2048]{3,2,1,0:T(8,128)(2,1)S(1)} %copy-done.2, bf16[1,8,64,2048]{3,2,1,0:T(8,128)(2,1)} %param.7, ...), kind=kLoop, calls=%fused_computation.50 | loop fusion | flops 2359296 | bytes 3670036 | tf_op jit(solution)/shard_map/add | solution.py:186
  15.7 0.5 collective-permute-start.1
  16.1 4.5 %collective-permute-done.10 = bf16[1,1,64,2048]{3,2,1,0:T(8,128)(2,1)S(1)} collective-permute-done((bf16[1,1,64,2048]{3,2,1,0:T(8,128)(2,1)S(1)}, bf16[1,1,64,2048]{3,2,1,0:T(8,128)(2,1)S(1)}, u32[]{:S(2)}, u32[]{:S(2)}) %collective-permute-start.10) | collective-permute-done | bytes 262176 | tf_op jit(solution)/shard_map/ppermute | solution.py:23
  20.7 0.5 collective-permute-start.11
  21.2 2.4 %fusion.4 = (bf16[2,1,64,2048]{3,2,1,0:T(8,128)(2,1)S(1)}, bf16[2,1,64,2048]{3,2,1,0:T(8,128)(2,1)S(1)}) fusion(bf16[2,1,64,2048]{3,2,1,0:T(8,128)(2,1)S(1)} %collective-permute-done.2, f32[1,8,64,2048]{3,2,1,0:T(8,128)} %param.6, s32[]{:T(128)S(6)} %select_n.140, f32[]{:T(128)S(6)} %sub.108, f32[]{:T(128)} %bitcast.1, ...), kind=kLoop, calls=%fused_computation.22 | loop fusion | flops 2621440 | bytes 4194320 | tf_op jit(solution)/shard_map/convert_element_type | solution.py:174
  23.6 0.4 collective-permute-start.3
  24.0 0.5 reshape.500
  24.5 2.0 %convert_bitcast_fusion.1 = (bf16[1,64,2048]{2,1,0:T(8,128)(2,1)S(1)}, f32[1,8,64,2048]{3,2,1,0:T(8,128)S(1)}) fusion(f32[1,1,64,2048]{3,2,1,0:T(8,128)S(1)} %get-tuple-element.36, bf16[1,1,64,2048]{3,2,1,0:T(8,128)(2,1)S(1)} %collective-permute-done.7, f32[]{:T(128)S(6)} %sub.113, bf16[1,1,64,2048]{3,2,1,0:T(8,128)(2,1)} %collective-permute-done.6, ...), kind=kLoop, calls=%fused_computation.86 | loop fusion | flops 1048576 | bytes 1835024 | tf_op jit(solution)/shard_map/convert_element_type | solution.py:195
  26.5 0.9 convert_bitcast_fusion
  27.4 3.9 %collective-permute-start.12 = (bf16[1,64,2048]{2,1,0:T(8,128)(2,1)S(1)}, bf16[1,64,2048]{2,1,0:T(8,128)(2,1)S(1)}, u32[]{:S(2)}, u32[]{:S(2)}) collective-permute-start(bf16[1,64,2048]{2,1,0:T(8,128)(2,1)S(1)} %get-tuple-element.50), channel_id=1, source_target_pairs={{0,6},{1,7},{2,4},{3,5},{4,2},{5,3},{6,0},{7,1},{8,14},{9,15},{10,... | collective-permute-start | bytes 786440 | tf_op jit(solution)/shard_map/ppermute | solution.py:23
  31.3 1.2 collective-permute-start.8
  32.5 1.5 %collective-permute-start.18 = (bf16[2,1,64,2048]{3,2,1,0:T(8,128)(2,1)S(1)}, bf16[2,1,64,2048]{3,2,1,0:T(8,128)(2,1)S(1)}, u32[]{:S(2)}, u32[]{:S(2)}) collective-permute-start(bf16[2,1,64,2048]{3,2,1,0:T(8,128)(2,1)S(1)} %get-tuple-element.41), channel_id=1, source_target_pairs={{0,16},{8,24},{16,0},{24,8},{1,17},{9,25},{17,1},{25,9},{2,18},{10... | collective-permute-start | bytes 1572872 | tf_op jit(solution)/shard_map/ppermute | solution.py:23
  34.0 0.7 fusion.3
  34.7 3.8 %collective-permute-done.3 = bf16[2,1,64,2048]{3,2,1,0:T(8,128)(2,1)S(1)} collective-permute-done((bf16[2,1,64,2048]{3,2,1,0:T(8,128)(2,1)S(1)}, bf16[2,1,64,2048]{3,2,1,0:T(8,128)(2,1)S(1)}, u32[]{:S(2)}, u32[]{:S(2)}) %collective-permute-start.3) | collective-permute-done | bytes 524320 | tf_op jit(solution)/shard_map/ppermute | solution.py:23
  38.8 2.8 %add_convert_fusion.1 = bf16[8,1,64,2048]{3,2,1,0:T(8,128)(2,1)} fusion(bf16[8,1,64,2048]{3,2,1,0:T(8,128)(2,1)S(1)} %collective-permute-done, f32[]{:T(128)S(6)} %sub.108, f32[]{:T(128)} %bitcast.1, bf16[1,8,64,2048]{3,2,1,0:T(8,128)(2,1)S(1)} %copy-done.6), kind=kLoop, calls=%fused_computation.1 | loop fusion | flops 6291456 | bytes 6291464 | tf_op jit(solution)/shard_map/convert_element_type | solution.py:155
  41.5 8.2 %collective-permute-done.18 = bf16[2,1,64,2048]{3,2,1,0:T(8,128)(2,1)S(1)} collective-permute-done((bf16[2,1,64,2048]{3,2,1,0:T(8,128)(2,1)S(1)}, bf16[2,1,64,2048]{3,2,1,0:T(8,128)(2,1)S(1)}, u32[]{:S(2)}, u32[]{:S(2)}) %collective-permute-start.18) | collective-permute-done | bytes 524320 | tf_op jit(solution)/shard_map/ppermute | solution.py:23
  49.7 1.7 %bitcast_dynamic-update-slice_fusion.2 = (f32[1,8,64,2048]{3,2,1,0:T(8,128)S(1)}, bf16[2,1,64,2048]{3,2,1,0:T(8,128)(2,1)S(1)}) fusion(f32[1,8,64,2048]{3,2,1,0:T(8,128)S(1)} %get-tuple-element.51, s32[]{:T(128)S(6)} %select_n.153, bf16[2,1,64,2048]{3,2,1,0:T(8,128)(2,1)S(1)} %collective-permute-done.18, f32[]{:T(128)S(6)} %sub.112, ...), kind=kLoop, calls=%fused_computation.10 | loop fusion | flops 3407872 | bytes 4718612 | tf_op jit(solution)/shard_map/dynamic_update_slice | solution.py:201
  51.5 1.7 %bitcast_dynamic-update-slice_fusion.1 = (f32[1,8,64,2048]{3,2,1,0:T(8,128)S(1)}, bf16[2,1,64,2048]{3,2,1,0:T(8,128)(2,1)S(1)}) fusion(f32[1,8,64,2048]{3,2,1,0:T(8,128)S(1)} %get-tuple-element.33, s32[]{:T(128)S(6)} %select_n.140, bf16[2,1,64,2048]{3,2,1,0:T(8,128)(2,1)S(1)} %collective-permute-done.3, f32[]{:T(128)S(6)} %sub.112, ...), kind=kLoop, calls=%fused_computation.9 | loop fusion | flops 3407872 | bytes 4718612 | tf_op jit(solution)/shard_map/dynamic_update_slice | solution.py:201
  53.3 1.6 %collective-permute-start.15 = (bf16[1,64,2048]{2,1,0:T(8,128)(2,1)S(1)}, bf16[1,64,2048]{2,1,0:T(8,128)(2,1)S(1)}, u32[]{:S(2)}, u32[]{:S(2)}) collective-permute-start(bf16[1,64,2048]{2,1,0:T(8,128)(2,1)S(1)} %get-tuple-element.47), channel_id=1, source_target_pairs={{0,2},{1,3},{2,0},{3,1},{4,6},{5,7},{6,4},{7,5},{8,10},{9,11},{10,... | collective-permute-start | bytes 786440 | tf_op jit(solution)/shard_map/ppermute | solution.py:23
  54.9 1.4 %collective-permute-start.16 = (bf16[1,64,2048]{2,1,0:T(8,128)(2,1)S(1)}, bf16[1,64,2048]{2,1,0:T(8,128)(2,1)S(1)}, u32[]{:S(2)}, u32[]{:S(2)}) collective-permute-start(bf16[1,64,2048]{2,1,0:T(8,128)(2,1)S(1)} %get-tuple-element.46), channel_id=1, source_target_pairs={{0,3},{1,2},{2,1},{3,0},{4,7},{5,6},{6,5},{7,4},{8,11},{9,10},{10,... | collective-permute-start | bytes 786440 | tf_op jit(solution)/shard_map/ppermute | solution.py:23
  56.4 2.7 %collective-permute-start.19 = (bf16[1,64,2048]{2,1,0:T(8,128)(2,1)S(1)}, bf16[1,64,2048]{2,1,0:T(8,128)(2,1)S(1)}, u32[]{:S(2)}, u32[]{:S(2)}) collective-permute-start(bf16[1,64,2048]{2,1,0:T(8,128)(2,1)S(1)} %get-tuple-element.45), channel_id=1, source_target_pairs={{0,4},{1,5},{2,6},{3,7},{4,0},{5,1},{6,2},{7,3},{8,12},{9,13},{10,... | collective-permute-start | bytes 786440 | tf_op jit(solution)/shard_map/ppermute | solution.py:23
  59.3 0.7 collective-permute-done.4
  60.3 1.7 %bitcast_dynamic-update-slice_fusion = (f32[1,8,64,2048]{3,2,1,0:T(8,128)S(1)}, bf16[2,1,64,2048]{3,2,0,1:T(8,128)(2,1)S(1)}) fusion(f32[1,8,64,2048]{3,2,1,0:T(8,128)S(1)} %get-tuple-element.31, s32[]{:T(128)S(6)} %select_n.138, bf16[2,1,64,2048]{3,2,0,1:T(8,128)(2,1)S(1)} %collective-permute-done.4, f32[]{:T(128)S(6)} %sub.112, ...), kind=kLoop, calls=%fused_computation.8 | loop fusion | flops 3407872 | bytes 4718612 | tf_op jit(solution)/shard_map/dynamic_update_slice | solution.py:201
  62.1 10.3 %collective-permute-done.15.refs_2_ = bf16[1,64,2048]{2,1,0:T(8,128)(2,1)S(1)} collective-permute-done((bf16[1,64,2048]{2,1,0:T(8,128)(2,1)S(1)}, bf16[1,64,2048]{2,1,0:T(8,128)(2,1)S(1)}, u32[]{:S(2)}, u32[]{:S(2)}) %collective-permute-start.15) | collective-permute-done | bytes 262176 | tf_op jit(solution)/shard_map/ppermute | solution.py:23
  72.4 1.9 %collective-permute-start.14 = (bf16[1,64,2048]{2,1,0:T(8,128)(2,1)S(1)}, bf16[1,64,2048]{2,1,0:T(8,128)(2,1)S(1)}, u32[]{:S(2)}, u32[]{:S(2)}) collective-permute-start(bf16[1,64,2048]{2,1,0:T(8,128)(2,1)S(1)} %get-tuple-element.48), channel_id=1, source_target_pairs={{0,1},{1,0},{2,3},{3,2},{4,5},{5,4},{6,7},{7,6},{8,9},{9,8},{10,11... | collective-permute-start | bytes 786440 | tf_op jit(solution)/shard_map/ppermute | solution.py:23
  74.3 2.5 %collective-permute-done.16.refs_3_ = bf16[1,64,2048]{2,1,0:T(8,128)(2,1)S(1)} collective-permute-done((bf16[1,64,2048]{2,1,0:T(8,128)(2,1)S(1)}, bf16[1,64,2048]{2,1,0:T(8,128)(2,1)S(1)}, u32[]{:S(2)}, u32[]{:S(2)}) %collective-permute-start.16) | collective-permute-done | bytes 262176 | tf_op jit(solution)/shard_map/ppermute | solution.py:23
  76.8 3.7 %collective-permute-done.20.refs_5_ = bf16[1,64,2048]{2,1,0:T(8,128)(2,1)S(1)} collective-permute-done((bf16[1,64,2048]{2,1,0:T(8,128)(2,1)S(1)}, bf16[1,64,2048]{2,1,0:T(8,128)(2,1)S(1)}, u32[]{:S(2)}, u32[]{:S(2)}) %collective-permute-start.20) | collective-permute-done | bytes 262176 | tf_op jit(solution)/shard_map/ppermute | solution.py:23
  80.5 0.4 collective-permute-done.14.refs_1_
  81.0 12.8 %orthogonalize.1 = (bf16[1,64,2048]{2,1,0:T(8,128)(2,1)S(1)}, bf16[1,64,2048]{2,1,0:T(8,128)(2,1)S(1)}, bf16[1,64,2048]{2,1,0:T(8,128)(2,1)S(1)}, bf16[1,64,2048...) custom-call(bf16[1,64,2048]{2,1,0:T(8,128)(2,1)S(1)} %get-tuple-elem, ...), custom_call_target="tpu_custom_call" | custom-call | flops 11005853696 | bytes 4194304 | tf_op jit(solution)/shard_map/orthogonalize/pallas_call | solution.py:102
  93.8 1.1 collective-permute-start.22
  94.9 3.4 %collective-permute-start.21 = (bf16[1,64,2048]{2,1,0:T(8,128)(2,1)S(1)}, bf16[1,64,2048]{2,1,0:T(8,128)(2,1)S(1)}, u32[]{:S(2)}, u32[]{:S(2)}) collective-permute-start(bf16[1,64,2048]{2,1,0:T(8,128)(2,1)S(1)} %get-tuple-element.20), channel_id=1, source_target_pairs={{0,7},{1,6},{2,5},{3,4},{4,3},{5,2},{6,1},{7,0},{8,15},{9,14},{10,... | collective-permute-start | bytes 786440 | tf_op jit(solution)/shard_map/ppermute | solution.py:23
  98.3 0.8 collective-permute-start.23
  99.1 3.8 %collective-permute-done.22 = bf16[1,64,2048]{2,1,0:T(8,128)(2,1)S(1)} collective-permute-done((bf16[1,64,2048]{2,1,0:T(8,128)(2,1)S(1)}, bf16[1,64,2048]{2,1,0:T(8,128)(2,1)S(1)}, u32[]{:S(2)}, u32[]{:S(2)}) %collective-permute-start.22) | collective-permute-done | bytes 262176 | tf_op jit(solution)/shard_map/ppermute | solution.py:23
  103.2 3.8 %collective-permute-done.13 = bf16[8,1,64,2048]{3,2,1,0:T(8,128)(2,1)} collective-permute-done((bf16[8,1,64,2048]{3,2,1,0:T(8,128)(2,1)}, bf16[8,1,64,2048]{3,2,1,0:T(8,128)(2,1)}, u32[]{:S(2)}, u32[]{:S(2)}) %collective-permute-start.13) | collective-permute-done | bytes 2097184 | tf_op jit(solution)/shard_map/ppermute | solution.py:23
  107.0 3.5 %collective-permute-start.26 = (bf16[1,64,2048]{2,1,0:T(8,128)(2,1)S(1)}, bf16[1,64,2048]{2,1,0:T(8,128)(2,1)S(1)}, u32[]{:S(2)}, u32[]{:S(2)}) collective-permute-start(bf16[1,64,2048]{2,1,0:T(8,128)(2,1)S(1)} %get-tuple-element.26), channel_id=1, source_target_pairs={{0,5},{1,4},{2,7},{3,6},{4,1},{5,0},{6,3},{7,2},{8,13},{9,12},{10,... | collective-permute-start | bytes 786440 | tf_op jit(solution)/shard_map/ppermute | solution.py:23
  110.6 3.8 %add_convert_fusion = bf16[8,1,64,2048]{3,2,1,0:T(8,128)(2,1)S(1)} fusion(bf16[8,1,64,2048]{3,2,1,0:T(8,128)(2,1)} %collective-permute-done.13, bf16[8,1,64,2048]{3,2,1,0:T(8,128)(2,1)} %add_convert_fusion.1, f32[]{:T(128)S(6)} %sub.112, f32[]{:T(128)} %bitcast), kind=kLoop, calls=%fused_computation | loop fusion | flops 6291456 | bytes 6291464 | tf_op jit(solution)/shard_map/convert_element_type | solution.py:207
  114.4 0.4 collective-permute-start.27
  115.3 1.0 collective-permute-done.24
  116.4 5.5 %collective-permute-done.25 = bf16[1,64,2048]{2,1,0:T(8,128)(2,1)S(1)} collective-permute-done((bf16[1,64,2048]{2,1,0:T(8,128)(2,1)S(1)}, bf16[1,64,2048]{2,1,0:T(8,128)(2,1)S(1)}, u32[]{:S(2)}, u32[]{:S(2)}) %collective-permute-start.25) | collective-permute-done | bytes 262176 | tf_op jit(solution)/shard_map/ppermute | solution.py:23
  122.0 13.4 %collective-permute-done.26 = bf16[1,64,2048]{2,1,0:T(8,128)(2,1)S(1)} collective-permute-done((bf16[1,64,2048]{2,1,0:T(8,128)(2,1)S(1)}, bf16[1,64,2048]{2,1,0:T(8,128)(2,1)S(1)}, u32[]{:S(2)}, u32[]{:S(2)}) %collective-permute-start.26) | collective-permute-done | bytes 262176 | tf_op jit(solution)/shard_map/ppermute | solution.py:23
  135.5 2.8 %collective-permute-done.27 = bf16[1,64,2048]{2,1,0:T(8,128)(2,1)S(1)} collective-permute-done((bf16[1,64,2048]{2,1,0:T(8,128)(2,1)S(1)}, bf16[1,64,2048]{2,1,0:T(8,128)(2,1)S(1)}, u32[]{:S(2)}, u32[]{:S(2)}) %collective-permute-start.27) | collective-permute-done | bytes 262176 | tf_op jit(solution)/shard_map/ppermute | solution.py:23
  138.5 1.3 copy-done.4
  139.8 0.7 copy-done.5
  (56 shorter events, 3.5 us)
Async XLA Ops:
  0.6 8.9 %copy-start.8 = (s32[4,2]{0,1:T(2,128)S(1)}, s32[4,2]{0,1:T(2,128)}, u32[]{:S(2)}) copy-start(s32[4,2]{0,1:T(2,128)} %param.9) | copy-start | bytes 100
  0.7 11.9 %copy-start.2 = (bf16[1,8,64,2048]{3,2,1,0:T(8,128)(2,1)S(1)}, bf16[1,8,64,2048]{3,2,1,0:T(8,128)(2,1)}, u32[]{:S(2)}) copy-start(bf16[1,8,64,2048]{3,2,1,0:T(8,128)(2,1)} %param.8) | copy-start | bytes 6291460
  2.8 9.3 %collective-permute-start.5 = (bf16[1,1,64,2048]{3,2,1,0:T(8,128)(2,1)}, bf16[1,1,64,2048]{3,2,1,0:T(8,128)(2,1)}, u32[]{:S(2)}, u32[]{:S(2)}) collective-permute-start(bf16[1,1,64,2048]{3,2,1,0:T(8,128)(2,1)} %get-tuple-element.43), channel_id=1, source_target_pairs={{0,8},{8,0},{16,24},{24,16},{1,9},{9,1},{17,25},{25,17},{2,10},{10... | collective-permute-start | bytes 786440 | tf_op jit(solution)/shard_map/ppermute | solution.py:23
  3.2 12.4 %collective-permute-start.6 = (bf16[1,1,64,2048]{3,2,1,0:T(8,128)(2,1)}, bf16[1,1,64,2048]{3,2,1,0:T(8,128)(2,1)}, u32[]{:S(2)}, u32[]{:S(2)}) collective-permute-start(bf16[1,1,64,2048]{3,2,1,0:T(8,128)(2,1)} %get-tuple-element.43), channel_id=1, source_target_pairs={{0,16},{8,24},{16,0},{24,8},{1,17},{9,25},{17,1},{25,9},{2,18},{10... | collective-permute-start | bytes 786440 | tf_op jit(solution)/shard_map/ppermute | solution.py:23
  5.7 6.7 %collective-permute-start.9 = (bf16[1,1,64,2048]{3,2,1,0:T(8,128)(2,1)S(1)}, bf16[1,1,64,2048]{3,2,1,0:T(8,128)(2,1)}, u32[]{:S(2)}, u32[]{:S(2)}) collective-permute-start(bf16[1,1,64,2048]{3,2,1,0:T(8,128)(2,1)S(1)} %get-tuple-element.42), channel_id=1, source_target_pairs={{0,8},{8,0},{16,24},{24,16},{1,9},{9,1},{17,25},{25,17},{2,10},{10... | collective-permute-start | bytes 786440 | tf_op jit(solution)/shard_map/ppermute | solution.py:23
  9.0 11.7 %collective-permute-start.17 = (bf16[2,1,64,2048]{3,2,0,1:T(8,128)(2,1)}, bf16[2,1,64,2048]{3,2,0,1:T(8,128)(2,1)S(1)}, u32[]{:S(2)}, u32[]{:S(2)}) collective-permute-start(bf16[2,1,64,2048]{3,2,0,1:T(8,128)(2,1)} %get-tuple-element.39), channel_id=1, source_target_pairs={{0,8},{8,0},{16,24},{24,16},{1,9},{9,1},{17,25},{25,17},{2,10},{10... | collective-permute-start | bytes 1572872 | tf_op jit(solution)/shard_map/ppermute | solution.py:23
  9.3 11.9 %collective-permute-start.2 = (bf16[2,1,64,2048]{3,2,1,0:T(8,128)(2,1)}, bf16[2,1,64,2048]{3,2,1,0:T(8,128)(2,1)S(1)}, u32[]{:S(2)}, u32[]{:S(2)}) collective-permute-start(bf16[2,1,64,2048]{3,2,1,0:T(8,128)(2,1)} %get-tuple-element.38), channel_id=1, source_target_pairs={{0,8},{8,0},{16,24},{24,16},{1,9},{9,1},{17,25},{25,17},{2,10},{10... | collective-permute-start | bytes 1572872 | tf_op jit(solution)/shard_map/ppermute | solution.py:23
  12.1 3.6 %copy-start.7 = (bf16[2,1,64,2048]{3,2,0,1:T(8,128)(2,1)S(1)}, bf16[2,1,64,2048]{3,2,0,1:T(8,128)(2,1)}, u32[]{:S(2)}) copy-start(bf16[2,1,64,2048]{3,2,0,1:T(8,128)(2,1)} %get-tuple-element.37) | copy-start | bytes 1572868
  12.1 8.6 %collective-permute-start.10 = (bf16[1,1,64,2048]{3,2,1,0:T(8,128)(2,1)S(1)}, bf16[1,1,64,2048]{3,2,1,0:T(8,128)(2,1)S(1)}, u32[]{:S(2)}, u32[]{:S(2)}) collective-permute-start(bf16[1,1,64,2048]{3,2,1,0:T(8,128)(2,1)S(1)} %get-tuple-element.42), channel_id=1, source_target_pairs={{0,16},{8,24},{16,0},{24,8},{1,17},{9,25},{17,1},{25,9},{2,18},{10... | collective-permute-start | bytes 786440 | tf_op jit(solution)/shard_map/ppermute | solution.py:23
  12.5 26.0 %collective-permute-start = (bf16[8,1,64,2048]{3,2,1,0:T(8,128)(2,1)}, bf16[8,1,64,2048]{3,2,1,0:T(8,128)(2,1)S(1)}, u32[]{:S(2)}, u32[]{:S(2)}) collective-permute-start(bf16[8,1,64,2048]{3,2,1,0:T(8,128)(2,1)} %bitcast.175), channel_id=1, source_target_pairs={{0,8},{8,0},{16,24},{24,16},{1,9},{9,1},{17,25},{25,17},{2,10},{10... | collective-permute-start | bytes 6291464 | tf_op jit(solution)/shard_map/ppermute | solution.py:23
  15.7 16.8 %collective-permute-start.1 = (bf16[2,1,64,2048]{3,2,0,1:T(8,128)(2,1)S(1)}, bf16[2,1,64,2048]{3,2,0,1:T(8,128)(2,1)S(1)}, u32[]{:S(2)}, u32[]{:S(2)}) collective-permute-start(bf16[2,1,64,2048]{3,2,0,1:T(8,128)(2,1)S(1)} %copy-done.7), channel_id=1, source_target_pairs={{0,8},{8,0},{16,24},{24,16},{1,9},{9,1},{17,25},{25,17},{2,10},{10... | collective-permute-start | bytes 1572872 | tf_op jit(solution)/shard_map/ppermute | solution.py:23
  20.7 3.3 %collective-permute-start.7 = (bf16[1,1,64,2048]{3,2,1,0:T(8,128)(2,1)}, bf16[1,1,64,2048]{3,2,1,0:T(8,128)(2,1)S(1)}, u32[]{:S(2)}, u32[]{:S(2)}) collective-permute-start(bf16[1,1,64,2048]{3,2,1,0:T(8,128)(2,1)} %collective-permute-done.6), channel_id=1, source_target_pairs={{0,8},{8,0},{16,24},{24,16},{1,9},{9,1},{17,25},{25,17},{2,10},{10... | collective-permute-start | bytes 786440 | tf_op jit(solution)/shard_map/ppermute | solution.py:23
  20.7 5.8 %collective-permute-start.11 = (bf16[1,1,64,2048]{3,2,1,0:T(8,128)(2,1)S(1)}, bf16[1,1,64,2048]{3,2,1,0:T(8,128)(2,1)S(1)}, u32[]{:S(2)}, u32[]{:S(2)}) collective-permute-start(bf16[1,1,64,2048]{3,2,1,0:T(8,128)(2,1)S(1)} %collective-permute-done.10), channel_id=1, source_target_pairs={{0,8},{8,0},{16,24},{24,16},{1,9},{9,1},{17,25},{25,17},{2,10},{10... | collective-permute-start | bytes 786440 | tf_op jit(solution)/shard_map/ppermute | solution.py:23
  23.6 14.9 %collective-permute-start.3 = (bf16[2,1,64,2048]{3,2,1,0:T(8,128)(2,1)S(1)}, bf16[2,1,64,2048]{3,2,1,0:T(8,128)(2,1)S(1)}, u32[]{:S(2)}, u32[]{:S(2)}) collective-permute-start(bf16[2,1,64,2048]{3,2,1,0:T(8,128)(2,1)S(1)} %get-tuple-element.40), channel_id=1, source_target_pairs={{0,16},{8,24},{16,0},{24,8},{1,17},{9,25},{17,1},{25,9},{2,18},{10... | collective-permute-start | bytes 1572872 | tf_op jit(solution)/shard_map/ppermute | solution.py:23
  24.0 10.0 %copy-start = (f32[1,8,64,2048]{3,2,1,0:T(8,128)S(1)}, f32[1,8,64,2048]{3,2,1,0:T(8,128)}, u32[]{:S(2)}) copy-start(f32[1,8,64,2048]{3,2,1,0:T(8,128)} %param.6) | copy-start | bytes 12582916
  26.5 12.3 %copy-start.6 = (bf16[1,8,64,2048]{3,2,1,0:T(8,128)(2,1)S(1)}, bf16[1,8,64,2048]{3,2,1,0:T(8,128)(2,1)}, u32[]{:S(2)}) copy-start(bf16[1,8,64,2048]{3,2,1,0:T(8,128)(2,1)} %param.5) | copy-start | bytes 6291460
  27.4 29.0 %collective-permute-start.12 = (bf16[1,64,2048]{2,1,0:T(8,128)(2,1)S(1)}, bf16[1,64,2048]{2,1,0:T(8,128)(2,1)S(1)}, u32[]{:S(2)}, u32[]{:S(2)}) collective-permute-start(bf16[1,64,2048]{2,1,0:T(8,128)(2,1)S(1)} %get-tuple-element.50), channel_id=1, source_target_pairs={{0,6},{1,7},{2,4},{3,5},{4,2},{5,3},{6,0},{7,1},{8,14},{9,15},{10,... | collective-permute-start | bytes 786440 | tf_op jit(solution)/shard_map/ppermute | solution.py:23
  31.3 27.7 %collective-permute-start.8 = (bf16[1,64,2048]{2,1,0:T(8,128)(2,1)S(1)}, bf16[1,64,2048]{2,1,0:T(8,128)(2,1)S(1)}, u32[]{:S(2)}, u32[]{:S(2)}) collective-permute-start(bf16[1,64,2048]{2,1,0:T(8,128)(2,1)S(1)} %get-tuple-element.52), channel_id=1, source_target_pairs={{0,7},{1,6},{2,5},{3,4},{4,3},{5,2},{6,1},{7,0},{8,15},{9,14},{10,... | collective-permute-start | bytes 786440 | tf_op jit(solution)/shard_map/ppermute | solution.py:23
  32.5 17.2 %collective-permute-start.18 = (bf16[2,1,64,2048]{3,2,1,0:T(8,128)(2,1)S(1)}, bf16[2,1,64,2048]{3,2,1,0:T(8,128)(2,1)S(1)}, u32[]{:S(2)}, u32[]{:S(2)}) collective-permute-start(bf16[2,1,64,2048]{3,2,1,0:T(8,128)(2,1)S(1)} %get-tuple-element.41), channel_id=1, source_target_pairs={{0,16},{8,24},{16,0},{24,8},{1,17},{9,25},{17,1},{25,9},{2,18},{10... | collective-permute-start | bytes 1572872 | tf_op jit(solution)/shard_map/ppermute | solution.py:23
  34.7 15.0 %copy-start.3 = (bf16[1,8,64,2048]{3,2,1,0:T(8,128)(2,1)S(1)}, bf16[1,8,64,2048]{3,2,1,0:T(8,128)(2,1)}, u32[]{:S(2)}) copy-start(bf16[1,8,64,2048]{3,2,1,0:T(8,128)(2,1)} %param.7) | copy-start | bytes 6291460
  38.5 21.5 %collective-permute-start.4 = (bf16[2,1,64,2048]{3,2,0,1:T(8,128)(2,1)S(1)}, bf16[2,1,64,2048]{3,2,0,1:T(8,128)(2,1)S(1)}, u32[]{:S(2)}, u32[]{:S(2)}) collective-permute-start(bf16[2,1,64,2048]{3,2,0,1:T(8,128)(2,1)S(1)} %fusion.3), channel_id=1, source_target_pairs={{0,16},{8,24},{16,0},{24,8},{1,17},{9,25},{17,1},{25,9},{2,18},{10... | collective-permute-start | bytes 1572872 | tf_op jit(solution)/shard_map/ppermute | solution.py:23
  53.3 19.2 %collective-permute-start.15 = (bf16[1,64,2048]{2,1,0:T(8,128)(2,1)S(1)}, bf16[1,64,2048]{2,1,0:T(8,128)(2,1)S(1)}, u32[]{:S(2)}, u32[]{:S(2)}) collective-permute-start(bf16[1,64,2048]{2,1,0:T(8,128)(2,1)S(1)} %get-tuple-element.47), channel_id=1, source_target_pairs={{0,2},{1,3},{2,0},{3,1},{4,6},{5,7},{6,4},{7,5},{8,10},{9,11},{10,... | collective-permute-start | bytes 786440 | tf_op jit(solution)/shard_map/ppermute | solution.py:23
  54.9 21.9 %collective-permute-start.16 = (bf16[1,64,2048]{2,1,0:T(8,128)(2,1)S(1)}, bf16[1,64,2048]{2,1,0:T(8,128)(2,1)S(1)}, u32[]{:S(2)}, u32[]{:S(2)}) collective-permute-start(bf16[1,64,2048]{2,1,0:T(8,128)(2,1)S(1)} %get-tuple-element.46), channel_id=1, source_target_pairs={{0,3},{1,2},{2,1},{3,0},{4,7},{5,6},{6,5},{7,4},{8,11},{9,10},{10,... | collective-permute-start | bytes 786440 | tf_op jit(solution)/shard_map/ppermute | solution.py:23
  56.4 20.5 %collective-permute-start.19 = (bf16[1,64,2048]{2,1,0:T(8,128)(2,1)S(1)}, bf16[1,64,2048]{2,1,0:T(8,128)(2,1)S(1)}, u32[]{:S(2)}, u32[]{:S(2)}) collective-permute-start(bf16[1,64,2048]{2,1,0:T(8,128)(2,1)S(1)} %get-tuple-element.45), channel_id=1, source_target_pairs={{0,4},{1,5},{2,6},{3,7},{4,0},{5,1},{6,2},{7,3},{8,12},{9,13},{10,... | collective-permute-start | bytes 786440 | tf_op jit(solution)/shard_map/ppermute | solution.py:23
  59.0 21.5 %collective-permute-start.20 = (bf16[1,64,2048]{2,1,0:T(8,128)(2,1)S(1)}, bf16[1,64,2048]{2,1,0:T(8,128)(2,1)S(1)}, u32[]{:S(2)}, u32[]{:S(2)}) collective-permute-start(bf16[1,64,2048]{2,1,0:T(8,128)(2,1)S(1)} %get-tuple-element.44), channel_id=1, source_target_pairs={{0,5},{1,4},{2,7},{3,6},{4,1},{5,0},{6,3},{7,2},{8,13},{9,12},{10,... | collective-permute-start | bytes 786440 | tf_op jit(solution)/shard_map/ppermute | solution.py:23
  60.0 47.0 %collective-permute-start.13 = (bf16[8,1,64,2048]{3,2,1,0:T(8,128)(2,1)}, bf16[8,1,64,2048]{3,2,1,0:T(8,128)(2,1)}, u32[]{:S(2)}, u32[]{:S(2)}) collective-permute-start(bf16[8,1,64,2048]{3,2,1,0:T(8,128)(2,1)} %add_convert_fusion.1), channel_id=1, source_target_pairs={{0,16},{8,24},{16,0},{24,8},{1,17},{9,25},{17,1},{25,9},{2,18},{10... | collective-permute-start | bytes 6291464 | tf_op jit(solution)/shard_map/ppermute | solution.py:23
  62.0 18.9 %copy-start.1 = (f32[1,8,64,2048]{3,2,1,0:T(8,128)}, f32[1,8,64,2048]{3,2,1,0:T(8,128)S(1)}, u32[]{:S(2)}) copy-start(f32[1,8,64,2048]{3,2,1,0:T(8,128)S(1)} %get-tuple-element.29) | copy-start | bytes 12582916
  72.4 8.6 %collective-permute-start.14 = (bf16[1,64,2048]{2,1,0:T(8,128)(2,1)S(1)}, bf16[1,64,2048]{2,1,0:T(8,128)(2,1)S(1)}, u32[]{:S(2)}, u32[]{:S(2)}) collective-permute-start(bf16[1,64,2048]{2,1,0:T(8,128)(2,1)S(1)} %get-tuple-element.48), channel_id=1, source_target_pairs={{0,1},{1,0},{2,3},{3,2},{4,5},{5,4},{6,7},{7,6},{8,9},{9,8},{10,11... | collective-permute-start | bytes 786440 | tf_op jit(solution)/shard_map/ppermute | solution.py:23
  93.8 9.1 %collective-permute-start.22 = (bf16[1,64,2048]{2,1,0:T(8,128)(2,1)S(1)}, bf16[1,64,2048]{2,1,0:T(8,128)(2,1)S(1)}, u32[]{:S(2)}, u32[]{:S(2)}) collective-permute-start(bf16[1,64,2048]{2,1,0:T(8,128)(2,1)S(1)} %get-tuple-element.22), channel_id=1, source_target_pairs={{0,1},{1,0},{2,3},{3,2},{4,5},{5,4},{6,7},{7,6},{8,9},{9,8},{10,11... | collective-permute-start | bytes 786440 | tf_op jit(solution)/shard_map/ppermute | solution.py:23
  94.9 19.4 %collective-permute-start.21 = (bf16[1,64,2048]{2,1,0:T(8,128)(2,1)S(1)}, bf16[1,64,2048]{2,1,0:T(8,128)(2,1)S(1)}, u32[]{:S(2)}, u32[]{:S(2)}) collective-permute-start(bf16[1,64,2048]{2,1,0:T(8,128)(2,1)S(1)} %get-tuple-element.20), channel_id=1, source_target_pairs={{0,7},{1,6},{2,5},{3,4},{4,3},{5,2},{6,1},{7,0},{8,15},{9,14},{10,... | collective-permute-start | bytes 786440 | tf_op jit(solution)/shard_map/ppermute | solution.py:23
  98.3 16.9 %collective-permute-start.23 = (bf16[1,64,2048]{2,1,0:T(8,128)(2,1)S(1)}, bf16[1,64,2048]{2,1,0:T(8,128)(2,1)S(1)}, u32[]{:S(2)}, u32[]{:S(2)}) collective-permute-start(bf16[1,64,2048]{2,1,0:T(8,128)(2,1)S(1)} %get-tuple-element.23), channel_id=1, source_target_pairs={{0,6},{1,7},{2,4},{3,5},{4,2},{5,3},{6,0},{7,1},{8,14},{9,15},{10,... | collective-permute-start | bytes 786440 | tf_op jit(solution)/shard_map/ppermute | solution.py:23
  99.1 17.2 %collective-permute-start.24 = (bf16[1,64,2048]{2,1,0:T(8,128)(2,1)S(1)}, bf16[1,64,2048]{2,1,0:T(8,128)(2,1)S(1)}, u32[]{:S(2)}, u32[]{:S(2)}) collective-permute-start(bf16[1,64,2048]{2,1,0:T(8,128)(2,1)S(1)} %get-tuple-element.24), channel_id=1, source_target_pairs={{0,2},{1,3},{2,0},{3,1},{4,6},{5,7},{6,4},{7,5},{8,10},{9,11},{10,... | collective-permute-start | bytes 786440 | tf_op jit(solution)/shard_map/ppermute | solution.py:23
  102.9 19.0 %collective-permute-start.25 = (bf16[1,64,2048]{2,1,0:T(8,128)(2,1)S(1)}, bf16[1,64,2048]{2,1,0:T(8,128)(2,1)S(1)}, u32[]{:S(2)}, u32[]{:S(2)}) collective-permute-start(bf16[1,64,2048]{2,1,0:T(8,128)(2,1)S(1)} %get-tuple-element.25), channel_id=1, source_target_pairs={{0,3},{1,2},{2,1},{3,0},{4,7},{5,6},{6,5},{7,4},{8,11},{9,10},{10,... | collective-permute-start | bytes 786440 | tf_op jit(solution)/shard_map/ppermute | solution.py:23
  107.0 28.4 %collective-permute-start.26 = (bf16[1,64,2048]{2,1,0:T(8,128)(2,1)S(1)}, bf16[1,64,2048]{2,1,0:T(8,128)(2,1)S(1)}, u32[]{:S(2)}, u32[]{:S(2)}) collective-permute-start(bf16[1,64,2048]{2,1,0:T(8,128)(2,1)S(1)} %get-tuple-element.26), channel_id=1, source_target_pairs={{0,5},{1,4},{2,7},{3,6},{4,1},{5,0},{6,3},{7,2},{8,13},{9,12},{10,... | collective-permute-start | bytes 786440 | tf_op jit(solution)/shard_map/ppermute | solution.py:23
  114.4 23.9 %collective-permute-start.27 = (bf16[1,64,2048]{2,1,0:T(8,128)(2,1)S(1)}, bf16[1,64,2048]{2,1,0:T(8,128)(2,1)S(1)}, u32[]{:S(2)}, u32[]{:S(2)}) collective-permute-start(bf16[1,64,2048]{2,1,0:T(8,128)(2,1)S(1)} %get-tuple-element.27), channel_id=1, source_target_pairs={{0,4},{1,5},{2,6},{3,7},{4,0},{5,1},{6,2},{7,3},{8,12},{9,13},{10,... | collective-permute-start | bytes 786440 | tf_op jit(solution)/shard_map/ppermute | solution.py:23
  138.5 1.3 copy-start.4
  138.5 2.0 %copy-start.5 = (bf16[1,8,64,2048]{3,2,1,0:T(8,128)(2,1)}, bf16[1,8,64,2048]{3,2,1,0:T(8,128)(2,1)S(1)}, u32[]{:S(2)}) copy-start(bf16[1,8,64,2048]{3,2,1,0:T(8,128)(2,1)S(1)} %get-tuple-element.54) | copy-start | bytes 6291460
